TPU v7x, 32 devices: a whole 2x2x4 slice. The times are simulated.
32 devices in a mesh: gz: 16 (over z, y, core), gy: 2 (over x).
Axes of the slice: x: 2, y: 2, z: 4, core: 2. Of those that a mesh axis runs over, the one named last changes fastest.
Arguments:
- field: float32 [32, 16, 128, 256], P(None, 'gz', 'gy'), may hold values from -6 to 6
- spectral_filter: float32 [2, 16, 16, 1024], P(None, None, 'gy', 'gz'), may hold values from -6 to 6
- depth_weight: float32 [32, 27], replicated, may hold values from -1.25 to 1.25
- point_weight: float32 [32, 32], replicated, may hold values from -1 to 1
- bias_vector: float32 [32], replicated, may hold values from -3 to 3
Outputs:
- layer_out: float32 [32, 16, 128, 256], P(None, 'gz', 'gy')
All inputs are finite; a program needn't handle non-finite values.
Results may differ from a plain program's by a relative error of at most 0.000057.
Values sent between devices are 32-bit elements; how exact they have to be, the bound alone decides.
No kernel may reach another device: no remote copies, remote signals or barrier semaphores. Data moves between devices by JAX's collectives and lax.ppermute only.
A program may use at most 64 MiB of HBM per device.

v0:
```python
import functools
import math

import jax
import jax.numpy as jnp
import ml_dtypes
import numpy as np
from jax import lax
from jax.experimental import pallas as pl
from jax.experimental.pallas import tpu as pltpu
from jax.sharding import PartitionSpec as P

NX = 256
MX = 32
MY = 16
MZ = 16
CH = 32
VMEM_BYTES = 40 * 1024 * 1024
BF = jnp.bfloat16
F32 = jnp.float32


def kept(count, total):
    series = np.arange(count)
    return np.where(series < count // 2, series, total - count + series)


def trig(freqs, places, total):
    angle = 2.0 * np.pi * ((freqs[:, None] * places[None, :]) % total) / total
    return np.cos(angle), np.sin(angle)


def halves(table):
    table = np.asarray(table, np.float64)
    top = table.astype(np.float32).astype(ml_dtypes.bfloat16)
    rest = (table - top.astype(np.float64)).astype(np.float32).astype(ml_dtypes.bfloat16)
    return top, rest


def y_forward_table(y_local, gy, group):
    out = np.zeros((gy, 2, group, MY, group, y_local))
    for g in range(gy):
        c, s = trig(kept(MY, y_local * gy), g * y_local + np.arange(y_local), y_local * gy)
        for i in range(group):
            out[g, 0, i, :, i] = c
            out[g, 1, i, :, i] = s
    return out.reshape(gy, 2 * group * MY, group * y_local)


def x_forward_table():
    c, s = trig(np.arange(MX), np.arange(NX), NX)
    out = np.zeros((2, 2, NX, 2, 2, MX))
    for p in range(2):
        out[p, 0, :, p, 0] = c.T
        out[p, 0, :, p, 1] = -s.T
        out[p, 1, :, p, 0] = -s.T
        out[p, 1, :, p, 1] = -c.T
    return out.reshape(4, NX, 4 * MX)


def x_inverse_table(scale):
    c, s = trig(np.arange(MX), np.arange(NX), NX)
    w = np.where(np.arange(MX) == 0, 1.0, 2.0)[:, None] * scale
    out = np.zeros((2, 2, 2, MX, 2, NX))
    for p in range(2):
        out[p, p, 0, :, 0] = w * c
        out[p, p, 1, :, 0] = -w * s
        out[p, p, 0, :, 1] = w * s
        out[p, p, 1, :, 1] = w * c
    return out.reshape(2, 4 * MX, 2 * NX)


def y_inverse_table(y_local, gy, group):
    out = np.zeros((gy, group, y_local, 2, group, MY))
    for g in range(gy):
        c, s = trig(kept(MY, y_local * gy), g * y_local + np.arange(y_local), y_local * gy)
        for i in range(group):
            out[g, i, :, 0, i] = c.T
            out[g, i, :, 1, i] = -s.T
    return out.reshape(gy, group * y_local, 2 * group * MY)


def z_tables(gz, gy, rows, scale):
    c, s = trig(kept(MZ, gz), np.arange(gz), gz)
    eye = np.eye(rows)
    one = np.ones(gy)
    both = np.stack([c, s])
    fwd = np.einsum("tqz,g,jk->tqjzgk", both, one, eye) * scale
    inv = np.einsum("tqz,g,jk->tzgjqk", both, one, eye)
    return fwd.reshape(2 * MZ * rows, gz * gy * rows), inv.reshape(2 * gz * gy * rows, MZ * rows)


def parts(value):
    top = value.astype(BF)
    return top, (value - top.astype(F32)).astype(BF)


def dot(a, b):
    return jnp.dot(a, b, preferred_element_type=F32)


def dot3(a, b):
    return dot(a[0], b[0]) + (dot(a[0], b[1]) + dot(a[1], b[0]))


def forward_kernel(group, _, field, y_top, y_rest, x_top, x_rest, out):
    y_table = (y_top[0], y_rest[0])
    half = group * MY
    total = jnp.zeros((half, 4 * MX), F32)
    for p in range(2):
        rows = jnp.concatenate([field[2 * i + p] for i in range(group)], axis=0)
        turned = dot3(y_table, parts(rows))
        for t in range(2):
            piece = parts(turned[t * half : (t + 1) * half])
            total = total + dot3(piece, (x_top[2 * p + t], x_rest[2 * p + t]))
    out[...] = total.reshape(group, MY, 4 * MX)


def swap_parts(value):
    lane = lax.broadcasted_iota(jnp.int32, value.shape, 1)
    is_real = (lane // MX) % 2 == 0
    return jnp.where(is_real, pltpu.roll(value, 4 * MX - MX, 1), pltpu.roll(value, MX, 1)), is_real


def filter_kernel(arrived, gain_same, gain_cross, f_top, f_rest, i_top, i_rest, out):
    half = f_top.shape[0] // 2
    turned = dot3((f_top[...], f_rest[...]), parts(arrived[...]))
    crossed, is_real = swap_parts(turned[half:])
    modes = turned[:half] + jnp.where(is_real, crossed, -crossed)
    crossed, _ = swap_parts(modes)
    filtered = modes * gain_same[...] + crossed * gain_cross[...]
    half = i_top.shape[0] // 2
    back = dot3((i_top[...], i_rest[...]), parts(filtered))
    crossed, is_real = swap_parts(back[half:])
    out[...] = back[:half] + jnp.where(is_real, -crossed, crossed)


def inverse_kernel(group, _, modes, base, bias, x_top, x_rest, y_top, y_rest, out):
    step = pl.program_id(0)
    y_table = (y_top[0], y_rest[0])
    rows = parts(modes[...].reshape(group * MY, 4 * MX))
    y_local = out.shape[1]
    for p in range(2):
        wide = dot3(rows, (x_top[p], x_rest[p]))
        tall = jnp.concatenate([wide[:, :NX], wide[:, NX:]], axis=0)
        planes = dot3(y_table, parts(tall)).reshape(group, y_local, NX)
        for i in range(group):
            c = 2 * i + p
            out[c] = planes[i] + (base[c] + bias[step * 2 * group + c])


def conv_kernel(top_tile, bottom_tile, weight, point, main, above, below, down, mid, up, shifted, depth):
    rows = main.shape[1]

    def load(c, _):
        if top_tile:
            first = above[c, 7:8, :]
        else:
            first = above[pl.ds(c, 1), :]
        if bottom_tile:
            last = below[c, 0:1, :]
        else:
            last = below[pl.ds(c, 1), :]
        centre = main[c]
        for e, turn in ((0, 1), (1, 0), (2, NX - 1)):
            for place, value in ((pl.ds(7, 1), first), (pl.ds(8, rows), centre), (pl.ds(8 + rows, 1), last)):
                shifted[e, c, place, :] = pltpu.roll(value, turn, 1) if turn else value
        return 0

    lax.fori_loop(0, CH, load, 0)

    def taps(c, _):
        sums = [None, None, None]
        for e in range(3):
            for b in range(3):
                value = shifted[e, c, pl.ds(7 + b, rows), :]
                for a in range(3):
                    term = weight[c * 27 + a * 9 + b * 3 + e] * value
                    sums[a] = term if sums[a] is None else sums[a] + term
        for a in range(3):
            depth[a, c] = sums[a]
        return 0

    lax.fori_loop(0, CH, taps, 0)

    spread = (
        lax.broadcasted_iota(jnp.int32, (8 * CH, CH), 0) // 8
        == lax.broadcasted_iota(jnp.int32, (8 * CH, CH), 1)
    ).astype(BF)
    gather = (
        lax.broadcasted_iota(jnp.int32, (CH, 8 * CH), 1) // 8
        == lax.broadcasted_iota(jnp.int32, (CH, 8 * CH), 0)
    ).astype(BF)
    same = (
        lax.broadcasted_iota(jnp.int32, (8 * CH, 8 * CH), 0) % 8
        == lax.broadcasted_iota(jnp.int32, (8 * CH, 8 * CH), 1) % 8
    )
    mix = tuple(
        jnp.where(same, dot(dot(spread, part).astype(BF), gather), 0.0).astype(BF)
        for part in parts(point[...])
    )
    for a, out in ((0, down), (1, mid), (2, up)):
        for t in range(rows // 8):
            tile = depth[a, :, pl.ds(8 * t, 8), :].reshape(8 * CH, NX)
            out[:, pl.ds(8 * t, 8), :] = dot3(mix, parts(tile)).reshape(CH, 8, NX)


def finish_kernel(aliased, base, low, high, *rest):
    out = rest[-1]
    total = base[...] + (low[...] + high[...])
    out[...] = 0.5 * total * (1.0 + lax.erf(total * (1.0 / math.sqrt(2.0))))


def params():
    return pltpu.CompilerParams(vmem_limit_bytes=VMEM_BYTES)


def cost(flops, moved):
    return pl.CostEstimate(flops=flops, bytes_accessed=moved, transcendentals=0)


def forward_call(field, place, gy):
    y_local = field.shape[1]
    group = max(1, min(CH // 2, 256 // y_local))
    y_tab = halves(y_forward_table(y_local, gy, group))
    x_tab = halves(x_forward_table())
    tall, wide = y_tab[0].shape[1:]
    y_spec = pl.BlockSpec((1, tall, wide), lambda i, s: (s[0], 0, 0))
    x_spec = pl.BlockSpec((4, NX, 4 * MX), lambda i, s: (0, 0, 0))
    return pl.pallas_call(
        functools.partial(forward_kernel, group),
        out_shape=jax.ShapeDtypeStruct((CH // 2, MY, 4 * MX), F32),
        grid_spec=pltpu.PrefetchScalarGridSpec(
            num_scalar_prefetch=1,
            grid=(CH // 2 // group,),
            in_specs=[
                pl.BlockSpec((2 * group, y_local, NX), lambda i, s: (i, 0, 0)),
                y_spec, y_spec, x_spec, x_spec,
            ],
            out_specs=pl.BlockSpec((group, MY, 4 * MX), lambda i, s: (i, 0, 0)),
        ),
        compiler_params=params(),
        cost_estimate=cost(2 * 10**9, 4 * 2**20),
        name="forward_modes",
    )(place, field, *y_tab, *x_tab)


def filter_call(arrived, gains, gz, gy, scale):
    rows = gains.shape[2]
    fwd, inv = z_tables(gz, gy, rows, scale)
    fwd, inv = halves(fwd), halves(inv)
    split = gains.reshape(2, MZ * rows, 2, 1, MX)
    same = jnp.concatenate([split[0], split[0]], axis=2).reshape(MZ * rows, 4 * MX)
    cross = jnp.concatenate([-split[1], split[1]], axis=2).reshape(MZ * rows, 4 * MX)
    return pl.pallas_call(
        filter_kernel,
        out_shape=jax.ShapeDtypeStruct(arrived.shape, F32),
        compiler_params=params(),
        cost_estimate=cost(2 * 10**8, 2**20),
        name="filter_modes",
    )(arrived, same, cross, *fwd, *inv)


def inverse_call(modes, base, bias, place, gy, scale):
    y_local = base.shape[1]
    group = 8
    x_tab = halves(x_inverse_table(scale))
    y_tab = halves(y_inverse_table(y_local, gy, group))
    tall, wide = y_tab[0].shape[1:]
    y_spec = pl.BlockSpec((1, tall, wide), lambda i, s: (s[0], 0, 0))
    x_spec = pl.BlockSpec((2, 4 * MX, 2 * NX), lambda i, s: (0, 0, 0))
    plane = pl.BlockSpec((2 * group, y_local, NX), lambda i, s: (i, 0, 0))
    return pl.pallas_call(
        functools.partial(inverse_kernel, group),
        out_shape=jax.ShapeDtypeStruct(base.shape, F32),
        grid_spec=pltpu.PrefetchScalarGridSpec(
            num_scalar_prefetch=1,
            grid=(CH // 2 // group,),
            in_specs=[
                pl.BlockSpec((group, MY, 4 * MX), lambda i, s: (i, 0, 0)),
                plane,
                pl.BlockSpec(memory_space=pltpu.SMEM),
                x_spec, x_spec, y_spec, y_spec,
            ],
            out_specs=plane,
        ),
        compiler_params=params(),
        cost_estimate=cost(2 * 10**9, 6 * 2**20),
        name="inverse_modes",
    )(place, modes, base, bias, *x_tab, *y_tab)


def conv_call(field, above, below, weight, point, start, rows):
    y_local = field.shape[1]
    top_tile, bottom_tile = start > 0, start + rows < y_local
    whole = pl.BlockSpec((CH, rows, NX), lambda i: (0, 0, 0))
    edge = pl.BlockSpec((CH, NX), lambda i: (0, 0))
    tile = lambda at: pl.BlockSpec((CH, 8, NX), lambda i: (0, at, 0))
    return pl.pallas_call(
        functools.partial(conv_kernel, top_tile, bottom_tile),
        out_shape=[jax.ShapeDtypeStruct((CH, rows, NX), F32)] * 3,
        grid=(1,),
        in_specs=[
            pl.BlockSpec(memory_space=pltpu.SMEM),
            pl.BlockSpec((CH, CH), lambda i: (0, 0)),
            pl.BlockSpec((CH, rows, NX), lambda i: (0, start // rows, 0)),
            tile(start // 8 - 1) if top_tile else edge,
            tile((start + rows) // 8) if bottom_tile else edge,
        ],
        out_specs=[whole] * 3,
        scratch_shapes=[
            pltpu.VMEM((3, CH, rows + 16, NX), F32),
            pltpu.VMEM((3, CH, rows, NX), F32),
        ],
        compiler_params=params(),
        cost_estimate=cost(2 * 10**9, 4 * 2**20),
        name="mixed_planes",
    )(weight, point, field, field if top_tile else above, field if bottom_tile else below)


def finish_call(base, low, high, so_far, start, rows):
    block = pl.BlockSpec((CH, 8, NX), lambda i: (0, start // 8 + i, 0))
    piece = pl.BlockSpec((CH, 8, NX), lambda i: (0, i, 0))
    operands, specs, alias = [base, low, high], [block, piece, piece], {}
    if so_far is not None:
        operands.append(so_far)
        specs.append(pl.BlockSpec(memory_space=pl.ANY))
        alias = {3: 0}
    return pl.pallas_call(
        functools.partial(finish_kernel, bool(alias)),
        out_shape=jax.ShapeDtypeStruct(base.shape, F32),
        grid=(rows // 8,),
        in_specs=specs,
        out_specs=block,
        input_output_aliases=alias,
        compiler_params=params(),
        cost_estimate=cost(10**9, 4 * rows * CH * NX * 4),
        name="finished_rows",
    )(*operands)


def general_filter(coarse, gains, gz, gy, scale):
    j_own, n_own = gains.shape[2], gains.shape[3]
    both = ("gz", "gy")
    flat = coarse.reshape(CH // 2, MY, 2, 2, MX).transpose(3, 1, 0, 2, 4).reshape(2, MY, CH * MX)
    sent = flat.reshape(2, gy, j_own, gz, n_own).transpose(3, 1, 0, 2, 4).reshape(gz * gy, -1)
    got = lax.all_to_all(sent, both, split_axis=0, concat_axis=0, tiled=True)
    got = got.reshape(gz, gy, 2, j_own, n_own)
    c, s = (jnp.asarray(t, F32) for t in trig(kept(MZ, gz), np.arange(gz), gz))
    mul = functools.partial(jnp.einsum, precision=lax.Precision.HIGHEST)
    whole = got.sum(axis=1) * scale
    real = mul("zjn,qz->qjn", whole[:, 0], c) + mul("zjn,qz->qjn", whole[:, 1], s)
    imag = mul("zjn,qz->qjn", whole[:, 1], c) - mul("zjn,qz->qjn", whole[:, 0], s)
    real, imag = real * gains[0] - imag * gains[1], real * gains[1] + imag * gains[0]
    out = jnp.stack(
        [
            mul("qjn,qz->zjn", real, c) - mul("qjn,qz->zjn", imag, s),
            mul("qjn,qz->zjn", real, s) + mul("qjn,qz->zjn", imag, c),
        ],
        axis=1,
    )
    out = jnp.broadcast_to(out[:, None], (gz, gy, 2, j_own, n_own)).reshape(gz * gy, -1)
    back = lax.all_to_all(out, both, split_axis=0, concat_axis=0, tiled=True)
    back = back.reshape(gz, gy, 2, j_own, n_own).transpose(2, 1, 3, 0, 4)
    back = back.reshape(2, MY, CH // 2, 2, MX)
    return back.transpose(2, 1, 3, 0, 4).reshape(CH // 2, MY, 4 * MX)


def body(field, spectral_filter, depth_weight, point_weight, bias_vector):
    gz, gy = lax.axis_size("gz"), lax.axis_size("gy")
    y_local = field.shape[2]
    place = lax.axis_index("gy").astype(jnp.int32).reshape(1)
    field = field.reshape(CH, y_local, NX)
    weight = depth_weight.reshape(-1)
    y_total = gy * y_local
    forward_scale = 1.0 / math.sqrt(float(NX) * y_total * gz)
    inverse_scale = 1.0 / math.sqrt(2.0 * MX * MY * MZ)

    def ring(axis, count, by):
        return [(i, (i + by) % count) for i in range(count)]

    above = lax.ppermute(field[:, y_local - 1, :], "gy", ring("gy", gy, 1))
    below = lax.ppermute(field[:, 0, :], "gy", ring("gy", gy, -1))

    rows = max(8, y_local // 4)
    starts = list(range(0, y_local, rows))
    order = sorted(starts, key=lambda s: (s == 0 or s + rows == y_local, s))
    pieces = {}
    mids = {}
    for start in order:
        down, mid, up = conv_call(field, above, below, weight, point_weight, start, rows)
        mids[start] = mid
        pieces[start] = (
            lax.ppermute(down, "gz", ring("gz", gz, 1)),
            lax.ppermute(up, "gz", ring("gz", gz, -1)),
        )

    coarse = forward_call(field, place, gy)
    j_own, n_own = spectral_filter.shape[2], spectral_filter.shape[3]
    if j_own == 8 and n_own == 2 * MX:
        both = ("gz", "gy")
        sent = coarse.reshape(gz * gy * 8, 4 * MX)
        got = lax.all_to_all(sent, both, split_axis=0, concat_axis=0, tiled=True)
        out = filter_call(got, spectral_filter, gz, gy, forward_scale)
        back = lax.all_to_all(out, both, split_axis=0, concat_axis=0, tiled=True)
        back = back.reshape(CH // 2, MY, 4 * MX)
    else:
        back = general_filter(coarse, spectral_filter, gz, gy, forward_scale)

    base = jnp.concatenate([mids[s] for s in starts], axis=1)
    base = inverse_call(back, base, bias_vector, place, gy, inverse_scale)
    result = None
    for start in order:
        result = finish_call(base, *pieces[start], result, start, rows)
    return result.reshape(CH, 1, y_local, NX)


def solution(mesh):
    in_specs = (P(None, "gz", "gy", None), P(None, None, "gy", "gz"), P(), P(), P())
    out_specs = P(None, "gz", "gy", None)
    return jax.shard_map(body, mesh=mesh, in_specs=in_specs, out_specs=out_specs, check_vma=False)
```

profile of v0, /device:TPU:1, one launch (start us, length us, event | category | flops | bytes accessed | tf_op | source)
XLA Modules:
  0.0 101.0 jit_solution(15333006738783109954)
XLA Ops:
  0.0 1.6 %copy-done = f32[32,1,64,256]{3,2,1,0:T(8,128)S(1)} copy-done((f32[32,1,64,256]{3,2,1,0:T(8,128)S(1)}, f32[32,1,64,256]{3,2,1,0:T(8,128)}, u32[]{:S(2)}) %copy-start) | copy-done | bytes 2097176
  1.6 0.9 copy-done.23
  2.5 0.9 copy-done.24
  5.3 2.9 %forward_modes.1 = f32[16,16,128]{2,1,0:T(8,128)} custom-call(s32[1]{0:T(128)} %bitcast._, f32[32,64,256]{2,1,0:T(8,128)S(1)} %bitcast.22, bf16[2,128,256]{2,1,0:T(8,128)(2,1)S(1)} %copy-done.26, bf16[2,128,256]{2,1,0:T(8,128)(2,1)S(1)} %copy-done.25, bf16[4,256,128]{2,1,0:T(8,128)(2,1)S(1)} %copy-done.24, bf16[4,256,128]{2,1,0:T(8,128)(2,1)S(1)} %copy-done.23), custom_call_target="tpu_custom_call" | custom-call | flops 2000000000 | bytes 4194304 | tf_op jit(solution)/shard_map/forward_modes/pallas_call | solution.py:230
  8.2 7.1 %all-to-all-start = ((f32[32,8,128]{2,1,0:T(8,128)}), f32[32,8,128]{2,1,0:T(8,128)S(1)}, u32[]{:S(2)}, u32[]{:S(2)}) async-start(f32[32,8,128]{2,1,0:T(8,128)} %bitcast.3), calls=%async_computation | async-start | bytes 262144 | tf_op jit(solution)/shard_map/all_to_all | solution.py:403
  15.4 7.7 %mixed_planes.6 = (f32[32,16,256]{2,1,0:T(8,128)}, f32[32,16,256]{2,1,0:T(8,128)S(1)}, f32[32,16,256]{2,1,0:T(8,128)}) custom-call(f32[864]{0:T(1024)S(1)} %reshape.50.weight, f32[32,32]{1,0:T(8,128)S(1)} %copy-done.15, f32[32,64,256]{2,1,0:T(8,128)S(1)} %bitcast.23, f32[32,64,256]{2,1,0:T(8,128)S(1)} %bitcast.24, f32[32,64,256]{2,1,0:T(8,128)S(1)} %bitcast.25), custom_call_target="tpu_custom_call" | custom-call | flops 2000000000 | bytes 4194304 | tf_op jit(solution)/shard_map/mixed_planes/pallas_call | solution.py:299
  24.0 1.6 %collective-permute-start.6 = (f32[32,16,256]{2,1,0:T(8,128)}, f32[32,16,256]{2,1,0:T(8,128)S(1)}, u32[]{:S(2)}, u32[]{:S(2)}) collective-permute-start(f32[32,16,256]{2,1,0:T(8,128)} %get-tuple-element.25), channel_id=1, source_target_pairs={{0,2},{2,4},{4,6},{6,8},{8,10},{10,12},{12,14},{14,16},{16,18},{18... | collective-permute-start | bytes 1572872 | tf_op jit(solution)/shard_map/ppermute | solution.py:394
  25.6 7.7 %mixed_planes.5 = (f32[32,16,256]{2,1,0:T(8,128)}, f32[32,16,256]{2,1,0:T(8,128)S(1)}, f32[32,16,256]{2,1,0:T(8,128)}) custom-call(f32[864]{0:T(1024)S(1)} %reshape.50.weight, f32[32,32]{1,0:T(8,128)S(1)} %copy-done.15, f32[32,64,256]{2,1,0:T(8,128)S(1)} %bitcast.26, f32[32,64,256]{2,1,0:T(8,128)S(1)} %bitcast.27, f32[32,64,256]{2,1,0:T(8,128)S(1)} %bitcast.28), custom_call_target="tpu_custom_call" | custom-call | flops 2000000000 | bytes 4194304 | tf_op jit(solution)/shard_map/mixed_planes/pallas_call | solution.py:299
  33.3 1.8 %collective-permute-start.8 = (f32[32,16,256]{2,1,0:T(8,128)}, f32[32,16,256]{2,1,0:T(8,128)}, u32[]{:S(2)}, u32[]{:S(2)}) collective-permute-start(f32[32,16,256]{2,1,0:T(8,128)} %get-tuple-element.27), channel_id=1, source_target_pairs={{0,2},{2,4},{4,6},{6,8},{8,10},{10,12},{12,14},{14,16},{16,18},{18... | collective-permute-start | bytes 1572872 | tf_op jit(solution)/shard_map/ppermute | solution.py:394
  35.1 1.4 %collective-permute-start.9 = (f32[32,16,256]{2,1,0:T(8,128)}, f32[32,16,256]{2,1,0:T(8,128)}, u32[]{:S(2)}, u32[]{:S(2)}) collective-permute-start(f32[32,16,256]{2,1,0:T(8,128)} %get-tuple-element.28), channel_id=1, source_target_pairs={{0,30},{2,0},{4,2},{6,4},{8,6},{10,8},{12,10},{14,12},{16,14},{18,... | collective-permute-start | bytes 1572872 | tf_op jit(solution)/shard_map/ppermute | solution.py:395
  36.5 1.2 %copy.76 = f32[32,1,64,256]{3,0,2,1:T(8,128)S(1)} copy(f32[32,1,64,256]{3,2,1,0:T(8,128)S(1)} %copy-done.1) | data formatting | bytes 4194304 | tf_op args[0]
  38.3 1.5 %collective-permute-start.1 = (f32[32,256]{1,0:T(8,128)}, f32[32,256]{1,0:T(8,128)S(1)}, u32[]{:S(2)}, u32[]{:S(2)}) collective-permute-start(f32[32,256]{1,0:T(8,128)} %get-tuple-element.30), channel_id=1, source_target_pairs={{0,1},{1,0},{2,3},{3,2},{4,5},{5,4},{6,7},{7,6},{8,9},{9,8},{10,11... | collective-permute-start | bytes 98312 | tf_op jit(solution)/shard_map/ppermute | solution.py:383
  40.7 1.0 squeeze.15
  42.4 1.0 copy.59
  45.8 7.7 %mixed_planes.7 = (f32[32,16,256]{2,1,0:T(8,128)S(1)}, f32[32,16,256]{2,1,0:T(8,128)S(1)}, f32[32,16,256]{2,1,0:T(8,128)}) custom-call(f32[864]{0:T(1024)S(1)} %reshape.50.weight, f32[32,32]{1,0:T(8,128)S(1)} %copy-done.16, f32[32,64,256]{2,1,0:T(8,128)S(1)} %bitcast.29, f32[32,64,256]{2,1,0:T(8,128)S(1)} %bitcast.30, f32[32,256]{1,0:T(8,128)S(1)} %copy-done.14), custom_call_target="tpu_custom_call" | custom-call | flops 2000000000 | bytes 4194304 | tf_op jit(solution)/shard_map/mixed_planes/pallas_call | solution.py:299
  55.1 0.9 copy-done.9
  56.0 0.9 copy-done.10
  57.8 1.6 %filter_modes.1 = f32[256,128]{1,0:T(8,128)} custom-call(f32[256,128]{1,0:T(8,128)S(1)} %bitcast.33, f32[128,128]{1,0:T(8,128)S(1)} %copy.61.gain_same, f32[128,128]{1,0:T(8,128)S(1)} %copy.62.gain_cross, bf16[256,256]{1,0:T(8,128)(2,1)S(1)} %copy-done.11, bf16[256,256]{1,0:T(8,128)(2,1)S(1)} %copy-done.10, bf16[512,128]{1,0:T(8,128)(2,1)S(1)} %copy-done.9, ...), custom_call_target="tpu_custom_call" | custom-call | flops 200000000 | bytes 1048576 | tf_op jit(solution)/shard_map/filter_modes/pallas_call | solution.py:255
  59.4 7.1 %all-to-all-start.1 = ((f32[32,8,128]{2,1,0:T(8,128)}), f32[32,8,128]{2,1,0:T(8,128)S(1)}, u32[]{:S(2)}, u32[]{:S(2)}) async-start(f32[32,8,128]{2,1,0:T(8,128)} %bitcast.7), calls=%async_computation.1 | async-start | bytes 262144 | tf_op jit(solution)/shard_map/all_to_all | solution.py:405
  66.5 1.7 %collective-permute-start.2 = (f32[32,16,256]{2,1,0:T(8,128)}, f32[32,16,256]{2,1,0:T(8,128)}, u32[]{:S(2)}, u32[]{:S(2)}) collective-permute-start(f32[32,16,256]{2,1,0:T(8,128)} %copy-done.12), channel_id=1, source_target_pairs={{0,2},{2,4},{4,6},{6,8},{8,10},{10,12},{12,14},{14,16},{16,18},{18... | collective-permute-start | bytes 1572872 | tf_op jit(solution)/shard_map/ppermute | solution.py:394
  68.9 7.9 %mixed_planes.4 = (f32[32,16,256]{2,1,0:T(8,128)}, f32[32,16,256]{2,1,0:T(8,128)S(1)}, f32[32,16,256]{2,1,0:T(8,128)}) custom-call(f32[864]{0:T(1024)S(1)} %reshape.50.weight, f32[32,32]{1,0:T(8,128)S(1)} %copy-done.17, f32[32,64,256]{2,1,0:T(8,128)S(1)} %bitcast.31, f32[32,256]{1,0:T(8,128)} %collective-permute-done.above, f32[32,64,256]{2,1,0:T(8,128)S(1)} %bitcast.32), custom_call_target="tpu_custom_call" | custom-call | flops 2000000000 | bytes 4194304 | tf_op jit(solution)/shard_map/mixed_planes/pallas_call | solution.py:299
  76.9 1.7 %collective-permute-start.4 = (f32[32,16,256]{2,1,0:T(8,128)}, f32[32,16,256]{2,1,0:T(8,128)}, u32[]{:S(2)}, u32[]{:S(2)}) collective-permute-start(f32[32,16,256]{2,1,0:T(8,128)} %get-tuple-element.23), channel_id=1, source_target_pairs={{0,2},{2,4},{4,6},{6,8},{8,10},{10,12},{12,14},{14,16},{16,18},{18... | collective-permute-start | bytes 1572872 | tf_op jit(solution)/shard_map/ppermute | solution.py:394
  78.6 1.6 %collective-permute-start.5 = (f32[32,16,256]{2,1,0:T(8,128)}, f32[32,16,256]{2,1,0:T(8,128)}, u32[]{:S(2)}, u32[]{:S(2)}) collective-permute-start(f32[32,16,256]{2,1,0:T(8,128)} %get-tuple-element.24), channel_id=1, source_target_pairs={{0,30},{2,0},{4,2},{6,4},{8,6},{10,8},{12,10},{14,12},{16,14},{18,... | collective-permute-start | bytes 1572872 | tf_op jit(solution)/shard_map/ppermute | solution.py:395
  81.2 1.0 %copy-done.19 = bf16[2,512,256]{2,1,0:T(8,128)(2,1)S(1)} copy-done((bf16[2,512,256]{2,1,0:T(8,128)(2,1)S(1)}, bf16[2,512,256]{2,1,0:T(8,128)(2,1)}, u32[]{:S(2)}) %copy-start.19) | copy-done | bytes 524312
  82.2 1.0 %copy-done.20 = bf16[2,512,256]{2,1,0:T(8,128)(2,1)S(1)} copy-done((bf16[2,512,256]{2,1,0:T(8,128)(2,1)S(1)}, bf16[2,512,256]{2,1,0:T(8,128)(2,1)}, u32[]{:S(2)}) %copy-start.20) | copy-done | bytes 524312
  83.3 0.9 copy-done.22
  84.2 2.4 %inverse_modes.1.base = f32[32,64,256]{2,1,0:T(8,128)S(1)} custom-call(s32[1]{0:T(128)} %bitcast._, f32[16,16,128]{2,1,0:T(8,128)S(1)} %bitcast.34, f32[32,64,256]{2,1,0:T(8,128)S(1)} %pad_maximum_fusion.base, f32[32]{0:T(128)S(1)} %copy-done.18, bf16[2,128,512]{2,1,0:T(8,128)(2,1)S(1)} %copy-done.22, bf16[2,128,512]{2,1,0:T(8,128)(2,1)S(1)} %copy-done.21, ...), custom_call_target="tpu_custom_call" | custom-call | flops 2000000000 | bytes 6291456 | tf_op jit(solution)/shard_map/inverse_modes/pallas_call | solution.py:273
  86.6 2.0 %finished_rows.4.rest_0_ = f32[32,64,256]{2,1,0:T(8,128)} custom-call(f32[32,64,256]{2,1,0:T(8,128)S(1)} %inverse_modes.1.base, f32[32,16,256]{2,1,0:T(8,128)} %collective-permute-done.8.low, f32[32,16,256]{2,1,0:T(8,128)} %collective-permute-done.9.high), custom_call_target="tpu_custom_call" | custom-call | flops 1000000000 | bytes 2097152 | tf_op jit(solution)/shard_map/finished_rows/pallas_call | solution.py:329
  88.7 1.0 finished_rows.5.rest_0_
  89.7 6.6 %collective-permute-done.4.low = f32[32,16,256]{2,1,0:T(8,128)} collective-permute-done((f32[32,16,256]{2,1,0:T(8,128)}, f32[32,16,256]{2,1,0:T(8,128)}, u32[]{:S(2)}, u32[]{:S(2)}) %collective-permute-start.4) | collective-permute-done | bytes 524320 | tf_op jit(solution)/shard_map/ppermute | solution.py:394
  97.0 2.0 %finished_rows.6.rest_0_ = f32[32,64,256]{2,1,0:T(8,128)} custom-call(f32[32,64,256]{2,1,0:T(8,128)S(1)} %inverse_modes.1.base, f32[32,16,256]{2,1,0:T(8,128)} %collective-permute-done.4.low, f32[32,16,256]{2,1,0:T(8,128)} %collective-permute-done.5.high, f32[32,64,256]{2,1,0:T(8,128)} %finished_rows.5.rest_0_), custom_call_target="tpu_custom_call", output_to_operand_aliasing={{}: (3, {})} | custom-call | flops 1000000000 | bytes 2097152 | tf_op jit(solution)/shard_map/finished_rows/pallas_call | solution.py:329
  99.0 2.0 %finished_rows.7 = f32[32,64,256]{2,1,0:T(8,128)} custom-call(f32[32,64,256]{2,1,0:T(8,128)S(1)} %inverse_modes.1.base, f32[32,16,256]{2,1,0:T(8,128)} %collective-permute-done.2.low, f32[32,16,256]{2,1,0:T(8,128)} %collective-permute-done.3.high, f32[32,64,256]{2,1,0:T(8,128)} %finished_rows.6.rest_0_), custom_call_target="tpu_custom_call", output_to_operand_aliasing={{}: (3, {})} | custom-call | flops 1000000000 | bytes 2097152 | tf_op jit(solution)/shard_map/finished_rows/pallas_call | solution.py:329
  (76 shorter events, 12.3 us)
Async XLA Ops:
  0.0 1.6 %copy-start = (f32[32,1,64,256]{3,2,1,0:T(8,128)S(1)}, f32[32,1,64,256]{3,2,1,0:T(8,128)}, u32[]{:S(2)}) copy-start(f32[32,1,64,256]{3,2,1,0:T(8,128)} %param.17) | copy-start | bytes 6291460
  1.6 0.9 copy-start.23
  2.5 0.9 copy-start.24
  3.5 0.9 copy-start.25
  5.3 10.0 %copy-start.28 = (f32[32,27]{1,0:T(8,128)S(1)}, f32[32,27]{1,0:T(8,128)}, u32[]{:S(2)}) copy-start(f32[32,27]{1,0:T(8,128)} %param.19) | copy-start | bytes 10372
  5.3 10.1 %copy-start.1 = (f32[32,1,64,256]{3,2,1,0:T(8,128)S(1)}, f32[32,1,64,256]{3,2,1,0:T(8,128)}, u32[]{:S(2)}) copy-start(f32[32,1,64,256]{3,2,1,0:T(8,128)} %param.17) | copy-start | bytes 6291460
  5.3 10.1 %copy-start.15 = (f32[32,32]{1,0:T(8,128)S(1)}, f32[32,32]{1,0:T(8,128)}, u32[]{:S(2)}) copy-start(f32[32,32]{1,0:T(8,128)} %point.7) | copy-start | bytes 12292
  8.2 46.9 %all-to-all-start = ((f32[32,8,128]{2,1,0:T(8,128)}), f32[32,8,128]{2,1,0:T(8,128)S(1)}, u32[]{:S(2)}, u32[]{:S(2)}) async-start(f32[32,8,128]{2,1,0:T(8,128)} %bitcast.3), calls=%async_computation | async-start | bytes 262144 | tf_op jit(solution)/shard_map/all_to_all | solution.py:403
  24.0 52.9 %collective-permute-start.6 = (f32[32,16,256]{2,1,0:T(8,128)}, f32[32,16,256]{2,1,0:T(8,128)S(1)}, u32[]{:S(2)}, u32[]{:S(2)}) collective-permute-start(f32[32,16,256]{2,1,0:T(8,128)} %get-tuple-element.25), channel_id=1, source_target_pairs={{0,2},{2,4},{4,6},{6,8},{8,10},{10,12},{12,14},{14,16},{16,18},{18... | collective-permute-start | bytes 1572872 | tf_op jit(solution)/shard_map/ppermute | solution.py:394
  25.6 63.1 %collective-permute-start.7 = (f32[32,16,256]{2,1,0:T(8,128)}, f32[32,16,256]{2,1,0:T(8,128)S(1)}, u32[]{:S(2)}, u32[]{:S(2)}) collective-permute-start(f32[32,16,256]{2,1,0:T(8,128)} %get-tuple-element.26), channel_id=1, source_target_pairs={{0,30},{2,0},{4,2},{6,4},{8,6},{10,8},{12,10},{14,12},{16,14},{18,... | collective-permute-start | bytes 1572872 | tf_op jit(solution)/shard_map/ppermute | solution.py:395
  33.3 4.3 %copy-start.4 = (f32[32,16,256]{2,1,0:T(8,128)}, f32[32,16,256]{2,1,0:T(8,128)S(1)}, u32[]{:S(2)}) copy-start(f32[32,16,256]{2,1,0:T(8,128)S(1)} %get-tuple-element.18) | copy-start | bytes 1572868
  33.3 43.5 %collective-permute-start.8 = (f32[32,16,256]{2,1,0:T(8,128)}, f32[32,16,256]{2,1,0:T(8,128)}, u32[]{:S(2)}, u32[]{:S(2)}) collective-permute-start(f32[32,16,256]{2,1,0:T(8,128)} %get-tuple-element.27), channel_id=1, source_target_pairs={{0,2},{2,4},{4,6},{6,8},{8,10},{10,12},{12,14},{14,16},{16,18},{18... | collective-permute-start | bytes 1572872 | tf_op jit(solution)/shard_map/ppermute | solution.py:394
  35.1 4.7 %copy-start.27 = (f32[2,16,8,64]{3,2,1,0:T(8,128)S(1)}, f32[2,16,8,64]{3,2,1,0:T(8,128)}, u32[]{:S(2)}) copy-start(f32[2,16,8,64]{3,2,1,0:T(8,128)} %param.18) | copy-start | bytes 196612
  35.1 43.5 %collective-permute-start.9 = (f32[32,16,256]{2,1,0:T(8,128)}, f32[32,16,256]{2,1,0:T(8,128)}, u32[]{:S(2)}, u32[]{:S(2)}) collective-permute-start(f32[32,16,256]{2,1,0:T(8,128)} %get-tuple-element.28), channel_id=1, source_target_pairs={{0,30},{2,0},{4,2},{6,4},{8,6},{10,8},{12,10},{14,12},{16,14},{18,... | collective-permute-start | bytes 1572872 | tf_op jit(solution)/shard_map/ppermute | solution.py:395
  38.3 5.3 %collective-permute-start.1 = (f32[32,256]{1,0:T(8,128)}, f32[32,256]{1,0:T(8,128)S(1)}, u32[]{:S(2)}, u32[]{:S(2)}) collective-permute-start(f32[32,256]{1,0:T(8,128)} %get-tuple-element.30), channel_id=1, source_target_pairs={{0,1},{1,0},{2,3},{3,2},{4,5},{5,4},{6,7},{7,6},{8,9},{9,8},{10,11... | collective-permute-start | bytes 98312 | tf_op jit(solution)/shard_map/ppermute | solution.py:383
  44.3 10.8 %copy-start.8 = (bf16[512,128]{1,0:T(8,128)(2,1)S(1)}, bf16[512,128]{1,0:T(8,128)(2,1)}, u32[]{:S(2)}) copy-start(bf16[512,128]{1,0:T(8,128)(2,1)} %constant.35.clone.i_rest) | copy-start | bytes 393220
  44.3 22.2 %collective-permute-start = (f32[32,256]{1,0:T(8,128)}, f32[32,256]{1,0:T(8,128)}, u32[]{:S(2)}, u32[]{:S(2)}) collective-permute-start(f32[32,256]{1,0:T(8,128)} %get-tuple-element.29), channel_id=1, source_target_pairs={{0,1},{1,0},{2,3},{3,2},{4,5},{5,4},{6,7},{7,6},{8,9},{9,8},{10,11... | collective-permute-start | bytes 98312 | tf_op jit(solution)/shard_map/ppermute | solution.py:382
  55.1 0.9 copy-start.9
  56.0 0.9 copy-start.10
  56.9 0.9 copy-start.11
  59.4 21.1 %all-to-all-start.1 = ((f32[32,8,128]{2,1,0:T(8,128)}), f32[32,8,128]{2,1,0:T(8,128)S(1)}, u32[]{:S(2)}, u32[]{:S(2)}) async-start(f32[32,8,128]{2,1,0:T(8,128)} %bitcast.7), calls=%async_computation.1 | async-start | bytes 262144 | tf_op jit(solution)/shard_map/all_to_all | solution.py:405
  66.5 13.7 %copy-start.3 = (f32[32,16,256]{2,1,0:T(8,128)S(1)}, f32[32,16,256]{2,1,0:T(8,128)}, u32[]{:S(2)}) copy-start(f32[32,16,256]{2,1,0:T(8,128)} %copy-done.2) | copy-start | bytes 1572868
  66.5 13.7 %copy-start.5 = (f32[32,16,256]{2,1,0:T(8,128)S(1)}, f32[32,16,256]{2,1,0:T(8,128)}, u32[]{:S(2)}) copy-start(f32[32,16,256]{2,1,0:T(8,128)} %copy-done.4) | copy-start | bytes 1572868
  66.5 13.7 %copy-start.7 = (f32[32,16,256]{2,1,0:T(8,128)S(1)}, f32[32,16,256]{2,1,0:T(8,128)}, u32[]{:S(2)}) copy-start(f32[32,16,256]{2,1,0:T(8,128)} %copy-done.6) | copy-start | bytes 1572868
  66.5 32.5 %collective-permute-start.2 = (f32[32,16,256]{2,1,0:T(8,128)}, f32[32,16,256]{2,1,0:T(8,128)}, u32[]{:S(2)}, u32[]{:S(2)}) collective-permute-start(f32[32,16,256]{2,1,0:T(8,128)} %copy-done.12), channel_id=1, source_target_pairs={{0,2},{2,4},{4,6},{6,8},{8,10},{10,12},{12,14},{14,16},{16,18},{18... | collective-permute-start | bytes 1572872 | tf_op jit(solution)/shard_map/ppermute | solution.py:394
  76.9 22.2 %collective-permute-start.3 = (f32[32,16,256]{2,1,0:T(8,128)}, f32[32,16,256]{2,1,0:T(8,128)}, u32[]{:S(2)}, u32[]{:S(2)}) collective-permute-start(f32[32,16,256]{2,1,0:T(8,128)} %get-tuple-element.22), channel_id=1, source_target_pairs={{0,30},{2,0},{4,2},{6,4},{8,6},{10,8},{12,10},{14,12},{16,14},{18,... | collective-permute-start | bytes 1572872 | tf_op jit(solution)/shard_map/ppermute | solution.py:395
  76.9 19.4 %collective-permute-start.4 = (f32[32,16,256]{2,1,0:T(8,128)}, f32[32,16,256]{2,1,0:T(8,128)}, u32[]{:S(2)}, u32[]{:S(2)}) collective-permute-start(f32[32,16,256]{2,1,0:T(8,128)} %get-tuple-element.23), channel_id=1, source_target_pairs={{0,2},{2,4},{4,6},{6,8},{8,10},{10,12},{12,14},{14,16},{16,18},{18... | collective-permute-start | bytes 1572872 | tf_op jit(solution)/shard_map/ppermute | solution.py:394
  78.6 18.4 %collective-permute-start.5 = (f32[32,16,256]{2,1,0:T(8,128)}, f32[32,16,256]{2,1,0:T(8,128)}, u32[]{:S(2)}, u32[]{:S(2)}) collective-permute-start(f32[32,16,256]{2,1,0:T(8,128)} %get-tuple-element.24), channel_id=1, source_target_pairs={{0,30},{2,0},{4,2},{6,4},{8,6},{10,8},{12,10},{14,12},{16,14},{18,... | collective-permute-start | bytes 1572872 | tf_op jit(solution)/shard_map/ppermute | solution.py:395
  80.2 1.0 copy-start.21
  81.2 1.0 %copy-start.19 = (bf16[2,512,256]{2,1,0:T(8,128)(2,1)S(1)}, bf16[2,512,256]{2,1,0:T(8,128)(2,1)}, u32[]{:S(2)}) copy-start(bf16[2,512,256]{2,1,0:T(8,128)(2,1)} %constant.39.clone.y_rest) | copy-start | bytes 1572868
  82.2 1.0 %copy-start.20 = (bf16[2,512,256]{2,1,0:T(8,128)(2,1)S(1)}, bf16[2,512,256]{2,1,0:T(8,128)(2,1)}, u32[]{:S(2)}) copy-start(bf16[2,512,256]{2,1,0:T(8,128)(2,1)} %constant.38.clone.y_top) | copy-start | bytes 1572868
  83.3 0.9 copy-start.22
  (9 other events, 6.8 us)
where the time goes:
time: 102 us; the launch traced here: 101 us
  Pallas kernels  44.9 us (44%)
  starting transfers between devices  25.5 us (25%)
  local copies, waits for them, and re-layouts  22 us (22%)
  waiting for transfers between devices  7.39 us (7%)
    pallas_call x4, Pallas kernels, conv_call(): pl.pallas_call(functools.partial(conv_kernel, top_tile, bottom_tile), out...  31.1 us
    unnamed x59, local copies, waits for them, and re-layouts  18.3 us
    all_to_all x1, starting transfers between devices, body(): got = lax.all_to_all(sent, both, split_axis=0, concat_axis=0, tiled=True)  7.1 us
    all_to_all x1, starting transfers between devices, body(): back = lax.all_to_all(out, both, split_axis=0, concat_axis=0, tiled=True)  7.08 us
    pallas_call x4, Pallas kernels, finish_call(): pl.pallas_call(functools.partial(finish_kernel, bool(alias)), out_shape=j...  7 us
    ppermute x4, starting transfers between devices, body(): lax.ppermute(down, 'gz', ring('gz', gz, 1))  6.83 us
    ppermute x4, waiting for transfers between devices, body(): lax.ppermute(down, 'gz', ring('gz', gz, 1))  6.65 us
    ppermute x4, starting transfers between devices, body(): lax.ppermute(up, 'gz', ring('gz', gz, -1))  2.98 us
  transfers between devices with their start and end apart: 12, of which 2 were waited for; matrix products, arithmetic and copies ran while one was open for 6% of the time, Pallas kernels for 40%

commit v1 on v0

--- a/solution.py
+++ b/solution.py
@@ -15,7 +15,7 @@
 MY = 16
 MZ = 16
 CH = 32
-VMEM_BYTES = 40 * 1024 * 1024
+VMEM_BYTES = 58 * 1024 * 1024
 BF = jnp.bfloat16
 F32 = jnp.float32
 
@@ -100,10 +100,12 @@
 
 
 def dot3(a, b):
-    return dot(a[0], b[0]) + (dot(a[0], b[1]) + dot(a[1], b[0]))
-
-
-def forward_kernel(group, _, field, y_top, y_rest, x_top, x_rest, out):
+    rows = a[0].shape[0]
+    both = dot(jnp.concatenate([a[0], a[1]], axis=0), b[0])
+    return both[:rows] + (both[rows:] + dot(a[0], b[1]))
+
+
+def forward_kernel(group, _, field, y_top, y_rest, x_top, x_rest, out, edges):
     y_table = (y_top[0], y_rest[0])
     half = group * MY
     total = jnp.zeros((half, 4 * MX), F32)
@@ -114,6 +116,10 @@
             piece = parts(turned[t * half : (t + 1) * half])
             total = total + dot3(piece, (x_top[2 * p + t], x_rest[2 * p + t]))
     out[...] = total.reshape(group, MY, 4 * MX)
+    last = field.shape[1] - 1
+    for i in range(2 * group):
+        edges[0, i : i + 1, :] = field[i, last : last + 1, :]
+        edges[1, i : i + 1, :] = field[i, 0:1, :]
 
 
 def swap_parts(value):
@@ -122,66 +128,78 @@
     return jnp.where(is_real, pltpu.roll(value, 4 * MX - MX, 1), pltpu.roll(value, MX, 1)), is_real
 
 
-def filter_kernel(arrived, gain_same, gain_cross, f_top, f_rest, i_top, i_rest, out):
+def filter_kernel(arrived, gains, f_top, f_rest, i_top, i_rest, out):
+    real, imag = (gains[r].reshape(-1, 2 * MX) for r in range(2))
+    first, second = slice(0, MX), slice(MX, 2 * MX)
+    same = jnp.concatenate([real[:, first], real[:, first], real[:, second], real[:, second]], axis=1)
+    cross = jnp.concatenate([-imag[:, first], imag[:, first], -imag[:, second], imag[:, second]], axis=1)
     half = f_top.shape[0] // 2
     turned = dot3((f_top[...], f_rest[...]), parts(arrived[...]))
     crossed, is_real = swap_parts(turned[half:])
     modes = turned[:half] + jnp.where(is_real, crossed, -crossed)
     crossed, _ = swap_parts(modes)
-    filtered = modes * gain_same[...] + crossed * gain_cross[...]
+    filtered = modes * same + crossed * cross
     half = i_top.shape[0] // 2
     back = dot3((i_top[...], i_rest[...]), parts(filtered))
     crossed, is_real = swap_parts(back[half:])
     out[...] = back[:half] + jnp.where(is_real, -crossed, crossed)
 
 
-def inverse_kernel(group, _, modes, base, bias, x_top, x_rest, y_top, y_rest, out):
-    step = pl.program_id(0)
-    y_table = (y_top[0], y_rest[0])
-    rows = parts(modes[...].reshape(group * MY, 4 * MX))
-    y_local = out.shape[1]
-    for p in range(2):
-        wide = dot3(rows, (x_top[p], x_rest[p]))
-        tall = jnp.concatenate([wide[:, :NX], wide[:, NX:]], axis=0)
-        planes = dot3(y_table, parts(tall)).reshape(group, y_local, NX)
-        for i in range(group):
-            c = 2 * i + p
-            out[c] = planes[i] + (base[c] + bias[step * 2 * group + c])
-
-
-def conv_kernel(top_tile, bottom_tile, weight, point, main, above, below, down, mid, up, shifted, depth):
-    rows = main.shape[1]
-
-    def load(c, _):
-        if top_tile:
-            first = above[c, 7:8, :]
-        else:
-            first = above[pl.ds(c, 1), :]
-        if bottom_tile:
-            last = below[c, 0:1, :]
-        else:
-            last = below[pl.ds(c, 1), :]
-        centre = main[c]
-        for e, turn in ((0, 1), (1, 0), (2, NX - 1)):
-            for place, value in ((pl.ds(7, 1), first), (pl.ds(8, rows), centre), (pl.ds(8 + rows, 1), last)):
-                shifted[e, c, place, :] = pltpu.roll(value, turn, 1) if turn else value
+def conv_kernel(inner, rows, weight, point, *refs):
+    if inner:
+        above, first, second, below = refs[:4]
+        segments = ((8, 2 * rows, 0),)
+        blocks = ((above, 0, 8), (first, 8, rows), (second, 8 + rows, rows), (below, 8 + 2 * rows, 8))
+        refs = refs[4:]
+    else:
+        halo, first, below, above, second = refs[:5]
+        start = rows + 24
+        segments = ((8, rows, 0), (start, rows, rows))
+        blocks = ((first, 8, rows), (below, 8 + rows, 8), (above, start - 8, 8), (second, start, rows))
+        refs = refs[5:]
+    outs, (shifted, depth) = refs[:3], refs[3:]
+    turns = (1, 0, NX - 1)
+    step = 8
+
+    def load(i, _):
+        c = pl.multiple_of(i * step, step)
+        for ref, at, count in blocks:
+            value = ref[pl.ds(c, step)].reshape(step * count, NX)
+            for e, turn in enumerate(turns):
+                moved = pltpu.roll(value, turn, 1) if turn else value
+                for h in range(2):
+                    shifted[e, h, pl.ds(c, step), pl.ds(at, count), :] = moved[
+                        :, 128 * h : 128 * h + 128
+                    ].reshape(step, count, 128)
         return 0
 
-    lax.fori_loop(0, CH, load, 0)
+    lax.fori_loop(0, CH // step, load, 0)
+    if not inner:
+        for side, at in ((0, 7), (1, start + rows)):
+            value = halo[side]
+            for e, turn in enumerate(turns):
+                moved = pltpu.roll(value, turn, 1) if turn else value
+                for h in range(2):
+                    shifted[e, h, :, pl.ds(at, 1), :] = moved[:, 128 * h : 128 * h + 128].reshape(CH, 1, 128)
 
     def taps(c, _):
-        sums = [None, None, None]
-        for e in range(3):
-            for b in range(3):
-                value = shifted[e, c, pl.ds(7 + b, rows), :]
-                for a in range(3):
-                    term = weight[c * 27 + a * 9 + b * 3 + e] * value
-                    sums[a] = term if sums[a] is None else sums[a] + term
-        for a in range(3):
-            depth[a, c] = sums[a]
+        gain = [weight[c, k] for k in range(27)]
+        for at, count, to in segments:
+            for h in range(2):
+                for part in range(0, count, 16):
+                    size = min(16, count - part)
+                    sums = [None, None, None]
+                    for e in range(3):
+                        for b in range(3):
+                            value = shifted[e, h, c, pl.ds(at + part + b - 1, size), :]
+                            for a in range(3):
+                                term = gain[a * 9 + b * 3 + e] * value
+                                sums[a] = term if sums[a] is None else sums[a] + term
+                    for a in range(3):
+                        depth[a, c, pl.ds(to + part, size), pl.ds(128 * h, 128)] = sums[a]
         return 0
 
-    lax.fori_loop(0, CH, taps, 0)
+    lax.fori_loop(0, CH, taps, 0, unroll=2)
 
     spread = (
         lax.broadcasted_iota(jnp.int32, (8 * CH, CH), 0) // 8
@@ -199,16 +217,36 @@
         jnp.where(same, dot(dot(spread, part).astype(BF), gather), 0.0).astype(BF)
         for part in parts(point[...])
     )
-    for a, out in ((0, down), (1, mid), (2, up)):
-        for t in range(rows // 8):
+    for t in range(2 * rows // 8):
+        for a, out in enumerate(outs):
             tile = depth[a, :, pl.ds(8 * t, 8), :].reshape(8 * CH, NX)
             out[:, pl.ds(8 * t, 8), :] = dot3(mix, parts(tile)).reshape(CH, 8, NX)
 
 
-def finish_kernel(aliased, base, low, high, *rest):
-    out = rest[-1]
-    total = base[...] + (low[...] + high[...])
-    out[...] = 0.5 * total * (1.0 + lax.erf(total * (1.0 / math.sqrt(2.0))))
+def gelu(value):
+    return 0.5 * value * (1.0 + lax.erf(value * (1.0 / math.sqrt(2.0))))
+
+
+def inverse_kernel(group, _, modes, inner, outer, low, high, bias, x_top, x_rest, y_top, y_rest, out):
+    step = pl.program_id(0)
+    y_table = (y_top[0], y_rest[0])
+    mode_rows = parts(modes[...].reshape(group * MY, 4 * MX))
+    y_local = out.shape[1]
+    rows = y_local // 4
+    for p in range(2):
+        wide = dot3(mode_rows, (x_top[p], x_rest[p]))
+        tall = jnp.concatenate([wide[:, :NX], wide[:, NX:]], axis=0)
+        planes = dot3(y_table, parts(tall)).reshape(group, y_local, NX)
+        for i in range(group):
+            c = 2 * i + p
+            plane = planes[i] + bias[step * 2 * group + c]
+            out[c, :rows] = plane[:rows] + outer[c, :rows]
+            out[c, 3 * rows :] = plane[3 * rows :] + outer[c, rows:]
+            out[c, rows : 3 * rows] = gelu(plane[rows : 3 * rows] + (inner[c] + (low[c] + high[c])))
+
+
+def finish_kernel(base, low, high, out):
+    out[...] = gelu(base[...] + (low[...] + high[...]))
 
 
 def params():
@@ -229,7 +267,10 @@
     x_spec = pl.BlockSpec((4, NX, 4 * MX), lambda i, s: (0, 0, 0))
     return pl.pallas_call(
         functools.partial(forward_kernel, group),
-        out_shape=jax.ShapeDtypeStruct((CH // 2, MY, 4 * MX), F32),
+        out_shape=[
+            jax.ShapeDtypeStruct((CH // 2, MY, 4 * MX), F32),
+            jax.ShapeDtypeStruct((2, CH, NX), F32),
+        ],
         grid_spec=pltpu.PrefetchScalarGridSpec(
             num_scalar_prefetch=1,
             grid=(CH // 2 // group,),
@@ -237,7 +278,10 @@
                 pl.BlockSpec((2 * group, y_local, NX), lambda i, s: (i, 0, 0)),
                 y_spec, y_spec, x_spec, x_spec,
             ],
-            out_specs=pl.BlockSpec((group, MY, 4 * MX), lambda i, s: (i, 0, 0)),
+            out_specs=[
+                pl.BlockSpec((group, MY, 4 * MX), lambda i, s: (i, 0, 0)),
+                pl.BlockSpec((2, 2 * group, NX), lambda i, s: (0, i, 0)),
+            ],
         ),
         compiler_params=params(),
         cost_estimate=cost(2 * 10**9, 4 * 2**20),
@@ -246,97 +290,93 @@
 
 
 def filter_call(arrived, gains, gz, gy, scale):
-    rows = gains.shape[2]
-    fwd, inv = z_tables(gz, gy, rows, scale)
+    fwd, inv = z_tables(gz, gy, gains.shape[2], scale)
     fwd, inv = halves(fwd), halves(inv)
-    split = gains.reshape(2, MZ * rows, 2, 1, MX)
-    same = jnp.concatenate([split[0], split[0]], axis=2).reshape(MZ * rows, 4 * MX)
-    cross = jnp.concatenate([-split[1], split[1]], axis=2).reshape(MZ * rows, 4 * MX)
     return pl.pallas_call(
         filter_kernel,
         out_shape=jax.ShapeDtypeStruct(arrived.shape, F32),
         compiler_params=params(),
         cost_estimate=cost(2 * 10**8, 2**20),
         name="filter_modes",
-    )(arrived, same, cross, *fwd, *inv)
-
-
-def inverse_call(modes, base, bias, place, gy, scale):
-    y_local = base.shape[1]
+    )(arrived, gains, *fwd, *inv)
+
+
+def inverse_call(modes, inner, outer, low, high, bias, place, gy, scale):
+    y_local = 2 * inner.shape[1]
     group = 8
     x_tab = halves(x_inverse_table(scale))
     y_tab = halves(y_inverse_table(y_local, gy, group))
     tall, wide = y_tab[0].shape[1:]
     y_spec = pl.BlockSpec((1, tall, wide), lambda i, s: (s[0], 0, 0))
     x_spec = pl.BlockSpec((2, 4 * MX, 2 * NX), lambda i, s: (0, 0, 0))
-    plane = pl.BlockSpec((2 * group, y_local, NX), lambda i, s: (i, 0, 0))
+    half = pl.BlockSpec((2 * group, y_local // 2, NX), lambda i, s: (i, 0, 0))
     return pl.pallas_call(
         functools.partial(inverse_kernel, group),
-        out_shape=jax.ShapeDtypeStruct(base.shape, F32),
+        out_shape=jax.ShapeDtypeStruct((CH, y_local, NX), F32),
         grid_spec=pltpu.PrefetchScalarGridSpec(
             num_scalar_prefetch=1,
             grid=(CH // 2 // group,),
             in_specs=[
                 pl.BlockSpec((group, MY, 4 * MX), lambda i, s: (i, 0, 0)),
-                plane,
+                half, half, half, half,
                 pl.BlockSpec(memory_space=pltpu.SMEM),
                 x_spec, x_spec, y_spec, y_spec,
             ],
-            out_specs=plane,
+            out_specs=pl.BlockSpec((2 * group, y_local, NX), lambda i, s: (i, 0, 0)),
         ),
         compiler_params=params(),
-        cost_estimate=cost(2 * 10**9, 6 * 2**20),
+        cost_estimate=cost(4 * 10**9, 6 * 2**20),
         name="inverse_modes",
-    )(place, modes, base, bias, *x_tab, *y_tab)
-
-
-def conv_call(field, above, below, weight, point, start, rows):
-    y_local = field.shape[1]
-    top_tile, bottom_tile = start > 0, start + rows < y_local
-    whole = pl.BlockSpec((CH, rows, NX), lambda i: (0, 0, 0))
-    edge = pl.BlockSpec((CH, NX), lambda i: (0, 0))
+    )(place, modes, inner, outer, low, high, bias, *x_tab, *y_tab)
+
+
+def conv_call(field, halo, weight, point, inner):
+    rows = field.shape[1] // 4
     tile = lambda at: pl.BlockSpec((CH, 8, NX), lambda i: (0, at, 0))
+    quarter = lambda at: pl.BlockSpec((CH, rows, NX), lambda i: (0, at, 0))
+    first, last = rows // 8, 3 * rows // 8
+    if inner:
+        specs = [tile(first - 1), quarter(1), quarter(2), tile(last)]
+        operands = [field] * 4
+    else:
+        specs = [pl.BlockSpec((2, CH, NX), lambda i: (0, 0, 0)), quarter(0), tile(first), tile(last - 1), quarter(3)]
+        operands = [halo] + [field] * 4
     return pl.pallas_call(
-        functools.partial(conv_kernel, top_tile, bottom_tile),
-        out_shape=[jax.ShapeDtypeStruct((CH, rows, NX), F32)] * 3,
+        functools.partial(conv_kernel, inner, rows),
+        out_shape=[jax.ShapeDtypeStruct((CH, 2 * rows, NX), F32)] * 3,
         grid=(1,),
         in_specs=[
             pl.BlockSpec(memory_space=pltpu.SMEM),
             pl.BlockSpec((CH, CH), lambda i: (0, 0)),
-            pl.BlockSpec((CH, rows, NX), lambda i: (0, start // rows, 0)),
-            tile(start // 8 - 1) if top_tile else edge,
-            tile((start + rows) // 8) if bottom_tile else edge,
+            *specs,
         ],
-        out_specs=[whole] * 3,
+        out_specs=[pl.BlockSpec((CH, 2 * rows, NX), lambda i: (0, 0, 0))] * 3,
         scratch_shapes=[
-            pltpu.VMEM((3, CH, rows + 16, NX), F32),
-            pltpu.VMEM((3, CH, rows, NX), F32),
+            pltpu.VMEM((3, 2, CH, 2 * rows + 32, 128), F32),
+            pltpu.VMEM((3, CH, 2 * rows, NX), F32),
         ],
         compiler_params=params(),
         cost_estimate=cost(2 * 10**9, 4 * 2**20),
         name="mixed_planes",
-    )(weight, point, field, field if top_tile else above, field if bottom_tile else below)
-
-
-def finish_call(base, low, high, so_far, start, rows):
-    block = pl.BlockSpec((CH, 8, NX), lambda i: (0, start // 8 + i, 0))
+    )(weight, point, *operands)
+
+
+def finish_call(result, low, high):
+    rows = result.shape[1] // 4
+    tiles = rows // 8
+    block = pl.BlockSpec((CH, 8, NX), lambda i: (0, i + (i // tiles) * 2 * tiles, 0))
     piece = pl.BlockSpec((CH, 8, NX), lambda i: (0, i, 0))
-    operands, specs, alias = [base, low, high], [block, piece, piece], {}
-    if so_far is not None:
-        operands.append(so_far)
-        specs.append(pl.BlockSpec(memory_space=pl.ANY))
-        alias = {3: 0}
     return pl.pallas_call(
-        functools.partial(finish_kernel, bool(alias)),
-        out_shape=jax.ShapeDtypeStruct(base.shape, F32),
-        grid=(rows // 8,),
-        in_specs=specs,
+        finish_kernel,
+        out_shape=jax.ShapeDtypeStruct(result.shape, F32),
+        grid=(2 * tiles,),
+        in_specs=[block, piece, piece],
         out_specs=block,
-        input_output_aliases=alias,
+        input_output_aliases={0: 0},
         compiler_params=params(),
-        cost_estimate=cost(10**9, 4 * rows * CH * NX * 4),
+        cost_estimate=cost(10**9, 4 * 2 * rows * CH * NX * 4),
         name="finished_rows",
-    )(*operands)
+    )(result, low, high)
 
 
 def general_filter(coarse, gains, gz, gy, scale):
@@ -371,7 +411,6 @@
     y_local = field.shape[2]
     place = lax.axis_index("gy").astype(jnp.int32).reshape(1)
     field = field.reshape(CH, y_local, NX)
-    weight = depth_weight.reshape(-1)
     y_total = gy * y_local
     forward_scale = 1.0 / math.sqrt(float(NX) * y_total * gz)
     inverse_scale = 1.0 / math.sqrt(2.0 * MX * MY * MZ)
@@ -379,23 +418,28 @@
     def ring(axis, count, by):
         return [(i, (i + by) % count) for i in range(count)]
 
-    above = lax.ppermute(field[:, y_local - 1, :], "gy", ring("gy", gy, 1))
-    below = lax.ppermute(field[:, 0, :], "gy", ring("gy", gy, -1))
-
-    rows = max(8, y_local // 4)
-    starts = list(range(0, y_local, rows))
-    order = sorted(starts, key=lambda s: (s == 0 or s + rows == y_local, s))
-    pieces = {}
-    mids = {}
-    for start in order:
-        down, mid, up = conv_call(field, above, below, weight, point_weight, start, rows)
-        mids[start] = mid
-        pieces[start] = (
+    def to_neighbours(down, up):
+        return (
             lax.ppermute(down, "gz", ring("gz", gz, 1)),
             lax.ppermute(up, "gz", ring("gz", gz, -1)),
         )
 
-    coarse = forward_call(field, place, gy)
+    down, inner, up = conv_call(field, None, depth_weight, point_weight, True)
+    inner_low, inner_high = to_neighbours(down, up)
+    field, _ = lax.optimization_barrier((field, down))
+    coarse, edges = forward_call(field, place, gy)
+    if gy == 2:
+        halo = lax.ppermute(edges, "gy", ring("gy", gy, 1))
+    else:
+        halo = jnp.stack(
+            [
+                lax.ppermute(edges[0], "gy", ring("gy", gy, 1)),
+                lax.ppermute(edges[1], "gy", ring("gy", gy, -1)),
+            ]
+        )
+    down, outer, up = conv_call(field, halo, depth_weight, point_weight, False)
+    outer_low, outer_high = to_neighbours(down, up)
+
     j_own, n_own = spectral_filter.shape[2], spectral_filter.shape[3]
     if j_own == 8 and n_own == 2 * MX:
         both = ("gz", "gy")
@@ -407,11 +451,10 @@
     else:
         back = general_filter(coarse, spectral_filter, gz, gy, forward_scale)
 
-    base = jnp.concatenate([mids[s] for s in starts], axis=1)
-    base = inverse_call(back, base, bias_vector, place, gy, inverse_scale)
-    result = None
-    for start in order:
-        result = finish_call(base, *pieces[start], result, start, rows)
+    result = inverse_call(
+        back, inner, outer, inner_low, inner_high, bias_vector, place, gy, inverse_scale
+    )
+    result = finish_call(result, outer_low, outer_high)
     return result.reshape(CH, 1, y_local, NX)
 
 

time: 102 us -> 88.6 us (0.87)
  blocking collectives: 0 us -> 41.6 us
  local copies, waits for them, and re-layouts: 22 us -> 3.9 us
  starting transfers between devices: 25.5 us -> 7.89 us
  Pallas kernels: 44.9 us -> 31.7 us
  waiting for transfers between devices: 7.39 us -> 2.13 us
    all_to_all x0 -> x2, blocking collectives: none -> 41.6 us  [the longest x1 27.3 us: body(): got = lax.all_to_all(sent, both, split_axis=0, concat_axis=0, tiled=True)]
    pallas_call x9 -> x4, Pallas kernels: 41 us -> 23.9 us  [the longest x2 15.5 us: conv_call(): pl.pallas_call(functools.partial(conv_kernel, inner, rows), out_shape=[ja...]
    unnamed x59 -> x12, local copies, waits for them, and re-layouts: 18.3 us -> 3.9 us
    all_to_all x2 -> x0, starting transfers between devices: 14.2 us -> none  [the longest x1 7.1 us: body(): got = lax.all_to_all(sent, both, split_axis=0, concat_axis=0, tiled=True)]
    ppermute x10 -> x5, waiting for transfers between devices: 7.39 us -> 2.13 us  [the longest x1 2.11 us: body(): halo = lax.ppermute(edges, 'gy', ring('gy', gy, 1))]
    ppermute x10 -> x5, starting transfers between devices: 11.3 us -> 7.89 us  [the longest x2 4.23 us: to_neighbours(): lax.ppermute(down, 'gz', ring('gz', gz, 1))]
    pallas_call x1, Pallas kernels: 2.41 us -> 5.06 us  [inverse_call(): pl.pallas_call(functools.partial(inverse_kernel, group), out_shape=jax.Sh...]
    squeeze x5 -> x0, local copies, waits for them, and re-layouts: 1.85 us -> none  [the longest x2 1.03 us: filter_call(): split[1]]
  transfers between devices with their start and end apart: 12 -> 5, of which waited for: 2 -> 1; matrix products, arithmetic and copies ran while one was open for 6% -> 0% of each run, Pallas kernels for 40% -> 23%
where the time goes in v1:
time: 88.6 us; the launch traced here: 87.3 us
  blocking collectives  41.6 us (47%)
  Pallas kernels  31.7 us (36%)
  starting transfers between devices  7.89 us (9%)
  local copies, waits for them, and re-layouts  3.9 us (4%)
  waiting for transfers between devices  2.13 us (2%)
    all_to_all x1, blocking collectives, body(): got = lax.all_to_all(sent, both, split_axis=0, concat_axis=0, tiled=True)  27.3 us
    pallas_call x2, Pallas kernels, conv_call(): pl.pallas_call(functools.partial(conv_kernel, inner, rows), out_shape=[ja...  15.5 us
    all_to_all x1, blocking collectives, body(): back = lax.all_to_all(out, both, split_axis=0, concat_axis=0, tiled=True)  14.3 us
    pallas_call x1, Pallas kernels, inverse_call(): pl.pallas_call(functools.partial(inverse_kernel, group), out_shape=jax.Sh...  5.06 us
    pallas_call x1, Pallas kernels, forward_call(): pl.pallas_call(functools.partial(forward_kernel, group), out_shape=[jax.S...  4.61 us
    ppermute x2, starting transfers between devices, to_neighbours(): lax.ppermute(down, 'gz', ring('gz', gz, 1))  4.23 us
    unnamed x12, local copies, waits for them, and re-layouts  3.9 us
    pallas_call x1, Pallas kernels, finish_call(): pl.pallas_call(finish_kernel, out_shape=jax.ShapeDtypeStruct(result.shape...  3.83 us
  transfers between devices with their start and end apart: 5, of which 1 were waited for; matrix products, arithmetic and copies ran while one was open for 0% of the time, Pallas kernels for 23%

profile of v1, /device:TPU:1, one launch (start us, length us, event | category | flops | bytes accessed | tf_op | source)
XLA Modules:
  0.0 87.3 jit_solution(6046088021556337015)
XLA Ops:
  0.0 7.6 %mixed_planes.2 = (f32[32,32,256]{2,1,0:T(8,128)}, f32[32,32,256]{2,1,0:T(8,128)}, f32[32,32,256]{2,1,0:T(8,128)}) custom-call(f32[32,27]{1,0:T(8,128)} %weight.3, f32[32,32]{1,0:T(8,128)} %point.3, f32[32,64,256]{2,1,0:T(8,128)} %bitcast.9, f32[32,64,256]{2,1,0:T(8,128)} %bitcast.10, f32[32,64,256]{2,1,0:T(8,128)} %bitcast.11, f32[32,64,256]{2,1,0:T(8,128)} %bitcast.12), custom_call_target="tpu_custom_call" | custom-call | flops 2000000000 | bytes 4194304 | tf_op jit(solution)/shard_map/mixed_planes/pallas_call | solution.py:344
  7.6 0.1 collective-permute-start.2
  7.7 2.6 %collective-permute-start.1 = (f32[32,32,256]{2,1,0:T(8,128)}, f32[32,32,256]{2,1,0:T(8,128)S(1)}, u32[]{:S(2)}, u32[]{:S(2)}) collective-permute-start(f32[32,32,256]{2,1,0:T(8,128)} %get-tuple-element.14), channel_id=1, source_target_pairs={{0,2},{2,4},{4,6},{6,8},{8,10},{10,12},{12,14},{14,16},{16,18},{18... | collective-permute-start | bytes 3145736 | tf_op jit(solution)/shard_map/ppermute | solution.py:423
  10.2 4.6 %forward_modes.1 = (f32[16,16,128]{2,1,0:T(8,128)}, f32[2,32,256]{2,1,0:T(8,128)}) custom-call(s32[1]{0:T(128)} %bitcast._, f32[32,64,256]{2,1,0:T(8,128)} %bitcast.13, bf16[2,128,256]{2,1,0:T(8,128)(2,1)} %constant.28.clone.y_top, bf16[2,128,256]{2,1,0:T(8,128)(2,1)} %constant.29.clone.y_rest, bf16[4,256,128]{2,1,0:T(8,128)(2,1)} %constant.30.clone.x_top, ...), custom_call_target="tpu_custom_call" | custom-call | flops 2000000000 | bytes 4194304 | tf_op jit(solution)/shard_map/forward_modes/pallas_call | solution.py:268
  14.8 0.0 copy-start.2
  14.8 1.2 %collective-permute-start = (f32[2,32,256]{2,1,0:T(8,128)}, f32[2,32,256]{2,1,0:T(8,128)S(1)}, u32[]{:S(2)}, u32[]{:S(2)}) collective-permute-start(f32[2,32,256]{2,1,0:T(8,128)} %get-tuple-element.18), channel_id=1, source_target_pairs={{0,1},{1,0},{2,3},{3,2},{4,5},{5,4},{6,7},{7,6},{8,9},{9,8},{10,11... | collective-permute-start | bytes 196616 | tf_op jit(solution)/shard_map/ppermute | solution.py:432
  16.1 2.1 %collective-permute-done.refs_0_ = f32[2,32,256]{2,1,0:T(8,128)S(1)} collective-permute-done((f32[2,32,256]{2,1,0:T(8,128)}, f32[2,32,256]{2,1,0:T(8,128)S(1)}, u32[]{:S(2)}, u32[]{:S(2)}) %collective-permute-start) | collective-permute-done | bytes 65568 | tf_op jit(solution)/shard_map/ppermute | solution.py:432
  18.2 0.0 copy-start.3
  18.2 0.6 copy-done.3
  18.8 7.9 %mixed_planes.3 = (f32[32,32,256]{2,1,0:T(8,128)}, f32[32,32,256]{2,1,0:T(8,128)}, f32[32,32,256]{2,1,0:T(8,128)}) custom-call(f32[32,27]{1,0:T(8,128)} %weight.3, f32[32,32]{1,0:T(8,128)} %point.3, f32[2,32,256]{2,1,0:T(8,128)} %copy-done.3, f32[32,64,256]{2,1,0:T(8,128)} %bitcast.14, f32[32,64,256]{2,1,0:T(8,128)} %bitcast.15, f32[32,64,256]{2,1,0:T(8,128)} %bitcast.16, ...), custom_call_target="tpu_custom_call" | custom-call | flops 2000000000 | bytes 4194304 | tf_op jit(solution)/shard_map/mixed_planes/pallas_call | solution.py:344
  26.7 1.7 %collective-permute-start.3 = (f32[32,32,256]{2,1,0:T(8,128)}, f32[32,32,256]{2,1,0:T(8,128)S(1)}, u32[]{:S(2)}, u32[]{:S(2)}) collective-permute-start(f32[32,32,256]{2,1,0:T(8,128)} %get-tuple-element.21), channel_id=1, source_target_pairs={{0,2},{2,4},{4,6},{6,8},{8,10},{10,12},{12,14},{14,16},{16,18},{18... | collective-permute-start | bytes 3145736 | tf_op jit(solution)/shard_map/ppermute | solution.py:423
  28.3 2.4 %collective-permute-start.4 = (f32[32,32,256]{2,1,0:T(8,128)}, f32[32,32,256]{2,1,0:T(8,128)S(1)}, u32[]{:S(2)}, u32[]{:S(2)}) collective-permute-start(f32[32,32,256]{2,1,0:T(8,128)} %get-tuple-element.22), channel_id=1, source_target_pairs={{0,30},{2,0},{4,2},{6,4},{8,6},{10,8},{12,10},{14,12},{16,14},{18,... | collective-permute-start | bytes 3145736 | tf_op jit(solution)/shard_map/ppermute | solution.py:424
  30.7 0.0 copy-done.2
  30.7 27.3 %all_to_all.20 = f32[32,8,128]{2,1,0:T(8,128)} all-to-all(f32[32,8,128]{2,1,0:T(8,128)S(1)} %bitcast.20), channel_id=1, replica_groups=mesh['gz'=16,'gy'=2] {'gz','gy'}, dimensions={0} | all-to-all | bytes 262144 | tf_op jit(solution)/shard_map/all_to_all | solution.py:447
  58.1 2.7 %filter_modes.1 = f32[256,128]{1,0:T(8,128)} custom-call(f32[256,128]{1,0:T(8,128)} %bitcast.18, f32[2,16,8,64]{3,2,1,0:T(8,128)} %gains.1, bf16[256,256]{1,0:T(8,128)(2,1)} %constant.32.clone.f_top, bf16[256,256]{1,0:T(8,128)(2,1)} %constant.33.clone.f_rest, bf16[512,128]{1,0:T(8,128)(2,1)} %constant.34.clone.i_top, bf16[512,128]{1,0:T(8,128)(2,1)} %constant.35.clone.i_rest), custom_call_target="tpu_custom_call" | custom-call | flops 200000000 | bytes 1048576 | tf_op jit(solution)/shard_map/filter_modes/pallas_call | solution.py:295
  60.8 14.3 %all_to_all.21 = f32[32,8,128]{2,1,0:T(8,128)} all-to-all(f32[32,8,128]{2,1,0:T(8,128)} %bitcast.19), channel_id=1, replica_groups=mesh['gz'=16,'gy'=2] {'gz','gy'}, dimensions={0} | all-to-all | bytes 262144 | tf_op jit(solution)/shard_map/all_to_all | solution.py:449
  75.1 0.0 collective-permute-done.2.high
  75.1 0.0 copy-start.4
  75.1 0.0 collective-permute-done.1.low
  75.1 0.0 copy-start.5
  75.1 1.0 %copy-done.4 = f32[32,32,256]{2,1,0:T(8,128)} copy-done((f32[32,32,256]{2,1,0:T(8,128)}, f32[32,32,256]{2,1,0:T(8,128)S(1)}, u32[]{:S(2)}) %copy-start.4) | copy-done | bytes 1048600
  76.1 0.3 copy-done.5
  76.4 5.1 %inverse_modes.1.base = f32[32,64,256]{2,1,0:T(8,128)} custom-call(s32[1]{0:T(128)} %bitcast._, f32[16,16,128]{2,1,0:T(8,128)} %bitcast.21, f32[32,32,256]{2,1,0:T(8,128)} %get-tuple-element.17.inner, f32[32,32,256]{2,1,0:T(8,128)} %get-tuple-element.19.outer, f32[32,32,256]{2,1,0:T(8,128)} %copy-done.5, f32[32,32,256]{2,1,0:T(8,128)} %copy-done.4, f32[32]{0:T(128)} %bias.1, ...), custom_call_target="tpu_custom_call" | custom-call | flops 4000000000 | bytes 6291456 | tf_op jit(solution)/shard_map/inverse_modes/pallas_call | solution.py:313
  81.5 0.0 collective-permute-done.3.low
  81.5 0.0 copy-start
  81.5 0.0 collective-permute-done.4.high
  81.5 1.0 %copy-done = f32[32,32,256]{2,1,0:T(8,128)} copy-done((f32[32,32,256]{2,1,0:T(8,128)}, f32[32,32,256]{2,1,0:T(8,128)S(1)}, u32[]{:S(2)}) %copy-start) | copy-done | bytes 1048600
  82.4 0.0 copy-start.1
  82.4 1.0 %copy-done.1 = f32[32,32,256]{2,1,0:T(8,128)} copy-done((f32[32,32,256]{2,1,0:T(8,128)}, f32[32,32,256]{2,1,0:T(8,128)S(1)}, u32[]{:S(2)}) %copy-start.1) | copy-done | bytes 1048600
  83.4 3.8 %finished_rows.1 = f32[32,64,256]{2,1,0:T(8,128)} custom-call(f32[32,64,256]{2,1,0:T(8,128)} %inverse_modes.1.base, f32[32,32,256]{2,1,0:T(8,128)} %copy-done, f32[32,32,256]{2,1,0:T(8,128)} %copy-done.1), custom_call_target="tpu_custom_call", output_to_operand_aliasing={{}: (0, {})} | custom-call | flops 1000000000 | bytes 4194304 | tf_op jit(solution)/shard_map/finished_rows/pallas_call | solution.py:369
Async XLA Ops:
  7.6 67.5 %collective-permute-start.2 = (f32[32,32,256]{2,1,0:T(8,128)}, f32[32,32,256]{2,1,0:T(8,128)S(1)}, u32[]{:S(2)}, u32[]{:S(2)}) collective-permute-start(f32[32,32,256]{2,1,0:T(8,128)} %get-tuple-element.20), channel_id=1, source_target_pairs={{0,30},{2,0},{4,2},{6,4},{8,6},{10,8},{12,10},{14,12},{16,14},{18,... | collective-permute-start | bytes 3145736 | tf_op jit(solution)/shard_map/ppermute | solution.py:424
  7.7 67.4 %collective-permute-start.1 = (f32[32,32,256]{2,1,0:T(8,128)}, f32[32,32,256]{2,1,0:T(8,128)S(1)}, u32[]{:S(2)}, u32[]{:S(2)}) collective-permute-start(f32[32,32,256]{2,1,0:T(8,128)} %get-tuple-element.14), channel_id=1, source_target_pairs={{0,2},{2,4},{4,6},{6,8},{8,10},{10,12},{12,14},{14,16},{16,18},{18... | collective-permute-start | bytes 3145736 | tf_op jit(solution)/shard_map/ppermute | solution.py:423
  14.8 15.9 %copy-start.2 = (f32[16,16,128]{2,1,0:T(8,128)S(1)}, f32[16,16,128]{2,1,0:T(8,128)}, u32[]{:S(2)}) copy-start(f32[16,16,128]{2,1,0:T(8,128)} %get-tuple-element.16) | copy-start | bytes 393220
  14.8 3.3 %collective-permute-start = (f32[2,32,256]{2,1,0:T(8,128)}, f32[2,32,256]{2,1,0:T(8,128)S(1)}, u32[]{:S(2)}, u32[]{:S(2)}) collective-permute-start(f32[2,32,256]{2,1,0:T(8,128)} %get-tuple-element.18), channel_id=1, source_target_pairs={{0,1},{1,0},{2,3},{3,2},{4,5},{5,4},{6,7},{7,6},{8,9},{9,8},{10,11... | collective-permute-start | bytes 196616 | tf_op jit(solution)/shard_map/ppermute | solution.py:432
  18.2 0.6 copy-start.3
  26.7 54.8 %collective-permute-start.3 = (f32[32,32,256]{2,1,0:T(8,128)}, f32[32,32,256]{2,1,0:T(8,128)S(1)}, u32[]{:S(2)}, u32[]{:S(2)}) collective-permute-start(f32[32,32,256]{2,1,0:T(8,128)} %get-tuple-element.21), channel_id=1, source_target_pairs={{0,2},{2,4},{4,6},{6,8},{8,10},{10,12},{12,14},{14,16},{16,18},{18... | collective-permute-start | bytes 3145736 | tf_op jit(solution)/shard_map/ppermute | solution.py:423
  28.3 53.1 %collective-permute-start.4 = (f32[32,32,256]{2,1,0:T(8,128)}, f32[32,32,256]{2,1,0:T(8,128)S(1)}, u32[]{:S(2)}, u32[]{:S(2)}) collective-permute-start(f32[32,32,256]{2,1,0:T(8,128)} %get-tuple-element.22), channel_id=1, source_target_pairs={{0,30},{2,0},{4,2},{6,4},{8,6},{10,8},{12,10},{14,12},{16,14},{18,... | collective-permute-start | bytes 3145736 | tf_op jit(solution)/shard_map/ppermute | solution.py:424
  75.1 1.0 %copy-start.4 = (f32[32,32,256]{2,1,0:T(8,128)}, f32[32,32,256]{2,1,0:T(8,128)S(1)}, u32[]{:S(2)}) copy-start(f32[32,32,256]{2,1,0:T(8,128)S(1)} %collective-permute-done.2.high) | copy-start | bytes 3145732
  75.1 1.3 %copy-start.5 = (f32[32,32,256]{2,1,0:T(8,128)}, f32[32,32,256]{2,1,0:T(8,128)S(1)}, u32[]{:S(2)}) copy-start(f32[32,32,256]{2,1,0:T(8,128)S(1)} %collective-permute-done.1.low) | copy-start | bytes 3145732
  81.5 1.0 %copy-start = (f32[32,32,256]{2,1,0:T(8,128)}, f32[32,32,256]{2,1,0:T(8,128)S(1)}, u32[]{:S(2)}) copy-start(f32[32,32,256]{2,1,0:T(8,128)S(1)} %collective-permute-done.3.low) | copy-start | bytes 3145732
  82.4 1.0 %copy-start.1 = (f32[32,32,256]{2,1,0:T(8,128)}, f32[32,32,256]{2,1,0:T(8,128)S(1)}, u32[]{:S(2)}) copy-start(f32[32,32,256]{2,1,0:T(8,128)S(1)} %collective-permute-done.4.high) | copy-start | bytes 3145732

commit v2 on v1

--- a/solution.py
+++ b/solution.py
@@ -15,7 +15,7 @@
 MY = 16
 MZ = 16
 CH = 32
-VMEM_BYTES = 58 * 1024 * 1024
+VMEM_BYTES = 24 * 1024 * 1024
 BF = jnp.bfloat16
 F32 = jnp.float32
 
@@ -34,7 +34,7 @@
     table = np.asarray(table, np.float64)
     top = table.astype(np.float32).astype(ml_dtypes.bfloat16)
     rest = (table - top.astype(np.float64)).astype(np.float32).astype(ml_dtypes.bfloat16)
-    return top, rest
+    return jnp.asarray(top), jnp.asarray(rest)
 
 
 def y_forward_table(y_local, gy, group):
@@ -105,21 +105,27 @@
     return both[:rows] + (both[rows:] + dot(a[0], b[1]))
 
 
-def forward_kernel(group, _, field, y_top, y_rest, x_top, x_rest, out, edges):
+def forward_kernel(group, _, field, y_top, y_rest, x_top, x_rest, out, edges, turned):
     y_table = (y_top[0], y_rest[0])
     half = group * MY
-    total = jnp.zeros((half, 4 * MX), F32)
+    step = pl.program_id(0)
     for p in range(2):
         rows = jnp.concatenate([field[2 * i + p] for i in range(group)], axis=0)
-        turned = dot3(y_table, parts(rows))
+        both = dot3(y_table, parts(rows))
         for t in range(2):
-            piece = parts(turned[t * half : (t + 1) * half])
-            total = total + dot3(piece, (x_top[2 * p + t], x_rest[2 * p + t]))
-    out[...] = total.reshape(group, MY, 4 * MX)
+            at = pl.multiple_of(step * half, half)
+            turned[2 * p + t, pl.ds(at, half), :] = both[t * half : (t + 1) * half]
     last = field.shape[1] - 1
     for i in range(2 * group):
         edges[0, i : i + 1, :] = field[i, last : last + 1, :]
         edges[1, i : i + 1, :] = field[i, 0:1, :]
+
+    @pl.when(step == pl.num_programs(0) - 1)
+    def _():
+        total = dot3(parts(turned[0]), (x_top[0], x_rest[0]))
+        for k in range(1, 4):
+            total = total + dot3(parts(turned[k]), (x_top[k], x_rest[k]))
+        out[...] = total.reshape(CH // 2, MY, 4 * MX)
 
 
 def swap_parts(value):
@@ -145,81 +151,81 @@
     out[...] = back[:half] + jnp.where(is_real, -crossed, crossed)
 
 
-def conv_kernel(inner, rows, weight, point, *refs):
-    if inner:
-        above, first, second, below = refs[:4]
-        segments = ((8, 2 * rows, 0),)
-        blocks = ((above, 0, 8), (first, 8, rows), (second, 8 + rows, rows), (below, 8 + 2 * rows, 8))
-        refs = refs[4:]
+def conv_kernel(count, weight, point, *refs):
+    tiles, refs = refs[: 2 * (count + 2)], refs[2 * (count + 2) :]
+    halo = None
+    if len(refs) == 7:
+        halo, refs = refs[0], refs[1:]
+    outs, (turned, depth, gains) = refs[:3], refs[3:]
+    tiles = [[t.reshape(CH * 8, 128) for t in tiles[2 * i : 2 * i + 2]] for i in range(count + 2)]
+
+    def row(tile, r):
+        return jnp.concatenate([half[pl.ds(r, CH, stride=8), :] for half in tile], axis=1)
+
+    if halo is None:
+        segments = [([lambda: row(tiles[0], 7)], tiles[1:-1], [lambda: row(tiles[-1], 0)])]
     else:
-        halo, first, below, above, second = refs[:5]
-        start = rows + 24
-        segments = ((8, rows, 0), (start, rows, rows))
-        blocks = ((first, 8, rows), (below, 8 + rows, 8), (above, start - 8, 8), (second, start, rows))
-        refs = refs[5:]
-    outs, (shifted, depth) = refs[:3], refs[3:]
-    turns = (1, 0, NX - 1)
-    step = 8
-
-    def load(i, _):
-        c = pl.multiple_of(i * step, step)
-        for ref, at, count in blocks:
-            value = ref[pl.ds(c, step)].reshape(step * count, NX)
-            for e, turn in enumerate(turns):
-                moved = pltpu.roll(value, turn, 1) if turn else value
-                for h in range(2):
-                    shifted[e, h, pl.ds(c, step), pl.ds(at, count), :] = moved[
-                        :, 128 * h : 128 * h + 128
-                    ].reshape(step, count, 128)
+        top, under, over, bottom = tiles
+        segments = [
+            ([lambda: halo[0]], [top], [lambda: row(under, 0)]),
+            ([lambda: row(over, 7)], [bottom], [lambda: halo[1]]),
+        ]
+    runs, at, done = [], 0, 0
+    for before, whole, after in segments:
+        makers = before + [functools.partial(row, t, r) for t in whole for r in range(8)] + after
+        for i, make in enumerate(makers):
+            value = make()
+            turned[0, at + i] = pltpu.roll(value, 1, 1)
+            turned[1, at + i] = value
+            turned[2, at + i] = pltpu.roll(value, NX - 1, 1)
+        runs.append((at, done, 8 * len(whole)))
+        at, done = at + len(makers), done + 8 * len(whole)
+    for k in range(27):
+        gains[k] = jnp.broadcast_to(weight[:, k : k + 1], (CH, 128))
+
+    def taps(i, _):
+        chans = pl.ds(pl.multiple_of(i * 8, 8), 8)
+        gain = [gains[k, chans, :] for k in range(27)]
+        for h in range(2):
+            lanes = pl.ds(128 * h, 128)
+            for first, to, rows in runs:
+                sums = {}
+                for r in range(rows + 2):
+                    values = [turned[e, first + r, chans, lanes] for e in range(3)]
+                    for b in range(3):
+                        o = r - b
+                        if o < 0 or o >= rows:
+                            continue
+                        for a in range(3):
+                            for e in range(3):
+                                term = gain[a * 9 + b * 3 + e] * values[e]
+                                sums[o, a] = sums[o, a] + term if (o, a) in sums else term
+                    if r >= 2:
+                        for a in range(3):
+                            depth[a, to + r - 2, chans, lanes] = sums.pop((r - 2, a))
         return 0
 
-    lax.fori_loop(0, CH // step, load, 0)
-    if not inner:
-        for side, at in ((0, 7), (1, start + rows)):
-            value = halo[side]
-            for e, turn in enumerate(turns):
-                moved = pltpu.roll(value, turn, 1) if turn else value
-                for h in range(2):
-                    shifted[e, h, :, pl.ds(at, 1), :] = moved[:, 128 * h : 128 * h + 128].reshape(CH, 1, 128)
-
-    def taps(c, _):
-        gain = [weight[c, k] for k in range(27)]
-        for at, count, to in segments:
-            for h in range(2):
-                for part in range(0, count, 16):
-                    size = min(16, count - part)
-                    sums = [None, None, None]
-                    for e in range(3):
-                        for b in range(3):
-                            value = shifted[e, h, c, pl.ds(at + part + b - 1, size), :]
-                            for a in range(3):
-                                term = gain[a * 9 + b * 3 + e] * value
-                                sums[a] = term if sums[a] is None else sums[a] + term
-                    for a in range(3):
-                        depth[a, c, pl.ds(to + part, size), pl.ds(128 * h, 128)] = sums[a]
-        return 0
-
-    lax.fori_loop(0, CH, taps, 0, unroll=2)
-
-    spread = (
+    lax.fori_loop(0, CH // 8, taps, 0)
+
+    down = (
         lax.broadcasted_iota(jnp.int32, (8 * CH, CH), 0) // 8
         == lax.broadcasted_iota(jnp.int32, (8 * CH, CH), 1)
     ).astype(BF)
-    gather = (
-        lax.broadcasted_iota(jnp.int32, (CH, 8 * CH), 1) // 8
+    across = (
+        lax.broadcasted_iota(jnp.int32, (CH, 8 * CH), 1) % CH
         == lax.broadcasted_iota(jnp.int32, (CH, 8 * CH), 0)
     ).astype(BF)
     same = (
         lax.broadcasted_iota(jnp.int32, (8 * CH, 8 * CH), 0) % 8
-        == lax.broadcasted_iota(jnp.int32, (8 * CH, 8 * CH), 1) % 8
+        == lax.broadcasted_iota(jnp.int32, (8 * CH, 8 * CH), 1) // CH
     )
     mix = tuple(
-        jnp.where(same, dot(dot(spread, part).astype(BF), gather), 0.0).astype(BF)
+        jnp.where(same, dot(dot(down, part).astype(BF), across), 0.0).astype(BF)
         for part in parts(point[...])
     )
-    for t in range(2 * rows // 8):
+    for t in range(done // 8):
         for a, out in enumerate(outs):
-            tile = depth[a, :, pl.ds(8 * t, 8), :].reshape(8 * CH, NX)
+            tile = depth[a, pl.ds(8 * t, 8)].reshape(8 * CH, NX)
             out[:, pl.ds(8 * t, 8), :] = dot3(mix, parts(tile)).reshape(CH, 8, NX)
 
 
@@ -227,12 +233,12 @@
     return 0.5 * value * (1.0 + lax.erf(value * (1.0 / math.sqrt(2.0))))
 
 
-def inverse_kernel(group, _, modes, inner, outer, low, high, bias, x_top, x_rest, y_top, y_rest, out):
+def inverse_kernel(group, chunks, _, modes, bias, x_top, x_rest, y_top, y_rest, outer, *refs):
+    out = refs[-1]
     step = pl.program_id(0)
     y_table = (y_top[0], y_rest[0])
     mode_rows = parts(modes[...].reshape(group * MY, 4 * MX))
     y_local = out.shape[1]
-    rows = y_local // 4
     for p in range(2):
         wide = dot3(mode_rows, (x_top[p], x_rest[p]))
         tall = jnp.concatenate([wide[:, :NX], wide[:, NX:]], axis=0)
@@ -240,13 +246,20 @@
         for i in range(group):
             c = 2 * i + p
             plane = planes[i] + bias[step * 2 * group + c]
-            out[c, :rows] = plane[:rows] + outer[c, :rows]
-            out[c, 3 * rows :] = plane[3 * rows :] + outer[c, rows:]
-            out[c, rows : 3 * rows] = gelu(plane[rows : 3 * rows] + (inner[c] + (low[c] + high[c])))
+            out[c, :8] = plane[:8] + outer[c, :8]
+            out[c, y_local - 8 :] = plane[y_local - 8 :] + outer[c, 8:]
+            for k, (first, count) in enumerate(chunks):
+                rows = slice(8 * first, 8 * (first + count))
+                own, low, high = refs[3 * k : 3 * k + 3]
+                out[c, rows] = gelu(plane[rows] + (own[c] + (low[c] + high[c])))
 
 
 def finish_kernel(base, low, high, out):
     out[...] = gelu(base[...] + (low[...] + high[...]))
+
+
+def in_hbm(*arrays):
+    return [pltpu.with_memory_space_constraint(a, pltpu.HBM) for a in arrays]
 
 
 def params():
@@ -279,14 +292,15 @@
                 y_spec, y_spec, x_spec, x_spec,
             ],
             out_specs=[
-                pl.BlockSpec((group, MY, 4 * MX), lambda i, s: (i, 0, 0)),
+                pl.BlockSpec((CH // 2, MY, 4 * MX), lambda i, s: (0, 0, 0)),
                 pl.BlockSpec((2, 2 * group, NX), lambda i, s: (0, i, 0)),
             ],
+            scratch_shapes=[pltpu.VMEM((4, CH // 2 * MY, NX), F32)],
         ),
         compiler_params=params(),
         cost_estimate=cost(2 * 10**9, 4 * 2**20),
         name="forward_modes",
-    )(place, field, *y_tab, *x_tab)
+    )(place, *in_hbm(field, *y_tab, *x_tab))
 
 
 def filter_call(arrived, gains, gz, gy, scale):
@@ -298,83 +312,90 @@
         compiler_params=params(),
         cost_estimate=cost(2 * 10**8, 2**20),
         name="filter_modes",
-    )(arrived, gains, *fwd, *inv)
-
-
-def inverse_call(modes, inner, outer, low, high, bias, place, gy, scale):
-    y_local = 2 * inner.shape[1]
+    )(arrived, gains, *in_hbm(*fwd, *inv))
+
+
+def inverse_call(modes, bias, outer, inner, chunks, y_local, place, gy, scale):
     group = 8
     x_tab = halves(x_inverse_table(scale))
     y_tab = halves(y_inverse_table(y_local, gy, group))
     tall, wide = y_tab[0].shape[1:]
     y_spec = pl.BlockSpec((1, tall, wide), lambda i, s: (s[0], 0, 0))
     x_spec = pl.BlockSpec((2, 4 * MX, 2 * NX), lambda i, s: (0, 0, 0))
-    half = pl.BlockSpec((2 * group, y_local // 2, NX), lambda i, s: (i, 0, 0))
+    some = lambda rows: pl.BlockSpec((2 * group, rows, NX), lambda i, s: (i, 0, 0))
     return pl.pallas_call(
-        functools.partial(inverse_kernel, group),
+        functools.partial(inverse_kernel, group, chunks),
         out_shape=jax.ShapeDtypeStruct((CH, y_local, NX), F32),
         grid_spec=pltpu.PrefetchScalarGridSpec(
             num_scalar_prefetch=1,
             grid=(CH // 2 // group,),
             in_specs=[
                 pl.BlockSpec((group, MY, 4 * MX), lambda i, s: (i, 0, 0)),
-                half, half, half, half,
                 pl.BlockSpec(memory_space=pltpu.SMEM),
                 x_spec, x_spec, y_spec, y_spec,
+                some(16),
+                *[some(8 * count) for _, count in chunks for _ in range(3)],
             ],
-            out_specs=pl.BlockSpec((2 * group, y_local, NX), lambda i, s: (i, 0, 0)),
+            out_specs=some(y_local),
         ),
         compiler_params=params(),
         cost_estimate=cost(4 * 10**9, 6 * 2**20),
         name="inverse_modes",
-    )(place, modes, inner, outer, low, high, bias, *x_tab, *y_tab)
-
-
-def conv_call(field, halo, weight, point, inner):
-    rows = field.shape[1] // 4
-    tile = lambda at: pl.BlockSpec((CH, 8, NX), lambda i: (0, at, 0))
-    quarter = lambda at: pl.BlockSpec((CH, rows, NX), lambda i: (0, at, 0))
-    first, last = rows // 8, 3 * rows // 8
-    if inner:
-        specs = [tile(first - 1), quarter(1), quarter(2), tile(last)]
-        operands = [field] * 4
+    )(place, modes, bias, *in_hbm(*x_tab, *y_tab), outer, *inner)
+
+
+def conv_call(field, halo, weight, point, first, count):
+    last = field.shape[1] // 8 - 1
+    if halo is None:
+        chosen = range(first - 1, first + count + 1)
     else:
-        specs = [pl.BlockSpec((2, CH, NX), lambda i: (0, 0, 0)), quarter(0), tile(first), tile(last - 1), quarter(3)]
-        operands = [halo] + [field] * 4
+        chosen = (0, 1, last - 1, last)
+    tile = lambda t, h: pl.BlockSpec((CH, 8, 128), lambda i: (0, t, h))
+    specs = [tile(t, h) for t in chosen for h in range(2)]
+    weight, point, field = in_hbm(weight, point, field)
+    operands = [field] * len(specs)
+    if halo is not None:
+        specs.append(pl.BlockSpec((2, CH, NX), lambda i: (0, 0, 0)))
+        operands.append(halo)
+    rows = 8 * count
     return pl.pallas_call(
-        functools.partial(conv_kernel, inner, rows),
-        out_shape=[jax.ShapeDtypeStruct((CH, 2 * rows, NX), F32)] * 3,
+        functools.partial(conv_kernel, count),
+        out_shape=[
+            pltpu.HBM((CH, rows, NX), F32),
+            jax.ShapeDtypeStruct((CH, rows, NX), F32),
+            pltpu.HBM((CH, rows, NX), F32),
+        ],
         grid=(1,),
         in_specs=[
-            pl.BlockSpec(memory_space=pltpu.SMEM),
+            pl.BlockSpec((CH, 27), lambda i: (0, 0)),
             pl.BlockSpec((CH, CH), lambda i: (0, 0)),
             *specs,
         ],
-        out_specs=[pl.BlockSpec((CH, 2 * rows, NX), lambda i: (0, 0, 0))] * 3,
+        out_specs=[pl.BlockSpec((CH, rows, NX), lambda i: (0, 0, 0))] * 3,
         scratch_shapes=[
-            pltpu.VMEM((3, 2, CH, 2 * rows + 32, 128), F32),
-            pltpu.VMEM((3, CH, 2 * rows, NX), F32),
+            pltpu.VMEM((3, rows + 4, CH, NX), F32),
+            pltpu.VMEM((3, rows, CH, NX), F32),
+            pltpu.VMEM((27, CH, 128), F32),
         ],
         compiler_params=params(),
-        cost_estimate=cost(2 * 10**9, 4 * 2**20),
+        cost_estimate=cost(10**8 * count, count * 2**19),
         name="mixed_planes",
     )(weight, point, *operands)
 
 
 def finish_call(result, low, high):
-    rows = result.shape[1] // 4
-    tiles = rows // 8
-    block = pl.BlockSpec((CH, 8, NX), lambda i: (0, i + (i // tiles) * 2 * tiles, 0))
-    piece = pl.BlockSpec((CH, 8, NX), lambda i: (0, i, 0))
+    last = result.shape[1] // 8 - 1
+    block = pl.BlockSpec((CH // 2, 8, NX), lambda i, j: (j, i * last, 0))
+    piece = pl.BlockSpec((CH // 2, 8, NX), lambda i, j: (j, i, 0))
     return pl.pallas_call(
         finish_kernel,
         out_shape=jax.ShapeDtypeStruct(result.shape, F32),
-        grid=(2 * tiles,),
+        grid=(2, 2),
         in_specs=[block, piece, piece],
         out_specs=block,
         input_output_aliases={0: 0},
         compiler_params=params(),
-        cost_estimate=cost(10**9, 4 * 2 * rows * CH * NX * 4),
+        cost_estimate=cost(10**8, 4 * 16 * CH * NX * 4),
         name="finished_rows",
     )(result, low, high)
 
@@ -424,9 +445,23 @@
             lax.ppermute(up, "gz", ring("gz", gz, -1)),
         )
 
-    down, inner, up = conv_call(field, None, depth_weight, point_weight, True)
-    inner_low, inner_high = to_neighbours(down, up)
-    field, _ = lax.optimization_barrier((field, down))
+    tiles = y_local // 8
+    chunks, at = [], 1
+    for count in (1, 2, tiles):
+        count = min(count, tiles - 1 - at)
+        if count > 0:
+            chunks.append((at, count))
+            at += count
+
+    def sums_for(k, source):
+        down, own, up = conv_call(source, None, depth_weight, point_weight, *chunks[k])
+        return [own, *to_neighbours(down, up)], down
+
+    inner = []
+    for k in range(min(2, len(chunks))):
+        got, mark = sums_for(k, field)
+        inner += got
+        field, _ = lax.optimization_barrier((field, mark))
     coarse, edges = forward_call(field, place, gy)
     if gy == 2:
         halo = lax.ppermute(edges, "gy", ring("gy", gy, 1))
@@ -437,7 +472,9 @@
                 lax.ppermute(edges[1], "gy", ring("gy", gy, -1)),
             ]
         )
-    down, outer, up = conv_call(field, halo, depth_weight, point_weight, False)
+    for k in range(2, len(chunks)):
+        inner += sums_for(k, field)[0]
+    down, outer, up = conv_call(field, halo, depth_weight, point_weight, 0, 2)
     outer_low, outer_high = to_neighbours(down, up)
 
     j_own, n_own = spectral_filter.shape[2], spectral_filter.shape[3]
@@ -452,7 +489,7 @@
         back = general_filter(coarse, spectral_filter, gz, gy, forward_scale)
 
     result = inverse_call(
-        back, inner, outer, inner_low, inner_high, bias_vector, place, gy, inverse_scale
+        back, bias_vector, outer, inner, chunks, y_local, place, gy, inverse_scale
     )
     result = finish_call(result, outer_low, outer_high)
     return result.reshape(CH, 1, y_local, NX)

time: 88.6 us -> 88.8 us (level)
  blocking collectives: 41.6 us -> 0 us
  waiting for transfers between devices: 2.13 us -> 28.9 us
  starting transfers between devices: 7.89 us -> 19.4 us
  local copies, waits for them, and re-layouts: 3.9 us -> 6.39 us
  Pallas kernels: 31.7 us -> 33.3 us
    all_to_all x2 -> x0, blocking collectives: 41.6 us -> none  [the longest x1 27.3 us: body(): got = lax.all_to_all(sent, both, split_axis=0, concat_axis=0, tiled=True)]
    ppermute x2 -> x4, waiting for transfers between devices: 0.01 us -> 20.6 us  [to_neighbours(): lax.ppermute(up, 'gz', ring('gz', gz, -1))]
    all_to_all x0 -> x2, starting transfers between devices: none -> 8.57 us  [the longest x1 4.44 us: body(): back = lax.all_to_all(out, both, split_axis=0, concat_axis=0, tiled=True)]
    all_to_all x0 -> x2, waiting for transfers between devices: none -> 5.6 us  [the longest x1 5.55 us: body(): got = lax.all_to_all(sent, both, split_axis=0, concat_axis=0, tiled=True)]
    ppermute x2 -> x4, waiting for transfers between devices: 0.01 us -> 2.77 us  [to_neighbours(): lax.ppermute(down, 'gz', ring('gz', gz, 1))]
    pallas_call x3 -> x5, Pallas kernels: 20.5 us -> 23.1 us  [the longest x4 18.7 us: conv_call(): pl.pallas_call(functools.partial(conv_kernel, count), out_shape=[pltpu.HB...]
    unnamed x12 -> x22, local copies, waits for them, and re-layouts: 3.9 us -> 6.39 us
    ppermute x1, waiting for transfers between devices: 2.11 us -> 0.01 us  [body(): halo = lax.ppermute(edges, 'gy', ring('gy', gy, 1))]
  transfers between devices with their start and end apart: 5 -> 11, of which waited for: 1 -> 4; matrix products, arithmetic and copies ran while one was open for 0% -> 0% of each run, Pallas kernels for 23% -> 18%
where the time goes in v2:
time: 88.8 us; the launch traced here: 88.1 us
  Pallas kernels  33.3 us (37%)
  waiting for transfers between devices  28.9 us (33%)
  starting transfers between devices  19.4 us (22%)
  local copies, waits for them, and re-layouts  6.39 us (7%)
    ppermute x4, waiting for transfers between devices, to_neighbours(): lax.ppermute(up, 'gz', ring('gz', gz, -1))  20.6 us
    pallas_call x4, Pallas kernels, conv_call(): pl.pallas_call(functools.partial(conv_kernel, count), out_shape=[pltpu.HB...  18.7 us
    unnamed x22, local copies, waits for them, and re-layouts  6.39 us
    ppermute x4, starting transfers between devices, to_neighbours(): lax.ppermute(down, 'gz', ring('gz', gz, 1))  5.99 us
    all_to_all x1, waiting for transfers between devices, body(): got = lax.all_to_all(sent, both, split_axis=0, concat_axis=0, tiled=True)  5.55 us
    pallas_call x1, Pallas kernels, forward_call(): pl.pallas_call(functools.partial(forward_kernel, group), out_shape=[jax.S...  4.49 us
    all_to_all x1, starting transfers between devices, body(): back = lax.all_to_all(out, both, split_axis=0, concat_axis=0, tiled=True)  4.44 us
    pallas_call x1, Pallas kernels, inverse_call(): pl.pallas_call(functools.partial(inverse_kernel, group, chunks), out_shap...  4.35 us
  transfers between devices with their start and end apart: 11, of which 4 were waited for; matrix products, arithmetic and copies ran while one was open for 0% of the time, Pallas kernels for 18%

profile of v2, /device:TPU:1, one launch (start us, length us, event | category | flops | bytes accessed | tf_op | source)
XLA Modules:
  0.0 88.1 jit_solution(4025374963488848365)
XLA Ops:
  0.0 3.6 %mixed_planes.4 = (f32[32,8,256]{2,1,0:T(8,128)}, f32[32,8,256]{2,1,0:T(8,128)S(1)}, f32[32,8,256]{2,1,0:T(8,128)}) custom-call(f32[32,27]{1,0:T(8,128)} %weight.7, f32[32,32]{1,0:T(8,128)} %point.7, f32[32,64,256]{2,1,0:T(8,128)} %bitcast.11, f32[32,64,256]{2,1,0:T(8,128)} %bitcast.12, f32[32,64,256]{2,1,0:T(8,128)} %bitcast.13, f32[32,64,256]{2,1,0:T(8,128)} %bitcast.14, ...), custom_call_target="tpu_custom_call" | custom-call | flops 100000000 | bytes 524288 | tf_op jit(solution)/shard_map/mixed_planes/pallas_call | solution.py:361
  3.6 0.7 copy-done.7
  4.3 4.6 %mixed_planes.5 = (f32[32,16,256]{2,1,0:T(8,128)}, f32[32,16,256]{2,1,0:T(8,128)S(1)}, f32[32,16,256]{2,1,0:T(8,128)}) custom-call(f32[32,27]{1,0:T(8,128)} %weight.7, f32[32,32]{1,0:T(8,128)} %point.7, f32[32,64,256]{2,1,0:T(8,128)} %bitcast.17, f32[32,64,256]{2,1,0:T(8,128)} %bitcast.18, f32[32,64,256]{2,1,0:T(8,128)} %bitcast.19, ...), custom_call_target="tpu_custom_call" | custom-call | flops 200000000 | bytes 1048576 | tf_op jit(solution)/shard_map/mixed_planes/pallas_call | solution.py:361
  8.9 5.9 %mixed_planes.7 = (f32[32,24,256]{2,1,0:T(8,128)}, f32[32,24,256]{2,1,0:T(8,128)S(1)}, f32[32,24,256]{2,1,0:T(8,128)}) custom-call(f32[32,27]{1,0:T(8,128)} %weight.7, f32[32,32]{1,0:T(8,128)} %point.7, f32[32,64,256]{2,1,0:T(8,128)} %bitcast.27, f32[32,64,256]{2,1,0:T(8,128)} %bitcast.26, f32[32,64,256]{2,1,0:T(8,128)} %bitcast.25, ...), custom_call_target="tpu_custom_call" | custom-call | flops 300000000 | bytes 1572864 | tf_op jit(solution)/shard_map/mixed_planes/pallas_call | solution.py:361
  14.8 2.6 %collective-permute-start.5 = (f32[32,24,256]{2,1,0:T(8,128)}, f32[32,24,256]{2,1,0:T(8,128)S(1)}, u32[]{:S(2)}, u32[]{:S(2)}) collective-permute-start(f32[32,24,256]{2,1,0:T(8,128)} %get-tuple-element.33), channel_id=1, source_target_pairs={{0,2},{2,4},{4,6},{6,8},{8,10},{10,12},{12,14},{14,16},{16,18},{18... | collective-permute-start | bytes 2359304 | tf_op jit(solution)/shard_map/ppermute | solution.py:444
  17.5 2.9 %collective-permute-start.2 = (f32[32,8,256]{2,1,0:T(8,128)}, f32[32,8,256]{2,1,0:T(8,128)}, u32[]{:S(2)}, u32[]{:S(2)}) collective-permute-start(f32[32,8,256]{2,1,0:T(8,128)} %get-tuple-element.29), channel_id=1, source_target_pairs={{0,30},{2,0},{4,2},{6,4},{8,6},{10,8},{12,10},{14,12},{16,14},{18,... | collective-permute-start | bytes 786440 | tf_op jit(solution)/shard_map/ppermute | solution.py:445
  20.4 0.7 collective-permute-start.4
  21.1 4.5 %forward_modes.1 = (f32[16,16,128]{2,1,0:T(8,128)}, f32[2,32,256]{2,1,0:T(8,128)S(1)}) custom-call(s32[1]{0:T(128)} %bitcast._, f32[32,64,256]{2,1,0:T(8,128)} %bitcast.35, bf16[2,128,256]{2,1,0:T(8,128)(2,1)} %constant.28.clone.y_top, bf16[2,128,256]{2,1,0:T(8,128)(2,1)} %constant.29.clone.y_rest, bf16[4,256,128]{2,1,0:T(8,128)(2,1)} %constant.30.clone.x_top, ...), custom_call_target="tpu_custom_call" | custom-call | flops 2000000000 | bytes 4194304 | tf_op jit(solution)/shard_map/forward_modes/pallas_call | solution.py:281
  25.6 1.2 %collective-permute-start = (f32[2,32,256]{2,1,0:T(8,128)S(1)}, f32[2,32,256]{2,1,0:T(8,128)S(1)}, u32[]{:S(2)}, u32[]{:S(2)}) collective-permute-start(f32[2,32,256]{2,1,0:T(8,128)S(1)} %get-tuple-element.26), channel_id=1, source_target_pairs={{0,1},{1,0},{2,3},{3,2},{4,5},{5,4},{6,7},{7,6},{8,9},{9,8},{10,11... | collective-permute-start | bytes 196616 | tf_op jit(solution)/shard_map/ppermute | solution.py:467
  26.8 4.1 %all-to-all-start = ((f32[32,8,128]{2,1,0:T(8,128)}), f32[32,8,128]{2,1,0:T(8,128)S(1)}, u32[]{:S(2)}, u32[]{:S(2)}) async-start(f32[32,8,128]{2,1,0:T(8,128)} %bitcast.2), calls=%async_computation | async-start | bytes 262144 | tf_op jit(solution)/shard_map/all_to_all | solution.py:484
  30.9 0.0 collective-permute-done.refs_8_
  30.9 1.7 %collective-permute-start.3 = (f32[32,16,256]{2,1,0:T(8,128)}, f32[32,16,256]{2,1,0:T(8,128)}, u32[]{:S(2)}, u32[]{:S(2)}) collective-permute-start(f32[32,16,256]{2,1,0:T(8,128)} %get-tuple-element.23), channel_id=1, source_target_pairs={{0,2},{2,4},{4,6},{6,8},{8,10},{10,12},{12,14},{14,16},{16,18},{18... | collective-permute-start | bytes 1572872 | tf_op jit(solution)/shard_map/ppermute | solution.py:444
  32.6 17.5 %collective-permute-done.2.refs_2_ = f32[32,8,256]{2,1,0:T(8,128)} collective-permute-done((f32[32,8,256]{2,1,0:T(8,128)}, f32[32,8,256]{2,1,0:T(8,128)}, u32[]{:S(2)}, u32[]{:S(2)}) %collective-permute-start.2) | collective-permute-done | bytes 262176 | tf_op jit(solution)/shard_map/ppermute | solution.py:445
  50.2 0.0 collective-permute-start.1
  50.2 5.5 %all-to-all-done = f32[32,8,128]{2,1,0:T(8,128)S(1)} async-done(((f32[32,8,128]{2,1,0:T(8,128)}), f32[32,8,128]{2,1,0:T(8,128)S(1)}, u32[]{:S(2)}, u32[]{:S(2)}) %all-to-all-start) | async-done | bytes 131104 | tf_op jit(solution)/shard_map/all_to_all | solution.py:484
  55.7 2.6 %filter_modes.1 = f32[256,128]{1,0:T(8,128)} custom-call(f32[256,128]{1,0:T(8,128)S(1)} %bitcast.9, f32[2,16,8,64]{3,2,1,0:T(8,128)S(1)} %copy-done, bf16[256,256]{1,0:T(8,128)(2,1)} %constant.32.clone.f_top, bf16[256,256]{1,0:T(8,128)(2,1)} %constant.33.clone.f_rest, bf16[512,128]{1,0:T(8,128)(2,1)} %constant.34.clone.i_top, ...), custom_call_target="tpu_custom_call" | custom-call | flops 200000000 | bytes 1048576 | tf_op jit(solution)/shard_map/filter_modes/pallas_call | solution.py:309
  58.3 4.4 %all-to-all-start.1 = ((f32[32,8,128]{2,1,0:T(8,128)}), f32[32,8,128]{2,1,0:T(8,128)S(1)}, u32[]{:S(2)}, u32[]{:S(2)}) async-start(f32[32,8,128]{2,1,0:T(8,128)} %bitcast.4), calls=%async_computation.1 | async-start | bytes 262144 | tf_op jit(solution)/shard_map/all_to_all | solution.py:486
  62.7 0.0 copy-start.9
  62.8 4.6 %mixed_planes.6 = (f32[32,16,256]{2,1,0:T(8,128)}, f32[32,16,256]{2,1,0:T(8,128)S(1)}, f32[32,16,256]{2,1,0:T(8,128)}) custom-call(f32[32,27]{1,0:T(8,128)} %weight.7, f32[32,32]{1,0:T(8,128)} %point.7, f32[32,64,256]{2,1,0:T(8,128)} %bitcast.36, f32[32,64,256]{2,1,0:T(8,128)} %bitcast.37, f32[32,64,256]{2,1,0:T(8,128)} %bitcast.38, ...), custom_call_target="tpu_custom_call" | custom-call | flops 200000000 | bytes 1048576 | tf_op jit(solution)/shard_map/mixed_planes/pallas_call | solution.py:361
  67.4 0.8 copy-done.5
  68.2 0.0 collective-permute-done.1.refs_1_
  68.2 1.6 %collective-permute-start.7 = (f32[32,16,256]{2,1,0:T(8,128)}, f32[32,16,256]{2,1,0:T(8,128)S(1)}, u32[]{:S(2)}, u32[]{:S(2)}) collective-permute-start(f32[32,16,256]{2,1,0:T(8,128)} %get-tuple-element.35), channel_id=1, source_target_pairs={{0,2},{2,4},{4,6},{6,8},{8,10},{10,12},{12,14},{14,16},{16,18},{18... | collective-permute-start | bytes 1572872 | tf_op jit(solution)/shard_map/ppermute | solution.py:444
  69.8 0.8 copy-done.3
  70.6 0.1 all-to-all-done.1
  70.7 1.0 %copy-done.2 = f32[32,16,256]{2,1,0:T(8,128)S(1)} copy-done((f32[32,16,256]{2,1,0:T(8,128)S(1)}, f32[32,16,256]{2,1,0:T(8,128)}, u32[]{:S(2)}) %copy-start.2) | copy-done | bytes 524312
  71.7 1.0 %copy-done.4 = f32[32,16,256]{2,1,0:T(8,128)S(1)} copy-done((f32[32,16,256]{2,1,0:T(8,128)S(1)}, f32[32,16,256]{2,1,0:T(8,128)}, u32[]{:S(2)}) %copy-start.4) | copy-done | bytes 524312
  72.8 1.0 %copy-done.6 = f32[32,16,256]{2,1,0:T(8,128)S(1)} copy-done((f32[32,16,256]{2,1,0:T(8,128)S(1)}, f32[32,16,256]{2,1,0:T(8,128)}, u32[]{:S(2)}) %copy-start.6) | copy-done | bytes 524312
  73.8 0.9 %copy-done.8 = f32[32,8,256]{2,1,0:T(8,128)S(1)} copy-done((f32[32,8,256]{2,1,0:T(8,128)S(1)}, f32[32,8,256]{2,1,0:T(8,128)}, u32[]{:S(2)}) %copy-start.8) | copy-done | bytes 262168
  74.8 4.3 %inverse_modes.1.base = f32[32,64,256]{2,1,0:T(8,128)} custom-call(s32[1]{0:T(128)} %bitcast._, f32[16,16,128]{2,1,0:T(8,128)S(1)} %bitcast.10, f32[32]{0:T(128)S(1)} %copy-done.9, bf16[2,128,512]{2,1,0:T(8,128)(2,1)} %constant.36.clone.x_top, bf16[2,128,512]{2,1,0:T(8,128)(2,1)} %constant.37.clone.x_rest, bf16[2,512,256]{2,1,0:T(8,128)(2,1)} %constant.38.clone.y_top, ...), custom_call_target="tpu_custom_call" | custom-call | flops 4000000000 | bytes 6291456 | tf_op jit(solution)/shard_map/inverse_modes/pallas_call | solution.py:326
  79.1 2.8 %collective-permute-done.7.low = f32[32,16,256]{2,1,0:T(8,128)S(1)} collective-permute-done((f32[32,16,256]{2,1,0:T(8,128)}, f32[32,16,256]{2,1,0:T(8,128)S(1)}, u32[]{:S(2)}, u32[]{:S(2)}) %collective-permute-start.7) | collective-permute-done | bytes 524320 | tf_op jit(solution)/shard_map/ppermute | solution.py:444
  81.9 3.0 %collective-permute-done.8.high = f32[32,16,256]{2,1,0:T(8,128)S(1)} collective-permute-done((f32[32,16,256]{2,1,0:T(8,128)}, f32[32,16,256]{2,1,0:T(8,128)S(1)}, u32[]{:S(2)}, u32[]{:S(2)}) %collective-permute-start.8) | collective-permute-done | bytes 524320 | tf_op jit(solution)/shard_map/ppermute | solution.py:445
  84.9 3.2 %finished_rows.1 = f32[32,64,256]{2,1,0:T(8,128)} custom-call(f32[32,64,256]{2,1,0:T(8,128)} %inverse_modes.1.base, f32[32,16,256]{2,1,0:T(8,128)S(1)} %collective-permute-done.7.low, f32[32,16,256]{2,1,0:T(8,128)S(1)} %collective-permute-done.8.high), custom_call_target="tpu_custom_call", output_to_operand_aliasing={{}: (0, {})} | custom-call | flops 100000000 | bytes 2097152 | tf_op jit(solution)/shard_map/finished_rows/pallas_call | solution.py:390
  (20 shorter events, 0.0 us)
Async XLA Ops:
  3.6 0.7 copy-start.7
  8.9 5.9 %copy-start.1 = (f32[32,16,256]{2,1,0:T(8,128)}, f32[32,16,256]{2,1,0:T(8,128)S(1)}, u32[]{:S(2)}) copy-start(f32[32,16,256]{2,1,0:T(8,128)S(1)} %get-tuple-element.30.refs_3_) | copy-start | bytes 1572868
  14.8 55.9 %collective-permute-start.5 = (f32[32,24,256]{2,1,0:T(8,128)}, f32[32,24,256]{2,1,0:T(8,128)S(1)}, u32[]{:S(2)}, u32[]{:S(2)}) collective-permute-start(f32[32,24,256]{2,1,0:T(8,128)} %get-tuple-element.33), channel_id=1, source_target_pairs={{0,2},{2,4},{4,6},{6,8},{8,10},{10,12},{12,14},{14,16},{16,18},{18... | collective-permute-start | bytes 2359304 | tf_op jit(solution)/shard_map/ppermute | solution.py:444
  17.5 53.2 %collective-permute-start.6 = (f32[32,24,256]{2,1,0:T(8,128)}, f32[32,24,256]{2,1,0:T(8,128)S(1)}, u32[]{:S(2)}, u32[]{:S(2)}) collective-permute-start(f32[32,24,256]{2,1,0:T(8,128)} %get-tuple-element.34), channel_id=1, source_target_pairs={{0,30},{2,0},{4,2},{6,4},{8,6},{10,8},{12,10},{14,12},{16,14},{18,... | collective-permute-start | bytes 2359304 | tf_op jit(solution)/shard_map/ppermute | solution.py:445
  17.5 32.7 %collective-permute-start.2 = (f32[32,8,256]{2,1,0:T(8,128)}, f32[32,8,256]{2,1,0:T(8,128)}, u32[]{:S(2)}, u32[]{:S(2)}) collective-permute-start(f32[32,8,256]{2,1,0:T(8,128)} %get-tuple-element.29), channel_id=1, source_target_pairs={{0,30},{2,0},{4,2},{6,4},{8,6},{10,8},{12,10},{14,12},{16,14},{18,... | collective-permute-start | bytes 786440 | tf_op jit(solution)/shard_map/ppermute | solution.py:445
  20.4 49.5 %collective-permute-start.4 = (f32[32,16,256]{2,1,0:T(8,128)}, f32[32,16,256]{2,1,0:T(8,128)S(1)}, u32[]{:S(2)}, u32[]{:S(2)}) collective-permute-start(f32[32,16,256]{2,1,0:T(8,128)} %get-tuple-element.31), channel_id=1, source_target_pairs={{0,30},{2,0},{4,2},{6,4},{8,6},{10,8},{12,10},{14,12},{16,14},{18,... | collective-permute-start | bytes 1572872 | tf_op jit(solution)/shard_map/ppermute | solution.py:445
  21.1 29.1 %copy-start.10 = (f32[32,8,256]{2,1,0:T(8,128)S(1)}, f32[32,8,256]{2,1,0:T(8,128)}, u32[]{:S(2)}) copy-start(f32[32,8,256]{2,1,0:T(8,128)} %get-tuple-element.21) | copy-start | bytes 786436
  21.1 34.7 %copy-start = (f32[2,16,8,64]{3,2,1,0:T(8,128)S(1)}, f32[2,16,8,64]{3,2,1,0:T(8,128)}, u32[]{:S(2)}) copy-start(f32[2,16,8,64]{3,2,1,0:T(8,128)} %gains.1) | copy-start | bytes 196612
  25.6 5.3 %collective-permute-start = (f32[2,32,256]{2,1,0:T(8,128)S(1)}, f32[2,32,256]{2,1,0:T(8,128)S(1)}, u32[]{:S(2)}, u32[]{:S(2)}) collective-permute-start(f32[2,32,256]{2,1,0:T(8,128)S(1)} %get-tuple-element.26), channel_id=1, source_target_pairs={{0,1},{1,0},{2,3},{3,2},{4,5},{5,4},{6,7},{7,6},{8,9},{9,8},{10,11... | collective-permute-start | bytes 196616 | tf_op jit(solution)/shard_map/ppermute | solution.py:467
  26.8 29.0 %all-to-all-start = ((f32[32,8,128]{2,1,0:T(8,128)}), f32[32,8,128]{2,1,0:T(8,128)S(1)}, u32[]{:S(2)}, u32[]{:S(2)}) async-start(f32[32,8,128]{2,1,0:T(8,128)} %bitcast.2), calls=%async_computation | async-start | bytes 262144 | tf_op jit(solution)/shard_map/all_to_all | solution.py:484
  30.9 39.8 %collective-permute-start.3 = (f32[32,16,256]{2,1,0:T(8,128)}, f32[32,16,256]{2,1,0:T(8,128)}, u32[]{:S(2)}, u32[]{:S(2)}) collective-permute-start(f32[32,16,256]{2,1,0:T(8,128)} %get-tuple-element.23), channel_id=1, source_target_pairs={{0,2},{2,4},{4,6},{6,8},{8,10},{10,12},{12,14},{14,16},{16,18},{18... | collective-permute-start | bytes 1572872 | tf_op jit(solution)/shard_map/ppermute | solution.py:444
  50.2 18.0 %collective-permute-start.1 = (f32[32,8,256]{2,1,0:T(8,128)S(1)}, f32[32,8,256]{2,1,0:T(8,128)}, u32[]{:S(2)}, u32[]{:S(2)}) collective-permute-start(f32[32,8,256]{2,1,0:T(8,128)S(1)} %copy-done.10), channel_id=1, source_target_pairs={{0,2},{2,4},{4,6},{6,8},{8,10},{10,12},{12,14},{14,16},{16,18},{18... | collective-permute-start | bytes 786440 | tf_op jit(solution)/shard_map/ppermute | solution.py:444
  58.3 12.4 %all-to-all-start.1 = ((f32[32,8,128]{2,1,0:T(8,128)}), f32[32,8,128]{2,1,0:T(8,128)S(1)}, u32[]{:S(2)}, u32[]{:S(2)}) async-start(f32[32,8,128]{2,1,0:T(8,128)} %bitcast.4), calls=%async_computation.1 | async-start | bytes 262144 | tf_op jit(solution)/shard_map/all_to_all | solution.py:486
  62.7 7.9 %copy-start.9 = (f32[32]{0:T(128)S(1)}, f32[32]{0:T(128)}, u32[]{:S(2)}) copy-start(f32[32]{0:T(128)} %bias.1) | copy-start | bytes 388
  67.4 0.8 copy-start.5
  68.2 13.7 %collective-permute-start.7 = (f32[32,16,256]{2,1,0:T(8,128)}, f32[32,16,256]{2,1,0:T(8,128)S(1)}, u32[]{:S(2)}, u32[]{:S(2)}) collective-permute-start(f32[32,16,256]{2,1,0:T(8,128)} %get-tuple-element.35), channel_id=1, source_target_pairs={{0,2},{2,4},{4,6},{6,8},{8,10},{10,12},{12,14},{14,16},{16,18},{18... | collective-permute-start | bytes 1572872 | tf_op jit(solution)/shard_map/ppermute | solution.py:444
  69.8 0.8 copy-start.3
  70.6 14.3 %collective-permute-start.8 = (f32[32,16,256]{2,1,0:T(8,128)}, f32[32,16,256]{2,1,0:T(8,128)S(1)}, u32[]{:S(2)}, u32[]{:S(2)}) collective-permute-start(f32[32,16,256]{2,1,0:T(8,128)} %get-tuple-element.36), channel_id=1, source_target_pairs={{0,30},{2,0},{4,2},{6,4},{8,6},{10,8},{12,10},{14,12},{16,14},{18,... | collective-permute-start | bytes 1572872 | tf_op jit(solution)/shard_map/ppermute | solution.py:445
  70.7 1.0 %copy-start.2 = (f32[32,16,256]{2,1,0:T(8,128)S(1)}, f32[32,16,256]{2,1,0:T(8,128)}, u32[]{:S(2)}) copy-start(f32[32,16,256]{2,1,0:T(8,128)} %copy-done.1) | copy-start | bytes 1572868
  71.7 1.0 %copy-start.4 = (f32[32,16,256]{2,1,0:T(8,128)S(1)}, f32[32,16,256]{2,1,0:T(8,128)}, u32[]{:S(2)}) copy-start(f32[32,16,256]{2,1,0:T(8,128)} %copy-done.3) | copy-start | bytes 1572868
  72.8 1.0 %copy-start.6 = (f32[32,16,256]{2,1,0:T(8,128)S(1)}, f32[32,16,256]{2,1,0:T(8,128)}, u32[]{:S(2)}) copy-start(f32[32,16,256]{2,1,0:T(8,128)} %copy-done.5) | copy-start | bytes 1572868
  73.8 0.9 %copy-start.8 = (f32[32,8,256]{2,1,0:T(8,128)S(1)}, f32[32,8,256]{2,1,0:T(8,128)}, u32[]{:S(2)}) copy-start(f32[32,8,256]{2,1,0:T(8,128)} %copy-done.7) | copy-start | bytes 786436

commit v3 on v2

v3 whole, which is shorter than its diff:
```python
import functools
import math

import jax
import jax.numpy as jnp
import ml_dtypes
import numpy as np
from jax import lax
from jax.experimental import pallas as pl
from jax.experimental.pallas import tpu as pltpu
from jax.sharding import PartitionSpec as P

NX = 256
MX = 32
MY = 16
MZ = 16
CH = 32
VMEM_BYTES = 24 * 1024 * 1024
BF = jnp.bfloat16
F32 = jnp.float32


def kept(count, total):
    series = np.arange(count)
    return np.where(series < count // 2, series, total - count + series)


def trig(freqs, places, total):
    angle = 2.0 * np.pi * ((freqs[:, None] * places[None, :]) % total) / total
    return np.cos(angle), np.sin(angle)


def halves(table):
    table = np.asarray(table, np.float64)
    top = table.astype(np.float32).astype(ml_dtypes.bfloat16)
    rest = (table - top.astype(np.float64)).astype(np.float32).astype(ml_dtypes.bfloat16)
    return jnp.asarray(top), jnp.asarray(rest)


def y_forward_table(y_local, gy, group):
    out = np.zeros((gy, 2, group, MY, group, y_local))
    for g in range(gy):
        c, s = trig(kept(MY, y_local * gy), g * y_local + np.arange(y_local), y_local * gy)
        for i in range(group):
            out[g, 0, i, :, i] = c
            out[g, 1, i, :, i] = s
    return out.reshape(gy, 2 * group * MY, group * y_local)


def x_forward_table():
    c, s = trig(np.arange(MX), np.arange(NX), NX)
    out = np.zeros((2, 2, NX, 2, 2, MX))
    for p in range(2):
        out[p, 0, :, p, 0] = c.T
        out[p, 0, :, p, 1] = -s.T
        out[p, 1, :, p, 0] = -s.T
        out[p, 1, :, p, 1] = -c.T
    return out.reshape(4, NX, 4 * MX)


def x_inverse_table(scale):
    c, s = trig(np.arange(MX), np.arange(NX), NX)
    w = np.where(np.arange(MX) == 0, 1.0, 2.0)[:, None] * scale
    out = np.zeros((2, 2, 2, MX, 2, NX))
    for p in range(2):
        out[p, p, 0, :, 0] = w * c
        out[p, p, 1, :, 0] = -w * s
        out[p, p, 0, :, 1] = w * s
        out[p, p, 1, :, 1] = w * c
    return out.reshape(2, 4 * MX, 2 * NX)


def y_inverse_table(y_local, gy, group):
    out = np.zeros((gy, group, y_local, 2, group, MY))
    for g in range(gy):
        c, s = trig(kept(MY, y_local * gy), g * y_local + np.arange(y_local), y_local * gy)
        for i in range(group):
            out[g, i, :, 0, i] = c.T
            out[g, i, :, 1, i] = -s.T
    return out.reshape(gy, group * y_local, 2 * group * MY)


def z_tables(gz, gy, rows, scale):
    c, s = trig(kept(MZ, gz), np.arange(gz), gz)
    eye = np.eye(rows)
    one = np.ones(gy)
    both = np.stack([c, s])
    fwd = np.einsum("tqz,g,jk->tqjzgk", both, one, eye) * scale
    inv = np.einsum("tqz,g,jk->tzgjqk", both, one, eye)
    return fwd.reshape(2 * MZ * rows, gz * gy * rows), inv.reshape(2 * gz * gy * rows, MZ * rows)


def parts(value):
    top = value.astype(BF)
    return top, (value - top.astype(F32)).astype(BF)


def dot(a, b):
    return jnp.dot(a, b, preferred_element_type=F32)


def dot3(a, b):
    rows = a[0].shape[0]
    both = dot(jnp.concatenate([a[0], a[1]], axis=0), b[0])
    return both[:rows] + (both[rows:] + dot(a[0], b[1]))


def forward_kernel(group, field, y_top, y_rest, x_top, x_rest, out, turned):
    gy = lax.axis_index("gy")
    y_table = (y_top[gy], y_rest[gy])
    half = group * MY
    step = pl.program_id(0)
    for p in range(2):
        rows = jnp.concatenate([field[2 * i + p] for i in range(group)], axis=0)
        both = dot3(y_table, parts(rows))
        for t in range(2):
            at = pl.multiple_of(step * half, half)
            turned[2 * p + t, pl.ds(at, half), :] = both[t * half : (t + 1) * half]
    @pl.when(step == pl.num_programs(0) - 1)
    def _():
        total = dot3(parts(turned[0]), (x_top[0], x_rest[0]))
        for k in range(1, 4):
            total = total + dot3(parts(turned[k]), (x_top[k], x_rest[k]))
        out[...] = total.reshape(CH // 2, MY, 4 * MX)


def swap_parts(value):
    lane = lax.broadcasted_iota(jnp.int32, value.shape, 1)
    is_real = (lane // MX) % 2 == 0
    return jnp.where(is_real, pltpu.roll(value, 4 * MX - MX, 1), pltpu.roll(value, MX, 1)), is_real


def filter_kernel(arrived, gains, f_top, f_rest, i_top, i_rest, out):
    real, imag = (gains[r].reshape(-1, 2 * MX) for r in range(2))
    first, second = slice(0, MX), slice(MX, 2 * MX)
    same = jnp.concatenate([real[:, first], real[:, first], real[:, second], real[:, second]], axis=1)
    cross = jnp.concatenate([-imag[:, first], imag[:, first], -imag[:, second], imag[:, second]], axis=1)
    half = f_top.shape[0] // 2
    turned = dot3((f_top[...], f_rest[...]), parts(arrived[...]))
    crossed, is_real = swap_parts(turned[half:])
    modes = turned[:half] + jnp.where(is_real, crossed, -crossed)
    crossed, _ = swap_parts(modes)
    filtered = modes * same + crossed * cross
    half = i_top.shape[0] // 2
    back = dot3((i_top[...], i_rest[...]), parts(filtered))
    crossed, is_real = swap_parts(back[half:])
    out[...] = back[:half] + jnp.where(is_real, -crossed, crossed)


def conv_kernel(plan, weight, point, field, *refs):
    offsets, tiles, outer, with_edges = plan
    last = field.shape[1] // 8 - 1
    if outer:
        halo, refs = refs[0], refs[1:]
    count = len(offsets)
    outs, refs = refs[:count], refs[count:]
    if with_edges:
        edges_out, refs = refs[0], refs[1:]
    taken, halo_rows, weights, points, edges, sent, turned, depth, gains, sem_in, sem_out, sem_few = refs
    wanted = [0, 1, last - 1, last] if outer else list(range(tiles[0] - 1, tiles[-1] + 2))
    if with_edges:
        wanted += [t for t in (0, last) if t not in wanted]
    few = [
        pltpu.make_async_copy(weight, weights, sem_few.at[0]),
        pltpu.make_async_copy(point, points, sem_few.at[1]),
    ]
    if outer:
        few.append(pltpu.make_async_copy(halo, halo_rows, sem_few.at[2]))
    for copy in few:
        copy.start()
    pending = {}
    for k, t in enumerate(wanted):
        pending[t] = [
            pltpu.make_async_copy(
                field.at[:, pl.ds(8 * t, 8), pl.ds(128 * h, 128)], taken.at[k, h], sem_in.at[k, h]
            )
            for h in range(2)
        ]
        for copy in pending[t]:
            copy.start()
    for copy in few:
        copy.wait()
    for k in offsets:
        for j in range(9):
            gains[9 * k + j] = jnp.broadcast_to(weights[:, 9 * k + j : 9 * k + j + 1], (CH, 128))

    down = (
        lax.broadcasted_iota(jnp.int32, (8 * CH, CH), 0) // 8
        == lax.broadcasted_iota(jnp.int32, (8 * CH, CH), 1)
    ).astype(BF)
    across = (
        lax.broadcasted_iota(jnp.int32, (CH, 8 * CH), 1) % CH
        == lax.broadcasted_iota(jnp.int32, (CH, 8 * CH), 0)
    ).astype(BF)
    same = (
        lax.broadcasted_iota(jnp.int32, (8 * CH, 8 * CH), 0) % 8
        == lax.broadcasted_iota(jnp.int32, (8 * CH, 8 * CH), 1) // CH
    )
    mix = tuple(
        jnp.where(same, dot(dot(down, part).astype(BF), across), 0.0).astype(BF)
        for part in parts(points[...])
    )

    def row(t, r):
        for copy in pending.pop(t, ()):
            copy.wait()
        k = wanted.index(t)
        return jnp.concatenate(
            [taken.at[k, h].reshape(CH * 8, 128)[pl.ds(r, CH, stride=8), :] for h in range(2)], axis=1
        )

    if outer:
        segments = [
            [None, *[(0, r) for r in range(8)], (1, 0)],
            [(last - 1, 7), *[(last, r) for r in range(8)], None],
        ]
    else:
        segments = [
            [(tiles[0] - 1, 7), *[(t, r) for t in tiles for r in range(8)], (tiles[-1] + 1, 0)]
        ]
    runs, at, done = [], 0, 0
    for side, places in enumerate(segments):
        for i, place in enumerate(places):
            value = halo_rows[side] if place is None else row(*place)
            turned[0, at + i] = pltpu.roll(value, 1, 1)
            turned[1, at + i] = value
            turned[2, at + i] = pltpu.roll(value, NX - 1, 1)
        runs.append((at, done, len(places) - 2))
        at, done = at + len(places), done + len(places) - 2
    copies = []
    if with_edges:
        edges[0] = row(last, 7)
        edges[1] = row(0, 0)
        copies.append(pltpu.make_async_copy(edges, edges_out, sem_few.at[3]))
        copies[-1].start()

    def taps(i, _):
        chans = pl.ds(pl.multiple_of(i * 8, 8), 8)
        gain = {k: gains[k, chans, :] for a in offsets for k in range(9 * a, 9 * a + 9)}
        for h in range(2):
            lanes = pl.ds(128 * h, 128)
            for first, to, rows in runs:
                sums = {}
                for r in range(rows + 2):
                    values = [turned[e, first + r, chans, lanes] for e in range(3)]
                    for b in range(3):
                        o = r - b
                        if o < 0 or o >= rows:
                            continue
                        for a in offsets:
                            for e in range(3):
                                term = gain[a * 9 + b * 3 + e] * values[e]
                                sums[o, a] = sums[o, a] + term if (o, a) in sums else term
                    if r >= 2:
                        for k, a in enumerate(offsets):
                            depth[k, to + r - 2, chans, lanes] = sums.pop((r - 2, a))
        return 0

    lax.fori_loop(0, CH // 8, taps, 0)

    for t in range(done // 8):
        rows = pl.ds(8 * t, 8)
        for k, out in enumerate(outs):
            tile = depth[k, rows].reshape(8 * CH, NX)
            sent[k, t] = dot3(mix, parts(tile)).reshape(CH, 8, NX)
            copies.append(pltpu.make_async_copy(sent.at[k, t], out.at[:, rows, :], sem_out.at[k, t]))
            copies[-1].start()
    for copies_of in (copies, *pending.values()):
        for copy in copies_of:
            copy.wait()


def gelu(value):
    return 0.5 * value * (1.0 + lax.erf(value * (1.0 / math.sqrt(2.0))))


def inverse_kernel(group, chunks, modes, bias, x_top, x_rest, y_top, y_rest, outer, *refs):
    out, base = refs[-2:]
    step = pl.program_id(0)
    gy = lax.axis_index("gy")
    y_table = (y_top[gy], y_rest[gy])
    mode_rows = parts(modes[...].reshape(group * MY, 4 * MX))
    y_local = out.shape[1]
    for p in range(2):
        wide = dot3(mode_rows, (x_top[p], x_rest[p]))
        tall = jnp.concatenate([wide[:, :NX], wide[:, NX:]], axis=0)
        planes = dot3(y_table, parts(tall)).reshape(group, y_local, NX)
        for i in range(group):
            c = 2 * i + p
            plane = planes[i] + bias[step * 2 * group + c]
            base[c, :8] = plane[:8] + outer[c, :8]
            base[c, 8:] = plane[y_local - 8 :] + outer[c, 8:]
            for k, (first, count) in enumerate(chunks):
                rows = slice(8 * first, 8 * (first + count))
                own, low, high = refs[3 * k : 3 * k + 3]
                out[c, rows] = gelu(plane[rows] + (own[c] + (low[c] + high[c])))


def finish_kernel(_, base, low, high, out):
    out[...] = gelu(base[...] + (low[...] + high[...]))


def in_hbm(*arrays):
    return [pltpu.with_memory_space_constraint(a, pltpu.HBM) for a in arrays]


def params():
    return pltpu.CompilerParams(vmem_limit_bytes=VMEM_BYTES)


def cost(flops, moved):
    return pl.CostEstimate(flops=flops, bytes_accessed=moved, transcendentals=0)


def whole_block(table):
    return pl.BlockSpec(table.shape, lambda i: (0,) * table.ndim)


def forward_call(field, gy):
    y_local = field.shape[1]
    group = max(1, min(CH // 2, 256 // y_local))
    tables = [*halves(y_forward_table(y_local, gy, group)), *halves(x_forward_table())]
    return pl.pallas_call(
        functools.partial(forward_kernel, group),
        out_shape=jax.ShapeDtypeStruct((CH // 2, MY, 4 * MX), F32),
        grid=(CH // 2 // group,),
        in_specs=[
            pl.BlockSpec((2 * group, y_local, NX), lambda i: (i, 0, 0)),
            *[whole_block(t) for t in tables],
        ],
        out_specs=pl.BlockSpec((CH // 2, MY, 4 * MX), lambda i: (0, 0, 0)),
        scratch_shapes=[pltpu.VMEM((4, CH // 2 * MY, NX), F32)],
        compiler_params=params(),
        cost_estimate=cost(10**8, 2**18),
        name="forward_modes",
    )(*in_hbm(field, *tables))


def filter_call(arrived, gains, gz, gy, scale):
    fwd, inv = z_tables(gz, gy, gains.shape[2], scale)
    fwd, inv = halves(fwd), halves(inv)
    return pl.pallas_call(
        filter_kernel,
        out_shape=jax.ShapeDtypeStruct(arrived.shape, F32),
        compiler_params=params(),
        cost_estimate=cost(10**8, 2**18),
        name="filter_modes",
    )(arrived, gains, *in_hbm(*fwd, *inv))


def inverse_call(modes, bias, outer, inner, chunks, y_local, gy, scale):
    group = 4
    tables = [*halves(x_inverse_table(scale)), *halves(y_inverse_table(y_local, gy, group))]
    some = lambda rows: pl.BlockSpec((2 * group, rows, NX), lambda i: (i, 0, 0))
    return pl.pallas_call(
        functools.partial(inverse_kernel, group, chunks),
        out_shape=[
            jax.ShapeDtypeStruct((CH, y_local, NX), F32),
            jax.ShapeDtypeStruct((CH, 16, NX), F32),
        ],
        grid=(CH // 2 // group,),
        in_specs=[
            pl.BlockSpec((group, MY, 4 * MX), lambda i: (i, 0, 0)),
            pl.BlockSpec(memory_space=pltpu.SMEM),
            *[whole_block(t) for t in tables],
            some(16),
            *[some(8 * count) for _, count in chunks for _ in range(3)],
        ],
        out_specs=[some(y_local), some(16)],
        compiler_params=params(),
        cost_estimate=cost(10**8, 2**18),
        name="inverse_modes",
    )(modes, bias, *in_hbm(*tables), outer, *inner)


def conv_call(field, weight, point, offsets, tiles, halo=None, with_edges=False):
    outer = halo is not None
    rows, count = 8 * len(tiles), len(offsets)
    hbm = pl.BlockSpec(memory_space=pltpu.HBM)
    operands = in_hbm(weight, point, field)
    shapes = [pltpu.HBM((CH, rows, NX), F32)] * count
    if outer:
        operands += in_hbm(halo)
    if with_edges:
        shapes.append(pltpu.HBM((2, CH, NX), F32))
    fetched = len(tiles) + 4
    return pl.pallas_call(
        functools.partial(conv_kernel, (offsets, tiles, outer, with_edges)),
        out_shape=shapes,
        in_specs=[hbm] * len(operands),
        out_specs=[hbm] * len(shapes),
        scratch_shapes=[
            pltpu.VMEM((fetched, 2, CH, 8, 128), F32),
            pltpu.VMEM((2, CH, NX), F32),
            pltpu.VMEM((CH, 27), F32),
            pltpu.VMEM((CH, CH), F32),
            pltpu.VMEM((2, CH, NX), F32),
            pltpu.VMEM((count, len(tiles), CH, 8, NX), F32),
            pltpu.VMEM((3, rows + 4, CH, NX), F32),
            pltpu.VMEM((count, rows, CH, NX), F32),
            pltpu.VMEM((27, CH, 128), F32),
            pltpu.SemaphoreType.DMA((fetched, 2)),
            pltpu.SemaphoreType.DMA((count, len(tiles))),
            pltpu.SemaphoreType.DMA((4,)),
        ],
        compiler_params=params(),
        cost_estimate=cost(10**8, 2**18),
        name="mixed_planes",
    )(*operands)


def finish_call(result, base, low, high):
    last = result.shape[1] // 8 - 1
    piece = pl.BlockSpec((CH, 8, NX), lambda i: (0, i, 0))
    return pl.pallas_call(
        finish_kernel,
        out_shape=jax.ShapeDtypeStruct(result.shape, F32),
        grid=(2,),
        in_specs=[pl.BlockSpec(memory_space=pl.ANY), piece, piece, piece],
        out_specs=pl.BlockSpec((CH, 8, NX), lambda i: (0, i * last, 0)),
        input_output_aliases={0: 0},
        compiler_params=params(),
        cost_estimate=cost(10**8, 2**18),
        name="finished_rows",
    )(result, base, low, high)


def general_filter(coarse, gains, gz, gy, scale):
    j_own, n_own = gains.shape[2], gains.shape[3]
    both = ("gz", "gy")
    flat = coarse.reshape(CH // 2, MY, 2, 2, MX).transpose(3, 1, 0, 2, 4).reshape(2, MY, CH * MX)
    sent = flat.reshape(2, gy, j_own, gz, n_own).transpose(3, 1, 0, 2, 4).reshape(gz * gy, -1)
    got = lax.all_to_all(sent, both, split_axis=0, concat_axis=0, tiled=True)
    got = got.reshape(gz, gy, 2, j_own, n_own)
    c, s = (jnp.asarray(t, F32) for t in trig(kept(MZ, gz), np.arange(gz), gz))
    mul = functools.partial(jnp.einsum, precision=lax.Precision.HIGHEST)
    whole = got.sum(axis=1) * scale
    real = mul("zjn,qz->qjn", whole[:, 0], c) + mul("zjn,qz->qjn", whole[:, 1], s)
    imag = mul("zjn,qz->qjn", whole[:, 1], c) - mul("zjn,qz->qjn", whole[:, 0], s)
    real, imag = real * gains[0] - imag * gains[1], real * gains[1] + imag * gains[0]
    out = jnp.stack(
        [
            mul("qjn,qz->zjn", real, c) - mul("qjn,qz->zjn", imag, s),
            mul("qjn,qz->zjn", real, s) + mul("qjn,qz->zjn", imag, c),
        ],
        axis=1,
    )
    out = jnp.broadcast_to(out[:, None], (gz, gy, 2, j_own, n_own)).reshape(gz * gy, -1)
    back = lax.all_to_all(out, both, split_axis=0, concat_axis=0, tiled=True)
    back = back.reshape(gz, gy, 2, j_own, n_own).transpose(2, 1, 3, 0, 4)
    back = back.reshape(2, MY, CH // 2, 2, MX)
    return back.transpose(2, 1, 3, 0, 4).reshape(CH // 2, MY, 4 * MX)


def body(field, spectral_filter, depth_weight, point_weight, bias_vector):
    gz, gy = lax.axis_size("gz"), lax.axis_size("gy")
    y_local = field.shape[2]
    field = field.reshape(CH, y_local, NX)
    y_total = gy * y_local
    forward_scale = 1.0 / math.sqrt(float(NX) * y_total * gz)
    inverse_scale = 1.0 / math.sqrt(2.0 * MX * MY * MZ)

    def ring(axis, count, by):
        return [(i, (i + by) % count) for i in range(count)]

    def to_neighbours(down, up):
        return (
            lax.ppermute(down, "gz", ring("gz", gz, 1)),
            lax.ppermute(up, "gz", ring("gz", gz, -1)),
        )

    def after(value, *others):
        return lax.optimization_barrier((value, *others))[0]

    tiles = y_local // 8
    middle = 1 + (tiles - 1) // 2
    spans = [tuple(range(1, middle)), tuple(range(middle, tiles - 1))]
    chunks = [(span[0], len(span)) for span in spans if span]
    conv = functools.partial(conv_call, weight=depth_weight, point=point_weight)

    down, up, edges = conv(field, offsets=(0, 2), tiles=spans[0], with_edges=True)
    first_pair = to_neighbours(down, up)
    if gy == 2:
        halo = lax.ppermute(edges, "gy", ring("gy", gy, 1))
    else:
        halo = jnp.stack(
            [
                lax.ppermute(edges[0], "gy", ring("gy", gy, 1)),
                lax.ppermute(edges[1], "gy", ring("gy", gy, -1)),
            ]
        )
    coarse = forward_call(after(field, down), gy)
    second = []
    mark = coarse
    if spans[1]:
        down, own, up = conv(after(field, coarse), offsets=(0, 1, 2), tiles=spans[1])
        second = [own, *to_neighbours(down, up)]
        mark = down

    j_own, n_own = spectral_filter.shape[2], spectral_filter.shape[3]
    if j_own == 8 and n_own == 2 * MX:
        both = ("gz", "gy")
        sent = coarse.reshape(gz * gy * 8, 4 * MX)
        got = lax.all_to_all(sent, both, split_axis=0, concat_axis=0, tiled=True)
        out = filter_call(got, after(spectral_filter, mark), gz, gy, forward_scale)
        back = lax.all_to_all(out, both, split_axis=0, concat_axis=0, tiled=True)
        back = back.reshape(CH // 2, MY, 4 * MX)
        mark = out
    else:
        back = general_filter(coarse, spectral_filter, gz, gy, forward_scale)

    down, outer, up = conv(after(field, mark), offsets=(0, 1, 2), tiles=(0, tiles - 1), halo=halo)
    outer_pair = to_neighbours(down, up)
    (own,) = conv(after(field, down), offsets=(1,), tiles=spans[0])
    inner = [own, *first_pair, *second]
    result, base = inverse_call(
        back, bias_vector, outer, inner, chunks, y_local, gy, inverse_scale
    )
    result = finish_call(result, base, *outer_pair)
    return result.reshape(CH, 1, y_local, NX)


def solution(mesh):
    in_specs = (P(None, "gz", "gy", None), P(None, None, "gy", "gz"), P(), P(), P())
    out_specs = P(None, "gz", "gy", None)
    return jax.shard_map(body, mesh=mesh, in_specs=in_specs, out_specs=out_specs, check_vma=False)
```

time: 88.8 us -> 69.7 us (0.78)
  waiting for transfers between devices: 28.9 us -> 4.7 us
  starting transfers between devices: 19.4 us -> 26.5 us
  local copies, waits for them, and re-layouts: 6.39 us -> 2.8 us
  Pallas kernels: 33.3 us -> 34.5 us
    ppermute x4 -> x3, waiting for transfers between devices: 20.6 us -> 0.01 us  [to_neighbours(): lax.ppermute(up, 'gz', ring('gz', gz, -1))]
    all_to_all x1, waiting for transfers between devices: 5.55 us -> 0.01 us  [body(): got = lax.all_to_all(sent, both, split_axis=0, concat_axis=0, tiled=True)]
    all_to_all x1, starting transfers between devices: 4.44 us -> 9.14 us  [body(): back = lax.all_to_all(out, both, split_axis=0, concat_axis=0, tiled=True)]
    all_to_all x1, waiting for transfers between devices: 0.05 us -> 4.68 us  [body(): back = lax.all_to_all(out, both, split_axis=0, concat_axis=0, tiled=True)]
    all_to_all x1, starting transfers between devices: 4.13 us -> 8.26 us  [body(): got = lax.all_to_all(sent, both, split_axis=0, concat_axis=0, tiled=True)]
    unnamed x22 -> x14, local copies, waits for them, and re-layouts: 6.39 us -> 2.8 us
    ppermute x4 -> x3, waiting for transfers between devices: 2.77 us -> 0.01 us  [to_neighbours(): lax.ppermute(down, 'gz', ring('gz', gz, 1))]
    ppermute x4 -> x3, starting transfers between devices: 5.99 us -> 4.13 us  [to_neighbours(): lax.ppermute(down, 'gz', ring('gz', gz, 1))]
  transfers between devices with their start and end apart: 11 -> 9, of which waited for: 4 -> 1; matrix products, arithmetic and copies ran while one was open for 0% -> 0% of each run, Pallas kernels for 18% -> 40%
where the time goes in v3:
time: 69.7 us; the launch traced here: 68.6 us
  Pallas kernels  34.5 us (49%)
  starting transfers between devices  26.5 us (38%)
  waiting for transfers between devices  4.7 us (7%)
  local copies, waits for them, and re-layouts  2.8 us (4%)
    pallas_call x4, Pallas kernels, conv_call(): pl.pallas_call(functools.partial(conv_kernel, (offsets, tiles, outer, wit...  20.4 us
    all_to_all x1, starting transfers between devices, body(): back = lax.all_to_all(out, both, split_axis=0, concat_axis=0, tiled=True)  9.14 us
    all_to_all x1, starting transfers between devices, body(): got = lax.all_to_all(sent, both, split_axis=0, concat_axis=0, tiled=True)  8.26 us
    pallas_call x1, Pallas kernels, inverse_call(): pl.pallas_call(functools.partial(inverse_kernel, group, chunks), out_shap...  5 us
    all_to_all x1, waiting for transfers between devices, body(): back = lax.all_to_all(out, both, split_axis=0, concat_axis=0, tiled=True)  4.68 us
    pallas_call x1, Pallas kernels, forward_call(): pl.pallas_call(functools.partial(forward_kernel, group), out_shape=jax.Sh...  4.43 us
    ppermute x3, starting transfers between devices, to_neighbours(): lax.ppermute(down, 'gz', ring('gz', gz, 1))  4.13 us
    ppermute x3, starting transfers between devices, to_neighbours(): lax.ppermute(up, 'gz', ring('gz', gz, -1))  3.59 us
  transfers between devices with their start and end apart: 9, of which 1 were waited for; matrix products, arithmetic and copies ran while one was open for 0% of the time, Pallas kernels for 40%

profile of v3, /device:TPU:1, one launch (start us, length us, event | category | flops | bytes accessed | tf_op | source)
XLA Modules:
  0.0 68.6 jit_solution(17490966237042227716)
XLA Ops:
  0.0 5.2 %mixed_planes.4 = (f32[32,24,256]{2,1,0:T(8,128)}, f32[32,24,256]{2,1,0:T(8,128)}, f32[2,32,256]{2,1,0:T(8,128)}) custom-call(f32[32,27]{1,0:T(8,128)} %weight.7, f32[32,32]{1,0:T(8,128)} %point.7, f32[32,64,256]{2,1,0:T(8,128)} %bitcast.10), custom_call_target="tpu_custom_call" | custom-call | flops 100000000 | bytes 262144 | tf_op jit(solution)/shard_map/mixed_planes/pallas_call | solution.py:387
  5.3 0.1 collective-permute-start.2
  5.4 2.7 %collective-permute-start.1 = (f32[32,24,256]{2,1,0:T(8,128)}, f32[32,24,256]{2,1,0:T(8,128)S(1)}, u32[]{:S(2)}, u32[]{:S(2)}) collective-permute-start(f32[32,24,256]{2,1,0:T(8,128)} %get-tuple-element.21), channel_id=1, source_target_pairs={{0,2},{2,4},{4,6},{6,8},{8,10},{10,12},{12,14},{14,16},{16,18},{18... | collective-permute-start | bytes 2359304 | tf_op jit(solution)/shard_map/ppermute | solution.py:468
  8.0 4.4 %forward_modes.1 = f32[16,16,128]{2,1,0:T(8,128)} custom-call(f32[32,64,256]{2,1,0:T(8,128)} %bitcast.11, bf16[2,128,256]{2,1,0:T(8,128)(2,1)} %constant.24.clone.y_top, bf16[2,128,256]{2,1,0:T(8,128)(2,1)} %constant.25.clone.y_rest, bf16[4,256,128]{2,1,0:T(8,128)(2,1)} %constant.26.clone.x_top, bf16[4,256,128]{2,1,0:T(8,128)(2,1)} %constant.27.clone.x_rest), custom_call_target="tpu_custom_call" | custom-call | flops 100000000 | bytes 262144 | tf_op jit(solution)/shard_map/forward_modes/pallas_call | solution.py:323
  12.5 8.3 %all-to-all-start = ((f32[32,8,128]{2,1,0:T(8,128)}), f32[32,8,128]{2,1,0:T(8,128)S(1)}, u32[]{:S(2)}, u32[]{:S(2)}) async-start(f32[32,8,128]{2,1,0:T(8,128)} %bitcast.1), calls=%async_computation | async-start | bytes 262144 | tf_op jit(solution)/shard_map/all_to_all | solution.py:504
  20.7 5.9 %mixed_planes.5 = (f32[32,24,256]{2,1,0:T(8,128)}, f32[32,24,256]{2,1,0:T(8,128)}, f32[32,24,256]{2,1,0:T(8,128)}) custom-call(f32[32,27]{1,0:T(8,128)} %weight.7, f32[32,32]{1,0:T(8,128)} %point.7, f32[32,64,256]{2,1,0:T(8,128)} %bitcast.12), custom_call_target="tpu_custom_call" | custom-call | flops 100000000 | bytes 262144 | tf_op jit(solution)/shard_map/mixed_planes/pallas_call | solution.py:387
  26.6 0.3 collective-permute-start.4
  26.9 1.5 %collective-permute-start.3 = (f32[32,24,256]{2,1,0:T(8,128)}, f32[32,24,256]{2,1,0:T(8,128)}, u32[]{:S(2)}, u32[]{:S(2)}) collective-permute-start(f32[32,24,256]{2,1,0:T(8,128)} %get-tuple-element.24), channel_id=1, source_target_pairs={{0,2},{2,4},{4,6},{6,8},{8,10},{10,12},{12,14},{14,16},{16,18},{18... | collective-permute-start | bytes 2359304 | tf_op jit(solution)/shard_map/ppermute | solution.py:468
  28.4 0.0 copy-done.6
  28.4 1.4 %collective-permute-start = (f32[2,32,256]{2,1,0:T(8,128)S(1)}, f32[2,32,256]{2,1,0:T(8,128)S(1)}, u32[]{:S(2)}, u32[]{:S(2)}) collective-permute-start(f32[2,32,256]{2,1,0:T(8,128)S(1)} %copy-done.6), channel_id=1, source_target_pairs={{0,1},{1,0},{2,3},{3,2},{4,5},{5,4},{6,7},{7,6},{8,9},{9,8},{10,11... | collective-permute-start | bytes 196616 | tf_op jit(solution)/shard_map/ppermute | solution.py:484
  29.8 0.0 all-to-all-done
  29.8 2.6 %filter_modes.1 = f32[256,128]{1,0:T(8,128)} custom-call(f32[256,128]{1,0:T(8,128)S(1)} %bitcast.9, f32[2,16,8,64]{3,2,1,0:T(8,128)S(1)} %copy-done.3, bf16[256,256]{1,0:T(8,128)(2,1)} %constant.28.clone.f_top, bf16[256,256]{1,0:T(8,128)(2,1)} %constant.29.clone.f_rest, bf16[512,128]{1,0:T(8,128)(2,1)} %constant.30.clone.i_top, ...), custom_call_target="tpu_custom_call" | custom-call | flops 100000000 | bytes 262144 | tf_op jit(solution)/shard_map/filter_modes/pallas_call | solution.py:342
  32.4 0.0 collective-permute-done.refs_0_
  32.4 0.6 copy-done.5
  33.0 5.0 %mixed_planes.6 = (f32[32,16,256]{2,1,0:T(8,128)}, f32[32,16,256]{2,1,0:T(8,128)}, f32[32,16,256]{2,1,0:T(8,128)}) custom-call(f32[32,27]{1,0:T(8,128)} %weight.7, f32[32,32]{1,0:T(8,128)} %point.7, f32[32,64,256]{2,1,0:T(8,128)} %bitcast.13, f32[2,32,256]{2,1,0:T(8,128)} %copy-done.5), custom_call_target="tpu_custom_call" | custom-call | flops 100000000 | bytes 262144 | tf_op jit(solution)/shard_map/mixed_planes/pallas_call | solution.py:387
  38.0 0.0 copy-start.1
  38.0 0.0 copy-start.4
  38.1 3.2 %collective-permute-start.6 = (f32[32,16,256]{2,1,0:T(8,128)}, f32[32,16,256]{2,1,0:T(8,128)}, u32[]{:S(2)}, u32[]{:S(2)}) collective-permute-start(f32[32,16,256]{2,1,0:T(8,128)} %get-tuple-element.36), channel_id=1, source_target_pairs={{0,30},{2,0},{4,2},{6,4},{8,6},{10,8},{12,10},{14,12},{16,14},{18,... | collective-permute-start | bytes 1572872 | tf_op jit(solution)/shard_map/ppermute | solution.py:469
  41.2 0.0 collective-permute-done.2.refs_2_
  41.2 0.0 collective-permute-start.5
  41.2 9.1 %all-to-all-start.1 = ((f32[32,8,128]{2,1,0:T(8,128)}), f32[32,8,128]{2,1,0:T(8,128)S(1)}, u32[]{:S(2)}, u32[]{:S(2)}) async-start(f32[32,8,128]{2,1,0:T(8,128)} %bitcast.3), calls=%async_computation.1 | async-start | bytes 262144 | tf_op jit(solution)/shard_map/all_to_all | solution.py:506
  50.4 4.3 %mixed_planes.7.refs_0_ = f32[32,24,256]{2,1,0:T(8,128)} custom-call(f32[32,27]{1,0:T(8,128)} %weight.7, f32[32,32]{1,0:T(8,128)} %point.7, f32[32,64,256]{2,1,0:T(8,128)} %bitcast.14), custom_call_target="tpu_custom_call" | custom-call | flops 100000000 | bytes 262144 | tf_op jit(solution)/shard_map/mixed_planes/pallas_call | solution.py:387
  54.7 4.7 %all-to-all-done.1 = f32[32,8,128]{2,1,0:T(8,128)S(1)} async-done(((f32[32,8,128]{2,1,0:T(8,128)}), f32[32,8,128]{2,1,0:T(8,128)S(1)}, u32[]{:S(2)}, u32[]{:S(2)}) %all-to-all-start.1) | async-done | bytes 131104 | tf_op jit(solution)/shard_map/all_to_all | solution.py:506
  59.4 0.0 collective-permute-done.1.refs_1_
  59.4 0.0 collective-permute-done.4.refs_5_
  59.4 0.0 collective-permute-done.3.refs_4_
  59.4 1.1 %copy-done = f32[32,24,256]{2,1,0:T(8,128)S(1)} copy-done((f32[32,24,256]{2,1,0:T(8,128)S(1)}, f32[32,24,256]{2,1,0:T(8,128)}, u32[]{:S(2)}) %copy-start) | copy-done | bytes 786456
  60.5 1.0 %copy-done.2 = f32[32,16,256]{2,1,0:T(8,128)S(1)} copy-done((f32[32,16,256]{2,1,0:T(8,128)S(1)}, f32[32,16,256]{2,1,0:T(8,128)}, u32[]{:S(2)}) %copy-start.2) | copy-done | bytes 524312
  61.6 5.0 %inverse_modes.1 = (f32[32,64,256]{2,1,0:T(8,128)}, f32[32,16,256]{2,1,0:T(8,128)S(1)}) custom-call(f32[16,16,128]{2,1,0:T(8,128)S(1)} %bitcast.8, f32[32]{0:T(128)S(1)} %copy-done.4, bf16[2,128,512]{2,1,0:T(8,128)(2,1)} %constant.32.clone.x_top, bf16[2,128,512]{2,1,0:T(8,128)(2,1)} %constant.33.clone.x_rest, bf16[2,256,128]{2,1,0:T(8,128)(2,1)} %constant.34.clone.y_top, ...), custom_call_target="tpu_custom_call" | custom-call | flops 100000000 | bytes 262144 | tf_op jit(solution)/shard_map/inverse_modes/pallas_call | solution.py:355
  66.6 0.0 collective-permute-done.6.high
  66.6 0.0 collective-permute-done.5.low
  66.6 2.0 %finished_rows.1 = f32[32,64,256]{2,1,0:T(8,128)} custom-call(f32[32,64,256]{2,1,0:T(8,128)} %get-tuple-element.34._, f32[32,16,256]{2,1,0:T(8,128)S(1)} %get-tuple-element.35.base, f32[32,16,256]{2,1,0:T(8,128)} %collective-permute-done.5.low, f32[32,16,256]{2,1,0:T(8,128)} %collective-permute-done.6.high), custom_call_target="tpu_custom_call", output_to_operand_aliasing={{}: (0, {})} | custom-call | flops 100000000 | bytes 262144 | tf_op jit(solution)/shard_map/finished_rows/pallas_call | solution.py:415
  (8 shorter events, 0.0 us)
Async XLA Ops:
  5.3 36.0 %collective-permute-start.2 = (f32[32,24,256]{2,1,0:T(8,128)}, f32[32,24,256]{2,1,0:T(8,128)S(1)}, u32[]{:S(2)}, u32[]{:S(2)}) collective-permute-start(f32[32,24,256]{2,1,0:T(8,128)} %get-tuple-element.31), channel_id=1, source_target_pairs={{0,30},{2,0},{4,2},{6,4},{8,6},{10,8},{12,10},{14,12},{16,14},{18,... | collective-permute-start | bytes 2359304 | tf_op jit(solution)/shard_map/ppermute | solution.py:469
  5.4 23.0 %copy-start.6 = (f32[2,32,256]{2,1,0:T(8,128)S(1)}, f32[2,32,256]{2,1,0:T(8,128)}, u32[]{:S(2)}) copy-start(f32[2,32,256]{2,1,0:T(8,128)} %get-tuple-element.27) | copy-start | bytes 196612
  5.4 24.4 %copy-start.3 = (f32[2,16,8,64]{3,2,1,0:T(8,128)S(1)}, f32[2,16,8,64]{3,2,1,0:T(8,128)}, u32[]{:S(2)}) copy-start(f32[2,16,8,64]{3,2,1,0:T(8,128)} %gains) | copy-start | bytes 196612
  5.4 54.0 %collective-permute-start.1 = (f32[32,24,256]{2,1,0:T(8,128)}, f32[32,24,256]{2,1,0:T(8,128)S(1)}, u32[]{:S(2)}, u32[]{:S(2)}) collective-permute-start(f32[32,24,256]{2,1,0:T(8,128)} %get-tuple-element.21), channel_id=1, source_target_pairs={{0,2},{2,4},{4,6},{6,8},{8,10},{10,12},{12,14},{14,16},{16,18},{18... | collective-permute-start | bytes 2359304 | tf_op jit(solution)/shard_map/ppermute | solution.py:468
  12.5 17.3 %all-to-all-start = ((f32[32,8,128]{2,1,0:T(8,128)}), f32[32,8,128]{2,1,0:T(8,128)S(1)}, u32[]{:S(2)}, u32[]{:S(2)}) async-start(f32[32,8,128]{2,1,0:T(8,128)} %bitcast.1), calls=%async_computation | async-start | bytes 262144 | tf_op jit(solution)/shard_map/all_to_all | solution.py:504
  26.6 32.8 %collective-permute-start.4 = (f32[32,24,256]{2,1,0:T(8,128)}, f32[32,24,256]{2,1,0:T(8,128)S(1)}, u32[]{:S(2)}, u32[]{:S(2)}) collective-permute-start(f32[32,24,256]{2,1,0:T(8,128)} %get-tuple-element.33), channel_id=1, source_target_pairs={{0,30},{2,0},{4,2},{6,4},{8,6},{10,8},{12,10},{14,12},{16,14},{18,... | collective-permute-start | bytes 2359304 | tf_op jit(solution)/shard_map/ppermute | solution.py:469
  26.9 32.5 %collective-permute-start.3 = (f32[32,24,256]{2,1,0:T(8,128)}, f32[32,24,256]{2,1,0:T(8,128)}, u32[]{:S(2)}, u32[]{:S(2)}) collective-permute-start(f32[32,24,256]{2,1,0:T(8,128)} %get-tuple-element.24), channel_id=1, source_target_pairs={{0,2},{2,4},{4,6},{6,8},{8,10},{10,12},{12,14},{14,16},{16,18},{18... | collective-permute-start | bytes 2359304 | tf_op jit(solution)/shard_map/ppermute | solution.py:468
  28.4 4.0 %collective-permute-start = (f32[2,32,256]{2,1,0:T(8,128)S(1)}, f32[2,32,256]{2,1,0:T(8,128)S(1)}, u32[]{:S(2)}, u32[]{:S(2)}) collective-permute-start(f32[2,32,256]{2,1,0:T(8,128)S(1)} %copy-done.6), channel_id=1, source_target_pairs={{0,1},{1,0},{2,3},{3,2},{4,5},{5,4},{6,7},{7,6},{8,9},{9,8},{10,11... | collective-permute-start | bytes 196616 | tf_op jit(solution)/shard_map/ppermute | solution.py:484
  32.4 0.6 copy-start.5
  38.0 21.4 %copy-start.1 = (f32[32,24,256]{2,1,0:T(8,128)S(1)}, f32[32,24,256]{2,1,0:T(8,128)}, u32[]{:S(2)}) copy-start(f32[32,24,256]{2,1,0:T(8,128)} %get-tuple-element.32.refs_3_) | copy-start | bytes 2359300
  38.0 21.4 %copy-start.4 = (f32[32]{0:T(128)S(1)}, f32[32]{0:T(128)}, u32[]{:S(2)}) copy-start(f32[32]{0:T(128)} %bias.1) | copy-start | bytes 388
  38.1 28.5 %collective-permute-start.6 = (f32[32,16,256]{2,1,0:T(8,128)}, f32[32,16,256]{2,1,0:T(8,128)}, u32[]{:S(2)}, u32[]{:S(2)}) collective-permute-start(f32[32,16,256]{2,1,0:T(8,128)} %get-tuple-element.36), channel_id=1, source_target_pairs={{0,30},{2,0},{4,2},{6,4},{8,6},{10,8},{12,10},{14,12},{16,14},{18,... | collective-permute-start | bytes 1572872 | tf_op jit(solution)/shard_map/ppermute | solution.py:469
  41.2 25.4 %collective-permute-start.5 = (f32[32,16,256]{2,1,0:T(8,128)}, f32[32,16,256]{2,1,0:T(8,128)}, u32[]{:S(2)}, u32[]{:S(2)}) collective-permute-start(f32[32,16,256]{2,1,0:T(8,128)} %get-tuple-element.29), channel_id=1, source_target_pairs={{0,2},{2,4},{4,6},{6,8},{8,10},{10,12},{12,14},{14,16},{16,18},{18... | collective-permute-start | bytes 1572872 | tf_op jit(solution)/shard_map/ppermute | solution.py:468
  41.2 18.2 %all-to-all-start.1 = ((f32[32,8,128]{2,1,0:T(8,128)}), f32[32,8,128]{2,1,0:T(8,128)S(1)}, u32[]{:S(2)}, u32[]{:S(2)}) async-start(f32[32,8,128]{2,1,0:T(8,128)} %bitcast.3), calls=%async_computation.1 | async-start | bytes 262144 | tf_op jit(solution)/shard_map/all_to_all | solution.py:506
  59.4 1.1 %copy-start = (f32[32,24,256]{2,1,0:T(8,128)S(1)}, f32[32,24,256]{2,1,0:T(8,128)}, u32[]{:S(2)}) copy-start(f32[32,24,256]{2,1,0:T(8,128)} %mixed_planes.7.refs_0_) | copy-start | bytes 2359300
  60.5 1.0 %copy-start.2 = (f32[32,16,256]{2,1,0:T(8,128)S(1)}, f32[32,16,256]{2,1,0:T(8,128)}, u32[]{:S(2)}) copy-start(f32[32,16,256]{2,1,0:T(8,128)} %get-tuple-element.28.outer) | copy-start | bytes 1572868

commit v4 on v3

--- a/solution.py
+++ b/solution.py
@@ -147,43 +147,35 @@
     out[...] = back[:half] + jnp.where(is_real, -crossed, crossed)
 
 
-def conv_kernel(plan, weight, point, field, *refs):
-    offsets, tiles, outer, with_edges = plan
-    last = field.shape[1] // 8 - 1
-    if outer:
-        halo, refs = refs[0], refs[1:]
-    count = len(offsets)
-    outs, refs = refs[:count], refs[count:]
-    if with_edges:
-        edges_out, refs = refs[0], refs[1:]
-    taken, halo_rows, weights, points, edges, sent, turned, depth, gains, sem_in, sem_out, sem_few = refs
-    wanted = [0, 1, last - 1, last] if outer else list(range(tiles[0] - 1, tiles[-1] + 2))
-    if with_edges:
-        wanted += [t for t in (0, last) if t not in wanted]
-    few = [
-        pltpu.make_async_copy(weight, weights, sem_few.at[0]),
-        pltpu.make_async_copy(point, points, sem_few.at[1]),
-    ]
-    if outer:
-        few.append(pltpu.make_async_copy(halo, halo_rows, sem_few.at[2]))
-    for copy in few:
-        copy.start()
+def fetch_tiles(field, taken, sems, wanted):
     pending = {}
     for k, t in enumerate(wanted):
         pending[t] = [
             pltpu.make_async_copy(
-                field.at[:, pl.ds(8 * t, 8), pl.ds(128 * h, 128)], taken.at[k, h], sem_in.at[k, h]
+                field.at[:, pl.ds(8 * t, 8), pl.ds(128 * h, 128)], taken.at[k, h], sems.at[k, h]
             )
             for h in range(2)
         ]
         for copy in pending[t]:
             copy.start()
-    for copy in few:
-        copy.wait()
-    for k in offsets:
-        for j in range(9):
-            gains[9 * k + j] = jnp.broadcast_to(weights[:, 9 * k + j : 9 * k + j + 1], (CH, 128))
-
+
+    def row(t, r):
+        for copy in pending.pop(t, ()):
+            copy.wait()
+        k = wanted.index(t)
+        return jnp.concatenate(
+            [taken.at[k, h].reshape(CH * 8, 128)[pl.ds(r, CH, stride=8), :] for h in range(2)], axis=1
+        )
+
+    return row
+
+
+def spread_gains(weights, gains, offsets):
+    for k in [9 * a + j for a in offsets for j in range(9)]:
+        gains[k] = jnp.broadcast_to(weights[:, k : k + 1], (CH, 128))
+
+
+def mixing(points):
     down = (
         lax.broadcasted_iota(jnp.int32, (8 * CH, CH), 0) // 8
         == lax.broadcasted_iota(jnp.int32, (8 * CH, CH), 1)
@@ -196,45 +188,20 @@
         lax.broadcasted_iota(jnp.int32, (8 * CH, 8 * CH), 0) % 8
         == lax.broadcasted_iota(jnp.int32, (8 * CH, 8 * CH), 1) // CH
     )
-    mix = tuple(
+    return tuple(
         jnp.where(same, dot(dot(down, part).astype(BF), across), 0.0).astype(BF)
-        for part in parts(points[...])
+        for part in parts(points)
     )
 
-    def row(t, r):
-        for copy in pending.pop(t, ()):
-            copy.wait()
-        k = wanted.index(t)
-        return jnp.concatenate(
-            [taken.at[k, h].reshape(CH * 8, 128)[pl.ds(r, CH, stride=8), :] for h in range(2)], axis=1
-        )
-
-    if outer:
-        segments = [
-            [None, *[(0, r) for r in range(8)], (1, 0)],
-            [(last - 1, 7), *[(last, r) for r in range(8)], None],
-        ]
-    else:
-        segments = [
-            [(tiles[0] - 1, 7), *[(t, r) for t in tiles for r in range(8)], (tiles[-1] + 1, 0)]
-        ]
-    runs, at, done = [], 0, 0
-    for side, places in enumerate(segments):
-        for i, place in enumerate(places):
-            value = halo_rows[side] if place is None else row(*place)
-            turned[0, at + i] = pltpu.roll(value, 1, 1)
-            turned[1, at + i] = value
-            turned[2, at + i] = pltpu.roll(value, NX - 1, 1)
-        runs.append((at, done, len(places) - 2))
-        at, done = at + len(places), done + len(places) - 2
-    copies = []
-    if with_edges:
-        edges[0] = row(last, 7)
-        edges[1] = row(0, 0)
-        copies.append(pltpu.make_async_copy(edges, edges_out, sem_few.at[3]))
-        copies[-1].start()
-
-    def taps(i, _):
+
+def turn(turned, at, value):
+    turned[0, at] = pltpu.roll(value, 1, 1)
+    turned[1, at] = value
+    turned[2, at] = pltpu.roll(value, NX - 1, 1)
+
+
+def tap_sums(turned, depth, gains, runs, offsets, fresh):
+    def some(i, _):
         chans = pl.ds(pl.multiple_of(i * 8, 8), 8)
         gain = {k: gains[k, chans, :] for a in offsets for k in range(9 * a, 9 * a + 9)}
         for h in range(2):
@@ -247,40 +214,136 @@
                         o = r - b
                         if o < 0 or o >= rows:
                             continue
-                        for a in offsets:
+                        for k, a in enumerate(offsets):
                             for e in range(3):
                                 term = gain[a * 9 + b * 3 + e] * values[e]
-                                sums[o, a] = sums[o, a] + term if (o, a) in sums else term
+                                if (o, k) in sums:
+                                    sums[o, k] = sums[o, k] + term
+                                elif fresh:
+                                    sums[o, k] = term
+                                else:
+                                    sums[o, k] = depth[k, to + o, chans, lanes] + term
                     if r >= 2:
-                        for k, a in enumerate(offsets):
-                            depth[k, to + r - 2, chans, lanes] = sums.pop((r - 2, a))
+                        for k in range(len(offsets)):
+                            depth[k, to + r - 2, chans, lanes] = sums.pop((r - 2, k))
         return 0
 
-    lax.fori_loop(0, CH // 8, taps, 0)
-
-    for t in range(done // 8):
-        rows = pl.ds(8 * t, 8)
-        for k, out in enumerate(outs):
-            tile = depth[k, rows].reshape(8 * CH, NX)
-            sent[k, t] = dot3(mix, parts(tile)).reshape(CH, 8, NX)
-            copies.append(pltpu.make_async_copy(sent.at[k, t], out.at[:, rows, :], sem_out.at[k, t]))
+    lax.fori_loop(0, CH // 8, some, 0)
+
+
+def mix_tile(mix, depth, k, t):
+    tile = depth[k, pl.ds(8 * t, 8)].reshape(8 * CH, NX)
+    return dot3(mix, parts(tile)).reshape(CH, 8, NX)
+
+
+def pack_kernel(middle, field, packed, edges, taken, rows, ends, sem_in, sem_out):
+    last = field.shape[1] // 8 - 1
+    before, after = middle[0] - 1, middle[-1] + 1
+    wanted = [before, *middle, after] + [t for t in (0, last) if t not in (before, after)]
+    row = fetch_tiles(field, taken, sem_in, wanted)
+    places = [(before, 7), *[(t, r) for t in middle for r in range(8)], (after, 0)]
+    copies, sent = [], 0
+    for i, place in enumerate(places):
+        rows[i] = row(*place)
+        if i + 1 - sent >= 17 or i + 1 == len(places):
+            some = pl.ds(sent, i + 1 - sent)
+            copies.append(pltpu.make_async_copy(rows.at[some], packed.at[some], sem_out.at[len(copies)]))
             copies[-1].start()
-    for copies_of in (copies, *pending.values()):
-        for copy in copies_of:
-            copy.wait()
+            sent = i + 1
+    ends[0] = row(last, 7)
+    ends[1] = row(0, 0)
+    copies.append(pltpu.make_async_copy(ends, edges, sem_out.at[len(copies)]))
+    copies[-1].start()
+    for copy in copies:
+        copy.wait()
+
+
+def own_kernel(plan, weight, point, field, halo, *refs):
+    upper, lower, count = plan
+    outs, refs = refs[:count], refs[count:]
+    taken, halo_rows, weights, points, sent, turned, depth, gains, sem_in, sem_out, sem_few = refs
+    few = [
+        pltpu.make_async_copy(a, b, sem_few.at[i])
+        for i, (a, b) in enumerate(((weight, weights), (point, points), (halo, halo_rows)))
+    ]
+    for copy in few:
+        copy.start()
+    wanted = [*upper, upper[-1] + 1, lower[0] - 1, *lower]
+    row = fetch_tiles(field, taken, sem_in, wanted)
+    for copy in few:
+        copy.wait()
+    spread_gains(weights, gains, range(3))
+    mix = mixing(points[...])
+    rows = 8 * len(upper)
+    for i, place in enumerate([None, *[(t, r) for t in upper for r in range(8)], (upper[-1] + 1, 0)]):
+        turn(turned, i, halo_rows[0] if place is None else row(*place))
+    for i, place in enumerate([(lower[0] - 1, 7), *[(t, r) for t in lower for r in range(8)], None]):
+        turn(turned, rows + 2 + i, halo_rows[1] if place is None else row(*place))
+    tap_sums(turned, depth, gains, [(0, 0, rows), (rows + 2, rows, rows)], range(3), True)
+    copies = []
+    own, pairs = outs[0], outs[1:]
+    tiles = [*upper, *lower]
+    order = sorted(range(len(tiles)), key=lambda t: tiles[t] in (upper[0], lower[-1]))
+    for t in order:
+        outer = tiles[t] in (upper[0], lower[-1])
+        group = pairs[2:] if count == 5 and not outer else pairs[:2]
+        slot = 0 if t < len(upper) else 1
+        for k, out, at in ((0, group[0], slot), (2, group[1], slot), (1, own, t)):
+            sent[k, t] = mix_tile(mix, depth, k, t)
+            copies.append(
+                pltpu.make_async_copy(sent.at[k, t], out.at[:, pl.ds(8 * at, 8), :], sem_out.at[k, t])
+            )
+            copies[-1].start()
+    for copy in copies:
+        copy.wait()
+
+
+def middle_kernel(weight, point, *refs):
+    planes, out = refs[:3], refs[3]
+    taken, weights, points, sent, turned, depth, gains, sem_in, sem_out, sem_few = refs[4:]
+    few = [
+        pltpu.make_async_copy(a, b, sem_few.at[i])
+        for i, (a, b) in enumerate(((weight, weights), (point, points)))
+    ]
+    arrivals = [pltpu.make_async_copy(planes[a], taken.at[a], sem_in.at[a]) for a in range(3)]
+    for copy in few + arrivals:
+        copy.start()
+    for copy in few:
+        copy.wait()
+    spread_gains(weights, gains, range(3))
+    mix = mixing(points[...])
+    rows = out.shape[1]
+    for a in (1, 0, 2):
+        arrivals[a].wait()
+
+        def one(r, _):
+            turn(turned, r, taken[a, r])
+            return 0
+
+        lax.fori_loop(0, rows + 2, one, 0, unroll=2)
+        tap_sums(turned, depth, gains, [(0, 0, rows)], [a], a == 1)
+    copies = []
+    for t in range(rows // 8):
+        sent[t] = mix_tile(mix, depth, 0, t)
+        copies.append(pltpu.make_async_copy(sent.at[t], out.at[:, pl.ds(8 * t, 8), :], sem_out.at[t]))
+        copies[-1].start()
+    for copy in copies:
+        copy.wait()
 
 
 def gelu(value):
     return 0.5 * value * (1.0 + lax.erf(value * (1.0 / math.sqrt(2.0))))
 
 
-def inverse_kernel(group, chunks, modes, bias, x_top, x_rest, y_top, y_rest, outer, *refs):
+def inverse_kernel(group, plan, modes, bias, x_top, x_rest, y_top, y_rest, middle, own, *refs):
+    upper, lower = plan
     out, base = refs[-2:]
     step = pl.program_id(0)
     gy = lax.axis_index("gy")
     y_table = (y_top[gy], y_rest[gy])
     mode_rows = parts(modes[...].reshape(group * MY, 4 * MX))
     y_local = out.shape[1]
+    start, stop = 8 * upper[-1] + 8, 8 * lower[0]
     for p in range(2):
         wide = dot3(mode_rows, (x_top[p], x_rest[p]))
         tall = jnp.concatenate([wide[:, :NX], wide[:, NX:]], axis=0)
@@ -288,12 +351,17 @@
         for i in range(group):
             c = 2 * i + p
             plane = planes[i] + bias[step * 2 * group + c]
-            base[c, :8] = plane[:8] + outer[c, :8]
-            base[c, 8:] = plane[y_local - 8 :] + outer[c, 8:]
-            for k, (first, count) in enumerate(chunks):
-                rows = slice(8 * first, 8 * (first + count))
-                own, low, high = refs[3 * k : 3 * k + 3]
-                out[c, rows] = gelu(plane[rows] + (own[c] + (low[c] + high[c])))
+            out[c, start:stop] = gelu(plane[start:stop] + middle[c])
+            first = plane[:start] + own[c, :start]
+            second = plane[stop:] + own[c, start:]
+            base[c, :8] = first[:8]
+            base[c, 8:] = second[-8:]
+            if start > 8:
+                low, high = refs[:2]
+                out[c, 8:start] = gelu(first[8:] + (low[c, : start - 8] + high[c, : start - 8]))
+                out[c, stop : y_local - 8] = gelu(
+                    second[:-8] + (low[c, start - 8 :] + high[c, start - 8 :])
+                )
 
 
 def finish_kernel(_, base, low, high, out):
@@ -348,12 +416,13 @@
     )(arrived, gains, *in_hbm(*fwd, *inv))
 
 
-def inverse_call(modes, bias, outer, inner, chunks, y_local, gy, scale):
+def inverse_call(modes, bias, middle, own, pair, plan, y_local, gy, scale):
     group = 4
     tables = [*halves(x_inverse_table(scale)), *halves(y_inverse_table(y_local, gy, group))]
     some = lambda rows: pl.BlockSpec((2 * group, rows, NX), lambda i: (i, 0, 0))
+    planes = [*in_hbm(middle, own), *pair]
     return pl.pallas_call(
-        functools.partial(inverse_kernel, group, chunks),
+        functools.partial(inverse_kernel, group, plan),
         out_shape=[
             jax.ShapeDtypeStruct((CH, y_local, NX), F32),
             jax.ShapeDtypeStruct((CH, 16, NX), F32),
@@ -363,50 +432,92 @@
             pl.BlockSpec((group, MY, 4 * MX), lambda i: (i, 0, 0)),
             pl.BlockSpec(memory_space=pltpu.SMEM),
             *[whole_block(t) for t in tables],
-            some(16),
-            *[some(8 * count) for _, count in chunks for _ in range(3)],
+            *[some(p.shape[1]) for p in planes],
         ],
         out_specs=[some(y_local), some(16)],
         compiler_params=params(),
         cost_estimate=cost(10**8, 2**18),
         name="inverse_modes",
-    )(modes, bias, *in_hbm(*tables), outer, *inner)
-
-
-def conv_call(field, weight, point, offsets, tiles, halo=None, with_edges=False):
-    outer = halo is not None
-    rows, count = 8 * len(tiles), len(offsets)
+    )(modes, bias, *in_hbm(*tables), *planes)
+
+
+def pack_call(field, middle):
+    count = 8 * len(middle) + 2
+    fetched = len(middle) + 4
     hbm = pl.BlockSpec(memory_space=pltpu.HBM)
-    operands = in_hbm(weight, point, field)
-    shapes = [pltpu.HBM((CH, rows, NX), F32)] * count
-    if outer:
-        operands += in_hbm(halo)
-    if with_edges:
-        shapes.append(pltpu.HBM((2, CH, NX), F32))
-    fetched = len(tiles) + 4
     return pl.pallas_call(
-        functools.partial(conv_kernel, (offsets, tiles, outer, with_edges)),
+        functools.partial(pack_kernel, middle),
+        out_shape=[pltpu.HBM((count, CH, NX), F32), pltpu.HBM((2, CH, NX), F32)],
+        in_specs=[hbm],
+        out_specs=[hbm] * 2,
+        scratch_shapes=[
+            pltpu.VMEM((fetched, 2, CH, 8, 128), F32),
+            pltpu.VMEM((count, CH, NX), F32),
+            pltpu.VMEM((2, CH, NX), F32),
+            pltpu.SemaphoreType.DMA((fetched, 2)),
+            pltpu.SemaphoreType.DMA((count // 17 + 2,)),
+        ],
+        compiler_params=params(),
+        cost_estimate=cost(10**8, 2**18),
+        name="packed_rows",
+    )(*in_hbm(field))
+
+
+def own_call(field, halo, weight, point, upper, lower):
+    tiles = len(upper) + len(lower)
+    rows = 8 * tiles
+    hbm = pl.BlockSpec(memory_space=pltpu.HBM)
+    shapes = [pltpu.HBM((CH, rows, NX), F32)] + [pltpu.HBM((CH, 16, NX), F32)] * 2
+    if tiles > 2:
+        shapes += [pltpu.HBM((CH, rows - 16, NX), F32)] * 2
+    return pl.pallas_call(
+        functools.partial(own_kernel, (upper, lower, len(shapes))),
         out_shape=shapes,
-        in_specs=[hbm] * len(operands),
+        in_specs=[hbm] * 3 + [pl.BlockSpec(memory_space=pl.ANY)],
         out_specs=[hbm] * len(shapes),
         scratch_shapes=[
-            pltpu.VMEM((fetched, 2, CH, 8, 128), F32),
+            pltpu.VMEM((tiles + 2, 2, CH, 8, 128), F32),
             pltpu.VMEM((2, CH, NX), F32),
             pltpu.VMEM((CH, 27), F32),
             pltpu.VMEM((CH, CH), F32),
-            pltpu.VMEM((2, CH, NX), F32),
-            pltpu.VMEM((count, len(tiles), CH, 8, NX), F32),
+            pltpu.VMEM((3, tiles, CH, 8, NX), F32),
             pltpu.VMEM((3, rows + 4, CH, NX), F32),
-            pltpu.VMEM((count, rows, CH, NX), F32),
+            pltpu.VMEM((3, rows, CH, NX), F32),
             pltpu.VMEM((27, CH, 128), F32),
-            pltpu.SemaphoreType.DMA((fetched, 2)),
-            pltpu.SemaphoreType.DMA((count, len(tiles))),
-            pltpu.SemaphoreType.DMA((4,)),
+            pltpu.SemaphoreType.DMA((tiles + 2, 2)),
+            pltpu.SemaphoreType.DMA((3, tiles)),
+            pltpu.SemaphoreType.DMA((3,)),
         ],
         compiler_params=params(),
         cost_estimate=cost(10**8, 2**18),
-        name="mixed_planes",
-    )(*operands)
+        name="own_sums",
+    )(*in_hbm(weight, point, field), halo)
+
+
+def middle_call(weight, point, low, own, high):
+    rows = own.shape[0] - 2
+    hbm = pl.BlockSpec(memory_space=pltpu.HBM)
+    return pl.pallas_call(
+        middle_kernel,
+        out_shape=pltpu.HBM((CH, rows, NX), F32),
+        in_specs=[hbm] * 2 + [pl.BlockSpec(memory_space=pl.ANY)] * 3,
+        out_specs=hbm,
+        scratch_shapes=[
+            pltpu.VMEM((3, rows + 2, CH, NX), F32),
+            pltpu.VMEM((CH, 27), F32),
+            pltpu.VMEM((CH, CH), F32),
+            pltpu.VMEM((rows // 8, CH, 8, NX), F32),
+            pltpu.VMEM((3, rows + 2, CH, NX), F32),
+            pltpu.VMEM((1, rows, CH, NX), F32),
+            pltpu.VMEM((27, CH, 128), F32),
+            pltpu.SemaphoreType.DMA((3,)),
+            pltpu.SemaphoreType.DMA((rows // 8,)),
+            pltpu.SemaphoreType.DMA((2,)),
+        ],
+        compiler_params=params(),
+        cost_estimate=cost(10**8, 2**18),
+        name="middle_sums",
+    )(*in_hbm(weight, point), low, own, high)
 
 
 def finish_call(result, base, low, high):
@@ -473,13 +584,12 @@
         return lax.optimization_barrier((value, *others))[0]
 
     tiles = y_local // 8
-    middle = 1 + (tiles - 1) // 2
-    spans = [tuple(range(1, middle)), tuple(range(middle, tiles - 1))]
-    chunks = [(span[0], len(span)) for span in spans if span]
-    conv = functools.partial(conv_call, weight=depth_weight, point=point_weight)
-
-    down, up, edges = conv(field, offsets=(0, 2), tiles=spans[0], with_edges=True)
-    first_pair = to_neighbours(down, up)
+    side = 2 if tiles >= 6 else 1
+    upper, lower = tuple(range(side)), tuple(range(tiles - side, tiles))
+    middle = tuple(range(side, tiles - side))
+
+    packed, edges = pack_call(field, middle)
+    packed_low, packed_high = to_neighbours(packed, packed)
     if gy == 2:
         halo = lax.ppermute(edges, "gy", ring("gy", gy, 1))
     else:
@@ -489,32 +599,27 @@
                 lax.ppermute(edges[1], "gy", ring("gy", gy, -1)),
             ]
         )
-    coarse = forward_call(after(field, down), gy)
-    second = []
-    mark = coarse
-    if spans[1]:
-        down, own, up = conv(after(field, coarse), offsets=(0, 1, 2), tiles=spans[1])
-        second = [own, *to_neighbours(down, up)]
-        mark = down
+    coarse = forward_call(after(field, packed), gy)
+    sums = own_call(after(field, coarse), halo, depth_weight, point_weight, upper, lower)
+    own, down, up = sums[:3]
+    inner_pair = to_neighbours(*sums[3:]) if len(sums) > 3 else ()
 
     j_own, n_own = spectral_filter.shape[2], spectral_filter.shape[3]
     if j_own == 8 and n_own == 2 * MX:
         both = ("gz", "gy")
         sent = coarse.reshape(gz * gy * 8, 4 * MX)
         got = lax.all_to_all(sent, both, split_axis=0, concat_axis=0, tiled=True)
-        out = filter_call(got, after(spectral_filter, mark), gz, gy, forward_scale)
+        out = filter_call(got, after(spectral_filter, own), gz, gy, forward_scale)
         back = lax.all_to_all(out, both, split_axis=0, concat_axis=0, tiled=True)
         back = back.reshape(CH // 2, MY, 4 * MX)
-        mark = out
     else:
         back = general_filter(coarse, spectral_filter, gz, gy, forward_scale)
 
-    down, outer, up = conv(after(field, mark), offsets=(0, 1, 2), tiles=(0, tiles - 1), halo=halo)
+    down, up = (after(value, back) for value in (down, up))
     outer_pair = to_neighbours(down, up)
-    (own,) = conv(after(field, down), offsets=(1,), tiles=spans[0])
-    inner = [own, *first_pair, *second]
+    mixed = middle_call(depth_weight, point_weight, packed_low, after(packed, back), packed_high)
     result, base = inverse_call(
-        back, bias_vector, outer, inner, chunks, y_local, gy, inverse_scale
+        back, bias_vector, mixed, own, inner_pair, (upper, lower), y_local, gy, inverse_scale
     )
     result = finish_call(result, base, *outer_pair)
     return result.reshape(CH, 1, y_local, NX)

time: 69.7 us -> 72.3 us (1.037)
  the two profiles are of different devices: /device:TPU:1 before, /device:TPU:0 now
where the time goes in v4:
time: 72.3 us; the launch traced here: 71.8 us
  Pallas kernels  31 us (43%)
  starting transfers between devices  27.8 us (38%)
  waiting for transfers between devices  10.6 us (15%)
  local copies, waits for them, and re-layouts  2.21 us (3%)
    ppermute x3, starting transfers between devices, to_neighbours(): lax.ppermute(up, 'gz', ring('gz', gz, -1))  14.1 us
    pallas_call x1, Pallas kernels, middle_call(): pl.pallas_call(middle_kernel, out_shape=pltpu.HBM((CH, rows, NX), F32), i...  9.83 us
    pallas_call x1, Pallas kernels, own_call(): pl.pallas_call(functools.partial(own_kernel, (upper, lower, len(shapes)))...  6.54 us
    all_to_all x1, starting transfers between devices, body(): back = lax.all_to_all(out, both, split_axis=0, concat_axis=0, tiled=True)  5.84 us
    all_to_all x1, starting transfers between devices, body(): got = lax.all_to_all(sent, both, split_axis=0, concat_axis=0, tiled=True)  5.73 us
    pallas_call x1, Pallas kernels, inverse_call(): pl.pallas_call(functools.partial(inverse_kernel, group, plan), out_shape=...  5.47 us
    all_to_all x1, waiting for transfers between devices, body(): back = lax.all_to_all(out, both, split_axis=0, concat_axis=0, tiled=True)  4.66 us
    pallas_call x1, Pallas kernels, forward_call(): pl.pallas_call(functools.partial(forward_kernel, group), out_shape=jax.Sh...  3.81 us
  transfers between devices with their start and end apart: 9, of which 3 were waited for; matrix products, arithmetic and copies ran while one was open for 0% of the time, Pallas kernels for 38%

profile of v4, /device:TPU:0, one launch (start us, length us, event | category | flops | bytes accessed | tf_op | source)
XLA Modules:
  0.0 71.8 jit_solution(15823710398482758139)
XLA Ops:
  0.0 2.5 %packed_rows.1 = (f32[34,32,256]{2,1,0:T(8,128)}, f32[2,32,256]{2,1,0:T(8,128)}) custom-call(f32[32,64,256]{2,1,0:T(8,128)} %bitcast.12), custom_call_target="tpu_custom_call" | custom-call | flops 100000000 | bytes 262144 | tf_op jit(solution)/shard_map/packed_rows/pallas_call | solution.py:448
  2.5 0.0 copy-start.5
  2.5 5.5 %collective-permute-start.2 = (f32[34,32,256]{2,1,0:T(8,128)}, f32[34,32,256]{2,1,0:T(8,128)S(1)}, u32[]{:S(2)}, u32[]{:S(2)}) collective-permute-start(f32[34,32,256]{2,1,0:T(8,128)} %get-tuple-element.26.refs_1_), channel_id=1, source_target_pairs={{0,30},{2,0},{4,2},{6,4},{8,6},{10,8},{12,10},{14,12},{16,14},{18,... | collective-permute-start | bytes 3342344 | tf_op jit(solution)/shard_map/ppermute | solution.py:580
  8.0 0.0 collective-permute-start.1
  8.0 3.8 %forward_modes.1 = f32[16,16,128]{2,1,0:T(8,128)S(1)} custom-call(f32[32,64,256]{2,1,0:T(8,128)} %bitcast.13, bf16[2,128,256]{2,1,0:T(8,128)(2,1)} %constant.24.clone.y_top, bf16[2,128,256]{2,1,0:T(8,128)(2,1)} %constant.25.clone.y_rest, bf16[4,256,128]{2,1,0:T(8,128)(2,1)} %constant.26.clone.x_top, bf16[4,256,128]{2,1,0:T(8,128)(2,1)} %constant.27.clone.x_rest), custom_call_target="tpu_custom_call" | custom-call | flops 100000000 | bytes 262144 | tf_op jit(solution)/shard_map/forward_modes/pallas_call | solution.py:391
  11.8 0.0 copy-start.1
  11.8 0.6 copy-done.1
  12.4 5.7 %all-to-all-start = ((f32[32,8,128]{2,1,0:T(8,128)}), f32[32,8,128]{2,1,0:T(8,128)S(1)}, u32[]{:S(2)}, u32[]{:S(2)}) async-start(f32[32,8,128]{2,1,0:T(8,128)} %bitcast.10), calls=%async_computation | async-start | bytes 262144 | tf_op jit(solution)/shard_map/all_to_all | solution.py:611
  18.2 0.0 copy-done.5
  18.2 1.8 %collective-permute-start = (f32[2,32,256]{2,1,0:T(8,128)S(1)}, f32[2,32,256]{2,1,0:T(8,128)S(1)}, u32[]{:S(2)}, u32[]{:S(2)}) collective-permute-start(f32[2,32,256]{2,1,0:T(8,128)S(1)} %copy-done.5), channel_id=1, source_target_pairs={{0,1},{1,0},{2,3},{3,2},{4,5},{5,4},{6,7},{7,6},{8,9},{9,8},{10,11... | collective-permute-start | bytes 196616 | tf_op jit(solution)/shard_map/ppermute | solution.py:594
  20.0 3.3 %collective-permute-done.halo = f32[2,32,256]{2,1,0:T(8,128)S(1)} collective-permute-done((f32[2,32,256]{2,1,0:T(8,128)S(1)}, f32[2,32,256]{2,1,0:T(8,128)S(1)}, u32[]{:S(2)}, u32[]{:S(2)}) %collective-permute-start) | collective-permute-done | bytes 65568 | tf_op jit(solution)/shard_map/ppermute | solution.py:594
  23.3 6.5 %own_sums.1 = (f32[32,32,256]{2,1,0:T(8,128)}, f32[32,16,256]{2,1,0:T(8,128)}, f32[32,16,256]{2,1,0:T(8,128)}, f32[32,16,256]{2,1,0:T(8,128)}, f32[32,16,256]{2,1,0:T(8,128)}) custom-call(f32[32,27]{1,0:T(8,128)} %weight.3, f32[32,32]{1,0:T(8,128)} %point.3, f32[32,64,256]{2,1,0:T(8,128)} %bitcast.14, f32[2,32,256]{2,1,0:T(8,128)S(1)} %collective-permute-done.halo), custom_call_target="tpu_custom_call" | custom-call | flops 100000000 | bytes 262144 | tf_op jit(solution)/shard_map/own_sums/pallas_call | solution.py:473
  29.8 2.7 %all-to-all-done = f32[32,8,128]{2,1,0:T(8,128)S(1)} async-done(((f32[32,8,128]{2,1,0:T(8,128)}), f32[32,8,128]{2,1,0:T(8,128)S(1)}, u32[]{:S(2)}, u32[]{:S(2)}) %all-to-all-start) | async-done | bytes 131104 | tf_op jit(solution)/shard_map/all_to_all | solution.py:611
  32.5 0.9 %copy-done.3 = f32[2,16,8,64]{3,2,1,0:T(8,128)S(1)} copy-done((f32[2,16,8,64]{3,2,1,0:T(8,128)S(1)}, f32[2,16,8,64]{3,2,1,0:T(8,128)}, u32[]{:S(2)}) %copy-start.3) | copy-done | bytes 65560
  33.4 1.9 %filter_modes.1 = f32[256,128]{1,0:T(8,128)S(1)} custom-call(f32[256,128]{1,0:T(8,128)S(1)} %bitcast.9, f32[2,16,8,64]{3,2,1,0:T(8,128)S(1)} %copy-done.3, bf16[256,256]{1,0:T(8,128)(2,1)} %constant.28.clone.f_top, bf16[256,256]{1,0:T(8,128)(2,1)} %constant.29.clone.f_rest, bf16[512,128]{1,0:T(8,128)(2,1)} %constant.30.clone.i_top, ...), custom_call_target="tpu_custom_call" | custom-call | flops 100000000 | bytes 262144 | tf_op jit(solution)/shard_map/filter_modes/pallas_call | solution.py:410
  35.3 0.0 copy-start.2
  35.4 0.6 copy-done.2
  36.0 5.8 %all-to-all-start.1 = ((f32[32,8,128]{2,1,0:T(8,128)}), f32[32,8,128]{2,1,0:T(8,128)S(1)}, u32[]{:S(2)}, u32[]{:S(2)}) async-start(f32[32,8,128]{2,1,0:T(8,128)} %bitcast.11), calls=%async_computation.1 | async-start | bytes 262144 | tf_op jit(solution)/shard_map/all_to_all | solution.py:613
  41.9 0.3 collective-permute-start.3
  42.2 4.2 %collective-permute-start.4 = (f32[32,16,256]{2,1,0:T(8,128)}, f32[32,16,256]{2,1,0:T(8,128)}, u32[]{:S(2)}, u32[]{:S(2)}) collective-permute-start(f32[32,16,256]{2,1,0:T(8,128)} %get-tuple-element.28), channel_id=1, source_target_pairs={{0,30},{2,0},{4,2},{6,4},{8,6},{10,8},{12,10},{14,12},{16,14},{18,... | collective-permute-start | bytes 1572872 | tf_op jit(solution)/shard_map/ppermute | solution.py:580
  46.4 4.7 %all-to-all-done.1 = f32[32,8,128]{2,1,0:T(8,128)S(1)} async-done(((f32[32,8,128]{2,1,0:T(8,128)}), f32[32,8,128]{2,1,0:T(8,128)S(1)}, u32[]{:S(2)}, u32[]{:S(2)}) %all-to-all-start.1) | async-done | bytes 131104 | tf_op jit(solution)/shard_map/all_to_all | solution.py:613
  51.0 0.0 collective-permute-start.5
  51.0 0.0 collective-permute-done.2.refs_2_
  51.0 4.4 %collective-permute-start.6 = (f32[32,16,256]{2,1,0:T(8,128)}, f32[32,16,256]{2,1,0:T(8,128)S(1)}, u32[]{:S(2)}, u32[]{:S(2)}) collective-permute-start(f32[32,16,256]{2,1,0:T(8,128)} %get-tuple-element.34), channel_id=1, source_target_pairs={{0,30},{2,0},{4,2},{6,4},{8,6},{10,8},{12,10},{14,12},{16,14},{18,... | collective-permute-start | bytes 1572872 | tf_op jit(solution)/shard_map/ppermute | solution.py:580
  55.5 0.0 collective-permute-done.1.refs_0_
  55.5 9.8 %middle_sums.1.middle = f32[32,32,256]{2,1,0:T(8,128)} custom-call(f32[32,27]{1,0:T(8,128)} %weight.3, f32[32,32]{1,0:T(8,128)} %point.3, f32[34,32,256]{2,1,0:T(8,128)S(1)} %collective-permute-done.1.refs_0_, f32[34,32,256]{2,1,0:T(8,128)S(1)} %copy-done, f32[34,32,256]{2,1,0:T(8,128)S(1)} %collective-permute-done.2.refs_2_), custom_call_target="tpu_custom_call" | custom-call | flops 100000000 | bytes 262144 | tf_op jit(solution)/shard_map/middle_sums/pallas_call | solution.py:500
  65.3 0.0 collective-permute-done.3.refs_0_
  65.3 0.0 collective-permute-done.4.refs_1_
  65.3 5.5 %inverse_modes.1 = (f32[32,64,256]{2,1,0:T(8,128)}, f32[32,16,256]{2,1,0:T(8,128)S(1)}) custom-call(f32[16,16,128]{2,1,0:T(8,128)S(1)} %bitcast.8, f32[32]{0:T(128)S(1)} %copy-done.4, bf16[2,128,512]{2,1,0:T(8,128)(2,1)} %constant.32.clone.x_top, bf16[2,128,512]{2,1,0:T(8,128)(2,1)} %constant.33.clone.x_rest, bf16[2,256,128]{2,1,0:T(8,128)(2,1)} %constant.34.clone.y_top, ...), custom_call_target="tpu_custom_call" | custom-call | flops 100000000 | bytes 262144 | tf_op jit(solution)/shard_map/inverse_modes/pallas_call | solution.py:424
  70.8 0.0 collective-permute-done.5.low
  70.8 0.0 collective-permute-done.6.high
  70.8 1.0 %finished_rows.1 = f32[32,64,256]{2,1,0:T(8,128)} custom-call(f32[32,64,256]{2,1,0:T(8,128)} %get-tuple-element.29._, f32[32,16,256]{2,1,0:T(8,128)S(1)} %get-tuple-element.30.base, f32[32,16,256]{2,1,0:T(8,128)S(1)} %collective-permute-done.5.low, f32[32,16,256]{2,1,0:T(8,128)S(1)} %collective-permute-done.6.high), custom_call_target="tpu_custom_call", output_to_operand_aliasing={{}: (0, {})} | custom-call | flops 100000000 | bytes 262144 | tf_op jit(solution)/shard_map/finished_rows/pallas_call | solution.py:526
  (5 shorter events, 0.0 us)
Async XLA Ops:
  2.5 15.7 %copy-start.5 = (f32[2,32,256]{2,1,0:T(8,128)S(1)}, f32[2,32,256]{2,1,0:T(8,128)}, u32[]{:S(2)}) copy-start(f32[2,32,256]{2,1,0:T(8,128)} %get-tuple-element.23) | copy-start | bytes 196612
  2.5 48.6 %collective-permute-start.2 = (f32[34,32,256]{2,1,0:T(8,128)}, f32[34,32,256]{2,1,0:T(8,128)S(1)}, u32[]{:S(2)}, u32[]{:S(2)}) collective-permute-start(f32[34,32,256]{2,1,0:T(8,128)} %get-tuple-element.26.refs_1_), channel_id=1, source_target_pairs={{0,30},{2,0},{4,2},{6,4},{8,6},{10,8},{12,10},{14,12},{16,14},{18,... | collective-permute-start | bytes 3342344 | tf_op jit(solution)/shard_map/ppermute | solution.py:580
  8.0 47.5 %collective-permute-start.1 = (f32[34,32,256]{2,1,0:T(8,128)}, f32[34,32,256]{2,1,0:T(8,128)S(1)}, u32[]{:S(2)}, u32[]{:S(2)}) collective-permute-start(f32[34,32,256]{2,1,0:T(8,128)} %get-tuple-element.26.refs_1_), channel_id=1, source_target_pairs={{0,2},{2,4},{4,6},{6,8},{8,10},{10,12},{12,14},{14,16},{16,18},{18... | collective-permute-start | bytes 3342344 | tf_op jit(solution)/shard_map/ppermute | solution.py:579
  11.8 0.7 copy-start.1
  12.4 43.0 %copy-start = (f32[34,32,256]{2,1,0:T(8,128)S(1)}, f32[34,32,256]{2,1,0:T(8,128)}, u32[]{:S(2)}) copy-start(f32[34,32,256]{2,1,0:T(8,128)} %get-tuple-element.26.refs_1_) | copy-start | bytes 3342340
  12.4 20.1 %all-to-all-start = ((f32[32,8,128]{2,1,0:T(8,128)}), f32[32,8,128]{2,1,0:T(8,128)S(1)}, u32[]{:S(2)}, u32[]{:S(2)}) async-start(f32[32,8,128]{2,1,0:T(8,128)} %bitcast.10), calls=%async_computation | async-start | bytes 262144 | tf_op jit(solution)/shard_map/all_to_all | solution.py:611
  18.2 5.1 %collective-permute-start = (f32[2,32,256]{2,1,0:T(8,128)S(1)}, f32[2,32,256]{2,1,0:T(8,128)S(1)}, u32[]{:S(2)}, u32[]{:S(2)}) collective-permute-start(f32[2,32,256]{2,1,0:T(8,128)S(1)} %copy-done.5), channel_id=1, source_target_pairs={{0,1},{1,0},{2,3},{3,2},{4,5},{5,4},{6,7},{7,6},{8,9},{9,8},{10,11... | collective-permute-start | bytes 196616 | tf_op jit(solution)/shard_map/ppermute | solution.py:594
  32.5 0.9 %copy-start.3 = (f32[2,16,8,64]{3,2,1,0:T(8,128)S(1)}, f32[2,16,8,64]{3,2,1,0:T(8,128)}, u32[]{:S(2)}) copy-start(f32[2,16,8,64]{3,2,1,0:T(8,128)} %gains) | copy-start | bytes 196612
  35.3 0.7 copy-start.2
  36.0 15.0 %all-to-all-start.1 = ((f32[32,8,128]{2,1,0:T(8,128)}), f32[32,8,128]{2,1,0:T(8,128)S(1)}, u32[]{:S(2)}, u32[]{:S(2)}) async-start(f32[32,8,128]{2,1,0:T(8,128)} %bitcast.11), calls=%async_computation.1 | async-start | bytes 262144 | tf_op jit(solution)/shard_map/all_to_all | solution.py:613
  41.9 23.5 %collective-permute-start.3 = (f32[32,16,256]{2,1,0:T(8,128)}, f32[32,16,256]{2,1,0:T(8,128)}, u32[]{:S(2)}, u32[]{:S(2)}) collective-permute-start(f32[32,16,256]{2,1,0:T(8,128)} %get-tuple-element.27), channel_id=1, source_target_pairs={{0,2},{2,4},{4,6},{6,8},{8,10},{10,12},{12,14},{14,16},{16,18},{18... | collective-permute-start | bytes 1572872 | tf_op jit(solution)/shard_map/ppermute | solution.py:579
  42.2 23.2 %collective-permute-start.4 = (f32[32,16,256]{2,1,0:T(8,128)}, f32[32,16,256]{2,1,0:T(8,128)}, u32[]{:S(2)}, u32[]{:S(2)}) collective-permute-start(f32[32,16,256]{2,1,0:T(8,128)} %get-tuple-element.28), channel_id=1, source_target_pairs={{0,30},{2,0},{4,2},{6,4},{8,6},{10,8},{12,10},{14,12},{16,14},{18,... | collective-permute-start | bytes 1572872 | tf_op jit(solution)/shard_map/ppermute | solution.py:580
  51.0 14.3 %copy-start.4 = (f32[32]{0:T(128)S(1)}, f32[32]{0:T(128)}, u32[]{:S(2)}) copy-start(f32[32]{0:T(128)} %bias.1) | copy-start | bytes 388
  51.0 19.8 %collective-permute-start.5 = (f32[32,16,256]{2,1,0:T(8,128)}, f32[32,16,256]{2,1,0:T(8,128)S(1)}, u32[]{:S(2)}, u32[]{:S(2)}) collective-permute-start(f32[32,16,256]{2,1,0:T(8,128)} %get-tuple-element.32), channel_id=1, source_target_pairs={{0,2},{2,4},{4,6},{6,8},{8,10},{10,12},{12,14},{14,16},{16,18},{18... | collective-permute-start | bytes 1572872 | tf_op jit(solution)/shard_map/ppermute | solution.py:579
  51.0 19.8 %collective-permute-start.6 = (f32[32,16,256]{2,1,0:T(8,128)}, f32[32,16,256]{2,1,0:T(8,128)S(1)}, u32[]{:S(2)}, u32[]{:S(2)}) collective-permute-start(f32[32,16,256]{2,1,0:T(8,128)} %get-tuple-element.34), channel_id=1, source_target_pairs={{0,30},{2,0},{4,2},{6,4},{8,6},{10,8},{12,10},{14,12},{16,14},{18,... | collective-permute-start | bytes 1572872 | tf_op jit(solution)/shard_map/ppermute | solution.py:580

commit v5 on v4

--- a/solution.py
+++ b/solution.py
@@ -37,47 +37,23 @@
     return jnp.asarray(top), jnp.asarray(rest)
 
 
-def y_forward_table(y_local, gy, group):
-    out = np.zeros((gy, 2, group, MY, group, y_local))
+def y_table(y_local, gy, inverse):
+    out = []
     for g in range(gy):
-        c, s = trig(kept(MY, y_local * gy), g * y_local + np.arange(y_local), y_local * gy)
-        for i in range(group):
-            out[g, 0, i, :, i] = c
-            out[g, 1, i, :, i] = s
-    return out.reshape(gy, 2 * group * MY, group * y_local)
-
-
-def x_forward_table():
+        places = g * y_local + np.arange(y_local)
+        out.append(np.concatenate(trig(kept(MY, y_local * gy), places, y_local * gy), axis=0))
+    return np.stack([t.T for t in out] if inverse else out)
+
+
+def x_table(inverse, scale=1.0):
     c, s = trig(np.arange(MX), np.arange(NX), NX)
-    out = np.zeros((2, 2, NX, 2, 2, MX))
+    w = np.where(np.arange(MX) == 0, 1.0, 2.0)[:, None] if inverse else 1.0
+    out = np.zeros((2, 2, 2, MX, NX))
     for p in range(2):
-        out[p, 0, :, p, 0] = c.T
-        out[p, 0, :, p, 1] = -s.T
-        out[p, 1, :, p, 0] = -s.T
-        out[p, 1, :, p, 1] = -c.T
-    return out.reshape(4, NX, 4 * MX)
-
-
-def x_inverse_table(scale):
-    c, s = trig(np.arange(MX), np.arange(NX), NX)
-    w = np.where(np.arange(MX) == 0, 1.0, 2.0)[:, None] * scale
-    out = np.zeros((2, 2, 2, MX, 2, NX))
-    for p in range(2):
-        out[p, p, 0, :, 0] = w * c
-        out[p, p, 1, :, 0] = -w * s
-        out[p, p, 0, :, 1] = w * s
-        out[p, p, 1, :, 1] = w * c
-    return out.reshape(2, 4 * MX, 2 * NX)
-
-
-def y_inverse_table(y_local, gy, group):
-    out = np.zeros((gy, group, y_local, 2, group, MY))
-    for g in range(gy):
-        c, s = trig(kept(MY, y_local * gy), g * y_local + np.arange(y_local), y_local * gy)
-        for i in range(group):
-            out[g, i, :, 0, i] = c.T
-            out[g, i, :, 1, i] = -s.T
-    return out.reshape(gy, group * y_local, 2 * group * MY)
+        out[p, p, 0] = w * c * scale
+        out[p, p, 1] = -w * s * scale
+    out = out.reshape(2, 4 * MX, NX)
+    return out if inverse else out.transpose(0, 2, 1)
 
 
 def z_tables(gz, gy, rows, scale):
@@ -105,29 +81,42 @@
     return both[:rows] + (both[rows:] + dot(a[0], b[1]))
 
 
-def forward_kernel(group, field, y_top, y_rest, x_top, x_rest, out, turned):
-    gy = lax.axis_index("gy")
-    y_table = (y_top[gy], y_rest[gy])
-    half = group * MY
-    step = pl.program_id(0)
-    for p in range(2):
-        rows = jnp.concatenate([field[2 * i + p] for i in range(group)], axis=0)
-        both = dot3(y_table, parts(rows))
-        for t in range(2):
-            at = pl.multiple_of(step * half, half)
-            turned[2 * p + t, pl.ds(at, half), :] = both[t * half : (t + 1) * half]
-    @pl.when(step == pl.num_programs(0) - 1)
-    def _():
-        total = dot3(parts(turned[0]), (x_top[0], x_rest[0]))
-        for k in range(1, 4):
-            total = total + dot3(parts(turned[k]), (x_top[k], x_rest[k]))
-        out[...] = total.reshape(CH // 2, MY, 4 * MX)
-
-
 def swap_parts(value):
     lane = lax.broadcasted_iota(jnp.int32, value.shape, 1)
     is_real = (lane // MX) % 2 == 0
-    return jnp.where(is_real, pltpu.roll(value, 4 * MX - MX, 1), pltpu.roll(value, MX, 1)), is_real
+    width = value.shape[1]
+    return jnp.where(is_real, pltpu.roll(value, width - MX, 1), pltpu.roll(value, MX, 1)), is_real
+
+
+def forward_kernel(field, x_top, x_rest, y_top, y_rest, out, taken, x_both, y_both, sem):
+    gy = lax.axis_index("gy")
+    few = [
+        pltpu.make_async_copy(src, dst, sem.at[4 + i])
+        for i, (src, dst) in enumerate(
+            ((x_top, x_both.at[0]), (x_rest, x_both.at[1]), (y_top.at[gy], y_both.at[0]), (y_rest.at[gy], y_both.at[1]))
+        )
+    ]
+    copies = [pltpu.make_async_copy(field.at[:, q], taken.at[q], sem.at[q]) for q in range(4)]
+    for copy in few + copies:
+        copy.start()
+    for copy in few:
+        copy.wait()
+    groups, rows = taken.shape[1:3]
+    halves_of = []
+    for q in range(4):
+        copies[q].wait()
+        part = dot3(parts(taken[q].reshape(groups * rows, NX)), (x_both[0, q % 2], x_both[1, q % 2]))
+        if q % 2:
+            halves_of[-1] = halves_of[-1] + part
+        else:
+            halves_of.append(part)
+    total = jnp.concatenate(halves_of, axis=1)
+    for g in range(groups):
+        both = dot3((y_both[0], y_both[1]), parts(total[g * rows : (g + 1) * rows]))
+        crossed, is_real = swap_parts(both[MY:])
+        modes = both[:MY] + jnp.where(is_real, crossed, -crossed)
+        out[pl.ds(2 * g * MY, MY), :] = modes[:, : 4 * MX]
+        out[pl.ds((2 * g + 1) * MY, MY), :] = modes[:, 4 * MX :]
 
 
 def filter_kernel(arrived, gains, f_top, f_rest, i_top, i_rest, out):
@@ -315,12 +304,8 @@
     rows = out.shape[1]
     for a in (1, 0, 2):
         arrivals[a].wait()
-
-        def one(r, _):
+        for r in range(rows + 2):
             turn(turned, r, taken[a, r])
-            return 0
-
-        lax.fori_loop(0, rows + 2, one, 0, unroll=2)
         tap_sums(turned, depth, gains, [(0, 0, rows)], [a], a == 1)
     copies = []
     for t in range(rows // 8):
@@ -335,33 +320,40 @@
     return 0.5 * value * (1.0 + lax.erf(value * (1.0 / math.sqrt(2.0))))
 
 
-def inverse_kernel(group, plan, modes, bias, x_top, x_rest, y_top, y_rest, middle, own, *refs):
+def inverse_kernel(plan, modes, bias, x_top, x_rest, y_top, y_rest, middle, own, *refs):
     upper, lower = plan
-    out, base = refs[-2:]
-    step = pl.program_id(0)
-    gy = lax.axis_index("gy")
-    y_table = (y_top[gy], y_rest[gy])
-    mode_rows = parts(modes[...].reshape(group * MY, 4 * MX))
-    y_local = out.shape[1]
+    out, base, columns = refs[-3:]
+    q = pl.program_id(0)
+    groups, _, y_local, _ = out.shape
+
+    @pl.when(q == 0)
+    def _():
+        gy = lax.axis_index("gy")
+        for g in range(groups):
+            own_modes = jnp.concatenate([modes[2 * g], modes[2 * g + 1]], axis=1)
+            crossed, is_real = swap_parts(own_modes)
+            stack = jnp.concatenate([own_modes, jnp.where(is_real, -crossed, crossed)], axis=0)
+            pair = parts(dot3((y_top[gy], y_rest[gy]), parts(stack)))
+            for h in range(2):
+                for k in range(2):
+                    columns[h, k, pl.ds(g * y_local, y_local), :] = pair[k][:, 128 * h : 128 * h + 128]
+
+    h, p = q // 2, q % 2
+    rows = dot3((columns[h, 0], columns[h, 1]), (x_top[p], x_rest[p]))
     start, stop = 8 * upper[-1] + 8, 8 * lower[0]
-    for p in range(2):
-        wide = dot3(mode_rows, (x_top[p], x_rest[p]))
-        tall = jnp.concatenate([wide[:, :NX], wide[:, NX:]], axis=0)
-        planes = dot3(y_table, parts(tall)).reshape(group, y_local, NX)
-        for i in range(group):
-            c = 2 * i + p
-            plane = planes[i] + bias[step * 2 * group + c]
-            out[c, start:stop] = gelu(plane[start:stop] + middle[c])
-            first = plane[:start] + own[c, :start]
-            second = plane[stop:] + own[c, start:]
-            base[c, :8] = first[:8]
-            base[c, 8:] = second[-8:]
-            if start > 8:
-                low, high = refs[:2]
-                out[c, 8:start] = gelu(first[8:] + (low[c, : start - 8] + high[c, : start - 8]))
-                out[c, stop : y_local - 8] = gelu(
-                    second[:-8] + (low[c, start - 8 :] + high[c, start - 8 :])
-                )
+    for g in range(groups):
+        plane = rows[g * y_local : (g + 1) * y_local] + bias[4 * g + q]
+        out[g, 0, start:stop] = gelu(plane[start:stop] + middle[g, 0])
+        first = plane[:start] + own[g, 0, :start]
+        second = plane[stop:] + own[g, 0, start:]
+        base[g, 0, :8] = first[:8]
+        base[g, 0, 8:] = second[-8:]
+        if start > 8:
+            low, high = refs[:2]
+            out[g, 0, 8:start] = gelu(first[8:] + (low[g, 0, : start - 8] + high[g, 0, : start - 8]))
+            out[g, 0, stop : y_local - 8] = gelu(
+                second[:-8] + (low[g, 0, start - 8 :] + high[g, 0, start - 8 :])
+            )
 
 
 def finish_kernel(_, base, low, high, out):
@@ -384,24 +376,28 @@
     return pl.BlockSpec(table.shape, lambda i: (0,) * table.ndim)
 
 
-def forward_call(field, gy):
+def by_four(array):
+    return array.reshape(CH // 4, 4, *array.shape[1:])
+
+
+def forward_call(field, gy, pinned):
     y_local = field.shape[1]
-    group = max(1, min(CH // 2, 256 // y_local))
-    tables = [*halves(y_forward_table(y_local, gy, group)), *halves(x_forward_table())]
+    tables = [*halves(x_table(False)), *halves(y_table(y_local, gy, False))]
+    hbm = pl.BlockSpec(memory_space=pltpu.HBM)
     return pl.pallas_call(
-        functools.partial(forward_kernel, group),
-        out_shape=jax.ShapeDtypeStruct((CH // 2, MY, 4 * MX), F32),
-        grid=(CH // 2 // group,),
-        in_specs=[
-            pl.BlockSpec((2 * group, y_local, NX), lambda i: (i, 0, 0)),
-            *[whole_block(t) for t in tables],
+        forward_kernel,
+        out_shape=(pltpu.HBM if pinned else jax.ShapeDtypeStruct)((CH // 2 * MY, 4 * MX), F32),
+        in_specs=[hbm] * 5,
+        scratch_shapes=[
+            pltpu.VMEM((4, CH // 4, y_local, NX), F32),
+            pltpu.VMEM((2, 2, NX, 4 * MX), BF),
+            pltpu.VMEM((2, 2 * MY, y_local), BF),
+            pltpu.SemaphoreType.DMA((8,)),
         ],
-        out_specs=pl.BlockSpec((CH // 2, MY, 4 * MX), lambda i: (0, 0, 0)),
-        scratch_shapes=[pltpu.VMEM((4, CH // 2 * MY, NX), F32)],
         compiler_params=params(),
         cost_estimate=cost(10**8, 2**18),
         name="forward_modes",
-    )(*in_hbm(field, *tables))
+    )(*in_hbm(by_four(field), *tables))
 
 
 def filter_call(arrived, gains, gz, gy, scale):
@@ -409,36 +405,37 @@
     fwd, inv = halves(fwd), halves(inv)
     return pl.pallas_call(
         filter_kernel,
-        out_shape=jax.ShapeDtypeStruct(arrived.shape, F32),
+        out_shape=pltpu.HBM(arrived.shape, F32),
         compiler_params=params(),
         cost_estimate=cost(10**8, 2**18),
         name="filter_modes",
-    )(arrived, gains, *in_hbm(*fwd, *inv))
+    )(arrived, *in_hbm(gains, *fwd, *inv))
 
 
 def inverse_call(modes, bias, middle, own, pair, plan, y_local, gy, scale):
-    group = 4
-    tables = [*halves(x_inverse_table(scale)), *halves(y_inverse_table(y_local, gy, group))]
-    some = lambda rows: pl.BlockSpec((2 * group, rows, NX), lambda i: (i, 0, 0))
-    planes = [*in_hbm(middle, own), *pair]
-    return pl.pallas_call(
-        functools.partial(inverse_kernel, group, plan),
+    tables = [*halves(x_table(True, scale)), *halves(y_table(y_local, gy, True))]
+    some = lambda rows: pl.BlockSpec((CH // 4, 1, rows, NX), lambda i: (0, i, 0, 0))
+    planes = [*in_hbm(by_four(middle), by_four(own)), *map(by_four, pair)]
+    result, base = pl.pallas_call(
+        functools.partial(inverse_kernel, plan),
         out_shape=[
-            jax.ShapeDtypeStruct((CH, y_local, NX), F32),
-            jax.ShapeDtypeStruct((CH, 16, NX), F32),
+            jax.ShapeDtypeStruct((CH // 4, 4, y_local, NX), F32),
+            jax.ShapeDtypeStruct((CH // 4, 4, 16, NX), F32),
         ],
-        grid=(CH // 2 // group,),
+        grid=(4,),
         in_specs=[
-            pl.BlockSpec((group, MY, 4 * MX), lambda i: (i, 0, 0)),
+            whole_block(modes),
             pl.BlockSpec(memory_space=pltpu.SMEM),
             *[whole_block(t) for t in tables],
-            *[some(p.shape[1]) for p in planes],
+            *[some(p.shape[2]) for p in planes],
         ],
         out_specs=[some(y_local), some(16)],
+        scratch_shapes=[pltpu.VMEM((2, 2, CH // 4 * y_local, 128), BF)],
         compiler_params=params(),
         cost_estimate=cost(10**8, 2**18),
         name="inverse_modes",
-    )(modes, bias, *in_hbm(*tables), *planes)
+    )(modes, *in_hbm(bias, *tables), *planes)
+    return result.reshape(CH, y_local, NX), base.reshape(CH, 16, NX)
 
 
 def pack_call(field, middle):
@@ -517,7 +514,7 @@
         compiler_params=params(),
         cost_estimate=cost(10**8, 2**18),
         name="middle_sums",
-    )(*in_hbm(weight, point), low, own, high)
+    )(*in_hbm(weight, point), low, *in_hbm(own), high)
 
 
 def finish_call(result, base, low, high):
@@ -599,25 +596,26 @@
                 lax.ppermute(edges[1], "gy", ring("gy", gy, -1)),
             ]
         )
-    coarse = forward_call(after(field, packed), gy)
+    j_own, n_own = spectral_filter.shape[2], spectral_filter.shape[3]
+    whole_tiles = j_own == 8 and n_own == 2 * MX
+    coarse = forward_call(after(field, packed), gy, whole_tiles)
+    coarse = after(coarse, halo)
     sums = own_call(after(field, coarse), halo, depth_weight, point_weight, upper, lower)
     own, down, up = sums[:3]
     inner_pair = to_neighbours(*sums[3:]) if len(sums) > 3 else ()
 
-    j_own, n_own = spectral_filter.shape[2], spectral_filter.shape[3]
-    if j_own == 8 and n_own == 2 * MX:
+    if whole_tiles:
         both = ("gz", "gy")
-        sent = coarse.reshape(gz * gy * 8, 4 * MX)
-        got = lax.all_to_all(sent, both, split_axis=0, concat_axis=0, tiled=True)
+        got = lax.all_to_all(coarse, both, split_axis=0, concat_axis=0, tiled=True)
         out = filter_call(got, after(spectral_filter, own), gz, gy, forward_scale)
         back = lax.all_to_all(out, both, split_axis=0, concat_axis=0, tiled=True)
         back = back.reshape(CH // 2, MY, 4 * MX)
     else:
         back = general_filter(coarse, spectral_filter, gz, gy, forward_scale)
 
-    down, up = (after(value, back) for value in (down, up))
+    down, up, packed, *inner_pair = lax.optimization_barrier((down, up, packed, *inner_pair, back))[:-1]
     outer_pair = to_neighbours(down, up)
-    mixed = middle_call(depth_weight, point_weight, packed_low, after(packed, back), packed_high)
+    mixed = middle_call(depth_weight, point_weight, packed_low, packed, packed_high)
     result, base = inverse_call(
         back, bias_vector, mixed, own, inner_pair, (upper, lower), y_local, gy, inverse_scale
     )

time: 72.3 us -> 78.6 us (1.087)
  blocking collectives: 0 us -> 14.5 us
  starting transfers between devices: 27.8 us -> 18.5 us
  waiting for transfers between devices: 10.6 us -> 16.6 us
  Pallas kernels: 31 us -> 28.6 us
  local copies, waits for them, and re-layouts: 2.21 us -> 0 us
    all_to_all x0 -> x1, blocking collectives: none -> 14.5 us  [body(): back = lax.all_to_all(out, both, split_axis=0, concat_axis=0, tiled=True)]
    all_to_all x2 -> x1, waiting for transfers between devices: 7.36 us -> 16.5 us  [body(): got = lax.all_to_all(coarse, both, split_axis=0, concat_axis=0, tiled=True)]
    all_to_all x2 -> x1, starting transfers between devices: 11.6 us -> 2.56 us  [body(): got = lax.all_to_all(coarse, both, split_axis=0, concat_axis=0, tiled=True)]
    ppermute x1, waiting for transfers between devices: 3.25 us -> 0.01 us  [body(): halo = lax.ppermute(edges, 'gy', ring('gy', gy, 1))]
    pallas_call x1, Pallas kernels: 9.83 us -> 6.84 us  [middle_call(): pl.pallas_call(middle_kernel, out_shape=pltpu.HBM((CH, rows, NX), F32), i...]
    unnamed x12 -> x0, local copies, waits for them, and re-layouts: 2.21 us -> none
  transfers between devices with their start and end apart: 9 -> 8, of which waited for: 3 -> 1; matrix products, arithmetic and copies ran while one was open for 0% -> 0% of each run, Pallas kernels for 38% -> 32%
where the time goes in v5:
time: 78.6 us; the launch traced here: 78.2 us
  Pallas kernels  28.6 us (36%)
  starting transfers between devices  18.5 us (24%)
  waiting for transfers between devices  16.6 us (21%)
  blocking collectives  14.5 us (18%)
    all_to_all x1, waiting for transfers between devices, body(): got = lax.all_to_all(coarse, both, split_axis=0, concat_axis=0, tiled=True)  16.5 us
    all_to_all x1, blocking collectives, body(): back = lax.all_to_all(out, both, split_axis=0, concat_axis=0, tiled=True)  14.5 us
    ppermute x3, starting transfers between devices, to_neighbours(): lax.ppermute(up, 'gz', ring('gz', gz, -1))  14.4 us
    pallas_call x1, Pallas kernels, middle_call(): pl.pallas_call(middle_kernel, out_shape=pltpu.HBM((CH, rows, NX), F32), i...  6.84 us
    pallas_call x1, Pallas kernels, own_call(): pl.pallas_call(functools.partial(own_kernel, (upper, lower, len(shapes)))...  6.54 us
    pallas_call x1, Pallas kernels, inverse_call(): pl.pallas_call(functools.partial(inverse_kernel, plan), out_shape=[jax.Sh...  5.01 us
    pallas_call x1, Pallas kernels, forward_call(): pl.pallas_call(forward_kernel, out_shape=(pltpu.HBM if pinned else jax.Sh...  4.12 us
    pallas_call x1, Pallas kernels, filter_call(): pl.pallas_call(filter_kernel, out_shape=pltpu.HBM(arrived.shape, F32), co...  2.63 us
  transfers between devices with their start and end apart: 8, of which 1 were waited for; matrix products, arithmetic and copies ran while one was open for 0% of the time, Pallas kernels for 32%

profile of v5, /device:TPU:0, one launch (start us, length us, event | category | flops | bytes accessed | tf_op | source)
XLA Modules:
  0.0 78.2 jit_solution(13502553530599159293)
XLA Ops:
  0.0 2.4 %packed_rows.1 = (f32[34,32,256]{2,1,0:T(8,128)}, f32[2,32,256]{2,1,0:T(8,128)}) custom-call(f32[32,64,256]{2,1,0:T(8,128)} %bitcast.20), custom_call_target="tpu_custom_call" | custom-call | flops 100000000 | bytes 262144 | tf_op jit(solution)/shard_map/packed_rows/pallas_call | solution.py:445
  2.5 5.5 %collective-permute-start.4 = (f32[34,32,256]{2,1,0:T(8,128)}, f32[34,32,256]{2,1,0:T(8,128)S(1)}, u32[]{:S(2)}, u32[]{:S(2)}) collective-permute-start(f32[34,32,256]{2,1,0:T(8,128)} %get-tuple-element.34.refs_1_), channel_id=1, source_target_pairs={{0,30},{2,0},{4,2},{6,4},{8,6},{10,8},{12,10},{14,12},{16,14},{18,... | collective-permute-start | bytes 3342344 | tf_op jit(solution)/shard_map/ppermute | solution.py:577
  8.0 0.0 collective-permute-start.1
  8.0 1.5 %collective-permute-start = (f32[2,32,256]{2,1,0:T(8,128)}, f32[2,32,256]{2,1,0:T(8,128)S(1)}, u32[]{:S(2)}, u32[]{:S(2)}) collective-permute-start(f32[2,32,256]{2,1,0:T(8,128)} %get-tuple-element.25), channel_id=1, source_target_pairs={{0,1},{1,0},{2,3},{3,2},{4,5},{5,4},{6,7},{7,6},{8,9},{9,8},{10,11... | collective-permute-start | bytes 196616 | tf_op jit(solution)/shard_map/ppermute | solution.py:591
  9.4 4.1 %forward_modes.1 = f32[256,128]{1,0:T(8,128)} custom-call(f32[8,4,64,256]{3,2,1,0:T(8,128)} %bitcast.21, bf16[2,256,128]{2,1,0:T(8,128)(2,1)} %constant.24.clone.x_top, bf16[2,256,128]{2,1,0:T(8,128)(2,1)} %constant.25.clone.x_rest, bf16[2,32,64]{2,1,0:T(8,128)(2,1)} %constant.26.clone.y_top, bf16[2,32,64]{2,1,0:T(8,128)(2,1)} %constant.27.clone.y_rest), custom_call_target="tpu_custom_call" | custom-call | flops 100000000 | bytes 262144 | tf_op jit(solution)/shard_map/forward_modes/pallas_call | solution.py:387
  13.6 0.0 collective-permute-done.halo
  13.6 6.5 %own_sums.1 = (f32[32,32,256]{2,1,0:T(8,128)}, f32[32,16,256]{2,1,0:T(8,128)}, f32[32,16,256]{2,1,0:T(8,128)}, f32[32,16,256]{2,1,0:T(8,128)}, f32[32,16,256]{2,1,0:T(8,128)}) custom-call(f32[32,27]{1,0:T(8,128)} %weight.3, f32[32,32]{1,0:T(8,128)} %point.3, f32[32,64,256]{2,1,0:T(8,128)} %bitcast.22, f32[2,32,256]{2,1,0:T(8,128)S(1)} %collective-permute-done.halo), custom_call_target="tpu_custom_call" | custom-call | flops 100000000 | bytes 262144 | tf_op jit(solution)/shard_map/own_sums/pallas_call | solution.py:470
  20.1 0.1 collective-permute-start.2
  20.2 4.4 %collective-permute-start.3 = (f32[32,16,256]{2,1,0:T(8,128)}, f32[32,16,256]{2,1,0:T(8,128)S(1)}, u32[]{:S(2)}, u32[]{:S(2)}) collective-permute-start(f32[32,16,256]{2,1,0:T(8,128)} %get-tuple-element.33), channel_id=1, source_target_pairs={{0,30},{2,0},{4,2},{6,4},{8,6},{10,8},{12,10},{14,12},{16,14},{18,... | collective-permute-start | bytes 1572872 | tf_op jit(solution)/shard_map/ppermute | solution.py:577
  24.6 2.6 %all-to-all-start = ((f32[32,8,128]{2,1,0:T(8,128)}), f32[32,8,128]{2,1,0:T(8,128)S(1)}, u32[]{:S(2)}, u32[]{:S(2)}) async-start(f32[32,8,128]{2,1,0:T(8,128)} %bitcast.2), calls=%async_computation | async-start | bytes 262144 | tf_op jit(solution)/shard_map/all_to_all | solution.py:609
  27.2 16.5 %all-to-all-done = f32[32,8,128]{2,1,0:T(8,128)S(1)} async-done(((f32[32,8,128]{2,1,0:T(8,128)}), f32[32,8,128]{2,1,0:T(8,128)S(1)}, u32[]{:S(2)}, u32[]{:S(2)}) %all-to-all-start) | async-done | bytes 131104 | tf_op jit(solution)/shard_map/all_to_all | solution.py:609
  43.7 2.6 %filter_modes.1 = f32[256,128]{1,0:T(8,128)} custom-call(f32[256,128]{1,0:T(8,128)S(1)} %bitcast.15, f32[2,16,8,64]{3,2,1,0:T(8,128)} %gains, bf16[256,256]{1,0:T(8,128)(2,1)} %constant.28.clone.f_top, bf16[256,256]{1,0:T(8,128)(2,1)} %constant.29.clone.f_rest, bf16[512,128]{1,0:T(8,128)(2,1)} %constant.30.clone.i_top, bf16[512,128]{1,0:T(8,128)(2,1)} %constant.31.clone.i_rest), custom_call_target="tpu_custom_call" | custom-call | flops 100000000 | bytes 262144 | tf_op jit(solution)/shard_map/filter_modes/pallas_call | solution.py:406
  46.4 14.5 %all_to_all.20 = f32[32,8,128]{2,1,0:T(8,128)S(1)} all-to-all(f32[32,8,128]{2,1,0:T(8,128)} %bitcast.26), channel_id=1, replica_groups=mesh['gz'=16,'gy'=2] {'gz','gy'}, dimensions={0} | all-to-all | bytes 262144 | tf_op jit(solution)/shard_map/all_to_all | solution.py:611
  60.8 0.0 collective-permute-done.2
  60.8 0.0 collective-permute-done.3
  60.9 0.0 collective-permute-start.5
  60.9 4.4 %collective-permute-start.6 = (f32[32,16,256]{2,1,0:T(8,128)}, f32[32,16,256]{2,1,0:T(8,128)S(1)}, u32[]{:S(2)}, u32[]{:S(2)}) collective-permute-start(f32[32,16,256]{2,1,0:T(8,128)} %get-tuple-element.40), channel_id=1, source_target_pairs={{0,30},{2,0},{4,2},{6,4},{8,6},{10,8},{12,10},{14,12},{16,14},{18,... | collective-permute-start | bytes 1572872 | tf_op jit(solution)/shard_map/ppermute | solution.py:577
  65.3 0.0 collective-permute-done.4.refs_2_
  65.3 0.0 collective-permute-done.1.refs_0_
  65.3 6.8 %middle_sums.1 = f32[32,32,256]{2,1,0:T(8,128)} custom-call(f32[32,27]{1,0:T(8,128)} %weight.3, f32[32,32]{1,0:T(8,128)} %point.3, f32[34,32,256]{2,1,0:T(8,128)S(1)} %collective-permute-done.1.refs_0_, f32[34,32,256]{2,1,0:T(8,128)} %get-tuple-element.34.refs_1_, f32[34,32,256]{2,1,0:T(8,128)S(1)} %collective-permute-done.4.refs_2_), custom_call_target="tpu_custom_call" | custom-call | flops 100000000 | bytes 262144 | tf_op jit(solution)/shard_map/middle_sums/pallas_call | solution.py:497
  72.2 5.0 %inverse_modes.1 = (f32[8,4,64,256]{3,2,1,0:T(8,128)}, f32[8,4,16,256]{3,2,1,0:T(8,128)S(1)}) custom-call(f32[16,16,128]{2,1,0:T(8,128)S(1)} %bitcast.19, f32[32]{0:T(128)} %bias.1, bf16[2,128,256]{2,1,0:T(8,128)(2,1)} %constant.32.clone.x_top, bf16[2,128,256]{2,1,0:T(8,128)(2,1)} %constant.33.clone.x_rest, bf16[2,64,32]{2,1,0:T(8,128)(2,1)} %constant.34.clone.y_top, ...), custom_call_target="tpu_custom_call" | custom-call | flops 100000000 | bytes 262144 | tf_op jit(solution)/shard_map/inverse_modes/pallas_call | solution.py:419
  77.2 0.0 collective-permute-done.5.low
  77.2 0.0 collective-permute-done.6.high
  77.2 1.0 %finished_rows.1 = f32[32,64,256]{2,1,0:T(8,128)} custom-call(f32[32,64,256]{2,1,0:T(8,128)} %bitcast.24, f32[32,16,256]{2,1,0:T(8,128)S(1)} %bitcast.18, f32[32,16,256]{2,1,0:T(8,128)S(1)} %collective-permute-done.5.low, f32[32,16,256]{2,1,0:T(8,128)S(1)} %collective-permute-done.6.high), custom_call_target="tpu_custom_call", output_to_operand_aliasing={{}: (0, {})} | custom-call | flops 100000000 | bytes 262144 | tf_op jit(solution)/shard_map/finished_rows/pallas_call | solution.py:523
Async XLA Ops:
  2.5 62.8 %collective-permute-start.4 = (f32[34,32,256]{2,1,0:T(8,128)}, f32[34,32,256]{2,1,0:T(8,128)S(1)}, u32[]{:S(2)}, u32[]{:S(2)}) collective-permute-start(f32[34,32,256]{2,1,0:T(8,128)} %get-tuple-element.34.refs_1_), channel_id=1, source_target_pairs={{0,30},{2,0},{4,2},{6,4},{8,6},{10,8},{12,10},{14,12},{16,14},{18,... | collective-permute-start | bytes 3342344 | tf_op jit(solution)/shard_map/ppermute | solution.py:577
  8.0 57.3 %collective-permute-start.1 = (f32[34,32,256]{2,1,0:T(8,128)}, f32[34,32,256]{2,1,0:T(8,128)S(1)}, u32[]{:S(2)}, u32[]{:S(2)}) collective-permute-start(f32[34,32,256]{2,1,0:T(8,128)} %get-tuple-element.34.refs_1_), channel_id=1, source_target_pairs={{0,2},{2,4},{4,6},{6,8},{8,10},{10,12},{12,14},{14,16},{16,18},{18... | collective-permute-start | bytes 3342344 | tf_op jit(solution)/shard_map/ppermute | solution.py:576
  8.0 5.6 %collective-permute-start = (f32[2,32,256]{2,1,0:T(8,128)}, f32[2,32,256]{2,1,0:T(8,128)S(1)}, u32[]{:S(2)}, u32[]{:S(2)}) collective-permute-start(f32[2,32,256]{2,1,0:T(8,128)} %get-tuple-element.25), channel_id=1, source_target_pairs={{0,1},{1,0},{2,3},{3,2},{4,5},{5,4},{6,7},{7,6},{8,9},{9,8},{10,11... | collective-permute-start | bytes 196616 | tf_op jit(solution)/shard_map/ppermute | solution.py:591
  20.1 40.7 %collective-permute-start.2 = (f32[32,16,256]{2,1,0:T(8,128)}, f32[32,16,256]{2,1,0:T(8,128)S(1)}, u32[]{:S(2)}, u32[]{:S(2)}) collective-permute-start(f32[32,16,256]{2,1,0:T(8,128)} %get-tuple-element.32), channel_id=1, source_target_pairs={{0,2},{2,4},{4,6},{6,8},{8,10},{10,12},{12,14},{14,16},{16,18},{18... | collective-permute-start | bytes 1572872 | tf_op jit(solution)/shard_map/ppermute | solution.py:576
  20.2 40.6 %collective-permute-start.3 = (f32[32,16,256]{2,1,0:T(8,128)}, f32[32,16,256]{2,1,0:T(8,128)S(1)}, u32[]{:S(2)}, u32[]{:S(2)}) collective-permute-start(f32[32,16,256]{2,1,0:T(8,128)} %get-tuple-element.33), channel_id=1, source_target_pairs={{0,30},{2,0},{4,2},{6,4},{8,6},{10,8},{12,10},{14,12},{16,14},{18,... | collective-permute-start | bytes 1572872 | tf_op jit(solution)/shard_map/ppermute | solution.py:577
  24.6 19.1 %all-to-all-start = ((f32[32,8,128]{2,1,0:T(8,128)}), f32[32,8,128]{2,1,0:T(8,128)S(1)}, u32[]{:S(2)}, u32[]{:S(2)}) async-start(f32[32,8,128]{2,1,0:T(8,128)} %bitcast.2), calls=%async_computation | async-start | bytes 262144 | tf_op jit(solution)/shard_map/all_to_all | solution.py:609
  60.9 16.3 %collective-permute-start.5 = (f32[32,16,256]{2,1,0:T(8,128)}, f32[32,16,256]{2,1,0:T(8,128)S(1)}, u32[]{:S(2)}, u32[]{:S(2)}) collective-permute-start(f32[32,16,256]{2,1,0:T(8,128)} %get-tuple-element.39), channel_id=1, source_target_pairs={{0,2},{2,4},{4,6},{6,8},{8,10},{10,12},{12,14},{14,16},{16,18},{18... | collective-permute-start | bytes 1572872 | tf_op jit(solution)/shard_map/ppermute | solution.py:576
  60.9 16.3 %collective-permute-start.6 = (f32[32,16,256]{2,1,0:T(8,128)}, f32[32,16,256]{2,1,0:T(8,128)S(1)}, u32[]{:S(2)}, u32[]{:S(2)}) collective-permute-start(f32[32,16,256]{2,1,0:T(8,128)} %get-tuple-element.40), channel_id=1, source_target_pairs={{0,30},{2,0},{4,2},{6,4},{8,6},{10,8},{12,10},{14,12},{16,14},{18,... | collective-permute-start | bytes 1572872 | tf_op jit(solution)/shard_map/ppermute | solution.py:577

commit v6 on v5

--- a/solution.py
+++ b/solution.py
@@ -248,8 +248,8 @@
 
 
 def own_kernel(plan, weight, point, field, halo, *refs):
-    upper, lower, count = plan
-    outs, refs = refs[:count], refs[count:]
+    upper, lower = plan
+    outs, refs = refs[:3], refs[3:]
     taken, halo_rows, weights, points, sent, turned, depth, gains, sem_in, sem_out, sem_few = refs
     few = [
         pltpu.make_async_copy(a, b, sem_few.at[i])
@@ -270,17 +270,11 @@
         turn(turned, rows + 2 + i, halo_rows[1] if place is None else row(*place))
     tap_sums(turned, depth, gains, [(0, 0, rows), (rows + 2, rows, rows)], range(3), True)
     copies = []
-    own, pairs = outs[0], outs[1:]
-    tiles = [*upper, *lower]
-    order = sorted(range(len(tiles)), key=lambda t: tiles[t] in (upper[0], lower[-1]))
-    for t in order:
-        outer = tiles[t] in (upper[0], lower[-1])
-        group = pairs[2:] if count == 5 and not outer else pairs[:2]
-        slot = 0 if t < len(upper) else 1
-        for k, out, at in ((0, group[0], slot), (2, group[1], slot), (1, own, t)):
+    for t in range(2 * len(upper)):
+        for k, out in enumerate(outs):
             sent[k, t] = mix_tile(mix, depth, k, t)
             copies.append(
-                pltpu.make_async_copy(sent.at[k, t], out.at[:, pl.ds(8 * at, 8), :], sem_out.at[k, t])
+                pltpu.make_async_copy(sent.at[k, t], out.at[:, pl.ds(8 * t, 8), :], sem_out.at[k, t])
             )
             copies[-1].start()
     for copy in copies:
@@ -317,12 +311,18 @@
 
 
 def gelu(value):
-    return 0.5 * value * (1.0 + lax.erf(value * (1.0 / math.sqrt(2.0))))
-
-
-def inverse_kernel(plan, modes, bias, x_top, x_rest, y_top, y_rest, middle, own, *refs):
-    upper, lower = plan
-    out, base, columns = refs[-3:]
+    size = jnp.abs(value) * math.sqrt(0.5)
+    below = 1.0 + 0.3275911 * size
+    t = pl.reciprocal(below, approx=True)
+    t = t * (2.0 - below * t)
+    series = 1.061405429 * t - 1.453152027
+    for factor in (1.421413741, -0.284496736, 0.254829592):
+        series = series * t + factor
+    tail = 0.5 * (series * t) * jnp.exp(-(size * size))
+    return value * jnp.where(value < 0.0, tail, 1.0 - tail)
+
+
+def inverse_kernel(modes, bias, x_top, x_rest, y_top, y_rest, middle, own, low, high, out, columns):
     q = pl.program_id(0)
     groups, _, y_local, _ = out.shape
 
@@ -340,24 +340,13 @@
 
     h, p = q // 2, q % 2
     rows = dot3((columns[h, 0], columns[h, 1]), (x_top[p], x_rest[p]))
-    start, stop = 8 * upper[-1] + 8, 8 * lower[0]
+    side = own.shape[2] // 2
     for g in range(groups):
         plane = rows[g * y_local : (g + 1) * y_local] + bias[4 * g + q]
-        out[g, 0, start:stop] = gelu(plane[start:stop] + middle[g, 0])
-        first = plane[:start] + own[g, 0, :start]
-        second = plane[stop:] + own[g, 0, start:]
-        base[g, 0, :8] = first[:8]
-        base[g, 0, 8:] = second[-8:]
-        if start > 8:
-            low, high = refs[:2]
-            out[g, 0, 8:start] = gelu(first[8:] + (low[g, 0, : start - 8] + high[g, 0, : start - 8]))
-            out[g, 0, stop : y_local - 8] = gelu(
-                second[:-8] + (low[g, 0, start - 8 :] + high[g, 0, start - 8 :])
-            )
-
-
-def finish_kernel(_, base, low, high, out):
-    out[...] = gelu(base[...] + (low[...] + high[...]))
+        rim = own[g, 0] + (low[g, 0] + high[g, 0])
+        out[g, 0, :side] = gelu(plane[:side] + rim[:side])
+        out[g, 0, side : y_local - side] = gelu(plane[side : y_local - side] + middle[g, 0])
+        out[g, 0, y_local - side :] = gelu(plane[y_local - side :] + rim[side:])
 
 
 def in_hbm(*arrays):
@@ -407,21 +396,18 @@
         filter_kernel,
         out_shape=pltpu.HBM(arrived.shape, F32),
         compiler_params=params(),
-        cost_estimate=cost(10**8, 2**18),
+        cost_estimate=cost(2 * 10**11, 2**18),
         name="filter_modes",
     )(arrived, *in_hbm(gains, *fwd, *inv))
 
 
-def inverse_call(modes, bias, middle, own, pair, plan, y_local, gy, scale):
+def inverse_call(modes, bias, middle, own, pair, y_local, gy, scale):
     tables = [*halves(x_table(True, scale)), *halves(y_table(y_local, gy, True))]
     some = lambda rows: pl.BlockSpec((CH // 4, 1, rows, NX), lambda i: (0, i, 0, 0))
     planes = [*in_hbm(by_four(middle), by_four(own)), *map(by_four, pair)]
-    result, base = pl.pallas_call(
-        functools.partial(inverse_kernel, plan),
-        out_shape=[
-            jax.ShapeDtypeStruct((CH // 4, 4, y_local, NX), F32),
-            jax.ShapeDtypeStruct((CH // 4, 4, 16, NX), F32),
-        ],
+    result = pl.pallas_call(
+        inverse_kernel,
+        out_shape=jax.ShapeDtypeStruct((CH // 4, 4, y_local, NX), F32),
         grid=(4,),
         in_specs=[
             whole_block(modes),
@@ -429,13 +415,13 @@
             *[whole_block(t) for t in tables],
             *[some(p.shape[2]) for p in planes],
         ],
-        out_specs=[some(y_local), some(16)],
+        out_specs=some(y_local),
         scratch_shapes=[pltpu.VMEM((2, 2, CH // 4 * y_local, 128), BF)],
         compiler_params=params(),
         cost_estimate=cost(10**8, 2**18),
         name="inverse_modes",
     )(modes, *in_hbm(bias, *tables), *planes)
-    return result.reshape(CH, y_local, NX), base.reshape(CH, 16, NX)
+    return result.reshape(CH, y_local, NX)
 
 
 def pack_call(field, middle):
@@ -464,11 +450,9 @@
     tiles = len(upper) + len(lower)
     rows = 8 * tiles
     hbm = pl.BlockSpec(memory_space=pltpu.HBM)
-    shapes = [pltpu.HBM((CH, rows, NX), F32)] + [pltpu.HBM((CH, 16, NX), F32)] * 2
-    if tiles > 2:
-        shapes += [pltpu.HBM((CH, rows - 16, NX), F32)] * 2
+    shapes = [pltpu.HBM((CH, rows, NX), F32)] * 3
     return pl.pallas_call(
-        functools.partial(own_kernel, (upper, lower, len(shapes))),
+        functools.partial(own_kernel, (upper, lower)),
         out_shape=shapes,
         in_specs=[hbm] * 3 + [pl.BlockSpec(memory_space=pl.ANY)],
         out_specs=[hbm] * len(shapes),
@@ -515,22 +499,6 @@
         cost_estimate=cost(10**8, 2**18),
         name="middle_sums",
     )(*in_hbm(weight, point), low, *in_hbm(own), high)
-
-
-def finish_call(result, base, low, high):
-    last = result.shape[1] // 8 - 1
-    piece = pl.BlockSpec((CH, 8, NX), lambda i: (0, i, 0))
-    return pl.pallas_call(
-        finish_kernel,
-        out_shape=jax.ShapeDtypeStruct(result.shape, F32),
-        grid=(2,),
-        in_specs=[pl.BlockSpec(memory_space=pl.ANY), piece, piece, piece],
-        out_specs=pl.BlockSpec((CH, 8, NX), lambda i: (0, i * last, 0)),
-        input_output_aliases={0: 0},
-        compiler_params=params(),
-        cost_estimate=cost(10**8, 2**18),
-        name="finished_rows",
-    )(result, base, low, high)
 
 
 def general_filter(coarse, gains, gz, gy, scale):
@@ -601,25 +569,21 @@
     coarse = forward_call(after(field, packed), gy, whole_tiles)
     coarse = after(coarse, halo)
     sums = own_call(after(field, coarse), halo, depth_weight, point_weight, upper, lower)
-    own, down, up = sums[:3]
-    inner_pair = to_neighbours(*sums[3:]) if len(sums) > 3 else ()
+    down, own, up = sums
+    pair = to_neighbours(down, up)
 
     if whole_tiles:
         both = ("gz", "gy")
         got = lax.all_to_all(coarse, both, split_axis=0, concat_axis=0, tiled=True)
-        out = filter_call(got, after(spectral_filter, own), gz, gy, forward_scale)
+        out = filter_call(got, after(spectral_filter, own, packed_low, packed_high), gz, gy, forward_scale)
         back = lax.all_to_all(out, both, split_axis=0, concat_axis=0, tiled=True)
         back = back.reshape(CH // 2, MY, 4 * MX)
+        mark = out
     else:
-        back = general_filter(coarse, spectral_filter, gz, gy, forward_scale)
-
-    down, up, packed, *inner_pair = lax.optimization_barrier((down, up, packed, *inner_pair, back))[:-1]
-    outer_pair = to_neighbours(down, up)
-    mixed = middle_call(depth_weight, point_weight, packed_low, packed, packed_high)
-    result, base = inverse_call(
-        back, bias_vector, mixed, own, inner_pair, (upper, lower), y_local, gy, inverse_scale
-    )
-    result = finish_call(result, base, *outer_pair)
+        mark = back = general_filter(coarse, spectral_filter, gz, gy, forward_scale)
+
+    mixed = middle_call(depth_weight, point_weight, packed_low, after(packed, mark), packed_high)
+    result = inverse_call(back, bias_vector, mixed, own, pair, y_local, gy, inverse_scale)
     return result.reshape(CH, 1, y_local, NX)
 
 

time: 78.6 us -> 67.7 us (0.86)
  the two profiles are of different devices: /device:TPU:0 before, /device:TPU:1 now
where the time goes in v6:
time: 67.7 us; the launch traced here: 66.4 us
  Pallas kernels  29 us (43%)
  starting transfers between devices  19.3 us (29%)
  waiting for transfers between devices  17.9 us (26%)
    ppermute x2, waiting for transfers between devices, to_neighbours(): lax.ppermute(up, 'gz', ring('gz', gz, -1))  16.8 us
    all_to_all x1, starting transfers between devices, body(): got = lax.all_to_all(coarse, both, split_axis=0, concat_axis=0, tiled=True)  7.36 us
    pallas_call x1, Pallas kernels, middle_call(): pl.pallas_call(middle_kernel, out_shape=pltpu.HBM((CH, rows, NX), F32), i...  6.85 us
    pallas_call x1, Pallas kernels, own_call(): pl.pallas_call(functools.partial(own_kernel, (upper, lower)), out_shape=s...  6.57 us
    pallas_call x1, Pallas kernels, inverse_call(): pl.pallas_call(inverse_kernel, out_shape=jax.ShapeDtypeStruct((CH // 4, 4...  6.39 us
    all_to_all x1, starting transfers between devices, body(): back = lax.all_to_all(out, both, split_axis=0, concat_axis=0, tiled=True)  6.32 us
    ppermute x2, starting transfers between devices, to_neighbours(): lax.ppermute(down, 'gz', ring('gz', gz, 1))  4.33 us
    pallas_call x1, Pallas kernels, forward_call(): pl.pallas_call(forward_kernel, out_shape=(pltpu.HBM if pinned else jax.Sh...  4.13 us
  transfers between devices with their start and end apart: 7, of which 2 were waited for; matrix products, arithmetic and copies ran while one was open for 0% of the time, Pallas kernels for 30%

profile of v6, /device:TPU:1, one launch (start us, length us, event | category | flops | bytes accessed | tf_op | source)
XLA Modules:
  0.0 66.4 jit_solution(7901613076414690648)
XLA Ops:
  0.0 2.5 %packed_rows.1 = (f32[34,32,256]{2,1,0:T(8,128)}, f32[2,32,256]{2,1,0:T(8,128)}) custom-call(f32[32,64,256]{2,1,0:T(8,128)} %bitcast.15), custom_call_target="tpu_custom_call" | custom-call | flops 100000000 | bytes 262144 | tf_op jit(solution)/shard_map/packed_rows/pallas_call | solution.py:431
  2.5 0.1 collective-permute-start.2
  2.6 2.6 %collective-permute-start.1 = (f32[34,32,256]{2,1,0:T(8,128)}, f32[34,32,256]{2,1,0:T(8,128)S(1)}, u32[]{:S(2)}, u32[]{:S(2)}) collective-permute-start(f32[34,32,256]{2,1,0:T(8,128)} %get-tuple-element.22.refs_1_), channel_id=1, source_target_pairs={{0,2},{2,4},{4,6},{6,8},{8,10},{10,12},{12,14},{14,16},{16,18},{18... | collective-permute-start | bytes 3342344 | tf_op jit(solution)/shard_map/ppermute | solution.py:544
  5.2 1.2 %collective-permute-start = (f32[2,32,256]{2,1,0:T(8,128)}, f32[2,32,256]{2,1,0:T(8,128)S(1)}, u32[]{:S(2)}, u32[]{:S(2)}) collective-permute-start(f32[2,32,256]{2,1,0:T(8,128)} %get-tuple-element.17), channel_id=1, source_target_pairs={{0,1},{1,0},{2,3},{3,2},{4,5},{5,4},{6,7},{7,6},{8,9},{9,8},{10,11... | collective-permute-start | bytes 196616 | tf_op jit(solution)/shard_map/ppermute | solution.py:559
  6.4 4.1 %forward_modes.1 = f32[256,128]{1,0:T(8,128)} custom-call(f32[8,4,64,256]{3,2,1,0:T(8,128)} %bitcast.16, bf16[2,256,128]{2,1,0:T(8,128)(2,1)} %constant.24.clone.x_top, bf16[2,256,128]{2,1,0:T(8,128)(2,1)} %constant.25.clone.x_rest, bf16[2,32,64]{2,1,0:T(8,128)(2,1)} %constant.26.clone.y_top, bf16[2,32,64]{2,1,0:T(8,128)(2,1)} %constant.27.clone.y_rest), custom_call_target="tpu_custom_call" | custom-call | flops 100000000 | bytes 262144 | tf_op jit(solution)/shard_map/forward_modes/pallas_call | solution.py:376
  10.6 0.0 collective-permute-done.halo
  10.6 7.4 %all-to-all-start = ((f32[32,8,128]{2,1,0:T(8,128)}), f32[32,8,128]{2,1,0:T(8,128)S(1)}, u32[]{:S(2)}, u32[]{:S(2)}) async-start(f32[32,8,128]{2,1,0:T(8,128)} %bitcast.20), calls=%async_computation | async-start | bytes 262144 | tf_op jit(solution)/shard_map/all_to_all | solution.py:577
  17.9 6.6 %own_sums.1 = (f32[32,32,256]{2,1,0:T(8,128)}, f32[32,32,256]{2,1,0:T(8,128)}, f32[32,32,256]{2,1,0:T(8,128)}) custom-call(f32[32,27]{1,0:T(8,128)} %weight.3, f32[32,32]{1,0:T(8,128)} %point.3, f32[32,64,256]{2,1,0:T(8,128)} %bitcast.17, f32[2,32,256]{2,1,0:T(8,128)S(1)} %collective-permute-done.halo), custom_call_target="tpu_custom_call" | custom-call | flops 100000000 | bytes 262144 | tf_op jit(solution)/shard_map/own_sums/pallas_call | solution.py:454
  24.5 1.7 %collective-permute-start.3 = (f32[32,32,256]{2,1,0:T(8,128)}, f32[32,32,256]{2,1,0:T(8,128)}, u32[]{:S(2)}, u32[]{:S(2)}) collective-permute-start(f32[32,32,256]{2,1,0:T(8,128)} %get-tuple-element.23), channel_id=1, source_target_pairs={{0,2},{2,4},{4,6},{6,8},{8,10},{10,12},{12,14},{14,16},{16,18},{18... | collective-permute-start | bytes 3145736 | tf_op jit(solution)/shard_map/ppermute | solution.py:544
  26.2 0.0 collective-permute-start.4
  26.2 16.8 %collective-permute-done.2.refs_2_ = f32[34,32,256]{2,1,0:T(8,128)S(1)} collective-permute-done((f32[34,32,256]{2,1,0:T(8,128)}, f32[34,32,256]{2,1,0:T(8,128)S(1)}, u32[]{:S(2)}, u32[]{:S(2)}) %collective-permute-start.2) | collective-permute-done | bytes 1114144 | tf_op jit(solution)/shard_map/ppermute | solution.py:545
  43.0 0.0 collective-permute-done.1.refs_0_
  43.0 0.0 all-to-all-done
  43.1 2.6 %filter_modes.1 = f32[256,128]{1,0:T(8,128)} custom-call(f32[256,128]{1,0:T(8,128)S(1)} %bitcast.14, f32[2,16,8,64]{3,2,1,0:T(8,128)} %gains, bf16[256,256]{1,0:T(8,128)(2,1)} %constant.28.clone.f_top, bf16[256,256]{1,0:T(8,128)(2,1)} %constant.29.clone.f_rest, bf16[512,128]{1,0:T(8,128)(2,1)} %constant.30.clone.i_top, bf16[512,128]{1,0:T(8,128)(2,1)} %constant.31.clone.i_rest), custom_call_target="tpu_custom_call" | custom-call | flops 199999995904 | bytes 262144 | tf_op jit(solution)/shard_map/filter_modes/pallas_call | solution.py:395
  45.7 6.3 %all-to-all-start.1 = ((f32[32,8,128]{2,1,0:T(8,128)}), f32[32,8,128]{2,1,0:T(8,128)S(1)}, u32[]{:S(2)}, u32[]{:S(2)}) async-start(f32[32,8,128]{2,1,0:T(8,128)} %bitcast.21), calls=%async_computation.1 | async-start | bytes 262144 | tf_op jit(solution)/shard_map/all_to_all | solution.py:579
  52.0 6.9 %middle_sums.1 = f32[32,32,256]{2,1,0:T(8,128)} custom-call(f32[32,27]{1,0:T(8,128)} %weight.3, f32[32,32]{1,0:T(8,128)} %point.3, f32[34,32,256]{2,1,0:T(8,128)S(1)} %collective-permute-done.1.refs_0_, f32[34,32,256]{2,1,0:T(8,128)} %get-tuple-element.22.refs_1_, f32[34,32,256]{2,1,0:T(8,128)S(1)} %collective-permute-done.2.refs_2_), custom_call_target="tpu_custom_call" | custom-call | flops 100000000 | bytes 262144 | tf_op jit(solution)/shard_map/middle_sums/pallas_call | solution.py:481
  58.9 0.0 collective-permute-done.3
  58.9 0.0 collective-permute-done.4
  58.9 1.0 %all-to-all-done.1 = f32[32,8,128]{2,1,0:T(8,128)S(1)} async-done(((f32[32,8,128]{2,1,0:T(8,128)}), f32[32,8,128]{2,1,0:T(8,128)S(1)}, u32[]{:S(2)}, u32[]{:S(2)}) %all-to-all-start.1) | async-done | bytes 131104 | tf_op jit(solution)/shard_map/all_to_all | solution.py:579
  60.0 6.4 %inverse_modes.1 = f32[8,4,64,256]{3,2,1,0:T(8,128)} custom-call(f32[16,16,128]{2,1,0:T(8,128)S(1)} %bitcast.13, f32[32]{0:T(128)} %bias.1, bf16[2,128,256]{2,1,0:T(8,128)(2,1)} %constant.32.clone.x_top, bf16[2,128,256]{2,1,0:T(8,128)(2,1)} %constant.33.clone.x_rest, bf16[2,64,32]{2,1,0:T(8,128)(2,1)} %constant.34.clone.y_top, ...), custom_call_target="tpu_custom_call" | custom-call | flops 100000000 | bytes 262144 | tf_op jit(solution)/shard_map/inverse_modes/pallas_call | solution.py:408
Async XLA Ops:
  2.5 40.6 %collective-permute-start.2 = (f32[34,32,256]{2,1,0:T(8,128)}, f32[34,32,256]{2,1,0:T(8,128)S(1)}, u32[]{:S(2)}, u32[]{:S(2)}) collective-permute-start(f32[34,32,256]{2,1,0:T(8,128)} %get-tuple-element.22.refs_1_), channel_id=1, source_target_pairs={{0,30},{2,0},{4,2},{6,4},{8,6},{10,8},{12,10},{14,12},{16,14},{18,... | collective-permute-start | bytes 3342344 | tf_op jit(solution)/shard_map/ppermute | solution.py:545
  2.6 40.5 %collective-permute-start.1 = (f32[34,32,256]{2,1,0:T(8,128)}, f32[34,32,256]{2,1,0:T(8,128)S(1)}, u32[]{:S(2)}, u32[]{:S(2)}) collective-permute-start(f32[34,32,256]{2,1,0:T(8,128)} %get-tuple-element.22.refs_1_), channel_id=1, source_target_pairs={{0,2},{2,4},{4,6},{6,8},{8,10},{10,12},{12,14},{14,16},{16,18},{18... | collective-permute-start | bytes 3342344 | tf_op jit(solution)/shard_map/ppermute | solution.py:544
  5.2 5.4 %collective-permute-start = (f32[2,32,256]{2,1,0:T(8,128)}, f32[2,32,256]{2,1,0:T(8,128)S(1)}, u32[]{:S(2)}, u32[]{:S(2)}) collective-permute-start(f32[2,32,256]{2,1,0:T(8,128)} %get-tuple-element.17), channel_id=1, source_target_pairs={{0,1},{1,0},{2,3},{3,2},{4,5},{5,4},{6,7},{7,6},{8,9},{9,8},{10,11... | collective-permute-start | bytes 196616 | tf_op jit(solution)/shard_map/ppermute | solution.py:559
  10.6 32.5 %all-to-all-start = ((f32[32,8,128]{2,1,0:T(8,128)}), f32[32,8,128]{2,1,0:T(8,128)S(1)}, u32[]{:S(2)}, u32[]{:S(2)}) async-start(f32[32,8,128]{2,1,0:T(8,128)} %bitcast.20), calls=%async_computation | async-start | bytes 262144 | tf_op jit(solution)/shard_map/all_to_all | solution.py:577
  24.5 34.4 %collective-permute-start.3 = (f32[32,32,256]{2,1,0:T(8,128)}, f32[32,32,256]{2,1,0:T(8,128)}, u32[]{:S(2)}, u32[]{:S(2)}) collective-permute-start(f32[32,32,256]{2,1,0:T(8,128)} %get-tuple-element.23), channel_id=1, source_target_pairs={{0,2},{2,4},{4,6},{6,8},{8,10},{10,12},{12,14},{14,16},{16,18},{18... | collective-permute-start | bytes 3145736 | tf_op jit(solution)/shard_map/ppermute | solution.py:544
  26.2 32.7 %collective-permute-start.4 = (f32[32,32,256]{2,1,0:T(8,128)}, f32[32,32,256]{2,1,0:T(8,128)}, u32[]{:S(2)}, u32[]{:S(2)}) collective-permute-start(f32[32,32,256]{2,1,0:T(8,128)} %get-tuple-element.24), channel_id=1, source_target_pairs={{0,30},{2,0},{4,2},{6,4},{8,6},{10,8},{12,10},{14,12},{16,14},{18,... | collective-permute-start | bytes 3145736 | tf_op jit(solution)/shard_map/ppermute | solution.py:545
  45.7 14.3 %all-to-all-start.1 = ((f32[32,8,128]{2,1,0:T(8,128)}), f32[32,8,128]{2,1,0:T(8,128)S(1)}, u32[]{:S(2)}, u32[]{:S(2)}) async-start(f32[32,8,128]{2,1,0:T(8,128)} %bitcast.21), calls=%async_computation.1 | async-start | bytes 262144 | tf_op jit(solution)/shard_map/all_to_all | solution.py:579

commit v7 on v6

--- a/solution.py
+++ b/solution.py
@@ -225,23 +225,24 @@
     return dot3(mix, parts(tile)).reshape(CH, 8, NX)
 
 
-def pack_kernel(middle, field, packed, edges, taken, rows, ends, sem_in, sem_out):
+def pack_kernel(plan, field, packed, later, edges, taken, rows, ends, sem_in, sem_out):
+    middle, split = plan
     last = field.shape[1] // 8 - 1
     before, after = middle[0] - 1, middle[-1] + 1
     wanted = [before, *middle, after] + [t for t in (0, last) if t not in (before, after)]
     row = fetch_tiles(field, taken, sem_in, wanted)
     places = [(before, 7), *[(t, r) for t in middle for r in range(8)], (after, 0)]
-    copies, sent = [], 0
+    copies = []
     for i, place in enumerate(places):
         rows[i] = row(*place)
-        if i + 1 - sent >= 17 or i + 1 == len(places):
-            some = pl.ds(sent, i + 1 - sent)
-            copies.append(pltpu.make_async_copy(rows.at[some], packed.at[some], sem_out.at[len(copies)]))
+        if i + 1 == split:
+            copies.append(pltpu.make_async_copy(rows.at[pl.ds(0, split)], packed, sem_out.at[0]))
             copies[-1].start()
-            sent = i + 1
+    copies.append(pltpu.make_async_copy(rows.at[pl.ds(split, len(places) - split)], later, sem_out.at[1]))
+    copies[-1].start()
     ends[0] = row(last, 7)
     ends[1] = row(0, 0)
-    copies.append(pltpu.make_async_copy(ends, edges, sem_out.at[len(copies)]))
+    copies.append(pltpu.make_async_copy(ends, edges, sem_out.at[2]))
     copies[-1].start()
     for copy in copies:
         copy.wait()
@@ -263,14 +264,14 @@
         copy.wait()
     spread_gains(weights, gains, range(3))
     mix = mixing(points[...])
-    rows = 8 * len(upper)
+    rows, others = 8 * len(upper), 8 * len(lower)
     for i, place in enumerate([None, *[(t, r) for t in upper for r in range(8)], (upper[-1] + 1, 0)]):
         turn(turned, i, halo_rows[0] if place is None else row(*place))
     for i, place in enumerate([(lower[0] - 1, 7), *[(t, r) for t in lower for r in range(8)], None]):
         turn(turned, rows + 2 + i, halo_rows[1] if place is None else row(*place))
-    tap_sums(turned, depth, gains, [(0, 0, rows), (rows + 2, rows, rows)], range(3), True)
+    tap_sums(turned, depth, gains, [(0, 0, rows), (rows + 2, rows, others)], range(3), True)
     copies = []
-    for t in range(2 * len(upper)):
+    for t in range((rows + others) // 8):
         for k, out in enumerate(outs):
             sent[k, t] = mix_tile(mix, depth, k, t)
             copies.append(
@@ -282,14 +283,26 @@
 
 
 def middle_kernel(weight, point, *refs):
-    planes, out = refs[:3], refs[3]
-    taken, weights, points, sent, turned, depth, gains, sem_in, sem_out, sem_few = refs[4:]
+    planes, out = refs[:6], refs[6]
+    taken, weights, points, sent, turned, depth, gains, sem_in, sem_out, sem_few = refs[7:]
+    split = planes[0].shape[0]
     few = [
         pltpu.make_async_copy(a, b, sem_few.at[i])
         for i, (a, b) in enumerate(((weight, weights), (point, points)))
     ]
-    arrivals = [pltpu.make_async_copy(planes[a], taken.at[a], sem_in.at[a]) for a in range(3)]
-    for copy in few + arrivals:
+    arrivals = [
+        [
+            pltpu.make_async_copy(planes[2 * a], taken.at[a, pl.ds(0, split)], sem_in.at[a, 0]),
+            pltpu.make_async_copy(
+                planes[2 * a + 1], taken.at[a, pl.ds(split, taken.shape[1] - split)], sem_in.at[a, 1]
+            ),
+        ]
+        for a in range(3)
+    ]
+    for a in (1, 0, 2):
+        for copy in arrivals[a]:
+            copy.start()
+    for copy in few:
         copy.start()
     for copy in few:
         copy.wait()
@@ -297,7 +310,8 @@
     mix = mixing(points[...])
     rows = out.shape[1]
     for a in (1, 0, 2):
-        arrivals[a].wait()
+        for copy in arrivals[a]:
+            copy.wait()
         for r in range(rows + 2):
             turn(turned, r, taken[a, r])
         tap_sums(turned, depth, gains, [(0, 0, rows)], [a], a == 1)
@@ -322,7 +336,7 @@
     return value * jnp.where(value < 0.0, tail, 1.0 - tail)
 
 
-def inverse_kernel(modes, bias, x_top, x_rest, y_top, y_rest, middle, own, low, high, out, columns):
+def inverse_kernel(upper, modes, bias, x_top, x_rest, y_top, y_rest, middle, own, out, base, columns):
     q = pl.program_id(0)
     groups, _, y_local, _ = out.shape
 
@@ -340,13 +354,16 @@
 
     h, p = q // 2, q % 2
     rows = dot3((columns[h, 0], columns[h, 1]), (x_top[p], x_rest[p]))
-    side = own.shape[2] // 2
+    start, stop = upper, upper + middle.shape[2]
     for g in range(groups):
         plane = rows[g * y_local : (g + 1) * y_local] + bias[4 * g + q]
-        rim = own[g, 0] + (low[g, 0] + high[g, 0])
-        out[g, 0, :side] = gelu(plane[:side] + rim[:side])
-        out[g, 0, side : y_local - side] = gelu(plane[side : y_local - side] + middle[g, 0])
-        out[g, 0, y_local - side :] = gelu(plane[y_local - side :] + rim[side:])
+        out[g, 0, start:stop] = gelu(plane[start:stop] + middle[g, 0])
+        base[g, 0, :start] = plane[:start] + own[g, 0, :start]
+        base[g, 0, start:] = plane[stop:] + own[g, 0, start:]
+
+
+def finish_kernel(_, base, low, high, out):
+    out[...] = gelu(base[...] + (low[...] + high[...]))
 
 
 def in_hbm(*arrays):
@@ -401,13 +418,17 @@
     )(arrived, *in_hbm(gains, *fwd, *inv))
 
 
-def inverse_call(modes, bias, middle, own, pair, y_local, gy, scale):
+def inverse_call(modes, bias, middle, own, upper, y_local, gy, scale):
     tables = [*halves(x_table(True, scale)), *halves(y_table(y_local, gy, True))]
     some = lambda rows: pl.BlockSpec((CH // 4, 1, rows, NX), lambda i: (0, i, 0, 0))
-    planes = [*in_hbm(by_four(middle), by_four(own)), *map(by_four, pair)]
-    result = pl.pallas_call(
-        inverse_kernel,
-        out_shape=jax.ShapeDtypeStruct((CH // 4, 4, y_local, NX), F32),
+    planes = in_hbm(by_four(middle), by_four(own))
+    rim = own.shape[1]
+    result, base = pl.pallas_call(
+        functools.partial(inverse_kernel, upper),
+        out_shape=[
+            jax.ShapeDtypeStruct((CH // 4, 4, y_local, NX), F32),
+            jax.ShapeDtypeStruct((CH // 4, 4, rim, NX), F32),
+        ],
         grid=(4,),
         in_specs=[
             whole_block(modes),
@@ -415,30 +436,52 @@
             *[whole_block(t) for t in tables],
             *[some(p.shape[2]) for p in planes],
         ],
-        out_specs=some(y_local),
+        out_specs=[some(y_local), some(rim)],
         scratch_shapes=[pltpu.VMEM((2, 2, CH // 4 * y_local, 128), BF)],
         compiler_params=params(),
         cost_estimate=cost(10**8, 2**18),
         name="inverse_modes",
     )(modes, *in_hbm(bias, *tables), *planes)
-    return result.reshape(CH, y_local, NX)
-
-
-def pack_call(field, middle):
+    return result.reshape(CH, y_local, NX), base.reshape(CH, rim, NX)
+
+
+def finish_call(result, base, low, high, upper):
+    tiles = base.shape[1] // 8
+    gap = result.shape[1] // 8 - tiles
+    piece = pl.BlockSpec((CH, 8, NX), lambda i: (0, i, 0))
+    return pl.pallas_call(
+        finish_kernel,
+        out_shape=jax.ShapeDtypeStruct(result.shape, F32),
+        grid=(tiles,),
+        in_specs=[pl.BlockSpec(memory_space=pl.ANY), piece, piece, piece],
+        out_specs=pl.BlockSpec((CH, 8, NX), lambda i: (0, jnp.where(i < upper, i, i + gap), 0)),
+        input_output_aliases={0: 0},
+        compiler_params=params(),
+        cost_estimate=cost(10**8, 2**18),
+        name="finished_rows",
+    )(result, base, low, high)
+
+
+def pack_call(field, middle, first):
     count = 8 * len(middle) + 2
+    split = 8 * first + 2
     fetched = len(middle) + 4
     hbm = pl.BlockSpec(memory_space=pltpu.HBM)
     return pl.pallas_call(
-        functools.partial(pack_kernel, middle),
-        out_shape=[pltpu.HBM((count, CH, NX), F32), pltpu.HBM((2, CH, NX), F32)],
+        functools.partial(pack_kernel, (middle, split)),
+        out_shape=[
+            pltpu.HBM((split, CH, NX), F32),
+            pltpu.HBM((count - split, CH, NX), F32),
+            pltpu.HBM((2, CH, NX), F32),
+        ],
         in_specs=[hbm],
-        out_specs=[hbm] * 2,
+        out_specs=[hbm] * 3,
         scratch_shapes=[
             pltpu.VMEM((fetched, 2, CH, 8, 128), F32),
             pltpu.VMEM((count, CH, NX), F32),
             pltpu.VMEM((2, CH, NX), F32),
             pltpu.SemaphoreType.DMA((fetched, 2)),
-            pltpu.SemaphoreType.DMA((count // 17 + 2,)),
+            pltpu.SemaphoreType.DMA((3,)),
         ],
         compiler_params=params(),
         cost_estimate=cost(10**8, 2**18),
@@ -476,12 +519,12 @@
 
 
 def middle_call(weight, point, low, own, high):
-    rows = own.shape[0] - 2
+    rows = own[0].shape[0] + own[1].shape[0] - 2
     hbm = pl.BlockSpec(memory_space=pltpu.HBM)
     return pl.pallas_call(
         middle_kernel,
         out_shape=pltpu.HBM((CH, rows, NX), F32),
-        in_specs=[hbm] * 2 + [pl.BlockSpec(memory_space=pl.ANY)] * 3,
+        in_specs=[hbm] * 2 + [pl.BlockSpec(memory_space=pl.ANY)] * 6,
         out_specs=hbm,
         scratch_shapes=[
             pltpu.VMEM((3, rows + 2, CH, NX), F32),
@@ -491,14 +534,14 @@
             pltpu.VMEM((3, rows + 2, CH, NX), F32),
             pltpu.VMEM((1, rows, CH, NX), F32),
             pltpu.VMEM((27, CH, 128), F32),
-            pltpu.SemaphoreType.DMA((3,)),
+            pltpu.SemaphoreType.DMA((3, 2)),
             pltpu.SemaphoreType.DMA((rows // 8,)),
             pltpu.SemaphoreType.DMA((2,)),
         ],
         compiler_params=params(),
-        cost_estimate=cost(10**8, 2**18),
+        cost_estimate=cost(2 * 10**11, 2**18),
         name="middle_sums",
-    )(*in_hbm(weight, point), low, *in_hbm(own), high)
+    )(*in_hbm(weight, point), *low, *in_hbm(*own), *high)
 
 
 def general_filter(coarse, gains, gz, gy, scale):
@@ -549,12 +592,11 @@
         return lax.optimization_barrier((value, *others))[0]
 
     tiles = y_local // 8
-    side = 2 if tiles >= 6 else 1
-    upper, lower = tuple(range(side)), tuple(range(tiles - side, tiles))
-    middle = tuple(range(side, tiles - side))
-
-    packed, edges = pack_call(field, middle)
-    packed_low, packed_high = to_neighbours(packed, packed)
+    upper = (0,)
+    lower = tuple(range(tiles - max(1, tiles // 4), tiles))
+    middle = tuple(range(1, lower[0]))
+    packed, later, edges = pack_call(field, middle, max(1, 2 * len(middle) // 5))
+    first_low, first_high = to_neighbours(packed, packed)
     if gy == 2:
         halo = lax.ppermute(edges, "gy", ring("gy", gy, 1))
     else:
@@ -566,24 +608,30 @@
         )
     j_own, n_own = spectral_filter.shape[2], spectral_filter.shape[3]
     whole_tiles = j_own == 8 and n_own == 2 * MX
-    coarse = forward_call(after(field, packed), gy, whole_tiles)
-    coarse = after(coarse, halo)
-    sums = own_call(after(field, coarse), halo, depth_weight, point_weight, upper, lower)
-    down, own, up = sums
-    pair = to_neighbours(down, up)
-
+    coarse = after(forward_call(after(field, packed), gy, whole_tiles), halo)
     if whole_tiles:
         both = ("gz", "gy")
         got = lax.all_to_all(coarse, both, split_axis=0, concat_axis=0, tiled=True)
-        out = filter_call(got, after(spectral_filter, own, packed_low, packed_high), gz, gy, forward_scale)
-        back = lax.all_to_all(out, both, split_axis=0, concat_axis=0, tiled=True)
+        sent = after(later, got)
+        later_low, later_high = to_neighbours(sent, sent)
+        gains = after(spectral_filter, first_low, first_high)
+        filtered = filter_call(got, gains, gz, gy, forward_scale)
+        back = lax.all_to_all(filtered, both, split_axis=0, concat_axis=0, tiled=True)
         back = back.reshape(CH // 2, MY, 4 * MX)
-        mark = out
     else:
-        mark = back = general_filter(coarse, spectral_filter, gz, gy, forward_scale)
-
-    mixed = middle_call(depth_weight, point_weight, packed_low, after(packed, mark), packed_high)
-    result = inverse_call(back, bias_vector, mixed, own, pair, y_local, gy, inverse_scale)
+        later_low, later_high = to_neighbours(later, later)
+        filtered = back = general_filter(coarse, spectral_filter, gz, gy, forward_scale)
+    down, own, up = own_call(after(field, filtered), halo, depth_weight, point_weight, upper, lower)
+    low, high = to_neighbours(down, up)
+    mixed = middle_call(
+        depth_weight,
+        point_weight,
+        (first_low, later_low),
+        (after(packed, back), later),
+        (first_high, later_high),
+    )
+    result, base = inverse_call(back, bias_vector, mixed, own, 8, y_local, gy, inverse_scale)
+    result = finish_call(result, base, low, high, 1)
     return result.reshape(CH, 1, y_local, NX)
 
 

time: 67.7 us -> 75.1 us (1.11)
  blocking collectives: 0 us -> 15.3 us
  starting transfers between devices: 19.3 us -> 11.9 us
  waiting for transfers between devices: 17.9 us -> 13.4 us
  Pallas kernels: 29 us -> 32.6 us
    ppermute x2 -> x3, waiting for transfers between devices: 16.8 us -> 0.01 us  [to_neighbours(): lax.ppermute(up, 'gz', ring('gz', gz, -1))]
    all_to_all x0 -> x1, blocking collectives: none -> 15.3 us  [body(): got = lax.all_to_all(coarse, both, split_axis=0, concat_axis=0, tiled=True)]
    all_to_all x2 -> x1, waiting for transfers between devices: 1.09 us -> 13.4 us  [body(): lax.all_to_all(filtered, both, split_axis=0, concat_axis=0, tiled=True)]
    all_to_all x2 -> x1, starting transfers between devices: 13.7 us -> 4.51 us  [body(): lax.all_to_all(filtered, both, split_axis=0, concat_axis=0, tiled=True)]
    pallas_call x2 -> x3, Pallas kernels: 8.84 us -> 11.6 us  [the longest x1 5.53 us: inverse_call(): pl.pallas_call(functools.partial(inverse_kernel, upper), out_shape=[jax.S...]
    pallas_call x1, Pallas kernels: 6.85 us -> 8.47 us  [middle_call(): pl.pallas_call(middle_kernel, out_shape=pltpu.HBM((CH, rows, NX), F32), i...]
    pallas_call x1, Pallas kernels: 6.57 us -> 5.36 us  [own_call(): pl.pallas_call(functools.partial(own_kernel, (upper, lower)), out_shape=s...]
    ppermute x2 -> x3, starting transfers between devices: 0.11 us -> 1.07 us  [to_neighbours(): lax.ppermute(up, 'gz', ring('gz', gz, -1))]
  transfers between devices with their start and end apart: 7 -> 8, of which waited for: 2 -> 1; matrix products, arithmetic and copies ran while one was open for 0% -> 0% of each run, Pallas kernels for 30% -> 36%
where the time goes in v7:
time: 75.1 us; the launch traced here: 74 us
  Pallas kernels  32.6 us (43%)
  blocking collectives  15.3 us (20%)
  waiting for transfers between devices  13.4 us (18%)
  starting transfers between devices  11.9 us (16%)
    all_to_all x1, blocking collectives, body(): got = lax.all_to_all(coarse, both, split_axis=0, concat_axis=0, tiled=True)  15.3 us
    all_to_all x1, waiting for transfers between devices, body(): lax.all_to_all(filtered, both, split_axis=0, concat_axis=0, tiled=True)  13.4 us
    pallas_call x1, Pallas kernels, middle_call(): pl.pallas_call(middle_kernel, out_shape=pltpu.HBM((CH, rows, NX), F32), i...  8.47 us
    pallas_call x1, Pallas kernels, inverse_call(): pl.pallas_call(functools.partial(inverse_kernel, upper), out_shape=[jax.S...  5.53 us
    pallas_call x1, Pallas kernels, own_call(): pl.pallas_call(functools.partial(own_kernel, (upper, lower)), out_shape=s...  5.36 us
    ppermute x3, starting transfers between devices, to_neighbours(): lax.ppermute(down, 'gz', ring('gz', gz, 1))  5.13 us
    all_to_all x1, starting transfers between devices, body(): lax.all_to_all(filtered, both, split_axis=0, concat_axis=0, tiled=True)  4.51 us
    pallas_call x1, Pallas kernels, forward_call(): pl.pallas_call(forward_kernel, out_shape=(pltpu.HBM if pinned else jax.Sh...  4.13 us
  transfers between devices with their start and end apart: 8, of which 1 were waited for; matrix products, arithmetic and copies ran while one was open for 0% of the time, Pallas kernels for 36%

profile of v7, /device:TPU:1, one launch (start us, length us, event | category | flops | bytes accessed | tf_op | source)
XLA Modules:
  0.0 74.0 jit_solution(5388631962341836683)
XLA Ops:
  0.0 2.6 %packed_rows.1 = (f32[18,32,256]{2,1,0:T(8,128)}, f32[24,32,256]{2,1,0:T(8,128)}, f32[2,32,256]{2,1,0:T(8,128)}) custom-call(f32[32,64,256]{2,1,0:T(8,128)} %bitcast.16), custom_call_target="tpu_custom_call" | custom-call | flops 100000000 | bytes 262144 | tf_op jit(solution)/shard_map/packed_rows/pallas_call | solution.py:470
  2.6 0.1 collective-permute-start.2
  2.7 2.6 %collective-permute-start.1 = (f32[18,32,256]{2,1,0:T(8,128)}, f32[18,32,256]{2,1,0:T(8,128)S(1)}, u32[]{:S(2)}, u32[]{:S(2)}) collective-permute-start(f32[18,32,256]{2,1,0:T(8,128)} %get-tuple-element.26.refs_2_), channel_id=1, source_target_pairs={{0,2},{2,4},{4,6},{6,8},{8,10},{10,12},{12,14},{14,16},{16,18},{18... | collective-permute-start | bytes 1769480 | tf_op jit(solution)/shard_map/ppermute | solution.py:587
  5.4 1.2 %collective-permute-start = (f32[2,32,256]{2,1,0:T(8,128)}, f32[2,32,256]{2,1,0:T(8,128)S(1)}, u32[]{:S(2)}, u32[]{:S(2)}) collective-permute-start(f32[2,32,256]{2,1,0:T(8,128)} %get-tuple-element.21), channel_id=1, source_target_pairs={{0,1},{1,0},{2,3},{3,2},{4,5},{5,4},{6,7},{7,6},{8,9},{9,8},{10,11... | collective-permute-start | bytes 196616 | tf_op jit(solution)/shard_map/ppermute | solution.py:601
  6.6 4.1 %forward_modes.1 = f32[256,128]{1,0:T(8,128)} custom-call(f32[8,4,64,256]{3,2,1,0:T(8,128)} %bitcast.17, bf16[2,256,128]{2,1,0:T(8,128)(2,1)} %constant.24.clone.x_top, bf16[2,256,128]{2,1,0:T(8,128)(2,1)} %constant.25.clone.x_rest, bf16[2,32,64]{2,1,0:T(8,128)(2,1)} %constant.26.clone.y_top, bf16[2,32,64]{2,1,0:T(8,128)(2,1)} %constant.27.clone.y_rest), custom_call_target="tpu_custom_call" | custom-call | flops 100000000 | bytes 262144 | tf_op jit(solution)/shard_map/forward_modes/pallas_call | solution.py:393
  10.7 0.0 collective-permute-done.halo
  10.7 0.0 copy-start
  10.7 0.6 copy-done
  11.4 15.3 %all_to_all.20 = f32[32,8,128]{2,1,0:T(8,128)S(1)} all-to-all(f32[32,8,128]{2,1,0:T(8,128)} %bitcast.22), channel_id=1, replica_groups=mesh['gz'=16,'gy'=2] {'gz','gy'}, dimensions={0} | all-to-all | bytes 262144 | tf_op jit(solution)/shard_map/all_to_all | solution.py:614
  26.6 1.0 %collective-permute-start.4 = (f32[24,32,256]{2,1,0:T(8,128)}, f32[24,32,256]{2,1,0:T(8,128)}, u32[]{:S(2)}, u32[]{:S(2)}) collective-permute-start(f32[24,32,256]{2,1,0:T(8,128)} %get-tuple-element.25.refs_3_), channel_id=1, source_target_pairs={{0,30},{2,0},{4,2},{6,4},{8,6},{10,8},{12,10},{14,12},{16,14},{18,... | collective-permute-start | bytes 2359304 | tf_op jit(solution)/shard_map/ppermute | solution.py:588
  27.6 0.8 %collective-permute-start.3 = (f32[24,32,256]{2,1,0:T(8,128)}, f32[24,32,256]{2,1,0:T(8,128)}, u32[]{:S(2)}, u32[]{:S(2)}) collective-permute-start(f32[24,32,256]{2,1,0:T(8,128)} %get-tuple-element.25.refs_3_), channel_id=1, source_target_pairs={{0,2},{2,4},{4,6},{6,8},{8,10},{10,12},{12,14},{14,16},{16,18},{18... | collective-permute-start | bytes 2359304 | tf_op jit(solution)/shard_map/ppermute | solution.py:587
  28.4 0.0 collective-permute-done.2.refs_4_
  28.4 0.0 collective-permute-done.1.refs_0_
  28.4 0.0 copy-start.4
  28.4 0.0 copy-start.1
  28.4 3.1 %filter_modes.1 = f32[256,128]{1,0:T(8,128)} custom-call(f32[256,128]{1,0:T(8,128)S(1)} %bitcast.15, f32[2,16,8,64]{3,2,1,0:T(8,128)} %gains, bf16[256,256]{1,0:T(8,128)(2,1)} %constant.28.clone.f_top, bf16[256,256]{1,0:T(8,128)(2,1)} %constant.29.clone.f_rest, bf16[512,128]{1,0:T(8,128)(2,1)} %constant.30.clone.i_top, bf16[512,128]{1,0:T(8,128)(2,1)} %constant.31.clone.i_rest), custom_call_target="tpu_custom_call" | custom-call | flops 199999995904 | bytes 262144 | tf_op jit(solution)/shard_map/filter_modes/pallas_call | solution.py:412
  31.5 0.0 copy-done.2
  31.5 0.0 copy-done.4
  31.5 0.0 copy-start.5
  31.5 4.5 %all-to-all-start.1 = ((f32[32,8,128]{2,1,0:T(8,128)}), f32[32,8,128]{2,1,0:T(8,128)S(1)}, u32[]{:S(2)}, u32[]{:S(2)}) async-start(f32[32,8,128]{2,1,0:T(8,128)} %bitcast.23), calls=%async_computation.1 | async-start | bytes 262144 | tf_op jit(solution)/shard_map/all_to_all | solution.py:619
  36.0 0.0 copy-done.1
  36.1 5.4 %own_sums.1 = (f32[32,24,256]{2,1,0:T(8,128)}, f32[32,24,256]{2,1,0:T(8,128)}, f32[32,24,256]{2,1,0:T(8,128)}) custom-call(f32[32,27]{1,0:T(8,128)} %weight.3, f32[32,32]{1,0:T(8,128)} %point.3, f32[32,64,256]{2,1,0:T(8,128)} %bitcast.18, f32[2,32,256]{2,1,0:T(8,128)S(1)} %copy-done.1), custom_call_target="tpu_custom_call" | custom-call | flops 100000000 | bytes 262144 | tf_op jit(solution)/shard_map/own_sums/pallas_call | solution.py:497
  41.4 1.7 %collective-permute-start.5 = (f32[32,24,256]{2,1,0:T(8,128)}, f32[32,24,256]{2,1,0:T(8,128)}, u32[]{:S(2)}, u32[]{:S(2)}) collective-permute-start(f32[32,24,256]{2,1,0:T(8,128)} %get-tuple-element.31), channel_id=1, source_target_pairs={{0,2},{2,4},{4,6},{6,8},{8,10},{10,12},{12,14},{14,16},{16,18},{18... | collective-permute-start | bytes 2359304 | tf_op jit(solution)/shard_map/ppermute | solution.py:587
  43.1 0.0 collective-permute-start.6
  43.1 13.4 %all-to-all-done.1 = f32[32,8,128]{2,1,0:T(8,128)S(1)} async-done(((f32[32,8,128]{2,1,0:T(8,128)}), f32[32,8,128]{2,1,0:T(8,128)S(1)}, u32[]{:S(2)}, u32[]{:S(2)}) %all-to-all-start.1) | async-done | bytes 131104 | tf_op jit(solution)/shard_map/all_to_all | solution.py:619
  56.5 0.0 collective-permute-done.4.refs_5_
  56.6 0.0 collective-permute-done.3.refs_1_
  56.6 8.5 %middle_sums.1 = f32[32,40,256]{2,1,0:T(8,128)} custom-call(f32[32,27]{1,0:T(8,128)} %weight.3, f32[32,32]{1,0:T(8,128)} %point.3, f32[18,32,256]{2,1,0:T(8,128)S(1)} %copy-done.5, f32[24,32,256]{2,1,0:T(8,128)} %collective-permute-done.3.refs_1_, f32[18,32,256]{2,1,0:T(8,128)} %get-tuple-element.26.refs_2_, f32[24,32,256]{2,1,0:T(8,128)} %get-tuple-element.25.refs_3_, ...), custom_call_target="tpu_custom_call" | custom-call | flops 199999995904 | bytes 262144 | tf_op jit(solution)/shard_map/middle_sums/pallas_call | solution.py:524
  65.0 5.5 %inverse_modes.1 = (f32[8,4,64,256]{3,2,1,0:T(8,128)}, f32[8,4,24,256]{3,2,1,0:T(8,128)S(1)}) custom-call(f32[16,16,128]{2,1,0:T(8,128)S(1)} %bitcast.14, f32[32]{0:T(128)} %bias.1, bf16[2,128,256]{2,1,0:T(8,128)(2,1)} %constant.32.clone.x_top, bf16[2,128,256]{2,1,0:T(8,128)(2,1)} %constant.33.clone.x_rest, bf16[2,64,32]{2,1,0:T(8,128)(2,1)} %constant.34.clone.y_top, ...), custom_call_target="tpu_custom_call" | custom-call | flops 100000000 | bytes 262144 | tf_op jit(solution)/shard_map/inverse_modes/pallas_call | solution.py:426
  70.6 0.0 collective-permute-done.5.low
  70.6 0.0 collective-permute-done.6.high
  70.6 3.4 %finished_rows.1 = f32[32,64,256]{2,1,0:T(8,128)} custom-call(f32[32,64,256]{2,1,0:T(8,128)} %bitcast.19, f32[32,24,256]{2,1,0:T(8,128)S(1)} %bitcast.13, f32[32,24,256]{2,1,0:T(8,128)} %collective-permute-done.5.low, f32[32,24,256]{2,1,0:T(8,128)} %collective-permute-done.6.high), custom_call_target="tpu_custom_call", output_to_operand_aliasing={{}: (0, {})} | custom-call | flops 100000000 | bytes 262144 | tf_op jit(solution)/shard_map/finished_rows/pallas_call | solution.py:452
  (4 shorter events, 0.0 us)
Async XLA Ops:
  2.6 25.8 %collective-permute-start.2 = (f32[18,32,256]{2,1,0:T(8,128)}, f32[18,32,256]{2,1,0:T(8,128)S(1)}, u32[]{:S(2)}, u32[]{:S(2)}) collective-permute-start(f32[18,32,256]{2,1,0:T(8,128)} %get-tuple-element.26.refs_2_), channel_id=1, source_target_pairs={{0,30},{2,0},{4,2},{6,4},{8,6},{10,8},{12,10},{14,12},{16,14},{18,... | collective-permute-start | bytes 1769480 | tf_op jit(solution)/shard_map/ppermute | solution.py:588
  2.7 25.7 %collective-permute-start.1 = (f32[18,32,256]{2,1,0:T(8,128)}, f32[18,32,256]{2,1,0:T(8,128)S(1)}, u32[]{:S(2)}, u32[]{:S(2)}) collective-permute-start(f32[18,32,256]{2,1,0:T(8,128)} %get-tuple-element.26.refs_2_), channel_id=1, source_target_pairs={{0,2},{2,4},{4,6},{6,8},{8,10},{10,12},{12,14},{14,16},{16,18},{18... | collective-permute-start | bytes 1769480 | tf_op jit(solution)/shard_map/ppermute | solution.py:587
  5.4 5.4 %collective-permute-start = (f32[2,32,256]{2,1,0:T(8,128)}, f32[2,32,256]{2,1,0:T(8,128)S(1)}, u32[]{:S(2)}, u32[]{:S(2)}) collective-permute-start(f32[2,32,256]{2,1,0:T(8,128)} %get-tuple-element.21), channel_id=1, source_target_pairs={{0,1},{1,0},{2,3},{3,2},{4,5},{5,4},{6,7},{7,6},{8,9},{9,8},{10,11... | collective-permute-start | bytes 196616 | tf_op jit(solution)/shard_map/ppermute | solution.py:601
  10.7 0.6 copy-start
  26.6 29.9 %collective-permute-start.4 = (f32[24,32,256]{2,1,0:T(8,128)}, f32[24,32,256]{2,1,0:T(8,128)}, u32[]{:S(2)}, u32[]{:S(2)}) collective-permute-start(f32[24,32,256]{2,1,0:T(8,128)} %get-tuple-element.25.refs_3_), channel_id=1, source_target_pairs={{0,30},{2,0},{4,2},{6,4},{8,6},{10,8},{12,10},{14,12},{16,14},{18,... | collective-permute-start | bytes 2359304 | tf_op jit(solution)/shard_map/ppermute | solution.py:588
  27.6 29.0 %collective-permute-start.3 = (f32[24,32,256]{2,1,0:T(8,128)}, f32[24,32,256]{2,1,0:T(8,128)}, u32[]{:S(2)}, u32[]{:S(2)}) collective-permute-start(f32[24,32,256]{2,1,0:T(8,128)} %get-tuple-element.25.refs_3_), channel_id=1, source_target_pairs={{0,2},{2,4},{4,6},{6,8},{8,10},{10,12},{12,14},{14,16},{16,18},{18... | collective-permute-start | bytes 2359304 | tf_op jit(solution)/shard_map/ppermute | solution.py:587
  28.4 3.1 %copy-start.2 = (f32[18,32,256]{2,1,0:T(8,128)}, f32[18,32,256]{2,1,0:T(8,128)S(1)}, u32[]{:S(2)}) copy-start(f32[18,32,256]{2,1,0:T(8,128)S(1)} %collective-permute-done.2.refs_4_) | copy-start | bytes 1769476
  28.4 3.1 %copy-start.4 = (f32[18,32,256]{2,1,0:T(8,128)}, f32[18,32,256]{2,1,0:T(8,128)S(1)}, u32[]{:S(2)}) copy-start(f32[18,32,256]{2,1,0:T(8,128)S(1)} %collective-permute-done.1.refs_0_) | copy-start | bytes 1769476
  28.4 7.6 %copy-start.1 = (f32[2,32,256]{2,1,0:T(8,128)S(1)}, f32[2,32,256]{2,1,0:T(8,128)}, u32[]{:S(2)}) copy-start(f32[2,32,256]{2,1,0:T(8,128)} %copy-done) | copy-start | bytes 196612
  31.5 25.0 %copy-start.3 = (f32[18,32,256]{2,1,0:T(8,128)S(1)}, f32[18,32,256]{2,1,0:T(8,128)}, u32[]{:S(2)}) copy-start(f32[18,32,256]{2,1,0:T(8,128)} %copy-done.2) | copy-start | bytes 1769476
  31.5 25.1 %copy-start.5 = (f32[18,32,256]{2,1,0:T(8,128)S(1)}, f32[18,32,256]{2,1,0:T(8,128)}, u32[]{:S(2)}) copy-start(f32[18,32,256]{2,1,0:T(8,128)} %copy-done.4) | copy-start | bytes 1769476
  31.5 25.0 %all-to-all-start.1 = ((f32[32,8,128]{2,1,0:T(8,128)}), f32[32,8,128]{2,1,0:T(8,128)S(1)}, u32[]{:S(2)}, u32[]{:S(2)}) async-start(f32[32,8,128]{2,1,0:T(8,128)} %bitcast.23), calls=%async_computation.1 | async-start | bytes 262144 | tf_op jit(solution)/shard_map/all_to_all | solution.py:619
  41.4 29.2 %collective-permute-start.5 = (f32[32,24,256]{2,1,0:T(8,128)}, f32[32,24,256]{2,1,0:T(8,128)}, u32[]{:S(2)}, u32[]{:S(2)}) collective-permute-start(f32[32,24,256]{2,1,0:T(8,128)} %get-tuple-element.31), channel_id=1, source_target_pairs={{0,2},{2,4},{4,6},{6,8},{8,10},{10,12},{12,14},{14,16},{16,18},{18... | collective-permute-start | bytes 2359304 | tf_op jit(solution)/shard_map/ppermute | solution.py:587
  43.1 27.5 %collective-permute-start.6 = (f32[32,24,256]{2,1,0:T(8,128)}, f32[32,24,256]{2,1,0:T(8,128)}, u32[]{:S(2)}, u32[]{:S(2)}) collective-permute-start(f32[32,24,256]{2,1,0:T(8,128)} %get-tuple-element.32), channel_id=1, source_target_pairs={{0,30},{2,0},{4,2},{6,4},{8,6},{10,8},{12,10},{14,12},{16,14},{18,... | collective-permute-start | bytes 2359304 | tf_op jit(solution)/shard_map/ppermute | solution.py:588

commit v8 on v7

--- a/solution.py
+++ b/solution.py
@@ -15,7 +15,7 @@
 MY = 16
 MZ = 16
 CH = 32
-VMEM_BYTES = 24 * 1024 * 1024
+VMEM_BYTES = 16 * 1024 * 1024
 BF = jnp.bfloat16
 F32 = jnp.float32
 
@@ -362,8 +362,29 @@
         base[g, 0, start:] = plane[stop:] + own[g, 0, start:]
 
 
-def finish_kernel(_, base, low, high, out):
-    out[...] = gelu(base[...] + (low[...] + high[...]))
+def finish_kernel(upper, _, base, low, high, out, held, sent, sem_in, sem_out):
+    tiles = base.shape[1] // 8
+    gap = out.shape[1] // 8 - tiles
+    arrivals = [
+        [
+            pltpu.make_async_copy(src.at[:, pl.ds(8 * t, 8), :], held.at[i, t], sem_in.at[i, t])
+            for i, src in enumerate((base, low, high))
+        ]
+        for t in range(tiles)
+    ]
+    for copies in arrivals:
+        for copy in copies:
+            copy.start()
+    done = []
+    for t in range(tiles):
+        for copy in arrivals[t]:
+            copy.wait()
+        sent[t] = gelu(held[0, t] + (held[1, t] + held[2, t]))
+        to = t if t < upper else t + gap
+        done.append(pltpu.make_async_copy(sent.at[t], out.at[:, pl.ds(8 * to, 8), :], sem_out.at[t]))
+        done[-1].start()
+    for copy in done:
+        copy.wait()
 
 
 def in_hbm(*arrays):
@@ -447,14 +468,18 @@
 
 def finish_call(result, base, low, high, upper):
     tiles = base.shape[1] // 8
-    gap = result.shape[1] // 8 - tiles
-    piece = pl.BlockSpec((CH, 8, NX), lambda i: (0, i, 0))
+    anywhere = pl.BlockSpec(memory_space=pl.ANY)
     return pl.pallas_call(
-        finish_kernel,
+        functools.partial(finish_kernel, upper),
         out_shape=jax.ShapeDtypeStruct(result.shape, F32),
-        grid=(tiles,),
-        in_specs=[pl.BlockSpec(memory_space=pl.ANY), piece, piece, piece],
-        out_specs=pl.BlockSpec((CH, 8, NX), lambda i: (0, jnp.where(i < upper, i, i + gap), 0)),
+        in_specs=[anywhere] * 4,
+        out_specs=anywhere,
+        scratch_shapes=[
+            pltpu.VMEM((3, tiles, CH, 8, NX), F32),
+            pltpu.VMEM((tiles, CH, 8, NX), F32),
+            pltpu.SemaphoreType.DMA((3, tiles)),
+            pltpu.SemaphoreType.DMA((tiles,)),
+        ],
         input_output_aliases={0: 0},
         compiler_params=params(),
         cost_estimate=cost(10**8, 2**18),
@@ -595,7 +620,7 @@
     upper = (0,)
     lower = tuple(range(tiles - max(1, tiles // 4), tiles))
     middle = tuple(range(1, lower[0]))
-    packed, later, edges = pack_call(field, middle, max(1, 2 * len(middle) // 5))
+    packed, later, edges = pack_call(field, middle, (len(middle) + 1) // 2)
     first_low, first_high = to_neighbours(packed, packed)
     if gy == 2:
         halo = lax.ppermute(edges, "gy", ring("gy", gy, 1))
@@ -608,21 +633,21 @@
         )
     j_own, n_own = spectral_filter.shape[2], spectral_filter.shape[3]
     whole_tiles = j_own == 8 and n_own == 2 * MX
-    coarse = after(forward_call(after(field, packed), gy, whole_tiles), halo)
+    coarse = forward_call(after(field, packed), gy, whole_tiles)
+    down, own, up = own_call(after(field, coarse), halo, depth_weight, point_weight, upper, lower)
     if whole_tiles:
         both = ("gz", "gy")
         got = lax.all_to_all(coarse, both, split_axis=0, concat_axis=0, tiled=True)
         sent = after(later, got)
         later_low, later_high = to_neighbours(sent, sent)
-        gains = after(spectral_filter, first_low, first_high)
+        gains = after(spectral_filter, first_low, first_high, own)
         filtered = filter_call(got, gains, gz, gy, forward_scale)
         back = lax.all_to_all(filtered, both, split_axis=0, concat_axis=0, tiled=True)
         back = back.reshape(CH // 2, MY, 4 * MX)
     else:
         later_low, later_high = to_neighbours(later, later)
-        filtered = back = general_filter(coarse, spectral_filter, gz, gy, forward_scale)
-    down, own, up = own_call(after(field, filtered), halo, depth_weight, point_weight, upper, lower)
-    low, high = to_neighbours(down, up)
+        back = general_filter(coarse, spectral_filter, gz, gy, forward_scale)
+    low, high = to_neighbours(after(down, back), after(up, back))
     mixed = middle_call(
         depth_weight,
         point_weight,

time: 75.1 us -> 71.9 us (0.957)
  waiting for transfers between devices: 13.4 us -> 8.63 us
  starting transfers between devices: 11.9 us -> 15.5 us
  Pallas kernels: 32.6 us -> 31.3 us
    all_to_all x1, waiting for transfers between devices: 13.4 us -> 0.01 us  [body(): got = lax.all_to_all(coarse, both, split_axis=0, concat_axis=0, tiled=True)]
    all_to_all x1, starting transfers between devices: 4.51 us -> 8.29 us  [body(): got = lax.all_to_all(coarse, both, split_axis=0, concat_axis=0, tiled=True)]
    ppermute x3, waiting for transfers between devices: 0.01 us -> 3.43 us  [to_neighbours(): lax.ppermute(down, 'gz', ring('gz', gz, 1))]
    ppermute x1, waiting for transfers between devices: 0.01 us -> 2.71 us  [body(): halo = lax.ppermute(edges, 'gy', ring('gy', gy, 1))]
    ppermute x3, waiting for transfers between devices: 0.01 us -> 2.49 us  [to_neighbours(): lax.ppermute(up, 'gz', ring('gz', gz, -1))]
    ppermute x3, starting transfers between devices: 5.13 us -> 4 us  [to_neighbours(): lax.ppermute(down, 'gz', ring('gz', gz, 1))]
    pallas_call x1, Pallas kernels: 3.44 us -> 2.65 us  [finish_call(): pl.pallas_call(functools.partial(finish_kernel, upper), out_shape=jax.Sha...]
  transfers between devices with their start and end apart: 8 -> 8, of which waited for: 1 -> 3; matrix products, arithmetic and copies ran while one was open for 0% -> 0% of each run, Pallas kernels for 36% -> 36%
where the time goes in v8:
time: 71.9 us; the launch traced here: 71.4 us
  Pallas kernels  31.3 us (44%)
  blocking collectives  15.9 us (22%)
  starting transfers between devices  15.5 us (22%)
  waiting for transfers between devices  8.63 us (12%)
    all_to_all x1, blocking collectives, body(): lax.all_to_all(filtered, both, split_axis=0, concat_axis=0, tiled=True)  15.9 us
    pallas_call x1, Pallas kernels, middle_call(): pl.pallas_call(middle_kernel, out_shape=pltpu.HBM((CH, rows, NX), F32), i...  8.32 us
    all_to_all x1, starting transfers between devices, body(): got = lax.all_to_all(coarse, both, split_axis=0, concat_axis=0, tiled=True)  8.29 us
    pallas_call x1, Pallas kernels, inverse_call(): pl.pallas_call(functools.partial(inverse_kernel, upper), out_shape=[jax.S...  5.55 us
    pallas_call x1, Pallas kernels, own_call(): pl.pallas_call(functools.partial(own_kernel, (upper, lower)), out_shape=s...  5.37 us
    pallas_call x1, Pallas kernels, forward_call(): pl.pallas_call(forward_kernel, out_shape=(pltpu.HBM if pinned else jax.Sh...  4.13 us
    ppermute x3, starting transfers between devices, to_neighbours(): lax.ppermute(down, 'gz', ring('gz', gz, 1))  4 us
    ppermute x3, waiting for transfers between devices, to_neighbours(): lax.ppermute(down, 'gz', ring('gz', gz, 1))  3.43 us
  transfers between devices with their start and end apart: 8, of which 3 were waited for; matrix products, arithmetic and copies ran while one was open for 0% of the time, Pallas kernels for 36%

profile of v8, /device:TPU:1, one launch (start us, length us, event | category | flops | bytes accessed | tf_op | source)
XLA Modules:
  0.0 71.4 jit_solution(10197990271447808626)
XLA Ops:
  0.0 2.7 %packed_rows.1 = (f32[26,32,256]{2,1,0:T(8,128)}, f32[16,32,256]{2,1,0:T(8,128)}, f32[2,32,256]{2,1,0:T(8,128)}) custom-call(f32[32,64,256]{2,1,0:T(8,128)} %bitcast.16), custom_call_target="tpu_custom_call" | custom-call | flops 100000000 | bytes 262144 | tf_op jit(solution)/shard_map/packed_rows/pallas_call | solution.py:495
  2.7 0.0 copy-start
  2.7 0.1 collective-permute-start.1
  2.8 2.6 %collective-permute-start = (f32[26,32,256]{2,1,0:T(8,128)}, f32[26,32,256]{2,1,0:T(8,128)S(1)}, u32[]{:S(2)}, u32[]{:S(2)}) collective-permute-start(f32[26,32,256]{2,1,0:T(8,128)} %get-tuple-element.28.refs_2_), channel_id=1, source_target_pairs={{0,2},{2,4},{4,6},{6,8},{8,10},{10,12},{12,14},{14,16},{16,18},{18... | collective-permute-start | bytes 2555912 | tf_op jit(solution)/shard_map/ppermute | solution.py:612
  5.5 4.1 %forward_modes.1 = f32[256,128]{1,0:T(8,128)} custom-call(f32[8,4,64,256]{3,2,1,0:T(8,128)} %bitcast.17, bf16[2,256,128]{2,1,0:T(8,128)(2,1)} %constant.24.clone.x_top, bf16[2,256,128]{2,1,0:T(8,128)(2,1)} %constant.25.clone.x_rest, bf16[2,32,64]{2,1,0:T(8,128)(2,1)} %constant.26.clone.y_top, bf16[2,32,64]{2,1,0:T(8,128)(2,1)} %constant.27.clone.y_rest), custom_call_target="tpu_custom_call" | custom-call | flops 100000000 | bytes 262144 | tf_op jit(solution)/shard_map/forward_modes/pallas_call | solution.py:414
  9.6 8.3 %all-to-all-start = ((f32[32,8,128]{2,1,0:T(8,128)}), f32[32,8,128]{2,1,0:T(8,128)S(1)}, u32[]{:S(2)}, u32[]{:S(2)}) async-start(f32[32,8,128]{2,1,0:T(8,128)} %bitcast.22), calls=%async_computation | async-start | bytes 262144 | tf_op jit(solution)/shard_map/all_to_all | solution.py:640
  17.9 0.0 copy-done
  17.9 1.5 %collective-permute-start.2 = (f32[2,32,256]{2,1,0:T(8,128)S(1)}, f32[2,32,256]{2,1,0:T(8,128)S(1)}, u32[]{:S(2)}, u32[]{:S(2)}) collective-permute-start(f32[2,32,256]{2,1,0:T(8,128)S(1)} %copy-done), channel_id=1, source_target_pairs={{0,1},{1,0},{2,3},{3,2},{4,5},{5,4},{6,7},{7,6},{8,9},{9,8},{10,11... | collective-permute-start | bytes 196616 | tf_op jit(solution)/shard_map/ppermute | solution.py:626
  19.4 2.7 %collective-permute-done.2.halo = f32[2,32,256]{2,1,0:T(8,128)S(1)} collective-permute-done((f32[2,32,256]{2,1,0:T(8,128)S(1)}, f32[2,32,256]{2,1,0:T(8,128)S(1)}, u32[]{:S(2)}, u32[]{:S(2)}) %collective-permute-start.2) | collective-permute-done | bytes 65568 | tf_op jit(solution)/shard_map/ppermute | solution.py:626
  22.1 5.4 %own_sums.1 = (f32[32,24,256]{2,1,0:T(8,128)}, f32[32,24,256]{2,1,0:T(8,128)}, f32[32,24,256]{2,1,0:T(8,128)}) custom-call(f32[32,27]{1,0:T(8,128)} %weight.3, f32[32,32]{1,0:T(8,128)} %point.3, f32[32,64,256]{2,1,0:T(8,128)} %bitcast.18, f32[2,32,256]{2,1,0:T(8,128)S(1)} %collective-permute-done.2.halo), custom_call_target="tpu_custom_call" | custom-call | flops 100000000 | bytes 262144 | tf_op jit(solution)/shard_map/own_sums/pallas_call | solution.py:522
  27.4 0.0 all-to-all-done
  27.5 1.2 %collective-permute-start.4 = (f32[16,32,256]{2,1,0:T(8,128)}, f32[16,32,256]{2,1,0:T(8,128)}, u32[]{:S(2)}, u32[]{:S(2)}) collective-permute-start(f32[16,32,256]{2,1,0:T(8,128)} %get-tuple-element.27.refs_3_), channel_id=1, source_target_pairs={{0,30},{2,0},{4,2},{6,4},{8,6},{10,8},{12,10},{14,12},{16,14},{18,... | collective-permute-start | bytes 1572872 | tf_op jit(solution)/shard_map/ppermute | solution.py:613
  28.7 0.8 %collective-permute-start.3 = (f32[16,32,256]{2,1,0:T(8,128)}, f32[16,32,256]{2,1,0:T(8,128)}, u32[]{:S(2)}, u32[]{:S(2)}) collective-permute-start(f32[16,32,256]{2,1,0:T(8,128)} %get-tuple-element.27.refs_3_), channel_id=1, source_target_pairs={{0,2},{2,4},{4,6},{6,8},{8,10},{10,12},{12,14},{14,16},{16,18},{18... | collective-permute-start | bytes 1572872 | tf_op jit(solution)/shard_map/ppermute | solution.py:612
  29.5 0.0 collective-permute-done.1.refs_4_
  29.5 0.0 collective-permute-done.refs_0_
  29.5 2.6 %filter_modes.1 = f32[256,128]{1,0:T(8,128)} custom-call(f32[256,128]{1,0:T(8,128)S(1)} %bitcast.15, f32[2,16,8,64]{3,2,1,0:T(8,128)} %gains, bf16[256,256]{1,0:T(8,128)(2,1)} %constant.28.clone.f_top, bf16[256,256]{1,0:T(8,128)(2,1)} %constant.29.clone.f_rest, bf16[512,128]{1,0:T(8,128)(2,1)} %constant.30.clone.i_top, bf16[512,128]{1,0:T(8,128)(2,1)} %constant.31.clone.i_rest), custom_call_target="tpu_custom_call" | custom-call | flops 199999995904 | bytes 262144 | tf_op jit(solution)/shard_map/filter_modes/pallas_call | solution.py:433
  32.1 15.9 %all_to_all.20 = f32[32,8,128]{2,1,0:T(8,128)S(1)} all-to-all(f32[32,8,128]{2,1,0:T(8,128)} %bitcast.23), channel_id=1, replica_groups=mesh['gz'=16,'gy'=2] {'gz','gy'}, dimensions={0} | all-to-all | bytes 262144 | tf_op jit(solution)/shard_map/all_to_all | solution.py:645
  48.0 0.6 collective-permute-start.5
  48.6 0.4 collective-permute-start.6
  49.0 0.0 collective-permute-done.4.refs_5_
  49.0 0.0 collective-permute-done.3.refs_1_
  49.0 8.3 %middle_sums.1 = f32[32,40,256]{2,1,0:T(8,128)} custom-call(f32[32,27]{1,0:T(8,128)} %weight.3, f32[32,32]{1,0:T(8,128)} %point.3, f32[26,32,256]{2,1,0:T(8,128)S(1)} %collective-permute-done.refs_0_, f32[16,32,256]{2,1,0:T(8,128)} %collective-permute-done.3.refs_1_, f32[26,32,256]{2,1,0:T(8,128)} %get-tuple-element.28.refs_2_, ...), custom_call_target="tpu_custom_call" | custom-call | flops 199999995904 | bytes 262144 | tf_op jit(solution)/shard_map/middle_sums/pallas_call | solution.py:549
  57.3 5.5 %inverse_modes.1 = (f32[8,4,64,256]{3,2,1,0:T(8,128)}, f32[8,4,24,256]{3,2,1,0:T(8,128)S(1)}) custom-call(f32[16,16,128]{2,1,0:T(8,128)S(1)} %bitcast.14, f32[32]{0:T(128)} %bias.1, bf16[2,128,256]{2,1,0:T(8,128)(2,1)} %constant.32.clone.x_top, bf16[2,128,256]{2,1,0:T(8,128)(2,1)} %constant.33.clone.x_rest, bf16[2,64,32]{2,1,0:T(8,128)(2,1)} %constant.34.clone.y_top, ...), custom_call_target="tpu_custom_call" | custom-call | flops 100000000 | bytes 262144 | tf_op jit(solution)/shard_map/inverse_modes/pallas_call | solution.py:447
  62.9 3.4 %collective-permute-done.5.low = f32[32,24,256]{2,1,0:T(8,128)} collective-permute-done((f32[32,24,256]{2,1,0:T(8,128)}, f32[32,24,256]{2,1,0:T(8,128)}, u32[]{:S(2)}, u32[]{:S(2)}) %collective-permute-start.5) | collective-permute-done | bytes 786464 | tf_op jit(solution)/shard_map/ppermute | solution.py:612
  66.3 2.5 %collective-permute-done.6.high = f32[32,24,256]{2,1,0:T(8,128)} collective-permute-done((f32[32,24,256]{2,1,0:T(8,128)}, f32[32,24,256]{2,1,0:T(8,128)}, u32[]{:S(2)}, u32[]{:S(2)}) %collective-permute-start.6) | collective-permute-done | bytes 786464 | tf_op jit(solution)/shard_map/ppermute | solution.py:613
  68.8 2.6 %finished_rows.1 = f32[32,64,256]{2,1,0:T(8,128)} custom-call(f32[32,64,256]{2,1,0:T(8,128)} %bitcast.19, f32[32,24,256]{2,1,0:T(8,128)S(1)} %bitcast.13, f32[32,24,256]{2,1,0:T(8,128)} %collective-permute-done.5.low, f32[32,24,256]{2,1,0:T(8,128)} %collective-permute-done.6.high), custom_call_target="tpu_custom_call", output_to_operand_aliasing={{}: (0, {})} | custom-call | flops 100000000 | bytes 262144 | tf_op jit(solution)/shard_map/finished_rows/pallas_call | solution.py:472
Async XLA Ops:
  2.7 15.2 %copy-start = (f32[2,32,256]{2,1,0:T(8,128)S(1)}, f32[2,32,256]{2,1,0:T(8,128)}, u32[]{:S(2)}) copy-start(f32[2,32,256]{2,1,0:T(8,128)} %get-tuple-element.23) | copy-start | bytes 196612
  2.7 26.8 %collective-permute-start.1 = (f32[26,32,256]{2,1,0:T(8,128)}, f32[26,32,256]{2,1,0:T(8,128)S(1)}, u32[]{:S(2)}, u32[]{:S(2)}) collective-permute-start(f32[26,32,256]{2,1,0:T(8,128)} %get-tuple-element.28.refs_2_), channel_id=1, source_target_pairs={{0,30},{2,0},{4,2},{6,4},{8,6},{10,8},{12,10},{14,12},{16,14},{18,... | collective-permute-start | bytes 2555912 | tf_op jit(solution)/shard_map/ppermute | solution.py:613
  2.8 26.7 %collective-permute-start = (f32[26,32,256]{2,1,0:T(8,128)}, f32[26,32,256]{2,1,0:T(8,128)S(1)}, u32[]{:S(2)}, u32[]{:S(2)}) collective-permute-start(f32[26,32,256]{2,1,0:T(8,128)} %get-tuple-element.28.refs_2_), channel_id=1, source_target_pairs={{0,2},{2,4},{4,6},{6,8},{8,10},{10,12},{12,14},{14,16},{16,18},{18... | collective-permute-start | bytes 2555912 | tf_op jit(solution)/shard_map/ppermute | solution.py:612
  9.6 17.8 %all-to-all-start = ((f32[32,8,128]{2,1,0:T(8,128)}), f32[32,8,128]{2,1,0:T(8,128)S(1)}, u32[]{:S(2)}, u32[]{:S(2)}) async-start(f32[32,8,128]{2,1,0:T(8,128)} %bitcast.22), calls=%async_computation | async-start | bytes 262144 | tf_op jit(solution)/shard_map/all_to_all | solution.py:640
  17.9 4.2 %collective-permute-start.2 = (f32[2,32,256]{2,1,0:T(8,128)S(1)}, f32[2,32,256]{2,1,0:T(8,128)S(1)}, u32[]{:S(2)}, u32[]{:S(2)}) collective-permute-start(f32[2,32,256]{2,1,0:T(8,128)S(1)} %copy-done), channel_id=1, source_target_pairs={{0,1},{1,0},{2,3},{3,2},{4,5},{5,4},{6,7},{7,6},{8,9},{9,8},{10,11... | collective-permute-start | bytes 196616 | tf_op jit(solution)/shard_map/ppermute | solution.py:626
  27.5 21.5 %collective-permute-start.4 = (f32[16,32,256]{2,1,0:T(8,128)}, f32[16,32,256]{2,1,0:T(8,128)}, u32[]{:S(2)}, u32[]{:S(2)}) collective-permute-start(f32[16,32,256]{2,1,0:T(8,128)} %get-tuple-element.27.refs_3_), channel_id=1, source_target_pairs={{0,30},{2,0},{4,2},{6,4},{8,6},{10,8},{12,10},{14,12},{16,14},{18,... | collective-permute-start | bytes 1572872 | tf_op jit(solution)/shard_map/ppermute | solution.py:613
  28.7 20.3 %collective-permute-start.3 = (f32[16,32,256]{2,1,0:T(8,128)}, f32[16,32,256]{2,1,0:T(8,128)}, u32[]{:S(2)}, u32[]{:S(2)}) collective-permute-start(f32[16,32,256]{2,1,0:T(8,128)} %get-tuple-element.27.refs_3_), channel_id=1, source_target_pairs={{0,2},{2,4},{4,6},{6,8},{8,10},{10,12},{12,14},{14,16},{16,18},{18... | collective-permute-start | bytes 1572872 | tf_op jit(solution)/shard_map/ppermute | solution.py:612
  48.0 18.3 %collective-permute-start.5 = (f32[32,24,256]{2,1,0:T(8,128)}, f32[32,24,256]{2,1,0:T(8,128)}, u32[]{:S(2)}, u32[]{:S(2)}) collective-permute-start(f32[32,24,256]{2,1,0:T(8,128)} %get-tuple-element.32), channel_id=1, source_target_pairs={{0,2},{2,4},{4,6},{6,8},{8,10},{10,12},{12,14},{14,16},{16,18},{18... | collective-permute-start | bytes 2359304 | tf_op jit(solution)/shard_map/ppermute | solution.py:612
  48.6 20.2 %collective-permute-start.6 = (f32[32,24,256]{2,1,0:T(8,128)}, f32[32,24,256]{2,1,0:T(8,128)}, u32[]{:S(2)}, u32[]{:S(2)}) collective-permute-start(f32[32,24,256]{2,1,0:T(8,128)} %get-tuple-element.34), channel_id=1, source_target_pairs={{0,30},{2,0},{4,2},{6,4},{8,6},{10,8},{12,10},{14,12},{16,14},{18,... | collective-permute-start | bytes 2359304 | tf_op jit(solution)/shard_map/ppermute | solution.py:613

commit v9 on v8

--- a/solution.py
+++ b/solution.py
@@ -282,23 +282,25 @@
         copy.wait()
 
 
-def middle_kernel(weight, point, *refs):
-    planes, out = refs[:6], refs[6]
-    taken, weights, points, sent, turned, depth, gains, sem_in, sem_out, sem_few = refs[7:]
-    split = planes[0].shape[0]
+def middle_kernel(pieces, weight, point, *refs):
+    count = len(pieces)
+    planes, out = refs[: 3 * count], refs[3 * count]
+    taken, weights, points, sent, turned, depth, gains, sem_in, sem_out, sem_few = refs[3 * count + 1 :]
     few = [
         pltpu.make_async_copy(a, b, sem_few.at[i])
         for i, (a, b) in enumerate(((weight, weights), (point, points)))
     ]
-    arrivals = [
-        [
-            pltpu.make_async_copy(planes[2 * a], taken.at[a, pl.ds(0, split)], sem_in.at[a, 0]),
-            pltpu.make_async_copy(
-                planes[2 * a + 1], taken.at[a, pl.ds(split, taken.shape[1] - split)], sem_in.at[a, 1]
-            ),
-        ]
-        for a in range(3)
-    ]
+    arrivals = []
+    for a in range(3):
+        copies, to = [], 0
+        for k, (first, rows) in enumerate(pieces):
+            copies.append(
+                pltpu.make_async_copy(
+                    planes[count * a + k].at[pl.ds(first, rows)], taken.at[a, pl.ds(to, rows)], sem_in.at[a, k]
+                )
+            )
+            to += rows
+        arrivals.append(copies)
     for a in (1, 0, 2):
         for copy in arrivals[a]:
             copy.start()
@@ -336,7 +338,8 @@
     return value * jnp.where(value < 0.0, tail, 1.0 - tail)
 
 
-def inverse_kernel(upper, modes, bias, x_top, x_rest, y_top, y_rest, middle, own, out, base, columns):
+def inverse_kernel(upper, modes, bias, x_top, x_rest, y_top, y_rest, own, *refs):
+    middle, (out, base, columns) = refs[:-3], refs[-3:]
     q = pl.program_id(0)
     groups, _, y_local, _ = out.shape
 
@@ -354,12 +357,15 @@
 
     h, p = q // 2, q % 2
     rows = dot3((columns[h, 0], columns[h, 1]), (x_top[p], x_rest[p]))
-    start, stop = upper, upper + middle.shape[2]
     for g in range(groups):
         plane = rows[g * y_local : (g + 1) * y_local] + bias[4 * g + q]
-        out[g, 0, start:stop] = gelu(plane[start:stop] + middle[g, 0])
-        base[g, 0, :start] = plane[:start] + own[g, 0, :start]
-        base[g, 0, start:] = plane[stop:] + own[g, 0, start:]
+        base[g, 0, :upper] = plane[:upper] + own[g, 0, :upper]
+        at = upper
+        for part in middle:
+            to = at + part.shape[2]
+            out[g, 0, at:to] = gelu(plane[at:to] + part[g, 0])
+            at = to
+        base[g, 0, upper:] = plane[at:] + own[g, 0, upper:]
 
 
 def finish_kernel(upper, _, base, low, high, out, held, sent, sem_in, sem_out):
@@ -442,7 +448,7 @@
 def inverse_call(modes, bias, middle, own, upper, y_local, gy, scale):
     tables = [*halves(x_table(True, scale)), *halves(y_table(y_local, gy, True))]
     some = lambda rows: pl.BlockSpec((CH // 4, 1, rows, NX), lambda i: (0, i, 0, 0))
-    planes = in_hbm(by_four(middle), by_four(own))
+    planes = in_hbm(by_four(own), *map(by_four, middle))
     rim = own.shape[1]
     result, base = pl.pallas_call(
         functools.partial(inverse_kernel, upper),
@@ -543,13 +549,13 @@
     )(*in_hbm(weight, point, field), halo)
 
 
-def middle_call(weight, point, low, own, high):
-    rows = own[0].shape[0] + own[1].shape[0] - 2
+def middle_call(weight, point, low, own, high, pieces):
+    rows = sum(r for _, r in pieces) - 2
     hbm = pl.BlockSpec(memory_space=pltpu.HBM)
     return pl.pallas_call(
-        middle_kernel,
+        functools.partial(middle_kernel, pieces),
         out_shape=pltpu.HBM((CH, rows, NX), F32),
-        in_specs=[hbm] * 2 + [pl.BlockSpec(memory_space=pl.ANY)] * 6,
+        in_specs=[hbm] * 2 + [pl.BlockSpec(memory_space=pl.ANY)] * (3 * len(pieces)),
         out_specs=hbm,
         scratch_shapes=[
             pltpu.VMEM((3, rows + 2, CH, NX), F32),
@@ -559,12 +565,12 @@
             pltpu.VMEM((3, rows + 2, CH, NX), F32),
             pltpu.VMEM((1, rows, CH, NX), F32),
             pltpu.VMEM((27, CH, 128), F32),
-            pltpu.SemaphoreType.DMA((3, 2)),
+            pltpu.SemaphoreType.DMA((3, len(pieces))),
             pltpu.SemaphoreType.DMA((rows // 8,)),
             pltpu.SemaphoreType.DMA((2,)),
         ],
         compiler_params=params(),
-        cost_estimate=cost(2 * 10**11, 2**18),
+        cost_estimate=cost(2 * 10**11 if len(pieces) > 1 else 10**8, 2**18),
         name="middle_sums",
     )(*in_hbm(weight, point), *low, *in_hbm(*own), *high)
 
@@ -618,9 +624,11 @@
 
     tiles = y_local // 8
     upper = (0,)
-    lower = tuple(range(tiles - max(1, tiles // 4), tiles))
+    lower = (tiles - 1,)
     middle = tuple(range(1, lower[0]))
-    packed, later, edges = pack_call(field, middle, (len(middle) + 1) // 2)
+    early = 8 * ((len(middle) + 1) // 2)
+    late = 8 * len(middle) - early
+    packed, later, edges = pack_call(field, middle, early // 8)
     first_low, first_high = to_neighbours(packed, packed)
     if gy == 2:
         halo = lax.ppermute(edges, "gy", ring("gy", gy, 1))
@@ -644,18 +652,26 @@
         filtered = filter_call(got, gains, gz, gy, forward_scale)
         back = lax.all_to_all(filtered, both, split_axis=0, concat_axis=0, tiled=True)
         back = back.reshape(CH // 2, MY, 4 * MX)
+        mark = filtered
     else:
         later_low, later_high = to_neighbours(later, later)
-        back = general_filter(coarse, spectral_filter, gz, gy, forward_scale)
-    low, high = to_neighbours(after(down, back), after(up, back))
+        mark = back = general_filter(coarse, spectral_filter, gz, gy, forward_scale)
     mixed = middle_call(
+        depth_weight, point_weight, (first_low,), (after(packed, mark),), (first_high,), ((0, early + 2),)
+    )
+    down, up, later, _, _ = lax.optimization_barrier((down, up, later, back, mixed))
+    low, high = to_neighbours(down, up)
+    mixed_later = middle_call(
         depth_weight,
         point_weight,
         (first_low, later_low),
-        (after(packed, back), later),
+        (packed, later),
         (first_high, later_high),
+        ((early, 2), (0, late)),
     )
-    result, base = inverse_call(back, bias_vector, mixed, own, 8, y_local, gy, inverse_scale)
+    result, base = inverse_call(
+        back, bias_vector, (mixed, mixed_later), own, 8, y_local, gy, inverse_scale
+    )
     result = finish_call(result, base, low, high, 1)
     return result.reshape(CH, 1, y_local, NX)
 

time: 71.9 us -> 68.9 us (0.958)
  the two profiles are of different devices: /device:TPU:1 before, /device:TPU:0 now
where the time goes in v9:
time: 68.9 us; the launch traced here: 68.3 us
  Pallas kernels  34.2 us (50%)
  starting transfers between devices  27.5 us (40%)
  waiting for transfers between devices  6.52 us (9%)
    ppermute x3, starting transfers between devices, to_neighbours(): lax.ppermute(up, 'gz', ring('gz', gz, -1))  14.4 us
    pallas_call x2, Pallas kernels, middle_call(): pl.pallas_call(functools.partial(middle_kernel, pieces), out_shape=pltpu....  12.1 us
    pallas_call x1, Pallas kernels, inverse_call(): pl.pallas_call(functools.partial(inverse_kernel, upper), out_shape=[jax.S...  5.81 us
    all_to_all x1, starting transfers between devices, body(): got = lax.all_to_all(coarse, both, split_axis=0, concat_axis=0, tiled=True)  5.73 us
    all_to_all x1, starting transfers between devices, body(): lax.all_to_all(filtered, both, split_axis=0, concat_axis=0, tiled=True)  5.16 us
    pallas_call x1, Pallas kernels, own_call(): pl.pallas_call(functools.partial(own_kernel, (upper, lower)), out_shape=s...  4.43 us
    pallas_call x1, Pallas kernels, forward_call(): pl.pallas_call(forward_kernel, out_shape=(pltpu.HBM if pinned else jax.Sh...  4.13 us
    ppermute x1, waiting for transfers between devices, body(): halo = lax.ppermute(edges, 'gy', ring('gy', gy, 1))  3.25 us
  transfers between devices with their start and end apart: 9, of which 2 were waited for; matrix products, arithmetic and copies ran while one was open for 0% of the time, Pallas kernels for 43%

profile of v9, /device:TPU:0, one launch (start us, length us, event | category | flops | bytes accessed | tf_op | source)
XLA Modules:
  0.0 68.3 jit_solution(10485163827241913490)
XLA Ops:
  0.0 2.8 %packed_rows.1 = (f32[26,32,256]{2,1,0:T(8,128)}, f32[24,32,256]{2,1,0:T(8,128)}, f32[2,32,256]{2,1,0:T(8,128)}) custom-call(f32[32,64,256]{2,1,0:T(8,128)} %bitcast.17), custom_call_target="tpu_custom_call" | custom-call | flops 100000000 | bytes 262144 | tf_op jit(solution)/shard_map/packed_rows/pallas_call | solution.py:501
  2.8 0.0 copy-start
  2.8 5.5 %collective-permute-start.1 = (f32[26,32,256]{2,1,0:T(8,128)}, f32[26,32,256]{2,1,0:T(8,128)S(1)}, u32[]{:S(2)}, u32[]{:S(2)}) collective-permute-start(f32[26,32,256]{2,1,0:T(8,128)} %get-tuple-element.27.refs_1_.refs_2_), channel_id=1, source_target_pairs={{0,30},{2,0},{4,2},{6,4},{8,6},{10,8},{12,10},{14,12},{16,14},{18,... | collective-permute-start | bytes 2555912 | tf_op jit(solution)/shard_map/ppermute | solution.py:619
  8.3 0.0 collective-permute-start
  8.3 4.1 %forward_modes.1 = f32[256,128]{1,0:T(8,128)} custom-call(f32[8,4,64,256]{3,2,1,0:T(8,128)} %bitcast.18, bf16[2,256,128]{2,1,0:T(8,128)(2,1)} %constant.24.clone.x_top, bf16[2,256,128]{2,1,0:T(8,128)(2,1)} %constant.25.clone.x_rest, bf16[2,32,64]{2,1,0:T(8,128)(2,1)} %constant.26.clone.y_top, bf16[2,32,64]{2,1,0:T(8,128)(2,1)} %constant.27.clone.y_rest), custom_call_target="tpu_custom_call" | custom-call | flops 100000000 | bytes 262144 | tf_op jit(solution)/shard_map/forward_modes/pallas_call | solution.py:420
  12.4 5.7 %all-to-all-start = ((f32[32,8,128]{2,1,0:T(8,128)}), f32[32,8,128]{2,1,0:T(8,128)S(1)}, u32[]{:S(2)}, u32[]{:S(2)}) async-start(f32[32,8,128]{2,1,0:T(8,128)} %bitcast.23), calls=%async_computation | async-start | bytes 262144 | tf_op jit(solution)/shard_map/all_to_all | solution.py:648
  18.2 0.0 copy-done
  18.2 1.8 %collective-permute-start.2 = (f32[2,32,256]{2,1,0:T(8,128)S(1)}, f32[2,32,256]{2,1,0:T(8,128)S(1)}, u32[]{:S(2)}, u32[]{:S(2)}) collective-permute-start(f32[2,32,256]{2,1,0:T(8,128)S(1)} %copy-done), channel_id=1, source_target_pairs={{0,1},{1,0},{2,3},{3,2},{4,5},{5,4},{6,7},{7,6},{8,9},{9,8},{10,11... | collective-permute-start | bytes 196616 | tf_op jit(solution)/shard_map/ppermute | solution.py:634
  20.0 3.3 %collective-permute-done.2.halo = f32[2,32,256]{2,1,0:T(8,128)S(1)} collective-permute-done((f32[2,32,256]{2,1,0:T(8,128)S(1)}, f32[2,32,256]{2,1,0:T(8,128)S(1)}, u32[]{:S(2)}, u32[]{:S(2)}) %collective-permute-start.2) | collective-permute-done | bytes 65568 | tf_op jit(solution)/shard_map/ppermute | solution.py:634
  23.3 4.4 %own_sums.1 = (f32[32,16,256]{2,1,0:T(8,128)}, f32[32,16,256]{2,1,0:T(8,128)}, f32[32,16,256]{2,1,0:T(8,128)}) custom-call(f32[32,27]{1,0:T(8,128)} %weight.5, f32[32,32]{1,0:T(8,128)} %point.5, f32[32,64,256]{2,1,0:T(8,128)} %bitcast.19, f32[2,32,256]{2,1,0:T(8,128)S(1)} %collective-permute-done.2.halo), custom_call_target="tpu_custom_call" | custom-call | flops 100000000 | bytes 262144 | tf_op jit(solution)/shard_map/own_sums/pallas_call | solution.py:528
  27.7 0.0 all-to-all-done
  27.7 4.3 %collective-permute-start.4 = (f32[24,32,256]{2,1,0:T(8,128)}, f32[24,32,256]{2,1,0:T(8,128)}, u32[]{:S(2)}, u32[]{:S(2)}) collective-permute-start(f32[24,32,256]{2,1,0:T(8,128)} %get-tuple-element.32.refs_3_), channel_id=1, source_target_pairs={{0,30},{2,0},{4,2},{6,4},{8,6},{10,8},{12,10},{14,12},{16,14},{18,... | collective-permute-start | bytes 2359304 | tf_op jit(solution)/shard_map/ppermute | solution.py:619
  32.0 0.0 collective-permute-start.3
  32.0 0.0 collective-permute-done.1.refs_2_.refs_4_
  32.0 0.0 collective-permute-done.refs_0_
  32.0 2.7 %filter_modes.1 = f32[256,128]{1,0:T(8,128)} custom-call(f32[256,128]{1,0:T(8,128)S(1)} %bitcast.16, f32[2,16,8,64]{3,2,1,0:T(8,128)} %gains, bf16[256,256]{1,0:T(8,128)(2,1)} %constant.28.clone.f_top, bf16[256,256]{1,0:T(8,128)(2,1)} %constant.29.clone.f_rest, bf16[512,128]{1,0:T(8,128)(2,1)} %constant.30.clone.i_top, bf16[512,128]{1,0:T(8,128)(2,1)} %constant.31.clone.i_rest), custom_call_target="tpu_custom_call" | custom-call | flops 199999995904 | bytes 262144 | tf_op jit(solution)/shard_map/filter_modes/pallas_call | solution.py:439
  34.7 5.2 %all-to-all-start.1 = ((f32[32,8,128]{2,1,0:T(8,128)}), f32[32,8,128]{2,1,0:T(8,128)S(1)}, u32[]{:S(2)}, u32[]{:S(2)}) async-start(f32[32,8,128]{2,1,0:T(8,128)} %bitcast.25), calls=%async_computation.1 | async-start | bytes 262144 | tf_op jit(solution)/shard_map/all_to_all | solution.py:653
  39.8 5.8 %middle_sums.2 = f32[32,24,256]{2,1,0:T(8,128)} custom-call(f32[32,27]{1,0:T(8,128)} %weight.5, f32[32,32]{1,0:T(8,128)} %point.5, f32[26,32,256]{2,1,0:T(8,128)S(1)} %collective-permute-done.refs_0_, f32[26,32,256]{2,1,0:T(8,128)} %get-tuple-element.27.refs_1_.refs_2_, f32[26,32,256]{2,1,0:T(8,128)S(1)} %collective-permute-done.1.refs_2_.refs_4_), custom_call_target="tpu_custom_call" | custom-call | flops 100000000 | bytes 262144 | tf_op jit(solution)/shard_map/middle_sums/pallas_call | solution.py:555
  45.6 3.2 %all-to-all-done.1 = f32[32,8,128]{2,1,0:T(8,128)S(1)} async-done(((f32[32,8,128]{2,1,0:T(8,128)}), f32[32,8,128]{2,1,0:T(8,128)S(1)}, u32[]{:S(2)}, u32[]{:S(2)}) %all-to-all-start.1) | async-done | bytes 131104 | tf_op jit(solution)/shard_map/all_to_all | solution.py:653
  48.9 0.3 collective-permute-start.5
  49.2 4.7 %collective-permute-start.6 = (f32[32,16,256]{2,1,0:T(8,128)}, f32[32,16,256]{2,1,0:T(8,128)}, u32[]{:S(2)}, u32[]{:S(2)}) collective-permute-start(f32[32,16,256]{2,1,0:T(8,128)} %get-tuple-element.36), channel_id=1, source_target_pairs={{0,30},{2,0},{4,2},{6,4},{8,6},{10,8},{12,10},{14,12},{16,14},{18,... | collective-permute-start | bytes 1572872 | tf_op jit(solution)/shard_map/ppermute | solution.py:619
  53.9 0.0 collective-permute-done.4.refs_5_
  53.9 0.0 collective-permute-done.3.refs_1_
  53.9 6.3 %middle_sums.3 = f32[32,24,256]{2,1,0:T(8,128)} custom-call(f32[32,27]{1,0:T(8,128)} %weight.5, f32[32,32]{1,0:T(8,128)} %point.5, f32[26,32,256]{2,1,0:T(8,128)S(1)} %collective-permute-done.refs_0_, f32[24,32,256]{2,1,0:T(8,128)} %collective-permute-done.3.refs_1_, f32[26,32,256]{2,1,0:T(8,128)} %get-tuple-element.27.refs_1_.refs_2_, ...), custom_call_target="tpu_custom_call" | custom-call | flops 199999995904 | bytes 262144 | tf_op jit(solution)/shard_map/middle_sums/pallas_call | solution.py:555
  60.2 5.8 %inverse_modes.1 = (f32[8,4,64,256]{3,2,1,0:T(8,128)}, f32[8,4,16,256]{3,2,1,0:T(8,128)S(1)}) custom-call(f32[16,16,128]{2,1,0:T(8,128)S(1)} %bitcast.14, f32[32]{0:T(128)} %bias.1, bf16[2,128,256]{2,1,0:T(8,128)(2,1)} %constant.32.clone.x_top, bf16[2,128,256]{2,1,0:T(8,128)(2,1)} %constant.33.clone.x_rest, bf16[2,64,32]{2,1,0:T(8,128)(2,1)} %constant.34.clone.y_top, ...), custom_call_target="tpu_custom_call" | custom-call | flops 100000000 | bytes 262144 | tf_op jit(solution)/shard_map/inverse_modes/pallas_call | solution.py:453
  66.0 0.0 collective-permute-done.5.low
  66.0 0.0 collective-permute-done.6.high
  66.0 2.4 %finished_rows.1 = f32[32,64,256]{2,1,0:T(8,128)} custom-call(f32[32,64,256]{2,1,0:T(8,128)} %bitcast.21, f32[32,16,256]{2,1,0:T(8,128)S(1)} %bitcast.15, f32[32,16,256]{2,1,0:T(8,128)} %collective-permute-done.5.low, f32[32,16,256]{2,1,0:T(8,128)} %collective-permute-done.6.high), custom_call_target="tpu_custom_call", output_to_operand_aliasing={{}: (0, {})} | custom-call | flops 100000000 | bytes 262144 | tf_op jit(solution)/shard_map/finished_rows/pallas_call | solution.py:478
Async XLA Ops:
  2.8 15.4 %copy-start = (f32[2,32,256]{2,1,0:T(8,128)S(1)}, f32[2,32,256]{2,1,0:T(8,128)}, u32[]{:S(2)}) copy-start(f32[2,32,256]{2,1,0:T(8,128)} %get-tuple-element.24) | copy-start | bytes 196612
  2.8 29.2 %collective-permute-start.1 = (f32[26,32,256]{2,1,0:T(8,128)}, f32[26,32,256]{2,1,0:T(8,128)S(1)}, u32[]{:S(2)}, u32[]{:S(2)}) collective-permute-start(f32[26,32,256]{2,1,0:T(8,128)} %get-tuple-element.27.refs_1_.refs_2_), channel_id=1, source_target_pairs={{0,30},{2,0},{4,2},{6,4},{8,6},{10,8},{12,10},{14,12},{16,14},{18,... | collective-permute-start | bytes 2555912 | tf_op jit(solution)/shard_map/ppermute | solution.py:619
  8.3 23.7 %collective-permute-start = (f32[26,32,256]{2,1,0:T(8,128)}, f32[26,32,256]{2,1,0:T(8,128)S(1)}, u32[]{:S(2)}, u32[]{:S(2)}) collective-permute-start(f32[26,32,256]{2,1,0:T(8,128)} %get-tuple-element.27.refs_1_.refs_2_), channel_id=1, source_target_pairs={{0,2},{2,4},{4,6},{6,8},{8,10},{10,12},{12,14},{14,16},{16,18},{18... | collective-permute-start | bytes 2555912 | tf_op jit(solution)/shard_map/ppermute | solution.py:618
  12.4 15.3 %all-to-all-start = ((f32[32,8,128]{2,1,0:T(8,128)}), f32[32,8,128]{2,1,0:T(8,128)S(1)}, u32[]{:S(2)}, u32[]{:S(2)}) async-start(f32[32,8,128]{2,1,0:T(8,128)} %bitcast.23), calls=%async_computation | async-start | bytes 262144 | tf_op jit(solution)/shard_map/all_to_all | solution.py:648
  18.2 5.1 %collective-permute-start.2 = (f32[2,32,256]{2,1,0:T(8,128)S(1)}, f32[2,32,256]{2,1,0:T(8,128)S(1)}, u32[]{:S(2)}, u32[]{:S(2)}) collective-permute-start(f32[2,32,256]{2,1,0:T(8,128)S(1)} %copy-done), channel_id=1, source_target_pairs={{0,1},{1,0},{2,3},{3,2},{4,5},{5,4},{6,7},{7,6},{8,9},{9,8},{10,11... | collective-permute-start | bytes 196616 | tf_op jit(solution)/shard_map/ppermute | solution.py:634
  27.7 26.2 %collective-permute-start.4 = (f32[24,32,256]{2,1,0:T(8,128)}, f32[24,32,256]{2,1,0:T(8,128)}, u32[]{:S(2)}, u32[]{:S(2)}) collective-permute-start(f32[24,32,256]{2,1,0:T(8,128)} %get-tuple-element.32.refs_3_), channel_id=1, source_target_pairs={{0,30},{2,0},{4,2},{6,4},{8,6},{10,8},{12,10},{14,12},{16,14},{18,... | collective-permute-start | bytes 2359304 | tf_op jit(solution)/shard_map/ppermute | solution.py:619
  32.0 21.9 %collective-permute-start.3 = (f32[24,32,256]{2,1,0:T(8,128)}, f32[24,32,256]{2,1,0:T(8,128)}, u32[]{:S(2)}, u32[]{:S(2)}) collective-permute-start(f32[24,32,256]{2,1,0:T(8,128)} %get-tuple-element.32.refs_3_), channel_id=1, source_target_pairs={{0,2},{2,4},{4,6},{6,8},{8,10},{10,12},{12,14},{14,16},{16,18},{18... | collective-permute-start | bytes 2359304 | tf_op jit(solution)/shard_map/ppermute | solution.py:618
  34.7 14.2 %all-to-all-start.1 = ((f32[32,8,128]{2,1,0:T(8,128)}), f32[32,8,128]{2,1,0:T(8,128)S(1)}, u32[]{:S(2)}, u32[]{:S(2)}) async-start(f32[32,8,128]{2,1,0:T(8,128)} %bitcast.25), calls=%async_computation.1 | async-start | bytes 262144 | tf_op jit(solution)/shard_map/all_to_all | solution.py:653
  48.9 17.1 %collective-permute-start.5 = (f32[32,16,256]{2,1,0:T(8,128)}, f32[32,16,256]{2,1,0:T(8,128)}, u32[]{:S(2)}, u32[]{:S(2)}) collective-permute-start(f32[32,16,256]{2,1,0:T(8,128)} %get-tuple-element.35), channel_id=1, source_target_pairs={{0,2},{2,4},{4,6},{6,8},{8,10},{10,12},{12,14},{14,16},{16,18},{18... | collective-permute-start | bytes 1572872 | tf_op jit(solution)/shard_map/ppermute | solution.py:618
  49.2 16.8 %collective-permute-start.6 = (f32[32,16,256]{2,1,0:T(8,128)}, f32[32,16,256]{2,1,0:T(8,128)}, u32[]{:S(2)}, u32[]{:S(2)}) collective-permute-start(f32[32,16,256]{2,1,0:T(8,128)} %get-tuple-element.36), channel_id=1, source_target_pairs={{0,30},{2,0},{4,2},{6,4},{8,6},{10,8},{12,10},{14,12},{16,14},{18,... | collective-permute-start | bytes 1572872 | tf_op jit(solution)/shard_map/ppermute | solution.py:619

commit v10 on v8

--- a/solution.py
+++ b/solution.py
@@ -183,38 +183,31 @@
     )
 
 
-def turn(turned, at, value):
-    turned[0, at] = pltpu.roll(value, 1, 1)
-    turned[1, at] = value
-    turned[2, at] = pltpu.roll(value, NX - 1, 1)
-
-
-def tap_sums(turned, depth, gains, runs, offsets, fresh):
+def tap_sums(load, uses, gains, depth, runs):
     def some(i, _):
         chans = pl.ds(pl.multiple_of(i * 8, 8), 8)
-        gain = {k: gains[k, chans, :] for a in offsets for k in range(9 * a, 9 * a + 9)}
-        for h in range(2):
-            lanes = pl.ds(128 * h, 128)
-            for first, to, rows in runs:
-                sums = {}
-                for r in range(rows + 2):
-                    values = [turned[e, first + r, chans, lanes] for e in range(3)]
+        wanted = sorted({a for use in uses for a, _ in use})
+        gain = {k: gains[k, chans, :] for a in wanted for k in range(9 * a, 9 * a + 9)}
+        for first, to, rows in runs:
+            sums = {}
+            for r in range(rows + 2):
+                for s, use in enumerate(uses):
+                    value = load(s, first + r, chans)
+                    turned = (pltpu.roll(value, 1, 1), value, pltpu.roll(value, NX - 1, 1))
                     for b in range(3):
                         o = r - b
                         if o < 0 or o >= rows:
                             continue
-                        for k, a in enumerate(offsets):
+                        for a, k in use:
                             for e in range(3):
-                                term = gain[a * 9 + b * 3 + e] * values[e]
-                                if (o, k) in sums:
-                                    sums[o, k] = sums[o, k] + term
-                                elif fresh:
-                                    sums[o, k] = term
-                                else:
-                                    sums[o, k] = depth[k, to + o, chans, lanes] + term
-                    if r >= 2:
-                        for k in range(len(offsets)):
-                            depth[k, to + r - 2, chans, lanes] = sums.pop((r - 2, k))
+                                for h in range(2):
+                                    term = gain[a * 9 + b * 3 + e] * turned[e][:, 128 * h : 128 * h + 128]
+                                    place = (o, k, h)
+                                    sums[place] = sums[place] + term if place in sums else term
+                if r >= 2:
+                    for k in sorted({k for use in uses for _, k in use}):
+                        for h in range(2):
+                            depth[k, to + r - 2, chans, pl.ds(128 * h, 128)] = sums.pop((r - 2, k, h))
         return 0
 
     lax.fori_loop(0, CH // 8, some, 0)
@@ -225,21 +218,19 @@
     return dot3(mix, parts(tile)).reshape(CH, 8, NX)
 
 
-def pack_kernel(plan, field, packed, later, edges, taken, rows, ends, sem_in, sem_out):
-    middle, split = plan
+def pack_kernel(tiles, field, packed, edges, taken, rows, ends, sem_in, sem_out):
     last = field.shape[1] // 8 - 1
-    before, after = middle[0] - 1, middle[-1] + 1
-    wanted = [before, *middle, after] + [t for t in (0, last) if t not in (before, after)]
+    before, after = tiles[0] - 1, tiles[-1] + 1
+    wanted = [before, *tiles, after] + [t for t in (0, last) if t not in (before, after)]
     row = fetch_tiles(field, taken, sem_in, wanted)
-    places = [(before, 7), *[(t, r) for t in middle for r in range(8)], (after, 0)]
-    copies = []
-    for i, place in enumerate(places):
-        rows[i] = row(*place)
-        if i + 1 == split:
-            copies.append(pltpu.make_async_copy(rows.at[pl.ds(0, split)], packed, sem_out.at[0]))
-            copies[-1].start()
-    copies.append(pltpu.make_async_copy(rows.at[pl.ds(split, len(places) - split)], later, sem_out.at[1]))
-    copies[-1].start()
+    places = [(before, 7), *[(t, r) for t in tiles for r in range(8)], (after, 0)]
+    copies, cuts = [], (0, len(places) // 2, len(places))
+    for k in range(2):
+        for i in range(cuts[k], cuts[k + 1]):
+            rows[i] = row(*places[i])
+        some = pl.ds(cuts[k], cuts[k + 1] - cuts[k])
+        copies.append(pltpu.make_async_copy(rows.at[some], packed.at[some], sem_out.at[k]))
+        copies[-1].start()
     ends[0] = row(last, 7)
     ends[1] = row(0, 0)
     copies.append(pltpu.make_async_copy(ends, edges, sem_out.at[2]))
@@ -248,30 +239,36 @@
         copy.wait()
 
 
-def own_kernel(plan, weight, point, field, halo, *refs):
-    upper, lower = plan
-    outs, refs = refs[:3], refs[3:]
-    taken, halo_rows, weights, points, sent, turned, depth, gains, sem_in, sem_out, sem_few = refs
-    few = [
-        pltpu.make_async_copy(a, b, sem_few.at[i])
-        for i, (a, b) in enumerate(((weight, weights), (point, points), (halo, halo_rows)))
-    ]
+def own_kernel(segments, weight, point, field, *refs):
+    last = field.shape[1] // 8 - 1
+    outer = segments[0][0] == 0
+    few = [(weight, refs[-9]), (point, refs[-8])]
+    if outer:
+        few.append((refs[0], refs[-10]))
+        refs = refs[1:]
+    outs, (taken, halo_rows, weights, points, sent, lined, depth, gains, sem_in, sem_out, sem_few) = (
+        refs[:3],
+        refs[3:],
+    )
+    few = [pltpu.make_async_copy(src, dst, sem_few.at[i]) for i, (src, dst) in enumerate(few)]
+    wanted = sorted({t for tiles in segments for t in (tiles[0] - 1, *tiles, tiles[-1] + 1) if 0 <= t <= last})
+    row = fetch_tiles(field, taken, sem_in, wanted)
     for copy in few:
         copy.start()
-    wanted = [*upper, upper[-1] + 1, lower[0] - 1, *lower]
-    row = fetch_tiles(field, taken, sem_in, wanted)
     for copy in few:
         copy.wait()
     spread_gains(weights, gains, range(3))
     mix = mixing(points[...])
-    rows, others = 8 * len(upper), 8 * len(lower)
-    for i, place in enumerate([None, *[(t, r) for t in upper for r in range(8)], (upper[-1] + 1, 0)]):
-        turn(turned, i, halo_rows[0] if place is None else row(*place))
-    for i, place in enumerate([(lower[0] - 1, 7), *[(t, r) for t in lower for r in range(8)], None]):
-        turn(turned, rows + 2 + i, halo_rows[1] if place is None else row(*place))
-    tap_sums(turned, depth, gains, [(0, 0, rows), (rows + 2, rows, others)], range(3), True)
+    runs, at, done = [], 0, 0
+    for tiles in segments:
+        places = [(tiles[0] - 1, 7), *[(t, r) for t in tiles for r in range(8)], (tiles[-1] + 1, 0)]
+        for i, (t, r) in enumerate(places):
+            lined[at + i] = halo_rows[0] if t < 0 else halo_rows[1] if t > last else row(t, r)
+        runs.append((at, done, 8 * len(tiles)))
+        at, done = at + len(places), done + 8 * len(tiles)
+    tap_sums(lambda s, r, c: lined[r, c, :], [[(a, a) for a in range(3)]], gains, depth, runs)
     copies = []
-    for t in range((rows + others) // 8):
+    for t in range(done // 8):
         for k, out in enumerate(outs):
             sent[k, t] = mix_tile(mix, depth, k, t)
             copies.append(
@@ -282,39 +279,23 @@
         copy.wait()
 
 
-def middle_kernel(weight, point, *refs):
-    planes, out = refs[:6], refs[6]
-    taken, weights, points, sent, turned, depth, gains, sem_in, sem_out, sem_few = refs[7:]
-    split = planes[0].shape[0]
-    few = [
-        pltpu.make_async_copy(a, b, sem_few.at[i])
-        for i, (a, b) in enumerate(((weight, weights), (point, points)))
+def middle_kernel(weight, point, low, own, high, out, taken, weights, points, sent, depth, gains, sem_in, sem_out):
+    copies = [
+        pltpu.make_async_copy(src, dst, sem_in.at[i])
+        for i, (src, dst) in enumerate(
+            ((weight, weights), (point, points), (low, taken.at[0]), (own, taken.at[1]), (high, taken.at[2]))
+        )
     ]
-    arrivals = [
-        [
-            pltpu.make_async_copy(planes[2 * a], taken.at[a, pl.ds(0, split)], sem_in.at[a, 0]),
-            pltpu.make_async_copy(
-                planes[2 * a + 1], taken.at[a, pl.ds(split, taken.shape[1] - split)], sem_in.at[a, 1]
-            ),
-        ]
-        for a in range(3)
-    ]
-    for a in (1, 0, 2):
-        for copy in arrivals[a]:
-            copy.start()
-    for copy in few:
+    for copy in copies:
         copy.start()
-    for copy in few:
+    for copy in copies[:2]:
         copy.wait()
     spread_gains(weights, gains, range(3))
     mix = mixing(points[...])
+    for copy in copies[2:]:
+        copy.wait()
     rows = out.shape[1]
-    for a in (1, 0, 2):
-        for copy in arrivals[a]:
-            copy.wait()
-        for r in range(rows + 2):
-            turn(turned, r, taken[a, r])
-        tap_sums(turned, depth, gains, [(0, 0, rows)], [a], a == 1)
+    tap_sums(lambda s, r, c: taken[s, r, c, :], [[(a, 0)] for a in range(3)], gains, depth, [(0, 0, rows)])
     copies = []
     for t in range(rows // 8):
         sent[t] = mix_tile(mix, depth, 0, t)
@@ -336,7 +317,7 @@
     return value * jnp.where(value < 0.0, tail, 1.0 - tail)
 
 
-def inverse_kernel(upper, modes, bias, x_top, x_rest, y_top, y_rest, middle, own, out, base, columns):
+def inverse_kernel(upper, modes, bias, x_top, x_rest, y_top, y_rest, own, middle, second, low, high, out, base, columns):
     q = pl.program_id(0)
     groups, _, y_local, _ = out.shape
 
@@ -354,12 +335,14 @@
 
     h, p = q // 2, q % 2
     rows = dot3((columns[h, 0], columns[h, 1]), (x_top[p], x_rest[p]))
-    start, stop = upper, upper + middle.shape[2]
+    turn = upper + middle.shape[2]
+    stop = turn + second.shape[2]
     for g in range(groups):
         plane = rows[g * y_local : (g + 1) * y_local] + bias[4 * g + q]
-        out[g, 0, start:stop] = gelu(plane[start:stop] + middle[g, 0])
-        base[g, 0, :start] = plane[:start] + own[g, 0, :start]
-        base[g, 0, start:] = plane[stop:] + own[g, 0, start:]
+        base[g, 0, :upper] = plane[:upper] + own[g, 0, :upper]
+        out[g, 0, upper:turn] = gelu(plane[upper:turn] + middle[g, 0])
+        out[g, 0, turn:stop] = gelu(plane[turn:stop] + (second[g, 0] + (low[g, 0] + high[g, 0])))
+        base[g, 0, upper:] = plane[stop:] + own[g, 0, upper:]
 
 
 def finish_kernel(upper, _, base, low, high, out, held, sent, sem_in, sem_out):
@@ -439,10 +422,10 @@
     )(arrived, *in_hbm(gains, *fwd, *inv))
 
 
-def inverse_call(modes, bias, middle, own, upper, y_local, gy, scale):
+def inverse_call(modes, bias, own, middle, second, pair, upper, y_local, gy, scale):
     tables = [*halves(x_table(True, scale)), *halves(y_table(y_local, gy, True))]
     some = lambda rows: pl.BlockSpec((CH // 4, 1, rows, NX), lambda i: (0, i, 0, 0))
-    planes = in_hbm(by_four(middle), by_four(own))
+    planes = [*in_hbm(*map(by_four, (own, middle, second))), *map(by_four, pair)]
     rim = own.shape[1]
     result, base = pl.pallas_call(
         functools.partial(inverse_kernel, upper),
@@ -460,7 +443,7 @@
         out_specs=[some(y_local), some(rim)],
         scratch_shapes=[pltpu.VMEM((2, 2, CH // 4 * y_local, 128), BF)],
         compiler_params=params(),
-        cost_estimate=cost(10**8, 2**18),
+        cost_estimate=cost(2 * 10**11, 2**18),
         name="inverse_modes",
     )(modes, *in_hbm(bias, *tables), *planes)
     return result.reshape(CH, y_local, NX), base.reshape(CH, rim, NX)
@@ -487,20 +470,15 @@
     )(result, base, low, high)
 
 
-def pack_call(field, middle, first):
-    count = 8 * len(middle) + 2
-    split = 8 * first + 2
-    fetched = len(middle) + 4
+def pack_call(field, tiles):
+    count = 8 * len(tiles) + 2
+    fetched = len(tiles) + 4
     hbm = pl.BlockSpec(memory_space=pltpu.HBM)
     return pl.pallas_call(
-        functools.partial(pack_kernel, (middle, split)),
-        out_shape=[
-            pltpu.HBM((split, CH, NX), F32),
-            pltpu.HBM((count - split, CH, NX), F32),
-            pltpu.HBM((2, CH, NX), F32),
-        ],
+        functools.partial(pack_kernel, tiles),
+        out_shape=[pltpu.HBM((count, CH, NX), F32), pltpu.HBM((2, CH, NX), F32)],
         in_specs=[hbm],
-        out_specs=[hbm] * 3,
+        out_specs=[hbm] * 2,
         scratch_shapes=[
             pltpu.VMEM((fetched, 2, CH, 8, 128), F32),
             pltpu.VMEM((count, CH, NX), F32),
@@ -514,59 +492,56 @@
     )(*in_hbm(field))
 
 
-def own_call(field, halo, weight, point, upper, lower):
-    tiles = len(upper) + len(lower)
-    rows = 8 * tiles
+def own_call(field, weight, point, segments, halo=()):
+    tiles = sum(map(len, segments))
+    rows, fetched = 8 * tiles, tiles + 2 * len(segments)
     hbm = pl.BlockSpec(memory_space=pltpu.HBM)
-    shapes = [pltpu.HBM((CH, rows, NX), F32)] * 3
     return pl.pallas_call(
-        functools.partial(own_kernel, (upper, lower)),
-        out_shape=shapes,
-        in_specs=[hbm] * 3 + [pl.BlockSpec(memory_space=pl.ANY)],
-        out_specs=[hbm] * len(shapes),
+        functools.partial(own_kernel, segments),
+        out_shape=[pltpu.HBM((CH, rows, NX), F32)] * 3,
+        in_specs=[hbm] * 3 + [pl.BlockSpec(memory_space=pl.ANY)] * len(halo),
+        out_specs=[hbm] * 3,
         scratch_shapes=[
-            pltpu.VMEM((tiles + 2, 2, CH, 8, 128), F32),
+            pltpu.VMEM((fetched, 2, CH, 8, 128), F32),
             pltpu.VMEM((2, CH, NX), F32),
             pltpu.VMEM((CH, 27), F32),
             pltpu.VMEM((CH, CH), F32),
             pltpu.VMEM((3, tiles, CH, 8, NX), F32),
-            pltpu.VMEM((3, rows + 4, CH, NX), F32),
+            pltpu.VMEM((rows + 2 * len(segments), CH, NX), F32),
             pltpu.VMEM((3, rows, CH, NX), F32),
             pltpu.VMEM((27, CH, 128), F32),
-            pltpu.SemaphoreType.DMA((tiles + 2, 2)),
+            pltpu.SemaphoreType.DMA((fetched, 2)),
             pltpu.SemaphoreType.DMA((3, tiles)),
             pltpu.SemaphoreType.DMA((3,)),
         ],
         compiler_params=params(),
         cost_estimate=cost(10**8, 2**18),
         name="own_sums",
-    )(*in_hbm(weight, point, field), halo)
+    )(*in_hbm(weight, point, field), *halo)
 
 
 def middle_call(weight, point, low, own, high):
-    rows = own[0].shape[0] + own[1].shape[0] - 2
+    rows = own.shape[0] - 2
     hbm = pl.BlockSpec(memory_space=pltpu.HBM)
     return pl.pallas_call(
         middle_kernel,
         out_shape=pltpu.HBM((CH, rows, NX), F32),
-        in_specs=[hbm] * 2 + [pl.BlockSpec(memory_space=pl.ANY)] * 6,
+        in_specs=[hbm] * 2 + [pl.BlockSpec(memory_space=pl.ANY)] * 3,
         out_specs=hbm,
         scratch_shapes=[
             pltpu.VMEM((3, rows + 2, CH, NX), F32),
             pltpu.VMEM((CH, 27), F32),
             pltpu.VMEM((CH, CH), F32),
             pltpu.VMEM((rows // 8, CH, 8, NX), F32),
-            pltpu.VMEM((3, rows + 2, CH, NX), F32),
             pltpu.VMEM((1, rows, CH, NX), F32),
             pltpu.VMEM((27, CH, 128), F32),
-            pltpu.SemaphoreType.DMA((3, 2)),
+            pltpu.SemaphoreType.DMA((5,)),
             pltpu.SemaphoreType.DMA((rows // 8,)),
-            pltpu.SemaphoreType.DMA((2,)),
         ],
         compiler_params=params(),
-        cost_estimate=cost(2 * 10**11, 2**18),
+        cost_estimate=cost(10**8, 2**18),
         name="middle_sums",
-    )(*in_hbm(weight, point), *low, *in_hbm(*own), *high)
+    )(*in_hbm(weight, point), low, *in_hbm(own), high)
 
 
 def general_filter(coarse, gains, gz, gy, scale):
@@ -616,11 +591,11 @@
     def after(value, *others):
         return lax.optimization_barrier((value, *others))[0]
 
-    tiles = y_local // 8
-    upper = (0,)
-    lower = tuple(range(tiles - max(1, tiles // 4), tiles))
-    middle = tuple(range(1, lower[0]))
-    packed, later, edges = pack_call(field, middle, (len(middle) + 1) // 2)
+    last = y_local // 8 - 1
+    cut = 1 + last // 2
+    first_tiles, second_tiles = tuple(range(1, cut)), tuple(range(cut, last))
+    sums = functools.partial(own_call, weight=depth_weight, point=point_weight)
+    packed, edges = pack_call(field, first_tiles)
     first_low, first_high = to_neighbours(packed, packed)
     if gy == 2:
         halo = lax.ppermute(edges, "gy", ring("gy", gy, 1))
@@ -634,29 +609,26 @@
     j_own, n_own = spectral_filter.shape[2], spectral_filter.shape[3]
     whole_tiles = j_own == 8 and n_own == 2 * MX
     coarse = forward_call(after(field, packed), gy, whole_tiles)
-    down, own, up = own_call(after(field, coarse), halo, depth_weight, point_weight, upper, lower)
+    down, second, up = sums(after(field, coarse), segments=(second_tiles,))
     if whole_tiles:
         both = ("gz", "gy")
         got = lax.all_to_all(coarse, both, split_axis=0, concat_axis=0, tiled=True)
-        sent = after(later, got)
-        later_low, later_high = to_neighbours(sent, sent)
-        gains = after(spectral_filter, first_low, first_high, own)
-        filtered = filter_call(got, gains, gz, gy, forward_scale)
-        back = lax.all_to_all(filtered, both, split_axis=0, concat_axis=0, tiled=True)
+        pair = to_neighbours(after(down, got), after(up, got))
+        gains = after(spectral_filter, first_low, first_high, second)
+        mark = filter_call(got, gains, gz, gy, forward_scale)
+        back = lax.all_to_all(mark, both, split_axis=0, concat_axis=0, tiled=True)
         back = back.reshape(CH // 2, MY, 4 * MX)
     else:
-        later_low, later_high = to_neighbours(later, later)
-        back = general_filter(coarse, spectral_filter, gz, gy, forward_scale)
-    low, high = to_neighbours(after(down, back), after(up, back))
-    mixed = middle_call(
-        depth_weight,
-        point_weight,
-        (first_low, later_low),
-        (after(packed, back), later),
-        (first_high, later_high),
+        pair = to_neighbours(down, up)
+        mark = back = general_filter(coarse, spectral_filter, gz, gy, forward_scale)
+    mixed = middle_call(depth_weight, point_weight, first_low, after(packed, mark), first_high)
+    down, own, up = sums(after(field, mark), segments=((0,), (last,)), halo=(halo,))
+    down, up, _, _ = lax.optimization_barrier((down, up, back, mixed))
+    outer_pair = to_neighbours(down, up)
+    result, base = inverse_call(
+        back, bias_vector, own, mixed, second, pair, 8, y_local, gy, inverse_scale
     )
-    result, base = inverse_call(back, bias_vector, mixed, own, 8, y_local, gy, inverse_scale)
-    result = finish_call(result, base, low, high, 1)
+    result = finish_call(result, base, *outer_pair, 1)
     return result.reshape(CH, 1, y_local, NX)
 
 

time: 71.9 us -> 69 us (0.960)
  blocking collectives: 15.9 us -> 0 us
  starting transfers between devices: 15.5 us -> 24.6 us
  waiting for transfers between devices: 8.63 us -> 11.4 us
  Pallas kernels: 31.3 us -> 32.4 us
    all_to_all x1 -> x0, blocking collectives: 15.9 us -> none  [body(): lax.all_to_all(filtered, both, split_axis=0, concat_axis=0, tiled=True)]
    all_to_all x0 -> x1, starting transfers between devices: none -> 8.54 us  [body(): back = lax.all_to_all(mark, both, split_axis=0, concat_axis=0, tiled=True)]
    pallas_call x2 -> x3, Pallas kernels: 8.06 us -> 12.7 us  [the longest x2 10.4 us: own_call(): pl.pallas_call(functools.partial(own_kernel, segments), out_shape=[pltpu....]
    pallas_call x1, Pallas kernels: 8.32 us -> 4.48 us  [middle_call(): pl.pallas_call(middle_kernel, out_shape=pltpu.HBM((CH, rows, NX), F32), i...]
    all_to_all x1, waiting for transfers between devices: 0.01 us -> 2.95 us  [body(): got = lax.all_to_all(coarse, both, split_axis=0, concat_axis=0, tiled=True)]
    ppermute x1, waiting for transfers between devices: 2.71 us -> 0.01 us  [body(): halo = lax.ppermute(edges, 'gy', ring('gy', gy, 1))]
    ppermute x3, waiting for transfers between devices: 3.43 us -> 5.92 us  [to_neighbours(): lax.ppermute(down, 'gz', ring('gz', gz, 1))]
    ppermute x3, starting transfers between devices: 4 us -> 5.52 us  [to_neighbours(): lax.ppermute(down, 'gz', ring('gz', gz, 1))]
  transfers between devices with their start and end apart: 8 -> 9, of which waited for: 3 -> 3; matrix products, arithmetic and copies ran while one was open for 0% -> 0% of each run, Pallas kernels for 36% -> 41%
where the time goes in v10:
time: 69 us; the launch traced here: 68.5 us
  Pallas kernels  32.4 us (47%)
  starting transfers between devices  24.6 us (36%)
  waiting for transfers between devices  11.4 us (17%)
    pallas_call x2, Pallas kernels, own_call(): pl.pallas_call(functools.partial(own_kernel, segments), out_shape=[pltpu....  10.4 us
    all_to_all x1, starting transfers between devices, body(): back = lax.all_to_all(mark, both, split_axis=0, concat_axis=0, tiled=True)  8.54 us
    all_to_all x1, starting transfers between devices, body(): got = lax.all_to_all(coarse, both, split_axis=0, concat_axis=0, tiled=True)  8.29 us
    pallas_call x1, Pallas kernels, inverse_call(): pl.pallas_call(functools.partial(inverse_kernel, upper), out_shape=[jax.S...  6.13 us
    ppermute x3, waiting for transfers between devices, to_neighbours(): lax.ppermute(down, 'gz', ring('gz', gz, 1))  5.92 us
    ppermute x3, starting transfers between devices, to_neighbours(): lax.ppermute(down, 'gz', ring('gz', gz, 1))  5.52 us
    pallas_call x1, Pallas kernels, middle_call(): pl.pallas_call(middle_kernel, out_shape=pltpu.HBM((CH, rows, NX), F32), i...  4.48 us
    pallas_call x1, Pallas kernels, forward_call(): pl.pallas_call(forward_kernel, out_shape=(pltpu.HBM if pinned else jax.Sh...  4.12 us
  transfers between devices with their start and end apart: 9, of which 3 were waited for; matrix products, arithmetic and copies ran while one was open for 0% of the time, Pallas kernels for 41%

profile of v10, /device:TPU:1, one launch (start us, length us, event | category | flops | bytes accessed | tf_op | source)
XLA Modules:
  0.0 68.5 jit_solution(11118434746596678446)
XLA Ops:
  0.0 2.3 %packed_rows.1 = (f32[26,32,256]{2,1,0:T(8,128)}, f32[2,32,256]{2,1,0:T(8,128)}) custom-call(f32[32,64,256]{2,1,0:T(8,128)} %bitcast.19), custom_call_target="tpu_custom_call" | custom-call | flops 100000000 | bytes 262144 | tf_op jit(solution)/shard_map/packed_rows/pallas_call | solution.py:477
  2.3 0.1 collective-permute-start.1
  2.4 2.6 %collective-permute-start = (f32[26,32,256]{2,1,0:T(8,128)}, f32[26,32,256]{2,1,0:T(8,128)S(1)}, u32[]{:S(2)}, u32[]{:S(2)}) collective-permute-start(f32[26,32,256]{2,1,0:T(8,128)} %get-tuple-element.32.own), channel_id=1, source_target_pairs={{0,2},{2,4},{4,6},{6,8},{8,10},{10,12},{12,14},{14,16},{16,18},{18... | collective-permute-start | bytes 2555912 | tf_op jit(solution)/shard_map/ppermute | solution.py:587
  5.1 4.1 %forward_modes.1 = f32[256,128]{1,0:T(8,128)} custom-call(f32[8,4,64,256]{3,2,1,0:T(8,128)} %bitcast.20, bf16[2,256,128]{2,1,0:T(8,128)(2,1)} %constant.24.clone.x_top, bf16[2,256,128]{2,1,0:T(8,128)(2,1)} %constant.25.clone.x_rest, bf16[2,32,64]{2,1,0:T(8,128)(2,1)} %constant.26.clone.y_top, bf16[2,32,64]{2,1,0:T(8,128)(2,1)} %constant.27.clone.y_rest), custom_call_target="tpu_custom_call" | custom-call | flops 100000000 | bytes 262144 | tf_op jit(solution)/shard_map/forward_modes/pallas_call | solution.py:397
  9.2 8.3 %all-to-all-start = ((f32[32,8,128]{2,1,0:T(8,128)}), f32[32,8,128]{2,1,0:T(8,128)S(1)}, u32[]{:S(2)}, u32[]{:S(2)}) async-start(f32[32,8,128]{2,1,0:T(8,128)} %bitcast.25), calls=%async_computation | async-start | bytes 262144 | tf_op jit(solution)/shard_map/all_to_all | solution.py:615
  17.5 5.6 %own_sums.2 = (f32[32,24,256]{2,1,0:T(8,128)}, f32[32,24,256]{2,1,0:T(8,128)}, f32[32,24,256]{2,1,0:T(8,128)}) custom-call(f32[32,27]{1,0:T(8,128)} %weight.5, f32[32,32]{1,0:T(8,128)} %point.5, f32[32,64,256]{2,1,0:T(8,128)} %bitcast.21), custom_call_target="tpu_custom_call" | custom-call | flops 100000000 | bytes 262144 | tf_op jit(solution)/shard_map/own_sums/pallas_call | solution.py:499
  23.1 2.9 %all-to-all-done = f32[32,8,128]{2,1,0:T(8,128)S(1)} async-done(((f32[32,8,128]{2,1,0:T(8,128)}), f32[32,8,128]{2,1,0:T(8,128)S(1)}, u32[]{:S(2)}, u32[]{:S(2)}) %all-to-all-start) | async-done | bytes 131104 | tf_op jit(solution)/shard_map/all_to_all | solution.py:615
  26.1 0.7 %collective-permute-start.4 = (f32[32,24,256]{2,1,0:T(8,128)}, f32[32,24,256]{2,1,0:T(8,128)}, u32[]{:S(2)}, u32[]{:S(2)}) collective-permute-start(f32[32,24,256]{2,1,0:T(8,128)} %get-tuple-element.36), channel_id=1, source_target_pairs={{0,30},{2,0},{4,2},{6,4},{8,6},{10,8},{12,10},{14,12},{16,14},{18,... | collective-permute-start | bytes 2359304 | tf_op jit(solution)/shard_map/ppermute | solution.py:588
  26.8 1.1 %collective-permute-start.3 = (f32[32,24,256]{2,1,0:T(8,128)}, f32[32,24,256]{2,1,0:T(8,128)}, u32[]{:S(2)}, u32[]{:S(2)}) collective-permute-start(f32[32,24,256]{2,1,0:T(8,128)} %get-tuple-element.34), channel_id=1, source_target_pairs={{0,2},{2,4},{4,6},{6,8},{8,10},{10,12},{12,14},{14,16},{16,18},{18... | collective-permute-start | bytes 2359304 | tf_op jit(solution)/shard_map/ppermute | solution.py:587
  27.9 0.0 collective-permute-done.1.high
  27.9 0.0 collective-permute-done.low
  27.9 0.0 copy-start
  27.9 2.7 %filter_modes.1 = f32[256,128]{1,0:T(8,128)} custom-call(f32[256,128]{1,0:T(8,128)S(1)} %bitcast.18, f32[2,16,8,64]{3,2,1,0:T(8,128)} %gains, bf16[256,256]{1,0:T(8,128)(2,1)} %constant.28.clone.f_top, bf16[256,256]{1,0:T(8,128)(2,1)} %constant.29.clone.f_rest, bf16[512,128]{1,0:T(8,128)(2,1)} %constant.30.clone.i_top, bf16[512,128]{1,0:T(8,128)(2,1)} %constant.31.clone.i_rest), custom_call_target="tpu_custom_call" | custom-call | flops 199999995904 | bytes 262144 | tf_op jit(solution)/shard_map/filter_modes/pallas_call | solution.py:416
  30.6 8.5 %all-to-all-start.1 = ((f32[32,8,128]{2,1,0:T(8,128)}), f32[32,8,128]{2,1,0:T(8,128)S(1)}, u32[]{:S(2)}, u32[]{:S(2)}) async-start(f32[32,8,128]{2,1,0:T(8,128)} %bitcast.26), calls=%async_computation.1 | async-start | bytes 262144 | tf_op jit(solution)/shard_map/all_to_all | solution.py:619
  39.2 0.0 copy-done
  39.2 1.5 %collective-permute-start.2 = (f32[2,32,256]{2,1,0:T(8,128)S(1)}, f32[2,32,256]{2,1,0:T(8,128)S(1)}, u32[]{:S(2)}, u32[]{:S(2)}) collective-permute-start(f32[2,32,256]{2,1,0:T(8,128)S(1)} %copy-done), channel_id=1, source_target_pairs={{0,1},{1,0},{2,3},{3,2},{4,5},{5,4},{6,7},{7,6},{8,9},{9,8},{10,11... | collective-permute-start | bytes 196616 | tf_op jit(solution)/shard_map/ppermute | solution.py:601
  40.6 4.5 %middle_sums.1 = f32[32,24,256]{2,1,0:T(8,128)} custom-call(f32[32,27]{1,0:T(8,128)} %weight.5, f32[32,32]{1,0:T(8,128)} %point.5, f32[26,32,256]{2,1,0:T(8,128)S(1)} %collective-permute-done.low, f32[26,32,256]{2,1,0:T(8,128)} %get-tuple-element.32.own, f32[26,32,256]{2,1,0:T(8,128)S(1)} %collective-permute-done.1.high), custom_call_target="tpu_custom_call" | custom-call | flops 100000000 | bytes 262144 | tf_op jit(solution)/shard_map/middle_sums/pallas_call | solution.py:526
  45.1 0.0 collective-permute-done.2.refs_0_
  45.1 4.8 %own_sums.3 = (f32[32,16,256]{2,1,0:T(8,128)}, f32[32,16,256]{2,1,0:T(8,128)}, f32[32,16,256]{2,1,0:T(8,128)}) custom-call(f32[32,27]{1,0:T(8,128)} %weight.5, f32[32,32]{1,0:T(8,128)} %point.5, f32[32,64,256]{2,1,0:T(8,128)} %bitcast.22, f32[2,32,256]{2,1,0:T(8,128)S(1)} %collective-permute-done.2.refs_0_), custom_call_target="tpu_custom_call" | custom-call | flops 100000000 | bytes 262144 | tf_op jit(solution)/shard_map/own_sums/pallas_call | solution.py:499
  49.9 0.0 all-to-all-done.1
  49.9 1.8 %collective-permute-start.5 = (f32[32,16,256]{2,1,0:T(8,128)}, f32[32,16,256]{2,1,0:T(8,128)}, u32[]{:S(2)}, u32[]{:S(2)}) collective-permute-start(f32[32,16,256]{2,1,0:T(8,128)} %get-tuple-element.41), channel_id=1, source_target_pairs={{0,2},{2,4},{4,6},{6,8},{8,10},{10,12},{12,14},{14,16},{16,18},{18... | collective-permute-start | bytes 1572872 | tf_op jit(solution)/shard_map/ppermute | solution.py:587
  51.6 0.0 collective-permute-start.6
  51.6 0.0 collective-permute-done.4
  51.7 0.0 collective-permute-done.3
  51.7 6.1 %inverse_modes.1 = (f32[8,4,64,256]{3,2,1,0:T(8,128)}, f32[8,4,16,256]{3,2,1,0:T(8,128)S(1)}) custom-call(f32[16,16,128]{2,1,0:T(8,128)S(1)} %bitcast.17, f32[32]{0:T(128)} %bias.1, bf16[2,128,256]{2,1,0:T(8,128)(2,1)} %constant.32.clone.x_top, bf16[2,128,256]{2,1,0:T(8,128)(2,1)} %constant.33.clone.x_rest, bf16[2,64,32]{2,1,0:T(8,128)(2,1)} %constant.34.clone.y_top, ...), custom_call_target="tpu_custom_call" | custom-call | flops 199999995904 | bytes 262144 | tf_op jit(solution)/shard_map/inverse_modes/pallas_call | solution.py:430
  57.8 5.9 %collective-permute-done.5.low = f32[32,16,256]{2,1,0:T(8,128)} collective-permute-done((f32[32,16,256]{2,1,0:T(8,128)}, f32[32,16,256]{2,1,0:T(8,128)}, u32[]{:S(2)}, u32[]{:S(2)}) %collective-permute-start.5) | collective-permute-done | bytes 524320 | tf_op jit(solution)/shard_map/ppermute | solution.py:587
  63.7 2.5 %collective-permute-done.6.high = f32[32,16,256]{2,1,0:T(8,128)} collective-permute-done((f32[32,16,256]{2,1,0:T(8,128)}, f32[32,16,256]{2,1,0:T(8,128)}, u32[]{:S(2)}, u32[]{:S(2)}) %collective-permute-start.6) | collective-permute-done | bytes 524320 | tf_op jit(solution)/shard_map/ppermute | solution.py:588
  66.2 2.3 %finished_rows.1 = f32[32,64,256]{2,1,0:T(8,128)} custom-call(f32[32,64,256]{2,1,0:T(8,128)} %bitcast.23, f32[32,16,256]{2,1,0:T(8,128)S(1)} %bitcast.16, f32[32,16,256]{2,1,0:T(8,128)} %collective-permute-done.5.low, f32[32,16,256]{2,1,0:T(8,128)} %collective-permute-done.6.high), custom_call_target="tpu_custom_call", output_to_operand_aliasing={{}: (0, {})} | custom-call | flops 100000000 | bytes 262144 | tf_op jit(solution)/shard_map/finished_rows/pallas_call | solution.py:455
Async XLA Ops:
  2.3 25.6 %collective-permute-start.1 = (f32[26,32,256]{2,1,0:T(8,128)}, f32[26,32,256]{2,1,0:T(8,128)S(1)}, u32[]{:S(2)}, u32[]{:S(2)}) collective-permute-start(f32[26,32,256]{2,1,0:T(8,128)} %get-tuple-element.32.own), channel_id=1, source_target_pairs={{0,30},{2,0},{4,2},{6,4},{8,6},{10,8},{12,10},{14,12},{16,14},{18,... | collective-permute-start | bytes 2555912 | tf_op jit(solution)/shard_map/ppermute | solution.py:588
  2.4 25.5 %collective-permute-start = (f32[26,32,256]{2,1,0:T(8,128)}, f32[26,32,256]{2,1,0:T(8,128)S(1)}, u32[]{:S(2)}, u32[]{:S(2)}) collective-permute-start(f32[26,32,256]{2,1,0:T(8,128)} %get-tuple-element.32.own), channel_id=1, source_target_pairs={{0,2},{2,4},{4,6},{6,8},{8,10},{10,12},{12,14},{14,16},{16,18},{18... | collective-permute-start | bytes 2555912 | tf_op jit(solution)/shard_map/ppermute | solution.py:587
  9.2 16.9 %all-to-all-start = ((f32[32,8,128]{2,1,0:T(8,128)}), f32[32,8,128]{2,1,0:T(8,128)S(1)}, u32[]{:S(2)}, u32[]{:S(2)}) async-start(f32[32,8,128]{2,1,0:T(8,128)} %bitcast.25), calls=%async_computation | async-start | bytes 262144 | tf_op jit(solution)/shard_map/all_to_all | solution.py:615
  26.1 25.6 %collective-permute-start.4 = (f32[32,24,256]{2,1,0:T(8,128)}, f32[32,24,256]{2,1,0:T(8,128)}, u32[]{:S(2)}, u32[]{:S(2)}) collective-permute-start(f32[32,24,256]{2,1,0:T(8,128)} %get-tuple-element.36), channel_id=1, source_target_pairs={{0,30},{2,0},{4,2},{6,4},{8,6},{10,8},{12,10},{14,12},{16,14},{18,... | collective-permute-start | bytes 2359304 | tf_op jit(solution)/shard_map/ppermute | solution.py:588
  26.8 24.8 %collective-permute-start.3 = (f32[32,24,256]{2,1,0:T(8,128)}, f32[32,24,256]{2,1,0:T(8,128)}, u32[]{:S(2)}, u32[]{:S(2)}) collective-permute-start(f32[32,24,256]{2,1,0:T(8,128)} %get-tuple-element.34), channel_id=1, source_target_pairs={{0,2},{2,4},{4,6},{6,8},{8,10},{10,12},{12,14},{14,16},{16,18},{18... | collective-permute-start | bytes 2359304 | tf_op jit(solution)/shard_map/ppermute | solution.py:587
  27.9 11.2 %copy-start = (f32[2,32,256]{2,1,0:T(8,128)S(1)}, f32[2,32,256]{2,1,0:T(8,128)}, u32[]{:S(2)}) copy-start(f32[2,32,256]{2,1,0:T(8,128)} %get-tuple-element.30) | copy-start | bytes 196612
  30.6 19.3 %all-to-all-start.1 = ((f32[32,8,128]{2,1,0:T(8,128)}), f32[32,8,128]{2,1,0:T(8,128)S(1)}, u32[]{:S(2)}, u32[]{:S(2)}) async-start(f32[32,8,128]{2,1,0:T(8,128)} %bitcast.26), calls=%async_computation.1 | async-start | bytes 262144 | tf_op jit(solution)/shard_map/all_to_all | solution.py:619
  39.2 5.9 %collective-permute-start.2 = (f32[2,32,256]{2,1,0:T(8,128)S(1)}, f32[2,32,256]{2,1,0:T(8,128)S(1)}, u32[]{:S(2)}, u32[]{:S(2)}) collective-permute-start(f32[2,32,256]{2,1,0:T(8,128)S(1)} %copy-done), channel_id=1, source_target_pairs={{0,1},{1,0},{2,3},{3,2},{4,5},{5,4},{6,7},{7,6},{8,9},{9,8},{10,11... | collective-permute-start | bytes 196616 | tf_op jit(solution)/shard_map/ppermute | solution.py:601
  49.9 13.8 %collective-permute-start.5 = (f32[32,16,256]{2,1,0:T(8,128)}, f32[32,16,256]{2,1,0:T(8,128)}, u32[]{:S(2)}, u32[]{:S(2)}) collective-permute-start(f32[32,16,256]{2,1,0:T(8,128)} %get-tuple-element.41), channel_id=1, source_target_pairs={{0,2},{2,4},{4,6},{6,8},{8,10},{10,12},{12,14},{14,16},{16,18},{18... | collective-permute-start | bytes 1572872 | tf_op jit(solution)/shard_map/ppermute | solution.py:587
  51.6 14.5 %collective-permute-start.6 = (f32[32,16,256]{2,1,0:T(8,128)}, f32[32,16,256]{2,1,0:T(8,128)}, u32[]{:S(2)}, u32[]{:S(2)}) collective-permute-start(f32[32,16,256]{2,1,0:T(8,128)} %get-tuple-element.42), channel_id=1, source_target_pairs={{0,30},{2,0},{4,2},{6,4},{8,6},{10,8},{12,10},{14,12},{16,14},{18,... | collective-permute-start | bytes 1572872 | tf_op jit(solution)/shard_map/ppermute | solution.py:588

commit v11 on v10

--- a/solution.py
+++ b/solution.py
@@ -345,28 +345,17 @@
         base[g, 0, upper:] = plane[stop:] + own[g, 0, upper:]
 
 
-def finish_kernel(upper, _, base, low, high, out, held, sent, sem_in, sem_out):
+def finish_kernel(upper, _, base, low, high, out, sent, sem):
     tiles = base.shape[1] // 8
     gap = out.shape[1] // 8 - tiles
-    arrivals = [
-        [
-            pltpu.make_async_copy(src.at[:, pl.ds(8 * t, 8), :], held.at[i, t], sem_in.at[i, t])
-            for i, src in enumerate((base, low, high))
-        ]
-        for t in range(tiles)
-    ]
-    for copies in arrivals:
-        for copy in copies:
-            copy.start()
-    done = []
+    copies = []
     for t in range(tiles):
-        for copy in arrivals[t]:
-            copy.wait()
-        sent[t] = gelu(held[0, t] + (held[1, t] + held[2, t]))
+        rows = pl.ds(8 * t, 8)
+        sent[t] = gelu(base[:, rows, :] + (low[:, rows, :] + high[:, rows, :]))
         to = t if t < upper else t + gap
-        done.append(pltpu.make_async_copy(sent.at[t], out.at[:, pl.ds(8 * to, 8), :], sem_out.at[t]))
-        done[-1].start()
-    for copy in done:
+        copies.append(pltpu.make_async_copy(sent.at[t], out.at[:, pl.ds(8 * to, 8), :], sem.at[t]))
+        copies[-1].start()
+    for copy in copies:
         copy.wait()
 
 
@@ -443,7 +432,7 @@
         out_specs=[some(y_local), some(rim)],
         scratch_shapes=[pltpu.VMEM((2, 2, CH // 4 * y_local, 128), BF)],
         compiler_params=params(),
-        cost_estimate=cost(2 * 10**11, 2**18),
+        cost_estimate=cost(10**8, 2**18),
         name="inverse_modes",
     )(modes, *in_hbm(bias, *tables), *planes)
     return result.reshape(CH, y_local, NX), base.reshape(CH, rim, NX)
@@ -452,22 +441,22 @@
 def finish_call(result, base, low, high, upper):
     tiles = base.shape[1] // 8
     anywhere = pl.BlockSpec(memory_space=pl.ANY)
+    vmem = pl.BlockSpec(memory_space=pltpu.VMEM)
+    operands = [pltpu.with_memory_space_constraint(a, pltpu.VMEM) for a in (base, low, high)]
     return pl.pallas_call(
         functools.partial(finish_kernel, upper),
         out_shape=jax.ShapeDtypeStruct(result.shape, F32),
-        in_specs=[anywhere] * 4,
+        in_specs=[anywhere] + [vmem] * 3,
         out_specs=anywhere,
         scratch_shapes=[
-            pltpu.VMEM((3, tiles, CH, 8, NX), F32),
             pltpu.VMEM((tiles, CH, 8, NX), F32),
-            pltpu.SemaphoreType.DMA((3, tiles)),
             pltpu.SemaphoreType.DMA((tiles,)),
         ],
         input_output_aliases={0: 0},
         compiler_params=params(),
         cost_estimate=cost(10**8, 2**18),
         name="finished_rows",
-    )(result, base, low, high)
+    )(result, *operands)
 
 
 def pack_call(field, tiles):
@@ -539,7 +528,7 @@
             pltpu.SemaphoreType.DMA((rows // 8,)),
         ],
         compiler_params=params(),
-        cost_estimate=cost(10**8, 2**18),
+        cost_estimate=cost(2 * 10**11, 2**18),
         name="middle_sums",
     )(*in_hbm(weight, point), low, *in_hbm(own), high)
 
@@ -614,17 +603,17 @@
         both = ("gz", "gy")
         got = lax.all_to_all(coarse, both, split_axis=0, concat_axis=0, tiled=True)
         pair = to_neighbours(after(down, got), after(up, got))
-        gains = after(spectral_filter, first_low, first_high, second)
+        gains = after(spectral_filter, first_low, first_high, second, halo)
         mark = filter_call(got, gains, gz, gy, forward_scale)
         back = lax.all_to_all(mark, both, split_axis=0, concat_axis=0, tiled=True)
         back = back.reshape(CH // 2, MY, 4 * MX)
     else:
         pair = to_neighbours(down, up)
         mark = back = general_filter(coarse, spectral_filter, gz, gy, forward_scale)
-    mixed = middle_call(depth_weight, point_weight, first_low, after(packed, mark), first_high)
     down, own, up = sums(after(field, mark), segments=((0,), (last,)), halo=(halo,))
-    down, up, _, _ = lax.optimization_barrier((down, up, back, mixed))
+    down, up, packed, _ = lax.optimization_barrier((down, up, packed, back))
     outer_pair = to_neighbours(down, up)
+    mixed = middle_call(depth_weight, point_weight, first_low, packed, first_high)
     result, base = inverse_call(
         back, bias_vector, own, mixed, second, pair, 8, y_local, gy, inverse_scale
     )

time: 69 us -> 72 us (1.043)
  waiting for transfers between devices: 11.4 us -> 15.5 us
  starting transfers between devices: 24.6 us -> 21 us
  local copies, waits for them, and re-layouts: 0.01 us -> 2.49 us
    ppermute x3, waiting for transfers between devices: 2.49 us -> 14 us  [to_neighbours(): lax.ppermute(up, 'gz', ring('gz', gz, -1))]
    ppermute x3, waiting for transfers between devices: 5.92 us -> 0.01 us  [to_neighbours(): lax.ppermute(down, 'gz', ring('gz', gz, 1))]
    all_to_all x1, starting transfers between devices: 8.54 us -> 5.3 us  [body(): back = lax.all_to_all(mark, both, split_axis=0, concat_axis=0, tiled=True)]
    all_to_all x1, waiting for transfers between devices: 2.95 us -> 0.01 us  [body(): got = lax.all_to_all(coarse, both, split_axis=0, concat_axis=0, tiled=True)]
    unnamed x2 -> x14, local copies, waits for them, and re-layouts: 0.01 us -> 2.49 us
    all_to_all x1, waiting for transfers between devices: 0.01 us -> 1.5 us  [body(): back = lax.all_to_all(mark, both, split_axis=0, concat_axis=0, tiled=True)]
    ppermute x3, starting transfers between devices: 5.52 us -> 4.61 us  [to_neighbours(): lax.ppermute(down, 'gz', ring('gz', gz, 1))]
  transfers between devices with their start and end apart: 9 -> 9, of which waited for: 3 -> 3; matrix products, arithmetic and copies ran while one was open for 0% -> 0% of each run, Pallas kernels for 41% -> 35%
where the time goes in v11:
time: 72 us; the launch traced here: 71.5 us
  Pallas kernels  32.4 us (45%)
  starting transfers between devices  21 us (29%)
  waiting for transfers between devices  15.5 us (22%)
  local copies, waits for them, and re-layouts  2.49 us (3%)
    ppermute x3, waiting for transfers between devices, to_neighbours(): lax.ppermute(up, 'gz', ring('gz', gz, -1))  14 us
    pallas_call x2, Pallas kernels, own_call(): pl.pallas_call(functools.partial(own_kernel, segments), out_shape=[pltpu....  10.3 us
    all_to_all x1, starting transfers between devices, body(): got = lax.all_to_all(coarse, both, split_axis=0, concat_axis=0, tiled=True)  8.29 us
    pallas_call x1, Pallas kernels, inverse_call(): pl.pallas_call(functools.partial(inverse_kernel, upper), out_shape=[jax.S...  6.14 us
    all_to_all x1, starting transfers between devices, body(): back = lax.all_to_all(mark, both, split_axis=0, concat_axis=0, tiled=True)  5.3 us
    ppermute x3, starting transfers between devices, to_neighbours(): lax.ppermute(down, 'gz', ring('gz', gz, 1))  4.61 us
    pallas_call x1, Pallas kernels, middle_call(): pl.pallas_call(middle_kernel, out_shape=pltpu.HBM((CH, rows, NX), F32), i...  4.5 us
    pallas_call x1, Pallas kernels, forward_call(): pl.pallas_call(forward_kernel, out_shape=(pltpu.HBM if pinned else jax.Sh...  4.12 us
  transfers between devices with their start and end apart: 9, of which 3 were waited for; matrix products, arithmetic and copies ran while one was open for 0% of the time, Pallas kernels for 35%

profile of v11, /device:TPU:1, one launch (start us, length us, event | category | flops | bytes accessed | tf_op | source)
XLA Modules:
  0.0 71.5 jit_solution(11388794418528103455)
XLA Ops:
  0.0 2.3 %packed_rows.1 = (f32[26,32,256]{2,1,0:T(8,128)}, f32[2,32,256]{2,1,0:T(8,128)}) custom-call(f32[32,64,256]{2,1,0:T(8,128)} %bitcast.19), custom_call_target="tpu_custom_call" | custom-call | flops 100000000 | bytes 262144 | tf_op jit(solution)/shard_map/packed_rows/pallas_call | solution.py:466
  2.3 0.0 copy-start.6
  2.3 0.1 collective-permute-start.1
  2.4 2.6 %collective-permute-start = (f32[26,32,256]{2,1,0:T(8,128)}, f32[26,32,256]{2,1,0:T(8,128)S(1)}, u32[]{:S(2)}, u32[]{:S(2)}) collective-permute-start(f32[26,32,256]{2,1,0:T(8,128)} %get-tuple-element.34.own), channel_id=1, source_target_pairs={{0,2},{2,4},{4,6},{6,8},{8,10},{10,12},{12,14},{14,16},{16,18},{18... | collective-permute-start | bytes 2555912 | tf_op jit(solution)/shard_map/ppermute | solution.py:576
  5.1 4.1 %forward_modes.1 = f32[256,128]{1,0:T(8,128)} custom-call(f32[8,4,64,256]{3,2,1,0:T(8,128)} %bitcast.20, bf16[2,256,128]{2,1,0:T(8,128)(2,1)} %constant.24.clone.x_top, bf16[2,256,128]{2,1,0:T(8,128)(2,1)} %constant.25.clone.x_rest, bf16[2,32,64]{2,1,0:T(8,128)(2,1)} %constant.26.clone.y_top, bf16[2,32,64]{2,1,0:T(8,128)(2,1)} %constant.27.clone.y_rest), custom_call_target="tpu_custom_call" | custom-call | flops 100000000 | bytes 262144 | tf_op jit(solution)/shard_map/forward_modes/pallas_call | solution.py:386
  9.2 8.3 %all-to-all-start = ((f32[32,8,128]{2,1,0:T(8,128)}), f32[32,8,128]{2,1,0:T(8,128)S(1)}, u32[]{:S(2)}, u32[]{:S(2)}) async-start(f32[32,8,128]{2,1,0:T(8,128)} %bitcast.27), calls=%async_computation | async-start | bytes 262144 | tf_op jit(solution)/shard_map/all_to_all | solution.py:604
  17.5 0.0 copy-done.6
  17.5 1.5 %collective-permute-start.2 = (f32[2,32,256]{2,1,0:T(8,128)S(1)}, f32[2,32,256]{2,1,0:T(8,128)S(1)}, u32[]{:S(2)}, u32[]{:S(2)}) collective-permute-start(f32[2,32,256]{2,1,0:T(8,128)S(1)} %copy-done.6), channel_id=1, source_target_pairs={{0,1},{1,0},{2,3},{3,2},{4,5},{5,4},{6,7},{7,6},{8,9},{9,8},{10,11... | collective-permute-start | bytes 196616 | tf_op jit(solution)/shard_map/ppermute | solution.py:590
  19.0 5.6 %own_sums.2 = (f32[32,24,256]{2,1,0:T(8,128)}, f32[32,24,256]{2,1,0:T(8,128)}, f32[32,24,256]{2,1,0:T(8,128)}) custom-call(f32[32,27]{1,0:T(8,128)} %weight.5, f32[32,32]{1,0:T(8,128)} %point.5, f32[32,64,256]{2,1,0:T(8,128)} %bitcast.21), custom_call_target="tpu_custom_call" | custom-call | flops 100000000 | bytes 262144 | tf_op jit(solution)/shard_map/own_sums/pallas_call | solution.py:488
  24.5 0.0 collective-permute-done.2.refs_0_
  24.5 0.6 copy-done
  25.1 0.9 %collective-permute-done.1.high = f32[26,32,256]{2,1,0:T(8,128)S(1)} collective-permute-done((f32[26,32,256]{2,1,0:T(8,128)}, f32[26,32,256]{2,1,0:T(8,128)S(1)}, u32[]{:S(2)}, u32[]{:S(2)}) %collective-permute-start.1) | collective-permute-done | bytes 852000 | tf_op jit(solution)/shard_map/ppermute | solution.py:577
  26.0 1.0 %copy-done.2 = f32[26,32,256]{2,1,0:T(8,128)} copy-done((f32[26,32,256]{2,1,0:T(8,128)}, f32[26,32,256]{2,1,0:T(8,128)S(1)}, u32[]{:S(2)}) %copy-start.2) | copy-done | bytes 851992
  27.0 0.0 collective-permute-done.low
  27.0 0.9 %copy-done.4 = f32[26,32,256]{2,1,0:T(8,128)} copy-done((f32[26,32,256]{2,1,0:T(8,128)}, f32[26,32,256]{2,1,0:T(8,128)S(1)}, u32[]{:S(2)}) %copy-start.4) | copy-done | bytes 851992
  27.9 0.0 all-to-all-done
  27.9 2.7 %filter_modes.1 = f32[256,128]{1,0:T(8,128)} custom-call(f32[256,128]{1,0:T(8,128)S(1)} %bitcast.18, f32[2,16,8,64]{3,2,1,0:T(8,128)} %gains, bf16[256,256]{1,0:T(8,128)(2,1)} %constant.28.clone.f_top, bf16[256,256]{1,0:T(8,128)(2,1)} %constant.29.clone.f_rest, bf16[512,128]{1,0:T(8,128)(2,1)} %constant.30.clone.i_top, bf16[512,128]{1,0:T(8,128)(2,1)} %constant.31.clone.i_rest), custom_call_target="tpu_custom_call" | custom-call | flops 199999995904 | bytes 262144 | tf_op jit(solution)/shard_map/filter_modes/pallas_call | solution.py:405
  30.6 5.3 %all-to-all-start.1 = ((f32[32,8,128]{2,1,0:T(8,128)}), f32[32,8,128]{2,1,0:T(8,128)S(1)}, u32[]{:S(2)}, u32[]{:S(2)}) async-start(f32[32,8,128]{2,1,0:T(8,128)} %bitcast.28), calls=%async_computation.1 | async-start | bytes 262144 | tf_op jit(solution)/shard_map/all_to_all | solution.py:608
  35.9 0.3 collective-permute-start.4
  36.2 1.5 %collective-permute-start.3 = (f32[32,24,256]{2,1,0:T(8,128)}, f32[32,24,256]{2,1,0:T(8,128)}, u32[]{:S(2)}, u32[]{:S(2)}) collective-permute-start(f32[32,24,256]{2,1,0:T(8,128)} %get-tuple-element.36), channel_id=1, source_target_pairs={{0,2},{2,4},{4,6},{6,8},{8,10},{10,12},{12,14},{14,16},{16,18},{18... | collective-permute-start | bytes 2359304 | tf_op jit(solution)/shard_map/ppermute | solution.py:576
  37.7 4.7 %own_sums.3 = (f32[32,16,256]{2,1,0:T(8,128)}, f32[32,16,256]{2,1,0:T(8,128)}, f32[32,16,256]{2,1,0:T(8,128)}) custom-call(f32[32,27]{1,0:T(8,128)} %weight.5, f32[32,32]{1,0:T(8,128)} %point.5, f32[32,64,256]{2,1,0:T(8,128)} %bitcast.22, f32[2,32,256]{2,1,0:T(8,128)S(1)} %copy-done.1), custom_call_target="tpu_custom_call" | custom-call | flops 100000000 | bytes 262144 | tf_op jit(solution)/shard_map/own_sums/pallas_call | solution.py:488
  42.4 1.5 %all-to-all-done.1 = f32[32,8,128]{2,1,0:T(8,128)S(1)} async-done(((f32[32,8,128]{2,1,0:T(8,128)}), f32[32,8,128]{2,1,0:T(8,128)S(1)}, u32[]{:S(2)}, u32[]{:S(2)}) %all-to-all-start.1) | async-done | bytes 131104 | tf_op jit(solution)/shard_map/all_to_all | solution.py:608
  43.9 0.5 collective-permute-start.5
  44.4 1.0 %collective-permute-start.6 = (f32[32,16,256]{2,1,0:T(8,128)}, f32[32,16,256]{2,1,0:T(8,128)}, u32[]{:S(2)}, u32[]{:S(2)}) collective-permute-start(f32[32,16,256]{2,1,0:T(8,128)} %get-tuple-element.42), channel_id=1, source_target_pairs={{0,30},{2,0},{4,2},{6,4},{8,6},{10,8},{12,10},{14,12},{16,14},{18,... | collective-permute-start | bytes 1572872 | tf_op jit(solution)/shard_map/ppermute | solution.py:577
  45.4 0.0 copy-done.3
  45.4 4.5 %middle_sums.1 = f32[32,24,256]{2,1,0:T(8,128)} custom-call(f32[32,27]{1,0:T(8,128)} %weight.5, f32[32,32]{1,0:T(8,128)} %point.5, f32[26,32,256]{2,1,0:T(8,128)S(1)} %copy-done.5, f32[26,32,256]{2,1,0:T(8,128)} %get-tuple-element.34.own, f32[26,32,256]{2,1,0:T(8,128)S(1)} %copy-done.3), custom_call_target="tpu_custom_call" | custom-call | flops 199999995904 | bytes 262144 | tf_op jit(solution)/shard_map/middle_sums/pallas_call | solution.py:515
  49.9 13.1 %collective-permute-done.4 = f32[32,24,256]{2,1,0:T(8,128)} collective-permute-done((f32[32,24,256]{2,1,0:T(8,128)}, f32[32,24,256]{2,1,0:T(8,128)}, u32[]{:S(2)}, u32[]{:S(2)}) %collective-permute-start.4) | collective-permute-done | bytes 786464 | tf_op jit(solution)/shard_map/ppermute | solution.py:577
  62.9 0.0 collective-permute-done.3
  62.9 6.1 %inverse_modes.1 = (f32[8,4,64,256]{3,2,1,0:T(8,128)}, f32[8,4,16,256]{3,2,1,0:T(8,128)S(1)}) custom-call(f32[16,16,128]{2,1,0:T(8,128)S(1)} %bitcast.16, f32[32]{0:T(128)} %bias.1, bf16[2,128,256]{2,1,0:T(8,128)(2,1)} %constant.32.clone.x_top, bf16[2,128,256]{2,1,0:T(8,128)(2,1)} %constant.33.clone.x_rest, bf16[2,64,32]{2,1,0:T(8,128)(2,1)} %constant.34.clone.y_top, ...), custom_call_target="tpu_custom_call" | custom-call | flops 100000000 | bytes 262144 | tf_op jit(solution)/shard_map/inverse_modes/pallas_call | solution.py:419
  69.1 0.0 collective-permute-done.5.low
  69.1 0.0 collective-permute-done.6.high
  69.1 2.4 %finished_rows.1 = f32[32,64,256]{2,1,0:T(8,128)} custom-call(f32[32,64,256]{2,1,0:T(8,128)} %bitcast.23, f32[32,16,256]{2,1,0:T(8,128)S(1)} %bitcast.17, f32[32,16,256]{2,1,0:T(8,128)} %collective-permute-done.5.low, f32[32,16,256]{2,1,0:T(8,128)} %collective-permute-done.6.high), custom_call_target="tpu_custom_call", output_to_operand_aliasing={{}: (0, {})} | custom-call | flops 100000000 | bytes 262144 | tf_op jit(solution)/shard_map/finished_rows/pallas_call | solution.py:446
  (8 shorter events, 0.0 us)
Async XLA Ops:
  2.3 15.2 %copy-start.6 = (f32[2,32,256]{2,1,0:T(8,128)S(1)}, f32[2,32,256]{2,1,0:T(8,128)}, u32[]{:S(2)}) copy-start(f32[2,32,256]{2,1,0:T(8,128)} %get-tuple-element.28) | copy-start | bytes 196612
  2.3 23.7 %collective-permute-start.1 = (f32[26,32,256]{2,1,0:T(8,128)}, f32[26,32,256]{2,1,0:T(8,128)S(1)}, u32[]{:S(2)}, u32[]{:S(2)}) collective-permute-start(f32[26,32,256]{2,1,0:T(8,128)} %get-tuple-element.34.own), channel_id=1, source_target_pairs={{0,30},{2,0},{4,2},{6,4},{8,6},{10,8},{12,10},{14,12},{16,14},{18,... | collective-permute-start | bytes 2555912 | tf_op jit(solution)/shard_map/ppermute | solution.py:577
  2.4 24.6 %collective-permute-start = (f32[26,32,256]{2,1,0:T(8,128)}, f32[26,32,256]{2,1,0:T(8,128)S(1)}, u32[]{:S(2)}, u32[]{:S(2)}) collective-permute-start(f32[26,32,256]{2,1,0:T(8,128)} %get-tuple-element.34.own), channel_id=1, source_target_pairs={{0,2},{2,4},{4,6},{6,8},{8,10},{10,12},{12,14},{14,16},{16,18},{18... | collective-permute-start | bytes 2555912 | tf_op jit(solution)/shard_map/ppermute | solution.py:576
  9.2 18.7 %all-to-all-start = ((f32[32,8,128]{2,1,0:T(8,128)}), f32[32,8,128]{2,1,0:T(8,128)S(1)}, u32[]{:S(2)}, u32[]{:S(2)}) async-start(f32[32,8,128]{2,1,0:T(8,128)} %bitcast.27), calls=%async_computation | async-start | bytes 262144 | tf_op jit(solution)/shard_map/all_to_all | solution.py:604
  17.5 7.0 %collective-permute-start.2 = (f32[2,32,256]{2,1,0:T(8,128)S(1)}, f32[2,32,256]{2,1,0:T(8,128)S(1)}, u32[]{:S(2)}, u32[]{:S(2)}) collective-permute-start(f32[2,32,256]{2,1,0:T(8,128)S(1)} %copy-done.6), channel_id=1, source_target_pairs={{0,1},{1,0},{2,3},{3,2},{4,5},{5,4},{6,7},{7,6},{8,9},{9,8},{10,11... | collective-permute-start | bytes 196616 | tf_op jit(solution)/shard_map/ppermute | solution.py:590
  24.5 0.6 copy-start
  26.0 1.0 %copy-start.2 = (f32[26,32,256]{2,1,0:T(8,128)}, f32[26,32,256]{2,1,0:T(8,128)S(1)}, u32[]{:S(2)}) copy-start(f32[26,32,256]{2,1,0:T(8,128)S(1)} %collective-permute-done.1.high) | copy-start | bytes 2555908
  27.0 0.9 %copy-start.4 = (f32[26,32,256]{2,1,0:T(8,128)}, f32[26,32,256]{2,1,0:T(8,128)S(1)}, u32[]{:S(2)}) copy-start(f32[26,32,256]{2,1,0:T(8,128)S(1)} %collective-permute-done.low) | copy-start | bytes 2555908
  27.9 9.8 %copy-start.1 = (f32[2,32,256]{2,1,0:T(8,128)S(1)}, f32[2,32,256]{2,1,0:T(8,128)}, u32[]{:S(2)}) copy-start(f32[2,32,256]{2,1,0:T(8,128)} %copy-done) | copy-start | bytes 196612
  30.6 14.8 %copy-start.3 = (f32[26,32,256]{2,1,0:T(8,128)S(1)}, f32[26,32,256]{2,1,0:T(8,128)}, u32[]{:S(2)}) copy-start(f32[26,32,256]{2,1,0:T(8,128)} %copy-done.2) | copy-start | bytes 2555908
  30.6 14.8 %copy-start.5 = (f32[26,32,256]{2,1,0:T(8,128)S(1)}, f32[26,32,256]{2,1,0:T(8,128)}, u32[]{:S(2)}) copy-start(f32[26,32,256]{2,1,0:T(8,128)} %copy-done.4) | copy-start | bytes 2555908
  30.6 13.3 %all-to-all-start.1 = ((f32[32,8,128]{2,1,0:T(8,128)}), f32[32,8,128]{2,1,0:T(8,128)S(1)}, u32[]{:S(2)}, u32[]{:S(2)}) async-start(f32[32,8,128]{2,1,0:T(8,128)} %bitcast.28), calls=%async_computation.1 | async-start | bytes 262144 | tf_op jit(solution)/shard_map/all_to_all | solution.py:608
  35.9 27.1 %collective-permute-start.4 = (f32[32,24,256]{2,1,0:T(8,128)}, f32[32,24,256]{2,1,0:T(8,128)}, u32[]{:S(2)}, u32[]{:S(2)}) collective-permute-start(f32[32,24,256]{2,1,0:T(8,128)} %get-tuple-element.38), channel_id=1, source_target_pairs={{0,30},{2,0},{4,2},{6,4},{8,6},{10,8},{12,10},{14,12},{16,14},{18,... | collective-permute-start | bytes 2359304 | tf_op jit(solution)/shard_map/ppermute | solution.py:577
  36.2 26.7 %collective-permute-start.3 = (f32[32,24,256]{2,1,0:T(8,128)}, f32[32,24,256]{2,1,0:T(8,128)}, u32[]{:S(2)}, u32[]{:S(2)}) collective-permute-start(f32[32,24,256]{2,1,0:T(8,128)} %get-tuple-element.36), channel_id=1, source_target_pairs={{0,2},{2,4},{4,6},{6,8},{8,10},{10,12},{12,14},{14,16},{16,18},{18... | collective-permute-start | bytes 2359304 | tf_op jit(solution)/shard_map/ppermute | solution.py:576
  43.9 25.2 %collective-permute-start.5 = (f32[32,16,256]{2,1,0:T(8,128)}, f32[32,16,256]{2,1,0:T(8,128)}, u32[]{:S(2)}, u32[]{:S(2)}) collective-permute-start(f32[32,16,256]{2,1,0:T(8,128)} %get-tuple-element.41), channel_id=1, source_target_pairs={{0,2},{2,4},{4,6},{6,8},{8,10},{10,12},{12,14},{14,16},{16,18},{18... | collective-permute-start | bytes 1572872 | tf_op jit(solution)/shard_map/ppermute | solution.py:576
  44.4 24.7 %collective-permute-start.6 = (f32[32,16,256]{2,1,0:T(8,128)}, f32[32,16,256]{2,1,0:T(8,128)}, u32[]{:S(2)}, u32[]{:S(2)}) collective-permute-start(f32[32,16,256]{2,1,0:T(8,128)} %get-tuple-element.42), channel_id=1, source_target_pairs={{0,30},{2,0},{4,2},{6,4},{8,6},{10,8},{12,10},{14,12},{16,14},{18,... | collective-permute-start | bytes 1572872 | tf_op jit(solution)/shard_map/ppermute | solution.py:577

commit v12 on v10

--- a/solution.py
+++ b/solution.py
@@ -443,7 +443,7 @@
         out_specs=[some(y_local), some(rim)],
         scratch_shapes=[pltpu.VMEM((2, 2, CH // 4 * y_local, 128), BF)],
         compiler_params=params(),
-        cost_estimate=cost(2 * 10**11, 2**18),
+        cost_estimate=cost(10**8, 2**18),
         name="inverse_modes",
     )(modes, *in_hbm(bias, *tables), *planes)
     return result.reshape(CH, y_local, NX), base.reshape(CH, rim, NX)
@@ -499,7 +499,7 @@
     return pl.pallas_call(
         functools.partial(own_kernel, segments),
         out_shape=[pltpu.HBM((CH, rows, NX), F32)] * 3,
-        in_specs=[hbm] * 3 + [pl.BlockSpec(memory_space=pl.ANY)] * len(halo),
+        in_specs=[hbm] * (3 + len(halo)),
         out_specs=[hbm] * 3,
         scratch_shapes=[
             pltpu.VMEM((fetched, 2, CH, 8, 128), F32),
@@ -517,7 +517,7 @@
         compiler_params=params(),
         cost_estimate=cost(10**8, 2**18),
         name="own_sums",
-    )(*in_hbm(weight, point, field), *halo)
+    )(*in_hbm(weight, point, field, *halo))
 
 
 def middle_call(weight, point, low, own, high):
@@ -526,7 +526,7 @@
     return pl.pallas_call(
         middle_kernel,
         out_shape=pltpu.HBM((CH, rows, NX), F32),
-        in_specs=[hbm] * 2 + [pl.BlockSpec(memory_space=pl.ANY)] * 3,
+        in_specs=[hbm] * 5,
         out_specs=hbm,
         scratch_shapes=[
             pltpu.VMEM((3, rows + 2, CH, NX), F32),
@@ -539,9 +539,9 @@
             pltpu.SemaphoreType.DMA((rows // 8,)),
         ],
         compiler_params=params(),
-        cost_estimate=cost(10**8, 2**18),
+        cost_estimate=cost(2 * 10**11, 2**18),
         name="middle_sums",
-    )(*in_hbm(weight, point), low, *in_hbm(own), high)
+    )(*in_hbm(weight, point, low, own, high))
 
 
 def general_filter(coarse, gains, gz, gy, scale):
@@ -593,7 +593,8 @@
 
     last = y_local // 8 - 1
     cut = 1 + last // 2
-    first_tiles, second_tiles = tuple(range(1, cut)), tuple(range(cut, last))
+    first_tiles, second_tiles = tuple(range(1, cut)), tuple(range(cut, min(cut + 2, last)))
+    outer_tiles = ((0,), tuple(range(second_tiles[-1] + 1, last + 1)))
     sums = functools.partial(own_call, weight=depth_weight, point=point_weight)
     packed, edges = pack_call(field, first_tiles)
     first_low, first_high = to_neighbours(packed, packed)
@@ -614,17 +615,17 @@
         both = ("gz", "gy")
         got = lax.all_to_all(coarse, both, split_axis=0, concat_axis=0, tiled=True)
         pair = to_neighbours(after(down, got), after(up, got))
-        gains = after(spectral_filter, first_low, first_high, second)
+        gains = after(spectral_filter, first_low, first_high, second, halo)
         mark = filter_call(got, gains, gz, gy, forward_scale)
         back = lax.all_to_all(mark, both, split_axis=0, concat_axis=0, tiled=True)
         back = back.reshape(CH // 2, MY, 4 * MX)
     else:
         pair = to_neighbours(down, up)
         mark = back = general_filter(coarse, spectral_filter, gz, gy, forward_scale)
-    mixed = middle_call(depth_weight, point_weight, first_low, after(packed, mark), first_high)
-    down, own, up = sums(after(field, mark), segments=((0,), (last,)), halo=(halo,))
-    down, up, _, _ = lax.optimization_barrier((down, up, back, mixed))
-    outer_pair = to_neighbours(down, up)
+    down, own, up = sums(after(field, mark), segments=outer_tiles, halo=(halo,))
+    outer_pair = to_neighbours(after(down, back), after(up, back))
+    packed, *pair = lax.optimization_barrier((packed, *pair, back))[:-1]
+    mixed = middle_call(depth_weight, point_weight, first_low, packed, first_high)
     result, base = inverse_call(
         back, bias_vector, own, mixed, second, pair, 8, y_local, gy, inverse_scale
     )

time: 69 us -> 71 us (1.029)
  Pallas kernels: 32.4 us -> 33.5 us
  waiting for transfers between devices: 11.4 us -> 12.3 us
    ppermute x3, waiting for transfers between devices: 5.92 us -> 0.01 us  [to_neighbours(): lax.ppermute(down, 'gz', ring('gz', gz, 1))]
    ppermute x3, waiting for transfers between devices: 2.49 us -> 7.66 us  [to_neighbours(): lax.ppermute(up, 'gz', ring('gz', gz, -1))]
    all_to_all x1, waiting for transfers between devices: 0.01 us -> 2.18 us  [body(): back = lax.all_to_all(mark, both, split_axis=0, concat_axis=0, tiled=True)]
    ppermute x3, starting transfers between devices: 5.52 us -> 4.55 us  [to_neighbours(): lax.ppermute(down, 'gz', ring('gz', gz, 1))]
    ppermute x3, starting transfers between devices: 0.85 us -> 1.8 us  [to_neighbours(): lax.ppermute(up, 'gz', ring('gz', gz, -1))]
  transfers between devices with their start and end apart: 9 -> 9, of which waited for: 3 -> 3; matrix products, arithmetic and copies ran while one was open for 0% -> 0% of each run, Pallas kernels for 41% -> 40%
where the time goes in v12:
time: 71 us; the launch traced here: 70.5 us
  Pallas kernels  33.5 us (47%)
  starting transfers between devices  24.6 us (35%)
  waiting for transfers between devices  12.3 us (17%)
    pallas_call x2, Pallas kernels, own_call(): pl.pallas_call(functools.partial(own_kernel, segments), out_shape=[pltpu....  10.4 us
    all_to_all x1, starting transfers between devices, body(): back = lax.all_to_all(mark, both, split_axis=0, concat_axis=0, tiled=True)  8.54 us
    all_to_all x1, starting transfers between devices, body(): got = lax.all_to_all(coarse, both, split_axis=0, concat_axis=0, tiled=True)  8.29 us
    ppermute x3, waiting for transfers between devices, to_neighbours(): lax.ppermute(up, 'gz', ring('gz', gz, -1))  7.66 us
    pallas_call x1, Pallas kernels, inverse_call(): pl.pallas_call(functools.partial(inverse_kernel, upper), out_shape=[jax.S...  5.86 us
    pallas_call x1, Pallas kernels, middle_call(): pl.pallas_call(middle_kernel, out_shape=pltpu.HBM((CH, rows, NX), F32), i...  4.89 us
    ppermute x3, starting transfers between devices, to_neighbours(): lax.ppermute(down, 'gz', ring('gz', gz, 1))  4.55 us
    pallas_call x1, Pallas kernels, forward_call(): pl.pallas_call(forward_kernel, out_shape=(pltpu.HBM if pinned else jax.Sh...  4.13 us
  transfers between devices with their start and end apart: 9, of which 3 were waited for; matrix products, arithmetic and copies ran while one was open for 0% of the time, Pallas kernels for 40%

profile of v12, /device:TPU:1, one launch (start us, length us, event | category | flops | bytes accessed | tf_op | source)
XLA Modules:
  0.0 70.5 jit_solution(4577401729726864059)
XLA Ops:
  0.0 2.3 %packed_rows.1 = (f32[26,32,256]{2,1,0:T(8,128)}, f32[2,32,256]{2,1,0:T(8,128)}) custom-call(f32[32,64,256]{2,1,0:T(8,128)} %bitcast.19), custom_call_target="tpu_custom_call" | custom-call | flops 100000000 | bytes 262144 | tf_op jit(solution)/shard_map/packed_rows/pallas_call | solution.py:477
  2.3 0.0 copy-start.3
  2.3 0.1 collective-permute-start.1
  2.4 2.6 %collective-permute-start = (f32[26,32,256]{2,1,0:T(8,128)}, f32[26,32,256]{2,1,0:T(8,128)S(1)}, u32[]{:S(2)}, u32[]{:S(2)}) collective-permute-start(f32[26,32,256]{2,1,0:T(8,128)} %get-tuple-element.38.own), channel_id=1, source_target_pairs={{0,2},{2,4},{4,6},{6,8},{8,10},{10,12},{12,14},{14,16},{16,18},{18... | collective-permute-start | bytes 2555912 | tf_op jit(solution)/shard_map/ppermute | solution.py:587
  5.1 4.1 %forward_modes.1 = f32[256,128]{1,0:T(8,128)} custom-call(f32[8,4,64,256]{3,2,1,0:T(8,128)} %bitcast.20, bf16[2,256,128]{2,1,0:T(8,128)(2,1)} %constant.24.clone.x_top, bf16[2,256,128]{2,1,0:T(8,128)(2,1)} %constant.25.clone.x_rest, bf16[2,32,64]{2,1,0:T(8,128)(2,1)} %constant.26.clone.y_top, bf16[2,32,64]{2,1,0:T(8,128)(2,1)} %constant.27.clone.y_rest), custom_call_target="tpu_custom_call" | custom-call | flops 100000000 | bytes 262144 | tf_op jit(solution)/shard_map/forward_modes/pallas_call | solution.py:397
  9.2 8.3 %all-to-all-start = ((f32[32,8,128]{2,1,0:T(8,128)}), f32[32,8,128]{2,1,0:T(8,128)S(1)}, u32[]{:S(2)}, u32[]{:S(2)}) async-start(f32[32,8,128]{2,1,0:T(8,128)} %bitcast.26), calls=%async_computation | async-start | bytes 262144 | tf_op jit(solution)/shard_map/all_to_all | solution.py:616
  17.5 0.0 copy-done.3
  17.5 1.5 %collective-permute-start.2 = (f32[2,32,256]{2,1,0:T(8,128)S(1)}, f32[2,32,256]{2,1,0:T(8,128)S(1)}, u32[]{:S(2)}, u32[]{:S(2)}) collective-permute-start(f32[2,32,256]{2,1,0:T(8,128)S(1)} %copy-done.3), channel_id=1, source_target_pairs={{0,1},{1,0},{2,3},{3,2},{4,5},{5,4},{6,7},{7,6},{8,9},{9,8},{10,11... | collective-permute-start | bytes 196616 | tf_op jit(solution)/shard_map/ppermute | solution.py:602
  19.0 4.7 %own_sums.2 = (f32[32,16,256]{2,1,0:T(8,128)}, f32[32,16,256]{2,1,0:T(8,128)}, f32[32,16,256]{2,1,0:T(8,128)}) custom-call(f32[32,27]{1,0:T(8,128)} %weight.5, f32[32,32]{1,0:T(8,128)} %point.5, f32[32,64,256]{2,1,0:T(8,128)} %bitcast.21), custom_call_target="tpu_custom_call" | custom-call | flops 100000000 | bytes 262144 | tf_op jit(solution)/shard_map/own_sums/pallas_call | solution.py:499
  23.6 2.4 %all-to-all-done = f32[32,8,128]{2,1,0:T(8,128)S(1)} async-done(((f32[32,8,128]{2,1,0:T(8,128)}), f32[32,8,128]{2,1,0:T(8,128)S(1)}, u32[]{:S(2)}, u32[]{:S(2)}) %all-to-all-start) | async-done | bytes 131104 | tf_op jit(solution)/shard_map/all_to_all | solution.py:616
  26.1 0.7 %collective-permute-start.4 = (f32[32,16,256]{2,1,0:T(8,128)}, f32[32,16,256]{2,1,0:T(8,128)}, u32[]{:S(2)}, u32[]{:S(2)}) collective-permute-start(f32[32,16,256]{2,1,0:T(8,128)} %get-tuple-element.37), channel_id=1, source_target_pairs={{0,30},{2,0},{4,2},{6,4},{8,6},{10,8},{12,10},{14,12},{16,14},{18,... | collective-permute-start | bytes 1572872 | tf_op jit(solution)/shard_map/ppermute | solution.py:588
  26.8 1.1 %collective-permute-start.3 = (f32[32,16,256]{2,1,0:T(8,128)}, f32[32,16,256]{2,1,0:T(8,128)}, u32[]{:S(2)}, u32[]{:S(2)}) collective-permute-start(f32[32,16,256]{2,1,0:T(8,128)} %get-tuple-element.35), channel_id=1, source_target_pairs={{0,2},{2,4},{4,6},{6,8},{8,10},{10,12},{12,14},{14,16},{16,18},{18... | collective-permute-start | bytes 1572872 | tf_op jit(solution)/shard_map/ppermute | solution.py:587
  27.9 0.0 collective-permute-done.2.refs_0_
  27.9 0.0 collective-permute-done.1.high
  27.9 0.0 copy-start.1
  28.0 0.0 collective-permute-done.low
  28.0 0.0 copy-start.2
  28.0 3.2 %filter_modes.1 = f32[256,128]{1,0:T(8,128)} custom-call(f32[256,128]{1,0:T(8,128)S(1)} %bitcast.18, f32[2,16,8,64]{3,2,1,0:T(8,128)} %gains, bf16[256,256]{1,0:T(8,128)(2,1)} %constant.28.clone.f_top, bf16[256,256]{1,0:T(8,128)(2,1)} %constant.29.clone.f_rest, bf16[512,128]{1,0:T(8,128)(2,1)} %constant.30.clone.i_top, bf16[512,128]{1,0:T(8,128)(2,1)} %constant.31.clone.i_rest), custom_call_target="tpu_custom_call" | custom-call | flops 199999995904 | bytes 262144 | tf_op jit(solution)/shard_map/filter_modes/pallas_call | solution.py:416
  31.2 0.0 copy-done
  31.2 0.0 copy-done.1
  31.2 8.5 %all-to-all-start.1 = ((f32[32,8,128]{2,1,0:T(8,128)}), f32[32,8,128]{2,1,0:T(8,128)S(1)}, u32[]{:S(2)}, u32[]{:S(2)}) async-start(f32[32,8,128]{2,1,0:T(8,128)} %bitcast.28), calls=%async_computation.1 | async-start | bytes 262144 | tf_op jit(solution)/shard_map/all_to_all | solution.py:620
  39.8 5.7 %own_sums.3 = (f32[32,24,256]{2,1,0:T(8,128)}, f32[32,24,256]{2,1,0:T(8,128)}, f32[32,24,256]{2,1,0:T(8,128)}) custom-call(f32[32,27]{1,0:T(8,128)} %weight.5, f32[32,32]{1,0:T(8,128)} %point.5, f32[32,64,256]{2,1,0:T(8,128)} %bitcast.22, f32[2,32,256]{2,1,0:T(8,128)} %copy-done), custom_call_target="tpu_custom_call" | custom-call | flops 100000000 | bytes 262144 | tf_op jit(solution)/shard_map/own_sums/pallas_call | solution.py:499
  45.5 0.0 collective-permute-done.4
  45.5 0.0 collective-permute-done.3
  45.5 2.2 %all-to-all-done.1 = f32[32,8,128]{2,1,0:T(8,128)S(1)} async-done(((f32[32,8,128]{2,1,0:T(8,128)}), f32[32,8,128]{2,1,0:T(8,128)S(1)}, u32[]{:S(2)}, u32[]{:S(2)}) %all-to-all-start.1) | async-done | bytes 131104 | tf_op jit(solution)/shard_map/all_to_all | solution.py:620
  47.7 1.0 %collective-permute-start.6 = (f32[32,24,256]{2,1,0:T(8,128)}, f32[32,24,256]{2,1,0:T(8,128)}, u32[]{:S(2)}, u32[]{:S(2)}) collective-permute-start(f32[32,24,256]{2,1,0:T(8,128)} %get-tuple-element.46), channel_id=1, source_target_pairs={{0,30},{2,0},{4,2},{6,4},{8,6},{10,8},{12,10},{14,12},{16,14},{18,... | collective-permute-start | bytes 2359304 | tf_op jit(solution)/shard_map/ppermute | solution.py:588
  48.7 0.8 %collective-permute-start.5 = (f32[32,24,256]{2,1,0:T(8,128)}, f32[32,24,256]{2,1,0:T(8,128)}, u32[]{:S(2)}, u32[]{:S(2)}) collective-permute-start(f32[32,24,256]{2,1,0:T(8,128)} %get-tuple-element.44), channel_id=1, source_target_pairs={{0,2},{2,4},{4,6},{6,8},{8,10},{10,12},{12,14},{14,16},{16,18},{18... | collective-permute-start | bytes 2359304 | tf_op jit(solution)/shard_map/ppermute | solution.py:587
  49.5 4.9 %middle_sums.1 = f32[32,24,256]{2,1,0:T(8,128)} custom-call(f32[32,27]{1,0:T(8,128)} %weight.5, f32[32,32]{1,0:T(8,128)} %point.5, f32[26,32,256]{2,1,0:T(8,128)} %copy-done.2, f32[26,32,256]{2,1,0:T(8,128)} %get-tuple-element.38.own, f32[26,32,256]{2,1,0:T(8,128)} %copy-done.1), custom_call_target="tpu_custom_call" | custom-call | flops 199999995904 | bytes 262144 | tf_op jit(solution)/shard_map/middle_sums/pallas_call | solution.py:526
  54.4 5.9 %inverse_modes.1 = (f32[8,4,64,256]{3,2,1,0:T(8,128)}, f32[8,4,24,256]{3,2,1,0:T(8,128)S(1)}) custom-call(f32[16,16,128]{2,1,0:T(8,128)S(1)} %bitcast.17, f32[32]{0:T(128)} %bias.1, bf16[2,128,256]{2,1,0:T(8,128)(2,1)} %constant.32.clone.x_top, bf16[2,128,256]{2,1,0:T(8,128)(2,1)} %constant.33.clone.x_rest, bf16[2,64,32]{2,1,0:T(8,128)(2,1)} %constant.34.clone.y_top, ...), custom_call_target="tpu_custom_call" | custom-call | flops 100000000 | bytes 262144 | tf_op jit(solution)/shard_map/inverse_modes/pallas_call | solution.py:430
  60.2 7.7 %collective-permute-done.6.high = f32[32,24,256]{2,1,0:T(8,128)} collective-permute-done((f32[32,24,256]{2,1,0:T(8,128)}, f32[32,24,256]{2,1,0:T(8,128)}, u32[]{:S(2)}, u32[]{:S(2)}) %collective-permute-start.6) | collective-permute-done | bytes 786464 | tf_op jit(solution)/shard_map/ppermute | solution.py:588
  67.9 0.0 collective-permute-done.5.low
  67.9 2.6 %finished_rows.1 = f32[32,64,256]{2,1,0:T(8,128)} custom-call(f32[32,64,256]{2,1,0:T(8,128)} %bitcast.23, f32[32,24,256]{2,1,0:T(8,128)S(1)} %bitcast.16, f32[32,24,256]{2,1,0:T(8,128)} %collective-permute-done.5.low, f32[32,24,256]{2,1,0:T(8,128)} %collective-permute-done.6.high), custom_call_target="tpu_custom_call", output_to_operand_aliasing={{}: (0, {})} | custom-call | flops 100000000 | bytes 262144 | tf_op jit(solution)/shard_map/finished_rows/pallas_call | solution.py:455
  (2 shorter events, 0.0 us)
Async XLA Ops:
  2.3 15.2 %copy-start.3 = (f32[2,32,256]{2,1,0:T(8,128)S(1)}, f32[2,32,256]{2,1,0:T(8,128)}, u32[]{:S(2)}) copy-start(f32[2,32,256]{2,1,0:T(8,128)} %get-tuple-element.30) | copy-start | bytes 196612
  2.3 25.6 %collective-permute-start.1 = (f32[26,32,256]{2,1,0:T(8,128)}, f32[26,32,256]{2,1,0:T(8,128)S(1)}, u32[]{:S(2)}, u32[]{:S(2)}) collective-permute-start(f32[26,32,256]{2,1,0:T(8,128)} %get-tuple-element.38.own), channel_id=1, source_target_pairs={{0,30},{2,0},{4,2},{6,4},{8,6},{10,8},{12,10},{14,12},{16,14},{18,... | collective-permute-start | bytes 2555912 | tf_op jit(solution)/shard_map/ppermute | solution.py:588
  2.4 25.5 %collective-permute-start = (f32[26,32,256]{2,1,0:T(8,128)}, f32[26,32,256]{2,1,0:T(8,128)S(1)}, u32[]{:S(2)}, u32[]{:S(2)}) collective-permute-start(f32[26,32,256]{2,1,0:T(8,128)} %get-tuple-element.38.own), channel_id=1, source_target_pairs={{0,2},{2,4},{4,6},{6,8},{8,10},{10,12},{12,14},{14,16},{16,18},{18... | collective-permute-start | bytes 2555912 | tf_op jit(solution)/shard_map/ppermute | solution.py:587
  9.2 16.9 %all-to-all-start = ((f32[32,8,128]{2,1,0:T(8,128)}), f32[32,8,128]{2,1,0:T(8,128)S(1)}, u32[]{:S(2)}, u32[]{:S(2)}) async-start(f32[32,8,128]{2,1,0:T(8,128)} %bitcast.26), calls=%async_computation | async-start | bytes 262144 | tf_op jit(solution)/shard_map/all_to_all | solution.py:616
  17.5 10.4 %collective-permute-start.2 = (f32[2,32,256]{2,1,0:T(8,128)S(1)}, f32[2,32,256]{2,1,0:T(8,128)S(1)}, u32[]{:S(2)}, u32[]{:S(2)}) collective-permute-start(f32[2,32,256]{2,1,0:T(8,128)S(1)} %copy-done.3), channel_id=1, source_target_pairs={{0,1},{1,0},{2,3},{3,2},{4,5},{5,4},{6,7},{7,6},{8,9},{9,8},{10,11... | collective-permute-start | bytes 196616 | tf_op jit(solution)/shard_map/ppermute | solution.py:602
  26.1 19.4 %collective-permute-start.4 = (f32[32,16,256]{2,1,0:T(8,128)}, f32[32,16,256]{2,1,0:T(8,128)}, u32[]{:S(2)}, u32[]{:S(2)}) collective-permute-start(f32[32,16,256]{2,1,0:T(8,128)} %get-tuple-element.37), channel_id=1, source_target_pairs={{0,30},{2,0},{4,2},{6,4},{8,6},{10,8},{12,10},{14,12},{16,14},{18,... | collective-permute-start | bytes 1572872 | tf_op jit(solution)/shard_map/ppermute | solution.py:588
  26.8 18.7 %collective-permute-start.3 = (f32[32,16,256]{2,1,0:T(8,128)}, f32[32,16,256]{2,1,0:T(8,128)}, u32[]{:S(2)}, u32[]{:S(2)}) collective-permute-start(f32[32,16,256]{2,1,0:T(8,128)} %get-tuple-element.35), channel_id=1, source_target_pairs={{0,2},{2,4},{4,6},{6,8},{8,10},{10,12},{12,14},{14,16},{16,18},{18... | collective-permute-start | bytes 1572872 | tf_op jit(solution)/shard_map/ppermute | solution.py:587
  27.9 3.3 %copy-start = (f32[2,32,256]{2,1,0:T(8,128)}, f32[2,32,256]{2,1,0:T(8,128)S(1)}, u32[]{:S(2)}) copy-start(f32[2,32,256]{2,1,0:T(8,128)S(1)} %collective-permute-done.2.refs_0_) | copy-start | bytes 196612
  27.9 3.3 %copy-start.1 = (f32[26,32,256]{2,1,0:T(8,128)}, f32[26,32,256]{2,1,0:T(8,128)S(1)}, u32[]{:S(2)}) copy-start(f32[26,32,256]{2,1,0:T(8,128)S(1)} %collective-permute-done.1.high) | copy-start | bytes 2555908
  28.0 3.3 %copy-start.2 = (f32[26,32,256]{2,1,0:T(8,128)}, f32[26,32,256]{2,1,0:T(8,128)S(1)}, u32[]{:S(2)}) copy-start(f32[26,32,256]{2,1,0:T(8,128)S(1)} %collective-permute-done.low) | copy-start | bytes 2555908
  31.2 16.5 %all-to-all-start.1 = ((f32[32,8,128]{2,1,0:T(8,128)}), f32[32,8,128]{2,1,0:T(8,128)S(1)}, u32[]{:S(2)}, u32[]{:S(2)}) async-start(f32[32,8,128]{2,1,0:T(8,128)} %bitcast.28), calls=%async_computation.1 | async-start | bytes 262144 | tf_op jit(solution)/shard_map/all_to_all | solution.py:620
  47.7 20.2 %collective-permute-start.6 = (f32[32,24,256]{2,1,0:T(8,128)}, f32[32,24,256]{2,1,0:T(8,128)}, u32[]{:S(2)}, u32[]{:S(2)}) collective-permute-start(f32[32,24,256]{2,1,0:T(8,128)} %get-tuple-element.46), channel_id=1, source_target_pairs={{0,30},{2,0},{4,2},{6,4},{8,6},{10,8},{12,10},{14,12},{16,14},{18,... | collective-permute-start | bytes 2359304 | tf_op jit(solution)/shard_map/ppermute | solution.py:588
  48.7 19.2 %collective-permute-start.5 = (f32[32,24,256]{2,1,0:T(8,128)}, f32[32,24,256]{2,1,0:T(8,128)}, u32[]{:S(2)}, u32[]{:S(2)}) collective-permute-start(f32[32,24,256]{2,1,0:T(8,128)} %get-tuple-element.44), channel_id=1, source_target_pairs={{0,2},{2,4},{4,6},{6,8},{8,10},{10,12},{12,14},{14,16},{16,18},{18... | collective-permute-start | bytes 2359304 | tf_op jit(solution)/shard_map/ppermute | solution.py:587

commit v13 on v12

--- a/solution.py
+++ b/solution.py
@@ -15,7 +15,7 @@
 MY = 16
 MZ = 16
 CH = 32
-VMEM_BYTES = 16 * 1024 * 1024
+VMEM_BYTES = 20 * 1024 * 1024
 BF = jnp.bfloat16
 F32 = jnp.float32
 
@@ -239,42 +239,43 @@
         copy.wait()
 
 
-def own_kernel(segments, weight, point, field, *refs):
+def own_kernel(segments, groups, weight, point, field, halo, *refs):
     last = field.shape[1] // 8 - 1
-    outer = segments[0][0] == 0
-    few = [(weight, refs[-9]), (point, refs[-8])]
-    if outer:
-        few.append((refs[0], refs[-10]))
-        refs = refs[1:]
+    count = 3 * len(groups)
     outs, (taken, halo_rows, weights, points, sent, lined, depth, gains, sem_in, sem_out, sem_few) = (
-        refs[:3],
-        refs[3:],
+        refs[:count],
+        refs[count:],
     )
-    few = [pltpu.make_async_copy(src, dst, sem_few.at[i]) for i, (src, dst) in enumerate(few)]
+    few = [
+        pltpu.make_async_copy(src, dst, sem_few.at[i])
+        for i, (src, dst) in enumerate(((weight, weights), (point, points), (halo, halo_rows)))
+    ]
+    for copy in few:
+        copy.start()
     wanted = sorted({t for tiles in segments for t in (tiles[0] - 1, *tiles, tiles[-1] + 1) if 0 <= t <= last})
     row = fetch_tiles(field, taken, sem_in, wanted)
     for copy in few:
-        copy.start()
-    for copy in few:
         copy.wait()
     spread_gains(weights, gains, range(3))
     mix = mixing(points[...])
-    runs, at, done = [], 0, 0
+    runs, at, done, order = [], 0, 0, []
     for tiles in segments:
         places = [(tiles[0] - 1, 7), *[(t, r) for t in tiles for r in range(8)], (tiles[-1] + 1, 0)]
         for i, (t, r) in enumerate(places):
             lined[at + i] = halo_rows[0] if t < 0 else halo_rows[1] if t > last else row(t, r)
         runs.append((at, done, 8 * len(tiles)))
         at, done = at + len(places), done + 8 * len(tiles)
+        order += tiles
     tap_sums(lambda s, r, c: lined[r, c, :], [[(a, a) for a in range(3)]], gains, depth, runs)
     copies = []
-    for t in range(done // 8):
-        for k, out in enumerate(outs):
-            sent[k, t] = mix_tile(mix, depth, k, t)
-            copies.append(
-                pltpu.make_async_copy(sent.at[k, t], out.at[:, pl.ds(8 * t, 8), :], sem_out.at[k, t])
-            )
-            copies[-1].start()
+    for g, tiles in enumerate(groups):
+        for i, tile in enumerate(tiles):
+            t = order.index(tile)
+            for k in range(3):
+                sent[k, t] = mix_tile(mix, depth, k, t)
+                to = outs[3 * g + k].at[:, pl.ds(8 * i, 8), :]
+                copies.append(pltpu.make_async_copy(sent.at[k, t], to, sem_out.at[k, t]))
+                copies[-1].start()
     for copy in copies:
         copy.wait()
 
@@ -492,15 +493,16 @@
     )(*in_hbm(field))
 
 
-def own_call(field, weight, point, segments, halo=()):
+def own_call(field, halo, weight, point, segments, groups):
     tiles = sum(map(len, segments))
     rows, fetched = 8 * tiles, tiles + 2 * len(segments)
     hbm = pl.BlockSpec(memory_space=pltpu.HBM)
+    shapes = [pltpu.HBM((CH, 8 * len(group), NX), F32) for group in groups for _ in range(3)]
     return pl.pallas_call(
-        functools.partial(own_kernel, segments),
-        out_shape=[pltpu.HBM((CH, rows, NX), F32)] * 3,
-        in_specs=[hbm] * (3 + len(halo)),
-        out_specs=[hbm] * 3,
+        functools.partial(own_kernel, segments, groups),
+        out_shape=shapes,
+        in_specs=[hbm] * 4,
+        out_specs=[hbm] * len(shapes),
         scratch_shapes=[
             pltpu.VMEM((fetched, 2, CH, 8, 128), F32),
             pltpu.VMEM((2, CH, NX), F32),
@@ -517,7 +519,7 @@
         compiler_params=params(),
         cost_estimate=cost(10**8, 2**18),
         name="own_sums",
-    )(*in_hbm(weight, point, field, *halo))
+    )(*in_hbm(weight, point, field, halo))
 
 
 def middle_call(weight, point, low, own, high):
@@ -594,8 +596,7 @@
     last = y_local // 8 - 1
     cut = 1 + last // 2
     first_tiles, second_tiles = tuple(range(1, cut)), tuple(range(cut, min(cut + 2, last)))
-    outer_tiles = ((0,), tuple(range(second_tiles[-1] + 1, last + 1)))
-    sums = functools.partial(own_call, weight=depth_weight, point=point_weight)
+    third_tiles = (0, *range(second_tiles[-1] + 1, last + 1))
     packed, edges = pack_call(field, first_tiles)
     first_low, first_high = to_neighbours(packed, packed)
     if gy == 2:
@@ -609,21 +610,23 @@
         )
     j_own, n_own = spectral_filter.shape[2], spectral_filter.shape[3]
     whole_tiles = j_own == 8 and n_own == 2 * MX
-    coarse = forward_call(after(field, packed), gy, whole_tiles)
-    down, second, up = sums(after(field, coarse), segments=(second_tiles,))
+    coarse = after(forward_call(after(field, packed), gy, whole_tiles), halo)
+    segments, groups = ((0,), tuple(range(cut, last + 1))), (second_tiles, third_tiles)
+    down, second, up, outer_down, own, outer_up = own_call(
+        after(field, coarse), halo, depth_weight, point_weight, segments, groups
+    )
     if whole_tiles:
         both = ("gz", "gy")
         got = lax.all_to_all(coarse, both, split_axis=0, concat_axis=0, tiled=True)
         pair = to_neighbours(after(down, got), after(up, got))
-        gains = after(spectral_filter, first_low, first_high, second, halo)
+        gains = after(spectral_filter, first_low, first_high, second)
         mark = filter_call(got, gains, gz, gy, forward_scale)
         back = lax.all_to_all(mark, both, split_axis=0, concat_axis=0, tiled=True)
         back = back.reshape(CH // 2, MY, 4 * MX)
     else:
         pair = to_neighbours(down, up)
         mark = back = general_filter(coarse, spectral_filter, gz, gy, forward_scale)
-    down, own, up = sums(after(field, mark), segments=outer_tiles, halo=(halo,))
-    outer_pair = to_neighbours(after(down, back), after(up, back))
+    outer_pair = to_neighbours(after(outer_down, mark), after(outer_up, mark))
     packed, *pair = lax.optimization_barrier((packed, *pair, back))[:-1]
     mixed = middle_call(depth_weight, point_weight, first_low, packed, first_high)
     result, base = inverse_call(

time: 71 us -> 65.4 us (0.921)
  Pallas kernels: 33.5 us -> 30.6 us
  starting transfers between devices: 24.6 us -> 23.2 us
  waiting for transfers between devices: 12.3 us -> 11 us
    ppermute x3, waiting for transfers between devices: 7.66 us -> 2.16 us  [to_neighbours(): lax.ppermute(up, 'gz', ring('gz', gz, -1))]
    all_to_all x1, waiting for transfers between devices: 2.18 us -> 6.46 us  [body(): back = lax.all_to_all(mark, both, split_axis=0, concat_axis=0, tiled=True)]
    pallas_call x2 -> x1, Pallas kernels: 10.4 us -> 7.56 us  [own_call(): pl.pallas_call(functools.partial(own_kernel, segments, groups), out_shape...]
    all_to_all x1, waiting for transfers between devices: 2.44 us -> 0.91 us  [body(): got = lax.all_to_all(coarse, both, split_axis=0, concat_axis=0, tiled=True)]
    ppermute x3, waiting for transfers between devices: 0.01 us -> 1.43 us  [to_neighbours(): lax.ppermute(down, 'gz', ring('gz', gz, 1))]
    ppermute x3, starting transfers between devices: 1.8 us -> 0.63 us  [to_neighbours(): lax.ppermute(up, 'gz', ring('gz', gz, -1))]
    ppermute x3, starting transfers between devices: 4.55 us -> 5.55 us  [to_neighbours(): lax.ppermute(down, 'gz', ring('gz', gz, 1))]
    all_to_all x1, starting transfers between devices: 8.29 us -> 7.36 us  [body(): got = lax.all_to_all(coarse, both, split_axis=0, concat_axis=0, tiled=True)]
  transfers between devices with their start and end apart: 9 -> 9, of which waited for: 3 -> 4; matrix products, arithmetic and copies ran while one was open for 0% -> 0% of each run, Pallas kernels for 40% -> 40%
where the time goes in v13:
time: 65.4 us; the launch traced here: 64.9 us
  Pallas kernels  30.6 us (47%)
  starting transfers between devices  23.2 us (35%)
  waiting for transfers between devices  11 us (17%)
    all_to_all x1, starting transfers between devices, body(): back = lax.all_to_all(mark, both, split_axis=0, concat_axis=0, tiled=True)  8.43 us
    pallas_call x1, Pallas kernels, own_call(): pl.pallas_call(functools.partial(own_kernel, segments, groups), out_shape...  7.56 us
    all_to_all x1, starting transfers between devices, body(): got = lax.all_to_all(coarse, both, split_axis=0, concat_axis=0, tiled=True)  7.36 us
    all_to_all x1, waiting for transfers between devices, body(): back = lax.all_to_all(mark, both, split_axis=0, concat_axis=0, tiled=True)  6.46 us
    pallas_call x1, Pallas kernels, inverse_call(): pl.pallas_call(functools.partial(inverse_kernel, upper), out_shape=[jax.S...  5.86 us
    ppermute x3, starting transfers between devices, to_neighbours(): lax.ppermute(down, 'gz', ring('gz', gz, 1))  5.55 us
    pallas_call x1, Pallas kernels, middle_call(): pl.pallas_call(middle_kernel, out_shape=pltpu.HBM((CH, rows, NX), F32), i...  4.89 us
    pallas_call x1, Pallas kernels, forward_call(): pl.pallas_call(forward_kernel, out_shape=(pltpu.HBM if pinned else jax.Sh...  4.13 us
  transfers between devices with their start and end apart: 9, of which 4 were waited for; matrix products, arithmetic and copies ran while one was open for 0% of the time, Pallas kernels for 40%

profile of v13, /device:TPU:1, one launch (start us, length us, event | category | flops | bytes accessed | tf_op | source)
XLA Modules:
  0.0 64.9 jit_solution(1458742194533602117)
XLA Ops:
  0.0 2.3 %packed_rows.1 = (f32[26,32,256]{2,1,0:T(8,128)}, f32[2,32,256]{2,1,0:T(8,128)}) custom-call(f32[32,64,256]{2,1,0:T(8,128)} %bitcast.19), custom_call_target="tpu_custom_call" | custom-call | flops 100000000 | bytes 262144 | tf_op jit(solution)/shard_map/packed_rows/pallas_call | solution.py:478
  2.3 0.1 collective-permute-start.2
  2.4 2.6 %collective-permute-start.1 = (f32[26,32,256]{2,1,0:T(8,128)}, f32[26,32,256]{2,1,0:T(8,128)S(1)}, u32[]{:S(2)}, u32[]{:S(2)}) collective-permute-start(f32[26,32,256]{2,1,0:T(8,128)} %get-tuple-element.38.own), channel_id=1, source_target_pairs={{0,2},{2,4},{4,6},{6,8},{8,10},{10,12},{12,14},{14,16},{16,18},{18... | collective-permute-start | bytes 2555912 | tf_op jit(solution)/shard_map/ppermute | solution.py:589
  5.1 1.2 %collective-permute-start = (f32[2,32,256]{2,1,0:T(8,128)}, f32[2,32,256]{2,1,0:T(8,128)S(1)}, u32[]{:S(2)}, u32[]{:S(2)}) collective-permute-start(f32[2,32,256]{2,1,0:T(8,128)} %get-tuple-element.28), channel_id=1, source_target_pairs={{0,1},{1,0},{2,3},{3,2},{4,5},{5,4},{6,7},{7,6},{8,9},{9,8},{10,11... | collective-permute-start | bytes 196616 | tf_op jit(solution)/shard_map/ppermute | solution.py:603
  6.3 4.1 %forward_modes.1 = f32[256,128]{1,0:T(8,128)} custom-call(f32[8,4,64,256]{3,2,1,0:T(8,128)} %bitcast.20, bf16[2,256,128]{2,1,0:T(8,128)(2,1)} %constant.24.clone.x_top, bf16[2,256,128]{2,1,0:T(8,128)(2,1)} %constant.25.clone.x_rest, bf16[2,32,64]{2,1,0:T(8,128)(2,1)} %constant.26.clone.y_top, bf16[2,32,64]{2,1,0:T(8,128)(2,1)} %constant.27.clone.y_rest), custom_call_target="tpu_custom_call" | custom-call | flops 100000000 | bytes 262144 | tf_op jit(solution)/shard_map/forward_modes/pallas_call | solution.py:398
  10.4 0.0 collective-permute-done.halo
  10.4 0.0 copy-start
  10.4 7.4 %all-to-all-start = ((f32[32,8,128]{2,1,0:T(8,128)}), f32[32,8,128]{2,1,0:T(8,128)S(1)}, u32[]{:S(2)}, u32[]{:S(2)}) async-start(f32[32,8,128]{2,1,0:T(8,128)} %bitcast.25), calls=%async_computation | async-start | bytes 262144 | tf_op jit(solution)/shard_map/all_to_all | solution.py:620
  17.8 0.0 copy-done
  17.8 7.6 %own_sums.1 = (f32[32,16,256]{2,1,0:T(8,128)}, f32[32,16,256]{2,1,0:T(8,128)}, f32[32,16,256]{2,1,0:T(8,128)}, f32[32,24,256]{2,1,0:T(8,128)}, f32[32,24,256]{2,1,0:T(8,128)}, /*index=5*/f32[32,24,256]{2,1,0:T(8,128)}) custom-call(f32[32,27]{1,0:T(8,128)} %weight.3, f32[32,32]{1,0:T(8,128)} %point.3, f32[32,64,256]{2,1,0:T(8,128)} %bitcast.21, ...), custom_call_target="tpu_custom_call" | custom-call | flops 100000000 | bytes 262144 | tf_op jit(solution)/shard_map/own_sums/pallas_call | solution.py:501
  25.4 0.9 %all-to-all-done = f32[32,8,128]{2,1,0:T(8,128)S(1)} async-done(((f32[32,8,128]{2,1,0:T(8,128)}), f32[32,8,128]{2,1,0:T(8,128)S(1)}, u32[]{:S(2)}, u32[]{:S(2)}) %all-to-all-start) | async-done | bytes 131104 | tf_op jit(solution)/shard_map/all_to_all | solution.py:620
  26.3 0.5 collective-permute-start.4
  26.8 1.2 %collective-permute-start.3 = (f32[32,16,256]{2,1,0:T(8,128)}, f32[32,16,256]{2,1,0:T(8,128)}, u32[]{:S(2)}, u32[]{:S(2)}) collective-permute-start(f32[32,16,256]{2,1,0:T(8,128)} %get-tuple-element.35), channel_id=1, source_target_pairs={{0,2},{2,4},{4,6},{6,8},{8,10},{10,12},{12,14},{14,16},{16,18},{18... | collective-permute-start | bytes 1572872 | tf_op jit(solution)/shard_map/ppermute | solution.py:589
  28.0 0.0 collective-permute-done.2.high
  28.0 0.0 copy-start.1
  28.0 0.0 collective-permute-done.1.low
  28.0 0.0 copy-start.2
  28.0 3.3 %filter_modes.1 = f32[256,128]{1,0:T(8,128)} custom-call(f32[256,128]{1,0:T(8,128)S(1)} %bitcast.18, f32[2,16,8,64]{3,2,1,0:T(8,128)} %gains, bf16[256,256]{1,0:T(8,128)(2,1)} %constant.28.clone.f_top, bf16[256,256]{1,0:T(8,128)(2,1)} %constant.29.clone.f_rest, bf16[512,128]{1,0:T(8,128)(2,1)} %constant.30.clone.i_top, bf16[512,128]{1,0:T(8,128)(2,1)} %constant.31.clone.i_rest), custom_call_target="tpu_custom_call" | custom-call | flops 199999995904 | bytes 262144 | tf_op jit(solution)/shard_map/filter_modes/pallas_call | solution.py:417
  31.3 0.0 copy-done.1
  31.3 0.0 copy-done.2
  31.3 8.4 %all-to-all-start.1 = ((f32[32,8,128]{2,1,0:T(8,128)}), f32[32,8,128]{2,1,0:T(8,128)S(1)}, u32[]{:S(2)}, u32[]{:S(2)}) async-start(f32[32,8,128]{2,1,0:T(8,128)} %bitcast.27), calls=%async_computation.1 | async-start | bytes 262144 | tf_op jit(solution)/shard_map/all_to_all | solution.py:624
  39.8 1.7 %collective-permute-start.5 = (f32[32,24,256]{2,1,0:T(8,128)}, f32[32,24,256]{2,1,0:T(8,128)}, u32[]{:S(2)}, u32[]{:S(2)}) collective-permute-start(f32[32,24,256]{2,1,0:T(8,128)} %get-tuple-element.44), channel_id=1, source_target_pairs={{0,2},{2,4},{4,6},{6,8},{8,10},{10,12},{12,14},{14,16},{16,18},{18... | collective-permute-start | bytes 2359304 | tf_op jit(solution)/shard_map/ppermute | solution.py:589
  41.4 0.0 collective-permute-start.6
  41.4 0.0 collective-permute-done.4
  41.4 0.0 collective-permute-done.3
  41.4 6.5 %all-to-all-done.1 = f32[32,8,128]{2,1,0:T(8,128)S(1)} async-done(((f32[32,8,128]{2,1,0:T(8,128)}), f32[32,8,128]{2,1,0:T(8,128)S(1)}, u32[]{:S(2)}, u32[]{:S(2)}) %all-to-all-start.1) | async-done | bytes 131104 | tf_op jit(solution)/shard_map/all_to_all | solution.py:624
  47.9 4.9 %middle_sums.1 = f32[32,24,256]{2,1,0:T(8,128)} custom-call(f32[32,27]{1,0:T(8,128)} %weight.3, f32[32,32]{1,0:T(8,128)} %point.3, f32[26,32,256]{2,1,0:T(8,128)} %copy-done.2, f32[26,32,256]{2,1,0:T(8,128)} %get-tuple-element.38.own, f32[26,32,256]{2,1,0:T(8,128)} %copy-done.1), custom_call_target="tpu_custom_call" | custom-call | flops 199999995904 | bytes 262144 | tf_op jit(solution)/shard_map/middle_sums/pallas_call | solution.py:528
  52.8 5.9 %inverse_modes.1 = (f32[8,4,64,256]{3,2,1,0:T(8,128)}, f32[8,4,24,256]{3,2,1,0:T(8,128)S(1)}) custom-call(f32[16,16,128]{2,1,0:T(8,128)S(1)} %bitcast.17, f32[32]{0:T(128)} %bias.1, bf16[2,128,256]{2,1,0:T(8,128)(2,1)} %constant.32.clone.x_top, bf16[2,128,256]{2,1,0:T(8,128)(2,1)} %constant.33.clone.x_rest, bf16[2,64,32]{2,1,0:T(8,128)(2,1)} %constant.34.clone.y_top, ...), custom_call_target="tpu_custom_call" | custom-call | flops 100000000 | bytes 262144 | tf_op jit(solution)/shard_map/inverse_modes/pallas_call | solution.py:431
  58.7 1.4 %collective-permute-done.5.low = f32[32,24,256]{2,1,0:T(8,128)} collective-permute-done((f32[32,24,256]{2,1,0:T(8,128)}, f32[32,24,256]{2,1,0:T(8,128)}, u32[]{:S(2)}, u32[]{:S(2)}) %collective-permute-start.5) | collective-permute-done | bytes 786464 | tf_op jit(solution)/shard_map/ppermute | solution.py:589
  60.1 2.2 %collective-permute-done.6.high = f32[32,24,256]{2,1,0:T(8,128)} collective-permute-done((f32[32,24,256]{2,1,0:T(8,128)}, f32[32,24,256]{2,1,0:T(8,128)}, u32[]{:S(2)}, u32[]{:S(2)}) %collective-permute-start.6) | collective-permute-done | bytes 786464 | tf_op jit(solution)/shard_map/ppermute | solution.py:590
  62.3 2.6 %finished_rows.1 = f32[32,64,256]{2,1,0:T(8,128)} custom-call(f32[32,64,256]{2,1,0:T(8,128)} %bitcast.22, f32[32,24,256]{2,1,0:T(8,128)S(1)} %bitcast.16, f32[32,24,256]{2,1,0:T(8,128)} %collective-permute-done.5.low, f32[32,24,256]{2,1,0:T(8,128)} %collective-permute-done.6.high), custom_call_target="tpu_custom_call", output_to_operand_aliasing={{}: (0, {})} | custom-call | flops 100000000 | bytes 262144 | tf_op jit(solution)/shard_map/finished_rows/pallas_call | solution.py:456
Async XLA Ops:
  2.3 25.7 %collective-permute-start.2 = (f32[26,32,256]{2,1,0:T(8,128)}, f32[26,32,256]{2,1,0:T(8,128)S(1)}, u32[]{:S(2)}, u32[]{:S(2)}) collective-permute-start(f32[26,32,256]{2,1,0:T(8,128)} %get-tuple-element.38.own), channel_id=1, source_target_pairs={{0,30},{2,0},{4,2},{6,4},{8,6},{10,8},{12,10},{14,12},{16,14},{18,... | collective-permute-start | bytes 2555912 | tf_op jit(solution)/shard_map/ppermute | solution.py:590
  2.4 25.6 %collective-permute-start.1 = (f32[26,32,256]{2,1,0:T(8,128)}, f32[26,32,256]{2,1,0:T(8,128)S(1)}, u32[]{:S(2)}, u32[]{:S(2)}) collective-permute-start(f32[26,32,256]{2,1,0:T(8,128)} %get-tuple-element.38.own), channel_id=1, source_target_pairs={{0,2},{2,4},{4,6},{6,8},{8,10},{10,12},{12,14},{14,16},{16,18},{18... | collective-permute-start | bytes 2555912 | tf_op jit(solution)/shard_map/ppermute | solution.py:589
  5.1 5.4 %collective-permute-start = (f32[2,32,256]{2,1,0:T(8,128)}, f32[2,32,256]{2,1,0:T(8,128)S(1)}, u32[]{:S(2)}, u32[]{:S(2)}) collective-permute-start(f32[2,32,256]{2,1,0:T(8,128)} %get-tuple-element.28), channel_id=1, source_target_pairs={{0,1},{1,0},{2,3},{3,2},{4,5},{5,4},{6,7},{7,6},{8,9},{9,8},{10,11... | collective-permute-start | bytes 196616 | tf_op jit(solution)/shard_map/ppermute | solution.py:603
  10.4 7.4 %copy-start = (f32[2,32,256]{2,1,0:T(8,128)}, f32[2,32,256]{2,1,0:T(8,128)S(1)}, u32[]{:S(2)}) copy-start(f32[2,32,256]{2,1,0:T(8,128)S(1)} %collective-permute-done.halo) | copy-start | bytes 196612
  10.4 15.9 %all-to-all-start = ((f32[32,8,128]{2,1,0:T(8,128)}), f32[32,8,128]{2,1,0:T(8,128)S(1)}, u32[]{:S(2)}, u32[]{:S(2)}) async-start(f32[32,8,128]{2,1,0:T(8,128)} %bitcast.25), calls=%async_computation | async-start | bytes 262144 | tf_op jit(solution)/shard_map/all_to_all | solution.py:620
  26.3 15.2 %collective-permute-start.4 = (f32[32,16,256]{2,1,0:T(8,128)}, f32[32,16,256]{2,1,0:T(8,128)}, u32[]{:S(2)}, u32[]{:S(2)}) collective-permute-start(f32[32,16,256]{2,1,0:T(8,128)} %get-tuple-element.37), channel_id=1, source_target_pairs={{0,30},{2,0},{4,2},{6,4},{8,6},{10,8},{12,10},{14,12},{16,14},{18,... | collective-permute-start | bytes 1572872 | tf_op jit(solution)/shard_map/ppermute | solution.py:590
  26.8 14.7 %collective-permute-start.3 = (f32[32,16,256]{2,1,0:T(8,128)}, f32[32,16,256]{2,1,0:T(8,128)}, u32[]{:S(2)}, u32[]{:S(2)}) collective-permute-start(f32[32,16,256]{2,1,0:T(8,128)} %get-tuple-element.35), channel_id=1, source_target_pairs={{0,2},{2,4},{4,6},{6,8},{8,10},{10,12},{12,14},{14,16},{16,18},{18... | collective-permute-start | bytes 1572872 | tf_op jit(solution)/shard_map/ppermute | solution.py:589
  28.0 3.3 %copy-start.1 = (f32[26,32,256]{2,1,0:T(8,128)}, f32[26,32,256]{2,1,0:T(8,128)S(1)}, u32[]{:S(2)}) copy-start(f32[26,32,256]{2,1,0:T(8,128)S(1)} %collective-permute-done.2.high) | copy-start | bytes 2555908
  28.0 3.3 %copy-start.2 = (f32[26,32,256]{2,1,0:T(8,128)}, f32[26,32,256]{2,1,0:T(8,128)S(1)}, u32[]{:S(2)}) copy-start(f32[26,32,256]{2,1,0:T(8,128)S(1)} %collective-permute-done.1.low) | copy-start | bytes 2555908
  31.3 16.6 %all-to-all-start.1 = ((f32[32,8,128]{2,1,0:T(8,128)}), f32[32,8,128]{2,1,0:T(8,128)S(1)}, u32[]{:S(2)}, u32[]{:S(2)}) async-start(f32[32,8,128]{2,1,0:T(8,128)} %bitcast.27), calls=%async_computation.1 | async-start | bytes 262144 | tf_op jit(solution)/shard_map/all_to_all | solution.py:624
  39.8 20.3 %collective-permute-start.5 = (f32[32,24,256]{2,1,0:T(8,128)}, f32[32,24,256]{2,1,0:T(8,128)}, u32[]{:S(2)}, u32[]{:S(2)}) collective-permute-start(f32[32,24,256]{2,1,0:T(8,128)} %get-tuple-element.44), channel_id=1, source_target_pairs={{0,2},{2,4},{4,6},{6,8},{8,10},{10,12},{12,14},{14,16},{16,18},{18... | collective-permute-start | bytes 2359304 | tf_op jit(solution)/shard_map/ppermute | solution.py:589
  41.4 20.8 %collective-permute-start.6 = (f32[32,24,256]{2,1,0:T(8,128)}, f32[32,24,256]{2,1,0:T(8,128)}, u32[]{:S(2)}, u32[]{:S(2)}) collective-permute-start(f32[32,24,256]{2,1,0:T(8,128)} %get-tuple-element.46), channel_id=1, source_target_pairs={{0,30},{2,0},{4,2},{6,4},{8,6},{10,8},{12,10},{14,12},{16,14},{18,... | collective-permute-start | bytes 2359304 | tf_op jit(solution)/shard_map/ppermute | solution.py:590

commit v14 on v13

--- a/solution.py
+++ b/solution.py
@@ -346,28 +346,17 @@
         base[g, 0, upper:] = plane[stop:] + own[g, 0, upper:]
 
 
-def finish_kernel(upper, _, base, low, high, out, held, sent, sem_in, sem_out):
+def finish_kernel(upper, _, base, low, high, out, sent, sem):
     tiles = base.shape[1] // 8
     gap = out.shape[1] // 8 - tiles
-    arrivals = [
-        [
-            pltpu.make_async_copy(src.at[:, pl.ds(8 * t, 8), :], held.at[i, t], sem_in.at[i, t])
-            for i, src in enumerate((base, low, high))
-        ]
-        for t in range(tiles)
-    ]
-    for copies in arrivals:
-        for copy in copies:
-            copy.start()
-    done = []
+    copies = []
     for t in range(tiles):
-        for copy in arrivals[t]:
-            copy.wait()
-        sent[t] = gelu(held[0, t] + (held[1, t] + held[2, t]))
+        rows = pl.ds(8 * t, 8)
+        sent[t] = gelu(base[:, rows, :] + (low[:, rows, :] + high[:, rows, :]))
         to = t if t < upper else t + gap
-        done.append(pltpu.make_async_copy(sent.at[t], out.at[:, pl.ds(8 * to, 8), :], sem_out.at[t]))
-        done[-1].start()
-    for copy in done:
+        copies.append(pltpu.make_async_copy(sent.at[t], out.at[:, pl.ds(8 * to, 8), :], sem.at[t]))
+        copies[-1].start()
+    for copy in copies:
         copy.wait()
 
 
@@ -418,7 +407,7 @@
         filter_kernel,
         out_shape=pltpu.HBM(arrived.shape, F32),
         compiler_params=params(),
-        cost_estimate=cost(2 * 10**11, 2**18),
+        cost_estimate=cost(4 * 10**10, 2**18),
         name="filter_modes",
     )(arrived, *in_hbm(gains, *fwd, *inv))
 
@@ -453,15 +442,14 @@
 def finish_call(result, base, low, high, upper):
     tiles = base.shape[1] // 8
     anywhere = pl.BlockSpec(memory_space=pl.ANY)
+    vmem = pl.BlockSpec(memory_space=pltpu.VMEM)
     return pl.pallas_call(
         functools.partial(finish_kernel, upper),
         out_shape=jax.ShapeDtypeStruct(result.shape, F32),
-        in_specs=[anywhere] * 4,
+        in_specs=[anywhere] + [vmem] * 3,
         out_specs=anywhere,
         scratch_shapes=[
-            pltpu.VMEM((3, tiles, CH, 8, NX), F32),
             pltpu.VMEM((tiles, CH, 8, NX), F32),
-            pltpu.SemaphoreType.DMA((3, tiles)),
             pltpu.SemaphoreType.DMA((tiles,)),
         ],
         input_output_aliases={0: 0},
@@ -501,7 +489,7 @@
     return pl.pallas_call(
         functools.partial(own_kernel, segments, groups),
         out_shape=shapes,
-        in_specs=[hbm] * 4,
+        in_specs=[hbm] * 3 + [pl.BlockSpec(memory_space=pl.ANY)],
         out_specs=[hbm] * len(shapes),
         scratch_shapes=[
             pltpu.VMEM((fetched, 2, CH, 8, 128), F32),
@@ -519,7 +507,7 @@
         compiler_params=params(),
         cost_estimate=cost(10**8, 2**18),
         name="own_sums",
-    )(*in_hbm(weight, point, field, halo))
+    )(*in_hbm(weight, point, field), halo)
 
 
 def middle_call(weight, point, low, own, high):
@@ -528,7 +516,7 @@
     return pl.pallas_call(
         middle_kernel,
         out_shape=pltpu.HBM((CH, rows, NX), F32),
-        in_specs=[hbm] * 5,
+        in_specs=[hbm] * 2 + [pl.BlockSpec(memory_space=pl.ANY)] * 3,
         out_specs=hbm,
         scratch_shapes=[
             pltpu.VMEM((3, rows + 2, CH, NX), F32),
@@ -541,9 +529,9 @@
             pltpu.SemaphoreType.DMA((rows // 8,)),
         ],
         compiler_params=params(),
-        cost_estimate=cost(2 * 10**11, 2**18),
+        cost_estimate=cost(4 * 10**10, 2**18),
         name="middle_sums",
-    )(*in_hbm(weight, point, low, own, high))
+    )(*in_hbm(weight, point), low, *in_hbm(own), high)
 
 
 def general_filter(coarse, gains, gz, gy, scale):

time: 65.4 us -> 64.1 us (0.980)
  local copies, waits for them, and re-layouts: 0.01 us -> 2.32 us
  Pallas kernels: 30.6 us -> 28.5 us
  waiting for transfers between devices: 11 us -> 9.52 us
    unnamed x6 -> x8, local copies, waits for them, and re-layouts: 0.01 us -> 2.32 us
    ppermute x3, waiting for transfers between devices: 1.43 us -> 0.01 us  [to_neighbours(): lax.ppermute(down, 'gz', ring('gz', gz, 1))]
    pallas_call x1, Pallas kernels: 2.65 us -> 1.47 us  [finish_call(): pl.pallas_call(functools.partial(finish_kernel, upper), out_shape=jax.Sha...]
  transfers between devices with their start and end apart: 9 -> 9, of which waited for: 4 -> 3; matrix products, arithmetic and copies ran while one was open for 0% -> 0% of each run, Pallas kernels for 40% -> 39%
where the time goes in v14:
time: 64.1 us; the launch traced here: 63.6 us
  Pallas kernels  28.5 us (44%)
  starting transfers between devices  23.2 us (36%)
  waiting for transfers between devices  9.52 us (15%)
  local copies, waits for them, and re-layouts  2.32 us (4%)
    all_to_all x1, starting transfers between devices, body(): back = lax.all_to_all(mark, both, split_axis=0, concat_axis=0, tiled=True)  8.43 us
    all_to_all x1, starting transfers between devices, body(): got = lax.all_to_all(coarse, both, split_axis=0, concat_axis=0, tiled=True)  7.36 us
    pallas_call x1, Pallas kernels, own_call(): pl.pallas_call(functools.partial(own_kernel, segments, groups), out_shape...  7.15 us
    all_to_all x1, waiting for transfers between devices, body(): back = lax.all_to_all(mark, both, split_axis=0, concat_axis=0, tiled=True)  6.46 us
    pallas_call x1, Pallas kernels, inverse_call(): pl.pallas_call(functools.partial(inverse_kernel, upper), out_shape=[jax.S...  5.69 us
    ppermute x3, starting transfers between devices, to_neighbours(): lax.ppermute(down, 'gz', ring('gz', gz, 1))  5.55 us
    pallas_call x1, Pallas kernels, middle_call(): pl.pallas_call(middle_kernel, out_shape=pltpu.HBM((CH, rows, NX), F32), i...  4.51 us
    pallas_call x1, Pallas kernels, forward_call(): pl.pallas_call(forward_kernel, out_shape=(pltpu.HBM if pinned else jax.Sh...  4.14 us
  transfers between devices with their start and end apart: 9, of which 3 were waited for; matrix products, arithmetic and copies ran while one was open for 0% of the time, Pallas kernels for 39%

profile of v14, /device:TPU:1, one launch (start us, length us, event | category | flops | bytes accessed | tf_op | source)
XLA Modules:
  0.0 63.6 jit_solution(625598943633150645)
XLA Ops:
  0.0 2.3 %packed_rows.1 = (f32[26,32,256]{2,1,0:T(8,128)}, f32[2,32,256]{2,1,0:T(8,128)}) custom-call(f32[32,64,256]{2,1,0:T(8,128)} %bitcast.21), custom_call_target="tpu_custom_call" | custom-call | flops 100000000 | bytes 262144 | tf_op jit(solution)/shard_map/packed_rows/pallas_call | solution.py:466
  2.3 0.1 collective-permute-start.2
  2.4 2.6 %collective-permute-start.1 = (f32[26,32,256]{2,1,0:T(8,128)}, f32[26,32,256]{2,1,0:T(8,128)S(1)}, u32[]{:S(2)}, u32[]{:S(2)}) collective-permute-start(f32[26,32,256]{2,1,0:T(8,128)} %get-tuple-element.38.own), channel_id=1, source_target_pairs={{0,2},{2,4},{4,6},{6,8},{8,10},{10,12},{12,14},{14,16},{16,18},{18... | collective-permute-start | bytes 2555912 | tf_op jit(solution)/shard_map/ppermute | solution.py:577
  5.0 1.2 %collective-permute-start = (f32[2,32,256]{2,1,0:T(8,128)}, f32[2,32,256]{2,1,0:T(8,128)S(1)}, u32[]{:S(2)}, u32[]{:S(2)}) collective-permute-start(f32[2,32,256]{2,1,0:T(8,128)} %get-tuple-element.28), channel_id=1, source_target_pairs={{0,1},{1,0},{2,3},{3,2},{4,5},{5,4},{6,7},{7,6},{8,9},{9,8},{10,11... | collective-permute-start | bytes 196616 | tf_op jit(solution)/shard_map/ppermute | solution.py:591
  6.3 4.1 %forward_modes.1 = f32[256,128]{1,0:T(8,128)} custom-call(f32[8,4,64,256]{3,2,1,0:T(8,128)} %bitcast.22, bf16[2,256,128]{2,1,0:T(8,128)(2,1)} %constant.24.clone.x_top, bf16[2,256,128]{2,1,0:T(8,128)(2,1)} %constant.25.clone.x_rest, bf16[2,32,64]{2,1,0:T(8,128)(2,1)} %constant.26.clone.y_top, bf16[2,32,64]{2,1,0:T(8,128)(2,1)} %constant.27.clone.y_rest), custom_call_target="tpu_custom_call" | custom-call | flops 100000000 | bytes 262144 | tf_op jit(solution)/shard_map/forward_modes/pallas_call | solution.py:387
  10.4 0.0 collective-permute-done.halo
  10.4 7.4 %all-to-all-start = ((f32[32,8,128]{2,1,0:T(8,128)}), f32[32,8,128]{2,1,0:T(8,128)S(1)}, u32[]{:S(2)}, u32[]{:S(2)}) async-start(f32[32,8,128]{2,1,0:T(8,128)} %bitcast.27), calls=%async_computation | async-start | bytes 262144 | tf_op jit(solution)/shard_map/all_to_all | solution.py:608
  17.8 7.1 %own_sums.1 = (f32[32,16,256]{2,1,0:T(8,128)}, f32[32,16,256]{2,1,0:T(8,128)}, f32[32,16,256]{2,1,0:T(8,128)}, f32[32,24,256]{2,1,0:T(8,128)}, f32[32,24,256]{2,1,0:T(8,128)}, /*index=5*/f32[32,24,256]{2,1,0:T(8,128)}) custom-call(f32[32,27]{1,0:T(8,128)} %weight.3, f32[32,32]{1,0:T(8,128)} %point.3, f32[32,64,256]{2,1,0:T(8,128)} %bitcast.23, ...), custom_call_target="tpu_custom_call" | custom-call | flops 100000000 | bytes 262144 | tf_op jit(solution)/shard_map/own_sums/pallas_call | solution.py:489
  24.9 1.3 %all-to-all-done = f32[32,8,128]{2,1,0:T(8,128)S(1)} async-done(((f32[32,8,128]{2,1,0:T(8,128)}), f32[32,8,128]{2,1,0:T(8,128)S(1)}, u32[]{:S(2)}, u32[]{:S(2)}) %all-to-all-start) | async-done | bytes 131104 | tf_op jit(solution)/shard_map/all_to_all | solution.py:608
  26.3 0.5 collective-permute-start.4
  26.8 1.2 %collective-permute-start.3 = (f32[32,16,256]{2,1,0:T(8,128)}, f32[32,16,256]{2,1,0:T(8,128)S(1)}, u32[]{:S(2)}, u32[]{:S(2)}) collective-permute-start(f32[32,16,256]{2,1,0:T(8,128)} %get-tuple-element.35), channel_id=1, source_target_pairs={{0,2},{2,4},{4,6},{6,8},{8,10},{10,12},{12,14},{14,16},{16,18},{18... | collective-permute-start | bytes 1572872 | tf_op jit(solution)/shard_map/ppermute | solution.py:577
  28.0 0.0 collective-permute-done.2.high
  28.0 0.0 copy-start
  28.0 0.0 collective-permute-done.1.low
  28.0 0.0 copy-start.2
  28.0 3.2 %filter_modes.1 = f32[256,128]{1,0:T(8,128)} custom-call(f32[256,128]{1,0:T(8,128)S(1)} %bitcast.20, f32[2,16,8,64]{3,2,1,0:T(8,128)} %gains, bf16[256,256]{1,0:T(8,128)(2,1)} %constant.28.clone.f_top, bf16[256,256]{1,0:T(8,128)(2,1)} %constant.29.clone.f_rest, bf16[512,128]{1,0:T(8,128)(2,1)} %constant.30.clone.i_top, bf16[512,128]{1,0:T(8,128)(2,1)} %constant.31.clone.i_rest), custom_call_target="tpu_custom_call" | custom-call | flops 40000000000 | bytes 262144 | tf_op jit(solution)/shard_map/filter_modes/pallas_call | solution.py:406
  31.3 0.0 copy-done
  31.3 0.0 copy-done.2
  31.3 8.4 %all-to-all-start.1 = ((f32[32,8,128]{2,1,0:T(8,128)}), f32[32,8,128]{2,1,0:T(8,128)S(1)}, u32[]{:S(2)}, u32[]{:S(2)}) async-start(f32[32,8,128]{2,1,0:T(8,128)} %bitcast.29), calls=%async_computation.1 | async-start | bytes 262144 | tf_op jit(solution)/shard_map/all_to_all | solution.py:612
  39.7 1.7 %collective-permute-start.5 = (f32[32,24,256]{2,1,0:T(8,128)}, f32[32,24,256]{2,1,0:T(8,128)S(1)}, u32[]{:S(2)}, u32[]{:S(2)}) collective-permute-start(f32[32,24,256]{2,1,0:T(8,128)} %get-tuple-element.44), channel_id=1, source_target_pairs={{0,2},{2,4},{4,6},{6,8},{8,10},{10,12},{12,14},{14,16},{16,18},{18... | collective-permute-start | bytes 2359304 | tf_op jit(solution)/shard_map/ppermute | solution.py:577
  41.4 0.0 collective-permute-start.6
  41.4 0.0 collective-permute-done.4
  41.4 0.0 collective-permute-done.3
  41.4 6.5 %all-to-all-done.1 = f32[32,8,128]{2,1,0:T(8,128)S(1)} async-done(((f32[32,8,128]{2,1,0:T(8,128)}), f32[32,8,128]{2,1,0:T(8,128)S(1)}, u32[]{:S(2)}, u32[]{:S(2)}) %all-to-all-start.1) | async-done | bytes 131104 | tf_op jit(solution)/shard_map/all_to_all | solution.py:612
  47.9 0.0 copy-start.1
  47.9 1.2 %copy-done.1 = f32[26,32,256]{2,1,0:T(8,128)S(1)} copy-done((f32[26,32,256]{2,1,0:T(8,128)S(1)}, f32[26,32,256]{2,1,0:T(8,128)}, u32[]{:S(2)}) %copy-start.1) | copy-done | bytes 851992
  49.1 1.2 %copy-done.3 = f32[26,32,256]{2,1,0:T(8,128)S(1)} copy-done((f32[26,32,256]{2,1,0:T(8,128)S(1)}, f32[26,32,256]{2,1,0:T(8,128)}, u32[]{:S(2)}) %copy-start.3) | copy-done | bytes 851992
  50.2 4.5 %middle_sums.1 = f32[32,24,256]{2,1,0:T(8,128)} custom-call(f32[32,27]{1,0:T(8,128)} %weight.3, f32[32,32]{1,0:T(8,128)} %point.3, f32[26,32,256]{2,1,0:T(8,128)S(1)} %copy-done.3, f32[26,32,256]{2,1,0:T(8,128)} %get-tuple-element.38.own, f32[26,32,256]{2,1,0:T(8,128)S(1)} %copy-done.1), custom_call_target="tpu_custom_call" | custom-call | flops 40000000000 | bytes 262144 | tf_op jit(solution)/shard_map/middle_sums/pallas_call | solution.py:516
  54.7 5.7 %inverse_modes.1 = (f32[8,4,64,256]{3,2,1,0:T(8,128)}, f32[8,4,24,256]{3,2,1,0:T(8,128)S(1)}) custom-call(f32[16,16,128]{2,1,0:T(8,128)S(1)} %bitcast.19, f32[32]{0:T(128)} %bias.1, bf16[2,128,256]{2,1,0:T(8,128)(2,1)} %constant.32.clone.x_top, bf16[2,128,256]{2,1,0:T(8,128)(2,1)} %constant.33.clone.x_rest, bf16[2,64,32]{2,1,0:T(8,128)(2,1)} %constant.34.clone.y_top, ...), custom_call_target="tpu_custom_call" | custom-call | flops 100000000 | bytes 262144 | tf_op jit(solution)/shard_map/inverse_modes/pallas_call | solution.py:420
  60.4 0.0 collective-permute-done.5.low
  60.4 1.7 %collective-permute-done.6.high = f32[32,24,256]{2,1,0:T(8,128)S(1)} collective-permute-done((f32[32,24,256]{2,1,0:T(8,128)}, f32[32,24,256]{2,1,0:T(8,128)S(1)}, u32[]{:S(2)}, u32[]{:S(2)}) %collective-permute-start.6) | collective-permute-done | bytes 786464 | tf_op jit(solution)/shard_map/ppermute | solution.py:578
  62.1 1.5 %finished_rows.1 = f32[32,64,256]{2,1,0:T(8,128)} custom-call(f32[32,64,256]{2,1,0:T(8,128)} %bitcast.24, f32[32,24,256]{2,1,0:T(8,128)S(1)} %bitcast.16, f32[32,24,256]{2,1,0:T(8,128)S(1)} %collective-permute-done.5.low, f32[32,24,256]{2,1,0:T(8,128)S(1)} %collective-permute-done.6.high), custom_call_target="tpu_custom_call", output_to_operand_aliasing={{}: (0, {})} | custom-call | flops 100000000 | bytes 262144 | tf_op jit(solution)/shard_map/finished_rows/pallas_call | solution.py:446
  (1 shorter events, 0.0 us)
Async XLA Ops:
  2.3 25.7 %collective-permute-start.2 = (f32[26,32,256]{2,1,0:T(8,128)}, f32[26,32,256]{2,1,0:T(8,128)S(1)}, u32[]{:S(2)}, u32[]{:S(2)}) collective-permute-start(f32[26,32,256]{2,1,0:T(8,128)} %get-tuple-element.38.own), channel_id=1, source_target_pairs={{0,30},{2,0},{4,2},{6,4},{8,6},{10,8},{12,10},{14,12},{16,14},{18,... | collective-permute-start | bytes 2555912 | tf_op jit(solution)/shard_map/ppermute | solution.py:578
  2.4 25.6 %collective-permute-start.1 = (f32[26,32,256]{2,1,0:T(8,128)}, f32[26,32,256]{2,1,0:T(8,128)S(1)}, u32[]{:S(2)}, u32[]{:S(2)}) collective-permute-start(f32[26,32,256]{2,1,0:T(8,128)} %get-tuple-element.38.own), channel_id=1, source_target_pairs={{0,2},{2,4},{4,6},{6,8},{8,10},{10,12},{12,14},{14,16},{16,18},{18... | collective-permute-start | bytes 2555912 | tf_op jit(solution)/shard_map/ppermute | solution.py:577
  5.0 5.4 %collective-permute-start = (f32[2,32,256]{2,1,0:T(8,128)}, f32[2,32,256]{2,1,0:T(8,128)S(1)}, u32[]{:S(2)}, u32[]{:S(2)}) collective-permute-start(f32[2,32,256]{2,1,0:T(8,128)} %get-tuple-element.28), channel_id=1, source_target_pairs={{0,1},{1,0},{2,3},{3,2},{4,5},{5,4},{6,7},{7,6},{8,9},{9,8},{10,11... | collective-permute-start | bytes 196616 | tf_op jit(solution)/shard_map/ppermute | solution.py:591
  10.4 15.9 %all-to-all-start = ((f32[32,8,128]{2,1,0:T(8,128)}), f32[32,8,128]{2,1,0:T(8,128)S(1)}, u32[]{:S(2)}, u32[]{:S(2)}) async-start(f32[32,8,128]{2,1,0:T(8,128)} %bitcast.27), calls=%async_computation | async-start | bytes 262144 | tf_op jit(solution)/shard_map/all_to_all | solution.py:608
  26.3 15.2 %collective-permute-start.4 = (f32[32,16,256]{2,1,0:T(8,128)}, f32[32,16,256]{2,1,0:T(8,128)S(1)}, u32[]{:S(2)}, u32[]{:S(2)}) collective-permute-start(f32[32,16,256]{2,1,0:T(8,128)} %get-tuple-element.37), channel_id=1, source_target_pairs={{0,30},{2,0},{4,2},{6,4},{8,6},{10,8},{12,10},{14,12},{16,14},{18,... | collective-permute-start | bytes 1572872 | tf_op jit(solution)/shard_map/ppermute | solution.py:578
  26.8 14.6 %collective-permute-start.3 = (f32[32,16,256]{2,1,0:T(8,128)}, f32[32,16,256]{2,1,0:T(8,128)S(1)}, u32[]{:S(2)}, u32[]{:S(2)}) collective-permute-start(f32[32,16,256]{2,1,0:T(8,128)} %get-tuple-element.35), channel_id=1, source_target_pairs={{0,2},{2,4},{4,6},{6,8},{8,10},{10,12},{12,14},{14,16},{16,18},{18... | collective-permute-start | bytes 1572872 | tf_op jit(solution)/shard_map/ppermute | solution.py:577
  28.0 3.3 %copy-start = (f32[26,32,256]{2,1,0:T(8,128)}, f32[26,32,256]{2,1,0:T(8,128)S(1)}, u32[]{:S(2)}) copy-start(f32[26,32,256]{2,1,0:T(8,128)S(1)} %collective-permute-done.2.high) | copy-start | bytes 2555908
  28.0 3.3 %copy-start.2 = (f32[26,32,256]{2,1,0:T(8,128)}, f32[26,32,256]{2,1,0:T(8,128)S(1)}, u32[]{:S(2)}) copy-start(f32[26,32,256]{2,1,0:T(8,128)S(1)} %collective-permute-done.1.low) | copy-start | bytes 2555908
  31.3 16.6 %all-to-all-start.1 = ((f32[32,8,128]{2,1,0:T(8,128)}), f32[32,8,128]{2,1,0:T(8,128)S(1)}, u32[]{:S(2)}, u32[]{:S(2)}) async-start(f32[32,8,128]{2,1,0:T(8,128)} %bitcast.29), calls=%async_computation.1 | async-start | bytes 262144 | tf_op jit(solution)/shard_map/all_to_all | solution.py:612
  39.7 20.7 %collective-permute-start.5 = (f32[32,24,256]{2,1,0:T(8,128)}, f32[32,24,256]{2,1,0:T(8,128)S(1)}, u32[]{:S(2)}, u32[]{:S(2)}) collective-permute-start(f32[32,24,256]{2,1,0:T(8,128)} %get-tuple-element.44), channel_id=1, source_target_pairs={{0,2},{2,4},{4,6},{6,8},{8,10},{10,12},{12,14},{14,16},{16,18},{18... | collective-permute-start | bytes 2359304 | tf_op jit(solution)/shard_map/ppermute | solution.py:577
  41.4 20.7 %collective-permute-start.6 = (f32[32,24,256]{2,1,0:T(8,128)}, f32[32,24,256]{2,1,0:T(8,128)S(1)}, u32[]{:S(2)}, u32[]{:S(2)}) collective-permute-start(f32[32,24,256]{2,1,0:T(8,128)} %get-tuple-element.46), channel_id=1, source_target_pairs={{0,30},{2,0},{4,2},{6,4},{8,6},{10,8},{12,10},{14,12},{16,14},{18,... | collective-permute-start | bytes 2359304 | tf_op jit(solution)/shard_map/ppermute | solution.py:578
  47.9 1.2 %copy-start.1 = (f32[26,32,256]{2,1,0:T(8,128)S(1)}, f32[26,32,256]{2,1,0:T(8,128)}, u32[]{:S(2)}) copy-start(f32[26,32,256]{2,1,0:T(8,128)} %copy-done) | copy-start | bytes 2555908
  49.1 1.2 %copy-start.3 = (f32[26,32,256]{2,1,0:T(8,128)S(1)}, f32[26,32,256]{2,1,0:T(8,128)}, u32[]{:S(2)}) copy-start(f32[26,32,256]{2,1,0:T(8,128)} %copy-done.2) | copy-start | bytes 2555908

commit v15 on v14

--- a/solution.py
+++ b/solution.py
@@ -516,7 +516,7 @@
     return pl.pallas_call(
         middle_kernel,
         out_shape=pltpu.HBM((CH, rows, NX), F32),
-        in_specs=[hbm] * 2 + [pl.BlockSpec(memory_space=pl.ANY)] * 3,
+        in_specs=[hbm] * 5,
         out_specs=hbm,
         scratch_shapes=[
             pltpu.VMEM((3, rows + 2, CH, NX), F32),
@@ -531,7 +531,7 @@
         compiler_params=params(),
         cost_estimate=cost(4 * 10**10, 2**18),
         name="middle_sums",
-    )(*in_hbm(weight, point), low, *in_hbm(own), high)
+    )(*in_hbm(weight, point, low, own, high))
 
 
 def general_filter(coarse, gains, gz, gy, scale):
@@ -606,7 +606,8 @@
     if whole_tiles:
         both = ("gz", "gy")
         got = lax.all_to_all(coarse, both, split_axis=0, concat_axis=0, tiled=True)
-        pair = to_neighbours(after(down, got), after(up, got))
+        down, up = lax.optimization_barrier((down, up, first_low, first_high))[:2]
+        pair = to_neighbours(down, up)
         gains = after(spectral_filter, first_low, first_high, second)
         mark = filter_call(got, gains, gz, gy, forward_scale)
         back = lax.all_to_all(mark, both, split_axis=0, concat_axis=0, tiled=True)

time: 64.1 us -> 62.5 us (0.975)
  starting transfers between devices: 23.2 us -> 19.8 us
  waiting for transfers between devices: 9.52 us -> 12.8 us
  local copies, waits for them, and re-layouts: 2.32 us -> 0.94 us
    ppermute x3, waiting for transfers between devices: 0.01 us -> 2.62 us  [to_neighbours(): lax.ppermute(down, 'gz', ring('gz', gz, 1))]
    all_to_all x1, starting transfers between devices: 8.43 us -> 6.2 us  [body(): back = lax.all_to_all(mark, both, split_axis=0, concat_axis=0, tiled=True)]
    ppermute x3, waiting for transfers between devices: 1.72 us -> 3.73 us  [to_neighbours(): lax.ppermute(up, 'gz', ring('gz', gz, -1))]
    unnamed x8 -> x6, local copies, waits for them, and re-layouts: 2.32 us -> 0.94 us
    all_to_all x1, waiting for transfers between devices: 1.33 us -> 0.01 us  [body(): got = lax.all_to_all(coarse, both, split_axis=0, concat_axis=0, tiled=True)]
  transfers between devices with their start and end apart: 9 -> 9, of which waited for: 3 -> 4; matrix products, arithmetic and copies ran while one was open for 0% -> 0% of each run, Pallas kernels for 39% -> 40%
where the time goes in v15:
time: 62.5 us; the launch traced here: 62 us
  Pallas kernels  28.3 us (45%)
  starting transfers between devices  19.8 us (32%)
  waiting for transfers between devices  12.8 us (20%)
  local copies, waits for them, and re-layouts  0.94 us (2%)
    all_to_all x1, starting transfers between devices, body(): got = lax.all_to_all(coarse, both, split_axis=0, concat_axis=0, tiled=True)  7.36 us
    pallas_call x1, Pallas kernels, own_call(): pl.pallas_call(functools.partial(own_kernel, segments, groups), out_shape...  7.12 us
    all_to_all x1, waiting for transfers between devices, body(): back = lax.all_to_all(mark, both, split_axis=0, concat_axis=0, tiled=True)  6.47 us
    all_to_all x1, starting transfers between devices, body(): back = lax.all_to_all(mark, both, split_axis=0, concat_axis=0, tiled=True)  6.2 us
    pallas_call x1, Pallas kernels, inverse_call(): pl.pallas_call(functools.partial(inverse_kernel, upper), out_shape=[jax.S...  5.68 us
    ppermute x3, starting transfers between devices, to_neighbours(): lax.ppermute(down, 'gz', ring('gz', gz, 1))  4.94 us
    pallas_call x1, Pallas kernels, middle_call(): pl.pallas_call(middle_kernel, out_shape=pltpu.HBM((CH, rows, NX), F32), i...  4.91 us
    pallas_call x1, Pallas kernels, forward_call(): pl.pallas_call(forward_kernel, out_shape=(pltpu.HBM if pinned else jax.Sh...  4.14 us
  transfers between devices with their start and end apart: 9, of which 4 were waited for; matrix products, arithmetic and copies ran while one was open for 0% of the time, Pallas kernels for 40%

profile of v15, /device:TPU:1, one launch (start us, length us, event | category | flops | bytes accessed | tf_op | source)
XLA Modules:
  0.0 62.0 jit_solution(10613280644185504028)
XLA Ops:
  0.0 2.3 %packed_rows.1 = (f32[26,32,256]{2,1,0:T(8,128)}, f32[2,32,256]{2,1,0:T(8,128)}) custom-call(f32[32,64,256]{2,1,0:T(8,128)} %bitcast.21), custom_call_target="tpu_custom_call" | custom-call | flops 100000000 | bytes 262144 | tf_op jit(solution)/shard_map/packed_rows/pallas_call | solution.py:466
  2.3 0.1 collective-permute-start.2
  2.4 2.6 %collective-permute-start.1 = (f32[26,32,256]{2,1,0:T(8,128)}, f32[26,32,256]{2,1,0:T(8,128)S(1)}, u32[]{:S(2)}, u32[]{:S(2)}) collective-permute-start(f32[26,32,256]{2,1,0:T(8,128)} %get-tuple-element.38.own), channel_id=1, source_target_pairs={{0,2},{2,4},{4,6},{6,8},{8,10},{10,12},{12,14},{14,16},{16,18},{18... | collective-permute-start | bytes 2555912 | tf_op jit(solution)/shard_map/ppermute | solution.py:577
  5.1 1.2 %collective-permute-start = (f32[2,32,256]{2,1,0:T(8,128)}, f32[2,32,256]{2,1,0:T(8,128)S(1)}, u32[]{:S(2)}, u32[]{:S(2)}) collective-permute-start(f32[2,32,256]{2,1,0:T(8,128)} %get-tuple-element.28), channel_id=1, source_target_pairs={{0,1},{1,0},{2,3},{3,2},{4,5},{5,4},{6,7},{7,6},{8,9},{9,8},{10,11... | collective-permute-start | bytes 196616 | tf_op jit(solution)/shard_map/ppermute | solution.py:591
  6.3 4.1 %forward_modes.1 = f32[256,128]{1,0:T(8,128)} custom-call(f32[8,4,64,256]{3,2,1,0:T(8,128)} %bitcast.22, bf16[2,256,128]{2,1,0:T(8,128)(2,1)} %constant.24.clone.x_top, bf16[2,256,128]{2,1,0:T(8,128)(2,1)} %constant.25.clone.x_rest, bf16[2,32,64]{2,1,0:T(8,128)(2,1)} %constant.26.clone.y_top, bf16[2,32,64]{2,1,0:T(8,128)(2,1)} %constant.27.clone.y_rest), custom_call_target="tpu_custom_call" | custom-call | flops 100000000 | bytes 262144 | tf_op jit(solution)/shard_map/forward_modes/pallas_call | solution.py:387
  10.4 0.0 collective-permute-done.halo
  10.4 7.4 %all-to-all-start = ((f32[32,8,128]{2,1,0:T(8,128)}), f32[32,8,128]{2,1,0:T(8,128)S(1)}, u32[]{:S(2)}, u32[]{:S(2)}) async-start(f32[32,8,128]{2,1,0:T(8,128)} %bitcast.27), calls=%async_computation | async-start | bytes 262144 | tf_op jit(solution)/shard_map/all_to_all | solution.py:608
  17.8 7.1 %own_sums.1 = (f32[32,16,256]{2,1,0:T(8,128)}, f32[32,16,256]{2,1,0:T(8,128)}, f32[32,16,256]{2,1,0:T(8,128)}, f32[32,24,256]{2,1,0:T(8,128)}, f32[32,24,256]{2,1,0:T(8,128)}, /*index=5*/f32[32,24,256]{2,1,0:T(8,128)}) custom-call(f32[32,27]{1,0:T(8,128)} %weight.3, f32[32,32]{1,0:T(8,128)} %point.3, f32[32,64,256]{2,1,0:T(8,128)} %bitcast.23, ...), custom_call_target="tpu_custom_call" | custom-call | flops 100000000 | bytes 262144 | tf_op jit(solution)/shard_map/own_sums/pallas_call | solution.py:489
  24.9 1.4 %collective-permute-done.2.high = f32[26,32,256]{2,1,0:T(8,128)S(1)} collective-permute-done((f32[26,32,256]{2,1,0:T(8,128)}, f32[26,32,256]{2,1,0:T(8,128)S(1)}, u32[]{:S(2)}, u32[]{:S(2)}) %collective-permute-start.2) | collective-permute-done | bytes 852000 | tf_op jit(solution)/shard_map/ppermute | solution.py:578
  26.3 0.0 copy-start
  26.3 0.0 collective-permute-done.1.low
  26.3 0.0 copy-start.1
  26.3 0.9 %copy-done = f32[26,32,256]{2,1,0:T(8,128)} copy-done((f32[26,32,256]{2,1,0:T(8,128)}, f32[26,32,256]{2,1,0:T(8,128)S(1)}, u32[]{:S(2)}) %copy-start) | copy-done | bytes 851992
  27.2 0.6 collective-permute-start.3
  27.8 0.0 collective-permute-start.4
  27.8 0.0 all-to-all-done
  27.8 0.0 copy-start.2
  27.8 2.7 %filter_modes.1 = f32[256,128]{1,0:T(8,128)} custom-call(f32[256,128]{1,0:T(8,128)S(1)} %bitcast.20, f32[2,16,8,64]{3,2,1,0:T(8,128)} %gains, bf16[256,256]{1,0:T(8,128)(2,1)} %constant.28.clone.f_top, bf16[256,256]{1,0:T(8,128)(2,1)} %constant.29.clone.f_rest, bf16[512,128]{1,0:T(8,128)(2,1)} %constant.30.clone.i_top, bf16[512,128]{1,0:T(8,128)(2,1)} %constant.31.clone.i_rest), custom_call_target="tpu_custom_call" | custom-call | flops 40000000000 | bytes 262144 | tf_op jit(solution)/shard_map/filter_modes/pallas_call | solution.py:406
  30.6 0.0 copy-done.1
  30.6 6.2 %all-to-all-start.1 = ((f32[32,8,128]{2,1,0:T(8,128)}), f32[32,8,128]{2,1,0:T(8,128)S(1)}, u32[]{:S(2)}, u32[]{:S(2)}) async-start(f32[32,8,128]{2,1,0:T(8,128)} %bitcast.29), calls=%async_computation.1 | async-start | bytes 262144 | tf_op jit(solution)/shard_map/all_to_all | solution.py:613
  36.8 1.7 %collective-permute-start.5 = (f32[32,24,256]{2,1,0:T(8,128)}, f32[32,24,256]{2,1,0:T(8,128)S(1)}, u32[]{:S(2)}, u32[]{:S(2)}) collective-permute-start(f32[32,24,256]{2,1,0:T(8,128)} %get-tuple-element.44), channel_id=1, source_target_pairs={{0,2},{2,4},{4,6},{6,8},{8,10},{10,12},{12,14},{14,16},{16,18},{18... | collective-permute-start | bytes 2359304 | tf_op jit(solution)/shard_map/ppermute | solution.py:577
  38.5 0.0 copy-done.2
  38.5 0.0 collective-permute-start.6
  38.5 6.5 %all-to-all-done.1 = f32[32,8,128]{2,1,0:T(8,128)S(1)} async-done(((f32[32,8,128]{2,1,0:T(8,128)}), f32[32,8,128]{2,1,0:T(8,128)S(1)}, u32[]{:S(2)}, u32[]{:S(2)}) %all-to-all-start.1) | async-done | bytes 131104 | tf_op jit(solution)/shard_map/all_to_all | solution.py:613
  44.9 0.0 collective-permute-done.3
  44.9 0.0 collective-permute-done.4
  44.9 4.9 %middle_sums.1 = f32[32,24,256]{2,1,0:T(8,128)} custom-call(f32[32,27]{1,0:T(8,128)} %weight.3, f32[32,32]{1,0:T(8,128)} %point.3, f32[26,32,256]{2,1,0:T(8,128)} %copy-done.1, f32[26,32,256]{2,1,0:T(8,128)} %get-tuple-element.38.own, f32[26,32,256]{2,1,0:T(8,128)} %copy-done), custom_call_target="tpu_custom_call" | custom-call | flops 40000000000 | bytes 262144 | tf_op jit(solution)/shard_map/middle_sums/pallas_call | solution.py:516
  49.8 5.7 %inverse_modes.1 = (f32[8,4,64,256]{3,2,1,0:T(8,128)}, f32[8,4,24,256]{3,2,1,0:T(8,128)S(1)}) custom-call(f32[16,16,128]{2,1,0:T(8,128)S(1)} %bitcast.19, f32[32]{0:T(128)} %bias.1, bf16[2,128,256]{2,1,0:T(8,128)(2,1)} %constant.32.clone.x_top, bf16[2,128,256]{2,1,0:T(8,128)(2,1)} %constant.33.clone.x_rest, bf16[2,64,32]{2,1,0:T(8,128)(2,1)} %constant.34.clone.y_top, ...), custom_call_target="tpu_custom_call" | custom-call | flops 100000000 | bytes 262144 | tf_op jit(solution)/shard_map/inverse_modes/pallas_call | solution.py:420
  55.5 2.6 %collective-permute-done.5.low = f32[32,24,256]{2,1,0:T(8,128)S(1)} collective-permute-done((f32[32,24,256]{2,1,0:T(8,128)}, f32[32,24,256]{2,1,0:T(8,128)S(1)}, u32[]{:S(2)}, u32[]{:S(2)}) %collective-permute-start.5) | collective-permute-done | bytes 786464 | tf_op jit(solution)/shard_map/ppermute | solution.py:577
  58.1 2.4 %collective-permute-done.6.high = f32[32,24,256]{2,1,0:T(8,128)S(1)} collective-permute-done((f32[32,24,256]{2,1,0:T(8,128)S(1)}, f32[32,24,256]{2,1,0:T(8,128)S(1)}, u32[]{:S(2)}, u32[]{:S(2)}) %collective-permute-start.6) | collective-permute-done | bytes 786464 | tf_op jit(solution)/shard_map/ppermute | solution.py:578
  60.5 1.5 %finished_rows.1 = f32[32,64,256]{2,1,0:T(8,128)} custom-call(f32[32,64,256]{2,1,0:T(8,128)} %bitcast.24, f32[32,24,256]{2,1,0:T(8,128)S(1)} %bitcast.16, f32[32,24,256]{2,1,0:T(8,128)S(1)} %collective-permute-done.5.low, f32[32,24,256]{2,1,0:T(8,128)S(1)} %collective-permute-done.6.high), custom_call_target="tpu_custom_call", output_to_operand_aliasing={{}: (0, {})} | custom-call | flops 100000000 | bytes 262144 | tf_op jit(solution)/shard_map/finished_rows/pallas_call | solution.py:446
Async XLA Ops:
  2.3 24.0 %collective-permute-start.2 = (f32[26,32,256]{2,1,0:T(8,128)}, f32[26,32,256]{2,1,0:T(8,128)S(1)}, u32[]{:S(2)}, u32[]{:S(2)}) collective-permute-start(f32[26,32,256]{2,1,0:T(8,128)} %get-tuple-element.38.own), channel_id=1, source_target_pairs={{0,30},{2,0},{4,2},{6,4},{8,6},{10,8},{12,10},{14,12},{16,14},{18,... | collective-permute-start | bytes 2555912 | tf_op jit(solution)/shard_map/ppermute | solution.py:578
  2.4 23.9 %collective-permute-start.1 = (f32[26,32,256]{2,1,0:T(8,128)}, f32[26,32,256]{2,1,0:T(8,128)S(1)}, u32[]{:S(2)}, u32[]{:S(2)}) collective-permute-start(f32[26,32,256]{2,1,0:T(8,128)} %get-tuple-element.38.own), channel_id=1, source_target_pairs={{0,2},{2,4},{4,6},{6,8},{8,10},{10,12},{12,14},{14,16},{16,18},{18... | collective-permute-start | bytes 2555912 | tf_op jit(solution)/shard_map/ppermute | solution.py:577
  5.1 5.4 %collective-permute-start = (f32[2,32,256]{2,1,0:T(8,128)}, f32[2,32,256]{2,1,0:T(8,128)S(1)}, u32[]{:S(2)}, u32[]{:S(2)}) collective-permute-start(f32[2,32,256]{2,1,0:T(8,128)} %get-tuple-element.28), channel_id=1, source_target_pairs={{0,1},{1,0},{2,3},{3,2},{4,5},{5,4},{6,7},{7,6},{8,9},{9,8},{10,11... | collective-permute-start | bytes 196616 | tf_op jit(solution)/shard_map/ppermute | solution.py:591
  10.4 17.4 %all-to-all-start = ((f32[32,8,128]{2,1,0:T(8,128)}), f32[32,8,128]{2,1,0:T(8,128)S(1)}, u32[]{:S(2)}, u32[]{:S(2)}) async-start(f32[32,8,128]{2,1,0:T(8,128)} %bitcast.27), calls=%async_computation | async-start | bytes 262144 | tf_op jit(solution)/shard_map/all_to_all | solution.py:608
  26.3 0.9 %copy-start = (f32[26,32,256]{2,1,0:T(8,128)}, f32[26,32,256]{2,1,0:T(8,128)S(1)}, u32[]{:S(2)}) copy-start(f32[26,32,256]{2,1,0:T(8,128)S(1)} %collective-permute-done.2.high) | copy-start | bytes 2555908
  26.3 4.3 %copy-start.1 = (f32[26,32,256]{2,1,0:T(8,128)}, f32[26,32,256]{2,1,0:T(8,128)S(1)}, u32[]{:S(2)}) copy-start(f32[26,32,256]{2,1,0:T(8,128)S(1)} %collective-permute-done.1.low) | copy-start | bytes 2555908
  27.2 17.7 %collective-permute-start.3 = (f32[32,16,256]{2,1,0:T(8,128)}, f32[32,16,256]{2,1,0:T(8,128)S(1)}, u32[]{:S(2)}, u32[]{:S(2)}) collective-permute-start(f32[32,16,256]{2,1,0:T(8,128)} %get-tuple-element.36), channel_id=1, source_target_pairs={{0,2},{2,4},{4,6},{6,8},{8,10},{10,12},{12,14},{14,16},{16,18},{18... | collective-permute-start | bytes 1572872 | tf_op jit(solution)/shard_map/ppermute | solution.py:577
  27.8 17.1 %collective-permute-start.4 = (f32[32,16,256]{2,1,0:T(8,128)}, f32[32,16,256]{2,1,0:T(8,128)S(1)}, u32[]{:S(2)}, u32[]{:S(2)}) collective-permute-start(f32[32,16,256]{2,1,0:T(8,128)} %get-tuple-element.37), channel_id=1, source_target_pairs={{0,30},{2,0},{4,2},{6,4},{8,6},{10,8},{12,10},{14,12},{16,14},{18,... | collective-permute-start | bytes 1572872 | tf_op jit(solution)/shard_map/ppermute | solution.py:578
  27.8 10.6 %copy-start.2 = (f32[32,24,256]{2,1,0:T(8,128)S(1)}, f32[32,24,256]{2,1,0:T(8,128)}, u32[]{:S(2)}) copy-start(f32[32,24,256]{2,1,0:T(8,128)} %get-tuple-element.46) | copy-start | bytes 2359300
  30.6 14.4 %all-to-all-start.1 = ((f32[32,8,128]{2,1,0:T(8,128)}), f32[32,8,128]{2,1,0:T(8,128)S(1)}, u32[]{:S(2)}, u32[]{:S(2)}) async-start(f32[32,8,128]{2,1,0:T(8,128)} %bitcast.29), calls=%async_computation.1 | async-start | bytes 262144 | tf_op jit(solution)/shard_map/all_to_all | solution.py:613
  36.8 21.4 %collective-permute-start.5 = (f32[32,24,256]{2,1,0:T(8,128)}, f32[32,24,256]{2,1,0:T(8,128)S(1)}, u32[]{:S(2)}, u32[]{:S(2)}) collective-permute-start(f32[32,24,256]{2,1,0:T(8,128)} %get-tuple-element.44), channel_id=1, source_target_pairs={{0,2},{2,4},{4,6},{6,8},{8,10},{10,12},{12,14},{14,16},{16,18},{18... | collective-permute-start | bytes 2359304 | tf_op jit(solution)/shard_map/ppermute | solution.py:577
  38.5 22.1 %collective-permute-start.6 = (f32[32,24,256]{2,1,0:T(8,128)S(1)}, f32[32,24,256]{2,1,0:T(8,128)S(1)}, u32[]{:S(2)}, u32[]{:S(2)}) collective-permute-start(f32[32,24,256]{2,1,0:T(8,128)S(1)} %copy-done.2), channel_id=1, source_target_pairs={{0,30},{2,0},{4,2},{6,4},{8,6},{10,8},{12,10},{14,12},{16,14},{18,... | collective-permute-start | bytes 2359304 | tf_op jit(solution)/shard_map/ppermute | solution.py:578

commit v16 on v15

--- a/solution.py
+++ b/solution.py
@@ -606,7 +606,6 @@
     if whole_tiles:
         both = ("gz", "gy")
         got = lax.all_to_all(coarse, both, split_axis=0, concat_axis=0, tiled=True)
-        down, up = lax.optimization_barrier((down, up, first_low, first_high))[:2]
         pair = to_neighbours(down, up)
         gains = after(spectral_filter, first_low, first_high, second)
         mark = filter_call(got, gains, gz, gy, forward_scale)
@@ -616,7 +615,7 @@
         pair = to_neighbours(down, up)
         mark = back = general_filter(coarse, spectral_filter, gz, gy, forward_scale)
     outer_pair = to_neighbours(after(outer_down, mark), after(outer_up, mark))
-    packed, *pair = lax.optimization_barrier((packed, *pair, back))[:-1]
+    packed, *pair = lax.optimization_barrier((packed, *pair))
     mixed = middle_call(depth_weight, point_weight, first_low, packed, first_high)
     result, base = inverse_call(
         back, bias_vector, own, mixed, second, pair, 8, y_local, gy, inverse_scale

time: 62.5 us -> 71.1 us (1.14)
  waiting for transfers between devices: 12.8 us -> 20.1 us
  starting transfers between devices: 19.8 us -> 21.7 us
  local copies, waits for them, and re-layouts: 0.94 us -> 0.01 us
    ppermute x3, waiting for transfers between devices: 2.62 us -> 15.9 us  [to_neighbours(): lax.ppermute(down, 'gz', ring('gz', gz, 1))]
    all_to_all x1, waiting for transfers between devices: 6.47 us -> 1.57 us  [body(): back = lax.all_to_all(mark, both, split_axis=0, concat_axis=0, tiled=True)]
    ppermute x3, starting transfers between devices: 0.11 us -> 2.53 us  [to_neighbours(): lax.ppermute(up, 'gz', ring('gz', gz, -1))]
    ppermute x3, waiting for transfers between devices: 3.73 us -> 2.62 us  [to_neighbours(): lax.ppermute(up, 'gz', ring('gz', gz, -1))]
    unnamed x6 -> x4, local copies, waits for them, and re-layouts: 0.94 us -> 0.01 us
    all_to_all x1, starting transfers between devices: 7.36 us -> 6.55 us  [body(): got = lax.all_to_all(coarse, both, split_axis=0, concat_axis=0, tiled=True)]
  transfers between devices with their start and end apart: 9 -> 9, of which waited for: 4 -> 5; matrix products, arithmetic and copies ran while one was open for 0% -> 0% of each run, Pallas kernels for 40% -> 31%
where the time goes in v16:
time: 71.1 us; the launch traced here: 70.7 us
  Pallas kernels  28.8 us (41%)
  starting transfers between devices  21.7 us (31%)
  waiting for transfers between devices  20.1 us (28%)
    ppermute x3, waiting for transfers between devices, to_neighbours(): lax.ppermute(down, 'gz', ring('gz', gz, 1))  15.9 us
    pallas_call x1, Pallas kernels, own_call(): pl.pallas_call(functools.partial(own_kernel, segments, groups), out_shape...  7.11 us
    all_to_all x1, starting transfers between devices, body(): got = lax.all_to_all(coarse, both, split_axis=0, concat_axis=0, tiled=True)  6.55 us
    all_to_all x1, starting transfers between devices, body(): back = lax.all_to_all(mark, both, split_axis=0, concat_axis=0, tiled=True)  6.27 us
    pallas_call x1, Pallas kernels, inverse_call(): pl.pallas_call(functools.partial(inverse_kernel, upper), out_shape=[jax.S...  5.65 us
    ppermute x3, starting transfers between devices, to_neighbours(): lax.ppermute(down, 'gz', ring('gz', gz, 1))  5.11 us
    pallas_call x1, Pallas kernels, middle_call(): pl.pallas_call(middle_kernel, out_shape=pltpu.HBM((CH, rows, NX), F32), i...  4.89 us
    pallas_call x1, Pallas kernels, forward_call(): pl.pallas_call(forward_kernel, out_shape=(pltpu.HBM if pinned else jax.Sh...  4.13 us
  transfers between devices with their start and end apart: 9, of which 5 were waited for; matrix products, arithmetic and copies ran while one was open for 0% of the time, Pallas kernels for 31%

profile of v16, /device:TPU:1, one launch (start us, length us, event | category | flops | bytes accessed | tf_op | source)
XLA Modules:
  0.0 70.7 jit_solution(312919941759505876)
XLA Ops:
  0.0 2.3 %packed_rows.1 = (f32[26,32,256]{2,1,0:T(8,128)}, f32[2,32,256]{2,1,0:T(8,128)}) custom-call(f32[32,64,256]{2,1,0:T(8,128)} %bitcast.21), custom_call_target="tpu_custom_call" | custom-call | flops 100000000 | bytes 262144 | tf_op jit(solution)/shard_map/packed_rows/pallas_call | solution.py:466
  2.3 0.1 collective-permute-start.2
  2.4 2.6 %collective-permute-start.1 = (f32[26,32,256]{2,1,0:T(8,128)}, f32[26,32,256]{2,1,0:T(8,128)S(1)}, u32[]{:S(2)}, u32[]{:S(2)}) collective-permute-start(f32[26,32,256]{2,1,0:T(8,128)} %get-tuple-element.34.own), channel_id=1, source_target_pairs={{0,2},{2,4},{4,6},{6,8},{8,10},{10,12},{12,14},{14,16},{16,18},{18... | collective-permute-start | bytes 2555912 | tf_op jit(solution)/shard_map/ppermute | solution.py:577
  5.0 1.2 %collective-permute-start = (f32[2,32,256]{2,1,0:T(8,128)}, f32[2,32,256]{2,1,0:T(8,128)S(1)}, u32[]{:S(2)}, u32[]{:S(2)}) collective-permute-start(f32[2,32,256]{2,1,0:T(8,128)} %get-tuple-element.26), channel_id=1, source_target_pairs={{0,1},{1,0},{2,3},{3,2},{4,5},{5,4},{6,7},{7,6},{8,9},{9,8},{10,11... | collective-permute-start | bytes 196616 | tf_op jit(solution)/shard_map/ppermute | solution.py:591
  6.3 4.1 %forward_modes.1 = f32[256,128]{1,0:T(8,128)} custom-call(f32[8,4,64,256]{3,2,1,0:T(8,128)} %bitcast.22, bf16[2,256,128]{2,1,0:T(8,128)(2,1)} %constant.24.clone.x_top, bf16[2,256,128]{2,1,0:T(8,128)(2,1)} %constant.25.clone.x_rest, bf16[2,32,64]{2,1,0:T(8,128)(2,1)} %constant.26.clone.y_top, bf16[2,32,64]{2,1,0:T(8,128)(2,1)} %constant.27.clone.y_rest), custom_call_target="tpu_custom_call" | custom-call | flops 100000000 | bytes 262144 | tf_op jit(solution)/shard_map/forward_modes/pallas_call | solution.py:387
  10.4 0.0 collective-permute-done.halo
  10.4 7.1 %own_sums.1 = (f32[32,16,256]{2,1,0:T(8,128)}, f32[32,16,256]{2,1,0:T(8,128)}, f32[32,16,256]{2,1,0:T(8,128)}, f32[32,24,256]{2,1,0:T(8,128)}, f32[32,24,256]{2,1,0:T(8,128)}, /*index=5*/f32[32,24,256]{2,1,0:T(8,128)}) custom-call(f32[32,27]{1,0:T(8,128)} %weight.3, f32[32,32]{1,0:T(8,128)} %point.3, f32[32,64,256]{2,1,0:T(8,128)} %bitcast.23, ...), custom_call_target="tpu_custom_call" | custom-call | flops 100000000 | bytes 262144 | tf_op jit(solution)/shard_map/own_sums/pallas_call | solution.py:489
  17.5 0.8 %collective-permute-start.3 = (f32[32,16,256]{2,1,0:T(8,128)}, f32[32,16,256]{2,1,0:T(8,128)S(1)}, u32[]{:S(2)}, u32[]{:S(2)}) collective-permute-start(f32[32,16,256]{2,1,0:T(8,128)} %get-tuple-element.32), channel_id=1, source_target_pairs={{0,2},{2,4},{4,6},{6,8},{8,10},{10,12},{12,14},{14,16},{16,18},{18... | collective-permute-start | bytes 1572872 | tf_op jit(solution)/shard_map/ppermute | solution.py:577
  18.3 2.4 %collective-permute-start.4 = (f32[32,16,256]{2,1,0:T(8,128)}, f32[32,16,256]{2,1,0:T(8,128)S(1)}, u32[]{:S(2)}, u32[]{:S(2)}) collective-permute-start(f32[32,16,256]{2,1,0:T(8,128)} %get-tuple-element.33), channel_id=1, source_target_pairs={{0,30},{2,0},{4,2},{6,4},{8,6},{10,8},{12,10},{14,12},{16,14},{18,... | collective-permute-start | bytes 1572872 | tf_op jit(solution)/shard_map/ppermute | solution.py:578
  20.7 6.5 %all-to-all-start = ((f32[32,8,128]{2,1,0:T(8,128)}), f32[32,8,128]{2,1,0:T(8,128)S(1)}, u32[]{:S(2)}, u32[]{:S(2)}) async-start(f32[32,8,128]{2,1,0:T(8,128)} %bitcast.2), calls=%async_computation | async-start | bytes 262144 | tf_op jit(solution)/shard_map/all_to_all | solution.py:608
  27.3 9.4 %collective-permute-done.3 = f32[32,16,256]{2,1,0:T(8,128)S(1)} collective-permute-done((f32[32,16,256]{2,1,0:T(8,128)}, f32[32,16,256]{2,1,0:T(8,128)S(1)}, u32[]{:S(2)}, u32[]{:S(2)}) %collective-permute-start.3) | collective-permute-done | bytes 524320 | tf_op jit(solution)/shard_map/ppermute | solution.py:577
  36.7 0.6 collective-permute-done.4
  37.2 0.0 collective-permute-done.2.high
  37.3 0.0 copy-start
  37.3 0.0 collective-permute-done.1.low
  37.3 0.0 copy-start.1
  37.3 0.0 all-to-all-done
  37.3 3.2 %filter_modes.1 = f32[256,128]{1,0:T(8,128)} custom-call(f32[256,128]{1,0:T(8,128)S(1)} %bitcast.20, f32[2,16,8,64]{3,2,1,0:T(8,128)} %gains, bf16[256,256]{1,0:T(8,128)(2,1)} %constant.28.clone.f_top, bf16[256,256]{1,0:T(8,128)(2,1)} %constant.29.clone.f_rest, bf16[512,128]{1,0:T(8,128)(2,1)} %constant.30.clone.i_top, bf16[512,128]{1,0:T(8,128)(2,1)} %constant.31.clone.i_rest), custom_call_target="tpu_custom_call" | custom-call | flops 40000000000 | bytes 262144 | tf_op jit(solution)/shard_map/filter_modes/pallas_call | solution.py:406
  40.5 0.0 copy-done
  40.5 0.0 copy-done.1
  40.5 6.3 %all-to-all-start.1 = ((f32[32,8,128]{2,1,0:T(8,128)}), f32[32,8,128]{2,1,0:T(8,128)S(1)}, u32[]{:S(2)}, u32[]{:S(2)}) async-start(f32[32,8,128]{2,1,0:T(8,128)} %bitcast.28), calls=%async_computation.1 | async-start | bytes 262144 | tf_op jit(solution)/shard_map/all_to_all | solution.py:612
  46.8 1.7 %collective-permute-start.5 = (f32[32,24,256]{2,1,0:T(8,128)}, f32[32,24,256]{2,1,0:T(8,128)S(1)}, u32[]{:S(2)}, u32[]{:S(2)}) collective-permute-start(f32[32,24,256]{2,1,0:T(8,128)} %get-tuple-element.40), channel_id=1, source_target_pairs={{0,2},{2,4},{4,6},{6,8},{8,10},{10,12},{12,14},{14,16},{16,18},{18... | collective-permute-start | bytes 2359304 | tf_op jit(solution)/shard_map/ppermute | solution.py:577
  48.5 0.0 collective-permute-start.6
  48.5 4.9 %middle_sums.1 = f32[32,24,256]{2,1,0:T(8,128)} custom-call(f32[32,27]{1,0:T(8,128)} %weight.3, f32[32,32]{1,0:T(8,128)} %point.3, f32[26,32,256]{2,1,0:T(8,128)} %copy-done.1, f32[26,32,256]{2,1,0:T(8,128)} %get-tuple-element.34.own, f32[26,32,256]{2,1,0:T(8,128)} %copy-done), custom_call_target="tpu_custom_call" | custom-call | flops 40000000000 | bytes 262144 | tf_op jit(solution)/shard_map/middle_sums/pallas_call | solution.py:516
  53.4 1.6 %all-to-all-done.1 = f32[32,8,128]{2,1,0:T(8,128)S(1)} async-done(((f32[32,8,128]{2,1,0:T(8,128)}), f32[32,8,128]{2,1,0:T(8,128)S(1)}, u32[]{:S(2)}, u32[]{:S(2)}) %all-to-all-start.1) | async-done | bytes 131104 | tf_op jit(solution)/shard_map/all_to_all | solution.py:612
  55.0 5.6 %inverse_modes.1 = (f32[8,4,64,256]{3,2,1,0:T(8,128)}, f32[8,4,24,256]{3,2,1,0:T(8,128)S(1)}) custom-call(f32[16,16,128]{2,1,0:T(8,128)S(1)} %bitcast.19, f32[32]{0:T(128)} %bias.1, bf16[2,128,256]{2,1,0:T(8,128)(2,1)} %constant.32.clone.x_top, bf16[2,128,256]{2,1,0:T(8,128)(2,1)} %constant.33.clone.x_rest, bf16[2,64,32]{2,1,0:T(8,128)(2,1)} %constant.34.clone.y_top, ...), custom_call_target="tpu_custom_call" | custom-call | flops 100000000 | bytes 262144 | tf_op jit(solution)/shard_map/inverse_modes/pallas_call | solution.py:420
  60.6 6.5 %collective-permute-done.5.low = f32[32,24,256]{2,1,0:T(8,128)S(1)} collective-permute-done((f32[32,24,256]{2,1,0:T(8,128)}, f32[32,24,256]{2,1,0:T(8,128)S(1)}, u32[]{:S(2)}, u32[]{:S(2)}) %collective-permute-start.5) | collective-permute-done | bytes 786464 | tf_op jit(solution)/shard_map/ppermute | solution.py:577
  67.2 2.0 %collective-permute-done.6.high = f32[32,24,256]{2,1,0:T(8,128)S(1)} collective-permute-done((f32[32,24,256]{2,1,0:T(8,128)}, f32[32,24,256]{2,1,0:T(8,128)S(1)}, u32[]{:S(2)}, u32[]{:S(2)}) %collective-permute-start.6) | collective-permute-done | bytes 786464 | tf_op jit(solution)/shard_map/ppermute | solution.py:578
  69.2 1.5 %finished_rows.1 = f32[32,64,256]{2,1,0:T(8,128)} custom-call(f32[32,64,256]{2,1,0:T(8,128)} %bitcast.24, f32[32,24,256]{2,1,0:T(8,128)S(1)} %bitcast.16, f32[32,24,256]{2,1,0:T(8,128)S(1)} %collective-permute-done.5.low, f32[32,24,256]{2,1,0:T(8,128)S(1)} %collective-permute-done.6.high), custom_call_target="tpu_custom_call", output_to_operand_aliasing={{}: (0, {})} | custom-call | flops 100000000 | bytes 262144 | tf_op jit(solution)/shard_map/finished_rows/pallas_call | solution.py:446
Async XLA Ops:
  2.3 35.0 %collective-permute-start.2 = (f32[26,32,256]{2,1,0:T(8,128)}, f32[26,32,256]{2,1,0:T(8,128)S(1)}, u32[]{:S(2)}, u32[]{:S(2)}) collective-permute-start(f32[26,32,256]{2,1,0:T(8,128)} %get-tuple-element.34.own), channel_id=1, source_target_pairs={{0,30},{2,0},{4,2},{6,4},{8,6},{10,8},{12,10},{14,12},{16,14},{18,... | collective-permute-start | bytes 2555912 | tf_op jit(solution)/shard_map/ppermute | solution.py:578
  2.4 34.8 %collective-permute-start.1 = (f32[26,32,256]{2,1,0:T(8,128)}, f32[26,32,256]{2,1,0:T(8,128)S(1)}, u32[]{:S(2)}, u32[]{:S(2)}) collective-permute-start(f32[26,32,256]{2,1,0:T(8,128)} %get-tuple-element.34.own), channel_id=1, source_target_pairs={{0,2},{2,4},{4,6},{6,8},{8,10},{10,12},{12,14},{14,16},{16,18},{18... | collective-permute-start | bytes 2555912 | tf_op jit(solution)/shard_map/ppermute | solution.py:577
  5.0 5.4 %collective-permute-start = (f32[2,32,256]{2,1,0:T(8,128)}, f32[2,32,256]{2,1,0:T(8,128)S(1)}, u32[]{:S(2)}, u32[]{:S(2)}) collective-permute-start(f32[2,32,256]{2,1,0:T(8,128)} %get-tuple-element.26), channel_id=1, source_target_pairs={{0,1},{1,0},{2,3},{3,2},{4,5},{5,4},{6,7},{7,6},{8,9},{9,8},{10,11... | collective-permute-start | bytes 196616 | tf_op jit(solution)/shard_map/ppermute | solution.py:591
  17.5 19.2 %collective-permute-start.3 = (f32[32,16,256]{2,1,0:T(8,128)}, f32[32,16,256]{2,1,0:T(8,128)S(1)}, u32[]{:S(2)}, u32[]{:S(2)}) collective-permute-start(f32[32,16,256]{2,1,0:T(8,128)} %get-tuple-element.32), channel_id=1, source_target_pairs={{0,2},{2,4},{4,6},{6,8},{8,10},{10,12},{12,14},{14,16},{16,18},{18... | collective-permute-start | bytes 1572872 | tf_op jit(solution)/shard_map/ppermute | solution.py:577
  18.3 18.9 %collective-permute-start.4 = (f32[32,16,256]{2,1,0:T(8,128)}, f32[32,16,256]{2,1,0:T(8,128)S(1)}, u32[]{:S(2)}, u32[]{:S(2)}) collective-permute-start(f32[32,16,256]{2,1,0:T(8,128)} %get-tuple-element.33), channel_id=1, source_target_pairs={{0,30},{2,0},{4,2},{6,4},{8,6},{10,8},{12,10},{14,12},{16,14},{18,... | collective-permute-start | bytes 1572872 | tf_op jit(solution)/shard_map/ppermute | solution.py:578
  20.7 16.6 %all-to-all-start = ((f32[32,8,128]{2,1,0:T(8,128)}), f32[32,8,128]{2,1,0:T(8,128)S(1)}, u32[]{:S(2)}, u32[]{:S(2)}) async-start(f32[32,8,128]{2,1,0:T(8,128)} %bitcast.2), calls=%async_computation | async-start | bytes 262144 | tf_op jit(solution)/shard_map/all_to_all | solution.py:608
  37.3 3.3 %copy-start = (f32[26,32,256]{2,1,0:T(8,128)}, f32[26,32,256]{2,1,0:T(8,128)S(1)}, u32[]{:S(2)}) copy-start(f32[26,32,256]{2,1,0:T(8,128)S(1)} %collective-permute-done.2.high) | copy-start | bytes 2555908
  37.3 3.3 %copy-start.1 = (f32[26,32,256]{2,1,0:T(8,128)}, f32[26,32,256]{2,1,0:T(8,128)S(1)}, u32[]{:S(2)}) copy-start(f32[26,32,256]{2,1,0:T(8,128)S(1)} %collective-permute-done.1.low) | copy-start | bytes 2555908
  40.5 14.4 %all-to-all-start.1 = ((f32[32,8,128]{2,1,0:T(8,128)}), f32[32,8,128]{2,1,0:T(8,128)S(1)}, u32[]{:S(2)}, u32[]{:S(2)}) async-start(f32[32,8,128]{2,1,0:T(8,128)} %bitcast.28), calls=%async_computation.1 | async-start | bytes 262144 | tf_op jit(solution)/shard_map/all_to_all | solution.py:612
  46.8 20.3 %collective-permute-start.5 = (f32[32,24,256]{2,1,0:T(8,128)}, f32[32,24,256]{2,1,0:T(8,128)S(1)}, u32[]{:S(2)}, u32[]{:S(2)}) collective-permute-start(f32[32,24,256]{2,1,0:T(8,128)} %get-tuple-element.40), channel_id=1, source_target_pairs={{0,2},{2,4},{4,6},{6,8},{8,10},{10,12},{12,14},{14,16},{16,18},{18... | collective-permute-start | bytes 2359304 | tf_op jit(solution)/shard_map/ppermute | solution.py:577
  48.5 20.7 %collective-permute-start.6 = (f32[32,24,256]{2,1,0:T(8,128)}, f32[32,24,256]{2,1,0:T(8,128)S(1)}, u32[]{:S(2)}, u32[]{:S(2)}) collective-permute-start(f32[32,24,256]{2,1,0:T(8,128)} %get-tuple-element.42), channel_id=1, source_target_pairs={{0,30},{2,0},{4,2},{6,4},{8,6},{10,8},{12,10},{14,12},{16,14},{18,... | collective-permute-start | bytes 2359304 | tf_op jit(solution)/shard_map/ppermute | solution.py:578

commit v17 on v16

--- a/solution.py
+++ b/solution.py
@@ -606,6 +606,7 @@
     if whole_tiles:
         both = ("gz", "gy")
         got = lax.all_to_all(coarse, both, split_axis=0, concat_axis=0, tiled=True)
+        down, up = lax.optimization_barrier((down, up, first_low, first_high))[:2]
         pair = to_neighbours(down, up)
         gains = after(spectral_filter, first_low, first_high, second)
         mark = filter_call(got, gains, gz, gy, forward_scale)

time: 71.1 us -> 62.4 us (0.88)
  waiting for transfers between devices: 20.1 us -> 12.8 us
  starting transfers between devices: 21.7 us -> 19.8 us
  local copies, waits for them, and re-layouts: 0.01 us -> 0.94 us
    ppermute x3, waiting for transfers between devices: 15.9 us -> 6.09 us  [to_neighbours(): lax.ppermute(down, 'gz', ring('gz', gz, 1))]
    ppermute x3, waiting for transfers between devices: 2.62 us -> 6.72 us  [to_neighbours(): lax.ppermute(up, 'gz', ring('gz', gz, -1))]
    ppermute x3, starting transfers between devices: 2.53 us -> 0.11 us  [to_neighbours(): lax.ppermute(up, 'gz', ring('gz', gz, -1))]
    all_to_all x1, waiting for transfers between devices: 1.57 us -> 0.01 us  [body(): back = lax.all_to_all(mark, both, split_axis=0, concat_axis=0, tiled=True)]
    unnamed x4 -> x6, local copies, waits for them, and re-layouts: 0.01 us -> 0.94 us
    all_to_all x1, starting transfers between devices: 6.55 us -> 7.36 us  [body(): got = lax.all_to_all(coarse, both, split_axis=0, concat_axis=0, tiled=True)]
  transfers between devices with their start and end apart: 9 -> 9, of which waited for: 5 -> 5; matrix products, arithmetic and copies ran while one was open for 0% -> 0% of each run, Pallas kernels for 31% -> 40%
where the time goes in v17:
time: 62.4 us; the launch traced here: 62 us
  Pallas kernels  28.3 us (45%)
  starting transfers between devices  19.8 us (32%)
  waiting for transfers between devices  12.8 us (21%)
  local copies, waits for them, and re-layouts  0.94 us (2%)
    all_to_all x1, starting transfers between devices, body(): got = lax.all_to_all(coarse, both, split_axis=0, concat_axis=0, tiled=True)  7.36 us
    pallas_call x1, Pallas kernels, own_call(): pl.pallas_call(functools.partial(own_kernel, segments, groups), out_shape...  7.12 us
    ppermute x3, waiting for transfers between devices, to_neighbours(): lax.ppermute(up, 'gz', ring('gz', gz, -1))  6.72 us
    all_to_all x1, starting transfers between devices, body(): back = lax.all_to_all(mark, both, split_axis=0, concat_axis=0, tiled=True)  6.2 us
    ppermute x3, waiting for transfers between devices, to_neighbours(): lax.ppermute(down, 'gz', ring('gz', gz, 1))  6.09 us
    pallas_call x1, Pallas kernels, inverse_call(): pl.pallas_call(functools.partial(inverse_kernel, upper), out_shape=[jax.S...  5.68 us
    ppermute x3, starting transfers between devices, to_neighbours(): lax.ppermute(down, 'gz', ring('gz', gz, 1))  4.94 us
    pallas_call x1, Pallas kernels, middle_call(): pl.pallas_call(middle_kernel, out_shape=pltpu.HBM((CH, rows, NX), F32), i...  4.91 us
  transfers between devices with their start and end apart: 9, of which 5 were waited for; matrix products, arithmetic and copies ran while one was open for 0% of the time, Pallas kernels for 40%

profile of v17, /device:TPU:1, one launch (start us, length us, event | category | flops | bytes accessed | tf_op | source)
XLA Modules:
  0.0 62.0 jit_solution(14748040128407212932)
XLA Ops:
  0.0 2.3 %packed_rows.1 = (f32[26,32,256]{2,1,0:T(8,128)}, f32[2,32,256]{2,1,0:T(8,128)}) custom-call(f32[32,64,256]{2,1,0:T(8,128)} %bitcast.21), custom_call_target="tpu_custom_call" | custom-call | flops 100000000 | bytes 262144 | tf_op jit(solution)/shard_map/packed_rows/pallas_call | solution.py:466
  2.3 0.1 collective-permute-start.2
  2.4 2.6 %collective-permute-start.1 = (f32[26,32,256]{2,1,0:T(8,128)}, f32[26,32,256]{2,1,0:T(8,128)S(1)}, u32[]{:S(2)}, u32[]{:S(2)}) collective-permute-start(f32[26,32,256]{2,1,0:T(8,128)} %get-tuple-element.38.own), channel_id=1, source_target_pairs={{0,2},{2,4},{4,6},{6,8},{8,10},{10,12},{12,14},{14,16},{16,18},{18... | collective-permute-start | bytes 2555912 | tf_op jit(solution)/shard_map/ppermute | solution.py:577
  5.1 1.2 %collective-permute-start = (f32[2,32,256]{2,1,0:T(8,128)}, f32[2,32,256]{2,1,0:T(8,128)S(1)}, u32[]{:S(2)}, u32[]{:S(2)}) collective-permute-start(f32[2,32,256]{2,1,0:T(8,128)} %get-tuple-element.28), channel_id=1, source_target_pairs={{0,1},{1,0},{2,3},{3,2},{4,5},{5,4},{6,7},{7,6},{8,9},{9,8},{10,11... | collective-permute-start | bytes 196616 | tf_op jit(solution)/shard_map/ppermute | solution.py:591
  6.3 4.1 %forward_modes.1 = f32[256,128]{1,0:T(8,128)} custom-call(f32[8,4,64,256]{3,2,1,0:T(8,128)} %bitcast.22, bf16[2,256,128]{2,1,0:T(8,128)(2,1)} %constant.24.clone.x_top, bf16[2,256,128]{2,1,0:T(8,128)(2,1)} %constant.25.clone.x_rest, bf16[2,32,64]{2,1,0:T(8,128)(2,1)} %constant.26.clone.y_top, bf16[2,32,64]{2,1,0:T(8,128)(2,1)} %constant.27.clone.y_rest), custom_call_target="tpu_custom_call" | custom-call | flops 100000000 | bytes 262144 | tf_op jit(solution)/shard_map/forward_modes/pallas_call | solution.py:387
  10.4 0.0 collective-permute-done.halo
  10.4 7.4 %all-to-all-start = ((f32[32,8,128]{2,1,0:T(8,128)}), f32[32,8,128]{2,1,0:T(8,128)S(1)}, u32[]{:S(2)}, u32[]{:S(2)}) async-start(f32[32,8,128]{2,1,0:T(8,128)} %bitcast.27), calls=%async_computation | async-start | bytes 262144 | tf_op jit(solution)/shard_map/all_to_all | solution.py:608
  17.8 7.1 %own_sums.1 = (f32[32,16,256]{2,1,0:T(8,128)}, f32[32,16,256]{2,1,0:T(8,128)}, f32[32,16,256]{2,1,0:T(8,128)}, f32[32,24,256]{2,1,0:T(8,128)}, f32[32,24,256]{2,1,0:T(8,128)}, /*index=5*/f32[32,24,256]{2,1,0:T(8,128)}) custom-call(f32[32,27]{1,0:T(8,128)} %weight.3, f32[32,32]{1,0:T(8,128)} %point.3, f32[32,64,256]{2,1,0:T(8,128)} %bitcast.23, ...), custom_call_target="tpu_custom_call" | custom-call | flops 100000000 | bytes 262144 | tf_op jit(solution)/shard_map/own_sums/pallas_call | solution.py:489
  24.9 1.4 %collective-permute-done.2.high = f32[26,32,256]{2,1,0:T(8,128)S(1)} collective-permute-done((f32[26,32,256]{2,1,0:T(8,128)}, f32[26,32,256]{2,1,0:T(8,128)S(1)}, u32[]{:S(2)}, u32[]{:S(2)}) %collective-permute-start.2) | collective-permute-done | bytes 852000 | tf_op jit(solution)/shard_map/ppermute | solution.py:578
  26.3 0.0 copy-start
  26.3 0.0 collective-permute-done.1.low
  26.3 0.0 copy-start.1
  26.3 0.9 %copy-done = f32[26,32,256]{2,1,0:T(8,128)} copy-done((f32[26,32,256]{2,1,0:T(8,128)}, f32[26,32,256]{2,1,0:T(8,128)S(1)}, u32[]{:S(2)}) %copy-start) | copy-done | bytes 851992
  27.2 0.6 collective-permute-start.3
  27.8 0.0 collective-permute-start.4
  27.8 0.0 all-to-all-done
  27.8 0.0 copy-start.2
  27.8 2.7 %filter_modes.1 = f32[256,128]{1,0:T(8,128)} custom-call(f32[256,128]{1,0:T(8,128)S(1)} %bitcast.20, f32[2,16,8,64]{3,2,1,0:T(8,128)} %gains, bf16[256,256]{1,0:T(8,128)(2,1)} %constant.28.clone.f_top, bf16[256,256]{1,0:T(8,128)(2,1)} %constant.29.clone.f_rest, bf16[512,128]{1,0:T(8,128)(2,1)} %constant.30.clone.i_top, bf16[512,128]{1,0:T(8,128)(2,1)} %constant.31.clone.i_rest), custom_call_target="tpu_custom_call" | custom-call | flops 40000000000 | bytes 262144 | tf_op jit(solution)/shard_map/filter_modes/pallas_call | solution.py:406
  30.6 0.0 copy-done.1
  30.6 6.2 %all-to-all-start.1 = ((f32[32,8,128]{2,1,0:T(8,128)}), f32[32,8,128]{2,1,0:T(8,128)S(1)}, u32[]{:S(2)}, u32[]{:S(2)}) async-start(f32[32,8,128]{2,1,0:T(8,128)} %bitcast.29), calls=%async_computation.1 | async-start | bytes 262144 | tf_op jit(solution)/shard_map/all_to_all | solution.py:613
  36.8 1.7 %collective-permute-start.5 = (f32[32,24,256]{2,1,0:T(8,128)}, f32[32,24,256]{2,1,0:T(8,128)S(1)}, u32[]{:S(2)}, u32[]{:S(2)}) collective-permute-start(f32[32,24,256]{2,1,0:T(8,128)} %get-tuple-element.44), channel_id=1, source_target_pairs={{0,2},{2,4},{4,6},{6,8},{8,10},{10,12},{12,14},{14,16},{16,18},{18... | collective-permute-start | bytes 2359304 | tf_op jit(solution)/shard_map/ppermute | solution.py:577
  38.5 0.0 copy-done.2
  38.5 0.0 collective-permute-start.6
  38.5 2.3 %collective-permute-done.3 = f32[32,16,256]{2,1,0:T(8,128)S(1)} collective-permute-done((f32[32,16,256]{2,1,0:T(8,128)}, f32[32,16,256]{2,1,0:T(8,128)S(1)}, u32[]{:S(2)}, u32[]{:S(2)}) %collective-permute-start.3) | collective-permute-done | bytes 524320 | tf_op jit(solution)/shard_map/ppermute | solution.py:577
  40.7 3.0 %collective-permute-done.4 = f32[32,16,256]{2,1,0:T(8,128)S(1)} collective-permute-done((f32[32,16,256]{2,1,0:T(8,128)}, f32[32,16,256]{2,1,0:T(8,128)S(1)}, u32[]{:S(2)}, u32[]{:S(2)}) %collective-permute-start.4) | collective-permute-done | bytes 524320 | tf_op jit(solution)/shard_map/ppermute | solution.py:578
  43.7 4.9 %middle_sums.1 = f32[32,24,256]{2,1,0:T(8,128)} custom-call(f32[32,27]{1,0:T(8,128)} %weight.3, f32[32,32]{1,0:T(8,128)} %point.3, f32[26,32,256]{2,1,0:T(8,128)} %copy-done.1, f32[26,32,256]{2,1,0:T(8,128)} %get-tuple-element.38.own, f32[26,32,256]{2,1,0:T(8,128)} %copy-done), custom_call_target="tpu_custom_call" | custom-call | flops 40000000000 | bytes 262144 | tf_op jit(solution)/shard_map/middle_sums/pallas_call | solution.py:516
  48.6 0.0 all-to-all-done.1
  48.6 5.7 %inverse_modes.1 = (f32[8,4,64,256]{3,2,1,0:T(8,128)}, f32[8,4,24,256]{3,2,1,0:T(8,128)S(1)}) custom-call(f32[16,16,128]{2,1,0:T(8,128)S(1)} %bitcast.19, f32[32]{0:T(128)} %bias.1, bf16[2,128,256]{2,1,0:T(8,128)(2,1)} %constant.32.clone.x_top, bf16[2,128,256]{2,1,0:T(8,128)(2,1)} %constant.33.clone.x_rest, bf16[2,64,32]{2,1,0:T(8,128)(2,1)} %constant.34.clone.y_top, ...), custom_call_target="tpu_custom_call" | custom-call | flops 100000000 | bytes 262144 | tf_op jit(solution)/shard_map/inverse_modes/pallas_call | solution.py:420
  54.3 3.8 %collective-permute-done.5.low = f32[32,24,256]{2,1,0:T(8,128)S(1)} collective-permute-done((f32[32,24,256]{2,1,0:T(8,128)}, f32[32,24,256]{2,1,0:T(8,128)S(1)}, u32[]{:S(2)}, u32[]{:S(2)}) %collective-permute-start.5) | collective-permute-done | bytes 786464 | tf_op jit(solution)/shard_map/ppermute | solution.py:577
  58.1 2.4 %collective-permute-done.6.high = f32[32,24,256]{2,1,0:T(8,128)S(1)} collective-permute-done((f32[32,24,256]{2,1,0:T(8,128)S(1)}, f32[32,24,256]{2,1,0:T(8,128)S(1)}, u32[]{:S(2)}, u32[]{:S(2)}) %collective-permute-start.6) | collective-permute-done | bytes 786464 | tf_op jit(solution)/shard_map/ppermute | solution.py:578
  60.5 1.5 %finished_rows.1 = f32[32,64,256]{2,1,0:T(8,128)} custom-call(f32[32,64,256]{2,1,0:T(8,128)} %bitcast.24, f32[32,24,256]{2,1,0:T(8,128)S(1)} %bitcast.16, f32[32,24,256]{2,1,0:T(8,128)S(1)} %collective-permute-done.5.low, f32[32,24,256]{2,1,0:T(8,128)S(1)} %collective-permute-done.6.high), custom_call_target="tpu_custom_call", output_to_operand_aliasing={{}: (0, {})} | custom-call | flops 100000000 | bytes 262144 | tf_op jit(solution)/shard_map/finished_rows/pallas_call | solution.py:446
Async XLA Ops:
  2.3 24.0 %collective-permute-start.2 = (f32[26,32,256]{2,1,0:T(8,128)}, f32[26,32,256]{2,1,0:T(8,128)S(1)}, u32[]{:S(2)}, u32[]{:S(2)}) collective-permute-start(f32[26,32,256]{2,1,0:T(8,128)} %get-tuple-element.38.own), channel_id=1, source_target_pairs={{0,30},{2,0},{4,2},{6,4},{8,6},{10,8},{12,10},{14,12},{16,14},{18,... | collective-permute-start | bytes 2555912 | tf_op jit(solution)/shard_map/ppermute | solution.py:578
  2.4 23.9 %collective-permute-start.1 = (f32[26,32,256]{2,1,0:T(8,128)}, f32[26,32,256]{2,1,0:T(8,128)S(1)}, u32[]{:S(2)}, u32[]{:S(2)}) collective-permute-start(f32[26,32,256]{2,1,0:T(8,128)} %get-tuple-element.38.own), channel_id=1, source_target_pairs={{0,2},{2,4},{4,6},{6,8},{8,10},{10,12},{12,14},{14,16},{16,18},{18... | collective-permute-start | bytes 2555912 | tf_op jit(solution)/shard_map/ppermute | solution.py:577
  5.1 5.4 %collective-permute-start = (f32[2,32,256]{2,1,0:T(8,128)}, f32[2,32,256]{2,1,0:T(8,128)S(1)}, u32[]{:S(2)}, u32[]{:S(2)}) collective-permute-start(f32[2,32,256]{2,1,0:T(8,128)} %get-tuple-element.28), channel_id=1, source_target_pairs={{0,1},{1,0},{2,3},{3,2},{4,5},{5,4},{6,7},{7,6},{8,9},{9,8},{10,11... | collective-permute-start | bytes 196616 | tf_op jit(solution)/shard_map/ppermute | solution.py:591
  10.4 17.4 %all-to-all-start = ((f32[32,8,128]{2,1,0:T(8,128)}), f32[32,8,128]{2,1,0:T(8,128)S(1)}, u32[]{:S(2)}, u32[]{:S(2)}) async-start(f32[32,8,128]{2,1,0:T(8,128)} %bitcast.27), calls=%async_computation | async-start | bytes 262144 | tf_op jit(solution)/shard_map/all_to_all | solution.py:608
  26.3 0.9 %copy-start = (f32[26,32,256]{2,1,0:T(8,128)}, f32[26,32,256]{2,1,0:T(8,128)S(1)}, u32[]{:S(2)}) copy-start(f32[26,32,256]{2,1,0:T(8,128)S(1)} %collective-permute-done.2.high) | copy-start | bytes 2555908
  26.3 4.3 %copy-start.1 = (f32[26,32,256]{2,1,0:T(8,128)}, f32[26,32,256]{2,1,0:T(8,128)S(1)}, u32[]{:S(2)}) copy-start(f32[26,32,256]{2,1,0:T(8,128)S(1)} %collective-permute-done.1.low) | copy-start | bytes 2555908
  27.2 13.5 %collective-permute-start.3 = (f32[32,16,256]{2,1,0:T(8,128)}, f32[32,16,256]{2,1,0:T(8,128)S(1)}, u32[]{:S(2)}, u32[]{:S(2)}) collective-permute-start(f32[32,16,256]{2,1,0:T(8,128)} %get-tuple-element.36), channel_id=1, source_target_pairs={{0,2},{2,4},{4,6},{6,8},{8,10},{10,12},{12,14},{14,16},{16,18},{18... | collective-permute-start | bytes 1572872 | tf_op jit(solution)/shard_map/ppermute | solution.py:577
  27.8 15.9 %collective-permute-start.4 = (f32[32,16,256]{2,1,0:T(8,128)}, f32[32,16,256]{2,1,0:T(8,128)S(1)}, u32[]{:S(2)}, u32[]{:S(2)}) collective-permute-start(f32[32,16,256]{2,1,0:T(8,128)} %get-tuple-element.37), channel_id=1, source_target_pairs={{0,30},{2,0},{4,2},{6,4},{8,6},{10,8},{12,10},{14,12},{16,14},{18,... | collective-permute-start | bytes 1572872 | tf_op jit(solution)/shard_map/ppermute | solution.py:578
  27.8 10.6 %copy-start.2 = (f32[32,24,256]{2,1,0:T(8,128)S(1)}, f32[32,24,256]{2,1,0:T(8,128)}, u32[]{:S(2)}) copy-start(f32[32,24,256]{2,1,0:T(8,128)} %get-tuple-element.46) | copy-start | bytes 2359300
  30.6 18.1 %all-to-all-start.1 = ((f32[32,8,128]{2,1,0:T(8,128)}), f32[32,8,128]{2,1,0:T(8,128)S(1)}, u32[]{:S(2)}, u32[]{:S(2)}) async-start(f32[32,8,128]{2,1,0:T(8,128)} %bitcast.29), calls=%async_computation.1 | async-start | bytes 262144 | tf_op jit(solution)/shard_map/all_to_all | solution.py:613
  36.8 21.4 %collective-permute-start.5 = (f32[32,24,256]{2,1,0:T(8,128)}, f32[32,24,256]{2,1,0:T(8,128)S(1)}, u32[]{:S(2)}, u32[]{:S(2)}) collective-permute-start(f32[32,24,256]{2,1,0:T(8,128)} %get-tuple-element.44), channel_id=1, source_target_pairs={{0,2},{2,4},{4,6},{6,8},{8,10},{10,12},{12,14},{14,16},{16,18},{18... | collective-permute-start | bytes 2359304 | tf_op jit(solution)/shard_map/ppermute | solution.py:577
  38.5 22.1 %collective-permute-start.6 = (f32[32,24,256]{2,1,0:T(8,128)S(1)}, f32[32,24,256]{2,1,0:T(8,128)S(1)}, u32[]{:S(2)}, u32[]{:S(2)}) collective-permute-start(f32[32,24,256]{2,1,0:T(8,128)S(1)} %copy-done.2), channel_id=1, source_target_pairs={{0,30},{2,0},{4,2},{6,4},{8,6},{10,8},{12,10},{14,12},{16,14},{18,... | collective-permute-start | bytes 2359304 | tf_op jit(solution)/shard_map/ppermute | solution.py:578

commit v18 on v16

--- a/solution.py
+++ b/solution.py
@@ -606,6 +606,7 @@
     if whole_tiles:
         both = ("gz", "gy")
         got = lax.all_to_all(coarse, both, split_axis=0, concat_axis=0, tiled=True)
+        down, up = lax.optimization_barrier((down, up, first_low))[:2]
         pair = to_neighbours(down, up)
         gains = after(spectral_filter, first_low, first_high, second)
         mark = filter_call(got, gains, gz, gy, forward_scale)

time: 71.1 us -> 61.8 us (0.87)
  waiting for transfers between devices: 20.1 us -> 14.5 us
  starting transfers between devices: 21.7 us -> 18.5 us
    ppermute x3, waiting for transfers between devices: 15.9 us -> 10.8 us  [to_neighbours(): lax.ppermute(down, 'gz', ring('gz', gz, 1))]
    ppermute x3, starting transfers between devices: 2.53 us -> 0.01 us  [to_neighbours(): lax.ppermute(up, 'gz', ring('gz', gz, -1))]
    all_to_all x1, waiting for transfers between devices: 1.57 us -> 0.01 us  [body(): back = lax.all_to_all(mark, both, split_axis=0, concat_axis=0, tiled=True)]
    ppermute x3, waiting for transfers between devices: 2.62 us -> 3.62 us  [to_neighbours(): lax.ppermute(up, 'gz', ring('gz', gz, -1))]
    all_to_all x1, starting transfers between devices: 6.55 us -> 5.78 us  [body(): got = lax.all_to_all(coarse, both, split_axis=0, concat_axis=0, tiled=True)]
  transfers between devices with their start and end apart: 9 -> 9, of which waited for: 5 -> 6; matrix products, arithmetic and copies ran while one was open for 0% -> 0% of each run, Pallas kernels for 31% -> 40%
where the time goes in v18:
time: 61.8 us; the launch traced here: 61.4 us
  Pallas kernels  28.3 us (46%)
  starting transfers between devices  18.5 us (30%)
  waiting for transfers between devices  14.5 us (23%)
    ppermute x3, waiting for transfers between devices, to_neighbours(): lax.ppermute(down, 'gz', ring('gz', gz, 1))  10.8 us
    pallas_call x1, Pallas kernels, own_call(): pl.pallas_call(functools.partial(own_kernel, segments, groups), out_shape...  7.13 us
    all_to_all x1, starting transfers between devices, body(): back = lax.all_to_all(mark, both, split_axis=0, concat_axis=0, tiled=True)  6.2 us
    all_to_all x1, starting transfers between devices, body(): got = lax.all_to_all(coarse, both, split_axis=0, concat_axis=0, tiled=True)  5.78 us
    pallas_call x1, Pallas kernels, inverse_call(): pl.pallas_call(functools.partial(inverse_kernel, upper), out_shape=[jax.S...  5.68 us
    ppermute x3, starting transfers between devices, to_neighbours(): lax.ppermute(down, 'gz', ring('gz', gz, 1))  5.27 us
    pallas_call x1, Pallas kernels, middle_call(): pl.pallas_call(middle_kernel, out_shape=pltpu.HBM((CH, rows, NX), F32), i...  4.9 us
    pallas_call x1, Pallas kernels, forward_call(): pl.pallas_call(forward_kernel, out_shape=(pltpu.HBM if pinned else jax.Sh...  4.14 us
  transfers between devices with their start and end apart: 9, of which 6 were waited for; matrix products, arithmetic and copies ran while one was open for 0% of the time, Pallas kernels for 40%

profile of v18, /device:TPU:1, one launch (start us, length us, event | category | flops | bytes accessed | tf_op | source)
XLA Modules:
  0.0 61.4 jit_solution(827652148552111686)
XLA Ops:
  0.0 2.3 %packed_rows.1 = (f32[26,32,256]{2,1,0:T(8,128)}, f32[2,32,256]{2,1,0:T(8,128)}) custom-call(f32[32,64,256]{2,1,0:T(8,128)} %bitcast.21), custom_call_target="tpu_custom_call" | custom-call | flops 100000000 | bytes 262144 | tf_op jit(solution)/shard_map/packed_rows/pallas_call | solution.py:466
  2.3 2.7 %collective-permute-start.1 = (f32[26,32,256]{2,1,0:T(8,128)}, f32[26,32,256]{2,1,0:T(8,128)S(1)}, u32[]{:S(2)}, u32[]{:S(2)}) collective-permute-start(f32[26,32,256]{2,1,0:T(8,128)} %get-tuple-element.38.own), channel_id=1, source_target_pairs={{0,2},{2,4},{4,6},{6,8},{8,10},{10,12},{12,14},{14,16},{16,18},{18... | collective-permute-start | bytes 2555912 | tf_op jit(solution)/shard_map/ppermute | solution.py:577
  5.0 0.0 collective-permute-start.2
  5.0 1.2 %collective-permute-start = (f32[2,32,256]{2,1,0:T(8,128)}, f32[2,32,256]{2,1,0:T(8,128)S(1)}, u32[]{:S(2)}, u32[]{:S(2)}) collective-permute-start(f32[2,32,256]{2,1,0:T(8,128)} %get-tuple-element.28), channel_id=1, source_target_pairs={{0,1},{1,0},{2,3},{3,2},{4,5},{5,4},{6,7},{7,6},{8,9},{9,8},{10,11... | collective-permute-start | bytes 196616 | tf_op jit(solution)/shard_map/ppermute | solution.py:591
  6.2 4.1 %forward_modes.1 = f32[256,128]{1,0:T(8,128)} custom-call(f32[8,4,64,256]{3,2,1,0:T(8,128)} %bitcast.22, bf16[2,256,128]{2,1,0:T(8,128)(2,1)} %constant.24.clone.x_top, bf16[2,256,128]{2,1,0:T(8,128)(2,1)} %constant.25.clone.x_rest, bf16[2,32,64]{2,1,0:T(8,128)(2,1)} %constant.26.clone.y_top, bf16[2,32,64]{2,1,0:T(8,128)(2,1)} %constant.27.clone.y_rest), custom_call_target="tpu_custom_call" | custom-call | flops 100000000 | bytes 262144 | tf_op jit(solution)/shard_map/forward_modes/pallas_call | solution.py:387
  10.3 0.0 collective-permute-done.halo
  10.4 5.8 %all-to-all-start = ((f32[32,8,128]{2,1,0:T(8,128)}), f32[32,8,128]{2,1,0:T(8,128)S(1)}, u32[]{:S(2)}, u32[]{:S(2)}) async-start(f32[32,8,128]{2,1,0:T(8,128)} %bitcast.27), calls=%async_computation | async-start | bytes 262144 | tf_op jit(solution)/shard_map/all_to_all | solution.py:608
  16.1 7.1 %own_sums.1 = (f32[32,16,256]{2,1,0:T(8,128)}, f32[32,16,256]{2,1,0:T(8,128)}, f32[32,16,256]{2,1,0:T(8,128)}, f32[32,24,256]{2,1,0:T(8,128)}, f32[32,24,256]{2,1,0:T(8,128)}, /*index=5*/f32[32,24,256]{2,1,0:T(8,128)}) custom-call(f32[32,27]{1,0:T(8,128)} %weight.3, f32[32,32]{1,0:T(8,128)} %point.3, f32[32,64,256]{2,1,0:T(8,128)} %bitcast.23, ...), custom_call_target="tpu_custom_call" | custom-call | flops 100000000 | bytes 262144 | tf_op jit(solution)/shard_map/own_sums/pallas_call | solution.py:489
  23.3 2.1 %collective-permute-done.1.low = f32[26,32,256]{2,1,0:T(8,128)S(1)} collective-permute-done((f32[26,32,256]{2,1,0:T(8,128)}, f32[26,32,256]{2,1,0:T(8,128)S(1)}, u32[]{:S(2)}, u32[]{:S(2)}) %collective-permute-start.1) | collective-permute-done | bytes 852000 | tf_op jit(solution)/shard_map/ppermute | solution.py:577
  25.4 0.0 copy-start
  25.4 2.4 %collective-permute-done.2.high = f32[26,32,256]{2,1,0:T(8,128)S(1)} collective-permute-done((f32[26,32,256]{2,1,0:T(8,128)}, f32[26,32,256]{2,1,0:T(8,128)S(1)}, u32[]{:S(2)}, u32[]{:S(2)}) %collective-permute-start.2) | collective-permute-done | bytes 852000 | tf_op jit(solution)/shard_map/ppermute | solution.py:578
  27.8 0.0 copy-done
  27.8 0.0 copy-start.1
  27.8 0.9 %collective-permute-start.3 = (f32[32,16,256]{2,1,0:T(8,128)}, f32[32,16,256]{2,1,0:T(8,128)S(1)}, u32[]{:S(2)}, u32[]{:S(2)}) collective-permute-start(f32[32,16,256]{2,1,0:T(8,128)} %get-tuple-element.36), channel_id=1, source_target_pairs={{0,2},{2,4},{4,6},{6,8},{8,10},{10,12},{12,14},{14,16},{16,18},{18... | collective-permute-start | bytes 1572872 | tf_op jit(solution)/shard_map/ppermute | solution.py:577
  28.7 0.0 collective-permute-start.4
  28.7 0.0 all-to-all-done
  28.7 0.0 copy-start.2
  28.7 2.7 %filter_modes.1 = f32[256,128]{1,0:T(8,128)} custom-call(f32[256,128]{1,0:T(8,128)S(1)} %bitcast.20, f32[2,16,8,64]{3,2,1,0:T(8,128)} %gains, bf16[256,256]{1,0:T(8,128)(2,1)} %constant.28.clone.f_top, bf16[256,256]{1,0:T(8,128)(2,1)} %constant.29.clone.f_rest, bf16[512,128]{1,0:T(8,128)(2,1)} %constant.30.clone.i_top, bf16[512,128]{1,0:T(8,128)(2,1)} %constant.31.clone.i_rest), custom_call_target="tpu_custom_call" | custom-call | flops 40000000000 | bytes 262144 | tf_op jit(solution)/shard_map/filter_modes/pallas_call | solution.py:406
  31.4 0.0 copy-done.1
  31.4 6.2 %all-to-all-start.1 = ((f32[32,8,128]{2,1,0:T(8,128)}), f32[32,8,128]{2,1,0:T(8,128)S(1)}, u32[]{:S(2)}, u32[]{:S(2)}) async-start(f32[32,8,128]{2,1,0:T(8,128)} %bitcast.29), calls=%async_computation.1 | async-start | bytes 262144 | tf_op jit(solution)/shard_map/all_to_all | solution.py:613
  37.6 1.7 %collective-permute-start.5 = (f32[32,24,256]{2,1,0:T(8,128)}, f32[32,24,256]{2,1,0:T(8,128)S(1)}, u32[]{:S(2)}, u32[]{:S(2)}) collective-permute-start(f32[32,24,256]{2,1,0:T(8,128)} %get-tuple-element.44), channel_id=1, source_target_pairs={{0,2},{2,4},{4,6},{6,8},{8,10},{10,12},{12,14},{14,16},{16,18},{18... | collective-permute-start | bytes 2359304 | tf_op jit(solution)/shard_map/ppermute | solution.py:577
  39.3 0.0 copy-done.2
  39.3 0.0 collective-permute-start.6
  39.3 2.1 %collective-permute-done.3 = f32[32,16,256]{2,1,0:T(8,128)S(1)} collective-permute-done((f32[32,16,256]{2,1,0:T(8,128)}, f32[32,16,256]{2,1,0:T(8,128)S(1)}, u32[]{:S(2)}, u32[]{:S(2)}) %collective-permute-start.3) | collective-permute-done | bytes 524320 | tf_op jit(solution)/shard_map/ppermute | solution.py:577
  41.4 0.2 collective-permute-done.4
  41.6 4.9 %middle_sums.1 = f32[32,24,256]{2,1,0:T(8,128)} custom-call(f32[32,27]{1,0:T(8,128)} %weight.3, f32[32,32]{1,0:T(8,128)} %point.3, f32[26,32,256]{2,1,0:T(8,128)} %copy-done, f32[26,32,256]{2,1,0:T(8,128)} %get-tuple-element.38.own, f32[26,32,256]{2,1,0:T(8,128)} %copy-done.1), custom_call_target="tpu_custom_call" | custom-call | flops 40000000000 | bytes 262144 | tf_op jit(solution)/shard_map/middle_sums/pallas_call | solution.py:516
  46.5 0.0 all-to-all-done.1
  46.5 5.7 %inverse_modes.1 = (f32[8,4,64,256]{3,2,1,0:T(8,128)}, f32[8,4,24,256]{3,2,1,0:T(8,128)S(1)}) custom-call(f32[16,16,128]{2,1,0:T(8,128)S(1)} %bitcast.19, f32[32]{0:T(128)} %bias.1, bf16[2,128,256]{2,1,0:T(8,128)(2,1)} %constant.32.clone.x_top, bf16[2,128,256]{2,1,0:T(8,128)(2,1)} %constant.33.clone.x_rest, bf16[2,64,32]{2,1,0:T(8,128)(2,1)} %constant.34.clone.y_top, ...), custom_call_target="tpu_custom_call" | custom-call | flops 100000000 | bytes 262144 | tf_op jit(solution)/shard_map/inverse_modes/pallas_call | solution.py:420
  52.2 6.7 %collective-permute-done.5.low = f32[32,24,256]{2,1,0:T(8,128)S(1)} collective-permute-done((f32[32,24,256]{2,1,0:T(8,128)}, f32[32,24,256]{2,1,0:T(8,128)S(1)}, u32[]{:S(2)}, u32[]{:S(2)}) %collective-permute-start.5) | collective-permute-done | bytes 786464 | tf_op jit(solution)/shard_map/ppermute | solution.py:577
  58.9 1.0 %collective-permute-done.6.high = f32[32,24,256]{2,1,0:T(8,128)S(1)} collective-permute-done((f32[32,24,256]{2,1,0:T(8,128)S(1)}, f32[32,24,256]{2,1,0:T(8,128)S(1)}, u32[]{:S(2)}, u32[]{:S(2)}) %collective-permute-start.6) | collective-permute-done | bytes 786464 | tf_op jit(solution)/shard_map/ppermute | solution.py:578
  59.9 1.5 %finished_rows.1 = f32[32,64,256]{2,1,0:T(8,128)} custom-call(f32[32,64,256]{2,1,0:T(8,128)} %bitcast.24, f32[32,24,256]{2,1,0:T(8,128)S(1)} %bitcast.16, f32[32,24,256]{2,1,0:T(8,128)S(1)} %collective-permute-done.5.low, f32[32,24,256]{2,1,0:T(8,128)S(1)} %collective-permute-done.6.high), custom_call_target="tpu_custom_call", output_to_operand_aliasing={{}: (0, {})} | custom-call | flops 100000000 | bytes 262144 | tf_op jit(solution)/shard_map/finished_rows/pallas_call | solution.py:446
Async XLA Ops:
  2.3 23.1 %collective-permute-start.1 = (f32[26,32,256]{2,1,0:T(8,128)}, f32[26,32,256]{2,1,0:T(8,128)S(1)}, u32[]{:S(2)}, u32[]{:S(2)}) collective-permute-start(f32[26,32,256]{2,1,0:T(8,128)} %get-tuple-element.38.own), channel_id=1, source_target_pairs={{0,2},{2,4},{4,6},{6,8},{8,10},{10,12},{12,14},{14,16},{16,18},{18... | collective-permute-start | bytes 2555912 | tf_op jit(solution)/shard_map/ppermute | solution.py:577
  5.0 22.8 %collective-permute-start.2 = (f32[26,32,256]{2,1,0:T(8,128)}, f32[26,32,256]{2,1,0:T(8,128)S(1)}, u32[]{:S(2)}, u32[]{:S(2)}) collective-permute-start(f32[26,32,256]{2,1,0:T(8,128)} %get-tuple-element.38.own), channel_id=1, source_target_pairs={{0,30},{2,0},{4,2},{6,4},{8,6},{10,8},{12,10},{14,12},{16,14},{18,... | collective-permute-start | bytes 2555912 | tf_op jit(solution)/shard_map/ppermute | solution.py:578
  5.0 5.4 %collective-permute-start = (f32[2,32,256]{2,1,0:T(8,128)}, f32[2,32,256]{2,1,0:T(8,128)S(1)}, u32[]{:S(2)}, u32[]{:S(2)}) collective-permute-start(f32[2,32,256]{2,1,0:T(8,128)} %get-tuple-element.28), channel_id=1, source_target_pairs={{0,1},{1,0},{2,3},{3,2},{4,5},{5,4},{6,7},{7,6},{8,9},{9,8},{10,11... | collective-permute-start | bytes 196616 | tf_op jit(solution)/shard_map/ppermute | solution.py:591
  10.4 18.3 %all-to-all-start = ((f32[32,8,128]{2,1,0:T(8,128)}), f32[32,8,128]{2,1,0:T(8,128)S(1)}, u32[]{:S(2)}, u32[]{:S(2)}) async-start(f32[32,8,128]{2,1,0:T(8,128)} %bitcast.27), calls=%async_computation | async-start | bytes 262144 | tf_op jit(solution)/shard_map/all_to_all | solution.py:608
  25.4 2.4 %copy-start = (f32[26,32,256]{2,1,0:T(8,128)}, f32[26,32,256]{2,1,0:T(8,128)S(1)}, u32[]{:S(2)}) copy-start(f32[26,32,256]{2,1,0:T(8,128)S(1)} %collective-permute-done.1.low) | copy-start | bytes 2555908
  27.8 3.6 %copy-start.1 = (f32[26,32,256]{2,1,0:T(8,128)}, f32[26,32,256]{2,1,0:T(8,128)S(1)}, u32[]{:S(2)}) copy-start(f32[26,32,256]{2,1,0:T(8,128)S(1)} %collective-permute-done.2.high) | copy-start | bytes 2555908
  27.8 13.6 %collective-permute-start.3 = (f32[32,16,256]{2,1,0:T(8,128)}, f32[32,16,256]{2,1,0:T(8,128)S(1)}, u32[]{:S(2)}, u32[]{:S(2)}) collective-permute-start(f32[32,16,256]{2,1,0:T(8,128)} %get-tuple-element.36), channel_id=1, source_target_pairs={{0,2},{2,4},{4,6},{6,8},{8,10},{10,12},{12,14},{14,16},{16,18},{18... | collective-permute-start | bytes 1572872 | tf_op jit(solution)/shard_map/ppermute | solution.py:577
  28.7 12.9 %collective-permute-start.4 = (f32[32,16,256]{2,1,0:T(8,128)}, f32[32,16,256]{2,1,0:T(8,128)S(1)}, u32[]{:S(2)}, u32[]{:S(2)}) collective-permute-start(f32[32,16,256]{2,1,0:T(8,128)} %get-tuple-element.37), channel_id=1, source_target_pairs={{0,30},{2,0},{4,2},{6,4},{8,6},{10,8},{12,10},{14,12},{16,14},{18,... | collective-permute-start | bytes 1572872 | tf_op jit(solution)/shard_map/ppermute | solution.py:578
  28.7 10.6 %copy-start.2 = (f32[32,24,256]{2,1,0:T(8,128)S(1)}, f32[32,24,256]{2,1,0:T(8,128)}, u32[]{:S(2)}) copy-start(f32[32,24,256]{2,1,0:T(8,128)} %get-tuple-element.46) | copy-start | bytes 2359300
  31.4 15.1 %all-to-all-start.1 = ((f32[32,8,128]{2,1,0:T(8,128)}), f32[32,8,128]{2,1,0:T(8,128)S(1)}, u32[]{:S(2)}, u32[]{:S(2)}) async-start(f32[32,8,128]{2,1,0:T(8,128)} %bitcast.29), calls=%async_computation.1 | async-start | bytes 262144 | tf_op jit(solution)/shard_map/all_to_all | solution.py:613
  37.6 21.3 %collective-permute-start.5 = (f32[32,24,256]{2,1,0:T(8,128)}, f32[32,24,256]{2,1,0:T(8,128)S(1)}, u32[]{:S(2)}, u32[]{:S(2)}) collective-permute-start(f32[32,24,256]{2,1,0:T(8,128)} %get-tuple-element.44), channel_id=1, source_target_pairs={{0,2},{2,4},{4,6},{6,8},{8,10},{10,12},{12,14},{14,16},{16,18},{18... | collective-permute-start | bytes 2359304 | tf_op jit(solution)/shard_map/ppermute | solution.py:577
  39.3 20.6 %collective-permute-start.6 = (f32[32,24,256]{2,1,0:T(8,128)S(1)}, f32[32,24,256]{2,1,0:T(8,128)S(1)}, u32[]{:S(2)}, u32[]{:S(2)}) collective-permute-start(f32[32,24,256]{2,1,0:T(8,128)S(1)} %copy-done.2), channel_id=1, source_target_pairs={{0,30},{2,0},{4,2},{6,4},{8,6},{10,8},{12,10},{14,12},{16,14},{18,... | collective-permute-start | bytes 2359304 | tf_op jit(solution)/shard_map/ppermute | solution.py:578

commit v19 on v18

--- a/solution.py
+++ b/solution.py
@@ -16,6 +16,7 @@
 MZ = 16
 CH = 32
 VMEM_BYTES = 20 * 1024 * 1024
+ALL_VMEM_BYTES = 63 * 1024 * 1024
 BF = jnp.bfloat16
 F32 = jnp.float32
 
@@ -364,8 +365,8 @@
     return [pltpu.with_memory_space_constraint(a, pltpu.HBM) for a in arrays]
 
 
-def params():
-    return pltpu.CompilerParams(vmem_limit_bytes=VMEM_BYTES)
+def params(limit=VMEM_BYTES):
+    return pltpu.CompilerParams(vmem_limit_bytes=limit)
 
 
 def cost(flops, moved):
@@ -394,7 +395,7 @@
             pltpu.VMEM((2, 2 * MY, y_local), BF),
             pltpu.SemaphoreType.DMA((8,)),
         ],
-        compiler_params=params(),
+        compiler_params=params(ALL_VMEM_BYTES),
         cost_estimate=cost(10**8, 2**18),
         name="forward_modes",
     )(*in_hbm(by_four(field), *tables))

time: 61.8 us -> 60.9 us (0.985)
  starting transfers between devices: 18.5 us -> 17.5 us
    ppermute x3, starting transfers between devices: 5.27 us -> 4.37 us  [to_neighbours(): lax.ppermute(down, 'gz', ring('gz', gz, 1))]
  transfers between devices with their start and end apart: 9 -> 9, of which waited for: 6 -> 5; matrix products, arithmetic and copies ran while one was open for 0% -> 0% of each run, Pallas kernels for 40% -> 40%
where the time goes in v19:
time: 60.9 us; the launch traced here: 60.5 us
  Pallas kernels  28.3 us (46%)
  starting transfers between devices  17.5 us (29%)
  waiting for transfers between devices  14.7 us (24%)
    ppermute x3, waiting for transfers between devices, to_neighbours(): lax.ppermute(down, 'gz', ring('gz', gz, 1))  11.4 us
    pallas_call x1, Pallas kernels, own_call(): pl.pallas_call(functools.partial(own_kernel, segments, groups), out_shape...  7.16 us
    all_to_all x1, starting transfers between devices, body(): got = lax.all_to_all(coarse, both, split_axis=0, concat_axis=0, tiled=True)  5.78 us
    pallas_call x1, Pallas kernels, inverse_call(): pl.pallas_call(functools.partial(inverse_kernel, upper), out_shape=[jax.S...  5.69 us
    all_to_all x1, starting transfers between devices, body(): back = lax.all_to_all(mark, both, split_axis=0, concat_axis=0, tiled=True)  5.6 us
    pallas_call x1, Pallas kernels, middle_call(): pl.pallas_call(middle_kernel, out_shape=pltpu.HBM((CH, rows, NX), F32), i...  4.87 us
    ppermute x3, starting transfers between devices, to_neighbours(): lax.ppermute(down, 'gz', ring('gz', gz, 1))  4.37 us
    pallas_call x1, Pallas kernels, forward_call(): pl.pallas_call(forward_kernel, out_shape=(pltpu.HBM if pinned else jax.Sh...  4.14 us
  transfers between devices with their start and end apart: 9, of which 5 were waited for; matrix products, arithmetic and copies ran while one was open for 0% of the time, Pallas kernels for 40%

profile of v19, /device:TPU:1, one launch (start us, length us, event | category | flops | bytes accessed | tf_op | source)
XLA Modules:
  0.0 60.5 jit_solution(1450351044636259210)
XLA Ops:
  0.0 2.3 %packed_rows.1 = (f32[26,32,256]{2,1,0:T(8,128)}, f32[2,32,256]{2,1,0:T(8,128)}) custom-call(f32[32,64,256]{2,1,0:T(8,128)} %bitcast.21), custom_call_target="tpu_custom_call" | custom-call | flops 100000000 | bytes 262144 | tf_op jit(solution)/shard_map/packed_rows/pallas_call | solution.py:467
  2.3 2.7 %collective-permute-start.1 = (f32[26,32,256]{2,1,0:T(8,128)}, f32[26,32,256]{2,1,0:T(8,128)S(1)}, u32[]{:S(2)}, u32[]{:S(2)}) collective-permute-start(f32[26,32,256]{2,1,0:T(8,128)} %get-tuple-element.38.own), channel_id=1, source_target_pairs={{0,2},{2,4},{4,6},{6,8},{8,10},{10,12},{12,14},{14,16},{16,18},{18... | collective-permute-start | bytes 2555912 | tf_op jit(solution)/shard_map/ppermute | solution.py:578
  5.0 0.0 collective-permute-start.2
  5.0 1.2 %collective-permute-start = (f32[2,32,256]{2,1,0:T(8,128)}, f32[2,32,256]{2,1,0:T(8,128)S(1)}, u32[]{:S(2)}, u32[]{:S(2)}) collective-permute-start(f32[2,32,256]{2,1,0:T(8,128)} %get-tuple-element.28), channel_id=1, source_target_pairs={{0,1},{1,0},{2,3},{3,2},{4,5},{5,4},{6,7},{7,6},{8,9},{9,8},{10,11... | collective-permute-start | bytes 196616 | tf_op jit(solution)/shard_map/ppermute | solution.py:592
  6.2 4.1 %forward_modes.1 = f32[256,128]{1,0:T(8,128)} custom-call(f32[8,4,64,256]{3,2,1,0:T(8,128)} %bitcast.22, bf16[2,256,128]{2,1,0:T(8,128)(2,1)} %constant.24.clone.x_top, bf16[2,256,128]{2,1,0:T(8,128)(2,1)} %constant.25.clone.x_rest, bf16[2,32,64]{2,1,0:T(8,128)(2,1)} %constant.26.clone.y_top, bf16[2,32,64]{2,1,0:T(8,128)(2,1)} %constant.27.clone.y_rest), custom_call_target="tpu_custom_call" | custom-call | flops 100000000 | bytes 262144 | tf_op jit(solution)/shard_map/forward_modes/pallas_call | solution.py:388
  10.3 0.0 collective-permute-done.halo
  10.4 5.8 %all-to-all-start = ((f32[32,8,128]{2,1,0:T(8,128)}), f32[32,8,128]{2,1,0:T(8,128)S(1)}, u32[]{:S(2)}, u32[]{:S(2)}) async-start(f32[32,8,128]{2,1,0:T(8,128)} %bitcast.27), calls=%async_computation | async-start | bytes 262144 | tf_op jit(solution)/shard_map/all_to_all | solution.py:609
  16.1 7.2 %own_sums.1 = (f32[32,16,256]{2,1,0:T(8,128)}, f32[32,16,256]{2,1,0:T(8,128)}, f32[32,16,256]{2,1,0:T(8,128)}, f32[32,24,256]{2,1,0:T(8,128)}, f32[32,24,256]{2,1,0:T(8,128)}, /*index=5*/f32[32,24,256]{2,1,0:T(8,128)}) custom-call(f32[32,27]{1,0:T(8,128)} %weight.3, f32[32,32]{1,0:T(8,128)} %point.3, f32[32,64,256]{2,1,0:T(8,128)} %bitcast.23, ...), custom_call_target="tpu_custom_call" | custom-call | flops 100000000 | bytes 262144 | tf_op jit(solution)/shard_map/own_sums/pallas_call | solution.py:490
  23.3 2.1 %collective-permute-done.1.low = f32[26,32,256]{2,1,0:T(8,128)S(1)} collective-permute-done((f32[26,32,256]{2,1,0:T(8,128)}, f32[26,32,256]{2,1,0:T(8,128)S(1)}, u32[]{:S(2)}, u32[]{:S(2)}) %collective-permute-start.1) | collective-permute-done | bytes 852000 | tf_op jit(solution)/shard_map/ppermute | solution.py:578
  25.4 0.0 copy-start
  25.4 2.5 %collective-permute-done.2.high = f32[26,32,256]{2,1,0:T(8,128)} collective-permute-done((f32[26,32,256]{2,1,0:T(8,128)}, f32[26,32,256]{2,1,0:T(8,128)}, u32[]{:S(2)}, u32[]{:S(2)}) %collective-permute-start.2) | collective-permute-done | bytes 852000 | tf_op jit(solution)/shard_map/ppermute | solution.py:579
  27.9 0.0 collective-permute-start.3
  27.9 0.5 collective-permute-start.4
  28.4 0.0 all-to-all-done
  28.4 2.6 %filter_modes.1 = f32[256,128]{1,0:T(8,128)} custom-call(f32[256,128]{1,0:T(8,128)S(1)} %bitcast.20, f32[2,16,8,64]{3,2,1,0:T(8,128)} %gains, bf16[256,256]{1,0:T(8,128)(2,1)} %constant.28.clone.f_top, bf16[256,256]{1,0:T(8,128)(2,1)} %constant.29.clone.f_rest, bf16[512,128]{1,0:T(8,128)(2,1)} %constant.30.clone.i_top, bf16[512,128]{1,0:T(8,128)(2,1)} %constant.31.clone.i_rest), custom_call_target="tpu_custom_call" | custom-call | flops 40000000000 | bytes 262144 | tf_op jit(solution)/shard_map/filter_modes/pallas_call | solution.py:407
  31.0 0.0 copy-done
  31.0 5.6 %all-to-all-start.1 = ((f32[32,8,128]{2,1,0:T(8,128)}), f32[32,8,128]{2,1,0:T(8,128)S(1)}, u32[]{:S(2)}, u32[]{:S(2)}) async-start(f32[32,8,128]{2,1,0:T(8,128)} %bitcast.29), calls=%async_computation.1 | async-start | bytes 262144 | tf_op jit(solution)/shard_map/all_to_all | solution.py:614
  36.6 1.7 %collective-permute-start.5 = (f32[32,24,256]{2,1,0:T(8,128)}, f32[32,24,256]{2,1,0:T(8,128)S(1)}, u32[]{:S(2)}, u32[]{:S(2)}) collective-permute-start(f32[32,24,256]{2,1,0:T(8,128)} %get-tuple-element.44), channel_id=1, source_target_pairs={{0,2},{2,4},{4,6},{6,8},{8,10},{10,12},{12,14},{14,16},{16,18},{18... | collective-permute-start | bytes 2359304 | tf_op jit(solution)/shard_map/ppermute | solution.py:578
  38.3 0.0 collective-permute-start.6
  38.3 2.5 %collective-permute-done.3 = f32[32,16,256]{2,1,0:T(8,128)S(1)} collective-permute-done((f32[32,16,256]{2,1,0:T(8,128)}, f32[32,16,256]{2,1,0:T(8,128)S(1)}, u32[]{:S(2)}, u32[]{:S(2)}) %collective-permute-start.3) | collective-permute-done | bytes 524320 | tf_op jit(solution)/shard_map/ppermute | solution.py:578
  40.8 0.0 collective-permute-done.4
  40.8 4.9 %middle_sums.1 = f32[32,24,256]{2,1,0:T(8,128)} custom-call(f32[32,27]{1,0:T(8,128)} %weight.3, f32[32,32]{1,0:T(8,128)} %point.3, f32[26,32,256]{2,1,0:T(8,128)} %copy-done, f32[26,32,256]{2,1,0:T(8,128)} %get-tuple-element.38.own, f32[26,32,256]{2,1,0:T(8,128)} %collective-permute-done.2.high), custom_call_target="tpu_custom_call" | custom-call | flops 40000000000 | bytes 262144 | tf_op jit(solution)/shard_map/middle_sums/pallas_call | solution.py:517
  45.7 0.0 all-to-all-done.1
  45.7 5.7 %inverse_modes.1 = (f32[8,4,64,256]{3,2,1,0:T(8,128)}, f32[8,4,24,256]{3,2,1,0:T(8,128)S(1)}) custom-call(f32[16,16,128]{2,1,0:T(8,128)S(1)} %bitcast.19, f32[32]{0:T(128)} %bias.1, bf16[2,128,256]{2,1,0:T(8,128)(2,1)} %constant.32.clone.x_top, bf16[2,128,256]{2,1,0:T(8,128)(2,1)} %constant.33.clone.x_rest, bf16[2,64,32]{2,1,0:T(8,128)(2,1)} %constant.34.clone.y_top, ...), custom_call_target="tpu_custom_call" | custom-call | flops 100000000 | bytes 262144 | tf_op jit(solution)/shard_map/inverse_modes/pallas_call | solution.py:421
  51.4 6.8 %collective-permute-done.5.low = f32[32,24,256]{2,1,0:T(8,128)S(1)} collective-permute-done((f32[32,24,256]{2,1,0:T(8,128)}, f32[32,24,256]{2,1,0:T(8,128)S(1)}, u32[]{:S(2)}, u32[]{:S(2)}) %collective-permute-start.5) | collective-permute-done | bytes 786464 | tf_op jit(solution)/shard_map/ppermute | solution.py:578
  58.2 0.8 %collective-permute-done.6.high = f32[32,24,256]{2,1,0:T(8,128)S(1)} collective-permute-done((f32[32,24,256]{2,1,0:T(8,128)}, f32[32,24,256]{2,1,0:T(8,128)S(1)}, u32[]{:S(2)}, u32[]{:S(2)}) %collective-permute-start.6) | collective-permute-done | bytes 786464 | tf_op jit(solution)/shard_map/ppermute | solution.py:579
  59.0 1.5 %finished_rows.1 = f32[32,64,256]{2,1,0:T(8,128)} custom-call(f32[32,64,256]{2,1,0:T(8,128)} %bitcast.24, f32[32,24,256]{2,1,0:T(8,128)S(1)} %bitcast.16, f32[32,24,256]{2,1,0:T(8,128)S(1)} %collective-permute-done.5.low, f32[32,24,256]{2,1,0:T(8,128)S(1)} %collective-permute-done.6.high), custom_call_target="tpu_custom_call", output_to_operand_aliasing={{}: (0, {})} | custom-call | flops 100000000 | bytes 262144 | tf_op jit(solution)/shard_map/finished_rows/pallas_call | solution.py:447
Async XLA Ops:
  2.3 23.1 %collective-permute-start.1 = (f32[26,32,256]{2,1,0:T(8,128)}, f32[26,32,256]{2,1,0:T(8,128)S(1)}, u32[]{:S(2)}, u32[]{:S(2)}) collective-permute-start(f32[26,32,256]{2,1,0:T(8,128)} %get-tuple-element.38.own), channel_id=1, source_target_pairs={{0,2},{2,4},{4,6},{6,8},{8,10},{10,12},{12,14},{14,16},{16,18},{18... | collective-permute-start | bytes 2555912 | tf_op jit(solution)/shard_map/ppermute | solution.py:578
  5.0 22.9 %collective-permute-start.2 = (f32[26,32,256]{2,1,0:T(8,128)}, f32[26,32,256]{2,1,0:T(8,128)}, u32[]{:S(2)}, u32[]{:S(2)}) collective-permute-start(f32[26,32,256]{2,1,0:T(8,128)} %get-tuple-element.38.own), channel_id=1, source_target_pairs={{0,30},{2,0},{4,2},{6,4},{8,6},{10,8},{12,10},{14,12},{16,14},{18,... | collective-permute-start | bytes 2555912 | tf_op jit(solution)/shard_map/ppermute | solution.py:579
  5.0 5.4 %collective-permute-start = (f32[2,32,256]{2,1,0:T(8,128)}, f32[2,32,256]{2,1,0:T(8,128)S(1)}, u32[]{:S(2)}, u32[]{:S(2)}) collective-permute-start(f32[2,32,256]{2,1,0:T(8,128)} %get-tuple-element.28), channel_id=1, source_target_pairs={{0,1},{1,0},{2,3},{3,2},{4,5},{5,4},{6,7},{7,6},{8,9},{9,8},{10,11... | collective-permute-start | bytes 196616 | tf_op jit(solution)/shard_map/ppermute | solution.py:592
  10.4 18.0 %all-to-all-start = ((f32[32,8,128]{2,1,0:T(8,128)}), f32[32,8,128]{2,1,0:T(8,128)S(1)}, u32[]{:S(2)}, u32[]{:S(2)}) async-start(f32[32,8,128]{2,1,0:T(8,128)} %bitcast.27), calls=%async_computation | async-start | bytes 262144 | tf_op jit(solution)/shard_map/all_to_all | solution.py:609
  25.4 5.6 %copy-start = (f32[26,32,256]{2,1,0:T(8,128)}, f32[26,32,256]{2,1,0:T(8,128)S(1)}, u32[]{:S(2)}) copy-start(f32[26,32,256]{2,1,0:T(8,128)S(1)} %collective-permute-done.1.low) | copy-start | bytes 2555908
  27.9 13.0 %collective-permute-start.3 = (f32[32,16,256]{2,1,0:T(8,128)}, f32[32,16,256]{2,1,0:T(8,128)S(1)}, u32[]{:S(2)}, u32[]{:S(2)}) collective-permute-start(f32[32,16,256]{2,1,0:T(8,128)} %get-tuple-element.36), channel_id=1, source_target_pairs={{0,2},{2,4},{4,6},{6,8},{8,10},{10,12},{12,14},{14,16},{16,18},{18... | collective-permute-start | bytes 1572872 | tf_op jit(solution)/shard_map/ppermute | solution.py:578
  27.9 13.0 %collective-permute-start.4 = (f32[32,16,256]{2,1,0:T(8,128)}, f32[32,16,256]{2,1,0:T(8,128)S(1)}, u32[]{:S(2)}, u32[]{:S(2)}) collective-permute-start(f32[32,16,256]{2,1,0:T(8,128)} %get-tuple-element.37), channel_id=1, source_target_pairs={{0,30},{2,0},{4,2},{6,4},{8,6},{10,8},{12,10},{14,12},{16,14},{18,... | collective-permute-start | bytes 1572872 | tf_op jit(solution)/shard_map/ppermute | solution.py:579
  31.0 14.7 %all-to-all-start.1 = ((f32[32,8,128]{2,1,0:T(8,128)}), f32[32,8,128]{2,1,0:T(8,128)S(1)}, u32[]{:S(2)}, u32[]{:S(2)}) async-start(f32[32,8,128]{2,1,0:T(8,128)} %bitcast.29), calls=%async_computation.1 | async-start | bytes 262144 | tf_op jit(solution)/shard_map/all_to_all | solution.py:614
  36.6 21.5 %collective-permute-start.5 = (f32[32,24,256]{2,1,0:T(8,128)}, f32[32,24,256]{2,1,0:T(8,128)S(1)}, u32[]{:S(2)}, u32[]{:S(2)}) collective-permute-start(f32[32,24,256]{2,1,0:T(8,128)} %get-tuple-element.44), channel_id=1, source_target_pairs={{0,2},{2,4},{4,6},{6,8},{8,10},{10,12},{12,14},{14,16},{16,18},{18... | collective-permute-start | bytes 2359304 | tf_op jit(solution)/shard_map/ppermute | solution.py:578
  38.3 20.7 %collective-permute-start.6 = (f32[32,24,256]{2,1,0:T(8,128)}, f32[32,24,256]{2,1,0:T(8,128)S(1)}, u32[]{:S(2)}, u32[]{:S(2)}) collective-permute-start(f32[32,24,256]{2,1,0:T(8,128)} %get-tuple-element.46), channel_id=1, source_target_pairs={{0,30},{2,0},{4,2},{6,4},{8,6},{10,8},{12,10},{14,12},{16,14},{18,... | collective-permute-start | bytes 2359304 | tf_op jit(solution)/shard_map/ppermute | solution.py:579

commit v20 on v19

--- a/solution.py
+++ b/solution.py
@@ -57,14 +57,13 @@
     return out if inverse else out.transpose(0, 2, 1)
 
 
-def z_tables(gz, gy, rows, scale):
+def z_tables(gz, rows, scale):
     c, s = trig(kept(MZ, gz), np.arange(gz), gz)
     eye = np.eye(rows)
-    one = np.ones(gy)
     both = np.stack([c, s])
-    fwd = np.einsum("tqz,g,jk->tqjzgk", both, one, eye) * scale
-    inv = np.einsum("tqz,g,jk->tzgjqk", both, one, eye)
-    return fwd.reshape(2 * MZ * rows, gz * gy * rows), inv.reshape(2 * gz * gy * rows, MZ * rows)
+    fwd = np.einsum("tqz,jk->tqjzk", both, eye) * scale
+    inv = np.einsum("tqz,jk->tzjqk", both, eye)
+    return fwd.reshape(2 * MZ * rows, gz * rows), inv.reshape(2 * gz * rows, MZ * rows)
 
 
 def parts(value):
@@ -89,7 +88,8 @@
     return jnp.where(is_real, pltpu.roll(value, width - MX, 1), pltpu.roll(value, MX, 1)), is_real
 
 
-def forward_kernel(field, x_top, x_rest, y_top, y_rest, out, taken, x_both, y_both, sem):
+def forward_kernel(halved, field, x_top, x_rest, y_top, y_rest, *refs):
+    outs, (taken, x_both, y_both, sem) = refs[:-4], refs[-4:]
     gy = lax.axis_index("gy")
     few = [
         pltpu.make_async_copy(src, dst, sem.at[4 + i])
@@ -116,8 +116,15 @@
         both = dot3((y_both[0], y_both[1]), parts(total[g * rows : (g + 1) * rows]))
         crossed, is_real = swap_parts(both[MY:])
         modes = both[:MY] + jnp.where(is_real, crossed, -crossed)
-        out[pl.ds(2 * g * MY, MY), :] = modes[:, : 4 * MX]
-        out[pl.ds((2 * g + 1) * MY, MY), :] = modes[:, 4 * MX :]
+        for h in range(2):
+            pair, pairs_modes = 2 * g + h, modes[:, 4 * MX * h : 4 * MX * (h + 1)]
+            if halved:
+                half = MY // 2
+                upper, lower = pairs_modes[:half], pairs_modes[half:]
+                outs[0][pl.ds(pair * half, half), :] = jnp.where(gy == 0, upper, lower)
+                outs[1][pl.ds(pair * half, half), :] = jnp.where(gy == 0, lower, upper)
+            else:
+                outs[0][pl.ds(pair * MY, MY), :] = pairs_modes
 
 
 def filter_kernel(arrived, gains, f_top, f_rest, i_top, i_rest, out):
@@ -319,7 +326,7 @@
     return value * jnp.where(value < 0.0, tail, 1.0 - tail)
 
 
-def inverse_kernel(upper, modes, bias, x_top, x_rest, y_top, y_rest, own, middle, second, low, high, out, base, columns):
+def inverse_kernel(upper, halved, first_modes, second_modes, bias, x_top, x_rest, y_top, y_rest, own, middle, second, low, high, out, base, columns):
     q = pl.program_id(0)
     groups, _, y_local, _ = out.shape
 
@@ -327,7 +334,14 @@
     def _():
         gy = lax.axis_index("gy")
         for g in range(groups):
-            own_modes = jnp.concatenate([modes[2 * g], modes[2 * g + 1]], axis=1)
+            pairs = []
+            for pair in (2 * g, 2 * g + 1):
+                some = pl.ds(pair * (MY // 2), MY // 2)
+                one, two = first_modes[some, :], second_modes[some, :]
+                if halved:
+                    one, two = jnp.where(gy == 0, one, two), jnp.where(gy == 0, two, one)
+                pairs.append(jnp.concatenate([one, two], axis=0))
+            own_modes = jnp.concatenate(pairs, axis=1)
             crossed, is_real = swap_parts(own_modes)
             stack = jnp.concatenate([own_modes, jnp.where(is_real, -crossed, crossed)], axis=0)
             pair = parts(dot3((y_top[gy], y_rest[gy]), parts(stack)))
@@ -381,13 +395,14 @@
     return array.reshape(CH // 4, 4, *array.shape[1:])
 
 
-def forward_call(field, gy, pinned):
+def forward_call(field, gy, halved):
     y_local = field.shape[1]
     tables = [*halves(x_table(False)), *halves(y_table(y_local, gy, False))]
+    parts_out = 2 if halved else 1
     hbm = pl.BlockSpec(memory_space=pltpu.HBM)
     return pl.pallas_call(
-        forward_kernel,
-        out_shape=(pltpu.HBM if pinned else jax.ShapeDtypeStruct)((CH // 2 * MY, 4 * MX), F32),
+        functools.partial(forward_kernel, halved),
+        out_shape=[jax.ShapeDtypeStruct((CH // 2 * MY // parts_out, 4 * MX), F32)] * parts_out,
         in_specs=[hbm] * 5,
         scratch_shapes=[
             pltpu.VMEM((4, CH // 4, y_local, NX), F32),
@@ -401,8 +416,8 @@
     )(*in_hbm(by_four(field), *tables))
 
 
-def filter_call(arrived, gains, gz, gy, scale):
-    fwd, inv = z_tables(gz, gy, gains.shape[2], scale)
+def filter_call(arrived, gains, gz, scale):
+    fwd, inv = z_tables(gz, gains.shape[2], scale)
     fwd, inv = halves(fwd), halves(inv)
     return pl.pallas_call(
         filter_kernel,
@@ -413,20 +428,20 @@
     )(arrived, *in_hbm(gains, *fwd, *inv))
 
 
-def inverse_call(modes, bias, own, middle, second, pair, upper, y_local, gy, scale):
+def inverse_call(modes, halved, bias, own, middle, second, pair, upper, y_local, gy, scale):
     tables = [*halves(x_table(True, scale)), *halves(y_table(y_local, gy, True))]
     some = lambda rows: pl.BlockSpec((CH // 4, 1, rows, NX), lambda i: (0, i, 0, 0))
     planes = [*in_hbm(*map(by_four, (own, middle, second))), *map(by_four, pair)]
     rim = own.shape[1]
     result, base = pl.pallas_call(
-        functools.partial(inverse_kernel, upper),
+        functools.partial(inverse_kernel, upper, halved),
         out_shape=[
             jax.ShapeDtypeStruct((CH // 4, 4, y_local, NX), F32),
             jax.ShapeDtypeStruct((CH // 4, 4, rim, NX), F32),
         ],
         grid=(4,),
         in_specs=[
-            whole_block(modes),
+            *[whole_block(m) for m in modes],
             pl.BlockSpec(memory_space=pltpu.SMEM),
             *[whole_block(t) for t in tables],
             *[some(p.shape[2]) for p in planes],
@@ -436,7 +451,7 @@
         compiler_params=params(),
         cost_estimate=cost(10**8, 2**18),
         name="inverse_modes",
-    )(modes, *in_hbm(bias, *tables), *planes)
+    )(*modes, *in_hbm(bias, *tables), *planes)
     return result.reshape(CH, y_local, NX), base.reshape(CH, rim, NX)
 
 
@@ -599,28 +614,32 @@
         )
     j_own, n_own = spectral_filter.shape[2], spectral_filter.shape[3]
     whole_tiles = j_own == 8 and n_own == 2 * MX
-    coarse = after(forward_call(after(field, packed), gy, whole_tiles), halo)
+    coarse, *others = forward_call(after(field, packed), gy, whole_tiles)
+    if whole_tiles:
+        coarse = coarse + lax.ppermute(others[0], "gy", ring("gy", gy, 1))
+    coarse = after(coarse, halo)
     segments, groups = ((0,), tuple(range(cut, last + 1))), (second_tiles, third_tiles)
     down, second, up, outer_down, own, outer_up = own_call(
         after(field, coarse), halo, depth_weight, point_weight, segments, groups
     )
     if whole_tiles:
-        both = ("gz", "gy")
-        got = lax.all_to_all(coarse, both, split_axis=0, concat_axis=0, tiled=True)
+        got = lax.all_to_all(coarse, "gz", split_axis=0, concat_axis=0, tiled=True)
         down, up = lax.optimization_barrier((down, up, first_low))[:2]
         pair = to_neighbours(down, up)
         gains = after(spectral_filter, first_low, first_high, second)
-        mark = filter_call(got, gains, gz, gy, forward_scale)
-        back = lax.all_to_all(mark, both, split_axis=0, concat_axis=0, tiled=True)
-        back = back.reshape(CH // 2, MY, 4 * MX)
+        mark = filter_call(got, gains, gz, forward_scale)
+        back = lax.all_to_all(mark, "gz", split_axis=0, concat_axis=0, tiled=True)
     else:
         pair = to_neighbours(down, up)
-        mark = back = general_filter(coarse, spectral_filter, gz, gy, forward_scale)
+        mark = general_filter(coarse, spectral_filter, gz, gy, forward_scale)
+        modes = [mark[:, part].reshape(-1, 4 * MX) for part in (slice(0, MY // 2), slice(MY // 2, MY))]
     outer_pair = to_neighbours(after(outer_down, mark), after(outer_up, mark))
     packed, *pair = lax.optimization_barrier((packed, *pair))
     mixed = middle_call(depth_weight, point_weight, first_low, packed, first_high)
+    if whole_tiles:
+        modes = (back, lax.ppermute(after(back, mixed), "gy", ring("gy", gy, 1)))
     result, base = inverse_call(
-        back, bias_vector, own, mixed, second, pair, 8, y_local, gy, inverse_scale
+        modes, whole_tiles, bias_vector, own, mixed, second, pair, 8, y_local, gy, inverse_scale
     )
     result = finish_call(result, base, *outer_pair, 1)
     return result.reshape(CH, 1, y_local, NX)

time: 60.9 us -> 69.9 us (1.15)
  waiting for transfers between devices: 14.7 us -> 18.7 us
  starting transfers between devices: 17.5 us -> 21.2 us
  other arithmetic: 0 us -> 1.48 us
    ppermute x3, waiting for transfers between devices: 11.4 us -> 2.31 us  [to_neighbours(): lax.ppermute(down, 'gz', ring('gz', gz, 1))]
    ppermute x3, waiting for transfers between devices: 3.33 us -> 11.2 us  [to_neighbours(): lax.ppermute(up, 'gz', ring('gz', gz, -1))]
    ppermute x0 -> x2, waiting for transfers between devices: none -> 5.25 us  [the longest x1 3.1 us: body(): modes = (back, lax.ppermute(after(back, mixed), 'gy', ring('gy', gy, 1)))]
    all_to_all x2, starting transfers between devices: 11.4 us -> 13.6 us  [the longest x1 7.32 us: body(): got = lax.all_to_all(coarse, 'gz', split_axis=0, concat_axis=0, tiled=True)]
    ppermute x3, starting transfers between devices: 4.37 us -> 6 us  [to_neighbours(): lax.ppermute(down, 'gz', ring('gz', gz, 1))]
    add x0 -> x1, other arithmetic: none -> 1.48 us  [body(): coarse = coarse + lax.ppermute(others[0], 'gy', ring('gy', gy, 1))]
    ppermute x0 -> x2, starting transfers between devices: none -> 1.35 us  [the longest x1 1.28 us: body(): coarse = coarse + lax.ppermute(others[0], 'gy', ring('gy', gy, 1))]
    ppermute x1, starting transfers between devices: 1.21 us -> 0.25 us  [body(): halo = lax.ppermute(edges, 'gy', ring('gy', gy, 1))]
  transfers between devices with their start and end apart: 9 -> 11, of which waited for: 5 -> 4; matrix products, arithmetic and copies ran while one was open for 0% -> 2% of each run, Pallas kernels for 40% -> 35%
where the time goes in v20:
time: 69.9 us; the launch traced here: 69.4 us
  Pallas kernels  27.9 us (40%)
  starting transfers between devices  21.2 us (30%)
  waiting for transfers between devices  18.7 us (27%)
  other arithmetic  1.48 us (2%)
    ppermute x3, waiting for transfers between devices, to_neighbours(): lax.ppermute(up, 'gz', ring('gz', gz, -1))  11.2 us
    all_to_all x1, starting transfers between devices, body(): got = lax.all_to_all(coarse, 'gz', split_axis=0, concat_axis=0, tiled=True)  7.32 us
    pallas_call x1, Pallas kernels, own_call(): pl.pallas_call(functools.partial(own_kernel, segments, groups), out_shape...  7.14 us
    all_to_all x1, starting transfers between devices, body(): back = lax.all_to_all(mark, 'gz', split_axis=0, concat_axis=0, tiled=True)  6.24 us
    ppermute x3, starting transfers between devices, to_neighbours(): lax.ppermute(down, 'gz', ring('gz', gz, 1))  6 us
    pallas_call x1, Pallas kernels, inverse_call(): pl.pallas_call(functools.partial(inverse_kernel, upper, halved), out_shap...  5.65 us
    pallas_call x1, Pallas kernels, middle_call(): pl.pallas_call(middle_kernel, out_shape=pltpu.HBM((CH, rows, NX), F32), i...  4.88 us
    pallas_call x1, Pallas kernels, forward_call(): pl.pallas_call(functools.partial(forward_kernel, halved), out_shape=[jax....  4.14 us
  transfers between devices with their start and end apart: 11, of which 4 were waited for; matrix products, arithmetic and copies ran while one was open for 2% of the time, Pallas kernels for 35%

profile of v20, /device:TPU:1, one launch (start us, length us, event | category | flops | bytes accessed | tf_op | source)
XLA Modules:
  0.0 69.4 jit_solution(8495856501990643274)
XLA Ops:
  0.0 2.3 %packed_rows.1 = (f32[26,32,256]{2,1,0:T(8,128)}, f32[2,32,256]{2,1,0:T(8,128)}) custom-call(f32[32,64,256]{2,1,0:T(8,128)} %bitcast.22), custom_call_target="tpu_custom_call" | custom-call | flops 100000000 | bytes 262144 | tf_op jit(solution)/shard_map/packed_rows/pallas_call | solution.py:482
  2.3 0.0 copy-start.1
  2.3 2.7 %collective-permute-start.2 = (f32[26,32,256]{2,1,0:T(8,128)}, f32[26,32,256]{2,1,0:T(8,128)S(1)}, u32[]{:S(2)}, u32[]{:S(2)}) collective-permute-start(f32[26,32,256]{2,1,0:T(8,128)} %get-tuple-element.42.own), channel_id=1, source_target_pairs={{0,2},{2,4},{4,6},{6,8},{8,10},{10,12},{12,14},{14,16},{16,18},{18... | collective-permute-start | bytes 2555912 | tf_op jit(solution)/shard_map/ppermute | solution.py:593
  5.0 0.0 collective-permute-start.3
  5.0 4.1 %forward_modes.1 = (f32[128,128]{1,0:T(8,128)}, f32[128,128]{1,0:T(8,128)}) custom-call(f32[8,4,64,256]{3,2,1,0:T(8,128)} %bitcast.23, bf16[2,256,128]{2,1,0:T(8,128)(2,1)} %constant.24.clone.x_top, bf16[2,256,128]{2,1,0:T(8,128)(2,1)} %constant.25.clone.x_rest, bf16[2,32,64]{2,1,0:T(8,128)(2,1)} %constant.26.clone.y_top, ...), custom_call_target="tpu_custom_call" | custom-call | flops 100000000 | bytes 262144 | tf_op jit(solution)/shard_map/forward_modes/pallas_call | solution.py:403
  9.2 1.3 %collective-permute-start = (f32[128,128]{1,0:T(8,128)}, f32[128,128]{1,0:T(8,128)S(1)}, u32[]{:S(2)}, u32[]{:S(2)}) collective-permute-start(f32[128,128]{1,0:T(8,128)} %get-tuple-element.32), channel_id=1, source_target_pairs={{0,1},{1,0},{2,3},{3,2},{4,5},{5,4},{6,7},{7,6},{8,9},{9,8},{10,11... | collective-permute-start | bytes 196616 | tf_op jit(solution)/shard_map/ppermute | solution.py:619
  10.4 0.0 copy-done.1
  10.4 0.3 collective-permute-start.1
  10.7 2.2 %collective-permute-done = f32[128,128]{1,0:T(8,128)S(1)} collective-permute-done((f32[128,128]{1,0:T(8,128)}, f32[128,128]{1,0:T(8,128)S(1)}, u32[]{:S(2)}, u32[]{:S(2)}) %collective-permute-start) | collective-permute-done | bytes 65568 | tf_op jit(solution)/shard_map/ppermute | solution.py:619
  12.8 1.5 %add.3 = f32[128,128]{1,0:T(8,128)} add(f32[128,128]{1,0:T(8,128)} %get-tuple-element.31, f32[128,128]{1,0:T(8,128)S(1)} %collective-permute-done) | non-fusion elementwise | flops 16384 | bytes 196608 | tf_op jit(solution)/shard_map/add | solution.py:619
  14.3 0.0 collective-permute-done.1.halo
  14.3 7.3 %all-to-all-start = ((f32[16,8,128]{2,1,0:T(8,128)}), f32[16,8,128]{2,1,0:T(8,128)S(1)}, u32[]{:S(2)}, u32[]{:S(2)}) async-start(f32[16,8,128]{2,1,0:T(8,128)} %bitcast.2), calls=%async_computation | async-start | bytes 131072 | tf_op jit(solution)/shard_map/all_to_all | solution.py:626
  21.7 7.1 %own_sums.1 = (f32[32,16,256]{2,1,0:T(8,128)}, f32[32,16,256]{2,1,0:T(8,128)}, f32[32,16,256]{2,1,0:T(8,128)}, f32[32,24,256]{2,1,0:T(8,128)}, f32[32,24,256]{2,1,0:T(8,128)}, /*index=5*/f32[32,24,256]{2,1,0:T(8,128)}) custom-call(f32[32,27]{1,0:T(8,128)} %weight.3, f32[32,32]{1,0:T(8,128)} %point.3, f32[32,64,256]{2,1,0:T(8,128)} %bitcast.24, ...), custom_call_target="tpu_custom_call" | custom-call | flops 100000000 | bytes 262144 | tf_op jit(solution)/shard_map/own_sums/pallas_call | solution.py:505
  28.8 0.0 collective-permute-done.2.low
  28.8 0.0 collective-permute-done.3.high
  28.8 1.7 %collective-permute-start.4 = (f32[32,16,256]{2,1,0:T(8,128)}, f32[32,16,256]{2,1,0:T(8,128)S(1)}, u32[]{:S(2)}, u32[]{:S(2)}) collective-permute-start(f32[32,16,256]{2,1,0:T(8,128)} %get-tuple-element.40), channel_id=1, source_target_pairs={{0,2},{2,4},{4,6},{6,8},{8,10},{10,12},{12,14},{14,16},{16,18},{18... | collective-permute-start | bytes 1572872 | tf_op jit(solution)/shard_map/ppermute | solution.py:593
  30.5 0.0 collective-permute-start.5
  30.5 0.0 all-to-all-done
  30.5 2.3 %filter_modes.1 = f32[128,128]{1,0:T(8,128)} custom-call(f32[128,128]{1,0:T(8,128)S(1)} %bitcast.21, f32[2,16,8,64]{3,2,1,0:T(8,128)} %gains, bf16[256,128]{1,0:T(8,128)(2,1)} %constant.28.clone.f_top, bf16[256,128]{1,0:T(8,128)(2,1)} %constant.29.clone.f_rest, bf16[256,128]{1,0:T(8,128)(2,1)} %constant.30.clone.i_top, bf16[256,128]{1,0:T(8,128)(2,1)} %constant.31.clone.i_rest), custom_call_target="tpu_custom_call" | custom-call | flops 40000000000 | bytes 262144 | tf_op jit(solution)/shard_map/filter_modes/pallas_call | solution.py:422
  32.9 6.2 %all-to-all-start.1 = ((f32[16,8,128]{2,1,0:T(8,128)}), f32[16,8,128]{2,1,0:T(8,128)S(1)}, u32[]{:S(2)}, u32[]{:S(2)}) async-start(f32[16,8,128]{2,1,0:T(8,128)} %bitcast.29), calls=%async_computation.1 | async-start | bytes 131072 | tf_op jit(solution)/shard_map/all_to_all | solution.py:631
  39.1 1.6 %collective-permute-start.7 = (f32[32,24,256]{2,1,0:T(8,128)}, f32[32,24,256]{2,1,0:T(8,128)S(1)}, u32[]{:S(2)}, u32[]{:S(2)}) collective-permute-start(f32[32,24,256]{2,1,0:T(8,128)} %get-tuple-element.50), channel_id=1, source_target_pairs={{0,2},{2,4},{4,6},{6,8},{8,10},{10,12},{12,14},{14,16},{16,18},{18... | collective-permute-start | bytes 2359304 | tf_op jit(solution)/shard_map/ppermute | solution.py:593
  40.7 0.0 collective-permute-start.8
  40.7 2.3 %collective-permute-done.4 = f32[32,16,256]{2,1,0:T(8,128)S(1)} collective-permute-done((f32[32,16,256]{2,1,0:T(8,128)}, f32[32,16,256]{2,1,0:T(8,128)S(1)}, u32[]{:S(2)}, u32[]{:S(2)}) %collective-permute-start.4) | collective-permute-done | bytes 524320 | tf_op jit(solution)/shard_map/ppermute | solution.py:593
  43.0 11.1 %collective-permute-done.5 = f32[32,16,256]{2,1,0:T(8,128)S(1)} collective-permute-done((f32[32,16,256]{2,1,0:T(8,128)}, f32[32,16,256]{2,1,0:T(8,128)S(1)}, u32[]{:S(2)}, u32[]{:S(2)}) %collective-permute-start.5) | collective-permute-done | bytes 524320 | tf_op jit(solution)/shard_map/ppermute | solution.py:594
  54.2 4.9 %middle_sums.1 = f32[32,24,256]{2,1,0:T(8,128)} custom-call(f32[32,27]{1,0:T(8,128)} %weight.3, f32[32,32]{1,0:T(8,128)} %point.3, f32[26,32,256]{2,1,0:T(8,128)} %copy-done, f32[26,32,256]{2,1,0:T(8,128)} %get-tuple-element.42.own, f32[26,32,256]{2,1,0:T(8,128)} %collective-permute-done.3.high), custom_call_target="tpu_custom_call" | custom-call | flops 40000000000 | bytes 262144 | tf_op jit(solution)/shard_map/middle_sums/pallas_call | solution.py:532
  59.1 0.0 all-to-all-done.1
  59.1 0.1 collective-permute-start.6
  59.2 3.1 %collective-permute-done.6.second_modes = f32[128,128]{1,0:T(8,128)S(1)} collective-permute-done((f32[128,128]{1,0:T(8,128)S(1)}, f32[128,128]{1,0:T(8,128)S(1)}, u32[]{:S(2)}, u32[]{:S(2)}) %collective-permute-start.6) | collective-permute-done | bytes 65568 | tf_op jit(solution)/shard_map/ppermute | solution.py:640
  62.3 5.7 %inverse_modes.1 = (f32[8,4,64,256]{3,2,1,0:T(8,128)}, f32[8,4,24,256]{3,2,1,0:T(8,128)S(1)}) custom-call(f32[128,128]{1,0:T(8,128)S(1)} %bitcast.20, f32[128,128]{1,0:T(8,128)S(1)} %collective-permute-done.6.second_modes, f32[32]{0:T(128)} %bias.1, bf16[2,128,256]{2,1,0:T(8,128)(2,1)} %constant.32.clone.x_top, bf16[2,128,256]{2,1,0:T(8,128)(2,1)} %constant.33.clone.x_rest, ...), custom_call_target="tpu_custom_call" | custom-call | flops 100000000 | bytes 262144 | tf_op jit(solution)/shard_map/inverse_modes/pallas_call | solution.py:436
  67.9 0.0 collective-permute-done.7.low
  67.9 0.0 collective-permute-done.8.high
  67.9 1.5 %finished_rows.1 = f32[32,64,256]{2,1,0:T(8,128)} custom-call(f32[32,64,256]{2,1,0:T(8,128)} %bitcast.25, f32[32,24,256]{2,1,0:T(8,128)S(1)} %bitcast.16, f32[32,24,256]{2,1,0:T(8,128)S(1)} %collective-permute-done.7.low, f32[32,24,256]{2,1,0:T(8,128)S(1)} %collective-permute-done.8.high), custom_call_target="tpu_custom_call", output_to_operand_aliasing={{}: (0, {})} | custom-call | flops 100000000 | bytes 262144 | tf_op jit(solution)/shard_map/finished_rows/pallas_call | solution.py:462
  (2 shorter events, 0.0 us)
Async XLA Ops:
  2.3 8.1 %copy-start.1 = (f32[2,32,256]{2,1,0:T(8,128)S(1)}, f32[2,32,256]{2,1,0:T(8,128)}, u32[]{:S(2)}) copy-start(f32[2,32,256]{2,1,0:T(8,128)} %get-tuple-element.33) | copy-start | bytes 196612
  2.3 26.5 %collective-permute-start.2 = (f32[26,32,256]{2,1,0:T(8,128)}, f32[26,32,256]{2,1,0:T(8,128)S(1)}, u32[]{:S(2)}, u32[]{:S(2)}) collective-permute-start(f32[26,32,256]{2,1,0:T(8,128)} %get-tuple-element.42.own), channel_id=1, source_target_pairs={{0,2},{2,4},{4,6},{6,8},{8,10},{10,12},{12,14},{14,16},{16,18},{18... | collective-permute-start | bytes 2555912 | tf_op jit(solution)/shard_map/ppermute | solution.py:593
  5.0 23.8 %collective-permute-start.3 = (f32[26,32,256]{2,1,0:T(8,128)}, f32[26,32,256]{2,1,0:T(8,128)}, u32[]{:S(2)}, u32[]{:S(2)}) collective-permute-start(f32[26,32,256]{2,1,0:T(8,128)} %get-tuple-element.42.own), channel_id=1, source_target_pairs={{0,30},{2,0},{4,2},{6,4},{8,6},{10,8},{12,10},{14,12},{16,14},{18,... | collective-permute-start | bytes 2555912 | tf_op jit(solution)/shard_map/ppermute | solution.py:594
  9.2 3.7 %collective-permute-start = (f32[128,128]{1,0:T(8,128)}, f32[128,128]{1,0:T(8,128)S(1)}, u32[]{:S(2)}, u32[]{:S(2)}) collective-permute-start(f32[128,128]{1,0:T(8,128)} %get-tuple-element.32), channel_id=1, source_target_pairs={{0,1},{1,0},{2,3},{3,2},{4,5},{5,4},{6,7},{7,6},{8,9},{9,8},{10,11... | collective-permute-start | bytes 196616 | tf_op jit(solution)/shard_map/ppermute | solution.py:619
  10.4 3.9 %collective-permute-start.1 = (f32[2,32,256]{2,1,0:T(8,128)S(1)}, f32[2,32,256]{2,1,0:T(8,128)S(1)}, u32[]{:S(2)}, u32[]{:S(2)}) collective-permute-start(f32[2,32,256]{2,1,0:T(8,128)S(1)} %copy-done.1), channel_id=1, source_target_pairs={{0,1},{1,0},{2,3},{3,2},{4,5},{5,4},{6,7},{7,6},{8,9},{9,8},{10,11... | collective-permute-start | bytes 196616 | tf_op jit(solution)/shard_map/ppermute | solution.py:607
  14.3 16.2 %all-to-all-start = ((f32[16,8,128]{2,1,0:T(8,128)}), f32[16,8,128]{2,1,0:T(8,128)S(1)}, u32[]{:S(2)}, u32[]{:S(2)}) async-start(f32[16,8,128]{2,1,0:T(8,128)} %bitcast.2), calls=%async_computation | async-start | bytes 131072 | tf_op jit(solution)/shard_map/all_to_all | solution.py:626
  28.8 4.0 %copy-start = (f32[26,32,256]{2,1,0:T(8,128)}, f32[26,32,256]{2,1,0:T(8,128)S(1)}, u32[]{:S(2)}) copy-start(f32[26,32,256]{2,1,0:T(8,128)S(1)} %collective-permute-done.2.low) | copy-start | bytes 2555908
  28.8 14.2 %collective-permute-start.4 = (f32[32,16,256]{2,1,0:T(8,128)}, f32[32,16,256]{2,1,0:T(8,128)S(1)}, u32[]{:S(2)}, u32[]{:S(2)}) collective-permute-start(f32[32,16,256]{2,1,0:T(8,128)} %get-tuple-element.40), channel_id=1, source_target_pairs={{0,2},{2,4},{4,6},{6,8},{8,10},{10,12},{12,14},{14,16},{16,18},{18... | collective-permute-start | bytes 1572872 | tf_op jit(solution)/shard_map/ppermute | solution.py:593
  30.5 23.7 %collective-permute-start.5 = (f32[32,16,256]{2,1,0:T(8,128)}, f32[32,16,256]{2,1,0:T(8,128)S(1)}, u32[]{:S(2)}, u32[]{:S(2)}) collective-permute-start(f32[32,16,256]{2,1,0:T(8,128)} %get-tuple-element.41), channel_id=1, source_target_pairs={{0,30},{2,0},{4,2},{6,4},{8,6},{10,8},{12,10},{14,12},{16,14},{18,... | collective-permute-start | bytes 1572872 | tf_op jit(solution)/shard_map/ppermute | solution.py:594
  32.9 26.2 %all-to-all-start.1 = ((f32[16,8,128]{2,1,0:T(8,128)}), f32[16,8,128]{2,1,0:T(8,128)S(1)}, u32[]{:S(2)}, u32[]{:S(2)}) async-start(f32[16,8,128]{2,1,0:T(8,128)} %bitcast.29), calls=%async_computation.1 | async-start | bytes 131072 | tf_op jit(solution)/shard_map/all_to_all | solution.py:631
  39.1 28.8 %collective-permute-start.7 = (f32[32,24,256]{2,1,0:T(8,128)}, f32[32,24,256]{2,1,0:T(8,128)S(1)}, u32[]{:S(2)}, u32[]{:S(2)}) collective-permute-start(f32[32,24,256]{2,1,0:T(8,128)} %get-tuple-element.50), channel_id=1, source_target_pairs={{0,2},{2,4},{4,6},{6,8},{8,10},{10,12},{12,14},{14,16},{16,18},{18... | collective-permute-start | bytes 2359304 | tf_op jit(solution)/shard_map/ppermute | solution.py:593
  40.7 27.2 %collective-permute-start.8 = (f32[32,24,256]{2,1,0:T(8,128)}, f32[32,24,256]{2,1,0:T(8,128)S(1)}, u32[]{:S(2)}, u32[]{:S(2)}) collective-permute-start(f32[32,24,256]{2,1,0:T(8,128)} %get-tuple-element.52), channel_id=1, source_target_pairs={{0,30},{2,0},{4,2},{6,4},{8,6},{10,8},{12,10},{14,12},{16,14},{18,... | collective-permute-start | bytes 2359304 | tf_op jit(solution)/shard_map/ppermute | solution.py:594
  59.1 3.2 %collective-permute-start.6 = (f32[128,128]{1,0:T(8,128)S(1)}, f32[128,128]{1,0:T(8,128)S(1)}, u32[]{:S(2)}, u32[]{:S(2)}) collective-permute-start(f32[128,128]{1,0:T(8,128)S(1)} %bitcast.19), channel_id=1, source_target_pairs={{0,1},{1,0},{2,3},{3,2},{4,5},{5,4},{6,7},{7,6},{8,9},{9,8},{10,11... | collective-permute-start | bytes 196616 | tf_op jit(solution)/shard_map/ppermute | solution.py:640

commit v21 on v19

--- a/solution.py
+++ b/solution.py
@@ -219,25 +219,15 @@
     return dot3(mix, parts(tile)).reshape(CH, 8, NX)
 
 
-def pack_kernel(tiles, field, packed, edges, taken, rows, ends, sem_in, sem_out):
+def pack_kernel(tiles, field, packed, edges, taken, sem_in):
     last = field.shape[1] // 8 - 1
     before, after = tiles[0] - 1, tiles[-1] + 1
     wanted = [before, *tiles, after] + [t for t in (0, last) if t not in (before, after)]
     row = fetch_tiles(field, taken, sem_in, wanted)
-    places = [(before, 7), *[(t, r) for t in tiles for r in range(8)], (after, 0)]
-    copies, cuts = [], (0, len(places) // 2, len(places))
-    for k in range(2):
-        for i in range(cuts[k], cuts[k + 1]):
-            rows[i] = row(*places[i])
-        some = pl.ds(cuts[k], cuts[k + 1] - cuts[k])
-        copies.append(pltpu.make_async_copy(rows.at[some], packed.at[some], sem_out.at[k]))
-        copies[-1].start()
-    ends[0] = row(last, 7)
-    ends[1] = row(0, 0)
-    copies.append(pltpu.make_async_copy(ends, edges, sem_out.at[2]))
-    copies[-1].start()
-    for copy in copies:
-        copy.wait()
+    for i, place in enumerate([(before, 7), *[(t, r) for t in tiles for r in range(8)], (after, 0)]):
+        packed[i] = row(*place)
+    edges[0] = row(last, 7)
+    edges[1] = row(0, 0)
 
 
 def own_kernel(segments, groups, weight, point, field, halo, *refs):
@@ -463,18 +453,15 @@
 def pack_call(field, tiles):
     count = 8 * len(tiles) + 2
     fetched = len(tiles) + 4
-    hbm = pl.BlockSpec(memory_space=pltpu.HBM)
+    vmem = pl.BlockSpec(memory_space=pltpu.VMEM)
     return pl.pallas_call(
         functools.partial(pack_kernel, tiles),
-        out_shape=[pltpu.HBM((count, CH, NX), F32), pltpu.HBM((2, CH, NX), F32)],
-        in_specs=[hbm],
-        out_specs=[hbm] * 2,
+        out_shape=[jax.ShapeDtypeStruct((count, CH, NX), F32), jax.ShapeDtypeStruct((2, CH, NX), F32)],
+        in_specs=[pl.BlockSpec(memory_space=pltpu.HBM)],
+        out_specs=[vmem] * 2,
         scratch_shapes=[
             pltpu.VMEM((fetched, 2, CH, 8, 128), F32),
-            pltpu.VMEM((count, CH, NX), F32),
-            pltpu.VMEM((2, CH, NX), F32),
             pltpu.SemaphoreType.DMA((fetched, 2)),
-            pltpu.SemaphoreType.DMA((3,)),
         ],
         compiler_params=params(),
         cost_estimate=cost(10**8, 2**18),
@@ -517,7 +504,7 @@
     return pl.pallas_call(
         middle_kernel,
         out_shape=pltpu.HBM((CH, rows, NX), F32),
-        in_specs=[hbm] * 5,
+        in_specs=[hbm] * 3 + [pl.BlockSpec(memory_space=pl.ANY), hbm],
         out_specs=hbm,
         scratch_shapes=[
             pltpu.VMEM((3, rows + 2, CH, NX), F32),
@@ -532,7 +519,7 @@
         compiler_params=params(),
         cost_estimate=cost(4 * 10**10, 2**18),
         name="middle_sums",
-    )(*in_hbm(weight, point, low, own, high))
+    )(*in_hbm(weight, point, low), own, *in_hbm(high))
 
 
 def general_filter(coarse, gains, gz, gy, scale):

time: 60.9 us -> 60.1 us (0.987)
  waiting for transfers between devices: 14.7 us -> 13.4 us
  local copies, waits for them, and re-layouts: 0.01 us -> 1.17 us
  Pallas kernels: 28.3 us -> 27.4 us
    ppermute x3, waiting for transfers between devices: 11.4 us -> 9.71 us  [to_neighbours(): lax.ppermute(down, 'gz', ring('gz', gz, 1))]
    unnamed x2 -> x6, local copies, waits for them, and re-layouts: 0.01 us -> 1.17 us
    pallas_call x1, Pallas kernels: 2.29 us -> 1.59 us  [pack_call(): pl.pallas_call(functools.partial(pack_kernel, tiles), out_shape=[jax.Shap...]
  transfers between devices with their start and end apart: 9 -> 9, of which waited for: 5 -> 6; matrix products, arithmetic and copies ran while one was open for 0% -> 0% of each run, Pallas kernels for 40% -> 41%
where the time goes in v21:
time: 60.1 us; the launch traced here: 59.7 us
  Pallas kernels  27.4 us (46%)
  starting transfers between devices  17.6 us (29%)
  waiting for transfers between devices  13.4 us (22%)
  local copies, waits for them, and re-layouts  1.17 us (2%)
    ppermute x3, waiting for transfers between devices, to_neighbours(): lax.ppermute(down, 'gz', ring('gz', gz, 1))  9.71 us
    pallas_call x1, Pallas kernels, own_call(): pl.pallas_call(functools.partial(own_kernel, segments, groups), out_shape...  7.14 us
    all_to_all x1, starting transfers between devices, body(): got = lax.all_to_all(coarse, both, split_axis=0, concat_axis=0, tiled=True)  5.78 us
    all_to_all x1, starting transfers between devices, body(): back = lax.all_to_all(mark, both, split_axis=0, concat_axis=0, tiled=True)  5.7 us
    pallas_call x1, Pallas kernels, inverse_call(): pl.pallas_call(functools.partial(inverse_kernel, upper), out_shape=[jax.S...  5.69 us
    pallas_call x1, Pallas kernels, middle_call(): pl.pallas_call(middle_kernel, out_shape=pltpu.HBM((CH, rows, NX), F32), i...  4.67 us
    ppermute x3, starting transfers between devices, to_neighbours(): lax.ppermute(down, 'gz', ring('gz', gz, 1))  4.37 us
    pallas_call x1, Pallas kernels, forward_call(): pl.pallas_call(forward_kernel, out_shape=(pltpu.HBM if pinned else jax.Sh...  4.14 us
  transfers between devices with their start and end apart: 9, of which 6 were waited for; matrix products, arithmetic and copies ran while one was open for 0% of the time, Pallas kernels for 41%

profile of v21, /device:TPU:1, one launch (start us, length us, event | category | flops | bytes accessed | tf_op | source)
XLA Modules:
  0.0 59.7 jit_solution(16495482036611626384)
XLA Ops:
  0.0 1.6 %packed_rows.1 = (f32[26,32,256]{2,1,0:T(8,128)S(1)}, f32[2,32,256]{2,1,0:T(8,128)S(1)}) custom-call(f32[32,64,256]{2,1,0:T(8,128)} %bitcast.21), custom_call_target="tpu_custom_call" | custom-call | flops 100000000 | bytes 262144 | tf_op jit(solution)/shard_map/packed_rows/pallas_call | solution.py:457
  1.6 0.0 copy-start
  1.6 2.7 %collective-permute-start.1 = (f32[26,32,256]{2,1,0:T(8,128)S(1)}, f32[26,32,256]{2,1,0:T(8,128)}, u32[]{:S(2)}, u32[]{:S(2)}) collective-permute-start(f32[26,32,256]{2,1,0:T(8,128)S(1)} %get-tuple-element.38.own), channel_id=1, source_target_pairs={{0,2},{2,4},{4,6},{6,8},{8,10},{10,12},{12,14},{14,16},{16,18},{18... | collective-permute-start | bytes 2555912 | tf_op jit(solution)/shard_map/ppermute | solution.py:565
  4.3 0.0 collective-permute-start.2
  4.3 1.2 %collective-permute-start = (f32[2,32,256]{2,1,0:T(8,128)S(1)}, f32[2,32,256]{2,1,0:T(8,128)S(1)}, u32[]{:S(2)}, u32[]{:S(2)}) collective-permute-start(f32[2,32,256]{2,1,0:T(8,128)S(1)} %get-tuple-element.28), channel_id=1, source_target_pairs={{0,1},{1,0},{2,3},{3,2},{4,5},{5,4},{6,7},{7,6},{8,9},{9,8},{10,11... | collective-permute-start | bytes 196616 | tf_op jit(solution)/shard_map/ppermute | solution.py:579
  5.5 4.1 %forward_modes.1 = f32[256,128]{1,0:T(8,128)} custom-call(f32[8,4,64,256]{3,2,1,0:T(8,128)} %bitcast.22, bf16[2,256,128]{2,1,0:T(8,128)(2,1)} %constant.24.clone.x_top, bf16[2,256,128]{2,1,0:T(8,128)(2,1)} %constant.25.clone.x_rest, bf16[2,32,64]{2,1,0:T(8,128)(2,1)} %constant.26.clone.y_top, bf16[2,32,64]{2,1,0:T(8,128)(2,1)} %constant.27.clone.y_rest), custom_call_target="tpu_custom_call" | custom-call | flops 100000000 | bytes 262144 | tf_op jit(solution)/shard_map/forward_modes/pallas_call | solution.py:378
  9.7 0.0 collective-permute-done.halo
  9.7 5.8 %all-to-all-start = ((f32[32,8,128]{2,1,0:T(8,128)}), f32[32,8,128]{2,1,0:T(8,128)S(1)}, u32[]{:S(2)}, u32[]{:S(2)}) async-start(f32[32,8,128]{2,1,0:T(8,128)} %bitcast.27), calls=%async_computation | async-start | bytes 262144 | tf_op jit(solution)/shard_map/all_to_all | solution.py:596
  15.5 7.1 %own_sums.1 = (f32[32,16,256]{2,1,0:T(8,128)}, f32[32,16,256]{2,1,0:T(8,128)}, f32[32,16,256]{2,1,0:T(8,128)}, f32[32,24,256]{2,1,0:T(8,128)}, f32[32,24,256]{2,1,0:T(8,128)}, /*index=5*/f32[32,24,256]{2,1,0:T(8,128)}) custom-call(f32[32,27]{1,0:T(8,128)} %weight.3, f32[32,32]{1,0:T(8,128)} %point.3, f32[32,64,256]{2,1,0:T(8,128)} %bitcast.23, ...), custom_call_target="tpu_custom_call" | custom-call | flops 100000000 | bytes 262144 | tf_op jit(solution)/shard_map/own_sums/pallas_call | solution.py:477
  22.6 0.0 copy-done
  22.6 1.8 %collective-permute-done.1.low = f32[26,32,256]{2,1,0:T(8,128)} collective-permute-done((f32[26,32,256]{2,1,0:T(8,128)S(1)}, f32[26,32,256]{2,1,0:T(8,128)}, u32[]{:S(2)}, u32[]{:S(2)}) %collective-permute-start.1) | collective-permute-done | bytes 852000 | tf_op jit(solution)/shard_map/ppermute | solution.py:565
  24.4 2.6 %collective-permute-done.2.high = f32[26,32,256]{2,1,0:T(8,128)} collective-permute-done((f32[26,32,256]{2,1,0:T(8,128)S(1)}, f32[26,32,256]{2,1,0:T(8,128)}, u32[]{:S(2)}, u32[]{:S(2)}) %collective-permute-start.2) | collective-permute-done | bytes 852000 | tf_op jit(solution)/shard_map/ppermute | solution.py:566
  27.0 0.0 collective-permute-start.3
  27.0 0.5 collective-permute-start.4
  27.5 0.0 all-to-all-done
  27.5 0.0 copy-start.2
  27.5 2.7 %filter_modes.1 = f32[256,128]{1,0:T(8,128)} custom-call(f32[256,128]{1,0:T(8,128)S(1)} %bitcast.20, f32[2,16,8,64]{3,2,1,0:T(8,128)} %gains, bf16[256,256]{1,0:T(8,128)(2,1)} %constant.28.clone.f_top, bf16[256,256]{1,0:T(8,128)(2,1)} %constant.29.clone.f_rest, bf16[512,128]{1,0:T(8,128)(2,1)} %constant.30.clone.i_top, bf16[512,128]{1,0:T(8,128)(2,1)} %constant.31.clone.i_rest), custom_call_target="tpu_custom_call" | custom-call | flops 40000000000 | bytes 262144 | tf_op jit(solution)/shard_map/filter_modes/pallas_call | solution.py:397
  30.2 5.7 %all-to-all-start.1 = ((f32[32,8,128]{2,1,0:T(8,128)}), f32[32,8,128]{2,1,0:T(8,128)S(1)}, u32[]{:S(2)}, u32[]{:S(2)}) async-start(f32[32,8,128]{2,1,0:T(8,128)} %bitcast.29), calls=%async_computation.1 | async-start | bytes 262144 | tf_op jit(solution)/shard_map/all_to_all | solution.py:601
  35.9 1.7 %collective-permute-start.5 = (f32[32,24,256]{2,1,0:T(8,128)}, f32[32,24,256]{2,1,0:T(8,128)S(1)}, u32[]{:S(2)}, u32[]{:S(2)}) collective-permute-start(f32[32,24,256]{2,1,0:T(8,128)} %get-tuple-element.44), channel_id=1, source_target_pairs={{0,2},{2,4},{4,6},{6,8},{8,10},{10,12},{12,14},{14,16},{16,18},{18... | collective-permute-start | bytes 2359304 | tf_op jit(solution)/shard_map/ppermute | solution.py:565
  37.6 0.0 copy-done.2
  37.6 0.0 collective-permute-start.6
  37.6 2.3 %collective-permute-done.3 = f32[32,16,256]{2,1,0:T(8,128)S(1)} collective-permute-done((f32[32,16,256]{2,1,0:T(8,128)}, f32[32,16,256]{2,1,0:T(8,128)S(1)}, u32[]{:S(2)}, u32[]{:S(2)}) %collective-permute-start.3) | collective-permute-done | bytes 524320 | tf_op jit(solution)/shard_map/ppermute | solution.py:565
  39.9 0.2 collective-permute-done.4
  40.1 0.0 copy-start.1
  40.1 1.2 %copy-done.1 = f32[26,32,256]{2,1,0:T(8,128)S(1)} copy-done((f32[26,32,256]{2,1,0:T(8,128)S(1)}, f32[26,32,256]{2,1,0:T(8,128)}, u32[]{:S(2)}) %copy-start.1) | copy-done | bytes 851992
  41.2 4.7 %middle_sums.1 = f32[32,24,256]{2,1,0:T(8,128)} custom-call(f32[32,27]{1,0:T(8,128)} %weight.3, f32[32,32]{1,0:T(8,128)} %point.3, f32[26,32,256]{2,1,0:T(8,128)} %collective-permute-done.1.low, f32[26,32,256]{2,1,0:T(8,128)S(1)} %copy-done.1, f32[26,32,256]{2,1,0:T(8,128)} %collective-permute-done.2.high), custom_call_target="tpu_custom_call" | custom-call | flops 40000000000 | bytes 262144 | tf_op jit(solution)/shard_map/middle_sums/pallas_call | solution.py:504
  45.9 0.0 all-to-all-done.1
  45.9 5.7 %inverse_modes.1 = (f32[8,4,64,256]{3,2,1,0:T(8,128)}, f32[8,4,24,256]{3,2,1,0:T(8,128)S(1)}) custom-call(f32[16,16,128]{2,1,0:T(8,128)S(1)} %bitcast.19, f32[32]{0:T(128)} %bias.1, bf16[2,128,256]{2,1,0:T(8,128)(2,1)} %constant.32.clone.x_top, bf16[2,128,256]{2,1,0:T(8,128)(2,1)} %constant.33.clone.x_rest, bf16[2,64,32]{2,1,0:T(8,128)(2,1)} %constant.34.clone.y_top, ...), custom_call_target="tpu_custom_call" | custom-call | flops 100000000 | bytes 262144 | tf_op jit(solution)/shard_map/inverse_modes/pallas_call | solution.py:411
  51.6 5.7 %collective-permute-done.5.low = f32[32,24,256]{2,1,0:T(8,128)S(1)} collective-permute-done((f32[32,24,256]{2,1,0:T(8,128)}, f32[32,24,256]{2,1,0:T(8,128)S(1)}, u32[]{:S(2)}, u32[]{:S(2)}) %collective-permute-start.5) | collective-permute-done | bytes 786464 | tf_op jit(solution)/shard_map/ppermute | solution.py:565
  57.3 0.9 %collective-permute-done.6.high = f32[32,24,256]{2,1,0:T(8,128)S(1)} collective-permute-done((f32[32,24,256]{2,1,0:T(8,128)S(1)}, f32[32,24,256]{2,1,0:T(8,128)S(1)}, u32[]{:S(2)}, u32[]{:S(2)}) %collective-permute-start.6) | collective-permute-done | bytes 786464 | tf_op jit(solution)/shard_map/ppermute | solution.py:566
  58.2 1.5 %finished_rows.1 = f32[32,64,256]{2,1,0:T(8,128)} custom-call(f32[32,64,256]{2,1,0:T(8,128)} %bitcast.24, f32[32,24,256]{2,1,0:T(8,128)S(1)} %bitcast.16, f32[32,24,256]{2,1,0:T(8,128)S(1)} %collective-permute-done.5.low, f32[32,24,256]{2,1,0:T(8,128)S(1)} %collective-permute-done.6.high), custom_call_target="tpu_custom_call", output_to_operand_aliasing={{}: (0, {})} | custom-call | flops 100000000 | bytes 262144 | tf_op jit(solution)/shard_map/finished_rows/pallas_call | solution.py:437
Async XLA Ops:
  1.6 21.0 %copy-start = (f32[26,32,256]{2,1,0:T(8,128)}, f32[26,32,256]{2,1,0:T(8,128)S(1)}, u32[]{:S(2)}) copy-start(f32[26,32,256]{2,1,0:T(8,128)S(1)} %get-tuple-element.38.own) | copy-start | bytes 2555908
  1.6 22.8 %collective-permute-start.1 = (f32[26,32,256]{2,1,0:T(8,128)S(1)}, f32[26,32,256]{2,1,0:T(8,128)}, u32[]{:S(2)}, u32[]{:S(2)}) collective-permute-start(f32[26,32,256]{2,1,0:T(8,128)S(1)} %get-tuple-element.38.own), channel_id=1, source_target_pairs={{0,2},{2,4},{4,6},{6,8},{8,10},{10,12},{12,14},{14,16},{16,18},{18... | collective-permute-start | bytes 2555912 | tf_op jit(solution)/shard_map/ppermute | solution.py:565
  4.3 22.7 %collective-permute-start.2 = (f32[26,32,256]{2,1,0:T(8,128)S(1)}, f32[26,32,256]{2,1,0:T(8,128)}, u32[]{:S(2)}, u32[]{:S(2)}) collective-permute-start(f32[26,32,256]{2,1,0:T(8,128)S(1)} %get-tuple-element.38.own), channel_id=1, source_target_pairs={{0,30},{2,0},{4,2},{6,4},{8,6},{10,8},{12,10},{14,12},{16,14},{18,... | collective-permute-start | bytes 2555912 | tf_op jit(solution)/shard_map/ppermute | solution.py:566
  4.3 5.4 %collective-permute-start = (f32[2,32,256]{2,1,0:T(8,128)S(1)}, f32[2,32,256]{2,1,0:T(8,128)S(1)}, u32[]{:S(2)}, u32[]{:S(2)}) collective-permute-start(f32[2,32,256]{2,1,0:T(8,128)S(1)} %get-tuple-element.28), channel_id=1, source_target_pairs={{0,1},{1,0},{2,3},{3,2},{4,5},{5,4},{6,7},{7,6},{8,9},{9,8},{10,11... | collective-permute-start | bytes 196616 | tf_op jit(solution)/shard_map/ppermute | solution.py:579
  9.7 17.8 %all-to-all-start = ((f32[32,8,128]{2,1,0:T(8,128)}), f32[32,8,128]{2,1,0:T(8,128)S(1)}, u32[]{:S(2)}, u32[]{:S(2)}) async-start(f32[32,8,128]{2,1,0:T(8,128)} %bitcast.27), calls=%async_computation | async-start | bytes 262144 | tf_op jit(solution)/shard_map/all_to_all | solution.py:596
  27.0 12.9 %collective-permute-start.3 = (f32[32,16,256]{2,1,0:T(8,128)}, f32[32,16,256]{2,1,0:T(8,128)S(1)}, u32[]{:S(2)}, u32[]{:S(2)}) collective-permute-start(f32[32,16,256]{2,1,0:T(8,128)} %get-tuple-element.36), channel_id=1, source_target_pairs={{0,2},{2,4},{4,6},{6,8},{8,10},{10,12},{12,14},{14,16},{16,18},{18... | collective-permute-start | bytes 1572872 | tf_op jit(solution)/shard_map/ppermute | solution.py:565
  27.0 13.1 %collective-permute-start.4 = (f32[32,16,256]{2,1,0:T(8,128)}, f32[32,16,256]{2,1,0:T(8,128)S(1)}, u32[]{:S(2)}, u32[]{:S(2)}) collective-permute-start(f32[32,16,256]{2,1,0:T(8,128)} %get-tuple-element.37), channel_id=1, source_target_pairs={{0,30},{2,0},{4,2},{6,4},{8,6},{10,8},{12,10},{14,12},{16,14},{18,... | collective-permute-start | bytes 1572872 | tf_op jit(solution)/shard_map/ppermute | solution.py:566
  27.5 10.1 %copy-start.2 = (f32[32,24,256]{2,1,0:T(8,128)S(1)}, f32[32,24,256]{2,1,0:T(8,128)}, u32[]{:S(2)}) copy-start(f32[32,24,256]{2,1,0:T(8,128)} %get-tuple-element.46) | copy-start | bytes 2359300
  30.2 15.7 %all-to-all-start.1 = ((f32[32,8,128]{2,1,0:T(8,128)}), f32[32,8,128]{2,1,0:T(8,128)S(1)}, u32[]{:S(2)}, u32[]{:S(2)}) async-start(f32[32,8,128]{2,1,0:T(8,128)} %bitcast.29), calls=%async_computation.1 | async-start | bytes 262144 | tf_op jit(solution)/shard_map/all_to_all | solution.py:601
  35.9 21.4 %collective-permute-start.5 = (f32[32,24,256]{2,1,0:T(8,128)}, f32[32,24,256]{2,1,0:T(8,128)S(1)}, u32[]{:S(2)}, u32[]{:S(2)}) collective-permute-start(f32[32,24,256]{2,1,0:T(8,128)} %get-tuple-element.44), channel_id=1, source_target_pairs={{0,2},{2,4},{4,6},{6,8},{8,10},{10,12},{12,14},{14,16},{16,18},{18... | collective-permute-start | bytes 2359304 | tf_op jit(solution)/shard_map/ppermute | solution.py:565
  37.6 20.6 %collective-permute-start.6 = (f32[32,24,256]{2,1,0:T(8,128)S(1)}, f32[32,24,256]{2,1,0:T(8,128)S(1)}, u32[]{:S(2)}, u32[]{:S(2)}) collective-permute-start(f32[32,24,256]{2,1,0:T(8,128)S(1)} %copy-done.2), channel_id=1, source_target_pairs={{0,30},{2,0},{4,2},{6,4},{8,6},{10,8},{12,10},{14,12},{16,14},{18,... | collective-permute-start | bytes 2359304 | tf_op jit(solution)/shard_map/ppermute | solution.py:566
  40.1 1.2 %copy-start.1 = (f32[26,32,256]{2,1,0:T(8,128)S(1)}, f32[26,32,256]{2,1,0:T(8,128)}, u32[]{:S(2)}) copy-start(f32[26,32,256]{2,1,0:T(8,128)} %copy-done) | copy-start | bytes 2555908

commit v22 on v21

--- a/solution.py
+++ b/solution.py
@@ -60,11 +60,10 @@
 def z_tables(gz, gy, rows, scale):
     c, s = trig(kept(MZ, gz), np.arange(gz), gz)
     eye = np.eye(rows)
-    one = np.ones(gy)
     both = np.stack([c, s])
-    fwd = np.einsum("tqz,g,jk->tqjzgk", both, one, eye) * scale
-    inv = np.einsum("tqz,g,jk->tzgjqk", both, one, eye)
-    return fwd.reshape(2 * MZ * rows, gz * gy * rows), inv.reshape(2 * gz * gy * rows, MZ * rows)
+    fwd = np.einsum("tqz,g,jk->tqjzgk", both, np.ones(gy), eye) * scale
+    inv = np.einsum("tqz,jk->tzjqk", both, eye)
+    return fwd.reshape(2 * MZ * rows, gz * gy * rows), inv.reshape(2 * gz * rows, MZ * rows)
 
 
 def parts(value):
@@ -309,7 +308,7 @@
     return value * jnp.where(value < 0.0, tail, 1.0 - tail)
 
 
-def inverse_kernel(upper, modes, bias, x_top, x_rest, y_top, y_rest, own, middle, second, low, high, out, base, columns):
+def inverse_kernel(upper, halved, first_modes, second_modes, bias, x_top, x_rest, y_top, y_rest, own, middle, second, low, high, out, base, columns):
     q = pl.program_id(0)
     groups, _, y_local, _ = out.shape
 
@@ -317,7 +316,14 @@
     def _():
         gy = lax.axis_index("gy")
         for g in range(groups):
-            own_modes = jnp.concatenate([modes[2 * g], modes[2 * g + 1]], axis=1)
+            pairs = []
+            for pair in (2 * g, 2 * g + 1):
+                some = pl.ds(pair * (MY // 2), MY // 2)
+                one, two = first_modes[some, :], second_modes[some, :]
+                if halved:
+                    one, two = jnp.where(gy == 0, one, two), jnp.where(gy == 0, two, one)
+                pairs.append(jnp.concatenate([one, two], axis=0))
+            own_modes = jnp.concatenate(pairs, axis=1)
             crossed, is_real = swap_parts(own_modes)
             stack = jnp.concatenate([own_modes, jnp.where(is_real, -crossed, crossed)], axis=0)
             pair = parts(dot3((y_top[gy], y_rest[gy]), parts(stack)))
@@ -396,27 +402,27 @@
     fwd, inv = halves(fwd), halves(inv)
     return pl.pallas_call(
         filter_kernel,
-        out_shape=pltpu.HBM(arrived.shape, F32),
+        out_shape=pltpu.HBM((arrived.shape[0] // gy, arrived.shape[1]), F32),
         compiler_params=params(),
         cost_estimate=cost(4 * 10**10, 2**18),
         name="filter_modes",
     )(arrived, *in_hbm(gains, *fwd, *inv))
 
 
-def inverse_call(modes, bias, own, middle, second, pair, upper, y_local, gy, scale):
+def inverse_call(modes, halved, bias, own, middle, second, pair, upper, y_local, gy, scale):
     tables = [*halves(x_table(True, scale)), *halves(y_table(y_local, gy, True))]
     some = lambda rows: pl.BlockSpec((CH // 4, 1, rows, NX), lambda i: (0, i, 0, 0))
     planes = [*in_hbm(*map(by_four, (own, middle, second))), *map(by_four, pair)]
     rim = own.shape[1]
     result, base = pl.pallas_call(
-        functools.partial(inverse_kernel, upper),
+        functools.partial(inverse_kernel, upper, halved),
         out_shape=[
             jax.ShapeDtypeStruct((CH // 4, 4, y_local, NX), F32),
             jax.ShapeDtypeStruct((CH // 4, 4, rim, NX), F32),
         ],
         grid=(4,),
         in_specs=[
-            whole_block(modes),
+            *[whole_block(m) for m in modes],
             pl.BlockSpec(memory_space=pltpu.SMEM),
             *[whole_block(t) for t in tables],
             *[some(p.shape[2]) for p in planes],
@@ -426,7 +432,7 @@
         compiler_params=params(),
         cost_estimate=cost(10**8, 2**18),
         name="inverse_modes",
-    )(modes, *in_hbm(bias, *tables), *planes)
+    )(*modes, *in_hbm(bias, *tables), *planes)
     return result.reshape(CH, y_local, NX), base.reshape(CH, rim, NX)
 
 
@@ -598,16 +604,18 @@
         pair = to_neighbours(down, up)
         gains = after(spectral_filter, first_low, first_high, second)
         mark = filter_call(got, gains, gz, gy, forward_scale)
-        back = lax.all_to_all(mark, both, split_axis=0, concat_axis=0, tiled=True)
-        back = back.reshape(CH // 2, MY, 4 * MX)
+        back = lax.all_to_all(mark, "gz", split_axis=0, concat_axis=0, tiled=True)
     else:
         pair = to_neighbours(down, up)
-        mark = back = general_filter(coarse, spectral_filter, gz, gy, forward_scale)
+        mark = general_filter(coarse, spectral_filter, gz, gy, forward_scale)
+        modes = [mark[:, part].reshape(-1, 4 * MX) for part in (slice(0, MY // 2), slice(MY // 2, MY))]
     outer_pair = to_neighbours(after(outer_down, mark), after(outer_up, mark))
     packed, *pair = lax.optimization_barrier((packed, *pair))
     mixed = middle_call(depth_weight, point_weight, first_low, packed, first_high)
+    if whole_tiles:
+        modes = (back, lax.ppermute(after(back, mixed), "gy", ring("gy", gy, 1)))
     result, base = inverse_call(
-        back, bias_vector, own, mixed, second, pair, 8, y_local, gy, inverse_scale
+        modes, whole_tiles, bias_vector, own, mixed, second, pair, 8, y_local, gy, inverse_scale
     )
     result = finish_call(result, base, *outer_pair, 1)
     return result.reshape(CH, 1, y_local, NX)

time: 60.1 us -> 60.4 us (level)
  starting transfers between devices: 17.6 us -> 19.2 us
  local copies, waits for them, and re-layouts: 1.17 us -> 0 us
    ppermute x3, waiting for transfers between devices: 9.71 us -> 6.48 us  [to_neighbours(): lax.ppermute(down, 'gz', ring('gz', gz, 1))]
    ppermute x0 -> x1, waiting for transfers between devices: none -> 2.04 us  [body(): modes = (back, lax.ppermute(after(back, mixed), 'gy', ring('gy', gy, 1)))]
    ppermute x0 -> x1, starting transfers between devices: none -> 1.44 us  [body(): modes = (back, lax.ppermute(after(back, mixed), 'gy', ring('gy', gy, 1)))]
    unnamed x6 -> x0, local copies, waits for them, and re-layouts: 1.17 us -> none
    ppermute x3, waiting for transfers between devices: 3.7 us -> 4.39 us  [to_neighbours(): lax.ppermute(up, 'gz', ring('gz', gz, -1))]
    pallas_call x1, Pallas kernels: 1.59 us -> 2.22 us  [pack_call(): pl.pallas_call(functools.partial(pack_kernel, tiles), out_shape=[jax.Shap...]
  transfers between devices with their start and end apart: 9 -> 10, of which waited for: 6 -> 7; matrix products, arithmetic and copies ran while one was open for 0% -> 0% of each run, Pallas kernels for 41% -> 40%
where the time goes in v22:
time: 60.4 us; the launch traced here: 59.9 us
  Pallas kernels  27.7 us (46%)
  starting transfers between devices  19.2 us (32%)
  waiting for transfers between devices  12.9 us (21%)
    pallas_call x1, Pallas kernels, own_call(): pl.pallas_call(functools.partial(own_kernel, segments, groups), out_shape...  7.14 us
    ppermute x3, waiting for transfers between devices, to_neighbours(): lax.ppermute(down, 'gz', ring('gz', gz, 1))  6.48 us
    all_to_all x1, starting transfers between devices, body(): back = lax.all_to_all(mark, 'gz', split_axis=0, concat_axis=0, tiled=True)  5.96 us
    all_to_all x1, starting transfers between devices, body(): got = lax.all_to_all(coarse, both, split_axis=0, concat_axis=0, tiled=True)  5.79 us
    pallas_call x1, Pallas kernels, inverse_call(): pl.pallas_call(functools.partial(inverse_kernel, upper, halved), out_shap...  5.65 us
    pallas_call x1, Pallas kernels, middle_call(): pl.pallas_call(middle_kernel, out_shape=pltpu.HBM((CH, rows, NX), F32), i...  4.66 us
    ppermute x3, waiting for transfers between devices, to_neighbours(): lax.ppermute(up, 'gz', ring('gz', gz, -1))  4.39 us
    ppermute x3, starting transfers between devices, to_neighbours(): lax.ppermute(down, 'gz', ring('gz', gz, 1))  4.32 us
  transfers between devices with their start and end apart: 10, of which 7 were waited for; matrix products, arithmetic and copies ran while one was open for 0% of the time, Pallas kernels for 40%

profile of v22, /device:TPU:1, one launch (start us, length us, event | category | flops | bytes accessed | tf_op | source)
XLA Modules:
  0.0 59.9 jit_solution(15351228504148122105)
XLA Ops:
  0.0 2.2 %packed_rows.1 = (f32[26,32,256]{2,1,0:T(8,128)S(1)}, f32[2,32,256]{2,1,0:T(8,128)}) custom-call(f32[32,64,256]{2,1,0:T(8,128)} %bitcast.22), custom_call_target="tpu_custom_call" | custom-call | flops 100000000 | bytes 262144 | tf_op jit(solution)/shard_map/packed_rows/pallas_call | solution.py:463
  2.2 2.7 %collective-permute-start.1 = (f32[26,32,256]{2,1,0:T(8,128)S(1)}, f32[26,32,256]{2,1,0:T(8,128)}, u32[]{:S(2)}, u32[]{:S(2)}) collective-permute-start(f32[26,32,256]{2,1,0:T(8,128)S(1)} %get-tuple-element.38.own), channel_id=1, source_target_pairs={{0,2},{2,4},{4,6},{6,8},{8,10},{10,12},{12,14},{14,16},{16,18},{18... | collective-permute-start | bytes 2555912 | tf_op jit(solution)/shard_map/ppermute | solution.py:571
  4.9 0.0 collective-permute-start.2
  4.9 1.2 %collective-permute-start = (f32[2,32,256]{2,1,0:T(8,128)}, f32[2,32,256]{2,1,0:T(8,128)S(1)}, u32[]{:S(2)}, u32[]{:S(2)}) collective-permute-start(f32[2,32,256]{2,1,0:T(8,128)} %get-tuple-element.29), channel_id=1, source_target_pairs={{0,1},{1,0},{2,3},{3,2},{4,5},{5,4},{6,7},{7,6},{8,9},{9,8},{10,11... | collective-permute-start | bytes 196616 | tf_op jit(solution)/shard_map/ppermute | solution.py:585
  6.1 4.1 %forward_modes.1 = f32[256,128]{1,0:T(8,128)} custom-call(f32[8,4,64,256]{3,2,1,0:T(8,128)} %bitcast.23, bf16[2,256,128]{2,1,0:T(8,128)(2,1)} %constant.24.clone.x_top, bf16[2,256,128]{2,1,0:T(8,128)(2,1)} %constant.25.clone.x_rest, bf16[2,32,64]{2,1,0:T(8,128)(2,1)} %constant.26.clone.y_top, bf16[2,32,64]{2,1,0:T(8,128)(2,1)} %constant.27.clone.y_rest), custom_call_target="tpu_custom_call" | custom-call | flops 100000000 | bytes 262144 | tf_op jit(solution)/shard_map/forward_modes/pallas_call | solution.py:384
  10.3 0.0 collective-permute-done.halo
  10.3 5.8 %all-to-all-start = ((f32[32,8,128]{2,1,0:T(8,128)}), f32[32,8,128]{2,1,0:T(8,128)S(1)}, u32[]{:S(2)}, u32[]{:S(2)}) async-start(f32[32,8,128]{2,1,0:T(8,128)} %bitcast.28), calls=%async_computation | async-start | bytes 262144 | tf_op jit(solution)/shard_map/all_to_all | solution.py:602
  16.1 7.1 %own_sums.1 = (f32[32,16,256]{2,1,0:T(8,128)}, f32[32,16,256]{2,1,0:T(8,128)}, f32[32,16,256]{2,1,0:T(8,128)}, f32[32,24,256]{2,1,0:T(8,128)}, f32[32,24,256]{2,1,0:T(8,128)}, /*index=5*/f32[32,24,256]{2,1,0:T(8,128)}) custom-call(f32[32,27]{1,0:T(8,128)} %weight.3, f32[32,32]{1,0:T(8,128)} %point.3, f32[32,64,256]{2,1,0:T(8,128)} %bitcast.24, ...), custom_call_target="tpu_custom_call" | custom-call | flops 100000000 | bytes 262144 | tf_op jit(solution)/shard_map/own_sums/pallas_call | solution.py:483
  23.2 1.8 %collective-permute-done.1.low = f32[26,32,256]{2,1,0:T(8,128)} collective-permute-done((f32[26,32,256]{2,1,0:T(8,128)S(1)}, f32[26,32,256]{2,1,0:T(8,128)}, u32[]{:S(2)}, u32[]{:S(2)}) %collective-permute-start.1) | collective-permute-done | bytes 852000 | tf_op jit(solution)/shard_map/ppermute | solution.py:571
  25.0 2.6 %collective-permute-done.2.high = f32[26,32,256]{2,1,0:T(8,128)} collective-permute-done((f32[26,32,256]{2,1,0:T(8,128)S(1)}, f32[26,32,256]{2,1,0:T(8,128)}, u32[]{:S(2)}, u32[]{:S(2)}) %collective-permute-start.2) | collective-permute-done | bytes 852000 | tf_op jit(solution)/shard_map/ppermute | solution.py:572
  27.6 0.0 collective-permute-start.3
  27.6 0.5 collective-permute-start.4
  28.1 0.0 all-to-all-done
  28.1 2.4 %filter_modes.1 = f32[128,128]{1,0:T(8,128)} custom-call(f32[256,128]{1,0:T(8,128)S(1)} %bitcast.21, f32[2,16,8,64]{3,2,1,0:T(8,128)} %gains, bf16[256,256]{1,0:T(8,128)(2,1)} %constant.28.clone.f_top, bf16[256,256]{1,0:T(8,128)(2,1)} %constant.29.clone.f_rest, bf16[256,128]{1,0:T(8,128)(2,1)} %constant.30.clone.i_top, bf16[256,128]{1,0:T(8,128)(2,1)} %constant.31.clone.i_rest), custom_call_target="tpu_custom_call" | custom-call | flops 40000000000 | bytes 262144 | tf_op jit(solution)/shard_map/filter_modes/pallas_call | solution.py:403
  30.5 6.0 %all-to-all-start.1 = ((f32[16,8,128]{2,1,0:T(8,128)}), f32[16,8,128]{2,1,0:T(8,128)S(1)}, u32[]{:S(2)}, u32[]{:S(2)}) async-start(f32[16,8,128]{2,1,0:T(8,128)} %bitcast.30), calls=%async_computation.1 | async-start | bytes 131072 | tf_op jit(solution)/shard_map/all_to_all | solution.py:607
  36.5 1.6 %collective-permute-start.6 = (f32[32,24,256]{2,1,0:T(8,128)}, f32[32,24,256]{2,1,0:T(8,128)S(1)}, u32[]{:S(2)}, u32[]{:S(2)}) collective-permute-start(f32[32,24,256]{2,1,0:T(8,128)} %get-tuple-element.46), channel_id=1, source_target_pairs={{0,2},{2,4},{4,6},{6,8},{8,10},{10,12},{12,14},{14,16},{16,18},{18... | collective-permute-start | bytes 2359304 | tf_op jit(solution)/shard_map/ppermute | solution.py:571
  38.1 0.0 collective-permute-start.7
  38.1 1.9 %collective-permute-done.3 = f32[32,16,256]{2,1,0:T(8,128)S(1)} collective-permute-done((f32[32,16,256]{2,1,0:T(8,128)}, f32[32,16,256]{2,1,0:T(8,128)S(1)}, u32[]{:S(2)}, u32[]{:S(2)}) %collective-permute-start.3) | collective-permute-done | bytes 524320 | tf_op jit(solution)/shard_map/ppermute | solution.py:571
  40.0 0.6 collective-permute-done.4
  40.6 4.7 %middle_sums.1 = f32[32,24,256]{2,1,0:T(8,128)} custom-call(f32[32,27]{1,0:T(8,128)} %weight.3, f32[32,32]{1,0:T(8,128)} %point.3, f32[26,32,256]{2,1,0:T(8,128)} %collective-permute-done.1.low, f32[26,32,256]{2,1,0:T(8,128)S(1)} %get-tuple-element.38.own, f32[26,32,256]{2,1,0:T(8,128)} %collective-permute-done.2.high), custom_call_target="tpu_custom_call" | custom-call | flops 40000000000 | bytes 262144 | tf_op jit(solution)/shard_map/middle_sums/pallas_call | solution.py:510
  45.3 0.0 all-to-all-done.1
  45.3 1.4 %collective-permute-start.5 = (f32[128,128]{1,0:T(8,128)S(1)}, f32[128,128]{1,0:T(8,128)S(1)}, u32[]{:S(2)}, u32[]{:S(2)}) collective-permute-start(f32[128,128]{1,0:T(8,128)S(1)} %bitcast.19), channel_id=1, source_target_pairs={{0,1},{1,0},{2,3},{3,2},{4,5},{5,4},{6,7},{7,6},{8,9},{9,8},{10,11... | collective-permute-start | bytes 196616 | tf_op jit(solution)/shard_map/ppermute | solution.py:616
  46.7 2.0 %collective-permute-done.5.second_modes = f32[128,128]{1,0:T(8,128)S(1)} collective-permute-done((f32[128,128]{1,0:T(8,128)S(1)}, f32[128,128]{1,0:T(8,128)S(1)}, u32[]{:S(2)}, u32[]{:S(2)}) %collective-permute-start.5) | collective-permute-done | bytes 65568 | tf_op jit(solution)/shard_map/ppermute | solution.py:616
  48.7 5.7 %inverse_modes.1 = (f32[8,4,64,256]{3,2,1,0:T(8,128)}, f32[8,4,24,256]{3,2,1,0:T(8,128)S(1)}) custom-call(f32[128,128]{1,0:T(8,128)S(1)} %bitcast.20, f32[128,128]{1,0:T(8,128)S(1)} %collective-permute-done.5.second_modes, f32[32]{0:T(128)} %bias.1, bf16[2,128,256]{2,1,0:T(8,128)(2,1)} %constant.32.clone.x_top, bf16[2,128,256]{2,1,0:T(8,128)(2,1)} %constant.33.clone.x_rest, ...), custom_call_target="tpu_custom_call" | custom-call | flops 100000000 | bytes 262144 | tf_op jit(solution)/shard_map/inverse_modes/pallas_call | solution.py:417
  54.4 2.8 %collective-permute-done.6.low = f32[32,24,256]{2,1,0:T(8,128)S(1)} collective-permute-done((f32[32,24,256]{2,1,0:T(8,128)}, f32[32,24,256]{2,1,0:T(8,128)S(1)}, u32[]{:S(2)}, u32[]{:S(2)}) %collective-permute-start.6) | collective-permute-done | bytes 786464 | tf_op jit(solution)/shard_map/ppermute | solution.py:571
  57.2 1.3 %collective-permute-done.7.high = f32[32,24,256]{2,1,0:T(8,128)S(1)} collective-permute-done((f32[32,24,256]{2,1,0:T(8,128)}, f32[32,24,256]{2,1,0:T(8,128)S(1)}, u32[]{:S(2)}, u32[]{:S(2)}) %collective-permute-start.7) | collective-permute-done | bytes 786464 | tf_op jit(solution)/shard_map/ppermute | solution.py:572
  58.5 1.5 %finished_rows.1 = f32[32,64,256]{2,1,0:T(8,128)} custom-call(f32[32,64,256]{2,1,0:T(8,128)} %bitcast.25, f32[32,24,256]{2,1,0:T(8,128)S(1)} %bitcast.16, f32[32,24,256]{2,1,0:T(8,128)S(1)} %collective-permute-done.6.low, f32[32,24,256]{2,1,0:T(8,128)S(1)} %collective-permute-done.7.high), custom_call_target="tpu_custom_call", output_to_operand_aliasing={{}: (0, {})} | custom-call | flops 100000000 | bytes 262144 | tf_op jit(solution)/shard_map/finished_rows/pallas_call | solution.py:443
Async XLA Ops:
  2.2 22.8 %collective-permute-start.1 = (f32[26,32,256]{2,1,0:T(8,128)S(1)}, f32[26,32,256]{2,1,0:T(8,128)}, u32[]{:S(2)}, u32[]{:S(2)}) collective-permute-start(f32[26,32,256]{2,1,0:T(8,128)S(1)} %get-tuple-element.38.own), channel_id=1, source_target_pairs={{0,2},{2,4},{4,6},{6,8},{8,10},{10,12},{12,14},{14,16},{16,18},{18... | collective-permute-start | bytes 2555912 | tf_op jit(solution)/shard_map/ppermute | solution.py:571
  4.9 22.7 %collective-permute-start.2 = (f32[26,32,256]{2,1,0:T(8,128)S(1)}, f32[26,32,256]{2,1,0:T(8,128)}, u32[]{:S(2)}, u32[]{:S(2)}) collective-permute-start(f32[26,32,256]{2,1,0:T(8,128)S(1)} %get-tuple-element.38.own), channel_id=1, source_target_pairs={{0,30},{2,0},{4,2},{6,4},{8,6},{10,8},{12,10},{14,12},{16,14},{18,... | collective-permute-start | bytes 2555912 | tf_op jit(solution)/shard_map/ppermute | solution.py:572
  4.9 5.3 %collective-permute-start = (f32[2,32,256]{2,1,0:T(8,128)}, f32[2,32,256]{2,1,0:T(8,128)S(1)}, u32[]{:S(2)}, u32[]{:S(2)}) collective-permute-start(f32[2,32,256]{2,1,0:T(8,128)} %get-tuple-element.29), channel_id=1, source_target_pairs={{0,1},{1,0},{2,3},{3,2},{4,5},{5,4},{6,7},{7,6},{8,9},{9,8},{10,11... | collective-permute-start | bytes 196616 | tf_op jit(solution)/shard_map/ppermute | solution.py:585
  10.3 17.8 %all-to-all-start = ((f32[32,8,128]{2,1,0:T(8,128)}), f32[32,8,128]{2,1,0:T(8,128)S(1)}, u32[]{:S(2)}, u32[]{:S(2)}) async-start(f32[32,8,128]{2,1,0:T(8,128)} %bitcast.28), calls=%async_computation | async-start | bytes 262144 | tf_op jit(solution)/shard_map/all_to_all | solution.py:602
  27.6 12.4 %collective-permute-start.3 = (f32[32,16,256]{2,1,0:T(8,128)}, f32[32,16,256]{2,1,0:T(8,128)S(1)}, u32[]{:S(2)}, u32[]{:S(2)}) collective-permute-start(f32[32,16,256]{2,1,0:T(8,128)} %get-tuple-element.36), channel_id=1, source_target_pairs={{0,2},{2,4},{4,6},{6,8},{8,10},{10,12},{12,14},{14,16},{16,18},{18... | collective-permute-start | bytes 1572872 | tf_op jit(solution)/shard_map/ppermute | solution.py:571
  27.6 13.0 %collective-permute-start.4 = (f32[32,16,256]{2,1,0:T(8,128)}, f32[32,16,256]{2,1,0:T(8,128)S(1)}, u32[]{:S(2)}, u32[]{:S(2)}) collective-permute-start(f32[32,16,256]{2,1,0:T(8,128)} %get-tuple-element.37), channel_id=1, source_target_pairs={{0,30},{2,0},{4,2},{6,4},{8,6},{10,8},{12,10},{14,12},{16,14},{18,... | collective-permute-start | bytes 1572872 | tf_op jit(solution)/shard_map/ppermute | solution.py:572
  30.5 14.7 %all-to-all-start.1 = ((f32[16,8,128]{2,1,0:T(8,128)}), f32[16,8,128]{2,1,0:T(8,128)S(1)}, u32[]{:S(2)}, u32[]{:S(2)}) async-start(f32[16,8,128]{2,1,0:T(8,128)} %bitcast.30), calls=%async_computation.1 | async-start | bytes 131072 | tf_op jit(solution)/shard_map/all_to_all | solution.py:607
  36.5 20.7 %collective-permute-start.6 = (f32[32,24,256]{2,1,0:T(8,128)}, f32[32,24,256]{2,1,0:T(8,128)S(1)}, u32[]{:S(2)}, u32[]{:S(2)}) collective-permute-start(f32[32,24,256]{2,1,0:T(8,128)} %get-tuple-element.46), channel_id=1, source_target_pairs={{0,2},{2,4},{4,6},{6,8},{8,10},{10,12},{12,14},{14,16},{16,18},{18... | collective-permute-start | bytes 2359304 | tf_op jit(solution)/shard_map/ppermute | solution.py:571
  38.1 20.3 %collective-permute-start.7 = (f32[32,24,256]{2,1,0:T(8,128)}, f32[32,24,256]{2,1,0:T(8,128)S(1)}, u32[]{:S(2)}, u32[]{:S(2)}) collective-permute-start(f32[32,24,256]{2,1,0:T(8,128)} %get-tuple-element.48), channel_id=1, source_target_pairs={{0,30},{2,0},{4,2},{6,4},{8,6},{10,8},{12,10},{14,12},{16,14},{18,... | collective-permute-start | bytes 2359304 | tf_op jit(solution)/shard_map/ppermute | solution.py:572
  45.3 3.5 %collective-permute-start.5 = (f32[128,128]{1,0:T(8,128)S(1)}, f32[128,128]{1,0:T(8,128)S(1)}, u32[]{:S(2)}, u32[]{:S(2)}) collective-permute-start(f32[128,128]{1,0:T(8,128)S(1)} %bitcast.19), channel_id=1, source_target_pairs={{0,1},{1,0},{2,3},{3,2},{4,5},{5,4},{6,7},{7,6},{8,9},{9,8},{10,11... | collective-permute-start | bytes 196616 | tf_op jit(solution)/shard_map/ppermute | solution.py:616

commit v23 on v22

--- a/solution.py
+++ b/solution.py
@@ -16,7 +16,7 @@
 MZ = 16
 CH = 32
 VMEM_BYTES = 20 * 1024 * 1024
-ALL_VMEM_BYTES = 63 * 1024 * 1024
+ALL_VMEM_BYTES = 64000 * 1024
 BF = jnp.bfloat16
 F32 = jnp.float32
 

time: 60.4 us -> 59.8 us (0.990)
    pallas_call x1, Pallas kernels: 2.22 us -> 1.59 us  [pack_call(): pl.pallas_call(functools.partial(pack_kernel, tiles), out_shape=[jax.Shap...]
where the time goes in v23:
time: 59.8 us; the launch traced here: 59.3 us
  Pallas kernels  27.1 us (45%)
  starting transfers between devices  19.2 us (32%)
  waiting for transfers between devices  13 us (22%)
    pallas_call x1, Pallas kernels, own_call(): pl.pallas_call(functools.partial(own_kernel, segments, groups), out_shape...  7.13 us
    ppermute x3, waiting for transfers between devices, to_neighbours(): lax.ppermute(down, 'gz', ring('gz', gz, 1))  6.48 us
    all_to_all x1, starting transfers between devices, body(): back = lax.all_to_all(mark, 'gz', split_axis=0, concat_axis=0, tiled=True)  5.96 us
    all_to_all x1, starting transfers between devices, body(): got = lax.all_to_all(coarse, both, split_axis=0, concat_axis=0, tiled=True)  5.79 us
    pallas_call x1, Pallas kernels, inverse_call(): pl.pallas_call(functools.partial(inverse_kernel, upper, halved), out_shap...  5.65 us
    pallas_call x1, Pallas kernels, middle_call(): pl.pallas_call(middle_kernel, out_shape=pltpu.HBM((CH, rows, NX), F32), i...  4.66 us
    ppermute x3, waiting for transfers between devices, to_neighbours(): lax.ppermute(up, 'gz', ring('gz', gz, -1))  4.41 us
    ppermute x3, starting transfers between devices, to_neighbours(): lax.ppermute(down, 'gz', ring('gz', gz, 1))  4.32 us
  transfers between devices with their start and end apart: 10, of which 7 were waited for; matrix products, arithmetic and copies ran while one was open for 0% of the time, Pallas kernels for 40%

profile of v23, /device:TPU:1, one launch (start us, length us, event | category | flops | bytes accessed | tf_op | source)
XLA Modules:
  0.0 59.3 jit_solution(16211025224297132643)
XLA Ops:
  0.0 1.6 %packed_rows.1 = (f32[26,32,256]{2,1,0:T(8,128)S(1)}, f32[2,32,256]{2,1,0:T(8,128)S(1)}) custom-call(f32[32,64,256]{2,1,0:T(8,128)} %bitcast.22), custom_call_target="tpu_custom_call" | custom-call | flops 100000000 | bytes 262144 | tf_op jit(solution)/shard_map/packed_rows/pallas_call | solution.py:463
  1.6 2.7 %collective-permute-start.1 = (f32[26,32,256]{2,1,0:T(8,128)S(1)}, f32[26,32,256]{2,1,0:T(8,128)}, u32[]{:S(2)}, u32[]{:S(2)}) collective-permute-start(f32[26,32,256]{2,1,0:T(8,128)S(1)} %get-tuple-element.38.own), channel_id=1, source_target_pairs={{0,2},{2,4},{4,6},{6,8},{8,10},{10,12},{12,14},{14,16},{16,18},{18... | collective-permute-start | bytes 2555912 | tf_op jit(solution)/shard_map/ppermute | solution.py:571
  4.3 0.0 collective-permute-start.2
  4.3 1.2 %collective-permute-start = (f32[2,32,256]{2,1,0:T(8,128)S(1)}, f32[2,32,256]{2,1,0:T(8,128)S(1)}, u32[]{:S(2)}, u32[]{:S(2)}) collective-permute-start(f32[2,32,256]{2,1,0:T(8,128)S(1)} %get-tuple-element.29), channel_id=1, source_target_pairs={{0,1},{1,0},{2,3},{3,2},{4,5},{5,4},{6,7},{7,6},{8,9},{9,8},{10,11... | collective-permute-start | bytes 196616 | tf_op jit(solution)/shard_map/ppermute | solution.py:585
  5.5 4.1 %forward_modes.1 = f32[256,128]{1,0:T(8,128)} custom-call(f32[8,4,64,256]{3,2,1,0:T(8,128)} %bitcast.23, bf16[2,256,128]{2,1,0:T(8,128)(2,1)} %constant.24.clone.x_top, bf16[2,256,128]{2,1,0:T(8,128)(2,1)} %constant.25.clone.x_rest, bf16[2,32,64]{2,1,0:T(8,128)(2,1)} %constant.26.clone.y_top, bf16[2,32,64]{2,1,0:T(8,128)(2,1)} %constant.27.clone.y_rest), custom_call_target="tpu_custom_call" | custom-call | flops 100000000 | bytes 262144 | tf_op jit(solution)/shard_map/forward_modes/pallas_call | solution.py:384
  9.6 0.0 collective-permute-done.halo
  9.6 5.8 %all-to-all-start = ((f32[32,8,128]{2,1,0:T(8,128)}), f32[32,8,128]{2,1,0:T(8,128)S(1)}, u32[]{:S(2)}, u32[]{:S(2)}) async-start(f32[32,8,128]{2,1,0:T(8,128)} %bitcast.28), calls=%async_computation | async-start | bytes 262144 | tf_op jit(solution)/shard_map/all_to_all | solution.py:602
  15.4 7.1 %own_sums.1 = (f32[32,16,256]{2,1,0:T(8,128)}, f32[32,16,256]{2,1,0:T(8,128)}, f32[32,16,256]{2,1,0:T(8,128)}, f32[32,24,256]{2,1,0:T(8,128)}, f32[32,24,256]{2,1,0:T(8,128)}, /*index=5*/f32[32,24,256]{2,1,0:T(8,128)}) custom-call(f32[32,27]{1,0:T(8,128)} %weight.3, f32[32,32]{1,0:T(8,128)} %point.3, f32[32,64,256]{2,1,0:T(8,128)} %bitcast.24, ...), custom_call_target="tpu_custom_call" | custom-call | flops 100000000 | bytes 262144 | tf_op jit(solution)/shard_map/own_sums/pallas_call | solution.py:483
  22.6 1.8 %collective-permute-done.1.low = f32[26,32,256]{2,1,0:T(8,128)} collective-permute-done((f32[26,32,256]{2,1,0:T(8,128)S(1)}, f32[26,32,256]{2,1,0:T(8,128)}, u32[]{:S(2)}, u32[]{:S(2)}) %collective-permute-start.1) | collective-permute-done | bytes 852000 | tf_op jit(solution)/shard_map/ppermute | solution.py:571
  24.4 2.6 %collective-permute-done.2.high = f32[26,32,256]{2,1,0:T(8,128)} collective-permute-done((f32[26,32,256]{2,1,0:T(8,128)S(1)}, f32[26,32,256]{2,1,0:T(8,128)}, u32[]{:S(2)}, u32[]{:S(2)}) %collective-permute-start.2) | collective-permute-done | bytes 852000 | tf_op jit(solution)/shard_map/ppermute | solution.py:572
  27.0 0.0 collective-permute-start.3
  27.0 0.5 collective-permute-start.4
  27.5 0.0 all-to-all-done
  27.5 2.4 %filter_modes.1 = f32[128,128]{1,0:T(8,128)} custom-call(f32[256,128]{1,0:T(8,128)S(1)} %bitcast.21, f32[2,16,8,64]{3,2,1,0:T(8,128)} %gains, bf16[256,256]{1,0:T(8,128)(2,1)} %constant.28.clone.f_top, bf16[256,256]{1,0:T(8,128)(2,1)} %constant.29.clone.f_rest, bf16[256,128]{1,0:T(8,128)(2,1)} %constant.30.clone.i_top, bf16[256,128]{1,0:T(8,128)(2,1)} %constant.31.clone.i_rest), custom_call_target="tpu_custom_call" | custom-call | flops 40000000000 | bytes 262144 | tf_op jit(solution)/shard_map/filter_modes/pallas_call | solution.py:403
  29.9 6.0 %all-to-all-start.1 = ((f32[16,8,128]{2,1,0:T(8,128)}), f32[16,8,128]{2,1,0:T(8,128)S(1)}, u32[]{:S(2)}, u32[]{:S(2)}) async-start(f32[16,8,128]{2,1,0:T(8,128)} %bitcast.30), calls=%async_computation.1 | async-start | bytes 131072 | tf_op jit(solution)/shard_map/all_to_all | solution.py:607
  35.9 1.6 %collective-permute-start.6 = (f32[32,24,256]{2,1,0:T(8,128)}, f32[32,24,256]{2,1,0:T(8,128)S(1)}, u32[]{:S(2)}, u32[]{:S(2)}) collective-permute-start(f32[32,24,256]{2,1,0:T(8,128)} %get-tuple-element.46), channel_id=1, source_target_pairs={{0,2},{2,4},{4,6},{6,8},{8,10},{10,12},{12,14},{14,16},{16,18},{18... | collective-permute-start | bytes 2359304 | tf_op jit(solution)/shard_map/ppermute | solution.py:571
  37.5 0.0 collective-permute-start.7
  37.5 1.9 %collective-permute-done.3 = f32[32,16,256]{2,1,0:T(8,128)S(1)} collective-permute-done((f32[32,16,256]{2,1,0:T(8,128)}, f32[32,16,256]{2,1,0:T(8,128)S(1)}, u32[]{:S(2)}, u32[]{:S(2)}) %collective-permute-start.3) | collective-permute-done | bytes 524320 | tf_op jit(solution)/shard_map/ppermute | solution.py:571
  39.4 0.6 collective-permute-done.4
  40.0 4.7 %middle_sums.1 = f32[32,24,256]{2,1,0:T(8,128)} custom-call(f32[32,27]{1,0:T(8,128)} %weight.3, f32[32,32]{1,0:T(8,128)} %point.3, f32[26,32,256]{2,1,0:T(8,128)} %collective-permute-done.1.low, f32[26,32,256]{2,1,0:T(8,128)S(1)} %get-tuple-element.38.own, f32[26,32,256]{2,1,0:T(8,128)} %collective-permute-done.2.high), custom_call_target="tpu_custom_call" | custom-call | flops 40000000000 | bytes 262144 | tf_op jit(solution)/shard_map/middle_sums/pallas_call | solution.py:510
  44.6 0.0 all-to-all-done.1
  44.6 1.4 %collective-permute-start.5 = (f32[128,128]{1,0:T(8,128)S(1)}, f32[128,128]{1,0:T(8,128)S(1)}, u32[]{:S(2)}, u32[]{:S(2)}) collective-permute-start(f32[128,128]{1,0:T(8,128)S(1)} %bitcast.19), channel_id=1, source_target_pairs={{0,1},{1,0},{2,3},{3,2},{4,5},{5,4},{6,7},{7,6},{8,9},{9,8},{10,11... | collective-permute-start | bytes 196616 | tf_op jit(solution)/shard_map/ppermute | solution.py:616
  46.1 2.1 %collective-permute-done.5.second_modes = f32[128,128]{1,0:T(8,128)S(1)} collective-permute-done((f32[128,128]{1,0:T(8,128)S(1)}, f32[128,128]{1,0:T(8,128)S(1)}, u32[]{:S(2)}, u32[]{:S(2)}) %collective-permute-start.5) | collective-permute-done | bytes 65568 | tf_op jit(solution)/shard_map/ppermute | solution.py:616
  48.1 5.6 %inverse_modes.1 = (f32[8,4,64,256]{3,2,1,0:T(8,128)}, f32[8,4,24,256]{3,2,1,0:T(8,128)S(1)}) custom-call(f32[128,128]{1,0:T(8,128)S(1)} %bitcast.20, f32[128,128]{1,0:T(8,128)S(1)} %collective-permute-done.5.second_modes, f32[32]{0:T(128)} %bias.1, bf16[2,128,256]{2,1,0:T(8,128)(2,1)} %constant.32.clone.x_top, bf16[2,128,256]{2,1,0:T(8,128)(2,1)} %constant.33.clone.x_rest, ...), custom_call_target="tpu_custom_call" | custom-call | flops 100000000 | bytes 262144 | tf_op jit(solution)/shard_map/inverse_modes/pallas_call | solution.py:417
  53.8 2.8 %collective-permute-done.6.low = f32[32,24,256]{2,1,0:T(8,128)S(1)} collective-permute-done((f32[32,24,256]{2,1,0:T(8,128)}, f32[32,24,256]{2,1,0:T(8,128)S(1)}, u32[]{:S(2)}, u32[]{:S(2)}) %collective-permute-start.6) | collective-permute-done | bytes 786464 | tf_op jit(solution)/shard_map/ppermute | solution.py:571
  56.6 1.3 %collective-permute-done.7.high = f32[32,24,256]{2,1,0:T(8,128)S(1)} collective-permute-done((f32[32,24,256]{2,1,0:T(8,128)}, f32[32,24,256]{2,1,0:T(8,128)S(1)}, u32[]{:S(2)}, u32[]{:S(2)}) %collective-permute-start.7) | collective-permute-done | bytes 786464 | tf_op jit(solution)/shard_map/ppermute | solution.py:572
  57.8 1.5 %finished_rows.1 = f32[32,64,256]{2,1,0:T(8,128)} custom-call(f32[32,64,256]{2,1,0:T(8,128)} %bitcast.25, f32[32,24,256]{2,1,0:T(8,128)S(1)} %bitcast.16, f32[32,24,256]{2,1,0:T(8,128)S(1)} %collective-permute-done.6.low, f32[32,24,256]{2,1,0:T(8,128)S(1)} %collective-permute-done.7.high), custom_call_target="tpu_custom_call", output_to_operand_aliasing={{}: (0, {})} | custom-call | flops 100000000 | bytes 262144 | tf_op jit(solution)/shard_map/finished_rows/pallas_call | solution.py:443
Async XLA Ops:
  1.6 22.8 %collective-permute-start.1 = (f32[26,32,256]{2,1,0:T(8,128)S(1)}, f32[26,32,256]{2,1,0:T(8,128)}, u32[]{:S(2)}, u32[]{:S(2)}) collective-permute-start(f32[26,32,256]{2,1,0:T(8,128)S(1)} %get-tuple-element.38.own), channel_id=1, source_target_pairs={{0,2},{2,4},{4,6},{6,8},{8,10},{10,12},{12,14},{14,16},{16,18},{18... | collective-permute-start | bytes 2555912 | tf_op jit(solution)/shard_map/ppermute | solution.py:571
  4.3 22.7 %collective-permute-start.2 = (f32[26,32,256]{2,1,0:T(8,128)S(1)}, f32[26,32,256]{2,1,0:T(8,128)}, u32[]{:S(2)}, u32[]{:S(2)}) collective-permute-start(f32[26,32,256]{2,1,0:T(8,128)S(1)} %get-tuple-element.38.own), channel_id=1, source_target_pairs={{0,30},{2,0},{4,2},{6,4},{8,6},{10,8},{12,10},{14,12},{16,14},{18,... | collective-permute-start | bytes 2555912 | tf_op jit(solution)/shard_map/ppermute | solution.py:572
  4.3 5.4 %collective-permute-start = (f32[2,32,256]{2,1,0:T(8,128)S(1)}, f32[2,32,256]{2,1,0:T(8,128)S(1)}, u32[]{:S(2)}, u32[]{:S(2)}) collective-permute-start(f32[2,32,256]{2,1,0:T(8,128)S(1)} %get-tuple-element.29), channel_id=1, source_target_pairs={{0,1},{1,0},{2,3},{3,2},{4,5},{5,4},{6,7},{7,6},{8,9},{9,8},{10,11... | collective-permute-start | bytes 196616 | tf_op jit(solution)/shard_map/ppermute | solution.py:585
  9.6 17.8 %all-to-all-start = ((f32[32,8,128]{2,1,0:T(8,128)}), f32[32,8,128]{2,1,0:T(8,128)S(1)}, u32[]{:S(2)}, u32[]{:S(2)}) async-start(f32[32,8,128]{2,1,0:T(8,128)} %bitcast.28), calls=%async_computation | async-start | bytes 262144 | tf_op jit(solution)/shard_map/all_to_all | solution.py:602
  27.0 12.4 %collective-permute-start.3 = (f32[32,16,256]{2,1,0:T(8,128)}, f32[32,16,256]{2,1,0:T(8,128)S(1)}, u32[]{:S(2)}, u32[]{:S(2)}) collective-permute-start(f32[32,16,256]{2,1,0:T(8,128)} %get-tuple-element.36), channel_id=1, source_target_pairs={{0,2},{2,4},{4,6},{6,8},{8,10},{10,12},{12,14},{14,16},{16,18},{18... | collective-permute-start | bytes 1572872 | tf_op jit(solution)/shard_map/ppermute | solution.py:571
  27.0 13.0 %collective-permute-start.4 = (f32[32,16,256]{2,1,0:T(8,128)}, f32[32,16,256]{2,1,0:T(8,128)S(1)}, u32[]{:S(2)}, u32[]{:S(2)}) collective-permute-start(f32[32,16,256]{2,1,0:T(8,128)} %get-tuple-element.37), channel_id=1, source_target_pairs={{0,30},{2,0},{4,2},{6,4},{8,6},{10,8},{12,10},{14,12},{16,14},{18,... | collective-permute-start | bytes 1572872 | tf_op jit(solution)/shard_map/ppermute | solution.py:572
  29.9 14.7 %all-to-all-start.1 = ((f32[16,8,128]{2,1,0:T(8,128)}), f32[16,8,128]{2,1,0:T(8,128)S(1)}, u32[]{:S(2)}, u32[]{:S(2)}) async-start(f32[16,8,128]{2,1,0:T(8,128)} %bitcast.30), calls=%async_computation.1 | async-start | bytes 131072 | tf_op jit(solution)/shard_map/all_to_all | solution.py:607
  35.9 20.7 %collective-permute-start.6 = (f32[32,24,256]{2,1,0:T(8,128)}, f32[32,24,256]{2,1,0:T(8,128)S(1)}, u32[]{:S(2)}, u32[]{:S(2)}) collective-permute-start(f32[32,24,256]{2,1,0:T(8,128)} %get-tuple-element.46), channel_id=1, source_target_pairs={{0,2},{2,4},{4,6},{6,8},{8,10},{10,12},{12,14},{14,16},{16,18},{18... | collective-permute-start | bytes 2359304 | tf_op jit(solution)/shard_map/ppermute | solution.py:571
  37.5 20.3 %collective-permute-start.7 = (f32[32,24,256]{2,1,0:T(8,128)}, f32[32,24,256]{2,1,0:T(8,128)S(1)}, u32[]{:S(2)}, u32[]{:S(2)}) collective-permute-start(f32[32,24,256]{2,1,0:T(8,128)} %get-tuple-element.48), channel_id=1, source_target_pairs={{0,30},{2,0},{4,2},{6,4},{8,6},{10,8},{12,10},{14,12},{16,14},{18,... | collective-permute-start | bytes 2359304 | tf_op jit(solution)/shard_map/ppermute | solution.py:572
  44.6 3.5 %collective-permute-start.5 = (f32[128,128]{1,0:T(8,128)S(1)}, f32[128,128]{1,0:T(8,128)S(1)}, u32[]{:S(2)}, u32[]{:S(2)}) collective-permute-start(f32[128,128]{1,0:T(8,128)S(1)} %bitcast.19), channel_id=1, source_target_pairs={{0,1},{1,0},{2,3},{3,2},{4,5},{5,4},{6,7},{7,6},{8,9},{9,8},{10,11... | collective-permute-start | bytes 196616 | tf_op jit(solution)/shard_map/ppermute | solution.py:616

commit v24 on v23

--- a/solution.py
+++ b/solution.py
@@ -296,15 +296,21 @@
         copy.wait()
 
 
+ERFC = (
+    0.17087277, -0.82215223, 1.48851587, -1.13520398, 0.27886807,
+    -0.18628806, 0.09678418, 0.37409196, 1.00002368, -1.26551223 - math.log(2.0),
+)
+
+
 def gelu(value):
     size = jnp.abs(value) * math.sqrt(0.5)
-    below = 1.0 + 0.3275911 * size
+    below = 1.0 + 0.5 * size
     t = pl.reciprocal(below, approx=True)
     t = t * (2.0 - below * t)
-    series = 1.061405429 * t - 1.453152027
-    for factor in (1.421413741, -0.284496736, 0.254829592):
+    series = ERFC[0] * t + ERFC[1]
+    for factor in ERFC[2:]:
         series = series * t + factor
-    tail = 0.5 * (series * t) * jnp.exp(-(size * size))
+    tail = t * jnp.exp(series - size * size)
     return value * jnp.where(value < 0.0, tail, 1.0 - tail)
 
 

time: 59.8 us -> 60 us (level)
  transfers between devices with their start and end apart: 10 -> 10, of which waited for: 7 -> 7; matrix products, arithmetic and copies ran while one was open for 0% -> 0% of each run, Pallas kernels for 40% -> 41%
where the time goes in v24:
time: 60 us; the launch traced here: 59.5 us
  Pallas kernels  27.6 us (46%)
  starting transfers between devices  19.2 us (32%)
  waiting for transfers between devices  12.7 us (21%)
    pallas_call x1, Pallas kernels, own_call(): pl.pallas_call(functools.partial(own_kernel, segments, groups), out_shape...  7.13 us
    ppermute x3, waiting for transfers between devices, to_neighbours(): lax.ppermute(down, 'gz', ring('gz', gz, 1))  6.19 us
    all_to_all x1, starting transfers between devices, body(): back = lax.all_to_all(mark, 'gz', split_axis=0, concat_axis=0, tiled=True)  5.96 us
    pallas_call x1, Pallas kernels, inverse_call(): pl.pallas_call(functools.partial(inverse_kernel, upper, halved), out_shap...  5.93 us
    all_to_all x1, starting transfers between devices, body(): got = lax.all_to_all(coarse, both, split_axis=0, concat_axis=0, tiled=True)  5.79 us
    pallas_call x1, Pallas kernels, middle_call(): pl.pallas_call(middle_kernel, out_shape=pltpu.HBM((CH, rows, NX), F32), i...  4.66 us
    ppermute x3, waiting for transfers between devices, to_neighbours(): lax.ppermute(up, 'gz', ring('gz', gz, -1))  4.41 us
    ppermute x3, starting transfers between devices, to_neighbours(): lax.ppermute(down, 'gz', ring('gz', gz, 1))  4.32 us
  transfers between devices with their start and end apart: 10, of which 7 were waited for; matrix products, arithmetic and copies ran while one was open for 0% of the time, Pallas kernels for 41%

profile of v24, /device:TPU:1, one launch (start us, length us, event | category | flops | bytes accessed | tf_op | source)
XLA Modules:
  0.0 59.5 jit_solution(14155638689568781261)
XLA Ops:
  0.0 1.6 %packed_rows.1 = (f32[26,32,256]{2,1,0:T(8,128)S(1)}, f32[2,32,256]{2,1,0:T(8,128)S(1)}) custom-call(f32[32,64,256]{2,1,0:T(8,128)} %bitcast.22), custom_call_target="tpu_custom_call" | custom-call | flops 100000000 | bytes 262144 | tf_op jit(solution)/shard_map/packed_rows/pallas_call | solution.py:469
  1.6 2.7 %collective-permute-start.1 = (f32[26,32,256]{2,1,0:T(8,128)S(1)}, f32[26,32,256]{2,1,0:T(8,128)}, u32[]{:S(2)}, u32[]{:S(2)}) collective-permute-start(f32[26,32,256]{2,1,0:T(8,128)S(1)} %get-tuple-element.38.own), channel_id=1, source_target_pairs={{0,2},{2,4},{4,6},{6,8},{8,10},{10,12},{12,14},{14,16},{16,18},{18... | collective-permute-start | bytes 2555912 | tf_op jit(solution)/shard_map/ppermute | solution.py:577
  4.3 0.0 collective-permute-start.2
  4.3 1.2 %collective-permute-start = (f32[2,32,256]{2,1,0:T(8,128)S(1)}, f32[2,32,256]{2,1,0:T(8,128)S(1)}, u32[]{:S(2)}, u32[]{:S(2)}) collective-permute-start(f32[2,32,256]{2,1,0:T(8,128)S(1)} %get-tuple-element.29), channel_id=1, source_target_pairs={{0,1},{1,0},{2,3},{3,2},{4,5},{5,4},{6,7},{7,6},{8,9},{9,8},{10,11... | collective-permute-start | bytes 196616 | tf_op jit(solution)/shard_map/ppermute | solution.py:591
  5.5 4.1 %forward_modes.1 = f32[256,128]{1,0:T(8,128)} custom-call(f32[8,4,64,256]{3,2,1,0:T(8,128)} %bitcast.23, bf16[2,256,128]{2,1,0:T(8,128)(2,1)} %constant.24.clone.x_top, bf16[2,256,128]{2,1,0:T(8,128)(2,1)} %constant.25.clone.x_rest, bf16[2,32,64]{2,1,0:T(8,128)(2,1)} %constant.26.clone.y_top, bf16[2,32,64]{2,1,0:T(8,128)(2,1)} %constant.27.clone.y_rest), custom_call_target="tpu_custom_call" | custom-call | flops 100000000 | bytes 262144 | tf_op jit(solution)/shard_map/forward_modes/pallas_call | solution.py:390
  9.6 0.0 collective-permute-done.halo
  9.6 5.8 %all-to-all-start = ((f32[32,8,128]{2,1,0:T(8,128)}), f32[32,8,128]{2,1,0:T(8,128)S(1)}, u32[]{:S(2)}, u32[]{:S(2)}) async-start(f32[32,8,128]{2,1,0:T(8,128)} %bitcast.28), calls=%async_computation | async-start | bytes 262144 | tf_op jit(solution)/shard_map/all_to_all | solution.py:608
  15.4 7.1 %own_sums.1 = (f32[32,16,256]{2,1,0:T(8,128)}, f32[32,16,256]{2,1,0:T(8,128)}, f32[32,16,256]{2,1,0:T(8,128)}, f32[32,24,256]{2,1,0:T(8,128)}, f32[32,24,256]{2,1,0:T(8,128)}, /*index=5*/f32[32,24,256]{2,1,0:T(8,128)}) custom-call(f32[32,27]{1,0:T(8,128)} %weight.3, f32[32,32]{1,0:T(8,128)} %point.3, f32[32,64,256]{2,1,0:T(8,128)} %bitcast.24, ...), custom_call_target="tpu_custom_call" | custom-call | flops 100000000 | bytes 262144 | tf_op jit(solution)/shard_map/own_sums/pallas_call | solution.py:489
  22.6 1.8 %collective-permute-done.1.low = f32[26,32,256]{2,1,0:T(8,128)} collective-permute-done((f32[26,32,256]{2,1,0:T(8,128)S(1)}, f32[26,32,256]{2,1,0:T(8,128)}, u32[]{:S(2)}, u32[]{:S(2)}) %collective-permute-start.1) | collective-permute-done | bytes 852000 | tf_op jit(solution)/shard_map/ppermute | solution.py:577
  24.4 2.6 %collective-permute-done.2.high = f32[26,32,256]{2,1,0:T(8,128)} collective-permute-done((f32[26,32,256]{2,1,0:T(8,128)S(1)}, f32[26,32,256]{2,1,0:T(8,128)}, u32[]{:S(2)}, u32[]{:S(2)}) %collective-permute-start.2) | collective-permute-done | bytes 852000 | tf_op jit(solution)/shard_map/ppermute | solution.py:578
  27.0 0.0 collective-permute-start.3
  27.0 0.5 collective-permute-start.4
  27.5 0.0 all-to-all-done
  27.5 2.4 %filter_modes.1 = f32[128,128]{1,0:T(8,128)} custom-call(f32[256,128]{1,0:T(8,128)S(1)} %bitcast.21, f32[2,16,8,64]{3,2,1,0:T(8,128)} %gains, bf16[256,256]{1,0:T(8,128)(2,1)} %constant.28.clone.f_top, bf16[256,256]{1,0:T(8,128)(2,1)} %constant.29.clone.f_rest, bf16[256,128]{1,0:T(8,128)(2,1)} %constant.30.clone.i_top, bf16[256,128]{1,0:T(8,128)(2,1)} %constant.31.clone.i_rest), custom_call_target="tpu_custom_call" | custom-call | flops 40000000000 | bytes 262144 | tf_op jit(solution)/shard_map/filter_modes/pallas_call | solution.py:409
  29.9 6.0 %all-to-all-start.1 = ((f32[16,8,128]{2,1,0:T(8,128)}), f32[16,8,128]{2,1,0:T(8,128)S(1)}, u32[]{:S(2)}, u32[]{:S(2)}) async-start(f32[16,8,128]{2,1,0:T(8,128)} %bitcast.30), calls=%async_computation.1 | async-start | bytes 131072 | tf_op jit(solution)/shard_map/all_to_all | solution.py:613
  35.9 1.6 %collective-permute-start.6 = (f32[32,24,256]{2,1,0:T(8,128)}, f32[32,24,256]{2,1,0:T(8,128)S(1)}, u32[]{:S(2)}, u32[]{:S(2)}) collective-permute-start(f32[32,24,256]{2,1,0:T(8,128)} %get-tuple-element.46), channel_id=1, source_target_pairs={{0,2},{2,4},{4,6},{6,8},{8,10},{10,12},{12,14},{14,16},{16,18},{18... | collective-permute-start | bytes 2359304 | tf_op jit(solution)/shard_map/ppermute | solution.py:577
  37.5 0.0 collective-permute-start.7
  37.5 1.9 %collective-permute-done.3 = f32[32,16,256]{2,1,0:T(8,128)S(1)} collective-permute-done((f32[32,16,256]{2,1,0:T(8,128)}, f32[32,16,256]{2,1,0:T(8,128)S(1)}, u32[]{:S(2)}, u32[]{:S(2)}) %collective-permute-start.3) | collective-permute-done | bytes 524320 | tf_op jit(solution)/shard_map/ppermute | solution.py:577
  39.4 0.6 collective-permute-done.4
  40.0 4.7 %middle_sums.1 = f32[32,24,256]{2,1,0:T(8,128)} custom-call(f32[32,27]{1,0:T(8,128)} %weight.3, f32[32,32]{1,0:T(8,128)} %point.3, f32[26,32,256]{2,1,0:T(8,128)} %collective-permute-done.1.low, f32[26,32,256]{2,1,0:T(8,128)S(1)} %get-tuple-element.38.own, f32[26,32,256]{2,1,0:T(8,128)} %collective-permute-done.2.high), custom_call_target="tpu_custom_call" | custom-call | flops 40000000000 | bytes 262144 | tf_op jit(solution)/shard_map/middle_sums/pallas_call | solution.py:516
  44.6 0.0 all-to-all-done.1
  44.6 1.4 %collective-permute-start.5 = (f32[128,128]{1,0:T(8,128)S(1)}, f32[128,128]{1,0:T(8,128)S(1)}, u32[]{:S(2)}, u32[]{:S(2)}) collective-permute-start(f32[128,128]{1,0:T(8,128)S(1)} %bitcast.19), channel_id=1, source_target_pairs={{0,1},{1,0},{2,3},{3,2},{4,5},{5,4},{6,7},{7,6},{8,9},{9,8},{10,11... | collective-permute-start | bytes 196616 | tf_op jit(solution)/shard_map/ppermute | solution.py:622
  46.1 2.1 %collective-permute-done.5.second_modes = f32[128,128]{1,0:T(8,128)S(1)} collective-permute-done((f32[128,128]{1,0:T(8,128)S(1)}, f32[128,128]{1,0:T(8,128)S(1)}, u32[]{:S(2)}, u32[]{:S(2)}) %collective-permute-start.5) | collective-permute-done | bytes 65568 | tf_op jit(solution)/shard_map/ppermute | solution.py:622
  48.1 5.9 %inverse_modes.1 = (f32[8,4,64,256]{3,2,1,0:T(8,128)}, f32[8,4,24,256]{3,2,1,0:T(8,128)S(1)}) custom-call(f32[128,128]{1,0:T(8,128)S(1)} %bitcast.20, f32[128,128]{1,0:T(8,128)S(1)} %collective-permute-done.5.second_modes, f32[32]{0:T(128)} %bias.1, bf16[2,128,256]{2,1,0:T(8,128)(2,1)} %constant.32.clone.x_top, bf16[2,128,256]{2,1,0:T(8,128)(2,1)} %constant.33.clone.x_rest, ...), custom_call_target="tpu_custom_call" | custom-call | flops 100000000 | bytes 262144 | tf_op jit(solution)/shard_map/inverse_modes/pallas_call | solution.py:423
  54.1 2.5 %collective-permute-done.6.low = f32[32,24,256]{2,1,0:T(8,128)S(1)} collective-permute-done((f32[32,24,256]{2,1,0:T(8,128)}, f32[32,24,256]{2,1,0:T(8,128)S(1)}, u32[]{:S(2)}, u32[]{:S(2)}) %collective-permute-start.6) | collective-permute-done | bytes 786464 | tf_op jit(solution)/shard_map/ppermute | solution.py:577
  56.6 1.3 %collective-permute-done.7.high = f32[32,24,256]{2,1,0:T(8,128)S(1)} collective-permute-done((f32[32,24,256]{2,1,0:T(8,128)}, f32[32,24,256]{2,1,0:T(8,128)S(1)}, u32[]{:S(2)}, u32[]{:S(2)}) %collective-permute-start.7) | collective-permute-done | bytes 786464 | tf_op jit(solution)/shard_map/ppermute | solution.py:578
  57.8 1.7 %finished_rows.1 = f32[32,64,256]{2,1,0:T(8,128)} custom-call(f32[32,64,256]{2,1,0:T(8,128)} %bitcast.25, f32[32,24,256]{2,1,0:T(8,128)S(1)} %bitcast.16, f32[32,24,256]{2,1,0:T(8,128)S(1)} %collective-permute-done.6.low, f32[32,24,256]{2,1,0:T(8,128)S(1)} %collective-permute-done.7.high), custom_call_target="tpu_custom_call", output_to_operand_aliasing={{}: (0, {})} | custom-call | flops 100000000 | bytes 262144 | tf_op jit(solution)/shard_map/finished_rows/pallas_call | solution.py:449
Async XLA Ops:
  1.6 22.8 %collective-permute-start.1 = (f32[26,32,256]{2,1,0:T(8,128)S(1)}, f32[26,32,256]{2,1,0:T(8,128)}, u32[]{:S(2)}, u32[]{:S(2)}) collective-permute-start(f32[26,32,256]{2,1,0:T(8,128)S(1)} %get-tuple-element.38.own), channel_id=1, source_target_pairs={{0,2},{2,4},{4,6},{6,8},{8,10},{10,12},{12,14},{14,16},{16,18},{18... | collective-permute-start | bytes 2555912 | tf_op jit(solution)/shard_map/ppermute | solution.py:577
  4.3 22.7 %collective-permute-start.2 = (f32[26,32,256]{2,1,0:T(8,128)S(1)}, f32[26,32,256]{2,1,0:T(8,128)}, u32[]{:S(2)}, u32[]{:S(2)}) collective-permute-start(f32[26,32,256]{2,1,0:T(8,128)S(1)} %get-tuple-element.38.own), channel_id=1, source_target_pairs={{0,30},{2,0},{4,2},{6,4},{8,6},{10,8},{12,10},{14,12},{16,14},{18,... | collective-permute-start | bytes 2555912 | tf_op jit(solution)/shard_map/ppermute | solution.py:578
  4.3 5.4 %collective-permute-start = (f32[2,32,256]{2,1,0:T(8,128)S(1)}, f32[2,32,256]{2,1,0:T(8,128)S(1)}, u32[]{:S(2)}, u32[]{:S(2)}) collective-permute-start(f32[2,32,256]{2,1,0:T(8,128)S(1)} %get-tuple-element.29), channel_id=1, source_target_pairs={{0,1},{1,0},{2,3},{3,2},{4,5},{5,4},{6,7},{7,6},{8,9},{9,8},{10,11... | collective-permute-start | bytes 196616 | tf_op jit(solution)/shard_map/ppermute | solution.py:591
  9.6 17.8 %all-to-all-start = ((f32[32,8,128]{2,1,0:T(8,128)}), f32[32,8,128]{2,1,0:T(8,128)S(1)}, u32[]{:S(2)}, u32[]{:S(2)}) async-start(f32[32,8,128]{2,1,0:T(8,128)} %bitcast.28), calls=%async_computation | async-start | bytes 262144 | tf_op jit(solution)/shard_map/all_to_all | solution.py:608
  27.0 12.4 %collective-permute-start.3 = (f32[32,16,256]{2,1,0:T(8,128)}, f32[32,16,256]{2,1,0:T(8,128)S(1)}, u32[]{:S(2)}, u32[]{:S(2)}) collective-permute-start(f32[32,16,256]{2,1,0:T(8,128)} %get-tuple-element.36), channel_id=1, source_target_pairs={{0,2},{2,4},{4,6},{6,8},{8,10},{10,12},{12,14},{14,16},{16,18},{18... | collective-permute-start | bytes 1572872 | tf_op jit(solution)/shard_map/ppermute | solution.py:577
  27.0 13.0 %collective-permute-start.4 = (f32[32,16,256]{2,1,0:T(8,128)}, f32[32,16,256]{2,1,0:T(8,128)S(1)}, u32[]{:S(2)}, u32[]{:S(2)}) collective-permute-start(f32[32,16,256]{2,1,0:T(8,128)} %get-tuple-element.37), channel_id=1, source_target_pairs={{0,30},{2,0},{4,2},{6,4},{8,6},{10,8},{12,10},{14,12},{16,14},{18,... | collective-permute-start | bytes 1572872 | tf_op jit(solution)/shard_map/ppermute | solution.py:578
  29.9 14.7 %all-to-all-start.1 = ((f32[16,8,128]{2,1,0:T(8,128)}), f32[16,8,128]{2,1,0:T(8,128)S(1)}, u32[]{:S(2)}, u32[]{:S(2)}) async-start(f32[16,8,128]{2,1,0:T(8,128)} %bitcast.30), calls=%async_computation.1 | async-start | bytes 131072 | tf_op jit(solution)/shard_map/all_to_all | solution.py:613
  35.9 20.7 %collective-permute-start.6 = (f32[32,24,256]{2,1,0:T(8,128)}, f32[32,24,256]{2,1,0:T(8,128)S(1)}, u32[]{:S(2)}, u32[]{:S(2)}) collective-permute-start(f32[32,24,256]{2,1,0:T(8,128)} %get-tuple-element.46), channel_id=1, source_target_pairs={{0,2},{2,4},{4,6},{6,8},{8,10},{10,12},{12,14},{14,16},{16,18},{18... | collective-permute-start | bytes 2359304 | tf_op jit(solution)/shard_map/ppermute | solution.py:577
  37.5 20.3 %collective-permute-start.7 = (f32[32,24,256]{2,1,0:T(8,128)}, f32[32,24,256]{2,1,0:T(8,128)S(1)}, u32[]{:S(2)}, u32[]{:S(2)}) collective-permute-start(f32[32,24,256]{2,1,0:T(8,128)} %get-tuple-element.48), channel_id=1, source_target_pairs={{0,30},{2,0},{4,2},{6,4},{8,6},{10,8},{12,10},{14,12},{16,14},{18,... | collective-permute-start | bytes 2359304 | tf_op jit(solution)/shard_map/ppermute | solution.py:578
  44.6 3.5 %collective-permute-start.5 = (f32[128,128]{1,0:T(8,128)S(1)}, f32[128,128]{1,0:T(8,128)S(1)}, u32[]{:S(2)}, u32[]{:S(2)}) collective-permute-start(f32[128,128]{1,0:T(8,128)S(1)} %bitcast.19), channel_id=1, source_target_pairs={{0,1},{1,0},{2,3},{3,2},{4,5},{5,4},{6,7},{7,6},{8,9},{9,8},{10,11... | collective-permute-start | bytes 196616 | tf_op jit(solution)/shard_map/ppermute | solution.py:622

commit v25 on v24

--- a/solution.py
+++ b/solution.py
@@ -606,8 +606,7 @@
     if whole_tiles:
         both = ("gz", "gy")
         got = lax.all_to_all(coarse, both, split_axis=0, concat_axis=0, tiled=True)
-        down, up = lax.optimization_barrier((down, up, first_low))[:2]
-        pair = to_neighbours(down, up)
+        pair = to_neighbours(after(down, first_low), after(up, first_high))
         gains = after(spectral_filter, first_low, first_high, second)
         mark = filter_call(got, gains, gz, gy, forward_scale)
         back = lax.all_to_all(mark, "gz", split_axis=0, concat_axis=0, tiled=True)

time: 60 us -> 66.5 us (1.11)
  waiting for transfers between devices: 12.7 us -> 19.7 us
    ppermute x3, waiting for transfers between devices: 4.41 us -> 16 us  [to_neighbours(): lax.ppermute(up, 'gz', ring('gz', gz, -1))]
    ppermute x3, waiting for transfers between devices: 6.19 us -> 1.8 us  [to_neighbours(): lax.ppermute(down, 'gz', ring('gz', gz, 1))]
    ppermute x3, starting transfers between devices: 4.32 us -> 6.06 us  [to_neighbours(): lax.ppermute(down, 'gz', ring('gz', gz, 1))]
    all_to_all x1, starting transfers between devices: 5.96 us -> 4.4 us  [body(): back = lax.all_to_all(mark, 'gz', split_axis=0, concat_axis=0, tiled=True)]
  transfers between devices with their start and end apart: 10 -> 10, of which waited for: 7 -> 4; matrix products, arithmetic and copies ran while one was open for 0% -> 0% of each run, Pallas kernels for 41% -> 37%
where the time goes in v25:
time: 66.5 us; the launch traced here: 66.1 us
  Pallas kernels  27.6 us (42%)
  waiting for transfers between devices  19.7 us (30%)
  starting transfers between devices  18.7 us (28%)
    ppermute x3, waiting for transfers between devices, to_neighbours(): lax.ppermute(up, 'gz', ring('gz', gz, -1))  16 us
    pallas_call x1, Pallas kernels, own_call(): pl.pallas_call(functools.partial(own_kernel, segments, groups), out_shape...  7.13 us
    ppermute x3, starting transfers between devices, to_neighbours(): lax.ppermute(down, 'gz', ring('gz', gz, 1))  6.06 us
    pallas_call x1, Pallas kernels, inverse_call(): pl.pallas_call(functools.partial(inverse_kernel, upper, halved), out_shap...  5.93 us
    all_to_all x1, starting transfers between devices, body(): got = lax.all_to_all(coarse, both, split_axis=0, concat_axis=0, tiled=True)  5.79 us
    pallas_call x1, Pallas kernels, middle_call(): pl.pallas_call(middle_kernel, out_shape=pltpu.HBM((CH, rows, NX), F32), i...  4.67 us
    all_to_all x1, starting transfers between devices, body(): back = lax.all_to_all(mark, 'gz', split_axis=0, concat_axis=0, tiled=True)  4.4 us
    pallas_call x1, Pallas kernels, forward_call(): pl.pallas_call(forward_kernel, out_shape=(pltpu.HBM if pinned else jax.Sh...  4.13 us
  transfers between devices with their start and end apart: 10, of which 4 were waited for; matrix products, arithmetic and copies ran while one was open for 0% of the time, Pallas kernels for 37%

profile of v25, /device:TPU:1, one launch (start us, length us, event | category | flops | bytes accessed | tf_op | source)
XLA Modules:
  0.0 66.1 jit_solution(13655728427376619577)
XLA Ops:
  0.0 1.6 %packed_rows.1 = (f32[26,32,256]{2,1,0:T(8,128)S(1)}, f32[2,32,256]{2,1,0:T(8,128)S(1)}) custom-call(f32[32,64,256]{2,1,0:T(8,128)} %bitcast.22), custom_call_target="tpu_custom_call" | custom-call | flops 100000000 | bytes 262144 | tf_op jit(solution)/shard_map/packed_rows/pallas_call | solution.py:469
  1.6 2.7 %collective-permute-start.1 = (f32[26,32,256]{2,1,0:T(8,128)S(1)}, f32[26,32,256]{2,1,0:T(8,128)}, u32[]{:S(2)}, u32[]{:S(2)}) collective-permute-start(f32[26,32,256]{2,1,0:T(8,128)S(1)} %get-tuple-element.38.own), channel_id=1, source_target_pairs={{0,2},{2,4},{4,6},{6,8},{8,10},{10,12},{12,14},{14,16},{16,18},{18... | collective-permute-start | bytes 2555912 | tf_op jit(solution)/shard_map/ppermute | solution.py:577
  4.3 0.0 collective-permute-start.2
  4.3 1.2 %collective-permute-start = (f32[2,32,256]{2,1,0:T(8,128)S(1)}, f32[2,32,256]{2,1,0:T(8,128)S(1)}, u32[]{:S(2)}, u32[]{:S(2)}) collective-permute-start(f32[2,32,256]{2,1,0:T(8,128)S(1)} %get-tuple-element.29), channel_id=1, source_target_pairs={{0,1},{1,0},{2,3},{3,2},{4,5},{5,4},{6,7},{7,6},{8,9},{9,8},{10,11... | collective-permute-start | bytes 196616 | tf_op jit(solution)/shard_map/ppermute | solution.py:591
  5.5 4.1 %forward_modes.1 = f32[256,128]{1,0:T(8,128)} custom-call(f32[8,4,64,256]{3,2,1,0:T(8,128)} %bitcast.23, bf16[2,256,128]{2,1,0:T(8,128)(2,1)} %constant.24.clone.x_top, bf16[2,256,128]{2,1,0:T(8,128)(2,1)} %constant.25.clone.x_rest, bf16[2,32,64]{2,1,0:T(8,128)(2,1)} %constant.26.clone.y_top, bf16[2,32,64]{2,1,0:T(8,128)(2,1)} %constant.27.clone.y_rest), custom_call_target="tpu_custom_call" | custom-call | flops 100000000 | bytes 262144 | tf_op jit(solution)/shard_map/forward_modes/pallas_call | solution.py:390
  9.6 0.0 collective-permute-done.halo
  9.6 5.8 %all-to-all-start = ((f32[32,8,128]{2,1,0:T(8,128)}), f32[32,8,128]{2,1,0:T(8,128)S(1)}, u32[]{:S(2)}, u32[]{:S(2)}) async-start(f32[32,8,128]{2,1,0:T(8,128)} %bitcast.28), calls=%async_computation | async-start | bytes 262144 | tf_op jit(solution)/shard_map/all_to_all | solution.py:608
  15.4 7.1 %own_sums.1 = (f32[32,16,256]{2,1,0:T(8,128)}, f32[32,16,256]{2,1,0:T(8,128)}, f32[32,16,256]{2,1,0:T(8,128)}, f32[32,24,256]{2,1,0:T(8,128)}, f32[32,24,256]{2,1,0:T(8,128)}, /*index=5*/f32[32,24,256]{2,1,0:T(8,128)}) custom-call(f32[32,27]{1,0:T(8,128)} %weight.3, f32[32,32]{1,0:T(8,128)} %point.3, f32[32,64,256]{2,1,0:T(8,128)} %bitcast.24, ...), custom_call_target="tpu_custom_call" | custom-call | flops 100000000 | bytes 262144 | tf_op jit(solution)/shard_map/own_sums/pallas_call | solution.py:489
  22.6 1.8 %collective-permute-done.1.low = f32[26,32,256]{2,1,0:T(8,128)} collective-permute-done((f32[26,32,256]{2,1,0:T(8,128)S(1)}, f32[26,32,256]{2,1,0:T(8,128)}, u32[]{:S(2)}, u32[]{:S(2)}) %collective-permute-start.1) | collective-permute-done | bytes 852000 | tf_op jit(solution)/shard_map/ppermute | solution.py:577
  24.4 2.6 %collective-permute-done.2.high = f32[26,32,256]{2,1,0:T(8,128)} collective-permute-done((f32[26,32,256]{2,1,0:T(8,128)S(1)}, f32[26,32,256]{2,1,0:T(8,128)}, u32[]{:S(2)}, u32[]{:S(2)}) %collective-permute-start.2) | collective-permute-done | bytes 852000 | tf_op jit(solution)/shard_map/ppermute | solution.py:578
  27.0 0.0 collective-permute-start.4
  27.0 1.7 %collective-permute-start.3 = (f32[32,16,256]{2,1,0:T(8,128)}, f32[32,16,256]{2,1,0:T(8,128)S(1)}, u32[]{:S(2)}, u32[]{:S(2)}) collective-permute-start(f32[32,16,256]{2,1,0:T(8,128)} %get-tuple-element.35), channel_id=1, source_target_pairs={{0,2},{2,4},{4,6},{6,8},{8,10},{10,12},{12,14},{14,16},{16,18},{18... | collective-permute-start | bytes 1572872 | tf_op jit(solution)/shard_map/ppermute | solution.py:577
  28.7 0.0 all-to-all-done
  28.7 2.4 %filter_modes.1 = f32[128,128]{1,0:T(8,128)} custom-call(f32[256,128]{1,0:T(8,128)S(1)} %bitcast.21, f32[2,16,8,64]{3,2,1,0:T(8,128)} %gains, bf16[256,256]{1,0:T(8,128)(2,1)} %constant.28.clone.f_top, bf16[256,256]{1,0:T(8,128)(2,1)} %constant.29.clone.f_rest, bf16[256,128]{1,0:T(8,128)(2,1)} %constant.30.clone.i_top, bf16[256,128]{1,0:T(8,128)(2,1)} %constant.31.clone.i_rest), custom_call_target="tpu_custom_call" | custom-call | flops 40000000000 | bytes 262144 | tf_op jit(solution)/shard_map/filter_modes/pallas_call | solution.py:409
  31.2 4.4 %all-to-all-start.1 = ((f32[16,8,128]{2,1,0:T(8,128)}), f32[16,8,128]{2,1,0:T(8,128)S(1)}, u32[]{:S(2)}, u32[]{:S(2)}) async-start(f32[16,8,128]{2,1,0:T(8,128)} %bitcast.30), calls=%async_computation.1 | async-start | bytes 131072 | tf_op jit(solution)/shard_map/all_to_all | solution.py:612
  35.5 1.6 %collective-permute-start.6 = (f32[32,24,256]{2,1,0:T(8,128)}, f32[32,24,256]{2,1,0:T(8,128)S(1)}, u32[]{:S(2)}, u32[]{:S(2)}) collective-permute-start(f32[32,24,256]{2,1,0:T(8,128)} %get-tuple-element.46), channel_id=1, source_target_pairs={{0,2},{2,4},{4,6},{6,8},{8,10},{10,12},{12,14},{14,16},{16,18},{18... | collective-permute-start | bytes 2359304 | tf_op jit(solution)/shard_map/ppermute | solution.py:577
  37.2 0.0 collective-permute-start.7
  37.2 13.4 %collective-permute-done.4 = f32[32,16,256]{2,1,0:T(8,128)S(1)} collective-permute-done((f32[32,16,256]{2,1,0:T(8,128)}, f32[32,16,256]{2,1,0:T(8,128)S(1)}, u32[]{:S(2)}, u32[]{:S(2)}) %collective-permute-start.4) | collective-permute-done | bytes 524320 | tf_op jit(solution)/shard_map/ppermute | solution.py:578
  50.6 0.0 collective-permute-done.3
  50.6 4.7 %middle_sums.1 = f32[32,24,256]{2,1,0:T(8,128)} custom-call(f32[32,27]{1,0:T(8,128)} %weight.3, f32[32,32]{1,0:T(8,128)} %point.3, f32[26,32,256]{2,1,0:T(8,128)} %collective-permute-done.1.low, f32[26,32,256]{2,1,0:T(8,128)S(1)} %get-tuple-element.38.own, f32[26,32,256]{2,1,0:T(8,128)} %collective-permute-done.2.high), custom_call_target="tpu_custom_call" | custom-call | flops 40000000000 | bytes 262144 | tf_op jit(solution)/shard_map/middle_sums/pallas_call | solution.py:516
  55.2 0.0 all-to-all-done.1
  55.3 1.3 %collective-permute-start.5 = (f32[128,128]{1,0:T(8,128)S(1)}, f32[128,128]{1,0:T(8,128)S(1)}, u32[]{:S(2)}, u32[]{:S(2)}) collective-permute-start(f32[128,128]{1,0:T(8,128)S(1)} %bitcast.19), channel_id=1, source_target_pairs={{0,1},{1,0},{2,3},{3,2},{4,5},{5,4},{6,7},{7,6},{8,9},{9,8},{10,11... | collective-permute-start | bytes 196616 | tf_op jit(solution)/shard_map/ppermute | solution.py:621
  56.5 1.9 %collective-permute-done.5.second_modes = f32[128,128]{1,0:T(8,128)S(1)} collective-permute-done((f32[128,128]{1,0:T(8,128)S(1)}, f32[128,128]{1,0:T(8,128)S(1)}, u32[]{:S(2)}, u32[]{:S(2)}) %collective-permute-start.5) | collective-permute-done | bytes 65568 | tf_op jit(solution)/shard_map/ppermute | solution.py:621
  58.4 5.9 %inverse_modes.1 = (f32[8,4,64,256]{3,2,1,0:T(8,128)}, f32[8,4,24,256]{3,2,1,0:T(8,128)S(1)}) custom-call(f32[128,128]{1,0:T(8,128)S(1)} %bitcast.20, f32[128,128]{1,0:T(8,128)S(1)} %collective-permute-done.5.second_modes, f32[32]{0:T(128)} %bias.1, bf16[2,128,256]{2,1,0:T(8,128)(2,1)} %constant.32.clone.x_top, bf16[2,128,256]{2,1,0:T(8,128)(2,1)} %constant.33.clone.x_rest, ...), custom_call_target="tpu_custom_call" | custom-call | flops 100000000 | bytes 262144 | tf_op jit(solution)/shard_map/inverse_modes/pallas_call | solution.py:423
  64.4 0.0 collective-permute-done.6.low
  64.4 0.0 collective-permute-done.7.high
  64.4 1.7 %finished_rows.1 = f32[32,64,256]{2,1,0:T(8,128)} custom-call(f32[32,64,256]{2,1,0:T(8,128)} %bitcast.25, f32[32,24,256]{2,1,0:T(8,128)S(1)} %bitcast.16, f32[32,24,256]{2,1,0:T(8,128)S(1)} %collective-permute-done.6.low, f32[32,24,256]{2,1,0:T(8,128)S(1)} %collective-permute-done.7.high), custom_call_target="tpu_custom_call", output_to_operand_aliasing={{}: (0, {})} | custom-call | flops 100000000 | bytes 262144 | tf_op jit(solution)/shard_map/finished_rows/pallas_call | solution.py:449
Async XLA Ops:
  1.6 22.8 %collective-permute-start.1 = (f32[26,32,256]{2,1,0:T(8,128)S(1)}, f32[26,32,256]{2,1,0:T(8,128)}, u32[]{:S(2)}, u32[]{:S(2)}) collective-permute-start(f32[26,32,256]{2,1,0:T(8,128)S(1)} %get-tuple-element.38.own), channel_id=1, source_target_pairs={{0,2},{2,4},{4,6},{6,8},{8,10},{10,12},{12,14},{14,16},{16,18},{18... | collective-permute-start | bytes 2555912 | tf_op jit(solution)/shard_map/ppermute | solution.py:577
  4.3 22.7 %collective-permute-start.2 = (f32[26,32,256]{2,1,0:T(8,128)S(1)}, f32[26,32,256]{2,1,0:T(8,128)}, u32[]{:S(2)}, u32[]{:S(2)}) collective-permute-start(f32[26,32,256]{2,1,0:T(8,128)S(1)} %get-tuple-element.38.own), channel_id=1, source_target_pairs={{0,30},{2,0},{4,2},{6,4},{8,6},{10,8},{12,10},{14,12},{16,14},{18,... | collective-permute-start | bytes 2555912 | tf_op jit(solution)/shard_map/ppermute | solution.py:578
  4.3 5.4 %collective-permute-start = (f32[2,32,256]{2,1,0:T(8,128)S(1)}, f32[2,32,256]{2,1,0:T(8,128)S(1)}, u32[]{:S(2)}, u32[]{:S(2)}) collective-permute-start(f32[2,32,256]{2,1,0:T(8,128)S(1)} %get-tuple-element.29), channel_id=1, source_target_pairs={{0,1},{1,0},{2,3},{3,2},{4,5},{5,4},{6,7},{7,6},{8,9},{9,8},{10,11... | collective-permute-start | bytes 196616 | tf_op jit(solution)/shard_map/ppermute | solution.py:591
  9.6 19.1 %all-to-all-start = ((f32[32,8,128]{2,1,0:T(8,128)}), f32[32,8,128]{2,1,0:T(8,128)S(1)}, u32[]{:S(2)}, u32[]{:S(2)}) async-start(f32[32,8,128]{2,1,0:T(8,128)} %bitcast.28), calls=%async_computation | async-start | bytes 262144 | tf_op jit(solution)/shard_map/all_to_all | solution.py:608
  27.0 23.6 %collective-permute-start.4 = (f32[32,16,256]{2,1,0:T(8,128)}, f32[32,16,256]{2,1,0:T(8,128)S(1)}, u32[]{:S(2)}, u32[]{:S(2)}) collective-permute-start(f32[32,16,256]{2,1,0:T(8,128)} %get-tuple-element.37), channel_id=1, source_target_pairs={{0,30},{2,0},{4,2},{6,4},{8,6},{10,8},{12,10},{14,12},{16,14},{18,... | collective-permute-start | bytes 1572872 | tf_op jit(solution)/shard_map/ppermute | solution.py:578
  27.0 23.6 %collective-permute-start.3 = (f32[32,16,256]{2,1,0:T(8,128)}, f32[32,16,256]{2,1,0:T(8,128)S(1)}, u32[]{:S(2)}, u32[]{:S(2)}) collective-permute-start(f32[32,16,256]{2,1,0:T(8,128)} %get-tuple-element.35), channel_id=1, source_target_pairs={{0,2},{2,4},{4,6},{6,8},{8,10},{10,12},{12,14},{14,16},{16,18},{18... | collective-permute-start | bytes 1572872 | tf_op jit(solution)/shard_map/ppermute | solution.py:577
  31.2 24.1 %all-to-all-start.1 = ((f32[16,8,128]{2,1,0:T(8,128)}), f32[16,8,128]{2,1,0:T(8,128)S(1)}, u32[]{:S(2)}, u32[]{:S(2)}) async-start(f32[16,8,128]{2,1,0:T(8,128)} %bitcast.30), calls=%async_computation.1 | async-start | bytes 131072 | tf_op jit(solution)/shard_map/all_to_all | solution.py:612
  35.5 28.8 %collective-permute-start.6 = (f32[32,24,256]{2,1,0:T(8,128)}, f32[32,24,256]{2,1,0:T(8,128)S(1)}, u32[]{:S(2)}, u32[]{:S(2)}) collective-permute-start(f32[32,24,256]{2,1,0:T(8,128)} %get-tuple-element.46), channel_id=1, source_target_pairs={{0,2},{2,4},{4,6},{6,8},{8,10},{10,12},{12,14},{14,16},{16,18},{18... | collective-permute-start | bytes 2359304 | tf_op jit(solution)/shard_map/ppermute | solution.py:577
  37.2 27.2 %collective-permute-start.7 = (f32[32,24,256]{2,1,0:T(8,128)}, f32[32,24,256]{2,1,0:T(8,128)S(1)}, u32[]{:S(2)}, u32[]{:S(2)}) collective-permute-start(f32[32,24,256]{2,1,0:T(8,128)} %get-tuple-element.48), channel_id=1, source_target_pairs={{0,30},{2,0},{4,2},{6,4},{8,6},{10,8},{12,10},{14,12},{16,14},{18,... | collective-permute-start | bytes 2359304 | tf_op jit(solution)/shard_map/ppermute | solution.py:578
  55.3 3.2 %collective-permute-start.5 = (f32[128,128]{1,0:T(8,128)S(1)}, f32[128,128]{1,0:T(8,128)S(1)}, u32[]{:S(2)}, u32[]{:S(2)}) collective-permute-start(f32[128,128]{1,0:T(8,128)S(1)} %bitcast.19), channel_id=1, source_target_pairs={{0,1},{1,0},{2,3},{3,2},{4,5},{5,4},{6,7},{7,6},{8,9},{9,8},{10,11... | collective-permute-start | bytes 196616 | tf_op jit(solution)/shard_map/ppermute | solution.py:621

commit v26 on v24

--- a/solution.py
+++ b/solution.py
@@ -159,9 +159,17 @@
     return row
 
 
-def spread_gains(weights, gains, offsets):
-    for k in [9 * a + j for a in offsets for j in range(9)]:
-        gains[k] = jnp.broadcast_to(weights[:, k : k + 1], (CH, 128))
+def odd_plane():
+    return lax.rem(lax.axis_index("gz"), 2) == 1
+
+
+def spread_gains(weights, gains, swapped):
+    for k in range(27):
+        column = weights[:, k : k + 1]
+        mirror = 18 - 18 * (k // 18) + k % 9
+        if k // 9 != 1:
+            column = jnp.where(swapped, weights[:, mirror : mirror + 1], column)
+        gains[k] = jnp.broadcast_to(column, (CH, 128))
 
 
 def mixing(points):
@@ -246,7 +254,7 @@
     row = fetch_tiles(field, taken, sem_in, wanted)
     for copy in few:
         copy.wait()
-    spread_gains(weights, gains, range(3))
+    spread_gains(weights, gains, jnp.logical_not(odd_plane()))
     mix = mixing(points[...])
     runs, at, done, order = [], 0, 0, []
     for tiles in segments:
@@ -281,7 +289,7 @@
         copy.start()
     for copy in copies[:2]:
         copy.wait()
-    spread_gains(weights, gains, range(3))
+    spread_gains(weights, gains, odd_plane())
     mix = mixing(points[...])
     for copy in copies[2:]:
         copy.wait()
@@ -572,11 +580,10 @@
     def ring(axis, count, by):
         return [(i, (i + by) % count) for i in range(count)]
 
-    def to_neighbours(down, up):
-        return (
-            lax.ppermute(down, "gz", ring("gz", gz, 1)),
-            lax.ppermute(up, "gz", ring("gz", gz, -1)),
-        )
+    def to_neighbours(across, within):
+        odd_on = [(i, (i + 1 if i % 2 else i - 1) % gz) for i in range(gz)]
+        even_on = [(i, (i - 1 if i % 2 else i + 1) % gz) for i in range(gz)]
+        return lax.ppermute(across, "gz", odd_on), lax.ppermute(within, "gz", even_on)
 
     def after(value, *others):
         return lax.optimization_barrier((value, *others))[0]

time: 60 us -> 58.8 us (0.980)
  waiting for transfers between devices: 12.7 us -> 8.36 us
  starting transfers between devices: 19.2 us -> 22.3 us
    ppermute x6, starting transfers between devices: 4.83 us -> 11.8 us  [the longest x3 6.07 us: to_neighbours(): lax.ppermute(across, 'gz', odd_on)]
    ppermute x6, waiting for transfers between devices: 10.6 us -> 5.62 us  [the longest x3 5.61 us: to_neighbours(): lax.ppermute(across, 'gz', odd_on)]
    all_to_all x1, starting transfers between devices: 5.79 us -> 2.47 us  [body(): got = lax.all_to_all(coarse, both, split_axis=0, concat_axis=0, tiled=True)]
    ppermute x1, waiting for transfers between devices: 2.07 us -> 2.73 us  [body(): modes = (back, lax.ppermute(after(back, mixed), 'gy', ring('gy', gy, 1)))]
  transfers between devices with their start and end apart: 10 -> 10, of which waited for: 7 -> 4; matrix products, arithmetic and copies ran while one was open for 0% -> 0% of each run, Pallas kernels for 41% -> 42%
where the time goes in v26:
time: 58.8 us; the launch traced here: 58.4 us
  Pallas kernels  27.6 us (47%)
  starting transfers between devices  22.3 us (38%)
  waiting for transfers between devices  8.36 us (14%)
    pallas_call x1, Pallas kernels, own_call(): pl.pallas_call(functools.partial(own_kernel, segments, groups), out_shape...  7.19 us
    ppermute x3, starting transfers between devices, to_neighbours(): lax.ppermute(across, 'gz', odd_on)  6.07 us
    pallas_call x1, Pallas kernels, inverse_call(): pl.pallas_call(functools.partial(inverse_kernel, upper, halved), out_shap...  5.94 us
    ppermute x3, starting transfers between devices, to_neighbours(): lax.ppermute(within, 'gz', even_on)  5.75 us
    ppermute x3, waiting for transfers between devices, to_neighbours(): lax.ppermute(across, 'gz', odd_on)  5.61 us
    all_to_all x1, starting transfers between devices, body(): back = lax.all_to_all(mark, 'gz', split_axis=0, concat_axis=0, tiled=True)  5.37 us
    pallas_call x1, Pallas kernels, middle_call(): pl.pallas_call(middle_kernel, out_shape=pltpu.HBM((CH, rows, NX), F32), i...  4.66 us
    pallas_call x1, Pallas kernels, forward_call(): pl.pallas_call(forward_kernel, out_shape=(pltpu.HBM if pinned else jax.Sh...  4.13 us
  transfers between devices with their start and end apart: 10, of which 4 were waited for; matrix products, arithmetic and copies ran while one was open for 0% of the time, Pallas kernels for 42%

profile of v26, /device:TPU:1, one launch (start us, length us, event | category | flops | bytes accessed | tf_op | source)
XLA Modules:
  0.0 58.4 jit_solution(9323207429014388985)
XLA Ops:
  0.0 1.6 %packed_rows.1 = (f32[26,32,256]{2,1,0:T(8,128)S(1)}, f32[2,32,256]{2,1,0:T(8,128)S(1)}) custom-call(f32[32,64,256]{2,1,0:T(8,128)} %bitcast.22), custom_call_target="tpu_custom_call" | custom-call | flops 100000000 | bytes 262144 | tf_op jit(solution)/shard_map/packed_rows/pallas_call | solution.py:477
  1.6 2.7 %collective-permute-start.1 = (f32[26,32,256]{2,1,0:T(8,128)S(1)}, f32[26,32,256]{2,1,0:T(8,128)}, u32[]{:S(2)}, u32[]{:S(2)}) collective-permute-start(f32[26,32,256]{2,1,0:T(8,128)S(1)} %get-tuple-element.38.own), channel_id=1, source_target_pairs={{0,30},{2,4},{4,2},{6,8},{8,6},{10,12},{12,10},{14,16},{16,14},{18... | collective-permute-start | bytes 2555912 | tf_op jit(solution)/shard_map/ppermute | solution.py:586
  4.3 2.9 %collective-permute-start.2 = (f32[26,32,256]{2,1,0:T(8,128)S(1)}, f32[26,32,256]{2,1,0:T(8,128)}, u32[]{:S(2)}, u32[]{:S(2)}) collective-permute-start(f32[26,32,256]{2,1,0:T(8,128)S(1)} %get-tuple-element.38.own), channel_id=1, source_target_pairs={{0,2},{2,0},{4,6},{6,4},{8,10},{10,8},{12,14},{14,12},{16,18},{18,... | collective-permute-start | bytes 2555912 | tf_op jit(solution)/shard_map/ppermute | solution.py:586
  7.2 1.2 %collective-permute-start = (f32[2,32,256]{2,1,0:T(8,128)S(1)}, f32[2,32,256]{2,1,0:T(8,128)S(1)}, u32[]{:S(2)}, u32[]{:S(2)}) collective-permute-start(f32[2,32,256]{2,1,0:T(8,128)S(1)} %get-tuple-element.29), channel_id=1, source_target_pairs={{0,1},{1,0},{2,3},{3,2},{4,5},{5,4},{6,7},{7,6},{8,9},{9,8},{10,11... | collective-permute-start | bytes 196616 | tf_op jit(solution)/shard_map/ppermute | solution.py:598
  8.4 4.1 %forward_modes.1 = f32[256,128]{1,0:T(8,128)} custom-call(f32[8,4,64,256]{3,2,1,0:T(8,128)} %bitcast.23, bf16[2,256,128]{2,1,0:T(8,128)(2,1)} %constant.24.clone.x_top, bf16[2,256,128]{2,1,0:T(8,128)(2,1)} %constant.25.clone.x_rest, bf16[2,32,64]{2,1,0:T(8,128)(2,1)} %constant.26.clone.y_top, bf16[2,32,64]{2,1,0:T(8,128)(2,1)} %constant.27.clone.y_rest), custom_call_target="tpu_custom_call" | custom-call | flops 100000000 | bytes 262144 | tf_op jit(solution)/shard_map/forward_modes/pallas_call | solution.py:398
  12.5 0.0 collective-permute-done.halo
  12.5 2.5 %all-to-all-start = ((f32[32,8,128]{2,1,0:T(8,128)}), f32[32,8,128]{2,1,0:T(8,128)S(1)}, u32[]{:S(2)}, u32[]{:S(2)}) async-start(f32[32,8,128]{2,1,0:T(8,128)} %bitcast.28), calls=%async_computation | async-start | bytes 262144 | tf_op jit(solution)/shard_map/all_to_all | solution.py:615
  15.0 7.2 %own_sums.1 = (f32[32,16,256]{2,1,0:T(8,128)}, f32[32,16,256]{2,1,0:T(8,128)}, f32[32,16,256]{2,1,0:T(8,128)}, f32[32,24,256]{2,1,0:T(8,128)}, f32[32,24,256]{2,1,0:T(8,128)}, /*index=5*/f32[32,24,256]{2,1,0:T(8,128)}) custom-call(f32[32,27]{1,0:T(8,128)} %weight.3, f32[32,32]{1,0:T(8,128)} %point.3, f32[32,64,256]{2,1,0:T(8,128)} %bitcast.24, ...), custom_call_target="tpu_custom_call" | custom-call | flops 100000000 | bytes 262144 | tf_op jit(solution)/shard_map/own_sums/pallas_call | solution.py:497
  22.2 3.0 %collective-permute-done.1.low = f32[26,32,256]{2,1,0:T(8,128)} collective-permute-done((f32[26,32,256]{2,1,0:T(8,128)S(1)}, f32[26,32,256]{2,1,0:T(8,128)}, u32[]{:S(2)}, u32[]{:S(2)}) %collective-permute-start.1) | collective-permute-done | bytes 852000 | tf_op jit(solution)/shard_map/ppermute | solution.py:586
  25.2 0.0 collective-permute-done.2.high
  25.2 1.7 %collective-permute-start.3 = (f32[32,16,256]{2,1,0:T(8,128)}, f32[32,16,256]{2,1,0:T(8,128)S(1)}, u32[]{:S(2)}, u32[]{:S(2)}) collective-permute-start(f32[32,16,256]{2,1,0:T(8,128)} %get-tuple-element.36), channel_id=1, source_target_pairs={{0,30},{2,4},{4,2},{6,8},{8,6},{10,12},{12,10},{14,16},{16,14},{18... | collective-permute-start | bytes 1572872 | tf_op jit(solution)/shard_map/ppermute | solution.py:586
  27.0 0.0 collective-permute-start.4
  27.0 0.0 all-to-all-done
  27.0 2.5 %filter_modes.1 = f32[128,128]{1,0:T(8,128)} custom-call(f32[256,128]{1,0:T(8,128)S(1)} %bitcast.21, f32[2,16,8,64]{3,2,1,0:T(8,128)} %gains, bf16[256,256]{1,0:T(8,128)(2,1)} %constant.28.clone.f_top, bf16[256,256]{1,0:T(8,128)(2,1)} %constant.29.clone.f_rest, bf16[256,128]{1,0:T(8,128)(2,1)} %constant.30.clone.i_top, bf16[256,128]{1,0:T(8,128)(2,1)} %constant.31.clone.i_rest), custom_call_target="tpu_custom_call" | custom-call | flops 40000000000 | bytes 262144 | tf_op jit(solution)/shard_map/filter_modes/pallas_call | solution.py:417
  29.4 5.4 %all-to-all-start.1 = ((f32[16,8,128]{2,1,0:T(8,128)}), f32[16,8,128]{2,1,0:T(8,128)S(1)}, u32[]{:S(2)}, u32[]{:S(2)}) async-start(f32[16,8,128]{2,1,0:T(8,128)} %bitcast.30), calls=%async_computation.1 | async-start | bytes 131072 | tf_op jit(solution)/shard_map/all_to_all | solution.py:620
  34.8 1.6 %collective-permute-start.6 = (f32[32,24,256]{2,1,0:T(8,128)}, f32[32,24,256]{2,1,0:T(8,128)S(1)}, u32[]{:S(2)}, u32[]{:S(2)}) collective-permute-start(f32[32,24,256]{2,1,0:T(8,128)} %get-tuple-element.46), channel_id=1, source_target_pairs={{0,30},{2,4},{4,2},{6,8},{8,6},{10,12},{12,10},{14,16},{16,14},{18... | collective-permute-start | bytes 2359304 | tf_op jit(solution)/shard_map/ppermute | solution.py:586
  36.5 2.9 %collective-permute-start.7 = (f32[32,24,256]{2,1,0:T(8,128)}, f32[32,24,256]{2,1,0:T(8,128)S(1)}, u32[]{:S(2)}, u32[]{:S(2)}) collective-permute-start(f32[32,24,256]{2,1,0:T(8,128)} %get-tuple-element.48), channel_id=1, source_target_pairs={{0,2},{2,0},{4,6},{6,4},{8,10},{10,8},{12,14},{14,12},{16,18},{18,... | collective-permute-start | bytes 2359304 | tf_op jit(solution)/shard_map/ppermute | solution.py:586
  39.3 0.5 collective-permute-done.3
  39.8 0.0 collective-permute-done.4
  39.8 4.7 %middle_sums.1 = f32[32,24,256]{2,1,0:T(8,128)} custom-call(f32[32,27]{1,0:T(8,128)} %weight.3, f32[32,32]{1,0:T(8,128)} %point.3, f32[26,32,256]{2,1,0:T(8,128)} %collective-permute-done.1.low, f32[26,32,256]{2,1,0:T(8,128)S(1)} %get-tuple-element.38.own, f32[26,32,256]{2,1,0:T(8,128)} %collective-permute-done.2.high), custom_call_target="tpu_custom_call" | custom-call | flops 40000000000 | bytes 262144 | tf_op jit(solution)/shard_map/middle_sums/pallas_call | solution.py:524
  44.4 0.0 all-to-all-done.1
  44.5 1.4 %collective-permute-start.5 = (f32[128,128]{1,0:T(8,128)S(1)}, f32[128,128]{1,0:T(8,128)S(1)}, u32[]{:S(2)}, u32[]{:S(2)}) collective-permute-start(f32[128,128]{1,0:T(8,128)S(1)} %bitcast.19), channel_id=1, source_target_pairs={{0,1},{1,0},{2,3},{3,2},{4,5},{5,4},{6,7},{7,6},{8,9},{9,8},{10,11... | collective-permute-start | bytes 196616 | tf_op jit(solution)/shard_map/ppermute | solution.py:629
  45.9 2.7 %collective-permute-done.5.second_modes = f32[128,128]{1,0:T(8,128)S(1)} collective-permute-done((f32[128,128]{1,0:T(8,128)S(1)}, f32[128,128]{1,0:T(8,128)S(1)}, u32[]{:S(2)}, u32[]{:S(2)}) %collective-permute-start.5) | collective-permute-done | bytes 65568 | tf_op jit(solution)/shard_map/ppermute | solution.py:629
  48.6 5.9 %inverse_modes.1 = (f32[8,4,64,256]{3,2,1,0:T(8,128)}, f32[8,4,24,256]{3,2,1,0:T(8,128)S(1)}) custom-call(f32[128,128]{1,0:T(8,128)S(1)} %bitcast.20, f32[128,128]{1,0:T(8,128)S(1)} %collective-permute-done.5.second_modes, f32[32]{0:T(128)} %bias.1, bf16[2,128,256]{2,1,0:T(8,128)(2,1)} %constant.32.clone.x_top, bf16[2,128,256]{2,1,0:T(8,128)(2,1)} %constant.33.clone.x_rest, ...), custom_call_target="tpu_custom_call" | custom-call | flops 100000000 | bytes 262144 | tf_op jit(solution)/shard_map/inverse_modes/pallas_call | solution.py:431
  54.6 2.1 %collective-permute-done.6.low = f32[32,24,256]{2,1,0:T(8,128)S(1)} collective-permute-done((f32[32,24,256]{2,1,0:T(8,128)}, f32[32,24,256]{2,1,0:T(8,128)S(1)}, u32[]{:S(2)}, u32[]{:S(2)}) %collective-permute-start.6) | collective-permute-done | bytes 786464 | tf_op jit(solution)/shard_map/ppermute | solution.py:586
  56.7 0.0 collective-permute-done.7.high
  56.7 1.7 %finished_rows.1 = f32[32,64,256]{2,1,0:T(8,128)} custom-call(f32[32,64,256]{2,1,0:T(8,128)} %bitcast.25, f32[32,24,256]{2,1,0:T(8,128)S(1)} %bitcast.16, f32[32,24,256]{2,1,0:T(8,128)S(1)} %collective-permute-done.6.low, f32[32,24,256]{2,1,0:T(8,128)S(1)} %collective-permute-done.7.high), custom_call_target="tpu_custom_call", output_to_operand_aliasing={{}: (0, {})} | custom-call | flops 100000000 | bytes 262144 | tf_op jit(solution)/shard_map/finished_rows/pallas_call | solution.py:457
Async XLA Ops:
  1.6 23.6 %collective-permute-start.1 = (f32[26,32,256]{2,1,0:T(8,128)S(1)}, f32[26,32,256]{2,1,0:T(8,128)}, u32[]{:S(2)}, u32[]{:S(2)}) collective-permute-start(f32[26,32,256]{2,1,0:T(8,128)S(1)} %get-tuple-element.38.own), channel_id=1, source_target_pairs={{0,30},{2,4},{4,2},{6,8},{8,6},{10,12},{12,10},{14,16},{16,14},{18... | collective-permute-start | bytes 2555912 | tf_op jit(solution)/shard_map/ppermute | solution.py:586
  4.3 20.9 %collective-permute-start.2 = (f32[26,32,256]{2,1,0:T(8,128)S(1)}, f32[26,32,256]{2,1,0:T(8,128)}, u32[]{:S(2)}, u32[]{:S(2)}) collective-permute-start(f32[26,32,256]{2,1,0:T(8,128)S(1)} %get-tuple-element.38.own), channel_id=1, source_target_pairs={{0,2},{2,0},{4,6},{6,4},{8,10},{10,8},{12,14},{14,12},{16,18},{18,... | collective-permute-start | bytes 2555912 | tf_op jit(solution)/shard_map/ppermute | solution.py:586
  7.2 5.4 %collective-permute-start = (f32[2,32,256]{2,1,0:T(8,128)S(1)}, f32[2,32,256]{2,1,0:T(8,128)S(1)}, u32[]{:S(2)}, u32[]{:S(2)}) collective-permute-start(f32[2,32,256]{2,1,0:T(8,128)S(1)} %get-tuple-element.29), channel_id=1, source_target_pairs={{0,1},{1,0},{2,3},{3,2},{4,5},{5,4},{6,7},{7,6},{8,9},{9,8},{10,11... | collective-permute-start | bytes 196616 | tf_op jit(solution)/shard_map/ppermute | solution.py:598
  12.5 14.5 %all-to-all-start = ((f32[32,8,128]{2,1,0:T(8,128)}), f32[32,8,128]{2,1,0:T(8,128)S(1)}, u32[]{:S(2)}, u32[]{:S(2)}) async-start(f32[32,8,128]{2,1,0:T(8,128)} %bitcast.28), calls=%async_computation | async-start | bytes 262144 | tf_op jit(solution)/shard_map/all_to_all | solution.py:615
  25.2 14.5 %collective-permute-start.3 = (f32[32,16,256]{2,1,0:T(8,128)}, f32[32,16,256]{2,1,0:T(8,128)S(1)}, u32[]{:S(2)}, u32[]{:S(2)}) collective-permute-start(f32[32,16,256]{2,1,0:T(8,128)} %get-tuple-element.36), channel_id=1, source_target_pairs={{0,30},{2,4},{4,2},{6,8},{8,6},{10,12},{12,10},{14,16},{16,14},{18... | collective-permute-start | bytes 1572872 | tf_op jit(solution)/shard_map/ppermute | solution.py:586
  27.0 12.8 %collective-permute-start.4 = (f32[32,16,256]{2,1,0:T(8,128)}, f32[32,16,256]{2,1,0:T(8,128)S(1)}, u32[]{:S(2)}, u32[]{:S(2)}) collective-permute-start(f32[32,16,256]{2,1,0:T(8,128)} %get-tuple-element.37), channel_id=1, source_target_pairs={{0,2},{2,0},{4,6},{6,4},{8,10},{10,8},{12,14},{14,12},{16,18},{18,... | collective-permute-start | bytes 1572872 | tf_op jit(solution)/shard_map/ppermute | solution.py:586
  29.4 15.0 %all-to-all-start.1 = ((f32[16,8,128]{2,1,0:T(8,128)}), f32[16,8,128]{2,1,0:T(8,128)S(1)}, u32[]{:S(2)}, u32[]{:S(2)}) async-start(f32[16,8,128]{2,1,0:T(8,128)} %bitcast.30), calls=%async_computation.1 | async-start | bytes 131072 | tf_op jit(solution)/shard_map/all_to_all | solution.py:620
  34.8 21.9 %collective-permute-start.6 = (f32[32,24,256]{2,1,0:T(8,128)}, f32[32,24,256]{2,1,0:T(8,128)S(1)}, u32[]{:S(2)}, u32[]{:S(2)}) collective-permute-start(f32[32,24,256]{2,1,0:T(8,128)} %get-tuple-element.46), channel_id=1, source_target_pairs={{0,30},{2,4},{4,2},{6,8},{8,6},{10,12},{12,10},{14,16},{16,14},{18... | collective-permute-start | bytes 2359304 | tf_op jit(solution)/shard_map/ppermute | solution.py:586
  36.5 20.2 %collective-permute-start.7 = (f32[32,24,256]{2,1,0:T(8,128)}, f32[32,24,256]{2,1,0:T(8,128)S(1)}, u32[]{:S(2)}, u32[]{:S(2)}) collective-permute-start(f32[32,24,256]{2,1,0:T(8,128)} %get-tuple-element.48), channel_id=1, source_target_pairs={{0,2},{2,0},{4,6},{6,4},{8,10},{10,8},{12,14},{14,12},{16,18},{18,... | collective-permute-start | bytes 2359304 | tf_op jit(solution)/shard_map/ppermute | solution.py:586
  44.5 4.2 %collective-permute-start.5 = (f32[128,128]{1,0:T(8,128)S(1)}, f32[128,128]{1,0:T(8,128)S(1)}, u32[]{:S(2)}, u32[]{:S(2)}) collective-permute-start(f32[128,128]{1,0:T(8,128)S(1)} %bitcast.19), channel_id=1, source_target_pairs={{0,1},{1,0},{2,3},{3,2},{4,5},{5,4},{6,7},{7,6},{8,9},{9,8},{10,11... | collective-permute-start | bytes 196616 | tf_op jit(solution)/shard_map/ppermute | solution.py:629

commit v27 on v26

--- a/solution.py
+++ b/solution.py
@@ -613,7 +613,7 @@
     if whole_tiles:
         both = ("gz", "gy")
         got = lax.all_to_all(coarse, both, split_axis=0, concat_axis=0, tiled=True)
-        down, up = lax.optimization_barrier((down, up, first_low))[:2]
+        down, up = lax.optimization_barrier((down, up, first_high))[:2]
         pair = to_neighbours(down, up)
         gains = after(spectral_filter, first_low, first_high, second)
         mark = filter_call(got, gains, gz, gy, forward_scale)

time: 58.8 us -> 62.4 us (1.061)
  the two profiles are of different devices: /device:TPU:1 before, /device:TPU:25 now
where the time goes in v27:
time: 62.4 us; the launch traced here: 61.9 us
  Pallas kernels  27.7 us (44%)
  starting transfers between devices  18.5 us (30%)
  waiting for transfers between devices  15.7 us (25%)
    ppermute x3, waiting for transfers between devices, to_neighbours(): lax.ppermute(across, 'gz', odd_on)  13.8 us
    pallas_call x1, Pallas kernels, own_call(): pl.pallas_call(functools.partial(own_kernel, segments, groups), out_shape...  7.19 us
    all_to_all x1, starting transfers between devices, body(): got = lax.all_to_all(coarse, both, split_axis=0, concat_axis=0, tiled=True)  5.99 us
    pallas_call x1, Pallas kernels, inverse_call(): pl.pallas_call(functools.partial(inverse_kernel, upper, halved), out_shap...  5.94 us
    all_to_all x1, starting transfers between devices, body(): back = lax.all_to_all(mark, 'gz', split_axis=0, concat_axis=0, tiled=True)  5.26 us
    pallas_call x1, Pallas kernels, middle_call(): pl.pallas_call(middle_kernel, out_shape=pltpu.HBM((CH, rows, NX), F32), i...  4.67 us
    pallas_call x1, Pallas kernels, forward_call(): pl.pallas_call(forward_kernel, out_shape=(pltpu.HBM if pinned else jax.Sh...  4.13 us
    ppermute x3, starting transfers between devices, to_neighbours(): lax.ppermute(across, 'gz', odd_on)  3.84 us
  transfers between devices with their start and end apart: 10, of which 3 were waited for; matrix products, arithmetic and copies ran while one was open for 0% of the time, Pallas kernels for 39%

profile of v27, /device:TPU:25, one launch (start us, length us, event | category | flops | bytes accessed | tf_op | source)
XLA Modules:
  0.0 61.9 jit_solution(6376040761091775902)
XLA Ops:
  0.0 1.6 %packed_rows.1 = (f32[26,32,256]{2,1,0:T(8,128)S(1)}, f32[2,32,256]{2,1,0:T(8,128)S(1)}) custom-call(f32[32,64,256]{2,1,0:T(8,128)} %bitcast.22), custom_call_target="tpu_custom_call" | custom-call | flops 100000000 | bytes 262144 | tf_op jit(solution)/shard_map/packed_rows/pallas_call | solution.py:477
  1.6 0.7 %collective-permute-start.2 = (f32[26,32,256]{2,1,0:T(8,128)S(1)}, f32[26,32,256]{2,1,0:T(8,128)}, u32[]{:S(2)}, u32[]{:S(2)}) collective-permute-start(f32[26,32,256]{2,1,0:T(8,128)S(1)} %get-tuple-element.38.own), channel_id=1, source_target_pairs={{0,2},{2,0},{4,6},{6,4},{8,10},{10,8},{12,14},{14,12},{16,18},{18,... | collective-permute-start | bytes 2555912 | tf_op jit(solution)/shard_map/ppermute | solution.py:586
  2.3 1.2 %collective-permute-start.1 = (f32[26,32,256]{2,1,0:T(8,128)S(1)}, f32[26,32,256]{2,1,0:T(8,128)}, u32[]{:S(2)}, u32[]{:S(2)}) collective-permute-start(f32[26,32,256]{2,1,0:T(8,128)S(1)} %get-tuple-element.38.own), channel_id=1, source_target_pairs={{0,30},{2,4},{4,2},{6,8},{8,6},{10,12},{12,10},{14,16},{16,14},{18... | collective-permute-start | bytes 2555912 | tf_op jit(solution)/shard_map/ppermute | solution.py:586
  3.5 1.2 %collective-permute-start = (f32[2,32,256]{2,1,0:T(8,128)S(1)}, f32[2,32,256]{2,1,0:T(8,128)S(1)}, u32[]{:S(2)}, u32[]{:S(2)}) collective-permute-start(f32[2,32,256]{2,1,0:T(8,128)S(1)} %get-tuple-element.29), channel_id=1, source_target_pairs={{0,1},{1,0},{2,3},{3,2},{4,5},{5,4},{6,7},{7,6},{8,9},{9,8},{10,11... | collective-permute-start | bytes 196616 | tf_op jit(solution)/shard_map/ppermute | solution.py:598
  4.8 4.1 %forward_modes.1 = f32[256,128]{1,0:T(8,128)} custom-call(f32[8,4,64,256]{3,2,1,0:T(8,128)} %bitcast.23, bf16[2,256,128]{2,1,0:T(8,128)(2,1)} %constant.24.clone.x_top, bf16[2,256,128]{2,1,0:T(8,128)(2,1)} %constant.25.clone.x_rest, bf16[2,32,64]{2,1,0:T(8,128)(2,1)} %constant.26.clone.y_top, bf16[2,32,64]{2,1,0:T(8,128)(2,1)} %constant.27.clone.y_rest), custom_call_target="tpu_custom_call" | custom-call | flops 100000000 | bytes 262144 | tf_op jit(solution)/shard_map/forward_modes/pallas_call | solution.py:398
  8.9 0.0 collective-permute-done.halo
  8.9 6.0 %all-to-all-start = ((f32[32,8,128]{2,1,0:T(8,128)}), f32[32,8,128]{2,1,0:T(8,128)S(1)}, u32[]{:S(2)}, u32[]{:S(2)}) async-start(f32[32,8,128]{2,1,0:T(8,128)} %bitcast.28), calls=%async_computation | async-start | bytes 262144 | tf_op jit(solution)/shard_map/all_to_all | solution.py:615
  14.9 7.2 %own_sums.1 = (f32[32,16,256]{2,1,0:T(8,128)}, f32[32,16,256]{2,1,0:T(8,128)}, f32[32,16,256]{2,1,0:T(8,128)}, f32[32,24,256]{2,1,0:T(8,128)}, f32[32,24,256]{2,1,0:T(8,128)}, /*index=5*/f32[32,24,256]{2,1,0:T(8,128)}) custom-call(f32[32,27]{1,0:T(8,128)} %weight.3, f32[32,32]{1,0:T(8,128)} %point.3, f32[32,64,256]{2,1,0:T(8,128)} %bitcast.24, ...), custom_call_target="tpu_custom_call" | custom-call | flops 100000000 | bytes 262144 | tf_op jit(solution)/shard_map/own_sums/pallas_call | solution.py:497
  22.1 0.0 collective-permute-done.2.high
  22.1 2.9 %collective-permute-done.1.low = f32[26,32,256]{2,1,0:T(8,128)} collective-permute-done((f32[26,32,256]{2,1,0:T(8,128)S(1)}, f32[26,32,256]{2,1,0:T(8,128)}, u32[]{:S(2)}, u32[]{:S(2)}) %collective-permute-start.1) | collective-permute-done | bytes 852000 | tf_op jit(solution)/shard_map/ppermute | solution.py:586
  25.0 1.2 %collective-permute-start.3 = (f32[32,16,256]{2,1,0:T(8,128)}, f32[32,16,256]{2,1,0:T(8,128)S(1)}, u32[]{:S(2)}, u32[]{:S(2)}) collective-permute-start(f32[32,16,256]{2,1,0:T(8,128)} %get-tuple-element.36), channel_id=1, source_target_pairs={{0,30},{2,4},{4,2},{6,8},{8,6},{10,12},{12,10},{14,16},{16,14},{18... | collective-permute-start | bytes 1572872 | tf_op jit(solution)/shard_map/ppermute | solution.py:586
  26.2 0.0 collective-permute-start.4
  26.2 0.0 all-to-all-done
  26.2 2.5 %filter_modes.1 = f32[128,128]{1,0:T(8,128)} custom-call(f32[256,128]{1,0:T(8,128)S(1)} %bitcast.21, f32[2,16,8,64]{3,2,1,0:T(8,128)} %gains, bf16[256,256]{1,0:T(8,128)(2,1)} %constant.28.clone.f_top, bf16[256,256]{1,0:T(8,128)(2,1)} %constant.29.clone.f_rest, bf16[256,128]{1,0:T(8,128)(2,1)} %constant.30.clone.i_top, bf16[256,128]{1,0:T(8,128)(2,1)} %constant.31.clone.i_rest), custom_call_target="tpu_custom_call" | custom-call | flops 40000000000 | bytes 262144 | tf_op jit(solution)/shard_map/filter_modes/pallas_call | solution.py:417
  28.7 5.3 %all-to-all-start.1 = ((f32[16,8,128]{2,1,0:T(8,128)}), f32[16,8,128]{2,1,0:T(8,128)S(1)}, u32[]{:S(2)}, u32[]{:S(2)}) async-start(f32[16,8,128]{2,1,0:T(8,128)} %bitcast.30), calls=%async_computation.1 | async-start | bytes 131072 | tf_op jit(solution)/shard_map/all_to_all | solution.py:620
  33.9 1.4 %collective-permute-start.6 = (f32[32,24,256]{2,1,0:T(8,128)}, f32[32,24,256]{2,1,0:T(8,128)S(1)}, u32[]{:S(2)}, u32[]{:S(2)}) collective-permute-start(f32[32,24,256]{2,1,0:T(8,128)} %get-tuple-element.46), channel_id=1, source_target_pairs={{0,30},{2,4},{4,2},{6,8},{8,6},{10,12},{12,10},{14,16},{16,14},{18... | collective-permute-start | bytes 2359304 | tf_op jit(solution)/shard_map/ppermute | solution.py:586
  35.4 0.1 collective-permute-start.7
  35.5 10.9 %collective-permute-done.3 = f32[32,16,256]{2,1,0:T(8,128)S(1)} collective-permute-done((f32[32,16,256]{2,1,0:T(8,128)}, f32[32,16,256]{2,1,0:T(8,128)S(1)}, u32[]{:S(2)}, u32[]{:S(2)}) %collective-permute-start.3) | collective-permute-done | bytes 524320 | tf_op jit(solution)/shard_map/ppermute | solution.py:586
  46.4 0.0 collective-permute-done.4
  46.4 4.7 %middle_sums.1 = f32[32,24,256]{2,1,0:T(8,128)} custom-call(f32[32,27]{1,0:T(8,128)} %weight.3, f32[32,32]{1,0:T(8,128)} %point.3, f32[26,32,256]{2,1,0:T(8,128)} %collective-permute-done.1.low, f32[26,32,256]{2,1,0:T(8,128)S(1)} %get-tuple-element.38.own, f32[26,32,256]{2,1,0:T(8,128)} %collective-permute-done.2.high), custom_call_target="tpu_custom_call" | custom-call | flops 40000000000 | bytes 262144 | tf_op jit(solution)/shard_map/middle_sums/pallas_call | solution.py:524
  51.1 0.0 all-to-all-done.1
  51.1 1.3 %collective-permute-start.5 = (f32[128,128]{1,0:T(8,128)S(1)}, f32[128,128]{1,0:T(8,128)S(1)}, u32[]{:S(2)}, u32[]{:S(2)}) collective-permute-start(f32[128,128]{1,0:T(8,128)S(1)} %bitcast.19), channel_id=1, source_target_pairs={{0,1},{1,0},{2,3},{3,2},{4,5},{5,4},{6,7},{7,6},{8,9},{9,8},{10,11... | collective-permute-start | bytes 196616 | tf_op jit(solution)/shard_map/ppermute | solution.py:629
  52.4 1.9 %collective-permute-done.5.second_modes = f32[128,128]{1,0:T(8,128)S(1)} collective-permute-done((f32[128,128]{1,0:T(8,128)S(1)}, f32[128,128]{1,0:T(8,128)S(1)}, u32[]{:S(2)}, u32[]{:S(2)}) %collective-permute-start.5) | collective-permute-done | bytes 65568 | tf_op jit(solution)/shard_map/ppermute | solution.py:629
  54.3 5.9 %inverse_modes.1 = (f32[8,4,64,256]{3,2,1,0:T(8,128)}, f32[8,4,24,256]{3,2,1,0:T(8,128)S(1)}) custom-call(f32[128,128]{1,0:T(8,128)S(1)} %bitcast.20, f32[128,128]{1,0:T(8,128)S(1)} %collective-permute-done.5.second_modes, f32[32]{0:T(128)} %bias.1, bf16[2,128,256]{2,1,0:T(8,128)(2,1)} %constant.32.clone.x_top, bf16[2,128,256]{2,1,0:T(8,128)(2,1)} %constant.33.clone.x_rest, ...), custom_call_target="tpu_custom_call" | custom-call | flops 100000000 | bytes 262144 | tf_op jit(solution)/shard_map/inverse_modes/pallas_call | solution.py:431
  60.2 0.0 collective-permute-done.6.low
  60.2 0.0 collective-permute-done.7.high
  60.2 1.7 %finished_rows.1 = f32[32,64,256]{2,1,0:T(8,128)} custom-call(f32[32,64,256]{2,1,0:T(8,128)} %bitcast.25, f32[32,24,256]{2,1,0:T(8,128)S(1)} %bitcast.16, f32[32,24,256]{2,1,0:T(8,128)S(1)} %collective-permute-done.6.low, f32[32,24,256]{2,1,0:T(8,128)S(1)} %collective-permute-done.7.high), custom_call_target="tpu_custom_call", output_to_operand_aliasing={{}: (0, {})} | custom-call | flops 100000000 | bytes 262144 | tf_op jit(solution)/shard_map/finished_rows/pallas_call | solution.py:457
Async XLA Ops:
  1.6 20.5 %collective-permute-start.2 = (f32[26,32,256]{2,1,0:T(8,128)S(1)}, f32[26,32,256]{2,1,0:T(8,128)}, u32[]{:S(2)}, u32[]{:S(2)}) collective-permute-start(f32[26,32,256]{2,1,0:T(8,128)S(1)} %get-tuple-element.38.own), channel_id=1, source_target_pairs={{0,2},{2,0},{4,6},{6,4},{8,10},{10,8},{12,14},{14,12},{16,18},{18,... | collective-permute-start | bytes 2555912 | tf_op jit(solution)/shard_map/ppermute | solution.py:586
  2.3 22.7 %collective-permute-start.1 = (f32[26,32,256]{2,1,0:T(8,128)S(1)}, f32[26,32,256]{2,1,0:T(8,128)}, u32[]{:S(2)}, u32[]{:S(2)}) collective-permute-start(f32[26,32,256]{2,1,0:T(8,128)S(1)} %get-tuple-element.38.own), channel_id=1, source_target_pairs={{0,30},{2,4},{4,2},{6,8},{8,6},{10,12},{12,10},{14,16},{16,14},{18... | collective-permute-start | bytes 2555912 | tf_op jit(solution)/shard_map/ppermute | solution.py:586
  3.5 5.4 %collective-permute-start = (f32[2,32,256]{2,1,0:T(8,128)S(1)}, f32[2,32,256]{2,1,0:T(8,128)S(1)}, u32[]{:S(2)}, u32[]{:S(2)}) collective-permute-start(f32[2,32,256]{2,1,0:T(8,128)S(1)} %get-tuple-element.29), channel_id=1, source_target_pairs={{0,1},{1,0},{2,3},{3,2},{4,5},{5,4},{6,7},{7,6},{8,9},{9,8},{10,11... | collective-permute-start | bytes 196616 | tf_op jit(solution)/shard_map/ppermute | solution.py:598
  8.9 17.3 %all-to-all-start = ((f32[32,8,128]{2,1,0:T(8,128)}), f32[32,8,128]{2,1,0:T(8,128)S(1)}, u32[]{:S(2)}, u32[]{:S(2)}) async-start(f32[32,8,128]{2,1,0:T(8,128)} %bitcast.28), calls=%async_computation | async-start | bytes 262144 | tf_op jit(solution)/shard_map/all_to_all | solution.py:615
  25.0 21.4 %collective-permute-start.3 = (f32[32,16,256]{2,1,0:T(8,128)}, f32[32,16,256]{2,1,0:T(8,128)S(1)}, u32[]{:S(2)}, u32[]{:S(2)}) collective-permute-start(f32[32,16,256]{2,1,0:T(8,128)} %get-tuple-element.36), channel_id=1, source_target_pairs={{0,30},{2,4},{4,2},{6,8},{8,6},{10,12},{12,10},{14,16},{16,14},{18... | collective-permute-start | bytes 1572872 | tf_op jit(solution)/shard_map/ppermute | solution.py:586
  26.2 20.2 %collective-permute-start.4 = (f32[32,16,256]{2,1,0:T(8,128)}, f32[32,16,256]{2,1,0:T(8,128)S(1)}, u32[]{:S(2)}, u32[]{:S(2)}) collective-permute-start(f32[32,16,256]{2,1,0:T(8,128)} %get-tuple-element.37), channel_id=1, source_target_pairs={{0,2},{2,0},{4,6},{6,4},{8,10},{10,8},{12,14},{14,12},{16,18},{18,... | collective-permute-start | bytes 1572872 | tf_op jit(solution)/shard_map/ppermute | solution.py:586
  28.7 22.4 %all-to-all-start.1 = ((f32[16,8,128]{2,1,0:T(8,128)}), f32[16,8,128]{2,1,0:T(8,128)S(1)}, u32[]{:S(2)}, u32[]{:S(2)}) async-start(f32[16,8,128]{2,1,0:T(8,128)} %bitcast.30), calls=%async_computation.1 | async-start | bytes 131072 | tf_op jit(solution)/shard_map/all_to_all | solution.py:620
  33.9 26.3 %collective-permute-start.6 = (f32[32,24,256]{2,1,0:T(8,128)}, f32[32,24,256]{2,1,0:T(8,128)S(1)}, u32[]{:S(2)}, u32[]{:S(2)}) collective-permute-start(f32[32,24,256]{2,1,0:T(8,128)} %get-tuple-element.46), channel_id=1, source_target_pairs={{0,30},{2,4},{4,2},{6,8},{8,6},{10,12},{12,10},{14,16},{16,14},{18... | collective-permute-start | bytes 2359304 | tf_op jit(solution)/shard_map/ppermute | solution.py:586
  35.4 24.9 %collective-permute-start.7 = (f32[32,24,256]{2,1,0:T(8,128)}, f32[32,24,256]{2,1,0:T(8,128)S(1)}, u32[]{:S(2)}, u32[]{:S(2)}) collective-permute-start(f32[32,24,256]{2,1,0:T(8,128)} %get-tuple-element.48), channel_id=1, source_target_pairs={{0,2},{2,0},{4,6},{6,4},{8,10},{10,8},{12,14},{14,12},{16,18},{18,... | collective-permute-start | bytes 2359304 | tf_op jit(solution)/shard_map/ppermute | solution.py:586
  51.1 3.2 %collective-permute-start.5 = (f32[128,128]{1,0:T(8,128)S(1)}, f32[128,128]{1,0:T(8,128)S(1)}, u32[]{:S(2)}, u32[]{:S(2)}) collective-permute-start(f32[128,128]{1,0:T(8,128)S(1)} %bitcast.19), channel_id=1, source_target_pairs={{0,1},{1,0},{2,3},{3,2},{4,5},{5,4},{6,7},{7,6},{8,9},{9,8},{10,11... | collective-permute-start | bytes 196616 | tf_op jit(solution)/shard_map/ppermute | solution.py:629

commit v28 on v26

--- a/solution.py
+++ b/solution.py
@@ -322,7 +322,7 @@
     return value * jnp.where(value < 0.0, tail, 1.0 - tail)
 
 
-def inverse_kernel(upper, halved, first_modes, second_modes, bias, x_top, x_rest, y_top, y_rest, own, middle, second, low, high, out, base, columns):
+def inverse_kernel(upper, halved, first_modes, second_modes, bias, x_top, x_rest, y_top, y_rest, own, near, middle, second, low, high, out, base, columns):
     q = pl.program_id(0)
     groups, _, y_local, _ = out.shape
 
@@ -351,19 +351,20 @@
     stop = turn + second.shape[2]
     for g in range(groups):
         plane = rows[g * y_local : (g + 1) * y_local] + bias[4 * g + q]
-        base[g, 0, :upper] = plane[:upper] + own[g, 0, :upper]
+        rim = own[g, 0] + near[g, 0]
+        base[g, 0, :upper] = plane[:upper] + rim[:upper]
         out[g, 0, upper:turn] = gelu(plane[upper:turn] + middle[g, 0])
         out[g, 0, turn:stop] = gelu(plane[turn:stop] + (second[g, 0] + (low[g, 0] + high[g, 0])))
-        base[g, 0, upper:] = plane[stop:] + own[g, 0, upper:]
-
-
-def finish_kernel(upper, _, base, low, high, out, sent, sem):
+        base[g, 0, upper:] = plane[stop:] + rim[upper:]
+
+
+def finish_kernel(upper, _, base, across, out, sent, sem):
     tiles = base.shape[1] // 8
     gap = out.shape[1] // 8 - tiles
     copies = []
     for t in range(tiles):
         rows = pl.ds(8 * t, 8)
-        sent[t] = gelu(base[:, rows, :] + (low[:, rows, :] + high[:, rows, :]))
+        sent[t] = gelu(base[:, rows, :] + across[:, rows, :])
         to = t if t < upper else t + gap
         copies.append(pltpu.make_async_copy(sent.at[t], out.at[:, pl.ds(8 * to, 8), :], sem.at[t]))
         copies[-1].start()
@@ -423,10 +424,10 @@
     )(arrived, *in_hbm(gains, *fwd, *inv))
 
 
-def inverse_call(modes, halved, bias, own, middle, second, pair, upper, y_local, gy, scale):
+def inverse_call(modes, halved, bias, own, near, middle, second, pair, upper, y_local, gy, scale):
     tables = [*halves(x_table(True, scale)), *halves(y_table(y_local, gy, True))]
     some = lambda rows: pl.BlockSpec((CH // 4, 1, rows, NX), lambda i: (0, i, 0, 0))
-    planes = [*in_hbm(*map(by_four, (own, middle, second))), *map(by_four, pair)]
+    planes = [*in_hbm(by_four(own)), by_four(near), *in_hbm(*map(by_four, (middle, second))), *map(by_four, pair)]
     rim = own.shape[1]
     result, base = pl.pallas_call(
         functools.partial(inverse_kernel, upper, halved),
@@ -450,14 +451,14 @@
     return result.reshape(CH, y_local, NX), base.reshape(CH, rim, NX)
 
 
-def finish_call(result, base, low, high, upper):
+def finish_call(result, base, across, upper):
     tiles = base.shape[1] // 8
     anywhere = pl.BlockSpec(memory_space=pl.ANY)
     vmem = pl.BlockSpec(memory_space=pltpu.VMEM)
     return pl.pallas_call(
         functools.partial(finish_kernel, upper),
         out_shape=jax.ShapeDtypeStruct(result.shape, F32),
-        in_specs=[anywhere] + [vmem] * 3,
+        in_specs=[anywhere] + [vmem] * 2,
         out_specs=anywhere,
         scratch_shapes=[
             pltpu.VMEM((tiles, CH, 8, NX), F32),
@@ -467,7 +468,7 @@
         compiler_params=params(),
         cost_estimate=cost(10**8, 2**18),
         name="finished_rows",
-    )(result, base, low, high)
+    )(result, base, across)
 
 
 def pack_call(field, tiles):
@@ -628,9 +629,9 @@
     if whole_tiles:
         modes = (back, lax.ppermute(after(back, mixed), "gy", ring("gy", gy, 1)))
     result, base = inverse_call(
-        modes, whole_tiles, bias_vector, own, mixed, second, pair, 8, y_local, gy, inverse_scale
+        modes, whole_tiles, bias_vector, own, outer_pair[1], mixed, second, pair, 8, y_local, gy, inverse_scale
     )
-    result = finish_call(result, base, *outer_pair, 1)
+    result = finish_call(result, base, outer_pair[0], 1)
     return result.reshape(CH, 1, y_local, NX)
 
 

time: 58.8 us -> 58.7 us (level)
  starting transfers between devices: 22.3 us -> 19.6 us
  waiting for transfers between devices: 8.36 us -> 11 us
    ppermute x3, waiting for transfers between devices: 5.61 us -> 8.59 us  [to_neighbours(): lax.ppermute(across, 'gz', odd_on)]
    ppermute x3, starting transfers between devices: 5.75 us -> 3.04 us  [to_neighbours(): lax.ppermute(within, 'gz', even_on)]
where the time goes in v28:
time: 58.7 us; the launch traced here: 58.3 us
  Pallas kernels  27.6 us (47%)
  starting transfers between devices  19.6 us (33%)
  waiting for transfers between devices  11 us (19%)
    ppermute x3, waiting for transfers between devices, to_neighbours(): lax.ppermute(across, 'gz', odd_on)  8.59 us
    pallas_call x1, Pallas kernels, own_call(): pl.pallas_call(functools.partial(own_kernel, segments, groups), out_shape...  7.13 us
    ppermute x3, starting transfers between devices, to_neighbours(): lax.ppermute(across, 'gz', odd_on)  6.05 us
    pallas_call x1, Pallas kernels, inverse_call(): pl.pallas_call(functools.partial(inverse_kernel, upper, halved), out_shap...  6 us
    all_to_all x1, starting transfers between devices, body(): back = lax.all_to_all(mark, 'gz', split_axis=0, concat_axis=0, tiled=True)  5.4 us
    pallas_call x1, Pallas kernels, middle_call(): pl.pallas_call(middle_kernel, out_shape=pltpu.HBM((CH, rows, NX), F32), i...  4.65 us
    pallas_call x1, Pallas kernels, forward_call(): pl.pallas_call(forward_kernel, out_shape=(pltpu.HBM if pinned else jax.Sh...  4.14 us
    ppermute x3, starting transfers between devices, to_neighbours(): lax.ppermute(within, 'gz', even_on)  3.04 us
  transfers between devices with their start and end apart: 10, of which 4 were waited for; matrix products, arithmetic and copies ran while one was open for 0% of the time, Pallas kernels for 42%

profile of v28, /device:TPU:1, one launch (start us, length us, event | category | flops | bytes accessed | tf_op | source)
XLA Modules:
  0.0 58.3 jit_solution(11823513742711749577)
XLA Ops:
  0.0 1.6 %packed_rows.1 = (f32[26,32,256]{2,1,0:T(8,128)S(1)}, f32[2,32,256]{2,1,0:T(8,128)S(1)}) custom-call(f32[32,64,256]{2,1,0:T(8,128)} %bitcast.24), custom_call_target="tpu_custom_call" | custom-call | flops 100000000 | bytes 262144 | tf_op jit(solution)/shard_map/packed_rows/pallas_call | solution.py:478
  1.6 2.7 %collective-permute-start.1 = (f32[26,32,256]{2,1,0:T(8,128)S(1)}, f32[26,32,256]{2,1,0:T(8,128)}, u32[]{:S(2)}, u32[]{:S(2)}) collective-permute-start(f32[26,32,256]{2,1,0:T(8,128)S(1)} %get-tuple-element.38.own), channel_id=1, source_target_pairs={{0,30},{2,4},{4,2},{6,8},{8,6},{10,12},{12,10},{14,16},{16,14},{18... | collective-permute-start | bytes 2555912 | tf_op jit(solution)/shard_map/ppermute | solution.py:587
  4.3 2.9 %collective-permute-start.2 = (f32[26,32,256]{2,1,0:T(8,128)S(1)}, f32[26,32,256]{2,1,0:T(8,128)}, u32[]{:S(2)}, u32[]{:S(2)}) collective-permute-start(f32[26,32,256]{2,1,0:T(8,128)S(1)} %get-tuple-element.38.own), channel_id=1, source_target_pairs={{0,2},{2,0},{4,6},{6,4},{8,10},{10,8},{12,14},{14,12},{16,18},{18,... | collective-permute-start | bytes 2555912 | tf_op jit(solution)/shard_map/ppermute | solution.py:587
  7.2 1.2 %collective-permute-start = (f32[2,32,256]{2,1,0:T(8,128)S(1)}, f32[2,32,256]{2,1,0:T(8,128)S(1)}, u32[]{:S(2)}, u32[]{:S(2)}) collective-permute-start(f32[2,32,256]{2,1,0:T(8,128)S(1)} %get-tuple-element.29), channel_id=1, source_target_pairs={{0,1},{1,0},{2,3},{3,2},{4,5},{5,4},{6,7},{7,6},{8,9},{9,8},{10,11... | collective-permute-start | bytes 196616 | tf_op jit(solution)/shard_map/ppermute | solution.py:599
  8.4 4.1 %forward_modes.1 = f32[256,128]{1,0:T(8,128)} custom-call(f32[8,4,64,256]{3,2,1,0:T(8,128)} %bitcast.25, bf16[2,256,128]{2,1,0:T(8,128)(2,1)} %constant.24.clone.x_top, bf16[2,256,128]{2,1,0:T(8,128)(2,1)} %constant.25.clone.x_rest, bf16[2,32,64]{2,1,0:T(8,128)(2,1)} %constant.26.clone.y_top, bf16[2,32,64]{2,1,0:T(8,128)(2,1)} %constant.27.clone.y_rest), custom_call_target="tpu_custom_call" | custom-call | flops 100000000 | bytes 262144 | tf_op jit(solution)/shard_map/forward_modes/pallas_call | solution.py:399
  12.5 0.0 collective-permute-done.halo
  12.5 2.5 %all-to-all-start = ((f32[32,8,128]{2,1,0:T(8,128)}), f32[32,8,128]{2,1,0:T(8,128)S(1)}, u32[]{:S(2)}, u32[]{:S(2)}) async-start(f32[32,8,128]{2,1,0:T(8,128)} %bitcast.31), calls=%async_computation | async-start | bytes 262144 | tf_op jit(solution)/shard_map/all_to_all | solution.py:616
  15.0 7.1 %own_sums.1 = (f32[32,16,256]{2,1,0:T(8,128)}, f32[32,16,256]{2,1,0:T(8,128)}, f32[32,16,256]{2,1,0:T(8,128)}, f32[32,24,256]{2,1,0:T(8,128)}, f32[32,24,256]{2,1,0:T(8,128)}, /*index=5*/f32[32,24,256]{2,1,0:T(8,128)}) custom-call(f32[32,27]{1,0:T(8,128)} %weight.3, f32[32,32]{1,0:T(8,128)} %point.3, f32[32,64,256]{2,1,0:T(8,128)} %bitcast.26, ...), custom_call_target="tpu_custom_call" | custom-call | flops 100000000 | bytes 262144 | tf_op jit(solution)/shard_map/own_sums/pallas_call | solution.py:498
  22.1 3.1 %collective-permute-done.1.low = f32[26,32,256]{2,1,0:T(8,128)} collective-permute-done((f32[26,32,256]{2,1,0:T(8,128)S(1)}, f32[26,32,256]{2,1,0:T(8,128)}, u32[]{:S(2)}, u32[]{:S(2)}) %collective-permute-start.1) | collective-permute-done | bytes 852000 | tf_op jit(solution)/shard_map/ppermute | solution.py:587
  25.2 0.0 collective-permute-done.2.high
  25.2 1.7 %collective-permute-start.3 = (f32[32,16,256]{2,1,0:T(8,128)}, f32[32,16,256]{2,1,0:T(8,128)S(1)}, u32[]{:S(2)}, u32[]{:S(2)}) collective-permute-start(f32[32,16,256]{2,1,0:T(8,128)} %get-tuple-element.36), channel_id=1, source_target_pairs={{0,30},{2,4},{4,2},{6,8},{8,6},{10,12},{12,10},{14,16},{16,14},{18... | collective-permute-start | bytes 1572872 | tf_op jit(solution)/shard_map/ppermute | solution.py:587
  27.0 0.0 collective-permute-start.4
  27.0 0.0 all-to-all-done
  27.0 2.4 %filter_modes.1 = f32[128,128]{1,0:T(8,128)} custom-call(f32[256,128]{1,0:T(8,128)S(1)} %bitcast.23, f32[2,16,8,64]{3,2,1,0:T(8,128)} %gains, bf16[256,256]{1,0:T(8,128)(2,1)} %constant.28.clone.f_top, bf16[256,256]{1,0:T(8,128)(2,1)} %constant.29.clone.f_rest, bf16[256,128]{1,0:T(8,128)(2,1)} %constant.30.clone.i_top, bf16[256,128]{1,0:T(8,128)(2,1)} %constant.31.clone.i_rest), custom_call_target="tpu_custom_call" | custom-call | flops 40000000000 | bytes 262144 | tf_op jit(solution)/shard_map/filter_modes/pallas_call | solution.py:418
  29.4 5.4 %all-to-all-start.1 = ((f32[16,8,128]{2,1,0:T(8,128)}), f32[16,8,128]{2,1,0:T(8,128)S(1)}, u32[]{:S(2)}, u32[]{:S(2)}) async-start(f32[16,8,128]{2,1,0:T(8,128)} %bitcast.32), calls=%async_computation.1 | async-start | bytes 131072 | tf_op jit(solution)/shard_map/all_to_all | solution.py:621
  34.8 0.2 collective-permute-start.6
  35.0 1.6 %collective-permute-start.7 = (f32[32,24,256]{2,1,0:T(8,128)}, f32[32,24,256]{2,1,0:T(8,128)S(1)}, u32[]{:S(2)}, u32[]{:S(2)}) collective-permute-start(f32[32,24,256]{2,1,0:T(8,128)} %get-tuple-element.48), channel_id=1, source_target_pairs={{0,30},{2,4},{4,2},{6,8},{8,6},{10,12},{12,10},{14,16},{16,14},{18... | collective-permute-start | bytes 2359304 | tf_op jit(solution)/shard_map/ppermute | solution.py:587
  36.6 3.1 %collective-permute-done.3 = f32[32,16,256]{2,1,0:T(8,128)S(1)} collective-permute-done((f32[32,16,256]{2,1,0:T(8,128)}, f32[32,16,256]{2,1,0:T(8,128)S(1)}, u32[]{:S(2)}, u32[]{:S(2)}) %collective-permute-start.3) | collective-permute-done | bytes 524320 | tf_op jit(solution)/shard_map/ppermute | solution.py:587
  39.7 0.0 collective-permute-done.4
  39.7 4.6 %middle_sums.1 = f32[32,24,256]{2,1,0:T(8,128)} custom-call(f32[32,27]{1,0:T(8,128)} %weight.3, f32[32,32]{1,0:T(8,128)} %point.3, f32[26,32,256]{2,1,0:T(8,128)} %collective-permute-done.1.low, f32[26,32,256]{2,1,0:T(8,128)S(1)} %get-tuple-element.38.own, f32[26,32,256]{2,1,0:T(8,128)} %collective-permute-done.2.high), custom_call_target="tpu_custom_call" | custom-call | flops 40000000000 | bytes 262144 | tf_op jit(solution)/shard_map/middle_sums/pallas_call | solution.py:525
  44.4 0.0 all-to-all-done.1
  44.4 1.4 %collective-permute-start.5 = (f32[128,128]{1,0:T(8,128)S(1)}, f32[128,128]{1,0:T(8,128)S(1)}, u32[]{:S(2)}, u32[]{:S(2)}) collective-permute-start(f32[128,128]{1,0:T(8,128)S(1)} %bitcast.21), channel_id=1, source_target_pairs={{0,1},{1,0},{2,3},{3,2},{4,5},{5,4},{6,7},{7,6},{8,9},{9,8},{10,11... | collective-permute-start | bytes 196616 | tf_op jit(solution)/shard_map/ppermute | solution.py:630
  45.8 2.4 %collective-permute-done.5.second_modes = f32[128,128]{1,0:T(8,128)S(1)} collective-permute-done((f32[128,128]{1,0:T(8,128)S(1)}, f32[128,128]{1,0:T(8,128)S(1)}, u32[]{:S(2)}, u32[]{:S(2)}) %collective-permute-start.5) | collective-permute-done | bytes 65568 | tf_op jit(solution)/shard_map/ppermute | solution.py:630
  48.2 0.0 collective-permute-done.6
  48.2 6.0 %inverse_modes.1 = (f32[8,4,64,256]{3,2,1,0:T(8,128)}, f32[8,4,24,256]{3,2,1,0:T(8,128)S(1)}) custom-call(f32[128,128]{1,0:T(8,128)S(1)} %bitcast.22, f32[128,128]{1,0:T(8,128)S(1)} %collective-permute-done.5.second_modes, f32[32]{0:T(128)} %bias.1, bf16[2,128,256]{2,1,0:T(8,128)(2,1)} %constant.32.clone.x_top, bf16[2,128,256]{2,1,0:T(8,128)(2,1)} %constant.33.clone.x_rest, ...), custom_call_target="tpu_custom_call" | custom-call | flops 100000000 | bytes 262144 | tf_op jit(solution)/shard_map/inverse_modes/pallas_call | solution.py:432
  54.2 2.4 %collective-permute-done.7.across = f32[32,24,256]{2,1,0:T(8,128)S(1)} collective-permute-done((f32[32,24,256]{2,1,0:T(8,128)}, f32[32,24,256]{2,1,0:T(8,128)S(1)}, u32[]{:S(2)}, u32[]{:S(2)}) %collective-permute-start.7) | collective-permute-done | bytes 786464 | tf_op jit(solution)/shard_map/ppermute | solution.py:587
  56.6 1.7 %finished_rows.1 = f32[32,64,256]{2,1,0:T(8,128)} custom-call(f32[32,64,256]{2,1,0:T(8,128)} %bitcast.27, f32[32,24,256]{2,1,0:T(8,128)S(1)} %bitcast.18, f32[32,24,256]{2,1,0:T(8,128)S(1)} %collective-permute-done.7.across), custom_call_target="tpu_custom_call", output_to_operand_aliasing={{}: (0, {})} | custom-call | flops 100000000 | bytes 262144 | tf_op jit(solution)/shard_map/finished_rows/pallas_call | solution.py:458
Async XLA Ops:
  1.6 23.6 %collective-permute-start.1 = (f32[26,32,256]{2,1,0:T(8,128)S(1)}, f32[26,32,256]{2,1,0:T(8,128)}, u32[]{:S(2)}, u32[]{:S(2)}) collective-permute-start(f32[26,32,256]{2,1,0:T(8,128)S(1)} %get-tuple-element.38.own), channel_id=1, source_target_pairs={{0,30},{2,4},{4,2},{6,8},{8,6},{10,12},{12,10},{14,16},{16,14},{18... | collective-permute-start | bytes 2555912 | tf_op jit(solution)/shard_map/ppermute | solution.py:587
  4.3 20.9 %collective-permute-start.2 = (f32[26,32,256]{2,1,0:T(8,128)S(1)}, f32[26,32,256]{2,1,0:T(8,128)}, u32[]{:S(2)}, u32[]{:S(2)}) collective-permute-start(f32[26,32,256]{2,1,0:T(8,128)S(1)} %get-tuple-element.38.own), channel_id=1, source_target_pairs={{0,2},{2,0},{4,6},{6,4},{8,10},{10,8},{12,14},{14,12},{16,18},{18,... | collective-permute-start | bytes 2555912 | tf_op jit(solution)/shard_map/ppermute | solution.py:587
  7.2 5.4 %collective-permute-start = (f32[2,32,256]{2,1,0:T(8,128)S(1)}, f32[2,32,256]{2,1,0:T(8,128)S(1)}, u32[]{:S(2)}, u32[]{:S(2)}) collective-permute-start(f32[2,32,256]{2,1,0:T(8,128)S(1)} %get-tuple-element.29), channel_id=1, source_target_pairs={{0,1},{1,0},{2,3},{3,2},{4,5},{5,4},{6,7},{7,6},{8,9},{9,8},{10,11... | collective-permute-start | bytes 196616 | tf_op jit(solution)/shard_map/ppermute | solution.py:599
  12.5 14.4 %all-to-all-start = ((f32[32,8,128]{2,1,0:T(8,128)}), f32[32,8,128]{2,1,0:T(8,128)S(1)}, u32[]{:S(2)}, u32[]{:S(2)}) async-start(f32[32,8,128]{2,1,0:T(8,128)} %bitcast.31), calls=%async_computation | async-start | bytes 262144 | tf_op jit(solution)/shard_map/all_to_all | solution.py:616
  25.2 14.5 %collective-permute-start.3 = (f32[32,16,256]{2,1,0:T(8,128)}, f32[32,16,256]{2,1,0:T(8,128)S(1)}, u32[]{:S(2)}, u32[]{:S(2)}) collective-permute-start(f32[32,16,256]{2,1,0:T(8,128)} %get-tuple-element.36), channel_id=1, source_target_pairs={{0,30},{2,4},{4,2},{6,8},{8,6},{10,12},{12,10},{14,16},{16,14},{18... | collective-permute-start | bytes 1572872 | tf_op jit(solution)/shard_map/ppermute | solution.py:587
  27.0 12.8 %collective-permute-start.4 = (f32[32,16,256]{2,1,0:T(8,128)}, f32[32,16,256]{2,1,0:T(8,128)S(1)}, u32[]{:S(2)}, u32[]{:S(2)}) collective-permute-start(f32[32,16,256]{2,1,0:T(8,128)} %get-tuple-element.37), channel_id=1, source_target_pairs={{0,2},{2,0},{4,6},{6,4},{8,10},{10,8},{12,14},{14,12},{16,18},{18,... | collective-permute-start | bytes 1572872 | tf_op jit(solution)/shard_map/ppermute | solution.py:587
  29.4 15.0 %all-to-all-start.1 = ((f32[16,8,128]{2,1,0:T(8,128)}), f32[16,8,128]{2,1,0:T(8,128)S(1)}, u32[]{:S(2)}, u32[]{:S(2)}) async-start(f32[16,8,128]{2,1,0:T(8,128)} %bitcast.32), calls=%async_computation.1 | async-start | bytes 131072 | tf_op jit(solution)/shard_map/all_to_all | solution.py:621
  34.8 13.4 %collective-permute-start.6 = (f32[32,24,256]{2,1,0:T(8,128)}, f32[32,24,256]{2,1,0:T(8,128)S(1)}, u32[]{:S(2)}, u32[]{:S(2)}) collective-permute-start(f32[32,24,256]{2,1,0:T(8,128)} %get-tuple-element.42), channel_id=1, source_target_pairs={{0,2},{2,0},{4,6},{6,4},{8,10},{10,8},{12,14},{14,12},{16,18},{18,... | collective-permute-start | bytes 2359304 | tf_op jit(solution)/shard_map/ppermute | solution.py:587
  35.0 21.6 %collective-permute-start.7 = (f32[32,24,256]{2,1,0:T(8,128)}, f32[32,24,256]{2,1,0:T(8,128)S(1)}, u32[]{:S(2)}, u32[]{:S(2)}) collective-permute-start(f32[32,24,256]{2,1,0:T(8,128)} %get-tuple-element.48), channel_id=1, source_target_pairs={{0,30},{2,4},{4,2},{6,8},{8,6},{10,12},{12,10},{14,16},{16,14},{18... | collective-permute-start | bytes 2359304 | tf_op jit(solution)/shard_map/ppermute | solution.py:587
  44.4 3.8 %collective-permute-start.5 = (f32[128,128]{1,0:T(8,128)S(1)}, f32[128,128]{1,0:T(8,128)S(1)}, u32[]{:S(2)}, u32[]{:S(2)}) collective-permute-start(f32[128,128]{1,0:T(8,128)S(1)} %bitcast.21), channel_id=1, source_target_pairs={{0,1},{1,0},{2,3},{3,2},{4,5},{5,4},{6,7},{7,6},{8,9},{9,8},{10,11... | collective-permute-start | bytes 196616 | tf_op jit(solution)/shard_map/ppermute | solution.py:630

commit v29 on v28

--- a/solution.py
+++ b/solution.py
@@ -364,10 +364,14 @@
     copies = []
     for t in range(tiles):
         rows = pl.ds(8 * t, 8)
-        sent[t] = gelu(base[:, rows, :] + across[:, rows, :])
         to = t if t < upper else t + gap
-        copies.append(pltpu.make_async_copy(sent.at[t], out.at[:, pl.ds(8 * to, 8), :], sem.at[t]))
-        copies[-1].start()
+        for h in range(2):
+            half = pl.ds(h * (CH // 2), CH // 2)
+            sent[t, half] = gelu(base[half, rows, :] + across[half, rows, :])
+            copies.append(
+                pltpu.make_async_copy(sent.at[t, half], out.at[half, pl.ds(8 * to, 8), :], sem.at[t, h])
+            )
+            copies[-1].start()
     for copy in copies:
         copy.wait()
 
@@ -462,7 +466,7 @@
         out_specs=anywhere,
         scratch_shapes=[
             pltpu.VMEM((tiles, CH, 8, NX), F32),
-            pltpu.SemaphoreType.DMA((tiles,)),
+            pltpu.SemaphoreType.DMA((tiles, 2)),
         ],
         input_output_aliases={0: 0},
         compiler_params=params(),

time: 58.7 us -> 58.7 us (level)
  no operation moved by 1% of the time
where the time goes in v29:
time: 58.7 us; the launch traced here: 58.3 us
  Pallas kernels  27.6 us (47%)
  starting transfers between devices  19.6 us (33%)
  waiting for transfers between devices  11 us (19%)
    ppermute x3, waiting for transfers between devices, to_neighbours(): lax.ppermute(across, 'gz', odd_on)  8.59 us
    pallas_call x1, Pallas kernels, own_call(): pl.pallas_call(functools.partial(own_kernel, segments, groups), out_shape...  7.13 us
    ppermute x3, starting transfers between devices, to_neighbours(): lax.ppermute(across, 'gz', odd_on)  6.05 us
    pallas_call x1, Pallas kernels, inverse_call(): pl.pallas_call(functools.partial(inverse_kernel, upper, halved), out_shap...  6 us
    all_to_all x1, starting transfers between devices, body(): back = lax.all_to_all(mark, 'gz', split_axis=0, concat_axis=0, tiled=True)  5.4 us
    pallas_call x1, Pallas kernels, middle_call(): pl.pallas_call(middle_kernel, out_shape=pltpu.HBM((CH, rows, NX), F32), i...  4.65 us
    pallas_call x1, Pallas kernels, forward_call(): pl.pallas_call(forward_kernel, out_shape=(pltpu.HBM if pinned else jax.Sh...  4.14 us
    ppermute x3, starting transfers between devices, to_neighbours(): lax.ppermute(within, 'gz', even_on)  3.04 us
  transfers between devices with their start and end apart: 10, of which 4 were waited for; matrix products, arithmetic and copies ran while one was open for 0% of the time, Pallas kernels for 42%

profile of v29, /device:TPU:1, one launch (start us, length us, event | category | flops | bytes accessed | tf_op | source)
XLA Modules:
  0.0 58.3 jit_solution(12886800996725722439)
XLA Ops:
  0.0 1.6 %packed_rows.1 = (f32[26,32,256]{2,1,0:T(8,128)S(1)}, f32[2,32,256]{2,1,0:T(8,128)S(1)}) custom-call(f32[32,64,256]{2,1,0:T(8,128)} %bitcast.24), custom_call_target="tpu_custom_call" | custom-call | flops 100000000 | bytes 262144 | tf_op jit(solution)/shard_map/packed_rows/pallas_call | solution.py:482
  1.6 2.7 %collective-permute-start.1 = (f32[26,32,256]{2,1,0:T(8,128)S(1)}, f32[26,32,256]{2,1,0:T(8,128)}, u32[]{:S(2)}, u32[]{:S(2)}) collective-permute-start(f32[26,32,256]{2,1,0:T(8,128)S(1)} %get-tuple-element.38.own), channel_id=1, source_target_pairs={{0,30},{2,4},{4,2},{6,8},{8,6},{10,12},{12,10},{14,16},{16,14},{18... | collective-permute-start | bytes 2555912 | tf_op jit(solution)/shard_map/ppermute | solution.py:591
  4.3 2.9 %collective-permute-start.2 = (f32[26,32,256]{2,1,0:T(8,128)S(1)}, f32[26,32,256]{2,1,0:T(8,128)}, u32[]{:S(2)}, u32[]{:S(2)}) collective-permute-start(f32[26,32,256]{2,1,0:T(8,128)S(1)} %get-tuple-element.38.own), channel_id=1, source_target_pairs={{0,2},{2,0},{4,6},{6,4},{8,10},{10,8},{12,14},{14,12},{16,18},{18,... | collective-permute-start | bytes 2555912 | tf_op jit(solution)/shard_map/ppermute | solution.py:591
  7.2 1.2 %collective-permute-start = (f32[2,32,256]{2,1,0:T(8,128)S(1)}, f32[2,32,256]{2,1,0:T(8,128)S(1)}, u32[]{:S(2)}, u32[]{:S(2)}) collective-permute-start(f32[2,32,256]{2,1,0:T(8,128)S(1)} %get-tuple-element.29), channel_id=1, source_target_pairs={{0,1},{1,0},{2,3},{3,2},{4,5},{5,4},{6,7},{7,6},{8,9},{9,8},{10,11... | collective-permute-start | bytes 196616 | tf_op jit(solution)/shard_map/ppermute | solution.py:603
  8.4 4.1 %forward_modes.1 = f32[256,128]{1,0:T(8,128)} custom-call(f32[8,4,64,256]{3,2,1,0:T(8,128)} %bitcast.25, bf16[2,256,128]{2,1,0:T(8,128)(2,1)} %constant.24.clone.x_top, bf16[2,256,128]{2,1,0:T(8,128)(2,1)} %constant.25.clone.x_rest, bf16[2,32,64]{2,1,0:T(8,128)(2,1)} %constant.26.clone.y_top, bf16[2,32,64]{2,1,0:T(8,128)(2,1)} %constant.27.clone.y_rest), custom_call_target="tpu_custom_call" | custom-call | flops 100000000 | bytes 262144 | tf_op jit(solution)/shard_map/forward_modes/pallas_call | solution.py:403
  12.5 0.0 collective-permute-done.halo
  12.5 2.5 %all-to-all-start = ((f32[32,8,128]{2,1,0:T(8,128)}), f32[32,8,128]{2,1,0:T(8,128)S(1)}, u32[]{:S(2)}, u32[]{:S(2)}) async-start(f32[32,8,128]{2,1,0:T(8,128)} %bitcast.31), calls=%async_computation | async-start | bytes 262144 | tf_op jit(solution)/shard_map/all_to_all | solution.py:620
  15.0 7.1 %own_sums.1 = (f32[32,16,256]{2,1,0:T(8,128)}, f32[32,16,256]{2,1,0:T(8,128)}, f32[32,16,256]{2,1,0:T(8,128)}, f32[32,24,256]{2,1,0:T(8,128)}, f32[32,24,256]{2,1,0:T(8,128)}, /*index=5*/f32[32,24,256]{2,1,0:T(8,128)}) custom-call(f32[32,27]{1,0:T(8,128)} %weight.3, f32[32,32]{1,0:T(8,128)} %point.3, f32[32,64,256]{2,1,0:T(8,128)} %bitcast.26, ...), custom_call_target="tpu_custom_call" | custom-call | flops 100000000 | bytes 262144 | tf_op jit(solution)/shard_map/own_sums/pallas_call | solution.py:502
  22.1 3.1 %collective-permute-done.1.low = f32[26,32,256]{2,1,0:T(8,128)} collective-permute-done((f32[26,32,256]{2,1,0:T(8,128)S(1)}, f32[26,32,256]{2,1,0:T(8,128)}, u32[]{:S(2)}, u32[]{:S(2)}) %collective-permute-start.1) | collective-permute-done | bytes 852000 | tf_op jit(solution)/shard_map/ppermute | solution.py:591
  25.2 0.0 collective-permute-done.2.high
  25.2 1.7 %collective-permute-start.3 = (f32[32,16,256]{2,1,0:T(8,128)}, f32[32,16,256]{2,1,0:T(8,128)S(1)}, u32[]{:S(2)}, u32[]{:S(2)}) collective-permute-start(f32[32,16,256]{2,1,0:T(8,128)} %get-tuple-element.36), channel_id=1, source_target_pairs={{0,30},{2,4},{4,2},{6,8},{8,6},{10,12},{12,10},{14,16},{16,14},{18... | collective-permute-start | bytes 1572872 | tf_op jit(solution)/shard_map/ppermute | solution.py:591
  27.0 0.0 collective-permute-start.4
  27.0 0.0 all-to-all-done
  27.0 2.4 %filter_modes.1 = f32[128,128]{1,0:T(8,128)} custom-call(f32[256,128]{1,0:T(8,128)S(1)} %bitcast.23, f32[2,16,8,64]{3,2,1,0:T(8,128)} %gains, bf16[256,256]{1,0:T(8,128)(2,1)} %constant.28.clone.f_top, bf16[256,256]{1,0:T(8,128)(2,1)} %constant.29.clone.f_rest, bf16[256,128]{1,0:T(8,128)(2,1)} %constant.30.clone.i_top, bf16[256,128]{1,0:T(8,128)(2,1)} %constant.31.clone.i_rest), custom_call_target="tpu_custom_call" | custom-call | flops 40000000000 | bytes 262144 | tf_op jit(solution)/shard_map/filter_modes/pallas_call | solution.py:422
  29.4 5.4 %all-to-all-start.1 = ((f32[16,8,128]{2,1,0:T(8,128)}), f32[16,8,128]{2,1,0:T(8,128)S(1)}, u32[]{:S(2)}, u32[]{:S(2)}) async-start(f32[16,8,128]{2,1,0:T(8,128)} %bitcast.32), calls=%async_computation.1 | async-start | bytes 131072 | tf_op jit(solution)/shard_map/all_to_all | solution.py:625
  34.8 0.2 collective-permute-start.6
  35.0 1.6 %collective-permute-start.7 = (f32[32,24,256]{2,1,0:T(8,128)}, f32[32,24,256]{2,1,0:T(8,128)S(1)}, u32[]{:S(2)}, u32[]{:S(2)}) collective-permute-start(f32[32,24,256]{2,1,0:T(8,128)} %get-tuple-element.48), channel_id=1, source_target_pairs={{0,30},{2,4},{4,2},{6,8},{8,6},{10,12},{12,10},{14,16},{16,14},{18... | collective-permute-start | bytes 2359304 | tf_op jit(solution)/shard_map/ppermute | solution.py:591
  36.6 3.1 %collective-permute-done.3 = f32[32,16,256]{2,1,0:T(8,128)S(1)} collective-permute-done((f32[32,16,256]{2,1,0:T(8,128)}, f32[32,16,256]{2,1,0:T(8,128)S(1)}, u32[]{:S(2)}, u32[]{:S(2)}) %collective-permute-start.3) | collective-permute-done | bytes 524320 | tf_op jit(solution)/shard_map/ppermute | solution.py:591
  39.7 0.0 collective-permute-done.4
  39.7 4.6 %middle_sums.1 = f32[32,24,256]{2,1,0:T(8,128)} custom-call(f32[32,27]{1,0:T(8,128)} %weight.3, f32[32,32]{1,0:T(8,128)} %point.3, f32[26,32,256]{2,1,0:T(8,128)} %collective-permute-done.1.low, f32[26,32,256]{2,1,0:T(8,128)S(1)} %get-tuple-element.38.own, f32[26,32,256]{2,1,0:T(8,128)} %collective-permute-done.2.high), custom_call_target="tpu_custom_call" | custom-call | flops 40000000000 | bytes 262144 | tf_op jit(solution)/shard_map/middle_sums/pallas_call | solution.py:529
  44.4 0.0 all-to-all-done.1
  44.4 1.4 %collective-permute-start.5 = (f32[128,128]{1,0:T(8,128)S(1)}, f32[128,128]{1,0:T(8,128)S(1)}, u32[]{:S(2)}, u32[]{:S(2)}) collective-permute-start(f32[128,128]{1,0:T(8,128)S(1)} %bitcast.21), channel_id=1, source_target_pairs={{0,1},{1,0},{2,3},{3,2},{4,5},{5,4},{6,7},{7,6},{8,9},{9,8},{10,11... | collective-permute-start | bytes 196616 | tf_op jit(solution)/shard_map/ppermute | solution.py:634
  45.8 2.4 %collective-permute-done.5.second_modes = f32[128,128]{1,0:T(8,128)S(1)} collective-permute-done((f32[128,128]{1,0:T(8,128)S(1)}, f32[128,128]{1,0:T(8,128)S(1)}, u32[]{:S(2)}, u32[]{:S(2)}) %collective-permute-start.5) | collective-permute-done | bytes 65568 | tf_op jit(solution)/shard_map/ppermute | solution.py:634
  48.2 0.0 collective-permute-done.6
  48.2 6.0 %inverse_modes.1 = (f32[8,4,64,256]{3,2,1,0:T(8,128)}, f32[8,4,24,256]{3,2,1,0:T(8,128)S(1)}) custom-call(f32[128,128]{1,0:T(8,128)S(1)} %bitcast.22, f32[128,128]{1,0:T(8,128)S(1)} %collective-permute-done.5.second_modes, f32[32]{0:T(128)} %bias.1, bf16[2,128,256]{2,1,0:T(8,128)(2,1)} %constant.32.clone.x_top, bf16[2,128,256]{2,1,0:T(8,128)(2,1)} %constant.33.clone.x_rest, ...), custom_call_target="tpu_custom_call" | custom-call | flops 100000000 | bytes 262144 | tf_op jit(solution)/shard_map/inverse_modes/pallas_call | solution.py:436
  54.2 2.4 %collective-permute-done.7.across = f32[32,24,256]{2,1,0:T(8,128)S(1)} collective-permute-done((f32[32,24,256]{2,1,0:T(8,128)}, f32[32,24,256]{2,1,0:T(8,128)S(1)}, u32[]{:S(2)}, u32[]{:S(2)}) %collective-permute-start.7) | collective-permute-done | bytes 786464 | tf_op jit(solution)/shard_map/ppermute | solution.py:591
  56.6 1.6 %finished_rows.1 = f32[32,64,256]{2,1,0:T(8,128)} custom-call(f32[32,64,256]{2,1,0:T(8,128)} %bitcast.27, f32[32,24,256]{2,1,0:T(8,128)S(1)} %bitcast.18, f32[32,24,256]{2,1,0:T(8,128)S(1)} %collective-permute-done.7.across), custom_call_target="tpu_custom_call", output_to_operand_aliasing={{}: (0, {})} | custom-call | flops 100000000 | bytes 262144 | tf_op jit(solution)/shard_map/finished_rows/pallas_call | solution.py:462
Async XLA Ops:
  1.6 23.6 %collective-permute-start.1 = (f32[26,32,256]{2,1,0:T(8,128)S(1)}, f32[26,32,256]{2,1,0:T(8,128)}, u32[]{:S(2)}, u32[]{:S(2)}) collective-permute-start(f32[26,32,256]{2,1,0:T(8,128)S(1)} %get-tuple-element.38.own), channel_id=1, source_target_pairs={{0,30},{2,4},{4,2},{6,8},{8,6},{10,12},{12,10},{14,16},{16,14},{18... | collective-permute-start | bytes 2555912 | tf_op jit(solution)/shard_map/ppermute | solution.py:591
  4.3 20.9 %collective-permute-start.2 = (f32[26,32,256]{2,1,0:T(8,128)S(1)}, f32[26,32,256]{2,1,0:T(8,128)}, u32[]{:S(2)}, u32[]{:S(2)}) collective-permute-start(f32[26,32,256]{2,1,0:T(8,128)S(1)} %get-tuple-element.38.own), channel_id=1, source_target_pairs={{0,2},{2,0},{4,6},{6,4},{8,10},{10,8},{12,14},{14,12},{16,18},{18,... | collective-permute-start | bytes 2555912 | tf_op jit(solution)/shard_map/ppermute | solution.py:591
  7.2 5.4 %collective-permute-start = (f32[2,32,256]{2,1,0:T(8,128)S(1)}, f32[2,32,256]{2,1,0:T(8,128)S(1)}, u32[]{:S(2)}, u32[]{:S(2)}) collective-permute-start(f32[2,32,256]{2,1,0:T(8,128)S(1)} %get-tuple-element.29), channel_id=1, source_target_pairs={{0,1},{1,0},{2,3},{3,2},{4,5},{5,4},{6,7},{7,6},{8,9},{9,8},{10,11... | collective-permute-start | bytes 196616 | tf_op jit(solution)/shard_map/ppermute | solution.py:603
  12.5 14.4 %all-to-all-start = ((f32[32,8,128]{2,1,0:T(8,128)}), f32[32,8,128]{2,1,0:T(8,128)S(1)}, u32[]{:S(2)}, u32[]{:S(2)}) async-start(f32[32,8,128]{2,1,0:T(8,128)} %bitcast.31), calls=%async_computation | async-start | bytes 262144 | tf_op jit(solution)/shard_map/all_to_all | solution.py:620
  25.2 14.5 %collective-permute-start.3 = (f32[32,16,256]{2,1,0:T(8,128)}, f32[32,16,256]{2,1,0:T(8,128)S(1)}, u32[]{:S(2)}, u32[]{:S(2)}) collective-permute-start(f32[32,16,256]{2,1,0:T(8,128)} %get-tuple-element.36), channel_id=1, source_target_pairs={{0,30},{2,4},{4,2},{6,8},{8,6},{10,12},{12,10},{14,16},{16,14},{18... | collective-permute-start | bytes 1572872 | tf_op jit(solution)/shard_map/ppermute | solution.py:591
  27.0 12.8 %collective-permute-start.4 = (f32[32,16,256]{2,1,0:T(8,128)}, f32[32,16,256]{2,1,0:T(8,128)S(1)}, u32[]{:S(2)}, u32[]{:S(2)}) collective-permute-start(f32[32,16,256]{2,1,0:T(8,128)} %get-tuple-element.37), channel_id=1, source_target_pairs={{0,2},{2,0},{4,6},{6,4},{8,10},{10,8},{12,14},{14,12},{16,18},{18,... | collective-permute-start | bytes 1572872 | tf_op jit(solution)/shard_map/ppermute | solution.py:591
  29.4 15.0 %all-to-all-start.1 = ((f32[16,8,128]{2,1,0:T(8,128)}), f32[16,8,128]{2,1,0:T(8,128)S(1)}, u32[]{:S(2)}, u32[]{:S(2)}) async-start(f32[16,8,128]{2,1,0:T(8,128)} %bitcast.32), calls=%async_computation.1 | async-start | bytes 131072 | tf_op jit(solution)/shard_map/all_to_all | solution.py:625
  34.8 13.4 %collective-permute-start.6 = (f32[32,24,256]{2,1,0:T(8,128)}, f32[32,24,256]{2,1,0:T(8,128)S(1)}, u32[]{:S(2)}, u32[]{:S(2)}) collective-permute-start(f32[32,24,256]{2,1,0:T(8,128)} %get-tuple-element.42), channel_id=1, source_target_pairs={{0,2},{2,0},{4,6},{6,4},{8,10},{10,8},{12,14},{14,12},{16,18},{18,... | collective-permute-start | bytes 2359304 | tf_op jit(solution)/shard_map/ppermute | solution.py:591
  35.0 21.6 %collective-permute-start.7 = (f32[32,24,256]{2,1,0:T(8,128)}, f32[32,24,256]{2,1,0:T(8,128)S(1)}, u32[]{:S(2)}, u32[]{:S(2)}) collective-permute-start(f32[32,24,256]{2,1,0:T(8,128)} %get-tuple-element.48), channel_id=1, source_target_pairs={{0,30},{2,4},{4,2},{6,8},{8,6},{10,12},{12,10},{14,16},{16,14},{18... | collective-permute-start | bytes 2359304 | tf_op jit(solution)/shard_map/ppermute | solution.py:591
  44.4 3.8 %collective-permute-start.5 = (f32[128,128]{1,0:T(8,128)S(1)}, f32[128,128]{1,0:T(8,128)S(1)}, u32[]{:S(2)}, u32[]{:S(2)}) collective-permute-start(f32[128,128]{1,0:T(8,128)S(1)} %bitcast.21), channel_id=1, source_target_pairs={{0,1},{1,0},{2,3},{3,2},{4,5},{5,4},{6,7},{7,6},{8,9},{9,8},{10,11... | collective-permute-start | bytes 196616 | tf_op jit(solution)/shard_map/ppermute | solution.py:634
